TPU v7x, 32 devices: a whole 2x2x4 slice. The times are simulated.
32 devices in a mesh: ctx: 8 (over z, y), fsdp: 4 (over x, core).
Axes of the slice: x: 2, y: 2, z: 4, core: 2. Of those that a mesh axis runs over, the one named last changes fastest.
Arguments:
- query_rows: bfloat16 [4096, 8192], P(('fsdp', 'ctx')), may hold values from -6 to 6
- key_rows: bfloat16 [4096, 1024], P(('fsdp', 'ctx')), may hold values from -6 to 6
- value_rows: bfloat16 [4096, 1024], P(('fsdp', 'ctx')), may hold values from -6 to 6
- grad_out: bfloat16 [4096, 8192], P(('fsdp', 'ctx')), may hold values from -384 to 384
- query_map: bfloat16 [64, 128, 64], P('ctx', 'fsdp'), may hold values from -1.5 to 1.5
- key_map: bfloat16 [64, 128, 64], P('ctx', 'fsdp'), may hold values from -1.5 to 1.5
- prefix_state: float32 [64, 128, 128], P('ctx'), may hold values from -24 to 24
- prefix_norm: float32 [64, 128], P('ctx'), may hold values from 16 to 256
Outputs:
- grad_queries: bfloat16 [4096, 8192], P(('fsdp', 'ctx'))
- grad_keys: bfloat16 [4096, 1024], P(('fsdp', 'ctx'))
- grad_values: bfloat16 [4096, 1024], P(('fsdp', 'ctx'))
- grad_query_map: float32 [64, 128, 64], P('ctx', 'fsdp')
- grad_key_map: float32 [64, 128, 64], P('ctx', 'fsdp')
- grad_prefix_state: float32 [64, 128, 128], P('ctx', 'fsdp')
All inputs are finite; a program needn't handle non-finite values.
Results may differ from a plain program's by a relative error of at most 0.014.
The roundings to bfloat16 on the way count: a program that leaves them out, or rounds other values in their place, can miss the bound.
Values may be sent and summed in bfloat16 or wider, within the bound.
No kernel may reach another device: no remote copies, remote signals or barrier semaphores. Data moves between devices by JAX's collectives and lax.ppermute only.
A program may use at most 128 MiB of HBM per device.

v0:
```python
import functools

import jax
import jax.numpy as jnp
from jax import lax
from jax.experimental import pallas as pl
from jax.experimental.pallas import tpu as pltpu
from jax.sharding import PartitionSpec as P

BLK = 512
TILE = 256
PAIR = 2
EXT = 16
LIMIT = 40 * 1024 * 1024

F32 = jnp.float32
BF16 = jnp.bfloat16
SMEM = pltpu.SMEM


def nn(left, right):
    return lax.dot_general(left, right, (((1,), (0,)), ((), ())), preferred_element_type=F32)


def nt(left, right):
    return lax.dot_general(left, right, (((1,), (1,)), ((), ())), preferred_element_type=F32)


def turned(array):
    return array.astype(F32).T.astype(array.dtype)


def column(row, width):
    n = row.shape[1]
    square = jnp.broadcast_to(row, (n, n)).T
    return jnp.concatenate([square] * (width // n), axis=1)


def thirds(row):
    rows = jnp.broadcast_to(row, (EXT, row.shape[1]))
    high = rows.astype(BF16).astype(F32)
    middle = (rows - high).astype(BF16).astype(F32)
    low = rows - high - middle
    place = lax.broadcasted_iota(jnp.int32, rows.shape, 0)
    picked = jnp.where(place == 0, high, jnp.where(place == 1, middle, low))
    return jnp.where(place < 3, picked, 0.0).astype(BF16)


def whole_row(block):
    return jnp.sum(block.astype(F32), axis=0, keepdims=True)


def weight_rows(ref, u):
    whole = jnp.concatenate([ref[i, u] for i in range(ref.shape[0])], axis=0)
    return turned(whole)


def features(weight, rows):
    logits = nt(weight, rows).astype(BF16).astype(F32)
    upper = jnp.exp(logits)
    lower = jnp.exp(-logits)
    upper = upper * (1.0 / jnp.sum(upper, axis=0, keepdims=True))
    lower = lower * (1.0 / jnp.sum(lower, axis=0, keepdims=True))
    return jnp.concatenate([upper, lower], axis=0)


def feature_back(feats, upstream):
    half = feats.shape[0] // 2
    weighted = feats * upstream
    first, second = weighted[:half], weighted[half:]
    first = first - feats[:half] * jnp.sum(first, axis=0, keepdims=True)
    second = second - feats[half:] * jnp.sum(second, axis=0, keepdims=True)
    return (first - second).astype(BF16)


def gather(offsets, refs, out):
    rows = refs[0].shape[0]
    for r, ref in enumerate(refs):
        out[pl.ds(pl.multiple_of(offsets[r], rows), rows), :] = ref[...]


def scatter(offsets, source, refs):
    rows = refs[0].shape[0]
    for r, ref in enumerate(refs):
        ref[...] = source[pl.ds(pl.multiple_of(offsets[r], rows), rows), :].astype(ref.dtype)


def pack_kernel(columns, inputs, width, table, *refs):
    sources, outs, sems = refs[:inputs], refs[inputs:-1], refs[-1]
    copies = []
    for r, out in enumerate(outs):
        for s in range(columns):
            at = pl.multiple_of(table[r * columns + s] * width, width)
            for i, source in enumerate(sources):
                to = (s * inputs + i) * width
                copies.append(
                    pltpu.make_async_copy(
                        source.at[:, pl.ds(at, width)],
                        out.at[:, pl.ds(to, width)],
                        sems.at[len(copies)],
                    )
                )
    for copy in copies:
        copy.start()
    for copy in copies:
        copy.wait()


def pack(table, sources, pieces, columns, width):
    rows = sources[0].shape[0]
    total = columns * len(sources) * width
    return pl.pallas_call(
        functools.partial(pack_kernel, columns, len(sources), width),
        out_shape=[jax.ShapeDtypeStruct((rows, total), sources[0].dtype)] * pieces,
        in_specs=[pl.BlockSpec(memory_space=SMEM)]
        + [pl.BlockSpec(memory_space=pl.ANY)] * len(sources),
        out_specs=[pl.BlockSpec(memory_space=pl.ANY)] * pieces,
        scratch_shapes=[pltpu.SemaphoreType.DMA((pieces * columns * len(sources),))],
        cost_estimate=pl.CostEstimate(
            flops=0, bytes_accessed=4 * pieces * rows * total, transcendentals=0
        ),
        name="pack",
    )(table, *sources)


def unpack_kernel(outputs, width, table, *refs):
    pieces, outs, sems = refs[: -outputs - 1], refs[-outputs - 1 : -1], refs[-1]
    copies = []
    for r, piece in enumerate(pieces):
        at = pl.multiple_of(table[r] * width, width)
        for i, out in enumerate(outs):
            copies.append(
                pltpu.make_async_copy(
                    piece.at[:, pl.ds(i * width, width)],
                    out.at[:, pl.ds(at, width)],
                    sems.at[len(copies)],
                )
            )
    for copy in copies:
        copy.start()
    for copy in copies:
        copy.wait()


def unpack(table, pieces, outputs, width):
    rows = pieces[0].shape[0]
    total = len(pieces) * width
    return pl.pallas_call(
        functools.partial(unpack_kernel, outputs, width),
        out_shape=[jax.ShapeDtypeStruct((rows, total), pieces[0].dtype)] * outputs,
        in_specs=[pl.BlockSpec(memory_space=SMEM)]
        + [pl.BlockSpec(memory_space=pl.ANY)] * len(pieces),
        out_specs=[pl.BlockSpec(memory_space=pl.ANY)] * outputs,
        scratch_shapes=[pltpu.SemaphoreType.DMA((len(pieces) * outputs,))],
        cost_estimate=pl.CostEstimate(
            flops=0, bytes_accessed=4 * rows * total * outputs, transcendentals=0
        ),
        name="unpack",
    )(table, *pieces)


def state_kernel(part, offsets, *refs):
    k_refs, v_refs, (w_ref, out, k_all, v_all) = refs[:part], refs[part : 2 * part], refs[2 * part :]
    hd = k_all.shape[1]

    @pl.when(pl.program_id(0) == 0)
    def _():
        gather(offsets, k_refs, k_all)
        gather(offsets, v_refs, v_all)

    for u in range(out.shape[0]):
        weight = weight_rows(w_ref, u)
        feats = features(weight[weight.shape[0] // 2 :], k_all[...]).astype(BF16)
        out[u, :hd, :] = nn(feats, v_all[...]).astype(BF16)
        ones = jnp.ones((EXT, feats.shape[1]), BF16)
        out[u, hd:, :] = thirds(nt(ones, feats)[:1])


def block_kernel(part, offsets, *refs):
    k_refs, v_refs = refs[:part], refs[part : 2 * part]
    q_refs, g_refs = refs[2 * part : 3 * part], refs[3 * part : 4 * part]
    w_ref, st_ref = refs[4 * part : 4 * part + 2]
    gq_refs = refs[4 * part + 2 : 5 * part + 2]
    dk_ref, dv_ref, sx_ref, gm_ref, k_all, v_all, vt_all, q_all, g_all, gq_all = refs[5 * part + 2 :]
    hd = k_all.shape[1]

    @pl.when(pl.program_id(0) == 0)
    def _():
        gather(offsets, k_refs, k_all)
        gather(offsets, v_refs, v_all)
        vt_all[...] = turned(v_all[...])
        dv_ref[...] = jnp.zeros_like(dv_ref)

    gather(offsets, q_refs, q_all)
    gather(offsets, g_refs, g_all)
    maps = []
    earlier = lax.broadcasted_iota(jnp.int32, (TILE, TILE), 0) <= lax.broadcasted_iota(
        jnp.int32, (TILE, TILE), 1
    )

    def causal(array, begin):
        masked = jnp.where(earlier, array[begin:], 0.0)
        return masked if begin == 0 else jnp.concatenate([array[:begin], masked], axis=0)

    for u in range(PAIR):
        weight = weight_rows(w_ref, u)
        half = weight.shape[0] // 2
        lanes = slice(u * hd, (u + 1) * hd)
        q_feat = features(weight[:half], q_all[:, lanes])
        k_low = features(weight[half:], k_all[...]).astype(BF16)
        q_low = q_feat.astype(BF16)
        k_turned = turned(k_low)
        state = st_ref[u, :hd, :]
        state_turned = turned(state)
        norm = column(whole_row(st_ref[u, hd:, :]), TILE)
        g_turned = g_all[:, lanes].astype(F32).T
        back = []
        dkey = [jnp.zeros((2 * half, TILE), F32) for _ in range(BLK // TILE)]
        dvalue = [jnp.zeros((hd, TILE), F32) for _ in range(BLK // TILE)]
        suffix = jnp.zeros((2 * half, hd), F32)
        suffix_norm = jnp.zeros((2 * half, 1), F32)
        for j in range(BLK // TILE):
            begin, end = j * TILE, (j + 1) * TILE
            own = q_low[:, begin:end]
            own_wide = own.astype(F32)
            scores = causal(nn(k_turned[:end], own), begin)
            scores_low = scores.astype(BF16)
            numerator = nn(state_turned, own) + nn(vt_all[:, :end], scores_low)
            denominator = jnp.sum(own_wide * norm, axis=0, keepdims=True) + jnp.sum(
                scores, axis=0, keepdims=True
            )
            inverse = 1.0 / denominator
            scaled = g_turned[:, begin:end] * inverse
            scaled_low = scaled.astype(BF16)
            norm_grad = -jnp.sum(scaled * (numerator * inverse), axis=0, keepdims=True)
            dscores = causal(nn(v_all[:end, :], scaled_low) + norm_grad, begin).astype(BF16)
            dquery = nn(state, scaled_low) + norm * norm_grad + nn(k_low[:, :end], dscores)
            back.append(feature_back(q_feat[:, begin:end], dquery))
            for i in range(j + 1):
                rows = slice(i * TILE, (i + 1) * TILE)
                dkey[i] = dkey[i] + nt(own, dscores[rows])
                dvalue[i] = dvalue[i] + nt(scaled_low, scores_low[rows])
            suffix = suffix + nt(own, scaled_low)
            suffix_norm = suffix_norm + jnp.sum(own_wide * norm_grad, axis=1, keepdims=True)
        dlog = jnp.concatenate(back, axis=1)
        gq_all[:, lanes] = nn(turned(dlog), weight[:half])
        maps.append(nn(dlog, q_all[:, lanes]))
        dk_ref[u] = jnp.concatenate(dkey, axis=1)
        dv_ref[...] += jnp.concatenate(dvalue, axis=1)
        sx_ref[u, :hd, :] = suffix.astype(BF16)
        sx_ref[u, hd:, :] = thirds(jnp.broadcast_to(suffix_norm, (2 * half, 2 * half)).T[:1])
    gm_ref[0] = jnp.concatenate(maps, axis=0).T.astype(gm_ref.dtype)
    scatter(offsets, gq_all, gq_refs)


def key_kernel(part, offsets, *refs):
    k_refs, v_refs = refs[:part], refs[part : 2 * part]
    w_ref, sx_ref, dk_ref, dv_ref = refs[2 * part : 2 * part + 4]
    outs = refs[2 * part + 4 : 3 * part + 4]
    gm_ref, k_all, v_all, vt_all, total, logs, weights, pair = refs[3 * part + 4 :]
    hd = k_all.shape[1]
    step = pl.program_id(0)

    @pl.when(step == 0)
    def _():
        gather(offsets, k_refs, k_all)
        gather(offsets, v_refs, v_all)
        vt_all[...] = turned(v_all[...])
        total[...] = dv_ref[...]

    maps = []
    for u in range(PAIR):
        weight = weight_rows(w_ref, u)
        half = weight.shape[0] // 2
        weight = weight[half:]
        feats = features(weight, k_all[...])
        suffix = sx_ref[u, :hd, :]
        norm = column(whole_row(sx_ref[u, hd:, :]), BLK)
        dlog = feature_back(feats, dk_ref[u] + nn(suffix, vt_all[...]) + norm)
        at = pl.ds(pl.multiple_of((step * PAIR + u) * half, half), half)
        logs[at, :] = dlog
        weights[at, :] = weight
        maps.append(nn(dlog, k_all[...]))
        total[...] += nn(turned(suffix), feats.astype(BF16))
    gm_ref[0] = jnp.concatenate(maps, axis=0).T.astype(gm_ref.dtype)

    @pl.when(step == pl.num_programs(0) - 1)
    def _():
        pair[:, :hd] = nn(turned(logs[...]), weights[...])
        pair[:, hd:] = total[...].T
        scatter(offsets, pair, outs)


def total_kernel(*refs):
    out = refs[-1]
    heads, hd = out.shape[0], out.shape[2]
    for h in range(heads):
        out[h, :hd, :] = sum(ref[h, :hd, :].astype(F32) for ref in refs[:-1]).astype(BF16)
        out[h, hd:, :] = thirds(sum(whole_row(ref[h, hd:, :]) for ref in refs[:-1]))


def spread_kernel(grp, others, closing, block_weight, total_weight, place, *refs):
    parts, totals, refs = refs[:grp], refs[grp : grp + others], refs[grp + others :]
    if closing:
        outs, grad, scratch = refs[:grp], refs[grp], refs[grp + 1]
    else:
        state_ref, norm_ref, outs = refs[0], refs[1], refs[2:]
    heads, hd = parts[0].shape[0], parts[0].shape[2]
    for h in range(heads):
        states = [ref[h, :hd, :].astype(F32) for ref in parts]
        norms = [whole_row(ref[h, hd:, :]) for ref in parts]
        others_state = [ref[h, :hd, :].astype(F32) for ref in totals]
        others_norm = [whole_row(ref[h, hd:, :]) for ref in totals]
        if closing:
            base, base_norm = jnp.zeros_like(states[0]), jnp.zeros_like(norms[0])
            scratch[...] = sum(states) + sum(others_state)
            rows = grad.shape[1]
            grad[h] = scratch[pl.ds(pl.multiple_of(place[0] * rows, rows), rows), :]
        else:
            base, base_norm = state_ref[h], norm_ref[pl.ds(h, 1), :]
        for i, (state, norm) in enumerate(zip(others_state, others_norm)):
            base = base + total_weight[i] * state
            base_norm = base_norm + total_weight[i] * norm
        for r, out in enumerate(outs):
            state, norm = base, base_norm
            for i in range(grp):
                if i != r:
                    state = state + block_weight[r * grp + i] * states[i]
                    norm = norm + block_weight[r * grp + i] * norms[i]
            out[h, :hd, :] = state.astype(BF16)
            out[h, hd:, :] = thirds(norm)


def whole_call(kernel, outs, smem, arrays, name, scratch=()):
    total = sum(a.size * a.dtype.itemsize for a in (*arrays, *outs))
    return pl.pallas_call(
        kernel,
        out_shape=outs,
        in_specs=[pl.BlockSpec(memory_space=SMEM)] * len(smem)
        + [pl.BlockSpec(memory_space=pltpu.VMEM)] * len(arrays),
        out_specs=[pl.BlockSpec(memory_space=pltpu.VMEM)] * len(outs),
        scratch_shapes=list(scratch),
        compiler_params=pltpu.CompilerParams(vmem_limit_bytes=LIMIT),
        cost_estimate=pl.CostEstimate(flops=total, bytes_accessed=total, transcendentals=0),
        name=name,
    )(*smem, *arrays)


def shards(
    query_rows, key_rows, value_rows, grad_out, query_map, key_map, prefix_state, prefix_norm
):
    ctx, fsdp = lax.axis_size("ctx"), lax.axis_size("fsdp")
    tok = query_rows.shape[0]
    heads, map_rows, half = query_map.shape
    hd = map_rows * fsdp
    kv_heads = key_rows.shape[1] // hd
    replicas = ctx // kv_heads
    part = BLK // tok
    grp = ctx // part
    mine = lax.axis_index("ctx")
    at, block, seq = mine % part, mine // part, lax.axis_index("fsdp")

    def within(array, shift):
        return lax.ppermute(
            array, "ctx", [(d, d // part * part + (d + shift) % part) for d in range(ctx)]
        )

    def across(array, shift):
        return lax.ppermute(array, "ctx", [(d, (d + shift * part) % ctx) for d in range(ctx)])

    def along(array, shift):
        return lax.ppermute(array, "fsdp", [(d, (d + shift) % fsdp) for d in range(fsdp)])

    def owner(shift, slot):
        return (block + slot) % grp * part + (at + shift) % part

    def ints(values):
        return jnp.stack([jnp.asarray(v, jnp.int32) for v in values])

    shifts, slots = range(part), range(grp)
    order = list(reversed(slots))
    offsets = ints([(at - r) % part * tok for r in shifts])

    own_maps = jnp.concatenate((query_map, key_map), axis=-1)
    kv_table = ints([owner(r, s) // replicas for r in shifts for s in slots])
    kv_sent = pack(kv_table, (key_rows, value_rows), part, grp, hd)
    kv = [kv_sent[0]] + [within(kv_sent[r], r) for r in shifts[1:]]
    maps = jnp.stack([own_maps] + [across(own_maps, -s) for s in slots[1:]])
    maps = lax.all_gather(maps, "fsdp")

    rows = {}
    for s in order:
        table = ints([owner(r, s) for r in shifts])
        sent = pack(table, (query_rows, grad_out), part, 1, heads * hd)
        rows[s] = [sent[0]] + [within(sent[r], r) for r in shifts[1:]]

    grid = (heads // PAIR,)
    params = pltpu.CompilerParams(
        dimension_semantics=("arbitrary",), vmem_limit_bytes=LIMIT
    )
    in_smem = pl.BlockSpec(memory_space=SMEM)

    def piece_specs(column, count):
        return [pl.BlockSpec((tok, count * hd), column)] * part

    def kv_specs(s):
        return piece_specs(lambda h: (0, 2 * s), 1) + piece_specs(lambda h: (0, 2 * s + 1), 1)

    def map_spec(s):
        return pl.BlockSpec((fsdp, None, PAIR, map_rows, 2 * half), lambda h: (0, s, h, 0, 0))

    ext_spec = pl.BlockSpec((PAIR, hd + EXT, hd), lambda h: (h, 0, 0))
    ext_shape = jax.ShapeDtypeStruct((heads, hd + EXT, hd), BF16)
    gm_spec = pl.BlockSpec((1, hd, PAIR * half), lambda h: (h, 0, 0))
    gm_shape = jax.ShapeDtypeStruct((heads // PAIR, hd, PAIR * half), BF16)
    dk_spec = pl.BlockSpec((PAIR, 2 * half, BLK), lambda h: (h, 0, 0))
    dv_spec = pl.BlockSpec((hd, BLK), lambda h: (0, 0))
    unit = 2 * heads * BLK * hd

    def states_of(s):
        return pl.pallas_call(
            functools.partial(state_kernel, part),
            out_shape=ext_shape,
            grid=grid,
            in_specs=[in_smem] + kv_specs(s) + [map_spec(s)],
            out_specs=ext_spec,
            scratch_shapes=[pltpu.VMEM((BLK, hd), BF16)] * 2,
            compiler_params=params,
            cost_estimate=pl.CostEstimate(
                flops=unit * 2 * hd, bytes_accessed=2 * heads * hd * hd, transcendentals=0
            ),
            name="states",
        )(offsets, *kv, *kv, maps)

    def scan(partial, before, extra, closing):
        parts = [partial[0]] + [across(partial[s], s) for s in slots[1:]]
        (total,) = whole_call(total_kernel, [ext_shape], [], parts, "totals")
        others = [along(total, r) for r in range(1, fsdp)]
        result = whole_call(
            functools.partial(spread_kernel, grp, fsdp - 1, closing),
            [ext_shape] * grp
            + [jax.ShapeDtypeStruct((heads, map_rows, hd), F32)] * closing,
            [*weights(before), ints([seq])],
            parts + others + extra,
            "spread",
            [pltpu.VMEM((hd, hd), F32)] * closing,
        )
        return [result[0]] + [across(result[s], -s) for s in slots[1:]], result[grp:]

    def weights(before):
        seqs = [(seq - r) % fsdp for r in range(1, fsdp)]
        blocks = [(block - r) % grp for r in slots]
        return (
            jnp.stack([before(b, a).astype(F32) for a in blocks for b in blocks]),
            jnp.stack([before(other, seq).astype(F32) for other in seqs]),
        )

    partial = {s: states_of(s) for s in order}
    state, _ = scan(partial, lambda a, b: a < b, [prefix_state, prefix_norm], False)

    def block_of(s):
        half_specs = piece_specs(lambda h: (0, h), PAIR) + piece_specs(
            lambda h: (0, grid[0] + h), PAIR
        )
        return pl.pallas_call(
            functools.partial(block_kernel, part),
            out_shape=[jax.ShapeDtypeStruct((tok, heads * hd), BF16)] * part
            + [
                jax.ShapeDtypeStruct((heads, 2 * half, BLK), F32),
                jax.ShapeDtypeStruct((hd, BLK), F32),
                ext_shape,
                gm_shape,
            ],
            grid=grid,
            in_specs=[in_smem] + kv_specs(s) + half_specs + [map_spec(s), ext_spec],
            out_specs=piece_specs(lambda h: (0, h), PAIR) + [dk_spec, dv_spec, ext_spec, gm_spec],
            scratch_shapes=[
                pltpu.VMEM((BLK, hd), BF16),
                pltpu.VMEM((BLK, hd), BF16),
                pltpu.VMEM((hd, BLK), BF16),
                pltpu.VMEM((BLK, PAIR * hd), BF16),
                pltpu.VMEM((BLK, PAIR * hd), BF16),
                pltpu.VMEM((BLK, PAIR * hd), F32),
            ],
            compiler_params=params,
            cost_estimate=pl.CostEstimate(
                flops=unit * 8 * BLK, bytes_accessed=16 * heads * BLK * hd, transcendentals=0
            ),
            name="blocks",
        )(offsets, *kv, *kv, *rows[s], *rows[s], maps, state[s])

    blocks = {}
    for s in order:
        result = block_of(s)
        blocks[s] = (result[:part], *result[part:])
    partial = {s: blocks[s][3] for s in slots}
    suffix, (grad_prefix,) = scan(partial, lambda a, b: a > b, [], True)

    kv_type = BF16 if replicas == 1 else F32

    def keys_of(s):
        return pl.pallas_call(
            functools.partial(key_kernel, part),
            out_shape=[jax.ShapeDtypeStruct((tok, 2 * hd), kv_type)] * part + [gm_shape],
            grid=grid,
            in_specs=[in_smem] + kv_specs(s) + [map_spec(s), ext_spec, dk_spec, dv_spec],
            out_specs=piece_specs(lambda h: (0, 0), 2) + [gm_spec],
            scratch_shapes=[
                pltpu.VMEM((BLK, hd), BF16),
                pltpu.VMEM((BLK, hd), BF16),
                pltpu.VMEM((hd, BLK), BF16),
                pltpu.VMEM((hd, BLK), F32),
                pltpu.VMEM((heads * half, BLK), BF16),
                pltpu.VMEM((heads * half, hd), BF16),
                pltpu.VMEM((BLK, 2 * hd), F32),
            ],
            compiler_params=params,
            cost_estimate=pl.CostEstimate(
                flops=unit * 4 * hd, bytes_accessed=4 * heads * BLK * hd, transcendentals=0
            ),
            name="keys",
        )(offsets, *kv, *kv, maps, suffix[s], blocks[s][1], blocks[s][2])

    def returned(pieces):
        return [pieces[0]] + [within(pieces[r], -r) for r in shifts[1:]]

    def fold(parts):
        stacked = jnp.stack([parts[s] for s in slots])
        pieces = stacked.reshape(grp, heads // PAIR, fsdp, map_rows, PAIR * half)

        def rows_for(device):
            return lax.dynamic_index_in_dim(pieces, device, 2, keepdims=False)

        summed = rows_for(seq).astype(F32)
        for r in range(1, fsdp):
            summed = summed + along(rows_for((seq + r) % fsdp), r).astype(F32)
        sent = summed.astype(BF16)
        result = summed[0]
        for s in slots[1:]:
            result = result + across(sent[s], s).astype(F32)
        result = result.reshape(heads // PAIR, map_rows, PAIR, half)
        return jnp.swapaxes(result, 1, 2).reshape(heads, map_rows, half)

    table = ints([owner(r, s) for s in order for r in shifts])
    back = [piece for s in order for piece in returned(blocks[s][0])]
    (grad_queries,) = unpack(table, back, 1, heads * hd)
    query_map_grad = fold({s: blocks[s][4] for s in slots})

    keys = {s: keys_of(s) for s in slots}
    back = [piece for s in order for piece in returned(keys[s][:part])]
    grad_keys, grad_values = unpack(table, back, 2, hd)
    if replicas > 1:
        grad_keys, grad_values = (
            jnp.sum(a.reshape(tok, kv_heads, replicas, hd), axis=2)
            .astype(BF16)
            .reshape(tok, kv_heads * hd)
            for a in (grad_keys, grad_values)
        )
    key_map_grad = fold({s: keys[s][part] for s in slots})
    return grad_queries, grad_keys, grad_values, query_map_grad, key_map_grad, grad_prefix


def solution(mesh):
    rows, maps = P(("fsdp", "ctx"), None), P("ctx", "fsdp", None)
    return jax.shard_map(
        shards,
        mesh=mesh,
        in_specs=(rows,) * 4 + (maps, maps, P("ctx", None, None), P("ctx", None)),
        out_specs=(rows,) * 3 + (maps,) * 3,
        check_vma=False,
    )
```

profile of v0, /device:TPU:1, one launch (start us, length us, event | category | flops | bytes accessed | tf_op | source)
XLA Modules:
  0.0 400.7 jit_solution(11375433114796025981)
XLA Ops:
  1.4 17.8 %pack.3 = (bf16[128,512]{1,0:T(8,128)(2,1)}, bf16[128,512]{1,0:T(8,128)(2,1)}, bf16[128,512]{1,0:T(8,128)(2,1)}, bf16[128,512]{1,0:T(8,128)(2,1)}) custom-call(s32[8]{0:T(128)} %stack.172.table, bf16[128,1024]{1,0:T(8,128)(2,1)} %refs_0_.3, bf16[128,1024]{1,0:T(8,128)(2,1)} %refs_1_.3), custom_call_target="tpu_custom_call" | custom-call | bytes 1048576 | tf_op jit(solution)/shard_map/pack/pallas_call | solution.py:112
  27.7 65.5 %pack.5 = (bf16[128,2048]{1,0:T(8,128)(2,1)}, bf16[128,2048]{1,0:T(8,128)(2,1)}, bf16[128,2048]{1,0:T(8,128)(2,1)}, bf16[128,2048]{1,0:T(8,128)(2,1)}) custom-call(s32[4]{0:T(128)} %get-tuple-element.107.table, bf16[128,8192]{1,0:T(8,128)(2,1)} %refs_0_.5, bf16[128,8192]{1,0:T(8,128)(2,1)} %refs_1_.5), custom_call_target="tpu_custom_call" | custom-call | bytes 4194304 | tf_op jit(solution)/shard_map/pack/pallas_call | solution.py:112
  93.8 9.1 %all-gather = bf16[8,8,32,128]{3,2,1,0:T(8,128)(2,1)S(1)} all-gather(bf16[2,8,32,128]{3,2,1,0:T(8,128)(2,1)S(1)} %pad_maximum_fusion), channel_id=2, replica_groups=mesh['ctx'=8,'fsdp'=4] {'fsdp'}, dimensions={0}, use_global_device_ids=true | all-gather | bytes 655360 | tf_op jit(solution)/shard_map/all_gather | solution.py:389
  102.9 3.5 states.3
  106.6 3.5 states.2.refs_0_
  110.0 12.6 %collective-permute-done.7.refs_1_ = bf16[8,144,128]{2,1,0:T(8,128)(2,1)S(1)} collective-permute-done((bf16[8,144,128]{2,1,0:T(8,128)(2,1)S(1)}, bf16[8,144,128]{2,1,0:T(8,128)(2,1)S(1)}, u32[]{:S(2)}, u32[]{:S(2)}) %collective-permute-start.7) | collective-permute-done | bytes 294944 | tf_op jit(solution)/shard_map/ppermute | solution.py:369
  127.6 65.5 %pack.4 = (bf16[128,2048]{1,0:T(8,128)(2,1)}, bf16[128,2048]{1,0:T(8,128)(2,1)}, bf16[128,2048]{1,0:T(8,128)(2,1)}, bf16[128,2048]{1,0:T(8,128)(2,1)}) custom-call(s32[4]{0:T(128)} %get-tuple-element.106.table, bf16[128,8192]{1,0:T(8,128)(2,1)} %refs_0_.5, bf16[128,8192]{1,0:T(8,128)(2,1)} %refs_1_.5), custom_call_target="tpu_custom_call" | custom-call | bytes 4194304 | tf_op jit(solution)/shard_map/pack/pallas_call | solution.py:112
  200.1 15.1 %blocks.3 = (bf16[128,1024]{1,0:T(8,128)(2,1)S(1)}, bf16[128,1024]{1,0:T(8,128)(2,1)S(1)}, bf16[128,1024]{1,0:T(8,128)(2,1)S(1)}, bf16[128,1024]{1,0:T(8,128)(2,...) custom-call(s32[4]{0:T(128)S(1)} %pad_add_fusion.4.offsets, ...), custom_call_target="tpu_custom_call" | custom-call | flops 4294967296 | bytes 8388608 | tf_op jit(solution)/shard_map/blocks/pallas_call | solution.py:465
  221.0 15.0 %blocks.2 = (bf16[128,1024]{1,0:T(8,128)(2,1)S(1)}, bf16[128,1024]{1,0:T(8,128)(2,1)S(1)}, bf16[128,1024]{1,0:T(8,128)(2,1)S(1)}, bf16[128,1024]{1,0:T(8,128)(2,...) custom-call(s32[4]{0:T(128)S(1)} %pad_add_fusion.4.offsets, ...), custom_call_target="tpu_custom_call" | custom-call | flops 4294967296 | bytes 8388608 | tf_op jit(solution)/shard_map/blocks/pallas_call | solution.py:465
  237.4 3.2 collective-permute-start.21
  240.6 3.0 collective-permute-start.34
  247.4 6.0 %collective-permute-done.21.refs_1_ = bf16[8,144,128]{2,1,0:T(8,128)(2,1)S(1)} collective-permute-done((bf16[8,144,128]{2,1,0:T(8,128)(2,1)S(1)}, bf16[8,144,128]{2,1,0:T(8,128)(2,1)S(1)}, u32[]{:S(2)}, u32[]{:S(2)}) %collective-permute-start.21) | collective-permute-done | bytes 294944 | tf_op jit(solution)/shard_map/ppermute | solution.py:369
  256.6 4.8 %collective-permute-done.22.refs_2_ = bf16[8,144,128]{2,1,0:T(8,128)(2,1)S(1)} collective-permute-done((bf16[8,144,128]{2,1,0:T(8,128)(2,1)S(1)}, bf16[8,144,128]{2,1,0:T(8,128)(2,1)S(1)}, u32[]{:S(2)}, u32[]{:S(2)}) %collective-permute-start.22) | collective-permute-done | bytes 294944 | tf_op jit(solution)/shard_map/ppermute | solution.py:372
  261.3 8.0 %collective-permute-done.23.refs_3_ = bf16[8,144,128]{2,1,0:T(8,128)(2,1)S(1)} collective-permute-done((bf16[8,144,128]{2,1,0:T(8,128)(2,1)S(1)}, bf16[8,144,128]{2,1,0:T(8,128)(2,1)S(1)}, u32[]{:S(2)}, u32[]{:S(2)}) %collective-permute-start.23) | collective-permute-done | bytes 294944 | tf_op jit(solution)/shard_map/ppermute | solution.py:372
  273.3 3.5 collective-permute-start.18
  279.8 4.8 %keys.3 = (bf16[128,256]{1,0:T(8,128)(2,1)S(1)}, bf16[128,256]{1,0:T(8,128)(2,1)S(1)}, bf16[128,256]{1,0:T(8,128)(2,1)S(1)}, bf16[128,256]{1,0:T(8,128)(2,1)S(1)}, bf16[4,128,128]{2,1,0:T(8,128)(2,1)S(1)}) custom-call(s32[4]{0:T(128)S(1)} %pad_add_fusion.4.offsets, bf16[128,512]{1,0:T(8,128)(2,1)S(1)} %copy-done, ...), custom_call_target="tpu_custom_call" | custom-call | flops 536870912 | bytes 2097152 | tf_op jit(solution)/shard_map/keys/pallas_call | solution.py:502
  286.5 4.8 %keys.2 = (bf16[128,256]{1,0:T(8,128)(2,1)S(1)}, bf16[128,256]{1,0:T(8,128)(2,1)S(1)}, bf16[128,256]{1,0:T(8,128)(2,1)S(1)}, bf16[128,256]{1,0:T(8,128)(2,1)S(1)}, bf16[4,128,128]{2,1,0:T(8,128)(2,1)S(1)}) custom-call(s32[4]{0:T(128)S(1)} %pad_add_fusion.4.offsets, bf16[128,512]{1,0:T(8,128)(2,1)S(1)} %copy-done, ...), custom_call_target="tpu_custom_call" | custom-call | flops 536870912 | bytes 2097152 | tf_op jit(solution)/shard_map/keys/pallas_call | solution.py:502
  297.0 2.4 collective-permute-start.13
  299.5 2.4 collective-permute-start.29
  302.0 4.6 %collective-permute-done.12.refs_1_ = bf16[128,1024]{1,0:T(8,128)(2,1)S(1)} collective-permute-done((bf16[128,1024]{1,0:T(8,128)(2,1)S(1)}, bf16[128,1024]{1,0:T(8,128)(2,1)S(1)}, u32[]{:S(2)}, u32[]{:S(2)}) %collective-permute-start.12) | collective-permute-done | bytes 262176 | tf_op jit(solution)/shard_map/ppermute | solution.py:364
  307.2 4.4 %collective-permute-done.13.refs_2_ = bf16[128,1024]{1,0:T(8,128)(2,1)S(1)} collective-permute-done((bf16[128,1024]{1,0:T(8,128)(2,1)S(1)}, bf16[128,1024]{1,0:T(8,128)(2,1)S(1)}, u32[]{:S(2)}, u32[]{:S(2)}) %collective-permute-start.13) | collective-permute-done | bytes 262176 | tf_op jit(solution)/shard_map/ppermute | solution.py:364
  311.7 2.5 collective-permute-start.28
  316.0 65.4 %unpack.2 = bf16[128,8192]{1,0:T(8,128)(2,1)} custom-call(s32[8]{0:T(128)} %stack.166.table, bf16[128,1024]{1,0:T(8,128)(2,1)} %copy-done.7, bf16[128,1024]{1,0:T(8,128)(2,1)} %copy-done.32, bf16[128,1024]{1,0:T(8,128)(2,1)} %copy-done.33, bf16[128,1024]{1,0:T(8,128)(2,1)} %copy-done.34, bf16[128,1024]{1,0:T(8,128)(2,1)} %copy-done.6, ...), custom_call_target="tpu_custom_call" | custom-call | bytes 4194304 | tf_op jit(solution)/shard_map/unpack/pallas_call | solution.py:148
  382.1 17.8 %unpack.3 = (bf16[128,1024]{1,0:T(8,128)(2,1)}, bf16[128,1024]{1,0:T(8,128)(2,1)}) custom-call(s32[8]{0:T(128)} %stack.166.table, bf16[128,256]{1,0:T(8,128)(2,1)} %copy-done.13, bf16[128,256]{1,0:T(8,128)(2,1)} %copy-done.40, bf16[128,256]{1,0:T(8,128)(2,1)} %copy-done.41, bf16[128,256]{1,0:T(8,128)(2,1)} %copy-done.42, bf16[128,256]{1,0:T(8,128)(2,1)} %copy-done.12, ...), custom_call_target="tpu_custom_call" | custom-call | bytes 1048576 | tf_op jit(solution)/shard_map/unpack/pallas_call | solution.py:148
  (181 shorter events, 54.4 us)
Async XLA Ops:
  19.2 83.8 %collective-permute-start = (bf16[128,512]{1,0:T(8,128)(2,1)}, bf16[128,512]{1,0:T(8,128)(2,1)S(1)}, u32[]{:S(2)}, u32[]{:S(2)}) collective-permute-start(bf16[128,512]{1,0:T(8,128)(2,1)} %get-tuple-element.52), channel_id=1, source_target_pairs={{0,4},{4,8},{8,12},{12,0},{16,20},{20,24},{24,28},{28,16},{1,5},{5... | collective-permute-start | bytes 393224 | tf_op jit(solution)/shard_map/ppermute | solution.py:364
  21.3 81.6 %collective-permute-start.1 = (bf16[128,512]{1,0:T(8,128)(2,1)}, bf16[128,512]{1,0:T(8,128)(2,1)S(1)}, u32[]{:S(2)}, u32[]{:S(2)}) collective-permute-start(bf16[128,512]{1,0:T(8,128)(2,1)} %get-tuple-element.53), channel_id=1, source_target_pairs={{0,8},{4,12},{8,0},{12,4},{16,24},{20,28},{24,16},{28,20},{1,9},{5... | collective-permute-start | bytes 393224 | tf_op jit(solution)/shard_map/ppermute | solution.py:364
  22.6 80.4 %collective-permute-start.2 = (bf16[128,512]{1,0:T(8,128)(2,1)}, bf16[128,512]{1,0:T(8,128)(2,1)S(1)}, u32[]{:S(2)}, u32[]{:S(2)}) collective-permute-start(bf16[128,512]{1,0:T(8,128)(2,1)} %get-tuple-element.54), channel_id=1, source_target_pairs={{0,12},{4,0},{8,4},{12,8},{16,28},{20,16},{24,20},{28,24},{1,13},{... | collective-permute-start | bytes 393224 | tf_op jit(solution)/shard_map/ppermute | solution.py:364
  24.7 69.1 %collective-permute-start.6 = (bf16[8,32,128]{2,1,0:T(8,128)(2,1)S(1)}, bf16[8,32,128]{2,1,0:T(8,128)(2,1)S(1)}, u32[]{:S(2)}, u32[]{:S(2)}) collective-permute-start(bf16[8,32,128]{2,1,0:T(8,128)(2,1)S(1)} %pad_maximum_fusion.3), channel_id=1, source_target_pairs={{0,16},{4,20},{8,24},{12,28},{16,0},{20,4},{24,8},{28,12},{1,17},{... | collective-permute-start | bytes 196616 | tf_op jit(solution)/shard_map/ppermute | solution.py:369
  93.2 31.3 %collective-permute-start.15 = (bf16[128,2048]{1,0:T(8,128)(2,1)}, bf16[128,2048]{1,0:T(8,128)(2,1)S(1)}, u32[]{:S(2)}, u32[]{:S(2)}) collective-permute-start(bf16[128,2048]{1,0:T(8,128)(2,1)} %get-tuple-element.65), channel_id=1, source_target_pairs={{0,4},{4,8},{8,12},{12,0},{16,20},{20,24},{24,28},{28,16},{1,5},{5... | collective-permute-start | bytes 1572872 | tf_op jit(solution)/shard_map/ppermute | solution.py:364
  106.4 16.1 %collective-permute-start.7 = (bf16[8,144,128]{2,1,0:T(8,128)(2,1)S(1)}, bf16[8,144,128]{2,1,0:T(8,128)(2,1)S(1)}, u32[]{:S(2)}, u32[]{:S(2)}) collective-permute-start(bf16[8,144,128]{2,1,0:T(8,128)(2,1)S(1)} %states.3), channel_id=1, source_target_pairs={{0,16},{4,20},{8,24},{12,28},{16,0},{20,4},{24,8},{28,12},{1,17},{... | collective-permute-start | bytes 884744 | tf_op jit(solution)/shard_map/ppermute | solution.py:369
  122.7 70.5 %collective-permute-start.8 = (bf16[8,144,128]{2,1,0:T(8,128)(2,1)S(1)}, bf16[8,144,128]{2,1,0:T(8,128)(2,1)S(1)}, u32[]{:S(2)}, u32[]{:S(2)}) collective-permute-start(bf16[8,144,128]{2,1,0:T(8,128)(2,1)S(1)} %totals.2), channel_id=1, source_target_pairs={{0,1},{1,2},{2,3},{3,0},{4,5},{5,6},{6,7},{7,4},{8,9},{9,10},{10,1... | collective-permute-start | bytes 884744 | tf_op jit(solution)/shard_map/ppermute | solution.py:372
  123.6 69.6 %collective-permute-start.9 = (bf16[8,144,128]{2,1,0:T(8,128)(2,1)S(1)}, bf16[8,144,128]{2,1,0:T(8,128)(2,1)S(1)}, u32[]{:S(2)}, u32[]{:S(2)}) collective-permute-start(bf16[8,144,128]{2,1,0:T(8,128)(2,1)S(1)} %totals.2), channel_id=1, source_target_pairs={{0,2},{1,3},{2,0},{3,1},{4,6},{5,7},{6,4},{7,5},{8,10},{9,11},{10,... | collective-permute-start | bytes 884744 | tf_op jit(solution)/shard_map/ppermute | solution.py:372
  124.5 69.3 %collective-permute-start.10 = (bf16[8,144,128]{2,1,0:T(8,128)(2,1)S(1)}, bf16[8,144,128]{2,1,0:T(8,128)(2,1)S(1)}, u32[]{:S(2)}, u32[]{:S(2)}) collective-permute-start(bf16[8,144,128]{2,1,0:T(8,128)(2,1)S(1)} %totals.2), channel_id=1, source_target_pairs={{0,3},{1,0},{2,1},{3,2},{4,7},{5,4},{6,5},{7,6},{8,11},{9,8},{10,9... | collective-permute-start | bytes 884744 | tf_op jit(solution)/shard_map/ppermute | solution.py:372
  124.5 72.2 %collective-permute-start.16 = (bf16[128,2048]{1,0:T(8,128)(2,1)}, bf16[128,2048]{1,0:T(8,128)(2,1)}, u32[]{:S(2)}, u32[]{:S(2)}) collective-permute-start(bf16[128,2048]{1,0:T(8,128)(2,1)} %get-tuple-element.66), channel_id=1, source_target_pairs={{0,8},{4,12},{8,0},{12,4},{16,24},{20,28},{24,16},{28,20},{1,9},{5... | collective-permute-start | bytes 1572872 | tf_op jit(solution)/shard_map/ppermute | solution.py:364
  125.3 72.7 %collective-permute-start.17 = (bf16[128,2048]{1,0:T(8,128)(2,1)}, bf16[128,2048]{1,0:T(8,128)(2,1)}, u32[]{:S(2)}, u32[]{:S(2)}) collective-permute-start(bf16[128,2048]{1,0:T(8,128)(2,1)} %get-tuple-element.67), channel_id=1, source_target_pairs={{0,12},{4,0},{8,4},{12,8},{16,28},{20,16},{24,20},{28,24},{1,13},{... | collective-permute-start | bytes 1572872 | tf_op jit(solution)/shard_map/ppermute | solution.py:364
  193.1 25.6 %collective-permute-start.3 = (bf16[128,2048]{1,0:T(8,128)(2,1)}, bf16[128,2048]{1,0:T(8,128)(2,1)}, u32[]{:S(2)}, u32[]{:S(2)}) collective-permute-start(bf16[128,2048]{1,0:T(8,128)(2,1)} %get-tuple-element.56), channel_id=1, source_target_pairs={{0,4},{4,8},{8,12},{12,0},{16,20},{20,24},{24,28},{28,16},{1,5},{5... | collective-permute-start | bytes 1572872 | tf_op jit(solution)/shard_map/ppermute | solution.py:364
  193.2 25.5 %collective-permute-start.4 = (bf16[128,2048]{1,0:T(8,128)(2,1)}, bf16[128,2048]{1,0:T(8,128)(2,1)}, u32[]{:S(2)}, u32[]{:S(2)}) collective-permute-start(bf16[128,2048]{1,0:T(8,128)(2,1)} %get-tuple-element.57), channel_id=1, source_target_pairs={{0,8},{4,12},{8,0},{12,4},{16,24},{20,28},{24,16},{28,20},{1,9},{5... | collective-permute-start | bytes 1572872 | tf_op jit(solution)/shard_map/ppermute | solution.py:364
  193.8 25.7 %collective-permute-start.5 = (bf16[128,2048]{1,0:T(8,128)(2,1)}, bf16[128,2048]{1,0:T(8,128)(2,1)}, u32[]{:S(2)}, u32[]{:S(2)}) collective-permute-start(bf16[128,2048]{1,0:T(8,128)(2,1)} %get-tuple-element.58), channel_id=1, source_target_pairs={{0,12},{4,0},{8,4},{12,8},{16,28},{20,16},{24,20},{28,24},{1,13},{... | collective-permute-start | bytes 1572872 | tf_op jit(solution)/shard_map/ppermute | solution.py:364
  196.8 24.3 %collective-permute-start.11 = (bf16[8,144,128]{2,1,0:T(8,128)(2,1)S(1)}, bf16[8,144,128]{2,1,0:T(8,128)(2,1)S(1)}, u32[]{:S(2)}, u32[]{:S(2)}) collective-permute-start(bf16[8,144,128]{2,1,0:T(8,128)(2,1)S(1)} %get-tuple-element.59), channel_id=1, source_target_pairs={{0,16},{4,20},{8,24},{12,28},{16,0},{20,4},{24,8},{28,12},{1,17},{... | collective-permute-start | bytes 884744 | tf_op jit(solution)/shard_map/ppermute | solution.py:369
  256.4 20.6 %collective-permute-start.35 = (bf16[4,32,128]{2,1,0:T(8,128)(2,1)S(1)}, bf16[4,32,128]{2,1,0:T(8,128)(2,1)S(1)}, u32[]{:S(2)}, u32[]{:S(2)}) collective-permute-start(bf16[4,32,128]{2,1,0:T(8,128)(2,1)S(1)} %fusion.22), channel_id=1, source_target_pairs={{0,16},{4,20},{8,24},{12,28},{16,0},{20,4},{24,8},{28,12},{1,17},{... | collective-permute-start | bytes 98312 | tf_op jit(solution)/shard_map/ppermute | solution.py:369
  273.3 19.9 %collective-permute-start.18 = (bf16[128,1024]{1,0:T(8,128)(2,1)}, bf16[128,1024]{1,0:T(8,128)(2,1)S(1)}, u32[]{:S(2)}, u32[]{:S(2)}) collective-permute-start(bf16[128,1024]{1,0:T(8,128)(2,1)} %copy-done.27), channel_id=1, source_target_pairs={{0,12},{4,0},{8,4},{12,8},{16,28},{20,16},{24,20},{28,24},{1,13},{... | collective-permute-start | bytes 786440 | tf_op jit(solution)/shard_map/ppermute | solution.py:364
  276.7 22.7 %collective-permute-start.19 = (bf16[128,1024]{1,0:T(8,128)(2,1)}, bf16[128,1024]{1,0:T(8,128)(2,1)S(1)}, u32[]{:S(2)}, u32[]{:S(2)}) collective-permute-start(bf16[128,1024]{1,0:T(8,128)(2,1)} %copy-done.22), channel_id=1, source_target_pairs={{0,8},{4,12},{8,0},{12,4},{16,24},{20,28},{24,16},{28,20},{1,9},{5... | collective-permute-start | bytes 786440 | tf_op jit(solution)/shard_map/ppermute | solution.py:364
  276.7 25.2 %collective-permute-start.20 = (bf16[128,1024]{1,0:T(8,128)(2,1)}, bf16[128,1024]{1,0:T(8,128)(2,1)S(1)}, u32[]{:S(2)}, u32[]{:S(2)}) collective-permute-start(bf16[128,1024]{1,0:T(8,128)(2,1)} %copy-done.19), channel_id=1, source_target_pairs={{0,4},{4,8},{8,12},{12,0},{16,20},{20,24},{24,28},{28,16},{1,5},{5... | collective-permute-start | bytes 786440 | tf_op jit(solution)/shard_map/ppermute | solution.py:364
  306.6 74.8 %collective-permute-start.31 = (bf16[128,256]{1,0:T(8,128)(2,1)S(1)}, bf16[128,256]{1,0:T(8,128)(2,1)S(1)}, u32[]{:S(2)}, u32[]{:S(2)}) collective-permute-start(bf16[128,256]{1,0:T(8,128)(2,1)S(1)} %get-tuple-element.88), channel_id=1, source_target_pairs={{0,4},{4,8},{8,12},{12,0},{16,20},{20,24},{24,28},{28,16},{1,5},{5... | collective-permute-start | bytes 196616 | tf_op jit(solution)/shard_map/ppermute | solution.py:364
  311.6 69.8 %collective-permute-start.26 = (bf16[128,256]{1,0:T(8,128)(2,1)S(1)}, bf16[128,256]{1,0:T(8,128)(2,1)S(1)}, u32[]{:S(2)}, u32[]{:S(2)}) collective-permute-start(bf16[128,256]{1,0:T(8,128)(2,1)S(1)} %get-tuple-element.79), channel_id=1, source_target_pairs={{0,12},{4,0},{8,4},{12,8},{16,28},{20,16},{24,20},{28,24},{1,13},{... | collective-permute-start | bytes 196616 | tf_op jit(solution)/shard_map/ppermute | solution.py:364
  311.6 69.8 %collective-permute-start.27 = (bf16[128,256]{1,0:T(8,128)(2,1)S(1)}, bf16[128,256]{1,0:T(8,128)(2,1)S(1)}, u32[]{:S(2)}, u32[]{:S(2)}) collective-permute-start(bf16[128,256]{1,0:T(8,128)(2,1)S(1)} %get-tuple-element.80), channel_id=1, source_target_pairs={{0,8},{4,12},{8,0},{12,4},{16,24},{20,28},{24,16},{28,20},{1,9},{5... | collective-permute-start | bytes 196616 | tf_op jit(solution)/shard_map/ppermute | solution.py:364
  311.7 69.7 %collective-permute-start.28 = (bf16[128,256]{1,0:T(8,128)(2,1)S(1)}, bf16[128,256]{1,0:T(8,128)(2,1)S(1)}, u32[]{:S(2)}, u32[]{:S(2)}) collective-permute-start(bf16[128,256]{1,0:T(8,128)(2,1)S(1)} %get-tuple-element.81), channel_id=1, source_target_pairs={{0,4},{4,8},{8,12},{12,0},{16,20},{20,24},{24,28},{28,16},{1,5},{5... | collective-permute-start | bytes 196616 | tf_op jit(solution)/shard_map/ppermute | solution.py:364
  314.4 85.5 %collective-permute-start.39 = (bf16[4,32,128]{2,1,0:T(8,128)(2,1)S(1)}, bf16[4,32,128]{2,1,0:T(8,128)(2,1)S(1)}, u32[]{:S(2)}, u32[]{:S(2)}) collective-permute-start(bf16[4,32,128]{2,1,0:T(8,128)(2,1)S(1)} %fusion.23), channel_id=1, source_target_pairs={{0,16},{4,20},{8,24},{12,28},{16,0},{20,4},{24,8},{28,12},{1,17},{... | collective-permute-start | bytes 98312 | tf_op jit(solution)/shard_map/ppermute | solution.py:369
  (59 other events, 990.4 us)
where the time goes:
time: 403 us; the launch traced here: 401 us
  Pallas kernels  281 us (70%)
  waiting for transfers between devices  47.6 us (12%)
  starting transfers between devices  43.7 us (11%)
  local copies, waits for them, and re-layouts  13.1 us (3%)
  blocking collectives  9.08 us (2%)
  other arithmetic  4.44 us (1%)
    pallas_call x3, Pallas kernels, pack(): pl.pallas_call(functools.partial(pack_kernel, columns, len(sources), widt...  149 us
    pallas_call x2, Pallas kernels, unpack(): pl.pallas_call(functools.partial(unpack_kernel, outputs, width), out_shap...  83.2 us
    pallas_call x2, Pallas kernels, block_of(): pl.pallas_call(functools.partial(block_kernel, part), out_shape=[jax.Shap...  30.1 us
    ppermute x21, starting transfers between devices, within(): lax.ppermute(array, 'ctx', [(d, d // part * part + (d + shift) % part) fo...  22.9 us
    ppermute x7, waiting for transfers between devices, across(): lax.ppermute(array, 'ctx', [(d, (d + shift * part) % ctx) for d in range(...  21.4 us
    ppermute x12, waiting for transfers between devices, along(): lax.ppermute(array, 'fsdp', [(d, (d + shift) % fsdp) for d in range(fsdp)])  16.1 us
    ppermute x12, starting transfers between devices, along(): lax.ppermute(array, 'fsdp', [(d, (d + shift) % fsdp) for d in range(fsdp)])  12.8 us
    unnamed x86, local copies, waits for them, and re-layouts  11.7 us
  transfers between devices with their start and end apart: 40, of which 14 were waited for; matrix products, arithmetic and copies ran while one was open for 1% of the time, Pallas kernels for 62%

commit v1 on v0

--- a/solution.py
+++ b/solution.py
@@ -85,73 +85,65 @@
         ref[...] = source[pl.ds(pl.multiple_of(offsets[r], rows), rows), :].astype(ref.dtype)
 
 
-def pack_kernel(columns, inputs, width, table, *refs):
-    sources, outs, sems = refs[:inputs], refs[inputs:-1], refs[-1]
-    copies = []
-    for r, out in enumerate(outs):
-        for s in range(columns):
-            at = pl.multiple_of(table[r * columns + s] * width, width)
-            for i, source in enumerate(sources):
-                to = (s * inputs + i) * width
-                copies.append(
-                    pltpu.make_async_copy(
-                        source.at[:, pl.ds(at, width)],
-                        out.at[:, pl.ds(to, width)],
-                        sems.at[len(copies)],
-                    )
-                )
-    for copy in copies:
-        copy.start()
-    for copy in copies:
-        copy.wait()
+def pack_kernel(columns, inputs, table, *refs):
+    count = columns * inputs
+    for r, out in enumerate(refs[-(len(refs) // (count + 1)) :]):
+        width = out.shape[1] // count
+        for i in range(count):
+            out[:, i * width : (i + 1) * width] = refs[r * count + i][...]
 
 
 def pack(table, sources, pieces, columns, width):
     rows = sources[0].shape[0]
-    total = columns * len(sources) * width
+    count = columns * len(sources)
+    step = rows // 2
+
+    def take(at):
+        return pl.BlockSpec((step, width), lambda i, t: (i, t[at]))
+
     return pl.pallas_call(
-        functools.partial(pack_kernel, columns, len(sources), width),
-        out_shape=[jax.ShapeDtypeStruct((rows, total), sources[0].dtype)] * pieces,
-        in_specs=[pl.BlockSpec(memory_space=SMEM)]
-        + [pl.BlockSpec(memory_space=pl.ANY)] * len(sources),
-        out_specs=[pl.BlockSpec(memory_space=pl.ANY)] * pieces,
-        scratch_shapes=[pltpu.SemaphoreType.DMA((pieces * columns * len(sources),))],
+        functools.partial(pack_kernel, columns, len(sources)),
+        out_shape=[jax.ShapeDtypeStruct((rows, count * width), sources[0].dtype)] * pieces,
+        grid_spec=pltpu.PrefetchScalarGridSpec(
+            num_scalar_prefetch=1,
+            grid=(rows // step,),
+            in_specs=[
+                take(r * columns + s)
+                for r in range(pieces)
+                for s in range(columns)
+                for _ in sources
+            ],
+            out_specs=[pl.BlockSpec((step, count * width), lambda i, t: (i, 0))] * pieces,
+        ),
+        compiler_params=pltpu.CompilerParams(vmem_limit_bytes=LIMIT),
         cost_estimate=pl.CostEstimate(
-            flops=0, bytes_accessed=4 * pieces * rows * total, transcendentals=0
+            flops=0, bytes_accessed=4 * pieces * rows * count * width, transcendentals=0
         ),
         name="pack",
-    )(table, *sources)
-
-
-def unpack_kernel(outputs, width, table, *refs):
-    pieces, outs, sems = refs[: -outputs - 1], refs[-outputs - 1 : -1], refs[-1]
-    copies = []
+    )(table, *(list(sources) * (pieces * columns)))
+
+
+def unpack_kernel(outputs, table, *refs):
+    pieces, outs = refs[:-outputs], refs[-outputs:]
     for r, piece in enumerate(pieces):
-        at = pl.multiple_of(table[r] * width, width)
+        width = piece.shape[1] // outputs
+        at = pl.ds(pl.multiple_of(table[r] * width, width), width)
         for i, out in enumerate(outs):
-            copies.append(
-                pltpu.make_async_copy(
-                    piece.at[:, pl.ds(i * width, width)],
-                    out.at[:, pl.ds(at, width)],
-                    sems.at[len(copies)],
-                )
-            )
-    for copy in copies:
-        copy.start()
-    for copy in copies:
-        copy.wait()
+            out[:, at] = piece[:, i * width : (i + 1) * width]
 
 
 def unpack(table, pieces, outputs, width):
     rows = pieces[0].shape[0]
     total = len(pieces) * width
+    step = rows // 2
     return pl.pallas_call(
-        functools.partial(unpack_kernel, outputs, width),
+        functools.partial(unpack_kernel, outputs),
         out_shape=[jax.ShapeDtypeStruct((rows, total), pieces[0].dtype)] * outputs,
+        grid=(rows // step,),
         in_specs=[pl.BlockSpec(memory_space=SMEM)]
-        + [pl.BlockSpec(memory_space=pl.ANY)] * len(pieces),
-        out_specs=[pl.BlockSpec(memory_space=pl.ANY)] * outputs,
-        scratch_shapes=[pltpu.SemaphoreType.DMA((len(pieces) * outputs,))],
+        + [pl.BlockSpec((step, outputs * width), lambda i: (i, 0))] * len(pieces),
+        out_specs=[pl.BlockSpec((step, total), lambda i: (i, 0))] * outputs,
+        compiler_params=pltpu.CompilerParams(vmem_limit_bytes=LIMIT),
         cost_estimate=pl.CostEstimate(
             flops=0, bytes_accessed=4 * rows * total * outputs, transcendentals=0
         ),

time: 403 us -> 201 us (0.50)
  Pallas kernels: 281 us -> 60.1 us
  waiting for transfers between devices: 47.6 us -> 65.5 us
    pallas_call x5, Pallas kernels: 232 us -> 9.33 us  [the longest x3 5.96 us: pack(): pl.pallas_call(functools.partial(pack_kernel, columns, len(sources)), out...]
    ppermute x12, waiting for transfers between devices: 16.1 us -> 23.6 us  [along(): lax.ppermute(array, 'fsdp', [(d, (d + shift) % fsdp) for d in range(fsdp)])]
    ppermute x7, waiting for transfers between devices: 21.4 us -> 27.8 us  [across(): lax.ppermute(array, 'ctx', [(d, (d + shift * part) % ctx) for d in range(...]
    unnamed x86 -> x74, local copies, waits for them, and re-layouts: 11.7 us -> 16.4 us
    ppermute x21, waiting for transfers between devices: 10.1 us -> 14.2 us  [within(): lax.ppermute(array, 'ctx', [(d, d // part * part + (d + shift) % part) fo...]
  transfers between devices with their start and end apart: 40 -> 40, of which waited for: 14 -> 18; matrix products, arithmetic and copies ran while one was open for 1% -> 2% of each run, Pallas kernels for 62% -> 22%
where the time goes in v1:
time: 201 us; the launch traced here: 198 us
  waiting for transfers between devices  65.5 us (33%)
  Pallas kernels  60.1 us (30%)
  starting transfers between devices  40.5 us (20%)
  local copies, waits for them, and re-layouts  16.8 us (8%)
  blocking collectives  9.08 us (5%)
  other arithmetic  5.3 us (3%)
    pallas_call x2, Pallas kernels, block_of(): pl.pallas_call(functools.partial(block_kernel, part), out_shape=[jax.Shap...  30.1 us
    ppermute x7, waiting for transfers between devices, across(): lax.ppermute(array, 'ctx', [(d, (d + shift * part) % ctx) for d in range(...  27.8 us
    ppermute x12, waiting for transfers between devices, along(): lax.ppermute(array, 'fsdp', [(d, (d + shift) % fsdp) for d in range(fsdp)])  23.6 us
    ppermute x21, starting transfers between devices, within(): lax.ppermute(array, 'ctx', [(d, d // part * part + (d + shift) % part) fo...  21.9 us
    unnamed x74, local copies, waits for them, and re-layouts  16.4 us
    ppermute x21, waiting for transfers between devices, within(): lax.ppermute(array, 'ctx', [(d, d // part * part + (d + shift) % part) fo...  14.2 us
    ppermute x12, starting transfers between devices, along(): lax.ppermute(array, 'fsdp', [(d, (d + shift) % fsdp) for d in range(fsdp)])  12 us
    pallas_call x2, Pallas kernels, keys_of(): pl.pallas_call(functools.partial(key_kernel, part), out_shape=[jax.ShapeD...  9.51 us
  transfers between devices with their start and end apart: 40, of which 18 were waited for; matrix products, arithmetic and copies ran while one was open for 2% of the time, Pallas kernels for 22%

profile of v1, /device:TPU:1, one launch (start us, length us, event | category | flops | bytes accessed | tf_op | source)
XLA Modules:
  0.0 198.5 jit_solution(8402750910867220252)
XLA Ops:
  9.9 2.3 %collective-permute-start.6 = (bf16[8,32,128]{2,1,0:T(8,128)(2,1)}, bf16[8,32,128]{2,1,0:T(8,128)(2,1)}, u32[]{:S(2)}, u32[]{:S(2)}) collective-permute-start(bf16[8,32,128]{2,1,0:T(8,128)(2,1)} %pad_maximum_fusion.3), channel_id=1, source_target_pairs={{0,16},{4,20},{8,24},{12,28},{16,0},{20,4},{24,8},{28,12},{1,17},{... | collective-permute-start | bytes 196616 | tf_op jit(solution)/shard_map/ppermute | solution.py:361
  17.4 9.1 %all-gather = bf16[8,8,32,128]{3,2,1,0:T(8,128)(2,1)S(1)} all-gather(bf16[2,8,32,128]{3,2,1,0:T(8,128)(2,1)S(1)} %pad_maximum_fusion), channel_id=2, replica_groups=mesh['ctx'=8,'fsdp'=4] {'fsdp'}, dimensions={0}, use_global_device_ids=true | all-gather | bytes 655360 | tf_op jit(solution)/shard_map/all_gather | solution.py:381
  26.5 3.5 %states.3 = bf16[8,144,128]{2,1,0:T(8,128)(2,1)S(1)} custom-call(s32[4]{0:T(128)S(1)} %pad_add_fusion.4.offsets, bf16[128,512]{1,0:T(8,128)(2,1)S(1)} %get-tuple-element.51.refs_0_.refs_4_, bf16[128,512]{1,0:T(8,128)(2,1)S(1)} %collective-permute-done.refs_1_.refs_5_, bf16[128,512]{1,0:T(8,128)(2,1)S(1)} %collective-permute-done.1.refs_2_.refs_6_, ...), custom_call_target="tpu_custom_call" | custom-call | flops 268435456 | bytes 262144 | tf_op jit(solution)/shard_map/states/pallas_call | solution.py:413
  30.6 3.5 %states.2.refs_0_ = bf16[8,144,128]{2,1,0:T(8,128)(2,1)S(1)} custom-call(s32[4]{0:T(128)S(1)} %pad_add_fusion.4.offsets, bf16[128,512]{1,0:T(8,128)(2,1)S(1)} %get-tuple-element.51.refs_0_.refs_4_, bf16[128,512]{1,0:T(8,128)(2,1)S(1)} %collective-permute-done.refs_1_.refs_5_, bf16[128,512]{1,0:T(8,128)(2,1)S(1)} %collective-permute-done.1.refs_2_.refs_6_, ...), custom_call_target="tpu_custom_call" | custom-call | flops 268435456 | bytes 262144 | tf_op jit(solution)/shard_map/states/pallas_call | solution.py:413
  34.1 11.7 %collective-permute-done.7.refs_1_ = bf16[8,144,128]{2,1,0:T(8,128)(2,1)S(1)} collective-permute-done((bf16[8,144,128]{2,1,0:T(8,128)(2,1)S(1)}, bf16[8,144,128]{2,1,0:T(8,128)(2,1)S(1)}, u32[]{:S(2)}, u32[]{:S(2)}) %collective-permute-start.7) | collective-permute-done | bytes 294944 | tf_op jit(solution)/shard_map/ppermute | solution.py:361
  56.2 7.0 %collective-permute-done.9.refs_3_ = bf16[8,144,128]{2,1,0:T(8,128)(2,1)} collective-permute-done((bf16[8,144,128]{2,1,0:T(8,128)(2,1)}, bf16[8,144,128]{2,1,0:T(8,128)(2,1)}, u32[]{:S(2)}, u32[]{:S(2)}) %collective-permute-start.9) | collective-permute-done | bytes 294944 | tf_op jit(solution)/shard_map/ppermute | solution.py:364
  69.5 2.2 %collective-permute-done.17.refs_11_.refs_15_ = bf16[128,2048]{1,0:T(8,128)(2,1)} collective-permute-done((bf16[128,2048]{1,0:T(8,128)(2,1)}, bf16[128,2048]{1,0:T(8,128)(2,1)}, u32[]{:S(2)}, u32[]{:S(2)}) %collective-permute-start.17) | collective-permute-done | bytes 524320 | tf_op jit(solution)/shard_map/ppermute | solution.py:356
  72.8 15.1 %blocks.3 = (bf16[128,1024]{1,0:T(8,128)(2,1)S(1)}, bf16[128,1024]{1,0:T(8,128)(2,1)S(1)}, bf16[128,1024]{1,0:T(8,128)(2,1)S(1)}, bf16[128,1024]{1,0:T(8,128)(2,...) custom-call(s32[4]{0:T(128)S(1)} %pad_add_fusion.4.offsets, ...), custom_call_target="tpu_custom_call" | custom-call | flops 4294967296 | bytes 8388608 | tf_op jit(solution)/shard_map/blocks/pallas_call | solution.py:457
  91.4 2.8 %collective-permute-done.5.refs_11_.refs_15_ = bf16[128,2048]{1,0:T(8,128)(2,1)} collective-permute-done((bf16[128,2048]{1,0:T(8,128)(2,1)}, bf16[128,2048]{1,0:T(8,128)(2,1)}, u32[]{:S(2)}, u32[]{:S(2)}) %collective-permute-start.5) | collective-permute-done | bytes 524320 | tf_op jit(solution)/shard_map/ppermute | solution.py:356
  94.2 6.2 %collective-permute-done.11.refs_17_ = bf16[8,144,128]{2,1,0:T(8,128)(2,1)S(1)} collective-permute-done((bf16[8,144,128]{2,1,0:T(8,128)(2,1)S(1)}, bf16[8,144,128]{2,1,0:T(8,128)(2,1)S(1)}, u32[]{:S(2)}, u32[]{:S(2)}) %collective-permute-start.11) | collective-permute-done | bytes 294944 | tf_op jit(solution)/shard_map/ppermute | solution.py:361
  100.4 15.0 %blocks.2 = (bf16[128,1024]{1,0:T(8,128)(2,1)S(1)}, bf16[128,1024]{1,0:T(8,128)(2,1)S(1)}, bf16[128,1024]{1,0:T(8,128)(2,1)S(1)}, bf16[128,1024]{1,0:T(8,128)(2,...) custom-call(s32[4]{0:T(128)S(1)} %pad_add_fusion.4.offsets, ...), custom_call_target="tpu_custom_call" | custom-call | flops 4294967296 | bytes 8388608 | tf_op jit(solution)/shard_map/blocks/pallas_call | solution.py:457
  116.8 3.2 %collective-permute-start.21 = (bf16[8,144,128]{2,1,0:T(8,128)(2,1)S(1)}, bf16[8,144,128]{2,1,0:T(8,128)(2,1)S(1)}, u32[]{:S(2)}, u32[]{:S(2)}) collective-permute-start(bf16[8,144,128]{2,1,0:T(8,128)(2,1)S(1)} %get-tuple-element.74), channel_id=1, source_target_pairs={{0,16},{4,20},{8,24},{12,28},{16,0},{20,4},{24,8},{28,12},{1,17},{... | collective-permute-start | bytes 884744 | tf_op jit(solution)/shard_map/ppermute | solution.py:361
  125.6 7.3 %collective-permute-done.21.refs_1_ = bf16[8,144,128]{2,1,0:T(8,128)(2,1)S(1)} collective-permute-done((bf16[8,144,128]{2,1,0:T(8,128)(2,1)S(1)}, bf16[8,144,128]{2,1,0:T(8,128)(2,1)S(1)}, u32[]{:S(2)}, u32[]{:S(2)}) %collective-permute-start.21) | collective-permute-done | bytes 294944 | tf_op jit(solution)/shard_map/ppermute | solution.py:361
  136.0 4.7 %collective-permute-done.22.refs_2_ = bf16[8,144,128]{2,1,0:T(8,128)(2,1)S(1)} collective-permute-done((bf16[8,144,128]{2,1,0:T(8,128)(2,1)S(1)}, bf16[8,144,128]{2,1,0:T(8,128)(2,1)S(1)}, u32[]{:S(2)}, u32[]{:S(2)}) %collective-permute-start.22) | collective-permute-done | bytes 294944 | tf_op jit(solution)/shard_map/ppermute | solution.py:364
  140.7 8.1 %collective-permute-done.23.refs_3_ = bf16[8,144,128]{2,1,0:T(8,128)(2,1)S(1)} collective-permute-done((bf16[8,144,128]{2,1,0:T(8,128)(2,1)S(1)}, bf16[8,144,128]{2,1,0:T(8,128)(2,1)S(1)}, u32[]{:S(2)}, u32[]{:S(2)}) %collective-permute-start.23) | collective-permute-done | bytes 294944 | tf_op jit(solution)/shard_map/ppermute | solution.py:364
  152.1 3.3 %collective-permute-start.18 = (bf16[128,1024]{1,0:T(8,128)(2,1)}, bf16[128,1024]{1,0:T(8,128)(2,1)S(1)}, u32[]{:S(2)}, u32[]{:S(2)}) collective-permute-start(bf16[128,1024]{1,0:T(8,128)(2,1)} %copy-done.33), channel_id=1, source_target_pairs={{0,12},{4,0},{8,4},{12,8},{16,28},{20,16},{24,20},{28,24},{1,13},{... | collective-permute-start | bytes 786440 | tf_op jit(solution)/shard_map/ppermute | solution.py:356
  158.5 4.8 %keys.3 = (bf16[128,256]{1,0:T(8,128)(2,1)S(1)}, bf16[128,256]{1,0:T(8,128)(2,1)S(1)}, bf16[128,256]{1,0:T(8,128)(2,1)S(1)}, bf16[128,256]{1,0:T(8,128)(2,1)S(1)}, bf16[4,128,128]{2,1,0:T(8,128)(2,1)S(1)}) custom-call(s32[4]{0:T(128)S(1)} %pad_add_fusion.4.offsets, bf16[128,512]{1,0:T(8,128)(2,1)S(1)} %get-tuple-element.51.refs_0_.refs_4_, ...), custom_call_target="tpu_custom_call" | custom-call | flops 536870912 | bytes 2097152 | tf_op jit(solution)/shard_map/keys/pallas_call | solution.py:494
  163.2 2.5 %collective-permute-done.25.refs_9_ = bf16[8,144,128]{2,1,0:T(8,128)(2,1)S(1)} collective-permute-done((bf16[8,144,128]{2,1,0:T(8,128)(2,1)}, bf16[8,144,128]{2,1,0:T(8,128)(2,1)S(1)}, u32[]{:S(2)}, u32[]{:S(2)}) %collective-permute-start.25) | collective-permute-done | bytes 294944 | tf_op jit(solution)/shard_map/ppermute | solution.py:361
  165.8 4.7 %keys.2 = (bf16[128,256]{1,0:T(8,128)(2,1)S(1)}, bf16[128,256]{1,0:T(8,128)(2,1)S(1)}, bf16[128,256]{1,0:T(8,128)(2,1)S(1)}, bf16[128,256]{1,0:T(8,128)(2,1)S(1)}, bf16[4,128,128]{2,1,0:T(8,128)(2,1)S(1)}) custom-call(s32[4]{0:T(128)S(1)} %pad_add_fusion.4.offsets, bf16[128,512]{1,0:T(8,128)(2,1)S(1)} %get-tuple-element.51.refs_0_.refs_4_, ...), custom_call_target="tpu_custom_call" | custom-call | flops 536870912 | bytes 2097152 | tf_op jit(solution)/shard_map/keys/pallas_call | solution.py:494
  175.2 3.3 %collective-permute-start.13 = (bf16[128,1024]{1,0:T(8,128)(2,1)S(1)}, bf16[128,1024]{1,0:T(8,128)(2,1)S(1)}, u32[]{:S(2)}, u32[]{:S(2)}) collective-permute-start(bf16[128,1024]{1,0:T(8,128)(2,1)S(1)} %copy-done.30), channel_id=1, source_target_pairs={{0,8},{4,12},{8,0},{12,4},{16,24},{20,28},{24,16},{28,20},{1,9},{5... | collective-permute-start | bytes 786440 | tf_op jit(solution)/shard_map/ppermute | solution.py:356
  178.6 2.4 %collective-permute-start.29 = (bf16[128,256]{1,0:T(8,128)(2,1)S(1)}, bf16[128,256]{1,0:T(8,128)(2,1)S(1)}, u32[]{:S(2)}, u32[]{:S(2)}) collective-permute-start(bf16[128,256]{1,0:T(8,128)(2,1)S(1)} %get-tuple-element.86), channel_id=1, source_target_pairs={{0,12},{4,0},{8,4},{12,8},{16,28},{20,16},{24,20},{28,24},{1,13},{... | collective-permute-start | bytes 196616 | tf_op jit(solution)/shard_map/ppermute | solution.py:356
  181.1 4.5 %collective-permute-done.12.refs_1_ = bf16[128,1024]{1,0:T(8,128)(2,1)S(1)} collective-permute-done((bf16[128,1024]{1,0:T(8,128)(2,1)S(1)}, bf16[128,1024]{1,0:T(8,128)(2,1)S(1)}, u32[]{:S(2)}, u32[]{:S(2)}) %collective-permute-start.12) | collective-permute-done | bytes 262176 | tf_op jit(solution)/shard_map/ppermute | solution.py:356
  186.3 4.4 %collective-permute-done.13.refs_2_ = bf16[128,1024]{1,0:T(8,128)(2,1)S(1)} collective-permute-done((bf16[128,1024]{1,0:T(8,128)(2,1)S(1)}, bf16[128,1024]{1,0:T(8,128)(2,1)S(1)}, u32[]{:S(2)}, u32[]{:S(2)}) %collective-permute-start.13) | collective-permute-done | bytes 262176 | tf_op jit(solution)/shard_map/ppermute | solution.py:356
  190.8 2.6 %collective-permute-start.28 = (bf16[128,256]{1,0:T(8,128)(2,1)S(1)}, bf16[128,256]{1,0:T(8,128)(2,1)S(1)}, u32[]{:S(2)}, u32[]{:S(2)}) collective-permute-start(bf16[128,256]{1,0:T(8,128)(2,1)S(1)} %get-tuple-element.81), channel_id=1, source_target_pairs={{0,4},{4,8},{8,12},{12,0},{16,20},{20,24},{24,28},{28,16},{1,5},{5... | collective-permute-start | bytes 196616 | tf_op jit(solution)/shard_map/ppermute | solution.py:356
  (169 shorter events, 63.3 us)
Async XLA Ops:
  4.7 21.8 %collective-permute-start = (bf16[128,512]{1,0:T(8,128)(2,1)}, bf16[128,512]{1,0:T(8,128)(2,1)S(1)}, u32[]{:S(2)}, u32[]{:S(2)}) collective-permute-start(bf16[128,512]{1,0:T(8,128)(2,1)} %get-tuple-element.52), channel_id=1, source_target_pairs={{0,4},{4,8},{8,12},{12,0},{16,20},{20,24},{24,28},{28,16},{1,5},{5... | collective-permute-start | bytes 393224 | tf_op jit(solution)/shard_map/ppermute | solution.py:356
  6.7 19.7 %collective-permute-start.1 = (bf16[128,512]{1,0:T(8,128)(2,1)S(1)}, bf16[128,512]{1,0:T(8,128)(2,1)S(1)}, u32[]{:S(2)}, u32[]{:S(2)}) collective-permute-start(bf16[128,512]{1,0:T(8,128)(2,1)S(1)} %get-tuple-element.53), channel_id=1, source_target_pairs={{0,8},{4,12},{8,0},{12,4},{16,24},{20,28},{24,16},{28,20},{1,9},{5... | collective-permute-start | bytes 393224 | tf_op jit(solution)/shard_map/ppermute | solution.py:356
  8.0 18.4 %collective-permute-start.2 = (bf16[128,512]{1,0:T(8,128)(2,1)S(1)}, bf16[128,512]{1,0:T(8,128)(2,1)S(1)}, u32[]{:S(2)}, u32[]{:S(2)}) collective-permute-start(bf16[128,512]{1,0:T(8,128)(2,1)S(1)} %get-tuple-element.54), channel_id=1, source_target_pairs={{0,12},{4,0},{8,4},{12,8},{16,28},{20,16},{24,20},{28,24},{1,13},{... | collective-permute-start | bytes 393224 | tf_op jit(solution)/shard_map/ppermute | solution.py:356
  15.1 34.4 %collective-permute-start.15 = (bf16[128,2048]{1,0:T(8,128)(2,1)}, bf16[128,2048]{1,0:T(8,128)(2,1)}, u32[]{:S(2)}, u32[]{:S(2)}) collective-permute-start(bf16[128,2048]{1,0:T(8,128)(2,1)} %get-tuple-element.65), channel_id=1, source_target_pairs={{0,4},{4,8},{8,12},{12,0},{16,20},{20,24},{24,28},{28,16},{1,5},{5... | collective-permute-start | bytes 1572872 | tf_op jit(solution)/shard_map/ppermute | solution.py:356
  29.9 15.9 %collective-permute-start.7 = (bf16[8,144,128]{2,1,0:T(8,128)(2,1)S(1)}, bf16[8,144,128]{2,1,0:T(8,128)(2,1)S(1)}, u32[]{:S(2)}, u32[]{:S(2)}) collective-permute-start(bf16[8,144,128]{2,1,0:T(8,128)(2,1)S(1)} %states.3), channel_id=1, source_target_pairs={{0,16},{4,20},{8,24},{12,28},{16,0},{20,4},{24,8},{28,12},{1,17},{... | collective-permute-start | bytes 884744 | tf_op jit(solution)/shard_map/ppermute | solution.py:361
  48.6 14.6 %collective-permute-start.9 = (bf16[8,144,128]{2,1,0:T(8,128)(2,1)}, bf16[8,144,128]{2,1,0:T(8,128)(2,1)}, u32[]{:S(2)}, u32[]{:S(2)}) collective-permute-start(bf16[8,144,128]{2,1,0:T(8,128)(2,1)} %totals.2), channel_id=1, source_target_pairs={{0,2},{1,3},{2,0},{3,1},{4,6},{5,7},{6,4},{7,5},{8,10},{9,11},{10,... | collective-permute-start | bytes 884744 | tf_op jit(solution)/shard_map/ppermute | solution.py:364
  49.5 14.2 %collective-permute-start.10 = (bf16[8,144,128]{2,1,0:T(8,128)(2,1)}, bf16[8,144,128]{2,1,0:T(8,128)(2,1)}, u32[]{:S(2)}, u32[]{:S(2)}) collective-permute-start(bf16[8,144,128]{2,1,0:T(8,128)(2,1)} %totals.2), channel_id=1, source_target_pairs={{0,3},{1,0},{2,1},{3,2},{4,7},{5,4},{6,5},{7,6},{8,11},{9,8},{10,9... | collective-permute-start | bytes 884744 | tf_op jit(solution)/shard_map/ppermute | solution.py:364
  49.5 19.6 %collective-permute-start.16 = (bf16[128,2048]{1,0:T(8,128)(2,1)}, bf16[128,2048]{1,0:T(8,128)(2,1)}, u32[]{:S(2)}, u32[]{:S(2)}) collective-permute-start(bf16[128,2048]{1,0:T(8,128)(2,1)} %get-tuple-element.66), channel_id=1, source_target_pairs={{0,8},{4,12},{8,0},{12,4},{16,24},{20,28},{24,16},{28,20},{1,9},{5... | collective-permute-start | bytes 1572872 | tf_op jit(solution)/shard_map/ppermute | solution.py:356
  49.5 22.2 %collective-permute-start.17 = (bf16[128,2048]{1,0:T(8,128)(2,1)}, bf16[128,2048]{1,0:T(8,128)(2,1)}, u32[]{:S(2)}, u32[]{:S(2)}) collective-permute-start(bf16[128,2048]{1,0:T(8,128)(2,1)} %get-tuple-element.67), channel_id=1, source_target_pairs={{0,12},{4,0},{8,4},{12,8},{16,28},{20,16},{24,20},{28,24},{1,13},{... | collective-permute-start | bytes 1572872 | tf_op jit(solution)/shard_map/ppermute | solution.py:356
  56.2 35.3 %collective-permute-start.3 = (bf16[128,2048]{1,0:T(8,128)(2,1)}, bf16[128,2048]{1,0:T(8,128)(2,1)}, u32[]{:S(2)}, u32[]{:S(2)}) collective-permute-start(bf16[128,2048]{1,0:T(8,128)(2,1)} %get-tuple-element.56), channel_id=1, source_target_pairs={{0,4},{4,8},{8,12},{12,0},{16,20},{20,24},{24,28},{28,16},{1,5},{5... | collective-permute-start | bytes 1572872 | tf_op jit(solution)/shard_map/ppermute | solution.py:356
  63.2 28.3 %collective-permute-start.4 = (bf16[128,2048]{1,0:T(8,128)(2,1)}, bf16[128,2048]{1,0:T(8,128)(2,1)}, u32[]{:S(2)}, u32[]{:S(2)}) collective-permute-start(bf16[128,2048]{1,0:T(8,128)(2,1)} %get-tuple-element.57), channel_id=1, source_target_pairs={{0,8},{4,12},{8,0},{12,4},{16,24},{20,28},{24,16},{28,20},{1,9},{5... | collective-permute-start | bytes 1572872 | tf_op jit(solution)/shard_map/ppermute | solution.py:356
  63.7 30.5 %collective-permute-start.5 = (bf16[128,2048]{1,0:T(8,128)(2,1)}, bf16[128,2048]{1,0:T(8,128)(2,1)}, u32[]{:S(2)}, u32[]{:S(2)}) collective-permute-start(bf16[128,2048]{1,0:T(8,128)(2,1)} %get-tuple-element.58), channel_id=1, source_target_pairs={{0,12},{4,0},{8,4},{12,8},{16,28},{20,16},{24,20},{28,24},{1,13},{... | collective-permute-start | bytes 1572872 | tf_op jit(solution)/shard_map/ppermute | solution.py:356
  69.1 31.3 %collective-permute-start.11 = (bf16[8,144,128]{2,1,0:T(8,128)(2,1)S(1)}, bf16[8,144,128]{2,1,0:T(8,128)(2,1)S(1)}, u32[]{:S(2)}, u32[]{:S(2)}) collective-permute-start(bf16[8,144,128]{2,1,0:T(8,128)(2,1)S(1)} %get-tuple-element.59), channel_id=1, source_target_pairs={{0,16},{4,20},{8,24},{12,28},{16,0},{20,4},{24,8},{28,12},{1,17},{... | collective-permute-start | bytes 884744 | tf_op jit(solution)/shard_map/ppermute | solution.py:361
  116.8 16.1 %collective-permute-start.21 = (bf16[8,144,128]{2,1,0:T(8,128)(2,1)S(1)}, bf16[8,144,128]{2,1,0:T(8,128)(2,1)S(1)}, u32[]{:S(2)}, u32[]{:S(2)}) collective-permute-start(bf16[8,144,128]{2,1,0:T(8,128)(2,1)S(1)} %get-tuple-element.74), channel_id=1, source_target_pairs={{0,16},{4,20},{8,24},{12,28},{16,0},{20,4},{24,8},{28,12},{1,17},{... | collective-permute-start | bytes 884744 | tf_op jit(solution)/shard_map/ppermute | solution.py:361
  134.5 14.3 %collective-permute-start.23 = (bf16[8,144,128]{2,1,0:T(8,128)(2,1)S(1)}, bf16[8,144,128]{2,1,0:T(8,128)(2,1)S(1)}, u32[]{:S(2)}, u32[]{:S(2)}) collective-permute-start(bf16[8,144,128]{2,1,0:T(8,128)(2,1)S(1)} %totals.3), channel_id=1, source_target_pairs={{0,2},{1,3},{2,0},{3,1},{4,6},{5,7},{6,4},{7,5},{8,10},{9,11},{10,... | collective-permute-start | bytes 884744 | tf_op jit(solution)/shard_map/ppermute | solution.py:364
  135.8 13.6 %collective-permute-start.24 = (bf16[8,144,128]{2,1,0:T(8,128)(2,1)S(1)}, bf16[8,144,128]{2,1,0:T(8,128)(2,1)S(1)}, u32[]{:S(2)}, u32[]{:S(2)}) collective-permute-start(bf16[8,144,128]{2,1,0:T(8,128)(2,1)S(1)} %totals.3), channel_id=1, source_target_pairs={{0,3},{1,0},{2,1},{3,2},{4,7},{5,4},{6,5},{7,6},{8,11},{9,8},{10,9... | collective-permute-start | bytes 884744 | tf_op jit(solution)/shard_map/ppermute | solution.py:364
  135.8 19.9 %collective-permute-start.35 = (bf16[4,32,128]{2,1,0:T(8,128)(2,1)S(1)}, bf16[4,32,128]{2,1,0:T(8,128)(2,1)S(1)}, u32[]{:S(2)}, u32[]{:S(2)}) collective-permute-start(bf16[4,32,128]{2,1,0:T(8,128)(2,1)S(1)} %fusion.22), channel_id=1, source_target_pairs={{0,16},{4,20},{8,24},{12,28},{16,0},{20,4},{24,8},{28,12},{1,17},{... | collective-permute-start | bytes 98312 | tf_op jit(solution)/shard_map/ppermute | solution.py:361
  151.9 13.8 %collective-permute-start.25 = (bf16[8,144,128]{2,1,0:T(8,128)(2,1)}, bf16[8,144,128]{2,1,0:T(8,128)(2,1)S(1)}, u32[]{:S(2)}, u32[]{:S(2)}) collective-permute-start(bf16[8,144,128]{2,1,0:T(8,128)(2,1)} %get-tuple-element.75), channel_id=1, source_target_pairs={{0,16},{4,20},{8,24},{12,28},{16,0},{20,4},{24,8},{28,12},{1,17},{... | collective-permute-start | bytes 884744 | tf_op jit(solution)/shard_map/ppermute | solution.py:361
  152.1 20.4 %collective-permute-start.18 = (bf16[128,1024]{1,0:T(8,128)(2,1)}, bf16[128,1024]{1,0:T(8,128)(2,1)S(1)}, u32[]{:S(2)}, u32[]{:S(2)}) collective-permute-start(bf16[128,1024]{1,0:T(8,128)(2,1)} %copy-done.33), channel_id=1, source_target_pairs={{0,12},{4,0},{8,4},{12,8},{16,28},{20,16},{24,20},{28,24},{1,13},{... | collective-permute-start | bytes 786440 | tf_op jit(solution)/shard_map/ppermute | solution.py:356
  155.3 23.2 %collective-permute-start.19 = (bf16[128,1024]{1,0:T(8,128)(2,1)}, bf16[128,1024]{1,0:T(8,128)(2,1)S(1)}, u32[]{:S(2)}, u32[]{:S(2)}) collective-permute-start(bf16[128,1024]{1,0:T(8,128)(2,1)} %copy-done.28), channel_id=1, source_target_pairs={{0,8},{4,12},{8,0},{12,4},{16,24},{20,28},{24,16},{28,20},{1,9},{5... | collective-permute-start | bytes 786440 | tf_op jit(solution)/shard_map/ppermute | solution.py:356
  155.3 25.6 %collective-permute-start.20 = (bf16[128,1024]{1,0:T(8,128)(2,1)}, bf16[128,1024]{1,0:T(8,128)(2,1)S(1)}, u32[]{:S(2)}, u32[]{:S(2)}) collective-permute-start(bf16[128,1024]{1,0:T(8,128)(2,1)} %copy-done.25), channel_id=1, source_target_pairs={{0,4},{4,8},{8,12},{12,0},{16,20},{20,24},{24,28},{28,16},{1,5},{5... | collective-permute-start | bytes 786440 | tf_op jit(solution)/shard_map/ppermute | solution.py:356
  175.2 15.6 %collective-permute-start.13 = (bf16[128,1024]{1,0:T(8,128)(2,1)S(1)}, bf16[128,1024]{1,0:T(8,128)(2,1)S(1)}, u32[]{:S(2)}, u32[]{:S(2)}) collective-permute-start(bf16[128,1024]{1,0:T(8,128)(2,1)S(1)} %copy-done.30), channel_id=1, source_target_pairs={{0,8},{4,12},{8,0},{12,4},{16,24},{20,28},{24,16},{28,20},{1,9},{5... | collective-permute-start | bytes 786440 | tf_op jit(solution)/shard_map/ppermute | solution.py:356
  178.5 12.3 %collective-permute-start.14 = (bf16[128,1024]{1,0:T(8,128)(2,1)S(1)}, bf16[128,1024]{1,0:T(8,128)(2,1)S(1)}, u32[]{:S(2)}, u32[]{:S(2)}) collective-permute-start(bf16[128,1024]{1,0:T(8,128)(2,1)S(1)} %copy-done.27), channel_id=1, source_target_pairs={{0,4},{4,8},{8,12},{12,0},{16,20},{20,24},{24,28},{28,16},{1,5},{5... | collective-permute-start | bytes 786440 | tf_op jit(solution)/shard_map/ppermute | solution.py:356
  181.0 12.6 %collective-permute-start.30 = (bf16[128,256]{1,0:T(8,128)(2,1)S(1)}, bf16[128,256]{1,0:T(8,128)(2,1)S(1)}, u32[]{:S(2)}, u32[]{:S(2)}) collective-permute-start(bf16[128,256]{1,0:T(8,128)(2,1)S(1)} %get-tuple-element.87), channel_id=1, source_target_pairs={{0,8},{4,12},{8,0},{12,4},{16,24},{20,28},{24,16},{28,20},{1,9},{5... | collective-permute-start | bytes 196616 | tf_op jit(solution)/shard_map/ppermute | solution.py:356
  (53 other events, 482.7 us)

commit v2 on v1

v2 whole, which is shorter than its diff:
```python
import functools

import jax
import jax.numpy as jnp
from jax import lax
from jax.experimental import pallas as pl
from jax.experimental.pallas import tpu as pltpu
from jax.sharding import PartitionSpec as P

BLK = 512
TILE = 256
PAIR = 2
EXT = 16
LIMIT = 40 * 1024 * 1024

F32 = jnp.float32
BF16 = jnp.bfloat16
SMEM = pltpu.SMEM


def nn(left, right):
    return lax.dot_general(left, right, (((1,), (0,)), ((), ())), preferred_element_type=F32)


def nt(left, right):
    return lax.dot_general(left, right, (((1,), (1,)), ((), ())), preferred_element_type=F32)


def turned(array):
    return array.astype(F32).T.astype(array.dtype)


def column(row, width):
    n = row.shape[1]
    square = jnp.broadcast_to(row, (n, n)).T
    return jnp.concatenate([square] * (width // n), axis=1)


def thirds(row):
    rows = jnp.broadcast_to(row, (EXT, row.shape[1]))
    high = rows.astype(BF16).astype(F32)
    middle = (rows - high).astype(BF16).astype(F32)
    low = rows - high - middle
    place = lax.broadcasted_iota(jnp.int32, rows.shape, 0)
    picked = jnp.where(place == 0, high, jnp.where(place == 1, middle, low))
    return jnp.where(place < 3, picked, 0.0).astype(BF16)


def whole_row(block):
    return jnp.sum(block.astype(F32), axis=0, keepdims=True)


def weight_rows(ref, u):
    whole = jnp.concatenate([ref[i, u] for i in range(ref.shape[0])], axis=0)
    return turned(whole)


def features(weight, rows):
    logits = nt(weight, rows).astype(BF16).astype(F32)
    upper = jnp.exp(logits)
    lower = jnp.exp(-logits)
    upper = upper * (1.0 / jnp.sum(upper, axis=0, keepdims=True))
    lower = lower * (1.0 / jnp.sum(lower, axis=0, keepdims=True))
    return jnp.concatenate([upper, lower], axis=0)


def feature_back(feats, upstream):
    half = feats.shape[0] // 2
    weighted = feats * upstream
    first, second = weighted[:half], weighted[half:]
    first = first - feats[:half] * jnp.sum(first, axis=0, keepdims=True)
    second = second - feats[half:] * jnp.sum(second, axis=0, keepdims=True)
    return (first - second).astype(BF16)


def flat(ref):
    return ref[...].reshape(-1, ref.shape[-1])


def pack_kernel(columns, table, *refs):
    sources, out = refs[:-1], refs[-1]
    width = sources[0].shape[1]
    for i, source in enumerate(sources):
        out[0, :, i * width : (i + 1) * width] = source[...]


def pack(table, sources, pieces, columns, width):
    rows = sources[0].shape[0]
    count = columns * len(sources)

    def take(s):
        return pl.BlockSpec((rows, width), lambda i, t: (0, t[s * pieces + i]))

    return pl.pallas_call(
        functools.partial(pack_kernel, columns),
        out_shape=jax.ShapeDtypeStruct((pieces, rows, count * width), sources[0].dtype),
        grid_spec=pltpu.PrefetchScalarGridSpec(
            num_scalar_prefetch=1,
            grid=(pieces,),
            in_specs=[take(s) for s in range(columns) for _ in sources],
            out_specs=pl.BlockSpec((1, rows, count * width), lambda i, t: (i, 0, 0)),
        ),
        compiler_params=pltpu.CompilerParams(vmem_limit_bytes=LIMIT),
        cost_estimate=pl.CostEstimate(
            flops=0, bytes_accessed=4 * pieces * rows * count * width, transcendentals=0
        ),
        name="pack",
    )(table, *(list(sources) * columns))


def unpack_kernel(outputs, table, *refs):
    sources, outs = refs[:-outputs], refs[-outputs:]
    for s, source in enumerate(sources):
        pieces = source.shape[0]
        width = source.shape[2] // outputs
        for r in range(pieces):
            at = pl.ds(pl.multiple_of(table[s * pieces + r] * width, width), width)
            for i, out in enumerate(outs):
                out[:, at] = source[r, :, i * width : (i + 1) * width]


def unpack(table, sources, outputs, width):
    pieces, rows = sources[0].shape[:2]
    total = len(sources) * pieces * width
    step = rows // 2
    return pl.pallas_call(
        functools.partial(unpack_kernel, outputs),
        out_shape=[jax.ShapeDtypeStruct((rows, total), sources[0].dtype)] * outputs,
        grid=(rows // step,),
        in_specs=[pl.BlockSpec(memory_space=SMEM)]
        + [pl.BlockSpec((pieces, step, outputs * width), lambda i: (0, i, 0))] * len(sources),
        out_specs=[pl.BlockSpec((step, total), lambda i: (i, 0))] * outputs,
        compiler_params=pltpu.CompilerParams(vmem_limit_bytes=LIMIT),
        cost_estimate=pl.CostEstimate(
            flops=0, bytes_accessed=4 * rows * total * outputs, transcendentals=0
        ),
        name="unpack",
    )(table, *sources)


def state_kernel(slot, k_ref, v_ref, w_ref, out):
    k_all, v_all = flat(k_ref), flat(v_ref)
    hd = k_all.shape[1]
    for u in range(out.shape[0]):
        weight = weight_rows(w_ref, u)
        feats = features(weight[weight.shape[0] // 2 :], k_all).astype(BF16)
        out[u, :hd, :] = nn(feats, v_all).astype(BF16)
        ones = jnp.ones((EXT, feats.shape[1]), BF16)
        out[u, hd:, :] = thirds(nt(ones, feats)[:1])


def block_kernel(
    slot, k_ref, v_ref, q_ref, g_ref, w_ref, st_ref, gq_ref, dk_ref, dv_ref, sx_ref, gm_ref, vt_all
):
    k_all, v_all, q_all, g_all = flat(k_ref), flat(v_ref), flat(q_ref), flat(g_ref)
    hd = k_all.shape[1]

    @pl.when(pl.program_id(0) == 0)
    def _():
        vt_all[...] = turned(v_all)
        dv_ref[...] = jnp.zeros_like(dv_ref)

    maps = []
    earlier = lax.broadcasted_iota(jnp.int32, (TILE, TILE), 0) <= lax.broadcasted_iota(
        jnp.int32, (TILE, TILE), 1
    )

    def causal(array, begin):
        masked = jnp.where(earlier, array[begin:], 0.0)
        return masked if begin == 0 else jnp.concatenate([array[:begin], masked], axis=0)

    for u in range(PAIR):
        weight = weight_rows(w_ref, u)
        half = weight.shape[0] // 2
        lanes = slice(u * hd, (u + 1) * hd)
        q_feat = features(weight[:half], q_all[:, lanes])
        k_low = features(weight[half:], k_all).astype(BF16)
        q_low = q_feat.astype(BF16)
        k_turned = turned(k_low)
        state = st_ref[u, :hd, :]
        state_turned = turned(state)
        norm = column(whole_row(st_ref[u, hd:, :]), TILE)
        g_turned = g_all[:, lanes].astype(F32).T
        back = []
        dkey = [jnp.zeros((2 * half, TILE), F32) for _ in range(BLK // TILE)]
        dvalue = [jnp.zeros((hd, TILE), F32) for _ in range(BLK // TILE)]
        suffix = jnp.zeros((2 * half, hd), F32)
        suffix_norm = jnp.zeros((2 * half, 1), F32)
        for j in range(BLK // TILE):
            begin, end = j * TILE, (j + 1) * TILE
            own = q_low[:, begin:end]
            own_wide = own.astype(F32)
            scores = causal(nn(k_turned[:end], own), begin)
            scores_low = scores.astype(BF16)
            numerator = nn(state_turned, own) + nn(vt_all[:, :end], scores_low)
            denominator = jnp.sum(own_wide * norm, axis=0, keepdims=True) + jnp.sum(
                scores, axis=0, keepdims=True
            )
            inverse = 1.0 / denominator
            scaled = g_turned[:, begin:end] * inverse
            scaled_low = scaled.astype(BF16)
            norm_grad = -jnp.sum(scaled * (numerator * inverse), axis=0, keepdims=True)
            dscores = causal(nn(v_all[:end], scaled_low) + norm_grad, begin).astype(BF16)
            dquery = nn(state, scaled_low) + norm * norm_grad + nn(k_low[:, :end], dscores)
            back.append(feature_back(q_feat[:, begin:end], dquery))
            for i in range(j + 1):
                rows = slice(i * TILE, (i + 1) * TILE)
                dkey[i] = dkey[i] + nt(own, dscores[rows])
                dvalue[i] = dvalue[i] + nt(scaled_low, scores_low[rows])
            suffix = suffix + nt(own, scaled_low)
            suffix_norm = suffix_norm + jnp.sum(own_wide * norm_grad, axis=1, keepdims=True)
        dlog = jnp.concatenate(back, axis=1)
        back = nn(turned(dlog), weight[:half]).astype(BF16)
        gq_ref[:, :, lanes] = back.reshape(gq_ref.shape[0], -1, hd)
        maps.append(nn(dlog, q_all[:, lanes]))
        dk_ref[u] = jnp.concatenate(dkey, axis=1)
        dv_ref[...] += jnp.concatenate(dvalue, axis=1)
        sx_ref[u, :hd, :] = suffix.astype(BF16)
        sx_ref[u, hd:, :] = thirds(jnp.broadcast_to(suffix_norm, (2 * half, 2 * half)).T[:1])
    gm_ref[0] = jnp.concatenate(maps, axis=0).T.astype(gm_ref.dtype)


def key_kernel(
    slot, k_ref, v_ref, w_ref, sx_ref, dk_ref, dv_ref, out, gm_ref, vt_all, total, logs, weights
):
    k_all, v_all = flat(k_ref), flat(v_ref)
    hd = k_all.shape[1]
    step = pl.program_id(0)

    @pl.when(step == 0)
    def _():
        vt_all[...] = turned(v_all)
        total[...] = dv_ref[...]

    maps = []
    for u in range(PAIR):
        weight = weight_rows(w_ref, u)
        half = weight.shape[0] // 2
        weight = weight[half:]
        feats = features(weight, k_all)
        suffix = sx_ref[u, :hd, :]
        norm = column(whole_row(sx_ref[u, hd:, :]), BLK)
        dlog = feature_back(feats, dk_ref[u] + nn(suffix, vt_all[...]) + norm)
        at = pl.ds(pl.multiple_of((step * PAIR + u) * half, half), half)
        logs[at, :] = dlog
        weights[at, :] = weight
        maps.append(nn(dlog, k_all))
        total[...] += nn(turned(suffix), feats.astype(BF16))
    gm_ref[0] = jnp.concatenate(maps, axis=0).T.astype(gm_ref.dtype)

    @pl.when(step == pl.num_programs(0) - 1)
    def _():
        pair = jnp.concatenate([nn(turned(logs[...]), weights[...]), total[...].T], axis=1)
        out[...] = pair.astype(out.dtype).reshape(out.shape)


def total_kernel(*refs):
    out = refs[-1]
    heads, hd = out.shape[0], out.shape[2]
    for h in range(heads):
        out[h, :hd, :] = sum(ref[h, :hd, :].astype(F32) for ref in refs[:-1]).astype(BF16)
        out[h, hd:, :] = thirds(sum(whole_row(ref[h, hd:, :]) for ref in refs[:-1]))


def spread_kernel(grp, others, closing, block_weight, total_weight, place, *refs):
    parts, totals, refs = refs[:grp], refs[grp : grp + others], refs[grp + others :]
    if closing:
        outs, grad, scratch = refs[:grp], refs[grp], refs[grp + 1]
    else:
        state_ref, norm_ref, outs = refs[0], refs[1], refs[2:]
    heads, hd = parts[0].shape[0], parts[0].shape[2]
    for h in range(heads):
        states = [ref[h, :hd, :].astype(F32) for ref in parts]
        norms = [whole_row(ref[h, hd:, :]) for ref in parts]
        others_state = [ref[h, :hd, :].astype(F32) for ref in totals]
        others_norm = [whole_row(ref[h, hd:, :]) for ref in totals]
        if closing:
            base, base_norm = jnp.zeros_like(states[0]), jnp.zeros_like(norms[0])
            scratch[...] = sum(states) + sum(others_state)
            rows = grad.shape[1]
            grad[h] = scratch[pl.ds(pl.multiple_of(place[0] * rows, rows), rows), :]
        else:
            base, base_norm = state_ref[h], norm_ref[pl.ds(h, 1), :]
        for i, (state, norm) in enumerate(zip(others_state, others_norm)):
            base = base + total_weight[i] * state
            base_norm = base_norm + total_weight[i] * norm
        for r, out in enumerate(outs):
            state, norm = base, base_norm
            for i in range(grp):
                if i != r:
                    state = state + block_weight[r * grp + i] * states[i]
                    norm = norm + block_weight[r * grp + i] * norms[i]
            out[h, :hd, :] = state.astype(BF16)
            out[h, hd:, :] = thirds(norm)


def whole_call(kernel, outs, smem, arrays, name, scratch=()):
    total = sum(a.size * a.dtype.itemsize for a in (*arrays, *outs))
    return pl.pallas_call(
        kernel,
        out_shape=outs,
        in_specs=[pl.BlockSpec(memory_space=SMEM)] * len(smem)
        + [pl.BlockSpec(memory_space=pltpu.VMEM)] * len(arrays),
        out_specs=[pl.BlockSpec(memory_space=pltpu.VMEM)] * len(outs),
        scratch_shapes=list(scratch),
        compiler_params=pltpu.CompilerParams(vmem_limit_bytes=LIMIT),
        cost_estimate=pl.CostEstimate(flops=total, bytes_accessed=total, transcendentals=0),
        name=name,
    )(*smem, *arrays)


def shards(
    query_rows, key_rows, value_rows, grad_out, query_map, key_map, prefix_state, prefix_norm
):
    ctx, fsdp = lax.axis_size("ctx"), lax.axis_size("fsdp")
    tok = query_rows.shape[0]
    heads, map_rows, half = query_map.shape
    hd = map_rows * fsdp
    kv_heads = key_rows.shape[1] // hd
    replicas = ctx // kv_heads
    part = BLK // tok
    grp = ctx // part
    mine = lax.axis_index("ctx")
    block, seq = mine // part, lax.axis_index("fsdp")

    blocks_of = [[g * part + p for p in range(part)] for g in range(grp)]
    owners_of = [
        [(g * part + p) * fsdp + i for g in range(grp) for i in range(fsdp)] for p in range(part)
    ]

    def within(array):
        return lax.all_to_all(array, "ctx", 0, 0, axis_index_groups=blocks_of, tiled=True)

    def across(array, shift):
        return lax.ppermute(array, "ctx", [(d, (d + shift * part) % ctx) for d in range(ctx)])

    def along(array, shift):
        return lax.ppermute(array, "fsdp", [(d, (d + shift) % fsdp) for d in range(fsdp)])

    def ints(values):
        return jnp.stack([jnp.asarray(v, jnp.int32) for v in values])

    slots = range(grp)
    order = list(reversed(slots))
    slot = {s: (block + s) % grp for s in slots}
    owner = {s: [slot[s] * part + p for p in range(part)] for s in slots}

    kv_table = ints([c // replicas for s in slots for c in owner[s]])
    kv = within(pack(kv_table, (key_rows, value_rows), part, grp, hd))
    own_maps = jnp.concatenate((query_map, key_map), axis=-1)
    maps = lax.all_gather(own_maps, ("ctx", "fsdp"), axis_index_groups=owners_of)
    rows = {
        s: within(pack(ints(owner[s]), (query_rows, grad_out), part, 1, heads * hd))
        for s in order
    }

    grid = (heads // PAIR,)
    params = pltpu.CompilerParams(
        dimension_semantics=("arbitrary",), vmem_limit_bytes=LIMIT
    )

    def piece_spec(column, count):
        return pl.BlockSpec((part, tok, count * hd), lambda h, t: (0, 0, column(h)))

    def kv_specs(s):
        return [piece_spec(lambda h: 2 * s, 1), piece_spec(lambda h: 2 * s + 1, 1)]

    map_spec = pl.BlockSpec((fsdp, PAIR, map_rows, 2 * half), lambda h, t: (t[0], h, 0, 0))

    def call(kernel, s, outs, specs, out_specs, arrays, scratch, name, flops):
        moved = sum(a.size * a.dtype.itemsize for a in (*arrays, *outs))
        return pl.pallas_call(
            kernel,
            out_shape=outs,
            grid_spec=pltpu.PrefetchScalarGridSpec(
                num_scalar_prefetch=1,
                grid=grid,
                in_specs=specs,
                out_specs=out_specs,
                scratch_shapes=scratch,
            ),
            compiler_params=params,
            cost_estimate=pl.CostEstimate(flops=flops, bytes_accessed=moved, transcendentals=0),
            name=name,
        )(ints([slot[s]]), *arrays)

    ext_spec = pl.BlockSpec((PAIR, hd + EXT, hd), lambda h, t: (h, 0, 0))
    ext_shape = jax.ShapeDtypeStruct((heads, hd + EXT, hd), BF16)
    gm_spec = pl.BlockSpec((1, hd, PAIR * half), lambda h, t: (h, 0, 0))
    gm_shape = jax.ShapeDtypeStruct((heads // PAIR, hd, PAIR * half), BF16)
    dk_spec = pl.BlockSpec((PAIR, 2 * half, BLK), lambda h, t: (h, 0, 0))
    dv_spec = pl.BlockSpec((hd, BLK), lambda h, t: (0, 0))
    unit = 2 * heads * BLK * hd

    def states_of(s):
        return call(
            state_kernel,
            s,
            [ext_shape],
            kv_specs(s) + [map_spec],
            [ext_spec],
            [kv, kv, maps],
            [],
            "states",
            unit * 2 * hd,
        )[0]

    def scan(partial, before, extra, closing):
        parts = [partial[0]] + [across(partial[s], s) for s in slots[1:]]
        (total,) = whole_call(total_kernel, [ext_shape], [], parts, "totals")
        others = [along(total, r) for r in range(1, fsdp)]
        result = whole_call(
            functools.partial(spread_kernel, grp, fsdp - 1, closing),
            [ext_shape] * grp
            + [jax.ShapeDtypeStruct((heads, map_rows, hd), F32)] * closing,
            [*weights(before), ints([seq])],
            parts + others + extra,
            "spread",
            [pltpu.VMEM((hd, hd), F32)] * closing,
        )
        return [result[0]] + [across(result[s], -s) for s in slots[1:]], result[grp:]

    def weights(before):
        seqs = [(seq - r) % fsdp for r in range(1, fsdp)]
        blocks = [(block - r) % grp for r in slots]
        return (
            jnp.stack([before(b, a).astype(F32) for a in blocks for b in blocks]),
            jnp.stack([before(other, seq).astype(F32) for other in seqs]),
        )

    partial = {s: states_of(s) for s in order}
    state, _ = scan(partial, lambda a, b: a < b, [prefix_state, prefix_norm], False)

    def block_of(s):
        return call(
            block_kernel,
            s,
            [
                jax.ShapeDtypeStruct((part, tok, heads * hd), BF16),
                jax.ShapeDtypeStruct((heads, 2 * half, BLK), F32),
                jax.ShapeDtypeStruct((hd, BLK), F32),
                ext_shape,
                gm_shape,
            ],
            kv_specs(s)
            + [piece_spec(lambda h: h, PAIR), piece_spec(lambda h: grid[0] + h, PAIR)]
            + [map_spec, ext_spec],
            [piece_spec(lambda h: h, PAIR), dk_spec, dv_spec, ext_spec, gm_spec],
            [kv, kv, rows[s], rows[s], maps, state[s]],
            [pltpu.VMEM((hd, BLK), BF16)],
            "blocks",
            unit * 8 * BLK,
        )

    blocks = {s: block_of(s) for s in order}
    partial = {s: blocks[s][3] for s in slots}
    suffix, (grad_prefix,) = scan(partial, lambda a, b: a > b, [], True)

    kv_type = BF16 if replicas == 1 else F32

    def keys_of(s):
        return call(
            key_kernel,
            s,
            [jax.ShapeDtypeStruct((part, tok, 2 * hd), kv_type), gm_shape],
            kv_specs(s) + [map_spec, ext_spec, dk_spec, dv_spec],
            [piece_spec(lambda h: 0, 2), gm_spec],
            [kv, kv, maps, suffix[s], blocks[s][1], blocks[s][2]],
            [
                pltpu.VMEM((hd, BLK), BF16),
                pltpu.VMEM((hd, BLK), F32),
                pltpu.VMEM((heads * half, BLK), BF16),
                pltpu.VMEM((heads * half, hd), BF16),
            ],
            "keys",
            unit * 4 * hd,
        )

    def fold(parts):
        stacked = jnp.stack([parts[s] for s in slots])
        pieces = stacked.reshape(grp, heads // PAIR, fsdp, map_rows, PAIR * half)

        def rows_for(device):
            return lax.dynamic_index_in_dim(pieces, device, 2, keepdims=False)

        summed = rows_for(seq).astype(F32)
        for r in range(1, fsdp):
            summed = summed + along(rows_for((seq + r) % fsdp), r).astype(F32)
        sent = summed.astype(BF16)
        result = summed[0]
        for s in slots[1:]:
            result = result + across(sent[s], s).astype(F32)
        result = result.reshape(heads // PAIR, map_rows, PAIR, half)
        return jnp.swapaxes(result, 1, 2).reshape(heads, map_rows, half)

    table = ints([c for s in slots for c in owner[s]])
    back = {s: within(blocks[s][0]) for s in order}
    (grad_queries,) = unpack(table, [back[s] for s in slots], 1, heads * hd)
    query_map_grad = fold({s: blocks[s][4] for s in slots})

    keys = {s: keys_of(s) for s in slots}
    back = {s: within(keys[s][0]) for s in slots}
    grad_keys, grad_values = unpack(table, [back[s] for s in slots], 2, hd)
    if replicas > 1:
        grad_keys, grad_values = (
            jnp.sum(a.reshape(tok, kv_heads, replicas, hd), axis=2)
            .astype(BF16)
            .reshape(tok, kv_heads * hd)
            for a in (grad_keys, grad_values)
        )
    key_map_grad = fold({s: keys[s][1] for s in slots})
    return grad_queries, grad_keys, grad_values, query_map_grad, key_map_grad, grad_prefix


def solution(mesh):
    rows, maps = P(("fsdp", "ctx"), None), P("ctx", "fsdp", None)
    return jax.shard_map(
        shards,
        mesh=mesh,
        in_specs=(rows,) * 4 + (maps, maps, P("ctx", None, None), P("ctx", None)),
        out_specs=(rows,) * 3 + (maps,) * 3,
        check_vma=False,
    )
```

time: 201 us -> 279 us (1.39)
  waiting for transfers between devices: 65.5 us -> 105 us
  blocking collectives: 9.08 us -> 42.7 us
  local copies, waits for them, and re-layouts: 16.8 us -> 27.1 us
  Pallas kernels: 60.1 us -> 54.3 us
  other arithmetic: 5.3 us -> 1.97 us
    all_to_all x0 -> x6, waiting for transfers between devices: none -> 27.5 us  [within(): lax.all_to_all(array, 'ctx', 0, 0, axis_index_groups=blocks_of, tiled=True)]
    all_gather x1, blocking collectives: 9.08 us -> 34.6 us  [shards(): lax.all_gather(own_maps, ('ctx', 'fsdp'), axis_index_groups=owners_of)]
    all_to_all x0 -> x6, starting transfers between devices: none -> 23.2 us  [within(): lax.all_to_all(array, 'ctx', 0, 0, axis_index_groups=blocks_of, tiled=True)]
    ppermute x21 -> x0, starting transfers between devices: 21.9 us -> none  [within(): lax.ppermute(array, 'ctx', [(d, d // part * part + (d + shift) % part) fo...]
    ppermute x7 -> x6, waiting for transfers between devices: 27.8 us -> 42.1 us  [across(): lax.ppermute(array, 'ctx', [(d, (d + shift * part) % ctx) for d in range(...]
    ppermute x21 -> x0, waiting for transfers between devices: 14.2 us -> none  [within(): lax.ppermute(array, 'ctx', [(d, d // part * part + (d + shift) % part) fo...]
    ppermute x12, waiting for transfers between devices: 23.6 us -> 35.1 us  [along(): lax.ppermute(array, 'fsdp', [(d, (d + shift) % fsdp) for d in range(fsdp)])]
    unnamed x74, local copies, waits for them, and re-layouts: 16.4 us -> 26.9 us
  transfers between devices with their start and end apart: 40 -> 24, of which waited for: 18 -> 19; matrix products, arithmetic and copies ran while one was open for 2% -> 1% of each run, Pallas kernels for 22% -> 17%
where the time goes in v2:
time: 279 us; the launch traced here: 275 us
  waiting for transfers between devices  105 us (38%)
  Pallas kernels  54.3 us (19%)
  starting transfers between devices  43.1 us (15%)
  blocking collectives  42.7 us (15%)
  local copies, waits for them, and re-layouts  27.1 us (10%)
    pallas_call x6, Pallas kernels, call(): pl.pallas_call(kernel, out_shape=outs, grid_spec=pltpu.PrefetchScalarGrid...  43.8 us
    ppermute x6, waiting for transfers between devices, across(): lax.ppermute(array, 'ctx', [(d, (d + shift * part) % ctx) for d in range(...  42.1 us
    ppermute x12, waiting for transfers between devices, along(): lax.ppermute(array, 'fsdp', [(d, (d + shift) % fsdp) for d in range(fsdp)])  35.1 us
    all_gather x1, blocking collectives, shards(): lax.all_gather(own_maps, ('ctx', 'fsdp'), axis_index_groups=owners_of)  34.6 us
    all_to_all x6, waiting for transfers between devices, within(): lax.all_to_all(array, 'ctx', 0, 0, axis_index_groups=blocks_of, tiled=True)  27.5 us
    unnamed x74, local copies, waits for them, and re-layouts  26.9 us
    all_to_all x6, starting transfers between devices, within(): lax.all_to_all(array, 'ctx', 0, 0, axis_index_groups=blocks_of, tiled=True)  23.2 us
    ppermute x12, starting transfers between devices, along(): lax.ppermute(array, 'fsdp', [(d, (d + shift) % fsdp) for d in range(fsdp)])  11.3 us
  transfers between devices with their start and end apart: 24, of which 19 were waited for; matrix products, arithmetic and copies ran while one was open for 1% of the time, Pallas kernels for 17%

profile of v2, /device:TPU:1, one launch (start us, length us, event | category | flops | bytes accessed | tf_op | source)
XLA Modules:
  0.0 275.0 jit_solution(832488255700366037)
XLA Ops:
  4.6 4.4 %all-to-all-start = ((bf16[4,128,512]{2,1,0:T(8,128)(2,1)}), bf16[4,128,512]{2,1,0:T(8,128)(2,1)S(1)}, u32[]{:S(2)}, u32[]{:S(2)}) async-start(bf16[4,128,512]{2,1,0:T(8,128)(2,1)} %copy-done.9), calls=%async_computation | async-start | bytes 1048576 | tf_op jit(solution)/shard_map/all_to_all | solution.py:332
  13.0 3.1 %all-to-all-done.k_ref.v_ref = bf16[4,128,512]{2,1,0:T(8,128)(2,1)S(1)} async-done(((bf16[4,128,512]{2,1,0:T(8,128)(2,1)}), bf16[4,128,512]{2,1,0:T(8,128)(2,1)S(1)}, u32[]{:S(2)}, u32[]{:S(2)}) %all-to-all-start) | async-done | bytes 524320 | tf_op jit(solution)/shard_map/all_to_all | solution.py:332
  16.1 4.5 %all-to-all-start.3 = ((bf16[4,128,2048]{2,1,0:T(8,128)(2,1)}), bf16[4,128,2048]{2,1,0:T(8,128)(2,1)}, u32[]{:S(2)}, u32[]{:S(2)}) async-start(bf16[4,128,2048]{2,1,0:T(8,128)(2,1)} %copy-done.4), calls=%async_computation.3 | async-start | bytes 4194304 | tf_op jit(solution)/shard_map/all_to_all | solution.py:332
  24.5 21.3 %all-to-all-done.3.q_ref.g_ref = bf16[4,128,2048]{2,1,0:T(8,128)(2,1)} async-done(((bf16[4,128,2048]{2,1,0:T(8,128)(2,1)}), bf16[4,128,2048]{2,1,0:T(8,128)(2,1)}, u32[]{:S(2)}, u32[]{:S(2)}) %all-to-all-start.3) | async-done | bytes 2097184 | tf_op jit(solution)/shard_map/all_to_all | solution.py:332
  45.8 3.6 %all-to-all-start.1 = ((bf16[4,128,2048]{2,1,0:T(8,128)(2,1)}), bf16[4,128,2048]{2,1,0:T(8,128)(2,1)S(1)}, u32[]{:S(2)}, u32[]{:S(2)}) async-start(bf16[4,128,2048]{2,1,0:T(8,128)(2,1)} %copy-done.3), calls=%async_computation.1 | async-start | bytes 4194304 | tf_op jit(solution)/shard_map/all_to_all | solution.py:332
  49.5 34.6 %all-gather = bf16[64,32,128]{2,1,0:T(8,128)(2,1)S(1)} all-gather(bf16[8,32,128]{2,1,0:T(8,128)(2,1)S(1)} %pad_maximum_fusion.2), channel_id=2, replica_groups={{0,1,2,3,16,17,18,19},{4,5,6,7,20,21,22,23},{8,9,10,11,24,25,26,27},{12..., dimensions={0}, use_global_device_ids=true | all-gather | bytes 589824 | tf_op jit(solution)/shard_map/all_gather | solution.py:351
  91.6 11.1 %collective-permute-done.refs_1_ = bf16[8,144,128]{2,1,0:T(8,128)(2,1)S(1)} collective-permute-done((bf16[8,144,128]{2,1,0:T(8,128)(2,1)S(1)}, bf16[8,144,128]{2,1,0:T(8,128)(2,1)S(1)}, u32[]{:S(2)}, u32[]{:S(2)}) %collective-permute-start) | collective-permute-done | bytes 294944 | tf_op jit(solution)/shard_map/ppermute | solution.py:335
  106.7 5.2 %collective-permute-done.1.refs_2_ = bf16[8,144,128]{2,1,0:T(8,128)(2,1)} collective-permute-done((bf16[8,144,128]{2,1,0:T(8,128)(2,1)}, bf16[8,144,128]{2,1,0:T(8,128)(2,1)}, u32[]{:S(2)}, u32[]{:S(2)}) %collective-permute-start.1) | collective-permute-done | bytes 294944 | tf_op jit(solution)/shard_map/ppermute | solution.py:338
  112.0 8.0 %collective-permute-done.2.refs_3_ = bf16[8,144,128]{2,1,0:T(8,128)(2,1)} collective-permute-done((bf16[8,144,128]{2,1,0:T(8,128)(2,1)}, bf16[8,144,128]{2,1,0:T(8,128)(2,1)}, u32[]{:S(2)}, u32[]{:S(2)}) %collective-permute-start.2) | collective-permute-done | bytes 294944 | tf_op jit(solution)/shard_map/ppermute | solution.py:338
  124.7 15.3 %collective-permute-done.4.st_ref = bf16[8,144,128]{2,1,0:T(8,128)(2,1)S(1)} collective-permute-done((bf16[8,144,128]{2,1,0:T(8,128)(2,1)S(1)}, bf16[8,144,128]{2,1,0:T(8,128)(2,1)S(1)}, u32[]{:S(2)}, u32[]{:S(2)}) %collective-permute-start.4) | collective-permute-done | bytes 294944 | tf_op jit(solution)/shard_map/ppermute | solution.py:335
  140.1 15.5 %blocks.3 = (bf16[4,128,1024]{2,1,0:T(8,128)(2,1)S(1)}, f32[8,128,512]{2,1,0:T(8,128)S(1)}, f32[128,512]{1,0:T(8,128)S(1)}, bf16[8,144,128]{2,1,0:T(8,128)(2,1)}, bf16[4,128,128]{2,1,0:T(8,128)(2,1)S(1)}) custom-call(s32[1]{0:T(128)} %bitcast.16.slot, bf16[4,128,512]{2,1,0:T(8,128)(2,1)S(1)} %all-to-all-done.k_ref.v_ref, ...), custom_call_target="tpu_custom_call" | custom-call | flops 4294967296 | bytes 9895936 | tf_op jit(solution)/shard_map/blocks/pallas_call | solution.py:372
  160.2 14.3 %blocks.2 = (bf16[4,128,1024]{2,1,0:T(8,128)(2,1)S(1)}, f32[8,128,512]{2,1,0:T(8,128)S(1)}, f32[128,512]{1,0:T(8,128)S(1)}, bf16[8,144,128]{2,1,0:T(8,128)(2,1)S(1)}, bf16[4,128,128]{2,1,0:T(8,128)(2,1)S(1)}) custom-call(s32[1]{0:T(128)} %bitcast.8.slot, bf16[4,128,512]{2,1,0:T(8,128)(2,1)S(1)} %all-to-all-done.k_ref.v_ref, ...), custom_call_target="tpu_custom_call" | custom-call | flops 4294967296 | bytes 9895936 | tf_op jit(solution)/shard_map/blocks/pallas_call | solution.py:372
  179.6 5.7 %collective-permute-done.6.refs_2_ = bf16[8,144,128]{2,1,0:T(8,128)(2,1)S(1)} collective-permute-done((bf16[8,144,128]{2,1,0:T(8,128)(2,1)S(1)}, bf16[8,144,128]{2,1,0:T(8,128)(2,1)S(1)}, u32[]{:S(2)}, u32[]{:S(2)}) %collective-permute-start.6) | collective-permute-done | bytes 294944 | tf_op jit(solution)/shard_map/ppermute | solution.py:338
  185.3 7.0 %collective-permute-done.7.refs_3_ = bf16[8,144,128]{2,1,0:T(8,128)(2,1)S(1)} collective-permute-done((bf16[8,144,128]{2,1,0:T(8,128)(2,1)S(1)}, bf16[8,144,128]{2,1,0:T(8,128)(2,1)S(1)}, u32[]{:S(2)}, u32[]{:S(2)}) %collective-permute-start.7) | collective-permute-done | bytes 294944 | tf_op jit(solution)/shard_map/ppermute | solution.py:338
  198.8 4.1 %keys.2 = (bf16[4,128,256]{2,1,0:T(8,128)(2,1)S(1)}, bf16[4,128,128]{2,1,0:T(8,128)(2,1)S(1)}) custom-call(s32[1]{0:T(128)} %bitcast.8.slot, bf16[4,128,512]{2,1,0:T(8,128)(2,1)S(1)} %all-to-all-done.k_ref.v_ref, bf16[4,128,512]{2,1,0:T(8,128)(2,1)S(1)} %all-to-all-done.k_ref.v_ref, bf16[8,8,32,128]{3,2,1,0:T(8,128)(2,1)S(1)} %bitcast.66, ...), custom_call_target="tpu_custom_call" | custom-call | flops 536870912 | bytes 4620288 | tf_op jit(solution)/shard_map/keys/pallas_call | solution.py:372
  203.7 3.7 %all-to-all-start.5 = ((bf16[4,128,256]{2,1,0:T(8,128)(2,1)}), bf16[4,128,256]{2,1,0:T(8,128)(2,1)S(1)}, u32[]{:S(2)}, u32[]{:S(2)}) async-start(bf16[4,128,256]{2,1,0:T(8,128)(2,1)} %copy-done.29), calls=%async_computation.5 | async-start | bytes 524288 | tf_op jit(solution)/shard_map/all_to_all | solution.py:332
  210.0 13.9 %collective-permute-done.9.sx_ref = bf16[8,144,128]{2,1,0:T(8,128)(2,1)S(1)} collective-permute-done((bf16[8,144,128]{2,1,0:T(8,128)(2,1)}, bf16[8,144,128]{2,1,0:T(8,128)(2,1)S(1)}, u32[]{:S(2)}, u32[]{:S(2)}) %collective-permute-start.9) | collective-permute-done | bytes 294944 | tf_op jit(solution)/shard_map/ppermute | solution.py:335
  224.8 4.2 %keys.3 = (bf16[4,128,256]{2,1,0:T(8,128)(2,1)S(1)}, bf16[4,128,128]{2,1,0:T(8,128)(2,1)S(1)}) custom-call(s32[1]{0:T(128)} %bitcast.16.slot, bf16[4,128,512]{2,1,0:T(8,128)(2,1)S(1)} %all-to-all-done.k_ref.v_ref, bf16[4,128,512]{2,1,0:T(8,128)(2,1)S(1)} %all-to-all-done.k_ref.v_ref, bf16[8,8,32,128]{3,2,1,0:T(8,128)(2,1)S(1)} %bitcast.67, ...), custom_call_target="tpu_custom_call" | custom-call | flops 536870912 | bytes 4620288 | tf_op jit(solution)/shard_map/keys/pallas_call | solution.py:372
  230.4 8.1 %all_to_all.35.refs_1_ = bf16[4,128,256]{2,1,0:T(8,128)(2,1)S(1)} all-to-all(bf16[4,128,256]{2,1,0:T(8,128)(2,1)} %copy-done.30), channel_id=1, replica_groups={{0,4,8,12},{16,20,24,28},{1,5,9,13},{17,21,25,29},{2,6,10,14},{18,22,26..., dimensions={0} | all-to-all | bytes 524288 | tf_op jit(solution)/shard_map/all_to_all | solution.py:332
  238.5 3.5 %all-to-all-start.4 = ((bf16[4,128,1024]{2,1,0:T(8,128)(2,1)}), bf16[4,128,1024]{2,1,0:T(8,128)(2,1)S(1)}, u32[]{:S(2)}, u32[]{:S(2)}) async-start(bf16[4,128,1024]{2,1,0:T(8,128)(2,1)} %copy-done.15), calls=%async_computation.4 | async-start | bytes 2097152 | tf_op jit(solution)/shard_map/all_to_all | solution.py:332
  245.9 3.1 %collective-permute-done.11 = bf16[2,4,32,128]{3,2,1,0:T(8,128)(2,1)S(1)} collective-permute-done((bf16[2,4,32,128]{3,2,1,0:T(8,128)(2,1)S(1)}, bf16[2,4,32,128]{3,2,1,0:T(8,128)(2,1)S(1)}, u32[]{:S(2)}, u32[]{:S(2)}) %collective-permute-start.11) | collective-permute-done | bytes 65568 | tf_op jit(solution)/shard_map/ppermute | solution.py:338
  252.0 3.1 %all-to-all-done.4.refs_1_ = bf16[4,128,1024]{2,1,0:T(8,128)(2,1)S(1)} async-done(((bf16[4,128,1024]{2,1,0:T(8,128)(2,1)}), bf16[4,128,1024]{2,1,0:T(8,128)(2,1)S(1)}, u32[]{:S(2)}, u32[]{:S(2)}) %all-to-all-start.4) | async-done | bytes 1048608 | tf_op jit(solution)/shard_map/all_to_all | solution.py:332
  255.1 3.5 %all-to-all-start.2 = ((bf16[4,128,1024]{2,1,0:T(8,128)(2,1)}), bf16[4,128,1024]{2,1,0:T(8,128)(2,1)S(1)}, u32[]{:S(2)}, u32[]{:S(2)}) async-start(bf16[4,128,1024]{2,1,0:T(8,128)(2,1)} %copy-done.14), calls=%async_computation.2 | async-start | bytes 2097152 | tf_op jit(solution)/shard_map/all_to_all | solution.py:332
  258.7 3.1 %collective-permute-start.14 = (bf16[2,4,32,128]{3,2,1,0:T(8,128)(2,1)S(1)}, bf16[2,4,32,128]{3,2,1,0:T(8,128)(2,1)S(1)}, u32[]{:S(2)}, u32[]{:S(2)}) collective-permute-start(bf16[2,4,32,128]{3,2,1,0:T(8,128)(2,1)S(1)} %get-tuple-element.48), channel_id=1, source_target_pairs={{0,1},{1,2},{2,3},{3,0},{4,5},{5,6},{6,7},{7,4},{8,9},{9,10},{10,1... | collective-permute-start | bytes 196616 | tf_op jit(solution)/shard_map/ppermute | solution.py:338
  (134 shorter events, 70.1 us)
Async XLA Ops:
  4.6 11.5 %all-to-all-start = ((bf16[4,128,512]{2,1,0:T(8,128)(2,1)}), bf16[4,128,512]{2,1,0:T(8,128)(2,1)S(1)}, u32[]{:S(2)}, u32[]{:S(2)}) async-start(bf16[4,128,512]{2,1,0:T(8,128)(2,1)} %copy-done.9), calls=%async_computation | async-start | bytes 1048576 | tf_op jit(solution)/shard_map/all_to_all | solution.py:332
  16.1 29.7 %all-to-all-start.3 = ((bf16[4,128,2048]{2,1,0:T(8,128)(2,1)}), bf16[4,128,2048]{2,1,0:T(8,128)(2,1)}, u32[]{:S(2)}, u32[]{:S(2)}) async-start(bf16[4,128,2048]{2,1,0:T(8,128)(2,1)} %copy-done.4), calls=%async_computation.3 | async-start | bytes 4194304 | tf_op jit(solution)/shard_map/all_to_all | solution.py:332
  45.8 113.5 %all-to-all-start.1 = ((bf16[4,128,2048]{2,1,0:T(8,128)(2,1)}), bf16[4,128,2048]{2,1,0:T(8,128)(2,1)S(1)}, u32[]{:S(2)}, u32[]{:S(2)}) async-start(bf16[4,128,2048]{2,1,0:T(8,128)(2,1)} %copy-done.3), calls=%async_computation.1 | async-start | bytes 4194304 | tf_op jit(solution)/shard_map/all_to_all | solution.py:332
  87.0 15.7 %collective-permute-start = (bf16[8,144,128]{2,1,0:T(8,128)(2,1)S(1)}, bf16[8,144,128]{2,1,0:T(8,128)(2,1)S(1)}, u32[]{:S(2)}, u32[]{:S(2)}) collective-permute-start(bf16[8,144,128]{2,1,0:T(8,128)(2,1)S(1)} %states.3), channel_id=1, source_target_pairs={{0,16},{4,20},{8,24},{12,28},{16,0},{20,4},{24,8},{28,12},{1,17},{... | collective-permute-start | bytes 884744 | tf_op jit(solution)/shard_map/ppermute | solution.py:335
  104.3 7.7 %collective-permute-start.1 = (bf16[8,144,128]{2,1,0:T(8,128)(2,1)}, bf16[8,144,128]{2,1,0:T(8,128)(2,1)}, u32[]{:S(2)}, u32[]{:S(2)}) collective-permute-start(bf16[8,144,128]{2,1,0:T(8,128)(2,1)} %totals.2), channel_id=1, source_target_pairs={{0,1},{1,2},{2,3},{3,0},{4,5},{5,6},{6,7},{7,4},{8,9},{9,10},{10,1... | collective-permute-start | bytes 884744 | tf_op jit(solution)/shard_map/ppermute | solution.py:338
  105.4 14.6 %collective-permute-start.2 = (bf16[8,144,128]{2,1,0:T(8,128)(2,1)}, bf16[8,144,128]{2,1,0:T(8,128)(2,1)}, u32[]{:S(2)}, u32[]{:S(2)}) collective-permute-start(bf16[8,144,128]{2,1,0:T(8,128)(2,1)} %totals.2), channel_id=1, source_target_pairs={{0,2},{1,3},{2,0},{3,1},{4,6},{5,7},{6,4},{7,5},{8,10},{9,11},{10,... | collective-permute-start | bytes 884744 | tf_op jit(solution)/shard_map/ppermute | solution.py:338
  106.6 13.9 %collective-permute-start.3 = (bf16[8,144,128]{2,1,0:T(8,128)(2,1)}, bf16[8,144,128]{2,1,0:T(8,128)(2,1)}, u32[]{:S(2)}, u32[]{:S(2)}) collective-permute-start(bf16[8,144,128]{2,1,0:T(8,128)(2,1)} %totals.2), channel_id=1, source_target_pairs={{0,3},{1,0},{2,1},{3,2},{4,7},{5,4},{6,5},{7,6},{8,11},{9,8},{10,9... | collective-permute-start | bytes 884744 | tf_op jit(solution)/shard_map/ppermute | solution.py:338
  124.7 15.3 %collective-permute-start.4 = (bf16[8,144,128]{2,1,0:T(8,128)(2,1)S(1)}, bf16[8,144,128]{2,1,0:T(8,128)(2,1)S(1)}, u32[]{:S(2)}, u32[]{:S(2)}) collective-permute-start(bf16[8,144,128]{2,1,0:T(8,128)(2,1)S(1)} %get-tuple-element.29), channel_id=1, source_target_pairs={{0,16},{4,20},{8,24},{12,28},{16,0},{20,4},{24,8},{28,12},{1,17},{... | collective-permute-start | bytes 884744 | tf_op jit(solution)/shard_map/ppermute | solution.py:335
  159.2 16.6 %collective-permute-start.5 = (bf16[8,144,128]{2,1,0:T(8,128)(2,1)}, bf16[8,144,128]{2,1,0:T(8,128)(2,1)S(1)}, u32[]{:S(2)}, u32[]{:S(2)}) collective-permute-start(bf16[8,144,128]{2,1,0:T(8,128)(2,1)} %get-tuple-element.32), channel_id=1, source_target_pairs={{0,16},{4,20},{8,24},{12,28},{16,0},{20,4},{24,8},{28,12},{1,17},{... | collective-permute-start | bytes 884744 | tf_op jit(solution)/shard_map/ppermute | solution.py:335
  177.5 7.7 %collective-permute-start.6 = (bf16[8,144,128]{2,1,0:T(8,128)(2,1)S(1)}, bf16[8,144,128]{2,1,0:T(8,128)(2,1)S(1)}, u32[]{:S(2)}, u32[]{:S(2)}) collective-permute-start(bf16[8,144,128]{2,1,0:T(8,128)(2,1)S(1)} %totals.3), channel_id=1, source_target_pairs={{0,1},{1,2},{2,3},{3,0},{4,5},{5,6},{6,7},{7,4},{8,9},{9,10},{10,1... | collective-permute-start | bytes 884744 | tf_op jit(solution)/shard_map/ppermute | solution.py:338
  179.0 13.2 %collective-permute-start.7 = (bf16[8,144,128]{2,1,0:T(8,128)(2,1)S(1)}, bf16[8,144,128]{2,1,0:T(8,128)(2,1)S(1)}, u32[]{:S(2)}, u32[]{:S(2)}) collective-permute-start(bf16[8,144,128]{2,1,0:T(8,128)(2,1)S(1)} %totals.3), channel_id=1, source_target_pairs={{0,2},{1,3},{2,0},{3,1},{4,6},{5,7},{6,4},{7,5},{8,10},{9,11},{10,... | collective-permute-start | bytes 884744 | tf_op jit(solution)/shard_map/ppermute | solution.py:338
  179.3 13.6 %collective-permute-start.8 = (bf16[8,144,128]{2,1,0:T(8,128)(2,1)S(1)}, bf16[8,144,128]{2,1,0:T(8,128)(2,1)S(1)}, u32[]{:S(2)}, u32[]{:S(2)}) collective-permute-start(bf16[8,144,128]{2,1,0:T(8,128)(2,1)S(1)} %totals.3), channel_id=1, source_target_pairs={{0,3},{1,0},{2,1},{3,2},{4,7},{5,4},{6,5},{7,6},{8,11},{9,8},{10,9... | collective-permute-start | bytes 884744 | tf_op jit(solution)/shard_map/ppermute | solution.py:338
  203.7 26.7 %all-to-all-start.5 = ((bf16[4,128,256]{2,1,0:T(8,128)(2,1)}), bf16[4,128,256]{2,1,0:T(8,128)(2,1)S(1)}, u32[]{:S(2)}, u32[]{:S(2)}) async-start(bf16[4,128,256]{2,1,0:T(8,128)(2,1)} %copy-done.29), calls=%async_computation.5 | async-start | bytes 524288 | tf_op jit(solution)/shard_map/all_to_all | solution.py:332
  207.4 16.5 %collective-permute-start.9 = (bf16[8,144,128]{2,1,0:T(8,128)(2,1)}, bf16[8,144,128]{2,1,0:T(8,128)(2,1)S(1)}, u32[]{:S(2)}, u32[]{:S(2)}) collective-permute-start(bf16[8,144,128]{2,1,0:T(8,128)(2,1)} %copy-done.34), channel_id=1, source_target_pairs={{0,16},{4,20},{8,24},{12,28},{16,0},{20,4},{24,8},{28,12},{1,17},{... | collective-permute-start | bytes 884744 | tf_op jit(solution)/shard_map/ppermute | solution.py:335
  238.5 16.6 %all-to-all-start.4 = ((bf16[4,128,1024]{2,1,0:T(8,128)(2,1)}), bf16[4,128,1024]{2,1,0:T(8,128)(2,1)S(1)}, u32[]{:S(2)}, u32[]{:S(2)}) async-start(bf16[4,128,1024]{2,1,0:T(8,128)(2,1)} %copy-done.15), calls=%async_computation.4 | async-start | bytes 2097152 | tf_op jit(solution)/shard_map/all_to_all | solution.py:332
  242.1 3.7 %collective-permute-start.10 = (bf16[2,4,32,128]{3,2,1,0:T(8,128)(2,1)S(1)}, bf16[2,4,32,128]{3,2,1,0:T(8,128)(2,1)S(1)}, u32[]{:S(2)}, u32[]{:S(2)}) collective-permute-start(bf16[2,4,32,128]{3,2,1,0:T(8,128)(2,1)S(1)} %get-tuple-element.51), channel_id=1, source_target_pairs={{0,1},{1,2},{2,3},{3,0},{4,5},{5,6},{6,7},{7,4},{8,9},{9,10},{10,1... | collective-permute-start | bytes 196616 | tf_op jit(solution)/shard_map/ppermute | solution.py:338
  244.5 4.4 %collective-permute-start.11 = (bf16[2,4,32,128]{3,2,1,0:T(8,128)(2,1)S(1)}, bf16[2,4,32,128]{3,2,1,0:T(8,128)(2,1)S(1)}, u32[]{:S(2)}, u32[]{:S(2)}) collective-permute-start(bf16[2,4,32,128]{3,2,1,0:T(8,128)(2,1)S(1)} %get-tuple-element.52), channel_id=1, source_target_pairs={{0,2},{1,3},{2,0},{3,1},{4,6},{5,7},{6,4},{7,5},{8,10},{9,11},{10,... | collective-permute-start | bytes 196616 | tf_op jit(solution)/shard_map/ppermute | solution.py:338
  245.6 4.1 %collective-permute-start.12 = (bf16[2,4,32,128]{3,2,1,0:T(8,128)(2,1)S(1)}, bf16[2,4,32,128]{3,2,1,0:T(8,128)(2,1)S(1)}, u32[]{:S(2)}, u32[]{:S(2)}) collective-permute-start(bf16[2,4,32,128]{3,2,1,0:T(8,128)(2,1)S(1)} %get-tuple-element.53), channel_id=1, source_target_pairs={{0,3},{1,0},{2,1},{3,2},{4,7},{5,4},{6,5},{7,6},{8,11},{9,8},{10,9... | collective-permute-start | bytes 196616 | tf_op jit(solution)/shard_map/ppermute | solution.py:338
  249.7 8.9 %collective-permute-start.13 = (bf16[4,32,128]{2,1,0:T(8,128)(2,1)S(1)}, bf16[4,32,128]{2,1,0:T(8,128)(2,1)S(1)}, u32[]{:S(2)}, u32[]{:S(2)}) collective-permute-start(bf16[4,32,128]{2,1,0:T(8,128)(2,1)S(1)} %fusion.22), channel_id=1, source_target_pairs={{0,16},{4,20},{8,24},{12,28},{16,0},{20,4},{24,8},{28,12},{1,17},{... | collective-permute-start | bytes 98312 | tf_op jit(solution)/shard_map/ppermute | solution.py:335
  255.1 17.9 %all-to-all-start.2 = ((bf16[4,128,1024]{2,1,0:T(8,128)(2,1)}), bf16[4,128,1024]{2,1,0:T(8,128)(2,1)S(1)}, u32[]{:S(2)}, u32[]{:S(2)}) async-start(bf16[4,128,1024]{2,1,0:T(8,128)(2,1)} %copy-done.14), calls=%async_computation.2 | async-start | bytes 2097152 | tf_op jit(solution)/shard_map/all_to_all | solution.py:332
  258.7 4.4 %collective-permute-start.14 = (bf16[2,4,32,128]{3,2,1,0:T(8,128)(2,1)S(1)}, bf16[2,4,32,128]{3,2,1,0:T(8,128)(2,1)S(1)}, u32[]{:S(2)}, u32[]{:S(2)}) collective-permute-start(bf16[2,4,32,128]{3,2,1,0:T(8,128)(2,1)S(1)} %get-tuple-element.48), channel_id=1, source_target_pairs={{0,1},{1,2},{2,3},{3,0},{4,5},{5,6},{6,7},{7,4},{8,9},{9,10},{10,1... | collective-permute-start | bytes 196616 | tf_op jit(solution)/shard_map/ppermute | solution.py:338
  261.7 4.0 %collective-permute-start.15 = (bf16[2,4,32,128]{3,2,1,0:T(8,128)(2,1)S(1)}, bf16[2,4,32,128]{3,2,1,0:T(8,128)(2,1)S(1)}, u32[]{:S(2)}, u32[]{:S(2)}) collective-permute-start(bf16[2,4,32,128]{3,2,1,0:T(8,128)(2,1)S(1)} %get-tuple-element.49), channel_id=1, source_target_pairs={{0,2},{1,3},{2,0},{3,1},{4,6},{5,7},{6,4},{7,5},{8,10},{9,11},{10,... | collective-permute-start | bytes 196616 | tf_op jit(solution)/shard_map/ppermute | solution.py:338
  262.3 4.1 %collective-permute-start.16 = (bf16[2,4,32,128]{3,2,1,0:T(8,128)(2,1)S(1)}, bf16[2,4,32,128]{3,2,1,0:T(8,128)(2,1)S(1)}, u32[]{:S(2)}, u32[]{:S(2)}) collective-permute-start(bf16[2,4,32,128]{3,2,1,0:T(8,128)(2,1)S(1)} %get-tuple-element.50), channel_id=1, source_target_pairs={{0,3},{1,0},{2,1},{3,2},{4,7},{5,4},{6,5},{7,6},{8,11},{9,8},{10,9... | collective-permute-start | bytes 196616 | tf_op jit(solution)/shard_map/ppermute | solution.py:338
  266.5 4.4 %collective-permute-start.17 = (bf16[4,32,128]{2,1,0:T(8,128)(2,1)S(1)}, bf16[4,32,128]{2,1,0:T(8,128)(2,1)S(1)}, u32[]{:S(2)}, u32[]{:S(2)}) collective-permute-start(bf16[4,32,128]{2,1,0:T(8,128)(2,1)S(1)} %fusion.23), channel_id=1, source_target_pairs={{0,16},{4,20},{8,24},{12,28},{16,0},{20,4},{24,8},{28,12},{1,17},{... | collective-permute-start | bytes 98312 | tf_op jit(solution)/shard_map/ppermute | solution.py:335
  (37 other events, 193.3 us)

commit v3 on v2

v3 whole, which is shorter than its diff:
```python
import functools

import jax
import jax.numpy as jnp
from jax import lax
from jax.experimental import pallas as pl
from jax.experimental.pallas import tpu as pltpu
from jax.sharding import PartitionSpec as P

BLK = 512
TILE = 256
PAIR = 2
LIMIT = 40 * 1024 * 1024

F32 = jnp.float32
BF16 = jnp.bfloat16
SMEM = pltpu.SMEM


def nn(left, right):
    return lax.dot_general(left, right, (((1,), (0,)), ((), ())), preferred_element_type=F32)


def nt(left, right):
    return lax.dot_general(left, right, (((1,), (1,)), ((), ())), preferred_element_type=F32)


def turned(array):
    return array.astype(F32).T.astype(array.dtype)


def column(row, width):
    n = row.shape[1]
    square = jnp.broadcast_to(row, (n, n)).T
    return jnp.concatenate([square] * (width // n), axis=1)


def pick(ref, weights, slot, blocks, before):
    heads = ref.shape[1] // (ref.shape[0] // blocks + 1 if before else ref.shape[0] // blocks)
    groups = ref.shape[0] // blocks
    total = jnp.zeros((heads, ref.shape[2]), F32)
    for i in range(ref.shape[0]):
        at = lax.rem(slot + groups - i // blocks, groups) * heads
        total = total + weights[i] * ref[i, pl.ds(pl.multiple_of(at, heads), heads), :]
    if before:
        total = total + ref[slot * blocks, groups * heads :, :]
    return total


def weight_rows(ref, u):
    whole = jnp.concatenate([ref[i, u] for i in range(ref.shape[0])], axis=0)
    return turned(whole)


def features(weight, rows):
    logits = nt(weight, rows).astype(BF16).astype(F32)
    upper = jnp.exp(logits)
    lower = jnp.exp(-logits)
    upper = upper * (1.0 / jnp.sum(upper, axis=0, keepdims=True))
    lower = lower * (1.0 / jnp.sum(lower, axis=0, keepdims=True))
    return jnp.concatenate([upper, lower], axis=0)


def feature_back(feats, upstream):
    half = feats.shape[0] // 2
    weighted = feats * upstream
    first, second = weighted[:half], weighted[half:]
    first = first - feats[:half] * jnp.sum(first, axis=0, keepdims=True)
    second = second - feats[half:] * jnp.sum(second, axis=0, keepdims=True)
    return (first - second).astype(BF16)


def flat(ref):
    return ref[...].reshape(-1, ref.shape[-1])


def pack_kernel(columns, table, *refs):
    sources, out = refs[:-1], refs[-1]
    width = sources[0].shape[1]
    for i, source in enumerate(sources):
        out[0, :, i * width : (i + 1) * width] = source[...]


def pack(table, sources, pieces, columns, width):
    rows = sources[0].shape[0]
    count = columns * len(sources)

    def take(s):
        return pl.BlockSpec((rows, width), lambda i, t: (0, t[s * pieces + i]))

    return pl.pallas_call(
        functools.partial(pack_kernel, columns),
        out_shape=jax.ShapeDtypeStruct((pieces, rows, count * width), sources[0].dtype),
        grid_spec=pltpu.PrefetchScalarGridSpec(
            num_scalar_prefetch=1,
            grid=(pieces,),
            in_specs=[take(s) for s in range(columns) for _ in sources],
            out_specs=pl.BlockSpec((1, rows, count * width), lambda i, t: (i, 0, 0)),
        ),
        compiler_params=pltpu.CompilerParams(vmem_limit_bytes=LIMIT),
        cost_estimate=pl.CostEstimate(
            flops=0, bytes_accessed=4 * pieces * rows * count * width, transcendentals=0
        ),
        name="pack",
    )(table, *(list(sources) * columns))


def unpack_kernel(outputs, table, *refs):
    sources, outs = refs[:-outputs], refs[-outputs:]
    for s, source in enumerate(sources):
        pieces = source.shape[0]
        width = source.shape[2] // outputs
        for r in range(pieces):
            at = pl.ds(pl.multiple_of(table[s * pieces + r] * width, width), width)
            for i, out in enumerate(outs):
                out[:, at] = source[r, :, i * width : (i + 1) * width]


def unpack(table, sources, outputs, width):
    pieces, rows = sources[0].shape[:2]
    total = len(sources) * pieces * width
    step = rows // 2
    return pl.pallas_call(
        functools.partial(unpack_kernel, outputs),
        out_shape=[jax.ShapeDtypeStruct((rows, total), sources[0].dtype)] * outputs,
        grid=(rows // step,),
        in_specs=[pl.BlockSpec(memory_space=SMEM)]
        + [pl.BlockSpec((pieces, step, outputs * width), lambda i: (0, i, 0))] * len(sources),
        out_specs=[pl.BlockSpec((step, total), lambda i: (i, 0))] * outputs,
        compiler_params=pltpu.CompilerParams(vmem_limit_bytes=LIMIT),
        cost_estimate=pl.CostEstimate(
            flops=0, bytes_accessed=4 * rows * total * outputs, transcendentals=0
        ),
        name="unpack",
    )(table, *sources)


def place(step, u):
    return pl.ds(step * PAIR + u, 1)


def state_kernel(slot, k_ref, v_ref, w_ref, out, norm_ref):
    k_all, v_all = flat(k_ref), flat(v_ref)
    step = pl.program_id(0)
    for u in range(PAIR):
        weight = weight_rows(w_ref, u)
        feats = features(weight[weight.shape[0] // 2 :], k_all).astype(BF16)
        out[u] = nn(feats, v_all).astype(BF16)
        ones = jnp.ones((8, feats.shape[1]), BF16)
        norm_ref[place(step, u), :] = nt(ones, feats)[:1]


def tiles_of(j):
    return range(j * (j + 1) // 2, (j + 1) * (j + 2) // 2)


def causal(array, begin):
    earlier = lax.broadcasted_iota(jnp.int32, (TILE, TILE), 0) <= lax.broadcasted_iota(
        jnp.int32, (TILE, TILE), 1
    )
    masked = jnp.where(earlier, array[begin:], 0.0)
    return masked if begin == 0 else jnp.concatenate([array[:begin], masked], axis=0)


def front_kernel(
    fsdp, slot, k_ref, q_ref, g_ref, w_ref, norms_ref, weights,
    qf_ref, kf_ref, scaled_ref, sc_ref, inv_ref, norm_ref, sx_ref,
):
    k_all, q_all, g_all = flat(k_ref), flat(q_ref), flat(g_ref)
    hd = k_all.shape[1]
    step = pl.program_id(0)

    @pl.when(step == 0)
    def _():
        norm_ref[...] = pick(norms_ref, weights, slot[0], fsdp, True)

    for u in range(PAIR):
        weight = weight_rows(w_ref, u)
        half = weight.shape[0] // 2
        lanes = slice(u * hd, (u + 1) * hd)
        q_feat = features(weight[:half], q_all[:, lanes])
        k_low = features(weight[half:], k_all).astype(BF16)
        qf_ref[u] = q_feat
        kf_ref[u] = k_low
        q_low = q_feat.astype(BF16)
        k_turned = turned(k_low)
        norm = column(norm_ref[place(step, u), :], TILE)
        g_turned = g_all[:, lanes].astype(F32).T
        suffix = jnp.zeros((2 * half, hd), F32)
        for j in range(BLK // TILE):
            begin, end = j * TILE, (j + 1) * TILE
            own = q_low[:, begin:end]
            scores = causal(nn(k_turned[:end], own), begin)
            for i, tile in enumerate(tiles_of(j)):
                sc_ref[u, tile] = scores[i * TILE : (i + 1) * TILE].astype(BF16)
            denominator = jnp.sum(own.astype(F32) * norm, axis=0, keepdims=True) + jnp.sum(
                scores, axis=0, keepdims=True
            )
            inverse = 1.0 / denominator
            inv_ref[place(step, u), begin:end] = inverse
            scaled = g_turned[:, begin:end] * inverse
            scaled_ref[u, :, begin:end] = scaled
            suffix = suffix + nt(own, scaled.astype(BF16))
        sx_ref[u] = suffix.astype(BF16)


def back_kernel(
    slot, k_ref, v_ref, q_ref, w_ref, qf_ref, kf_ref, scaled_ref, sc_ref, inv_ref, norm_ref, st_ref,
    gq_ref, dk_ref, dv_ref, sn_ref, gm_ref, vt_all,
):
    v_all, q_all = flat(v_ref), flat(q_ref)
    hd = v_all.shape[1]
    step = pl.program_id(0)

    @pl.when(step == 0)
    def _():
        vt_all[...] = turned(v_all)
        dv_ref[...] = jnp.zeros_like(dv_ref)

    maps = []
    for u in range(PAIR):
        half = w_ref.shape[3] // 2
        weight = weight_rows(w_ref, u)
        lanes = slice(u * hd, (u + 1) * hd)
        q_feat = qf_ref[u]
        k_low = kf_ref[u]
        state = st_ref[u]
        state_turned = turned(state)
        norm = column(norm_ref[place(step, u), :], TILE)
        back = []
        dkey = [jnp.zeros((2 * half, TILE), F32) for _ in range(BLK // TILE)]
        dvalue = [jnp.zeros((hd, TILE), F32) for _ in range(BLK // TILE)]
        suffix_norm = jnp.zeros((2 * half, 1), F32)
        for j in range(BLK // TILE):
            begin, end = j * TILE, (j + 1) * TILE
            own = q_feat[:, begin:end].astype(BF16)
            scores_low = [sc_ref[u, tile] for tile in tiles_of(j)]
            numerator = nn(state_turned, own) + nn(
                vt_all[:, :end], jnp.concatenate(scores_low, axis=0)
            )
            inverse = inv_ref[place(step, u), begin:end]
            scaled = scaled_ref[u, :, begin:end]
            scaled_low = scaled.astype(BF16)
            norm_grad = -jnp.sum(scaled * (numerator * inverse), axis=0, keepdims=True)
            dscores = causal(nn(v_all[:end], scaled_low) + norm_grad, begin).astype(BF16)
            dquery = nn(state, scaled_low) + norm * norm_grad + nn(k_low[:, :end], dscores)
            back.append(feature_back(q_feat[:, begin:end], dquery))
            for i in range(j + 1):
                dkey[i] = dkey[i] + nt(own, dscores[i * TILE : (i + 1) * TILE])
                dvalue[i] = dvalue[i] + nt(scaled_low, scores_low[i])
            suffix_norm = suffix_norm + jnp.sum(
                own.astype(F32) * norm_grad, axis=1, keepdims=True
            )
        dlog = jnp.concatenate(back, axis=1)
        grads = nn(turned(dlog), weight[:half]).astype(BF16)
        gq_ref[:, :, lanes] = grads.reshape(gq_ref.shape[0], -1, hd)
        maps.append(nn(dlog, q_all[:, lanes]))
        dk_ref[u] = jnp.concatenate(dkey, axis=1)
        dv_ref[...] += jnp.concatenate(dvalue, axis=1)
        sn_ref[place(step, u), :] = jnp.broadcast_to(suffix_norm, (2 * half, 2 * half)).T[:1]
    gm_ref[0] = jnp.concatenate(maps, axis=0).T.astype(gm_ref.dtype)


def key_kernel(
    fsdp, slot, k_ref, v_ref, w_ref, sx_ref, dk_ref, dv_ref, norms_ref, weights, _,
    out, gm_ref, vt_all, total, logs, all_weights, norm_all,
):
    k_all, v_all = flat(k_ref), flat(v_ref)
    hd = k_all.shape[1]
    step = pl.program_id(0)

    @pl.when(step == 0)
    def _():
        vt_all[...] = turned(v_all)
        total[...] = dv_ref[...]
        norm_all[...] = pick(norms_ref, weights, slot[0], fsdp, False)

    maps = []
    for u in range(PAIR):
        weight = weight_rows(w_ref, u)
        half = weight.shape[0] // 2
        weight = weight[half:]
        feats = features(weight, k_all)
        suffix = sx_ref[u]
        norm = column(norm_all[place(step, u), :], BLK)
        dlog = feature_back(feats, dk_ref[u] + nn(suffix, vt_all[...]) + norm)
        at = pl.ds(pl.multiple_of((step * PAIR + u) * half, half), half)
        logs[at, :] = dlog
        all_weights[at, :] = weight
        maps.append(nn(dlog, k_all))
        total[...] += nn(turned(suffix), feats.astype(BF16))
    gm_ref[0] = jnp.concatenate(maps, axis=0).T.astype(gm_ref.dtype)

    @pl.when(step == pl.num_programs(0) - 1)
    def _():
        pair = jnp.concatenate([nn(turned(logs[...]), all_weights[...]), total[...].T], axis=1)
        out[...] = pair.astype(out.dtype).reshape(out.shape)


def total_kernel(*refs):
    for h in range(refs[-1].shape[0]):
        refs[-1][h] = sum(ref[h].astype(F32) for ref in refs[:-1]).astype(BF16)


def spread_kernel(grp, others, closing, block_weight, total_weight, at, *refs):
    parts, totals, refs = refs[:grp], refs[grp : grp + others], refs[grp + others :]
    if closing:
        outs, grad, scratch = refs[:grp], refs[grp], refs[grp + 1]
    else:
        state_ref, outs = refs[0], refs[1:]
    for h in range(parts[0].shape[0]):
        states = [ref[h].astype(F32) for ref in parts]
        others_state = [ref[h].astype(F32) for ref in totals]
        if closing:
            base = jnp.zeros_like(states[0])
            scratch[...] = sum(states) + sum(others_state)
            rows = grad.shape[1]
            grad[h] = scratch[pl.ds(pl.multiple_of(at[0] * rows, rows), rows), :]
        else:
            base = state_ref[h]
        for i, state in enumerate(others_state):
            base = base + total_weight[i] * state
        for r, out in enumerate(outs):
            state = base
            for i in range(grp):
                if i != r:
                    state = state + block_weight[r * grp + i] * states[i]
            out[h] = state.astype(BF16)


def close_kernel(pairs, singles, at, q_ref, k_ref, *refs):
    both, q_parts, k_parts = (
        refs[:pairs],
        refs[pairs : pairs + singles],
        refs[pairs + singles : pairs + 2 * singles],
    )
    for i, (own, parts, out) in enumerate(
        ((q_ref, q_parts, refs[-2]), (k_ref, k_parts, refs[-1]))
    ):
        rows, half = out.shape[1:]
        mine = pl.ds(pl.multiple_of(at[0] * rows, rows), rows)
        for h in range(own.shape[0]):
            total = own[h, mine, :].astype(F32)
            for ref in both:
                total = total + ref[i, h].astype(F32)
            for ref in parts:
                total = total + ref[h].astype(F32)
            for u in range(PAIR):
                out[h * PAIR + u] = total[:, u * half : (u + 1) * half]


def whole_call(kernel, outs, smem, arrays, name, scratch=()):
    total = sum(a.size * a.dtype.itemsize for a in (*arrays, *outs))
    return pl.pallas_call(
        kernel,
        out_shape=outs,
        in_specs=[pl.BlockSpec(memory_space=SMEM)] * len(smem)
        + [pl.BlockSpec(memory_space=pltpu.VMEM)] * len(arrays),
        out_specs=[pl.BlockSpec(memory_space=pltpu.VMEM)] * len(outs),
        scratch_shapes=list(scratch),
        compiler_params=pltpu.CompilerParams(vmem_limit_bytes=LIMIT),
        cost_estimate=pl.CostEstimate(flops=total, bytes_accessed=total, transcendentals=0),
        name=name,
    )(*smem, *arrays)


def after(value, *others):
    return lax.optimization_barrier((value, *others))[0]


def shards(
    query_rows, key_rows, value_rows, grad_out, query_map, key_map, prefix_state, prefix_norm
):
    ctx, fsdp = lax.axis_size("ctx"), lax.axis_size("fsdp")
    tok = query_rows.shape[0]
    heads, map_rows, half = query_map.shape
    hd = map_rows * fsdp
    kv_heads = key_rows.shape[1] // hd
    replicas = ctx // kv_heads
    part = BLK // tok
    grp = ctx // part
    mine = lax.axis_index("ctx")
    block, seq = mine // part, lax.axis_index("fsdp")
    slots = range(grp)
    order = list(reversed(slots))
    grid = (heads // PAIR,)

    blocks_of = [[g * part + p for p in range(part)] for g in slots]
    owners_of = [
        [(g * part + p) * fsdp + i for g in slots for i in range(fsdp)] for p in range(part)
    ]

    def within(array):
        return lax.all_to_all(array, "ctx", 0, 0, axis_index_groups=blocks_of, tiled=True)

    def across(array, shift):
        return lax.ppermute(array, "ctx", [(d, (d + shift * part) % ctx) for d in range(ctx)])

    def along(array, shift):
        return lax.ppermute(array, "fsdp", [(d, (d + shift) % fsdp) for d in range(fsdp)])

    def apart(array, s, r):
        moves = [
            (d * fsdp + i, (d + s * part) % ctx * fsdp + (i + r) % fsdp)
            for d in range(ctx)
            for i in range(fsdp)
        ]
        return lax.ppermute(array, ("ctx", "fsdp"), moves)

    def gathered(array):
        return lax.all_gather(array, ("ctx", "fsdp"), axis_index_groups=owners_of)

    def ints(values):
        return jnp.stack([jnp.asarray(v, jnp.int32) for v in values])

    def flags(values):
        return jnp.stack([v.astype(F32) for v in values])

    slot = {s: (block + s) % grp for s in slots}
    owner = {s: [slot[s] * part + p for p in range(part)] for s in slots}
    place_of = [(g, i) for g in slots for i in range(fsdp)]
    earlier = flags([i * grp + g < seq * grp + block for g, i in place_of])
    later = flags([i * grp + g > seq * grp + block for g, i in place_of])

    own_maps = jnp.concatenate((query_map, key_map), axis=-1)
    maps = jnp.stack([own_maps] + [across(own_maps, -s) for s in slots[1:]])
    kv_table = ints([c // replicas for s in slots for c in owner[s]])
    kv = within(pack(kv_table, (key_rows, value_rows), part, grp, hd))
    maps = lax.all_gather(maps, "fsdp")

    params = pltpu.CompilerParams(
        dimension_semantics=("arbitrary",), vmem_limit_bytes=LIMIT
    )
    in_smem = pl.BlockSpec(memory_space=SMEM)
    anywhere = pl.BlockSpec(memory_space=pl.ANY)

    def piece_spec(column, count):
        return pl.BlockSpec((part, tok, count * hd), lambda h, t: (0, 0, column(h)))

    def head_spec(*shape):
        return pl.BlockSpec((PAIR, *shape), lambda h, t: (h,) + (0,) * len(shape))

    def fixed_spec(*shape):
        return pl.BlockSpec(shape, lambda h, t: (0,) * len(shape))

    def of(dtype, *shape):
        return jax.ShapeDtypeStruct(shape, dtype)

    def k_spec(s):
        return piece_spec(lambda h: 2 * s, 1)

    def v_spec(s):
        return piece_spec(lambda h: 2 * s + 1, 1)

    def map_spec(s):
        return pl.BlockSpec((fsdp, None, PAIR, map_rows, 2 * half), lambda h, t: (0, s, h, 0, 0))

    q_spec, g_spec = piece_spec(lambda h: h, PAIR), piece_spec(lambda h: grid[0] + h, PAIR)
    state_spec, state_shape = head_spec(hd, hd), of(BF16, heads, hd, hd)
    row_spec, row_shape = fixed_spec(heads, hd), of(F32, heads, hd)
    wide_spec, wide_shape = head_spec(2 * half, BLK), of(F32, heads, 2 * half, BLK)
    gm_spec = pl.BlockSpec((1, hd, PAIR * half), lambda h, t: (h, 0, 0))
    gm_shape = of(BF16, heads // PAIR, hd, PAIR * half)
    dv_spec, dv_shape = fixed_spec(hd, BLK), of(F32, hd, BLK)
    count = tiles_of(BLK // TILE - 1)[-1] + 1
    unit = 2 * heads * BLK * hd

    def call(kernel, s, outs, specs, out_specs, arrays, scratch, name, flops, alias=()):
        moved = sum(a.size * a.dtype.itemsize for a in (*arrays, *outs))
        return pl.pallas_call(
            kernel,
            out_shape=outs,
            grid_spec=pltpu.PrefetchScalarGridSpec(
                num_scalar_prefetch=1,
                grid=grid,
                in_specs=specs,
                out_specs=out_specs,
                scratch_shapes=scratch,
            ),
            compiler_params=params,
            cost_estimate=pl.CostEstimate(flops=flops, bytes_accessed=moved, transcendentals=0),
            input_output_aliases=dict(alias),
            name=name,
        )(ints([slot[s]]), *arrays)

    def scan(partial, before, extra, closing):
        parts = [partial[0]] + [across(partial[s], s) for s in slots[1:]]
        (total,) = whole_call(total_kernel, [state_shape], [], parts, "totals")
        others = [along(total, r) for r in range(1, fsdp)]
        blocks = [(block - r) % grp for r in slots]
        block_weight = flags([before(b, a) for a in blocks for b in blocks])
        total_weight = flags([before((seq - r) % fsdp, seq) for r in range(1, fsdp)])
        result = whole_call(
            functools.partial(spread_kernel, grp, fsdp - 1, closing),
            [state_shape] * grp + [of(F32, heads, map_rows, hd)] * closing,
            [block_weight, total_weight, ints([seq])],
            parts + others + extra,
            "spread",
            [pltpu.VMEM((hd, hd), F32)] * closing,
        )
        return [result[0]] + [across(result[s], -s) for s in slots[1:]], result[grp:]

    rows, partial, norm = {}, {}, {}
    for s in order:
        table, sources = ints(owner[s]), (query_rows, grad_out)
        if s != order[0]:
            table = after(table, *partial.values())
        else:
            table = after(table, kv)
        rows[s] = within(pack(table, sources, part, 1, heads * hd))
        if s == order[0]:
            for i in order:
                partial[i], norm[i] = call(
                    state_kernel,
                    i,
                    [state_shape, row_shape],
                    [k_spec(i), v_spec(i), map_spec(i)],
                    [state_spec, row_spec],
                    [kv, kv, maps],
                    [],
                    "states",
                    unit * 2 * hd,
                )
            norms = gathered(jnp.concatenate([norm[i] for i in slots] + [prefix_norm], axis=0))
    state, _ = scan(partial, lambda a, b: a < b, [prefix_state], False)

    def front_of(s):
        return call(
            functools.partial(front_kernel, fsdp),
            s,
            [
                wide_shape,
                of(BF16, heads, 2 * half, BLK),
                of(F32, heads, hd, BLK),
                of(BF16, heads, count, TILE, TILE),
                of(F32, heads, BLK),
                row_shape,
                state_shape,
            ],
            [k_spec(s), q_spec, g_spec, map_spec(s), fixed_spec(*norms.shape), in_smem],
            [
                wide_spec,
                wide_spec,
                wide_spec,
                head_spec(count, TILE, TILE),
                fixed_spec(heads, BLK),
                row_spec,
                state_spec,
            ],
            [kv, rows[s], rows[s], maps, norms, earlier],
            [],
            "front",
            unit * 3 * BLK,
        )

    def back_of(s):
        return call(
            back_kernel,
            s,
            [of(BF16, part, tok, heads * hd), wide_shape, dv_shape, row_shape, gm_shape],
            [
                k_spec(s),
                v_spec(s),
                q_spec,
                map_spec(s),
                wide_spec,
                wide_spec,
                wide_spec,
                head_spec(count, TILE, TILE),
                fixed_spec(heads, BLK),
                row_spec,
                state_spec,
            ],
            [q_spec, wide_spec, dv_spec, row_spec, gm_spec],
            [kv, kv, rows[s], maps, *fronts[s][:6], state[s]],
            [pltpu.VMEM((hd, BLK), BF16)],
            "back",
            unit * 6 * BLK,
        )

    def rows_for(array, device):
        pieces = array.reshape(*array.shape[:-2], fsdp, map_rows, array.shape[-1])
        return lax.dynamic_index_in_dim(pieces, device % fsdp, array.ndim - 2, keepdims=False)

    fronts = {s: front_of(s) for s in order}
    suffix, (grad_prefix,) = scan(
        {s: fronts[s][6] for s in slots}, lambda a, b: a > b, [], True
    )
    backs, returned, q_maps = {}, {}, []
    for s in order:
        backs[s] = back_of(s)
        returned[s] = within(backs[s][0])
        if s:
            q_maps += [apart(rows_for(backs[s][4], seq + r), s, r) for r in range(fsdp)]
    suffix_norms = gathered(jnp.concatenate([backs[s][3] for s in slots], axis=0))

    kv_type = BF16 if replicas == 1 else F32
    pairs = jnp.zeros((part, tok, grp * 2 * hd), kv_type)
    k_maps, both_maps, key_gm = [], [], {}
    for s in slots:
        if s == 0:
            suffix[s] = after(suffix[s], *[returned[i] for i in slots[1:]], *q_maps)
        pairs, key_gm[s] = call(
            functools.partial(key_kernel, fsdp),
            s,
            [of(kv_type, *pairs.shape), gm_shape],
            [k_spec(s), v_spec(s), map_spec(s), state_spec, wide_spec, dv_spec]
            + [fixed_spec(*suffix_norms.shape), in_smem, anywhere],
            [piece_spec(lambda h: s, 2), gm_spec],
            [kv, kv, maps, suffix[s], backs[s][1], backs[s][2], suffix_norms, later, pairs],
            [
                pltpu.VMEM((hd, BLK), BF16),
                pltpu.VMEM((hd, BLK), F32),
                pltpu.VMEM((heads * half, BLK), BF16),
                pltpu.VMEM((heads * half, hd), BF16),
                pltpu.VMEM((heads, hd), F32),
            ],
            "keys",
            unit * 4 * hd,
            {9: 0},
        )
        if s == 0:
            two = jnp.stack([backs[s][4], key_gm[s]])
            both_maps = [along(rows_for(two, seq + r), r) for r in range(1, fsdp)]
        else:
            k_maps += [apart(rows_for(key_gm[s], seq + r), s, r) for r in range(fsdp)]

    table = ints([c for s in slots for c in owner[s]])
    pairs = after(pairs, *returned.values())
    pairs = within(pairs)
    (grad_queries,) = unpack(table, [returned[s] for s in slots], 1, heads * hd)
    pairs = [pairs[:, :, s * 2 * hd : (s + 1) * 2 * hd] for s in slots]
    grad_keys, grad_values = unpack(table, pairs, 2, hd)
    if replicas > 1:
        grad_keys, grad_values = (
            jnp.sum(a.reshape(tok, kv_heads, replicas, hd), axis=2)
            .astype(BF16)
            .reshape(tok, kv_heads * hd)
            for a in (grad_keys, grad_values)
        )
    query_map_grad, key_map_grad = whole_call(
        functools.partial(close_kernel, len(both_maps), len(q_maps)),
        [of(F32, heads, map_rows, half)] * 2,
        [ints([seq])],
        [backs[0][4], key_gm[0]] + both_maps + q_maps + k_maps,
        "close",
    )
    return grad_queries, grad_keys, grad_values, query_map_grad, key_map_grad, grad_prefix


def solution(mesh):
    rows, maps = P(("fsdp", "ctx"), None), P("ctx", "fsdp", None)
    return jax.shard_map(
        shards,
        mesh=mesh,
        in_specs=(rows,) * 4 + (maps, maps, P("ctx", None, None), P("ctx", None)),
        out_specs=(rows,) * 3 + (maps,) * 3,
        check_vma=False,
    )
```

time: 279 us -> 296 us (1.061)
  starting transfers between devices: 43.1 us -> 55.7 us
  Pallas kernels: 54.3 us -> 62.8 us
  waiting for transfers between devices: 105 us -> 97.3 us
  blocking collectives: 42.7 us -> 49.6 us
    ppermute x6 -> x5, waiting for transfers between devices: 42.1 us -> 64.7 us  [across(): lax.ppermute(array, 'ctx', [(d, (d + shift * part) % ctx) for d in range(...]
    all_to_all x6, waiting for transfers between devices: 27.5 us -> 7.09 us  [within(): lax.all_to_all(array, 'ctx', 0, 0, axis_index_groups=blocks_of, tiled=True)]
    all_gather x1 -> x3, blocking collectives: 34.6 us -> 49.6 us  [the longest x2 40.1 us: gathered(): return lax.all_gather(array, ('ctx', 'fsdp'), axis_index_groups=owners_of)]
    ppermute x12 -> x9, waiting for transfers between devices: 35.1 us -> 23.1 us  [along(): lax.ppermute(array, 'fsdp', [(d, (d + shift) % fsdp) for d in range(fsdp)])]
    ppermute x0 -> x8, starting transfers between devices: none -> 10.7 us  [apart(): return lax.ppermute(array, ('ctx', 'fsdp'), moves)]
    all_to_all x1 -> x0, blocking collectives: 8.14 us -> none  [within(): lax.all_to_all(array, 'ctx', 0, 0, axis_index_groups=blocks_of, tiled=True)]
    pallas_call x6 -> x8, Pallas kernels: 43.8 us -> 50.8 us  [call(): pl.pallas_call(kernel, out_shape=outs, grid_spec=pltpu.PrefetchScalarGrid...]
    all_to_all x6, starting transfers between devices: 23.2 us -> 27.8 us  [within(): lax.all_to_all(array, 'ctx', 0, 0, axis_index_groups=blocks_of, tiled=True)]
  transfers between devices with their start and end apart: 24 -> 28, of which waited for: 19 -> 12; matrix products, arithmetic and copies ran while one was open for 1% -> 1% of each run, Pallas kernels for 17% -> 20%
where the time goes in v3:
time: 296 us; the launch traced here: 294 us
  waiting for transfers between devices  97.3 us (33%)
  Pallas kernels  62.8 us (21%)
  starting transfers between devices  55.7 us (19%)
  blocking collectives  49.6 us (17%)
  local copies, waits for them, and re-layouts  26.4 us (9%)
    ppermute x5, waiting for transfers between devices, across(): lax.ppermute(array, 'ctx', [(d, (d + shift * part) % ctx) for d in range(...  64.7 us
    pallas_call x8, Pallas kernels, call(): pl.pallas_call(kernel, out_shape=outs, grid_spec=pltpu.PrefetchScalarGrid...  50.8 us
    all_gather x2, blocking collectives, gathered(): return lax.all_gather(array, ('ctx', 'fsdp'), axis_index_groups=owners_of)  40.1 us
    all_to_all x6, starting transfers between devices, within(): lax.all_to_all(array, 'ctx', 0, 0, axis_index_groups=blocks_of, tiled=True)  27.8 us
    ppermute x9, waiting for transfers between devices, along(): lax.ppermute(array, 'fsdp', [(d, (d + shift) % fsdp) for d in range(fsdp)])  23.1 us
    unnamed x64, local copies, waits for them, and re-layouts  22.8 us
    ppermute x8, starting transfers between devices, apart(): return lax.ppermute(array, ('ctx', 'fsdp'), moves)  10.7 us
    all_gather x1, blocking collectives, shards(): maps = lax.all_gather(maps, 'fsdp')  9.47 us
  transfers between devices with their start and end apart: 28, of which 12 were waited for; matrix products, arithmetic and copies ran while one was open for 1% of the time, Pallas kernels for 20%

profile of v3, /device:TPU:1, one launch (start us, length us, event | category | flops | bytes accessed | tf_op | source)
XLA Modules:
  0.0 294.0 jit_solution(2012491438207493814)
XLA Ops:
  4.6 4.4 %all-to-all-start = ((bf16[4,128,512]{2,1,0:T(8,128)(2,1)}), bf16[4,128,512]{2,1,0:T(8,128)(2,1)S(1)}, u32[]{:S(2)}, u32[]{:S(2)}) async-start(bf16[4,128,512]{2,1,0:T(8,128)(2,1)} %copy-done.7), calls=%async_computation | async-start | bytes 1048576 | tf_op jit(solution)/shard_map/all_to_all | solution.py:394
  9.0 7.1 %all-to-all-done.k_ref.v_ref = bf16[4,128,512]{2,1,0:T(8,128)(2,1)S(1)} async-done(((bf16[4,128,512]{2,1,0:T(8,128)(2,1)}), bf16[4,128,512]{2,1,0:T(8,128)(2,1)S(1)}, u32[]{:S(2)}, u32[]{:S(2)}) %all-to-all-start) | async-done | bytes 524320 | tf_op jit(solution)/shard_map/all_to_all | solution.py:394
  20.0 4.6 %all-to-all-start.3 = ((bf16[4,128,2048]{2,1,0:T(8,128)(2,1)}), bf16[4,128,2048]{2,1,0:T(8,128)(2,1)}, u32[]{:S(2)}, u32[]{:S(2)}) async-start(bf16[4,128,2048]{2,1,0:T(8,128)(2,1)} %copy-done.4), calls=%async_computation.3 | async-start | bytes 4194304 | tf_op jit(solution)/shard_map/all_to_all | solution.py:394
  27.2 19.9 %collective-permute-done = bf16[8,32,128]{2,1,0:T(8,128)(2,1)S(1)} collective-permute-done((bf16[8,32,128]{2,1,0:T(8,128)(2,1)S(1)}, bf16[8,32,128]{2,1,0:T(8,128)(2,1)S(1)}, u32[]{:S(2)}, u32[]{:S(2)}) %collective-permute-start) | collective-permute-done | bytes 65568 | tf_op jit(solution)/shard_map/ppermute | solution.py:397
  47.2 9.5 %all-gather = bf16[8,8,32,128]{3,2,1,0:T(8,128)(2,1)S(1)} all-gather(bf16[2,8,32,128]{3,2,1,0:T(8,128)(2,1)S(1)} %pad_maximum_fusion), channel_id=2, replica_groups=mesh['ctx'=8,'fsdp'=4] {'fsdp'}, dimensions={0}, use_global_device_ids=true | all-gather | bytes 655360 | tf_op jit(solution)/shard_map/all_gather | solution.py:429
  65.3 6.8 %all-to-all-start.1 = ((bf16[4,128,2048]{2,1,0:T(8,128)(2,1)}), bf16[4,128,2048]{2,1,0:T(8,128)(2,1)S(1)}, u32[]{:S(2)}, u32[]{:S(2)}) async-start(bf16[4,128,2048]{2,1,0:T(8,128)(2,1)} %copy-done.3), calls=%async_computation.1 | async-start | bytes 4194304 | tf_op jit(solution)/shard_map/all_to_all | solution.py:394
  72.1 28.4 %collective-permute-done.1.refs_1_ = bf16[8,128,128]{2,1,0:T(8,128)(2,1)S(1)} collective-permute-done((bf16[8,128,128]{2,1,0:T(8,128)(2,1)}, bf16[8,128,128]{2,1,0:T(8,128)(2,1)S(1)}, u32[]{:S(2)}, u32[]{:S(2)}) %collective-permute-start.1) | collective-permute-done | bytes 262176 | tf_op jit(solution)/shard_map/ppermute | solution.py:397
  104.6 4.7 %collective-permute-done.2.refs_2_ = bf16[8,128,128]{2,1,0:T(8,128)(2,1)} collective-permute-done((bf16[8,128,128]{2,1,0:T(8,128)(2,1)}, bf16[8,128,128]{2,1,0:T(8,128)(2,1)}, u32[]{:S(2)}, u32[]{:S(2)}) %collective-permute-start.2) | collective-permute-done | bytes 262176 | tf_op jit(solution)/shard_map/ppermute | solution.py:400
  109.2 7.0 %collective-permute-done.3.refs_3_ = bf16[8,128,128]{2,1,0:T(8,128)(2,1)} collective-permute-done((bf16[8,128,128]{2,1,0:T(8,128)(2,1)}, bf16[8,128,128]{2,1,0:T(8,128)(2,1)}, u32[]{:S(2)}, u32[]{:S(2)}) %collective-permute-start.3) | collective-permute-done | bytes 262176 | tf_op jit(solution)/shard_map/ppermute | solution.py:400
  120.9 3.0 %collective-permute-start.5 = (bf16[8,128,128]{2,1,0:T(8,128)(2,1)S(1)}, bf16[8,128,128]{2,1,0:T(8,128)(2,1)S(1)}, u32[]{:S(2)}, u32[]{:S(2)}) collective-permute-start(bf16[8,128,128]{2,1,0:T(8,128)(2,1)S(1)} %get-tuple-element.71), channel_id=1, source_target_pairs={{0,16},{4,20},{8,24},{12,28},{16,0},{20,4},{24,8},{28,12},{1,17},{... | collective-permute-start | bytes 786440 | tf_op jit(solution)/shard_map/ppermute | solution.py:397
  123.9 20.3 %all-gather.1 = f32[192,128]{1,0:T(8,128)S(1)} all-gather(f32[24,128]{1,0:T(8,128)S(1)} %pad_maximum_fusion.2), channel_id=3, replica_groups={{0,1,2,3,16,17,18,19},{4,5,6,7,20,21,22,23},{8,9,10,11,24,25,26,27},{12..., dimensions={0}, use_global_device_ids=true | all-gather | bytes 110592 | tf_op jit(solution)/shard_map/all_gather | solution.py:411
  144.1 7.7 %front.3 = (f32[8,128,512]{2,1,0:T(8,128)S(1)}, bf16[8,128,512]{2,1,0:T(8,128)(2,1)S(1)}, f32[8,128,512]{2,1,0:T(8,128)S(1)}, bf16[8,3,256,256]{3,2,1,0:T(8,128)...) custom-call(s32[1]{0:T(128)} %bitcast.9.slot, ...), custom_call_target="tpu_custom_call" | custom-call | flops 1610612736 | bytes 14012448 | tf_op jit(solution)/shard_map/front/pallas_call | solution.py:470
  154.1 9.6 %back.3 = (bf16[4,128,1024]{2,1,0:T(8,128)(2,1)S(1)}, f32[8,128,512]{2,1,0:T(8,128)S(1)}, f32[128,512]{1,0:T(8,128)S(1)}, f32[8,128]{1,0:T(8,128)S(1)}, bf16[4,128,128]{2,1,0:T(8,128)(2,1)S(1)}) custom-call(s32[1]{0:T(128)} %bitcast.9.slot, bf16[4,128,512]{2,1,0:T(8,128)(2,1)S(1)} %all-to-all-done.k_ref.v_ref, ...), custom_call_target="tpu_custom_call" | custom-call | flops 3221225472 | bytes 15884288 | tf_op jit(solution)/shard_map/back/pallas_call | solution.py:470
  167.5 4.3 %all-to-all-start.4 = ((bf16[4,128,1024]{2,1,0:T(8,128)(2,1)}), bf16[4,128,1024]{2,1,0:T(8,128)(2,1)}, u32[]{:S(2)}, u32[]{:S(2)}) async-start(bf16[4,128,1024]{2,1,0:T(8,128)(2,1)} %copy-done.13), calls=%async_computation.4 | async-start | bytes 2097152 | tf_op jit(solution)/shard_map/all_to_all | solution.py:394
  171.8 7.4 %front.2 = (f32[8,128,512]{2,1,0:T(8,128)S(1)}, bf16[8,128,512]{2,1,0:T(8,128)(2,1)S(1)}, f32[8,128,512]{2,1,0:T(8,128)S(1)}, bf16[8,3,256,256]{3,2,1,0:T(8,128)...) custom-call(s32[1]{0:T(128)} %bitcast.8.slot, ...), custom_call_target="tpu_custom_call" | custom-call | flops 1610612736 | bytes 14012448 | tf_op jit(solution)/shard_map/front/pallas_call | solution.py:470
  180.9 9.6 %back.2 = (bf16[4,128,1024]{2,1,0:T(8,128)(2,1)S(1)}, f32[8,128,512]{2,1,0:T(8,128)S(1)}, f32[128,512]{1,0:T(8,128)S(1)}, f32[8,128]{1,0:T(8,128)S(1)}, bf16[4,128,128]{2,1,0:T(8,128)(2,1)S(1)}) custom-call(s32[1]{0:T(128)} %bitcast.8.slot, bf16[4,128,512]{2,1,0:T(8,128)(2,1)S(1)} %all-to-all-done.k_ref.v_ref, ...), custom_call_target="tpu_custom_call" | custom-call | flops 3221225472 | bytes 15884288 | tf_op jit(solution)/shard_map/back/pallas_call | solution.py:470
  193.5 3.7 %all-to-all-start.2 = ((bf16[4,128,1024]{2,1,0:T(8,128)(2,1)}), bf16[4,128,1024]{2,1,0:T(8,128)(2,1)S(1)}, u32[]{:S(2)}, u32[]{:S(2)}) async-start(bf16[4,128,1024]{2,1,0:T(8,128)(2,1)} %copy-done.12), calls=%async_computation.2 | async-start | bytes 2097152 | tf_op jit(solution)/shard_map/all_to_all | solution.py:394
  197.6 16.3 %collective-permute-done.6.refs_1_ = bf16[8,128,128]{2,1,0:T(8,128)(2,1)S(1)} collective-permute-done((bf16[8,128,128]{2,1,0:T(8,128)(2,1)S(1)}, bf16[8,128,128]{2,1,0:T(8,128)(2,1)S(1)}, u32[]{:S(2)}, u32[]{:S(2)}) %collective-permute-start.6) | collective-permute-done | bytes 262176 | tf_op jit(solution)/shard_map/ppermute | solution.py:397
  220.9 7.4 %collective-permute-done.8.refs_3_ = bf16[8,128,128]{2,1,0:T(8,128)(2,1)S(1)} collective-permute-done((bf16[8,128,128]{2,1,0:T(8,128)(2,1)S(1)}, bf16[8,128,128]{2,1,0:T(8,128)(2,1)S(1)}, u32[]{:S(2)}, u32[]{:S(2)}) %collective-permute-start.8) | collective-permute-done | bytes 262176 | tf_op jit(solution)/shard_map/ppermute | solution.py:400
  231.0 3.1 %collective-permute-start.10 = (bf16[8,128,128]{2,1,0:T(8,128)(2,1)S(1)}, bf16[8,128,128]{2,1,0:T(8,128)(2,1)S(1)}, u32[]{:S(2)}, u32[]{:S(2)}) collective-permute-start(bf16[8,128,128]{2,1,0:T(8,128)(2,1)S(1)} %get-tuple-element.75), channel_id=1, source_target_pairs={{0,16},{4,20},{8,24},{12,28},{16,0},{20,4},{24,8},{28,12},{1,17},{... | collective-permute-start | bytes 786440 | tf_op jit(solution)/shard_map/ppermute | solution.py:397
  240.2 19.9 %all-gather.2 = f32[128,128]{1,0:T(8,128)S(1)} all-gather(f32[16,128]{1,0:T(8,128)S(1)} %pad_maximum_fusion.3), channel_id=4, replica_groups={{0,1,2,3,16,17,18,19},{4,5,6,7,20,21,22,23},{8,9,10,11,24,25,26,27},{12..., dimensions={0}, use_global_device_ids=true | all-gather | bytes 73728 | tf_op jit(solution)/shard_map/all_gather | solution.py:411
  261.8 5.4 %keys.2 = (bf16[4,128,512]{2,1,0:T(8,128)(2,1)}, bf16[4,128,128]{2,1,0:T(8,128)(2,1)S(1)}) custom-call(s32[1]{0:T(128)} %bitcast.8.slot, bf16[4,128,512]{2,1,0:T(8,128)(2,1)S(1)} %all-to-all-done.k_ref.v_ref, bf16[4,128,512]{2,1,0:T(8,128)(2,1)S(1)} %all-to-all-done.k_ref.v_ref, ...), custom_call_target="tpu_custom_call", output_to_operand_aliasing={{0}: (9, {})} | custom-call | flops 536870912 | bytes 5439520 | tf_op jit(solution)/shard_map/keys/pallas_call | solution.py:470
  267.3 5.5 %keys.3 = (bf16[4,128,512]{2,1,0:T(8,128)(2,1)}, bf16[4,128,128]{2,1,0:T(8,128)(2,1)S(1)}) custom-call(s32[1]{0:T(128)} %bitcast.9.slot, bf16[4,128,512]{2,1,0:T(8,128)(2,1)S(1)} %all-to-all-done.k_ref.v_ref, bf16[4,128,512]{2,1,0:T(8,128)(2,1)S(1)} %all-to-all-done.k_ref.v_ref, ...), custom_call_target="tpu_custom_call", output_to_operand_aliasing={{0}: (9, {})} | custom-call | flops 536870912 | bytes 5439520 | tf_op jit(solution)/shard_map/keys/pallas_call | solution.py:470
  272.8 4.2 %all-to-all-start.5 = ((bf16[4,128,512]{2,1,0:T(8,128)(2,1)}), bf16[4,128,512]{2,1,0:T(8,128)(2,1)}, u32[]{:S(2)}, u32[]{:S(2)}) async-start(bf16[4,128,512]{2,1,0:T(8,128)(2,1)} %get-tuple-element.87), calls=%async_computation.5 | async-start | bytes 1048576 | tf_op jit(solution)/shard_map/all_to_all | solution.py:394
  (137 shorter events, 73.5 us)
Async XLA Ops:
  4.6 11.5 %all-to-all-start = ((bf16[4,128,512]{2,1,0:T(8,128)(2,1)}), bf16[4,128,512]{2,1,0:T(8,128)(2,1)S(1)}, u32[]{:S(2)}, u32[]{:S(2)}) async-start(bf16[4,128,512]{2,1,0:T(8,128)(2,1)} %copy-done.7), calls=%async_computation | async-start | bytes 1048576 | tf_op jit(solution)/shard_map/all_to_all | solution.py:394
  20.0 45.3 %all-to-all-start.3 = ((bf16[4,128,2048]{2,1,0:T(8,128)(2,1)}), bf16[4,128,2048]{2,1,0:T(8,128)(2,1)}, u32[]{:S(2)}, u32[]{:S(2)}) async-start(bf16[4,128,2048]{2,1,0:T(8,128)(2,1)} %copy-done.4), calls=%async_computation.3 | async-start | bytes 4194304 | tf_op jit(solution)/shard_map/all_to_all | solution.py:394
  24.7 22.4 %collective-permute-start = (bf16[8,32,128]{2,1,0:T(8,128)(2,1)S(1)}, bf16[8,32,128]{2,1,0:T(8,128)(2,1)S(1)}, u32[]{:S(2)}, u32[]{:S(2)}) collective-permute-start(bf16[8,32,128]{2,1,0:T(8,128)(2,1)S(1)} %pad_maximum_fusion.1), channel_id=1, source_target_pairs={{0,16},{4,20},{8,24},{12,28},{16,0},{20,4},{24,8},{28,12},{1,17},{... | collective-permute-start | bytes 196616 | tf_op jit(solution)/shard_map/ppermute | solution.py:397
  65.3 102.2 %all-to-all-start.1 = ((bf16[4,128,2048]{2,1,0:T(8,128)(2,1)}), bf16[4,128,2048]{2,1,0:T(8,128)(2,1)S(1)}, u32[]{:S(2)}, u32[]{:S(2)}) async-start(bf16[4,128,2048]{2,1,0:T(8,128)(2,1)} %copy-done.3), calls=%async_computation.1 | async-start | bytes 4194304 | tf_op jit(solution)/shard_map/all_to_all | solution.py:394
  72.1 28.4 %collective-permute-start.1 = (bf16[8,128,128]{2,1,0:T(8,128)(2,1)}, bf16[8,128,128]{2,1,0:T(8,128)(2,1)S(1)}, u32[]{:S(2)}, u32[]{:S(2)}) collective-permute-start(bf16[8,128,128]{2,1,0:T(8,128)(2,1)} %copy-done.28), channel_id=1, source_target_pairs={{0,16},{4,20},{8,24},{12,28},{16,0},{20,4},{24,8},{28,12},{1,17},{... | collective-permute-start | bytes 786440 | tf_op jit(solution)/shard_map/ppermute | solution.py:397
  101.9 7.3 %collective-permute-start.2 = (bf16[8,128,128]{2,1,0:T(8,128)(2,1)}, bf16[8,128,128]{2,1,0:T(8,128)(2,1)}, u32[]{:S(2)}, u32[]{:S(2)}) collective-permute-start(bf16[8,128,128]{2,1,0:T(8,128)(2,1)} %totals.2), channel_id=1, source_target_pairs={{0,1},{1,2},{2,3},{3,0},{4,5},{5,6},{6,7},{7,4},{8,9},{9,10},{10,1... | collective-permute-start | bytes 786440 | tf_op jit(solution)/shard_map/ppermute | solution.py:400
  103.3 12.9 %collective-permute-start.3 = (bf16[8,128,128]{2,1,0:T(8,128)(2,1)}, bf16[8,128,128]{2,1,0:T(8,128)(2,1)}, u32[]{:S(2)}, u32[]{:S(2)}) collective-permute-start(bf16[8,128,128]{2,1,0:T(8,128)(2,1)} %totals.2), channel_id=1, source_target_pairs={{0,2},{1,3},{2,0},{3,1},{4,6},{5,7},{6,4},{7,5},{8,10},{9,11},{10,... | collective-permute-start | bytes 786440 | tf_op jit(solution)/shard_map/ppermute | solution.py:400
  104.3 12.5 %collective-permute-start.4 = (bf16[8,128,128]{2,1,0:T(8,128)(2,1)}, bf16[8,128,128]{2,1,0:T(8,128)(2,1)}, u32[]{:S(2)}, u32[]{:S(2)}) collective-permute-start(bf16[8,128,128]{2,1,0:T(8,128)(2,1)} %totals.2), channel_id=1, source_target_pairs={{0,3},{1,0},{2,1},{3,2},{4,7},{5,4},{6,5},{7,6},{8,11},{9,8},{10,9... | collective-permute-start | bytes 786440 | tf_op jit(solution)/shard_map/ppermute | solution.py:400
  120.9 33.3 %collective-permute-start.5 = (bf16[8,128,128]{2,1,0:T(8,128)(2,1)S(1)}, bf16[8,128,128]{2,1,0:T(8,128)(2,1)S(1)}, u32[]{:S(2)}, u32[]{:S(2)}) collective-permute-start(bf16[8,128,128]{2,1,0:T(8,128)(2,1)S(1)} %get-tuple-element.71), channel_id=1, source_target_pairs={{0,16},{4,20},{8,24},{12,28},{16,0},{20,4},{24,8},{28,12},{1,17},{... | collective-permute-start | bytes 786440 | tf_op jit(solution)/shard_map/ppermute | solution.py:397
  167.5 26.0 %all-to-all-start.4 = ((bf16[4,128,1024]{2,1,0:T(8,128)(2,1)}), bf16[4,128,1024]{2,1,0:T(8,128)(2,1)}, u32[]{:S(2)}, u32[]{:S(2)}) async-start(bf16[4,128,1024]{2,1,0:T(8,128)(2,1)} %copy-done.13), calls=%async_computation.4 | async-start | bytes 2097152 | tf_op jit(solution)/shard_map/all_to_all | solution.py:394
  193.5 79.2 %all-to-all-start.2 = ((bf16[4,128,1024]{2,1,0:T(8,128)(2,1)}), bf16[4,128,1024]{2,1,0:T(8,128)(2,1)S(1)}, u32[]{:S(2)}, u32[]{:S(2)}) async-start(bf16[4,128,1024]{2,1,0:T(8,128)(2,1)} %copy-done.12), calls=%async_computation.2 | async-start | bytes 2097152 | tf_op jit(solution)/shard_map/all_to_all | solution.py:394
  197.2 16.7 %collective-permute-start.6 = (bf16[8,128,128]{2,1,0:T(8,128)(2,1)S(1)}, bf16[8,128,128]{2,1,0:T(8,128)(2,1)S(1)}, u32[]{:S(2)}, u32[]{:S(2)}) collective-permute-start(bf16[8,128,128]{2,1,0:T(8,128)(2,1)S(1)} %copy-done.27), channel_id=1, source_target_pairs={{0,16},{4,20},{8,24},{12,28},{16,0},{20,4},{24,8},{28,12},{1,17},{... | collective-permute-start | bytes 786440 | tf_op jit(solution)/shard_map/ppermute | solution.py:397
  215.4 12.9 %collective-permute-start.8 = (bf16[8,128,128]{2,1,0:T(8,128)(2,1)S(1)}, bf16[8,128,128]{2,1,0:T(8,128)(2,1)S(1)}, u32[]{:S(2)}, u32[]{:S(2)}) collective-permute-start(bf16[8,128,128]{2,1,0:T(8,128)(2,1)S(1)} %totals.3), channel_id=1, source_target_pairs={{0,2},{1,3},{2,0},{3,1},{4,6},{5,7},{6,4},{7,5},{8,10},{9,11},{10,... | collective-permute-start | bytes 786440 | tf_op jit(solution)/shard_map/ppermute | solution.py:400
  216.7 12.3 %collective-permute-start.9 = (bf16[8,128,128]{2,1,0:T(8,128)(2,1)S(1)}, bf16[8,128,128]{2,1,0:T(8,128)(2,1)}, u32[]{:S(2)}, u32[]{:S(2)}) collective-permute-start(bf16[8,128,128]{2,1,0:T(8,128)(2,1)S(1)} %totals.3), channel_id=1, source_target_pairs={{0,3},{1,0},{2,1},{3,2},{4,7},{5,4},{6,5},{7,6},{8,11},{9,8},{10,9... | collective-permute-start | bytes 786440 | tf_op jit(solution)/shard_map/ppermute | solution.py:400
  231.0 36.3 %collective-permute-start.10 = (bf16[8,128,128]{2,1,0:T(8,128)(2,1)S(1)}, bf16[8,128,128]{2,1,0:T(8,128)(2,1)S(1)}, u32[]{:S(2)}, u32[]{:S(2)}) collective-permute-start(bf16[8,128,128]{2,1,0:T(8,128)(2,1)S(1)} %get-tuple-element.75), channel_id=1, source_target_pairs={{0,16},{4,20},{8,24},{12,28},{16,0},{20,4},{24,8},{28,12},{1,17},{... | collective-permute-start | bytes 786440 | tf_op jit(solution)/shard_map/ppermute | solution.py:397
  234.9 25.1 %collective-permute-start.11 = (bf16[4,32,128]{2,1,0:T(8,128)(2,1)S(1)}, bf16[4,32,128]{2,1,0:T(8,128)(2,1)S(1)}, u32[]{:S(2)}, u32[]{:S(2)}) collective-permute-start(bf16[4,32,128]{2,1,0:T(8,128)(2,1)S(1)} %get-tuple-element.108), channel_id=1, source_target_pairs={{0,16},{1,17},{2,18},{3,19},{4,20},{5,21},{6,22},{7,23},{8,24},{9,... | collective-permute-start | bytes 98312 | tf_op jit(solution)/shard_map/ppermute | solution.py:408
  235.0 25.0 %collective-permute-start.12 = (bf16[4,32,128]{2,1,0:T(8,128)(2,1)S(1)}, bf16[4,32,128]{2,1,0:T(8,128)(2,1)S(1)}, u32[]{:S(2)}, u32[]{:S(2)}) collective-permute-start(bf16[4,32,128]{2,1,0:T(8,128)(2,1)S(1)} %get-tuple-element.107), channel_id=1, source_target_pairs={{0,17},{1,18},{2,19},{3,16},{4,21},{5,22},{6,23},{7,20},{8,25},{9,... | collective-permute-start | bytes 98312 | tf_op jit(solution)/shard_map/ppermute | solution.py:408
  237.3 22.7 %collective-permute-start.13 = (bf16[4,32,128]{2,1,0:T(8,128)(2,1)S(1)}, bf16[4,32,128]{2,1,0:T(8,128)(2,1)S(1)}, u32[]{:S(2)}, u32[]{:S(2)}) collective-permute-start(bf16[4,32,128]{2,1,0:T(8,128)(2,1)S(1)} %get-tuple-element.106), channel_id=1, source_target_pairs={{0,18},{1,19},{2,16},{3,17},{4,22},{5,23},{6,20},{7,21},{8,26},{9,... | collective-permute-start | bytes 98312 | tf_op jit(solution)/shard_map/ppermute | solution.py:408
  237.4 22.7 %collective-permute-start.14 = (bf16[4,32,128]{2,1,0:T(8,128)(2,1)S(1)}, bf16[4,32,128]{2,1,0:T(8,128)(2,1)S(1)}, u32[]{:S(2)}, u32[]{:S(2)}) collective-permute-start(bf16[4,32,128]{2,1,0:T(8,128)(2,1)S(1)} %get-tuple-element.105), channel_id=1, source_target_pairs={{0,19},{1,16},{2,17},{3,18},{4,23},{5,20},{6,21},{7,22},{8,27},{9,... | collective-permute-start | bytes 98312 | tf_op jit(solution)/shard_map/ppermute | solution.py:408
  272.8 18.7 %all-to-all-start.5 = ((bf16[4,128,512]{2,1,0:T(8,128)(2,1)}), bf16[4,128,512]{2,1,0:T(8,128)(2,1)}, u32[]{:S(2)}, u32[]{:S(2)}) async-start(bf16[4,128,512]{2,1,0:T(8,128)(2,1)} %get-tuple-element.87), calls=%async_computation.5 | async-start | bytes 1048576 | tf_op jit(solution)/shard_map/all_to_all | solution.py:394
  277.3 8.2 %collective-permute-start.19 = (bf16[4,32,128]{2,1,0:T(8,128)(2,1)S(1)}, bf16[4,32,128]{2,1,0:T(8,128)(2,1)S(1)}, u32[]{:S(2)}, u32[]{:S(2)}) collective-permute-start(bf16[4,32,128]{2,1,0:T(8,128)(2,1)S(1)} %get-tuple-element.103), channel_id=1, source_target_pairs={{0,17},{1,18},{2,19},{3,16},{4,21},{5,22},{6,23},{7,20},{8,25},{9,... | collective-permute-start | bytes 98312 | tf_op jit(solution)/shard_map/ppermute | solution.py:408
  278.5 12.2 %collective-permute-start.15 = (bf16[2,4,32,128]{3,2,1,0:T(8,128)(2,1)S(1)}, bf16[2,4,32,128]{3,2,1,0:T(8,128)(2,1)S(1)}, u32[]{:S(2)}, u32[]{:S(2)}) collective-permute-start(bf16[2,4,32,128]{3,2,1,0:T(8,128)(2,1)S(1)} %get-tuple-element.99), channel_id=1, source_target_pairs={{0,1},{1,2},{2,3},{3,0},{4,5},{5,6},{6,7},{7,4},{8,9},{9,10},{10,1... | collective-permute-start | bytes 196616 | tf_op jit(solution)/shard_map/ppermute | solution.py:400
  278.7 11.9 %collective-permute-start.16 = (bf16[2,4,32,128]{3,2,1,0:T(8,128)(2,1)S(1)}, bf16[2,4,32,128]{3,2,1,0:T(8,128)(2,1)S(1)}, u32[]{:S(2)}, u32[]{:S(2)}) collective-permute-start(bf16[2,4,32,128]{3,2,1,0:T(8,128)(2,1)S(1)} %get-tuple-element.100), channel_id=1, source_target_pairs={{0,2},{1,3},{2,0},{3,1},{4,6},{5,7},{6,4},{7,5},{8,10},{9,11},{10,... | collective-permute-start | bytes 196616 | tf_op jit(solution)/shard_map/ppermute | solution.py:400
  281.2 9.5 %collective-permute-start.17 = (bf16[2,4,32,128]{3,2,1,0:T(8,128)(2,1)S(1)}, bf16[2,4,32,128]{3,2,1,0:T(8,128)(2,1)S(1)}, u32[]{:S(2)}, u32[]{:S(2)}) collective-permute-start(bf16[2,4,32,128]{3,2,1,0:T(8,128)(2,1)S(1)} %get-tuple-element.98), channel_id=1, source_target_pairs={{0,3},{1,0},{2,1},{3,2},{4,7},{5,4},{6,5},{7,6},{8,11},{9,8},{10,9... | collective-permute-start | bytes 196616 | tf_op jit(solution)/shard_map/ppermute | solution.py:400
  (36 other events, 229.5 us)

commit v4 on v3

--- a/solution.py
+++ b/solution.py
@@ -10,7 +10,9 @@
 BLK = 512
 TILE = 256
 PAIR = 2
-LIMIT = 40 * 1024 * 1024
+LIMIT = 56 * 1024 * 1024
+
+LITTLE = pl.CostEstimate(flops=1000, bytes_accessed=1000, transcendentals=0)
 
 F32 = jnp.float32
 BF16 = jnp.bfloat16
@@ -35,15 +37,17 @@
     return jnp.concatenate([square] * (width // n), axis=1)
 
 
-def pick(ref, weights, slot, blocks, before):
-    heads = ref.shape[1] // (ref.shape[0] // blocks + 1 if before else ref.shape[0] // blocks)
-    groups = ref.shape[0] // blocks
-    total = jnp.zeros((heads, ref.shape[2]), F32)
-    for i in range(ref.shape[0]):
-        at = lax.rem(slot + groups - i // blocks, groups) * heads
-        total = total + weights[i] * ref[i, pl.ds(pl.multiple_of(at, heads), heads), :]
+def pick(ref, weights, slot, block, before):
+    blocks, groups = ref.shape[:2]
+    heads = ref.shape[2] // (groups + before)
+    total = jnp.zeros((heads, ref.shape[3]), F32)
+    for r in range(groups):
+        at = lax.rem(slot - block + r + groups, groups) * heads
+        rows = pl.ds(pl.multiple_of(at, heads), heads)
+        for i in range(blocks):
+            total = total + weights[i * groups + r] * ref[i, r, rows, :]
     if before:
-        total = total + ref[slot * blocks, groups * heads :, :]
+        total = total + ref[0, lax.rem(block - slot + groups, groups), groups * heads :, :]
     return total
 
 
@@ -98,11 +102,49 @@
             out_specs=pl.BlockSpec((1, rows, count * width), lambda i, t: (i, 0, 0)),
         ),
         compiler_params=pltpu.CompilerParams(vmem_limit_bytes=LIMIT),
-        cost_estimate=pl.CostEstimate(
-            flops=0, bytes_accessed=4 * pieces * rows * count * width, transcendentals=0
-        ),
+        cost_estimate=LITTLE,
         name="pack",
     )(table, *(list(sources) * columns))
+
+
+def deal_kernel(columns, inputs, table, *refs):
+    count = columns * inputs
+    for r, out in enumerate(refs[-(len(refs) // (count + 1)) :]):
+        width = out.shape[1] // count
+        for i in range(count):
+            out[:, i * width : (i + 1) * width] = refs[r * count + i][...]
+
+
+def deal(table, sources, pieces, columns, width):
+    rows = sources[0].shape[0]
+    count = columns * len(sources)
+
+    def take(at):
+        return pl.BlockSpec((rows, width), lambda i, t: (0, t[at]))
+
+    return pl.pallas_call(
+        functools.partial(deal_kernel, columns, len(sources)),
+        out_shape=[jax.ShapeDtypeStruct((rows, count * width), sources[0].dtype)] * pieces,
+        grid_spec=pltpu.PrefetchScalarGridSpec(
+            num_scalar_prefetch=1,
+            grid=(1,),
+            in_specs=[
+                take(r * columns + s)
+                for r in range(pieces)
+                for s in range(columns)
+                for _ in sources
+            ],
+            out_specs=[pl.BlockSpec((rows, count * width), lambda i, t: (0, 0))] * pieces,
+        ),
+        compiler_params=pltpu.CompilerParams(vmem_limit_bytes=LIMIT),
+        cost_estimate=LITTLE,
+        name="deal",
+    )(table, *(list(sources) * (pieces * columns)))
+
+
+def sort_kernel(table, *refs):
+    for r, ref in enumerate(refs[:-1]):
+        refs[-1][table[r]] = ref[...]
 
 
 def unpack_kernel(outputs, table, *refs):
@@ -128,9 +170,7 @@
         + [pl.BlockSpec((pieces, step, outputs * width), lambda i: (0, i, 0))] * len(sources),
         out_specs=[pl.BlockSpec((step, total), lambda i: (i, 0))] * outputs,
         compiler_params=pltpu.CompilerParams(vmem_limit_bytes=LIMIT),
-        cost_estimate=pl.CostEstimate(
-            flops=0, bytes_accessed=4 * rows * total * outputs, transcendentals=0
-        ),
+        cost_estimate=LITTLE,
         name="unpack",
     )(table, *sources)
 
@@ -163,7 +203,7 @@
 
 
 def front_kernel(
-    fsdp, slot, k_ref, q_ref, g_ref, w_ref, norms_ref, weights,
+    slot, k_ref, q_ref, g_ref, w_ref, norms_ref, weights,
     qf_ref, kf_ref, scaled_ref, sc_ref, inv_ref, norm_ref, sx_ref,
 ):
     k_all, q_all, g_all = flat(k_ref), flat(q_ref), flat(g_ref)
@@ -172,7 +212,7 @@
 
     @pl.when(step == 0)
     def _():
-        norm_ref[...] = pick(norms_ref, weights, slot[0], fsdp, True)
+        norm_ref[...] = pick(norms_ref, weights, slot[0], slot[1], True)
 
     for u in range(PAIR):
         weight = weight_rows(w_ref, u)
@@ -262,7 +302,7 @@
 
 
 def key_kernel(
-    fsdp, slot, k_ref, v_ref, w_ref, sx_ref, dk_ref, dv_ref, norms_ref, weights, _,
+    slot, k_ref, v_ref, w_ref, sx_ref, dk_ref, dv_ref, norms_ref, weights, _,
     out, gm_ref, vt_all, total, logs, all_weights, norm_all,
 ):
     k_all, v_all = flat(k_ref), flat(v_ref)
@@ -273,7 +313,7 @@
     def _():
         vt_all[...] = turned(v_all)
         total[...] = dv_ref[...]
-        norm_all[...] = pick(norms_ref, weights, slot[0], fsdp, False)
+        norm_all[...] = pick(norms_ref, weights, slot[0], slot[1], False)
 
     maps = []
     for u in range(PAIR):
@@ -359,7 +399,7 @@
         out_specs=[pl.BlockSpec(memory_space=pltpu.VMEM)] * len(outs),
         scratch_shapes=list(scratch),
         compiler_params=pltpu.CompilerParams(vmem_limit_bytes=LIMIT),
-        cost_estimate=pl.CostEstimate(flops=total, bytes_accessed=total, transcendentals=0),
+        cost_estimate=LITTLE,
         name=name,
     )(*smem, *arrays)
 
@@ -386,9 +426,6 @@
     grid = (heads // PAIR,)
 
     blocks_of = [[g * part + p for p in range(part)] for g in slots]
-    owners_of = [
-        [(g * part + p) * fsdp + i for g in slots for i in range(fsdp)] for p in range(part)
-    ]
 
     def within(array):
         return lax.all_to_all(array, "ctx", 0, 0, axis_index_groups=blocks_of, tiled=True)
@@ -408,7 +445,8 @@
         return lax.ppermute(array, ("ctx", "fsdp"), moves)
 
     def gathered(array):
-        return lax.all_gather(array, ("ctx", "fsdp"), axis_index_groups=owners_of)
+        pieces = jnp.stack([array] + [across(array, s) for s in slots[1:]])
+        return lax.all_gather(pieces, "fsdp")
 
     def ints(values):
         return jnp.stack([jnp.asarray(v, jnp.int32) for v in values])
@@ -418,15 +456,27 @@
 
     slot = {s: (block + s) % grp for s in slots}
     owner = {s: [slot[s] * part + p for p in range(part)] for s in slots}
-    place_of = [(g, i) for g in slots for i in range(fsdp)]
-    earlier = flags([i * grp + g < seq * grp + block for g, i in place_of])
-    later = flags([i * grp + g > seq * grp + block for g, i in place_of])
+    place_of = [i * grp + (block - r) % grp for i in range(fsdp) for r in slots]
+    earlier = flags([other < seq * grp + block for other in place_of])
+    later = flags([other > seq * grp + block for other in place_of])
 
     own_maps = jnp.concatenate((query_map, key_map), axis=-1)
     maps = jnp.stack([own_maps] + [across(own_maps, -s) for s in slots[1:]])
-    kv_table = ints([c // replicas for s in slots for c in owner[s]])
-    kv = within(pack(kv_table, (key_rows, value_rows), part, grp, hd))
     maps = lax.all_gather(maps, "fsdp")
+    at = mine % part
+    kv_table = ints(
+        [(slot[s] * part + (at + r) % part) // replicas for r in range(part) for s in slots]
+    )
+    dealt = deal(kv_table, (key_rows, value_rows), part, grp, hd)
+    moves = [[(d, d // part * part + (d + r) % part) for d in range(ctx)] for r in range(part)]
+    kv = [dealt[0]] + [lax.ppermute(dealt[r], "ctx", moves[r]) for r in range(1, part)]
+    (kv,) = whole_call(
+        sort_kernel,
+        [jax.ShapeDtypeStruct((part, *dealt[0].shape), BF16)],
+        [ints([(at - r) % part for r in range(part)])],
+        kv,
+        "sort",
+    )
 
     params = pltpu.CompilerParams(
         dimension_semantics=("arbitrary",), vmem_limit_bytes=LIMIT
@@ -478,14 +528,19 @@
                 scratch_shapes=scratch,
             ),
             compiler_params=params,
-            cost_estimate=pl.CostEstimate(flops=flops, bytes_accessed=moved, transcendentals=0),
+            cost_estimate=LITTLE,
             input_output_aliases=dict(alias),
             name=name,
-        )(ints([slot[s]]), *arrays)
-
-    def scan(partial, before, extra, closing):
-        parts = [partial[0]] + [across(partial[s], s) for s in slots[1:]]
-        (total,) = whole_call(total_kernel, [state_shape], [], parts, "totals")
+        )(ints([slot[s], block]), *arrays)
+
+    def totals_of(partial, sent=()):
+        sent = dict(sent)
+        parts = [partial[0]] + [
+            sent[s] if s in sent else across(partial[s], s) for s in slots[1:]
+        ]
+        return parts, whole_call(total_kernel, [state_shape], [], parts, "totals")[0]
+
+    def spread(parts, total, before, extra, closing):
         others = [along(total, r) for r in range(1, fsdp)]
         blocks = [(block - r) % grp for r in slots]
         block_weight = flags([before(b, a) for a in blocks for b in blocks])
@@ -500,33 +555,33 @@
         )
         return [result[0]] + [across(result[s], -s) for s in slots[1:]], result[grp:]
 
-    rows, partial, norm = {}, {}, {}
+    def sent_rows(s, table):
+        return within(pack(table, (query_rows, grad_out), part, 1, heads * hd))
+
+    first, others = order[0], order[1:]
+    rows = {first: sent_rows(first, ints(owner[first]))}
+    partial, norm = {}, {}
     for s in order:
-        table, sources = ints(owner[s]), (query_rows, grad_out)
-        if s != order[0]:
-            table = after(table, *partial.values())
-        else:
-            table = after(table, kv)
-        rows[s] = within(pack(table, sources, part, 1, heads * hd))
-        if s == order[0]:
-            for i in order:
-                partial[i], norm[i] = call(
-                    state_kernel,
-                    i,
-                    [state_shape, row_shape],
-                    [k_spec(i), v_spec(i), map_spec(i)],
-                    [state_spec, row_spec],
-                    [kv, kv, maps],
-                    [],
-                    "states",
-                    unit * 2 * hd,
-                )
-            norms = gathered(jnp.concatenate([norm[i] for i in slots] + [prefix_norm], axis=0))
-    state, _ = scan(partial, lambda a, b: a < b, [prefix_state], False)
-
-    def front_of(s):
+        partial[s], norm[s] = call(
+            state_kernel,
+            s,
+            [state_shape, row_shape],
+            [k_spec(s), v_spec(s), map_spec(s)],
+            [state_spec, row_spec],
+            [kv, kv, maps],
+            [],
+            "states",
+            unit * 2 * hd,
+        )
+    norms = gathered(jnp.concatenate([norm[i] for i in slots] + [prefix_norm], axis=0))
+    parts, total = totals_of(partial)
+    for s in others:
+        rows[s] = sent_rows(s, after(ints(owner[s]), *parts))
+    state, _ = spread(parts, total, lambda a, b: a < b, [prefix_state], False)
+
+    def front_of(s, norms):
         return call(
-            functools.partial(front_kernel, fsdp),
+            front_kernel,
             s,
             [
                 wide_shape,
@@ -582,12 +637,17 @@
         pieces = array.reshape(*array.shape[:-2], fsdp, map_rows, array.shape[-1])
         return lax.dynamic_index_in_dim(pieces, device % fsdp, array.ndim - 2, keepdims=False)
 
-    fronts = {s: front_of(s) for s in order}
-    suffix, (grad_prefix,) = scan(
-        {s: fronts[s][6] for s in slots}, lambda a, b: a > b, [], True
-    )
+    fronts = {first: front_of(first, norms)}
+    sent = {s: across(fronts[first][6], s) for s in (first,) if s}
+    for s in others:
+        fronts[s] = front_of(s, after(norms, state[0], *sent.values()))
+    parts, total = totals_of({s: fronts[s][6] for s in slots}, sent)
+    state[0] = after(state[0], total)
+    suffix, (grad_prefix,) = spread(parts, total, lambda a, b: a > b, [], True)
     backs, returned, q_maps = {}, {}, []
-    for s in order:
+    for s in slots:
+        if s:
+            state[s] = after(state[s], suffix[0])
         backs[s] = back_of(s)
         returned[s] = within(backs[s][0])
         if s:
@@ -598,10 +658,10 @@
     pairs = jnp.zeros((part, tok, grp * 2 * hd), kv_type)
     k_maps, both_maps, key_gm = [], [], {}
     for s in slots:
-        if s == 0:
-            suffix[s] = after(suffix[s], *[returned[i] for i in slots[1:]], *q_maps)
+        if s:
+            suffix[s] = after(suffix[s], returned[0], *q_maps, *both_maps)
         pairs, key_gm[s] = call(
-            functools.partial(key_kernel, fsdp),
+            key_kernel,
             s,
             [of(kv_type, *pairs.shape), gm_shape],
             [k_spec(s), v_spec(s), map_spec(s), state_spec, wide_spec, dv_spec]

time: 296 us -> 279 us (0.943)
  Pallas kernels: 62.8 us -> 95.1 us
  blocking collectives: 49.6 us -> 25.2 us
  waiting for transfers between devices: 97.3 us -> 74.7 us
  local copies, waits for them, and re-layouts: 26.4 us -> 9.87 us
  starting transfers between devices: 55.7 us -> 63.3 us
  other arithmetic: 1.23 us -> 7.48 us
    all_gather x2, blocking collectives: 40.1 us -> 16.2 us  [gathered(): return lax.all_gather(pieces, 'fsdp')]
    unnamed x64 -> x81, local copies, waits for them, and re-layouts: 22.8 us -> 5.88 us
    pallas_call x8, Pallas kernels: 50.8 us -> 66.6 us  [call(): pl.pallas_call(kernel, out_shape=outs, grid_spec=pltpu.PrefetchScalarGrid...]
    ppermute x9, waiting for transfers between devices: 23.1 us -> 8.58 us  [along(): lax.ppermute(array, 'fsdp', [(d, (d + shift) % fsdp) for d in range(fsdp)])]
    pallas_call x5 -> x6, Pallas kernels: 5.03 us -> 12.5 us  [whole_call(): pl.pallas_call(kernel, out_shape=outs, in_specs=[pl.BlockSpec(memory_spac...]
    all_to_all x6 -> x5, waiting for transfers between devices: 7.09 us -> 0.01 us  [within(): lax.all_to_all(array, 'ctx', 0, 0, axis_index_groups=blocks_of, tiled=True)]
    ppermute x5 -> x7, waiting for transfers between devices: 64.7 us -> 58 us  [across(): lax.ppermute(array, 'ctx', [(d, (d + shift * part) % ctx) for d in range(...]
    ppermute x5 -> x7, starting transfers between devices: 8.84 us -> 15.4 us  [across(): lax.ppermute(array, 'ctx', [(d, (d + shift * part) % ctx) for d in range(...]
  transfers between devices with their start and end apart: 28 -> 32, of which waited for: 12 -> 11; matrix products, arithmetic and copies ran while one was open for 1% -> 4% of each run, Pallas kernels for 20% -> 24%
where the time goes in v4:
time: 279 us; the launch traced here: 277 us
  Pallas kernels  95.1 us (34%)
  waiting for transfers between devices  74.7 us (27%)
  starting transfers between devices  63.3 us (23%)
  blocking collectives  25.2 us (9%)
  local copies, waits for them, and re-layouts  9.87 us (4%)
  other arithmetic  7.48 us (3%)
    pallas_call x8, Pallas kernels, call(): pl.pallas_call(kernel, out_shape=outs, grid_spec=pltpu.PrefetchScalarGrid...  66.6 us
    ppermute x7, waiting for transfers between devices, across(): lax.ppermute(array, 'ctx', [(d, (d + shift * part) % ctx) for d in range(...  58 us
    all_to_all x5, starting transfers between devices, within(): lax.all_to_all(array, 'ctx', 0, 0, axis_index_groups=blocks_of, tiled=True)  22.9 us
    all_gather x2, blocking collectives, gathered(): return lax.all_gather(pieces, 'fsdp')  16.2 us
    ppermute x8, starting transfers between devices, apart(): return lax.ppermute(array, ('ctx', 'fsdp'), moves)  15.7 us
    ppermute x7, starting transfers between devices, across(): lax.ppermute(array, 'ctx', [(d, (d + shift * part) % ctx) for d in range(...  15.4 us
    pallas_call x6, Pallas kernels, whole_call(): pl.pallas_call(kernel, out_shape=outs, in_specs=[pl.BlockSpec(memory_spac...  12.5 us
    all_gather x1, blocking collectives, shards(): maps = lax.all_gather(maps, 'fsdp')  9.08 us
  transfers between devices with their start and end apart: 32, of which 11 were waited for; matrix products, arithmetic and copies ran while one was open for 4% of the time, Pallas kernels for 24%

profile of v4, /device:TPU:1, one launch (start us, length us, event | category | flops | bytes accessed | tf_op | source)
XLA Modules:
  0.0 276.9 jit_solution(15994212394879632059)
XLA Ops:
  1.3 4.4 %pack.3 = bf16[4,128,2048]{2,1,0:T(8,128)(2,1)} custom-call(s32[4]{0:T(128)} %pad_add_fusion.8.table, bf16[128,8192]{1,0:T(8,128)(2,1)} %refs_0_.5, bf16[128,8192]{1,0:T(8,128)(2,1)} %refs_1_.5), custom_call_target="tpu_custom_call" | custom-call | flops 1000 | bytes 1000 | tf_op jit(solution)/shard_map/pack/pallas_call | solution.py:95
  5.7 4.4 %all-to-all-start.1 = ((bf16[4,128,2048]{2,1,0:T(8,128)(2,1)}), bf16[4,128,2048]{2,1,0:T(8,128)(2,1)S(1)}, u32[]{:S(2)}, u32[]{:S(2)}) async-start(bf16[4,128,2048]{2,1,0:T(8,128)(2,1)} %pack.3), calls=%async_computation.1 | async-start | bytes 4194304 | tf_op jit(solution)/shard_map/all_to_all | solution.py:431
  21.1 18.1 %collective-permute-done.3 = bf16[8,32,128]{2,1,0:T(8,128)(2,1)S(1)} collective-permute-done((bf16[8,32,128]{2,1,0:T(8,128)(2,1)S(1)}, bf16[8,32,128]{2,1,0:T(8,128)(2,1)S(1)}, u32[]{:S(2)}, u32[]{:S(2)}) %collective-permute-start.3) | collective-permute-done | bytes 65568 | tf_op jit(solution)/shard_map/ppermute | solution.py:434
  39.2 9.1 %all-gather = bf16[8,8,32,128]{3,2,1,0:T(8,128)(2,1)} all-gather(bf16[2,8,32,128]{3,2,1,0:T(8,128)(2,1)S(1)} %pad_maximum_fusion), channel_id=2, replica_groups=mesh['ctx'=8,'fsdp'=4] {'fsdp'}, dimensions={0}, use_global_device_ids=true | all-gather | bytes 655360 | tf_op jit(solution)/shard_map/all_gather | solution.py:465
  51.0 5.2 %states.3 = (bf16[8,128,128]{2,1,0:T(8,128)(2,1)}, f32[8,128]{1,0:T(8,128)}) custom-call(s32[2]{0:T(128)} %pad_add_fusion.7.slot, bf16[4,128,512]{2,1,0:T(8,128)(2,1)} %sort.1.k_ref.v_ref, bf16[4,128,512]{2,1,0:T(8,128)(2,1)} %sort.1.k_ref.v_ref, bf16[4,2,8,32,128]{4,3,2,1,0:T(8,128)(2,1)} %bitcast.108), custom_call_target="tpu_custom_call" | custom-call | flops 1000 | bytes 1000 | tf_op jit(solution)/shard_map/states/pallas_call | solution.py:520
  60.5 5.2 %states.2 = (bf16[8,128,128]{2,1,0:T(8,128)(2,1)}, f32[8,128]{1,0:T(8,128)}) custom-call(s32[2]{0:T(128)} %pad_add_fusion.4.slot, bf16[4,128,512]{2,1,0:T(8,128)(2,1)} %sort.1.k_ref.v_ref, bf16[4,128,512]{2,1,0:T(8,128)(2,1)} %sort.1.k_ref.v_ref, bf16[4,2,8,32,128]{4,3,2,1,0:T(8,128)(2,1)} %bitcast.109), custom_call_target="tpu_custom_call" | custom-call | flops 1000 | bytes 1000 | tf_op jit(solution)/shard_map/states/pallas_call | solution.py:520
  65.7 5.9 %collective-permute-done.4.refs_1_ = bf16[8,128,128]{2,1,0:T(8,128)(2,1)S(1)} collective-permute-done((bf16[8,128,128]{2,1,0:T(8,128)(2,1)}, bf16[8,128,128]{2,1,0:T(8,128)(2,1)S(1)}, u32[]{:S(2)}, u32[]{:S(2)}) %collective-permute-start.4) | collective-permute-done | bytes 262176 | tf_op jit(solution)/shard_map/ppermute | solution.py:434
  71.6 4.4 %pack.2 = bf16[4,128,2048]{2,1,0:T(8,128)(2,1)} custom-call(s32[4]{0:T(128)} %pad_add_fusion.6.table, bf16[128,8192]{1,0:T(8,128)(2,1)} %refs_0_.5, bf16[128,8192]{1,0:T(8,128)(2,1)} %refs_1_.5), custom_call_target="tpu_custom_call" | custom-call | flops 1000 | bytes 1000 | tf_op jit(solution)/shard_map/pack/pallas_call | solution.py:95
  77.5 4.5 %all-to-all-start = ((bf16[4,128,2048]{2,1,0:T(8,128)(2,1)}), bf16[4,128,2048]{2,1,0:T(8,128)(2,1)}, u32[]{:S(2)}, u32[]{:S(2)}) async-start(bf16[4,128,2048]{2,1,0:T(8,128)(2,1)} %pack.2), calls=%async_computation | async-start | bytes 4194304 | tf_op jit(solution)/shard_map/all_to_all | solution.py:431
  84.4 20.2 %collective-permute-done.5 = f32[24,128]{1,0:T(8,128)S(1)} collective-permute-done((f32[24,128]{1,0:T(8,128)S(1)}, f32[24,128]{1,0:T(8,128)S(1)}, u32[]{:S(2)}, u32[]{:S(2)}) %collective-permute-start.5) | collective-permute-done | bytes 12320 | tf_op jit(solution)/shard_map/ppermute | solution.py:434
  104.6 6.9 %all-gather.1 = f32[8,24,128]{2,1,0:T(8,128)} all-gather(f32[2,24,128]{2,1,0:T(8,128)S(1)} %pad_maximum_fusion.2), channel_id=3, replica_groups=mesh['ctx'=8,'fsdp'=4] {'fsdp'}, dimensions={0}, use_global_device_ids=true | all-gather | bytes 122880 | tf_op jit(solution)/shard_map/all_gather | solution.py:449
  114.8 9.5 %front.2 = (f32[8,128,512]{2,1,0:T(8,128)}, bf16[8,128,512]{2,1,0:T(8,128)(2,1)}, f32[8,128,512]{2,1,0:T(8,128)}, bf16[8,3,256,256]{3,2,1,0:T(8,128)(2,1)}, f32[...) custom-call(s32[2]{0:T(128)} %pad_add_fusion.7.slot, bf16[4,128,512]{2,1,0:T(8,128)(2,1)} %sort.1.k_ref.v_ref, ...), custom_call_target="tpu_custom_call" | custom-call | flops 1000 | bytes 1000 | tf_op jit(solution)/shard_map/front/pallas_call | solution.py:520
  132.1 6.9 %collective-permute-done.9.refs_1_ = bf16[8,128,128]{2,1,0:T(8,128)(2,1)S(1)} collective-permute-done((bf16[8,128,128]{2,1,0:T(8,128)(2,1)}, bf16[8,128,128]{2,1,0:T(8,128)(2,1)S(1)}, u32[]{:S(2)}, u32[]{:S(2)}) %collective-permute-start.9) | collective-permute-done | bytes 262176 | tf_op jit(solution)/shard_map/ppermute | solution.py:434
  139.0 9.5 %front.3 = (f32[8,128,512]{2,1,0:T(8,128)}, bf16[8,128,512]{2,1,0:T(8,128)(2,1)}, f32[8,128,512]{2,1,0:T(8,128)}, bf16[8,3,256,256]{3,2,1,0:T(8,128)(2,1)}, f32[...) custom-call(s32[2]{0:T(128)} %pad_add_fusion.4.slot, bf16[4,128,512]{2,1,0:T(8,128)(2,1)} %sort.1.k_ref.v_ref, ...), custom_call_target="tpu_custom_call" | custom-call | flops 1000 | bytes 1000 | tf_op jit(solution)/shard_map/front/pallas_call | solution.py:520
  150.3 11.4 %back.2 = (bf16[4,128,1024]{2,1,0:T(8,128)(2,1)}, f32[8,128,512]{2,1,0:T(8,128)}, f32[128,512]{1,0:T(8,128)}, f32[8,128]{1,0:T(8,128)}, bf16[4,128,128]{2,1,0:T(8,128)(2,1)}) custom-call(s32[2]{0:T(128)} %pad_add_fusion.4.slot, bf16[4,128,512]{2,1,0:T(8,128)(2,1)} %sort.1.k_ref.v_ref, bf16[4,128,512]{2,1,0:T(8,128)(2,1)} %sort.1.k_ref.v_ref, ...), custom_call_target="tpu_custom_call" | custom-call | flops 1000 | bytes 1000 | tf_op jit(solution)/shard_map/back/pallas_call | solution.py:520
  173.1 7.1 %collective-permute-done.12.refs_3_ = bf16[8,128,128]{2,1,0:T(8,128)(2,1)S(1)} collective-permute-done((bf16[8,128,128]{2,1,0:T(8,128)(2,1)S(1)}, bf16[8,128,128]{2,1,0:T(8,128)(2,1)S(1)}, u32[]{:S(2)}, u32[]{:S(2)}) %collective-permute-start.12) | collective-permute-done | bytes 262176 | tf_op jit(solution)/shard_map/ppermute | solution.py:437
  184.8 11.5 %back.3 = (bf16[4,128,1024]{2,1,0:T(8,128)(2,1)}, f32[8,128,512]{2,1,0:T(8,128)}, f32[128,512]{1,0:T(8,128)}, f32[8,128]{1,0:T(8,128)}, bf16[4,128,128]{2,1,0:T(8,128)(2,1)}) custom-call(s32[2]{0:T(128)} %pad_add_fusion.7.slot, bf16[4,128,512]{2,1,0:T(8,128)(2,1)} %sort.1.k_ref.v_ref, bf16[4,128,512]{2,1,0:T(8,128)(2,1)} %sort.1.k_ref.v_ref, ...), custom_call_target="tpu_custom_call" | custom-call | flops 1000 | bytes 1000 | tf_op jit(solution)/shard_map/back/pallas_call | solution.py:520
  196.3 5.7 %all-to-all-start.3 = ((bf16[4,128,1024]{2,1,0:T(8,128)(2,1)}), bf16[4,128,1024]{2,1,0:T(8,128)(2,1)S(1)}, u32[]{:S(2)}, u32[]{:S(2)}) async-start(bf16[4,128,1024]{2,1,0:T(8,128)(2,1)} %get-tuple-element.87), calls=%async_computation.3 | async-start | bytes 2097152 | tf_op jit(solution)/shard_map/all_to_all | solution.py:431
  206.2 4.4 %collective-permute-start.16 = (bf16[4,32,128]{2,1,0:T(8,128)(2,1)S(1)}, bf16[4,32,128]{2,1,0:T(8,128)(2,1)S(1)}, u32[]{:S(2)}, u32[]{:S(2)}) collective-permute-start(bf16[4,32,128]{2,1,0:T(8,128)(2,1)S(1)} %get-tuple-element.119), channel_id=1, source_target_pairs={{0,17},{1,18},{2,19},{3,16},{4,21},{5,22},{6,23},{7,20},{8,25},{9,... | collective-permute-start | bytes 98312 | tf_op jit(solution)/shard_map/ppermute | solution.py:445
  210.8 6.9 %collective-permute-done.19 = f32[16,128]{1,0:T(8,128)S(1)} collective-permute-done((f32[16,128]{1,0:T(8,128)S(1)}, f32[16,128]{1,0:T(8,128)S(1)}, u32[]{:S(2)}, u32[]{:S(2)}) %collective-permute-start.19) | collective-permute-done | bytes 8224 | tf_op jit(solution)/shard_map/ppermute | solution.py:434
  217.7 9.3 %all-gather.2 = f32[8,16,128]{2,1,0:T(8,128)} all-gather(f32[2,16,128]{2,1,0:T(8,128)S(1)} %pad_maximum_fusion.3), channel_id=4, replica_groups=mesh['ctx'=8,'fsdp'=4] {'fsdp'}, dimensions={0}, use_global_device_ids=true | all-gather | bytes 81920 | tf_op jit(solution)/shard_map/all_gather | solution.py:449
  227.8 7.2 %keys.2 = (bf16[4,128,512]{2,1,0:T(8,128)(2,1)}, bf16[4,128,128]{2,1,0:T(8,128)(2,1)}) custom-call(s32[2]{0:T(128)} %pad_add_fusion.4.slot, bf16[4,128,512]{2,1,0:T(8,128)(2,1)} %sort.1.k_ref.v_ref, bf16[4,128,512]{2,1,0:T(8,128)(2,1)} %sort.1.k_ref.v_ref, bf16[4,2,8,32,128]{4,3,2,1,0:T(8,128)(2,1)} %bitcast.114, ...), custom_call_target="tpu_custom_call", output_to_operand_aliasing={{0}: (9, {})} | custom-call | flops 1000 | bytes 1000 | tf_op jit(solution)/shard_map/keys/pallas_call | solution.py:520
  244.4 7.1 %keys.3 = (bf16[4,128,512]{2,1,0:T(8,128)(2,1)}, bf16[4,128,128]{2,1,0:T(8,128)(2,1)}) custom-call(s32[2]{0:T(128)} %pad_add_fusion.7.slot, bf16[4,128,512]{2,1,0:T(8,128)(2,1)} %sort.1.k_ref.v_ref, bf16[4,128,512]{2,1,0:T(8,128)(2,1)} %sort.1.k_ref.v_ref, bf16[4,2,8,32,128]{4,3,2,1,0:T(8,128)(2,1)} %bitcast.115, ...), custom_call_target="tpu_custom_call", output_to_operand_aliasing={{0}: (9, {})} | custom-call | flops 1000 | bytes 1000 | tf_op jit(solution)/shard_map/keys/pallas_call | solution.py:520
  251.5 4.2 %all-to-all-start.4 = ((bf16[4,128,512]{2,1,0:T(8,128)(2,1)}), bf16[4,128,512]{2,1,0:T(8,128)(2,1)S(1)}, u32[]{:S(2)}, u32[]{:S(2)}) async-start(bf16[4,128,512]{2,1,0:T(8,128)(2,1)} %get-tuple-element.101), calls=%async_computation.4 | async-start | bytes 1048576 | tf_op jit(solution)/shard_map/all_to_all | solution.py:431
  (170 shorter events, 86.8 us)
Async XLA Ops:
  5.7 70.4 %all-to-all-start.1 = ((bf16[4,128,2048]{2,1,0:T(8,128)(2,1)}), bf16[4,128,2048]{2,1,0:T(8,128)(2,1)S(1)}, u32[]{:S(2)}, u32[]{:S(2)}) async-start(bf16[4,128,2048]{2,1,0:T(8,128)(2,1)} %pack.3), calls=%async_computation.1 | async-start | bytes 4194304 | tf_op jit(solution)/shard_map/all_to_all | solution.py:431
  13.4 34.9 %collective-permute-start = (bf16[128,512]{1,0:T(8,128)(2,1)}, bf16[128,512]{1,0:T(8,128)(2,1)S(1)}, u32[]{:S(2)}, u32[]{:S(2)}) collective-permute-start(bf16[128,512]{1,0:T(8,128)(2,1)} %get-tuple-element.58), channel_id=1, source_target_pairs={{0,4},{4,8},{8,12},{12,0},{16,20},{20,24},{24,28},{28,16},{1,5},{5... | collective-permute-start | bytes 393224 | tf_op jit(solution)/shard_map/ppermute | solution.py:472
  14.8 33.4 %collective-permute-start.1 = (bf16[128,512]{1,0:T(8,128)(2,1)}, bf16[128,512]{1,0:T(8,128)(2,1)S(1)}, u32[]{:S(2)}, u32[]{:S(2)}) collective-permute-start(bf16[128,512]{1,0:T(8,128)(2,1)} %get-tuple-element.59), channel_id=1, source_target_pairs={{0,8},{4,12},{8,0},{12,4},{16,24},{20,28},{24,16},{28,20},{1,9},{5... | collective-permute-start | bytes 393224 | tf_op jit(solution)/shard_map/ppermute | solution.py:472
  16.1 32.2 %collective-permute-start.2 = (bf16[128,512]{1,0:T(8,128)(2,1)}, bf16[128,512]{1,0:T(8,128)(2,1)S(1)}, u32[]{:S(2)}, u32[]{:S(2)}) collective-permute-start(bf16[128,512]{1,0:T(8,128)(2,1)} %get-tuple-element.60), channel_id=1, source_target_pairs={{0,12},{4,0},{8,4},{12,8},{16,28},{20,16},{24,20},{28,24},{1,13},{... | collective-permute-start | bytes 393224 | tf_op jit(solution)/shard_map/ppermute | solution.py:472
  17.3 21.8 %collective-permute-start.3 = (bf16[8,32,128]{2,1,0:T(8,128)(2,1)S(1)}, bf16[8,32,128]{2,1,0:T(8,128)(2,1)S(1)}, u32[]{:S(2)}, u32[]{:S(2)}) collective-permute-start(bf16[8,32,128]{2,1,0:T(8,128)(2,1)S(1)} %pad_maximum_fusion.1), channel_id=1, source_target_pairs={{0,16},{4,20},{8,24},{12,28},{16,0},{20,4},{24,8},{28,12},{1,17},{... | collective-permute-start | bytes 196616 | tf_op jit(solution)/shard_map/ppermute | solution.py:434
  56.2 15.4 %collective-permute-start.4 = (bf16[8,128,128]{2,1,0:T(8,128)(2,1)}, bf16[8,128,128]{2,1,0:T(8,128)(2,1)S(1)}, u32[]{:S(2)}, u32[]{:S(2)}) collective-permute-start(bf16[8,128,128]{2,1,0:T(8,128)(2,1)} %get-tuple-element.62), channel_id=1, source_target_pairs={{0,16},{4,20},{8,24},{12,28},{16,0},{20,4},{24,8},{28,12},{1,17},{... | collective-permute-start | bytes 786440 | tf_op jit(solution)/shard_map/ppermute | solution.py:434
  77.5 61.5 %all-to-all-start = ((bf16[4,128,2048]{2,1,0:T(8,128)(2,1)}), bf16[4,128,2048]{2,1,0:T(8,128)(2,1)}, u32[]{:S(2)}, u32[]{:S(2)}) async-start(bf16[4,128,2048]{2,1,0:T(8,128)(2,1)} %pack.2), calls=%async_computation | async-start | bytes 4194304 | tf_op jit(solution)/shard_map/all_to_all | solution.py:431
  82.1 22.5 %collective-permute-start.5 = (f32[24,128]{1,0:T(8,128)S(1)}, f32[24,128]{1,0:T(8,128)S(1)}, u32[]{:S(2)}, u32[]{:S(2)}) collective-permute-start(f32[24,128]{1,0:T(8,128)S(1)} %constant_dynamic-update-slice_fusion), channel_id=1, source_target_pairs={{0,16},{4,20},{8,24},{12,28},{16,0},{20,4},{24,8},{28,12},{1,17},{... | collective-permute-start | bytes 36872 | tf_op jit(solution)/shard_map/ppermute | solution.py:434
  113.3 15.3 %collective-permute-start.6 = (bf16[8,128,128]{2,1,0:T(8,128)(2,1)}, bf16[8,128,128]{2,1,0:T(8,128)(2,1)S(1)}, u32[]{:S(2)}, u32[]{:S(2)}) collective-permute-start(bf16[8,128,128]{2,1,0:T(8,128)(2,1)} %totals.2), channel_id=1, source_target_pairs={{0,1},{1,2},{2,3},{3,0},{4,5},{5,6},{6,7},{7,4},{8,9},{9,10},{10,1... | collective-permute-start | bytes 786440 | tf_op jit(solution)/shard_map/ppermute | solution.py:437
  113.9 14.7 %collective-permute-start.7 = (bf16[8,128,128]{2,1,0:T(8,128)(2,1)}, bf16[8,128,128]{2,1,0:T(8,128)(2,1)S(1)}, u32[]{:S(2)}, u32[]{:S(2)}) collective-permute-start(bf16[8,128,128]{2,1,0:T(8,128)(2,1)} %totals.2), channel_id=1, source_target_pairs={{0,2},{1,3},{2,0},{3,1},{4,6},{5,7},{6,4},{7,5},{8,10},{9,11},{10,... | collective-permute-start | bytes 786440 | tf_op jit(solution)/shard_map/ppermute | solution.py:437
  114.8 13.8 %collective-permute-start.8 = (bf16[8,128,128]{2,1,0:T(8,128)(2,1)}, bf16[8,128,128]{2,1,0:T(8,128)(2,1)S(1)}, u32[]{:S(2)}, u32[]{:S(2)}) collective-permute-start(bf16[8,128,128]{2,1,0:T(8,128)(2,1)} %totals.2), channel_id=1, source_target_pairs={{0,3},{1,0},{2,1},{3,2},{4,7},{5,4},{6,5},{7,6},{8,11},{9,8},{10,9... | collective-permute-start | bytes 786440 | tf_op jit(solution)/shard_map/ppermute | solution.py:437
  124.3 14.7 %collective-permute-start.9 = (bf16[8,128,128]{2,1,0:T(8,128)(2,1)}, bf16[8,128,128]{2,1,0:T(8,128)(2,1)S(1)}, u32[]{:S(2)}, u32[]{:S(2)}) collective-permute-start(bf16[8,128,128]{2,1,0:T(8,128)(2,1)} %get-tuple-element.67), channel_id=1, source_target_pairs={{0,16},{4,20},{8,24},{12,28},{16,0},{20,4},{24,8},{28,12},{1,17},{... | collective-permute-start | bytes 786440 | tf_op jit(solution)/shard_map/ppermute | solution.py:434
  161.8 34.6 %all-to-all-start.2 = ((bf16[4,128,1024]{2,1,0:T(8,128)(2,1)}), bf16[4,128,1024]{2,1,0:T(8,128)(2,1)S(1)}, u32[]{:S(2)}, u32[]{:S(2)}) async-start(bf16[4,128,1024]{2,1,0:T(8,128)(2,1)} %get-tuple-element.77), calls=%async_computation.2 | async-start | bytes 2097152 | tf_op jit(solution)/shard_map/all_to_all | solution.py:431
  167.6 12.6 %collective-permute-start.12 = (bf16[8,128,128]{2,1,0:T(8,128)(2,1)S(1)}, bf16[8,128,128]{2,1,0:T(8,128)(2,1)S(1)}, u32[]{:S(2)}, u32[]{:S(2)}) collective-permute-start(bf16[8,128,128]{2,1,0:T(8,128)(2,1)S(1)} %copy-done.6), channel_id=1, source_target_pairs={{0,2},{1,3},{2,0},{3,1},{4,6},{5,7},{6,4},{7,5},{8,10},{9,11},{10,... | collective-permute-start | bytes 786440 | tf_op jit(solution)/shard_map/ppermute | solution.py:437
  168.4 12.5 %collective-permute-start.13 = (bf16[8,128,128]{2,1,0:T(8,128)(2,1)S(1)}, bf16[8,128,128]{2,1,0:T(8,128)(2,1)S(1)}, u32[]{:S(2)}, u32[]{:S(2)}) collective-permute-start(bf16[8,128,128]{2,1,0:T(8,128)(2,1)S(1)} %copy-done.6), channel_id=1, source_target_pairs={{0,3},{1,0},{2,1},{3,2},{4,7},{5,4},{6,5},{7,6},{8,11},{9,8},{10,9... | collective-permute-start | bytes 786440 | tf_op jit(solution)/shard_map/ppermute | solution.py:437
  168.4 15.7 %collective-permute-start.10 = (bf16[8,128,128]{2,1,0:T(8,128)(2,1)S(1)}, bf16[8,128,128]{2,1,0:T(8,128)(2,1)S(1)}, u32[]{:S(2)}, u32[]{:S(2)}) collective-permute-start(bf16[8,128,128]{2,1,0:T(8,128)(2,1)S(1)} %copy-done.38), channel_id=1, source_target_pairs={{0,16},{4,20},{8,24},{12,28},{16,0},{20,4},{24,8},{28,12},{1,17},{... | collective-permute-start | bytes 786440 | tf_op jit(solution)/shard_map/ppermute | solution.py:434
  196.3 55.1 %all-to-all-start.3 = ((bf16[4,128,1024]{2,1,0:T(8,128)(2,1)}), bf16[4,128,1024]{2,1,0:T(8,128)(2,1)S(1)}, u32[]{:S(2)}, u32[]{:S(2)}) async-start(bf16[4,128,1024]{2,1,0:T(8,128)(2,1)} %get-tuple-element.87), calls=%async_computation.3 | async-start | bytes 2097152 | tf_op jit(solution)/shard_map/all_to_all | solution.py:431
  202.7 41.0 %collective-permute-start.14 = (bf16[8,128,128]{2,1,0:T(8,128)(2,1)S(1)}, bf16[8,128,128]{2,1,0:T(8,128)(2,1)S(1)}, u32[]{:S(2)}, u32[]{:S(2)}) collective-permute-start(bf16[8,128,128]{2,1,0:T(8,128)(2,1)S(1)} %copy-done.37), channel_id=1, source_target_pairs={{0,16},{4,20},{8,24},{12,28},{16,0},{20,4},{24,8},{28,12},{1,17},{... | collective-permute-start | bytes 786440 | tf_op jit(solution)/shard_map/ppermute | solution.py:434
  203.8 13.9 %collective-permute-start.19 = (f32[16,128]{1,0:T(8,128)S(1)}, f32[16,128]{1,0:T(8,128)S(1)}, u32[]{:S(2)}, u32[]{:S(2)}) collective-permute-start(f32[16,128]{1,0:T(8,128)S(1)} %constant_dynamic-update-slice_fusion.3), channel_id=1, source_target_pairs={{0,16},{4,20},{8,24},{12,28},{16,0},{20,4},{24,8},{28,12},{1,17},{... | collective-permute-start | bytes 24584 | tf_op jit(solution)/shard_map/ppermute | solution.py:434
  205.0 31.7 %collective-permute-start.15 = (bf16[4,32,128]{2,1,0:T(8,128)(2,1)S(1)}, bf16[4,32,128]{2,1,0:T(8,128)(2,1)S(1)}, u32[]{:S(2)}, u32[]{:S(2)}) collective-permute-start(bf16[4,32,128]{2,1,0:T(8,128)(2,1)S(1)} %get-tuple-element.120), channel_id=1, source_target_pairs={{0,16},{1,17},{2,18},{3,19},{4,20},{5,21},{6,22},{7,23},{8,24},{9,... | collective-permute-start | bytes 98312 | tf_op jit(solution)/shard_map/ppermute | solution.py:445
  206.2 31.2 %collective-permute-start.16 = (bf16[4,32,128]{2,1,0:T(8,128)(2,1)S(1)}, bf16[4,32,128]{2,1,0:T(8,128)(2,1)S(1)}, u32[]{:S(2)}, u32[]{:S(2)}) collective-permute-start(bf16[4,32,128]{2,1,0:T(8,128)(2,1)S(1)} %get-tuple-element.119), channel_id=1, source_target_pairs={{0,17},{1,18},{2,19},{3,16},{4,21},{5,22},{6,23},{7,20},{8,25},{9,... | collective-permute-start | bytes 98312 | tf_op jit(solution)/shard_map/ppermute | solution.py:445
  210.6 26.9 %collective-permute-start.17 = (bf16[4,32,128]{2,1,0:T(8,128)(2,1)S(1)}, bf16[4,32,128]{2,1,0:T(8,128)(2,1)S(1)}, u32[]{:S(2)}, u32[]{:S(2)}) collective-permute-start(bf16[4,32,128]{2,1,0:T(8,128)(2,1)S(1)} %get-tuple-element.118), channel_id=1, source_target_pairs={{0,18},{1,19},{2,16},{3,17},{4,22},{5,23},{6,20},{7,21},{8,26},{9,... | collective-permute-start | bytes 98312 | tf_op jit(solution)/shard_map/ppermute | solution.py:445
  235.9 7.8 %collective-permute-start.20 = (bf16[2,4,32,128]{3,2,1,0:T(8,128)(2,1)S(1)}, bf16[2,4,32,128]{3,2,1,0:T(8,128)(2,1)S(1)}, u32[]{:S(2)}, u32[]{:S(2)}) collective-permute-start(bf16[2,4,32,128]{3,2,1,0:T(8,128)(2,1)S(1)} %get-tuple-element.111), channel_id=1, source_target_pairs={{0,1},{1,2},{2,3},{3,0},{4,5},{5,6},{6,7},{7,4},{8,9},{9,10},{10,1... | collective-permute-start | bytes 196616 | tf_op jit(solution)/shard_map/ppermute | solution.py:437
  251.5 22.7 %all-to-all-start.4 = ((bf16[4,128,512]{2,1,0:T(8,128)(2,1)}), bf16[4,128,512]{2,1,0:T(8,128)(2,1)S(1)}, u32[]{:S(2)}, u32[]{:S(2)}) async-start(bf16[4,128,512]{2,1,0:T(8,128)(2,1)} %get-tuple-element.101), calls=%async_computation.4 | async-start | bytes 1048576 | tf_op jit(solution)/shard_map/all_to_all | solution.py:431
  (47 other events, 430.1 us)

commit v5 on v4

--- a/solution.py
+++ b/solution.py
@@ -10,7 +10,7 @@
 BLK = 512
 TILE = 256
 PAIR = 2
-LIMIT = 56 * 1024 * 1024
+LIMIT = 40 * 1024 * 1024
 
 LITTLE = pl.CostEstimate(flops=1000, bytes_accessed=1000, transcendentals=0)
 
@@ -37,15 +37,16 @@
     return jnp.concatenate([square] * (width // n), axis=1)
 
 
-def pick(ref, weights, slot, block, before):
+def pick(ref, table, slot, block, weights, before):
     blocks, groups = ref.shape[:2]
     heads = ref.shape[2] // (groups + before)
     total = jnp.zeros((heads, ref.shape[3]), F32)
+    slot, block = table[slot], table[block]
     for r in range(groups):
         at = lax.rem(slot - block + r + groups, groups) * heads
         rows = pl.ds(pl.multiple_of(at, heads), heads)
         for i in range(blocks):
-            total = total + weights[i * groups + r] * ref[i, r, rows, :]
+            total = total + table[weights + i * groups + r].astype(F32) * ref[i, r, rows, :]
     if before:
         total = total + ref[0, lax.rem(block - slot + groups, groups), groups * heads :, :]
     return total
@@ -85,12 +86,12 @@
         out[0, :, i * width : (i + 1) * width] = source[...]
 
 
-def pack(table, sources, pieces, columns, width):
+def pack(table, base, sources, pieces, columns, width):
     rows = sources[0].shape[0]
     count = columns * len(sources)
 
     def take(s):
-        return pl.BlockSpec((rows, width), lambda i, t: (0, t[s * pieces + i]))
+        return pl.BlockSpec((rows, width), lambda i, t: (0, t[base + s * pieces + i]))
 
     return pl.pallas_call(
         functools.partial(pack_kernel, columns),
@@ -115,12 +116,12 @@
             out[:, i * width : (i + 1) * width] = refs[r * count + i][...]
 
 
-def deal(table, sources, pieces, columns, width):
+def deal(table, base, sources, pieces, columns, width):
     rows = sources[0].shape[0]
     count = columns * len(sources)
 
     def take(at):
-        return pl.BlockSpec((rows, width), lambda i, t: (0, t[at]))
+        return pl.BlockSpec((rows, width), lambda i, t: (0, t[base + at]))
 
     return pl.pallas_call(
         functools.partial(deal_kernel, columns, len(sources)),
@@ -142,28 +143,28 @@
     )(table, *(list(sources) * (pieces * columns)))
 
 
-def sort_kernel(table, *refs):
+def sort_kernel(base, table, *refs):
     for r, ref in enumerate(refs[:-1]):
-        refs[-1][table[r]] = ref[...]
-
-
-def unpack_kernel(outputs, table, *refs):
+        refs[-1][table[base + r]] = ref[...]
+
+
+def unpack_kernel(outputs, base, table, *refs):
     sources, outs = refs[:-outputs], refs[-outputs:]
     for s, source in enumerate(sources):
         pieces = source.shape[0]
         width = source.shape[2] // outputs
         for r in range(pieces):
-            at = pl.ds(pl.multiple_of(table[s * pieces + r] * width, width), width)
+            at = pl.ds(pl.multiple_of(table[base + s * pieces + r] * width, width), width)
             for i, out in enumerate(outs):
                 out[:, at] = source[r, :, i * width : (i + 1) * width]
 
 
-def unpack(table, sources, outputs, width):
+def unpack(table, base, sources, outputs, width):
     pieces, rows = sources[0].shape[:2]
     total = len(sources) * pieces * width
     step = rows // 2
     return pl.pallas_call(
-        functools.partial(unpack_kernel, outputs),
+        functools.partial(unpack_kernel, outputs, base),
         out_shape=[jax.ShapeDtypeStruct((rows, total), sources[0].dtype)] * outputs,
         grid=(rows // step,),
         in_specs=[pl.BlockSpec(memory_space=SMEM)]
@@ -203,7 +204,7 @@
 
 
 def front_kernel(
-    slot, k_ref, q_ref, g_ref, w_ref, norms_ref, weights,
+    where, table, k_ref, q_ref, g_ref, w_ref, norms_ref,
     qf_ref, kf_ref, scaled_ref, sc_ref, inv_ref, norm_ref, sx_ref,
 ):
     k_all, q_all, g_all = flat(k_ref), flat(q_ref), flat(g_ref)
@@ -212,7 +213,7 @@
 
     @pl.when(step == 0)
     def _():
-        norm_ref[...] = pick(norms_ref, weights, slot[0], slot[1], True)
+        norm_ref[...] = pick(norms_ref, table, *where, True)
 
     for u in range(PAIR):
         weight = weight_rows(w_ref, u)
@@ -302,7 +303,7 @@
 
 
 def key_kernel(
-    slot, k_ref, v_ref, w_ref, sx_ref, dk_ref, dv_ref, norms_ref, weights, _,
+    where, table, k_ref, v_ref, w_ref, sx_ref, dk_ref, dv_ref, norms_ref, _,
     out, gm_ref, vt_all, total, logs, all_weights, norm_all,
 ):
     k_all, v_all = flat(k_ref), flat(v_ref)
@@ -313,7 +314,7 @@
     def _():
         vt_all[...] = turned(v_all)
         total[...] = dv_ref[...]
-        norm_all[...] = pick(norms_ref, weights, slot[0], slot[1], False)
+        norm_all[...] = pick(norms_ref, table, *where, False)
 
     maps = []
     for u in range(PAIR):
@@ -337,12 +338,12 @@
         out[...] = pair.astype(out.dtype).reshape(out.shape)
 
 
-def total_kernel(*refs):
+def total_kernel(table, *refs):
     for h in range(refs[-1].shape[0]):
         refs[-1][h] = sum(ref[h].astype(F32) for ref in refs[:-1]).astype(BF16)
 
 
-def spread_kernel(grp, others, closing, block_weight, total_weight, at, *refs):
+def spread_kernel(grp, others, closing, block_weight, total_weight, at, table, *refs):
     parts, totals, refs = refs[:grp], refs[grp : grp + others], refs[grp + others :]
     if closing:
         outs, grad, scratch = refs[:grp], refs[grp], refs[grp + 1]
@@ -355,20 +356,20 @@
             base = jnp.zeros_like(states[0])
             scratch[...] = sum(states) + sum(others_state)
             rows = grad.shape[1]
-            grad[h] = scratch[pl.ds(pl.multiple_of(at[0] * rows, rows), rows), :]
+            grad[h] = scratch[pl.ds(pl.multiple_of(table[at] * rows, rows), rows), :]
         else:
             base = state_ref[h]
         for i, state in enumerate(others_state):
-            base = base + total_weight[i] * state
+            base = base + table[total_weight + i].astype(F32) * state
         for r, out in enumerate(outs):
             state = base
             for i in range(grp):
                 if i != r:
-                    state = state + block_weight[r * grp + i] * states[i]
+                    state = state + table[block_weight + r * grp + i].astype(F32) * states[i]
             out[h] = state.astype(BF16)
 
 
-def close_kernel(pairs, singles, at, q_ref, k_ref, *refs):
+def close_kernel(pairs, singles, at, table, q_ref, k_ref, *refs):
     both, q_parts, k_parts = (
         refs[:pairs],
         refs[pairs : pairs + singles],
@@ -378,7 +379,7 @@
         ((q_ref, q_parts, refs[-2]), (k_ref, k_parts, refs[-1]))
     ):
         rows, half = out.shape[1:]
-        mine = pl.ds(pl.multiple_of(at[0] * rows, rows), rows)
+        mine = pl.ds(pl.multiple_of(table[at] * rows, rows), rows)
         for h in range(own.shape[0]):
             total = own[h, mine, :].astype(F32)
             for ref in both:
@@ -389,19 +390,18 @@
                 out[h * PAIR + u] = total[:, u * half : (u + 1) * half]
 
 
-def whole_call(kernel, outs, smem, arrays, name, scratch=()):
-    total = sum(a.size * a.dtype.itemsize for a in (*arrays, *outs))
+def whole_call(kernel, outs, table, arrays, name, scratch=()):
     return pl.pallas_call(
         kernel,
         out_shape=outs,
-        in_specs=[pl.BlockSpec(memory_space=SMEM)] * len(smem)
+        in_specs=[pl.BlockSpec(memory_space=SMEM)]
         + [pl.BlockSpec(memory_space=pltpu.VMEM)] * len(arrays),
         out_specs=[pl.BlockSpec(memory_space=pltpu.VMEM)] * len(outs),
         scratch_shapes=list(scratch),
         compiler_params=pltpu.CompilerParams(vmem_limit_bytes=LIMIT),
         cost_estimate=LITTLE,
         name=name,
-    )(*smem, *arrays)
+    )(table, *arrays)
 
 
 def after(value, *others):
@@ -444,36 +444,51 @@
         ]
         return lax.ppermute(array, ("ctx", "fsdp"), moves)
 
-    def gathered(array):
-        pieces = jnp.stack([array] + [across(array, s) for s in slots[1:]])
-        return lax.all_gather(pieces, "fsdp")
+    def both_halves(array):
+        return jnp.stack([array] + [across(array, s) for s in slots[1:]])
 
     def ints(values):
         return jnp.stack([jnp.asarray(v, jnp.int32) for v in values])
 
-    def flags(values):
-        return jnp.stack([v.astype(F32) for v in values])
-
-    slot = {s: (block + s) % grp for s in slots}
-    owner = {s: [slot[s] * part + p for p in range(part)] for s in slots}
-    place_of = [i * grp + (block - r) % grp for i in range(fsdp) for r in slots]
-    earlier = flags([other < seq * grp + block for other in place_of])
-    later = flags([other > seq * grp + block for other in place_of])
+    slot = [(block + s) % grp for s in slots]
+    owner = [slot[s] * part + p for s in slots for p in range(part)]
+    at = mine % part
+    here = seq * grp + block
+    places = [i * grp + (block - r) % grp for i in range(fsdp) for r in slots]
+    near = [(block - r) % grp for r in slots]
+    far = [(seq - r) % fsdp for r in range(1, fsdp)]
+    lists = {
+        "slot": slot,
+        "block": [block],
+        "seq": [seq],
+        "owner": owner,
+        "kv": [
+            (slot[s] * part + (at + r) % part) // replicas for r in range(part) for s in slots
+        ],
+        "sorted": [(at - r) % part for r in range(part)],
+        "places before": [other < here for other in places],
+        "places after": [other > here for other in places],
+        "near before": [b < a for a in near for b in near],
+        "near after": [b > a for a in near for b in near],
+        "far before": [other < seq for other in far],
+        "far after": [other > seq for other in far],
+    }
+    base, values = {}, []
+    for name, entries in lists.items():
+        base[name] = len(values)
+        values += entries
+    table = ints(values)
 
     own_maps = jnp.concatenate((query_map, key_map), axis=-1)
     maps = jnp.stack([own_maps] + [across(own_maps, -s) for s in slots[1:]])
     maps = lax.all_gather(maps, "fsdp")
-    at = mine % part
-    kv_table = ints(
-        [(slot[s] * part + (at + r) % part) // replicas for r in range(part) for s in slots]
-    )
-    dealt = deal(kv_table, (key_rows, value_rows), part, grp, hd)
+    dealt = deal(table, base["kv"], (key_rows, value_rows), part, grp, hd)
     moves = [[(d, d // part * part + (d + r) % part) for d in range(ctx)] for r in range(part)]
     kv = [dealt[0]] + [lax.ppermute(dealt[r], "ctx", moves[r]) for r in range(1, part)]
     (kv,) = whole_call(
-        sort_kernel,
+        functools.partial(sort_kernel, base["sorted"]),
         [jax.ShapeDtypeStruct((part, *dealt[0].shape), BF16)],
-        [ints([(at - r) % part for r in range(part)])],
+        table,
         kv,
         "sort",
     )
@@ -481,7 +496,6 @@
     params = pltpu.CompilerParams(
         dimension_semantics=("arbitrary",), vmem_limit_bytes=LIMIT
     )
-    in_smem = pl.BlockSpec(memory_space=SMEM)
     anywhere = pl.BlockSpec(memory_space=pl.ANY)
 
     def piece_spec(column, count):
@@ -516,7 +530,6 @@
     unit = 2 * heads * BLK * hd
 
     def call(kernel, s, outs, specs, out_specs, arrays, scratch, name, flops, alias=()):
-        moved = sum(a.size * a.dtype.itemsize for a in (*arrays, *outs))
         return pl.pallas_call(
             kernel,
             out_shape=outs,
@@ -531,35 +544,41 @@
             cost_estimate=LITTLE,
             input_output_aliases=dict(alias),
             name=name,
-        )(ints([slot[s], block]), *arrays)
+        )(table, *arrays)
 
     def totals_of(partial, sent=()):
         sent = dict(sent)
         parts = [partial[0]] + [
             sent[s] if s in sent else across(partial[s], s) for s in slots[1:]
         ]
-        return parts, whole_call(total_kernel, [state_shape], [], parts, "totals")[0]
-
-    def spread(parts, total, before, extra, closing):
+        return parts, whole_call(total_kernel, [state_shape], table, parts, "totals")[0]
+
+    def spread(parts, total, when, extra, closing):
         others = [along(total, r) for r in range(1, fsdp)]
-        blocks = [(block - r) % grp for r in slots]
-        block_weight = flags([before(b, a) for a in blocks for b in blocks])
-        total_weight = flags([before((seq - r) % fsdp, seq) for r in range(1, fsdp)])
+        weights = [base["near " + when], base["far " + when], base["seq"]]
         result = whole_call(
-            functools.partial(spread_kernel, grp, fsdp - 1, closing),
+            functools.partial(spread_kernel, grp, fsdp - 1, closing, *weights),
             [state_shape] * grp + [of(F32, heads, map_rows, hd)] * closing,
-            [block_weight, total_weight, ints([seq])],
+            table,
             parts + others + extra,
             "spread",
             [pltpu.VMEM((hd, hd), F32)] * closing,
         )
         return [result[0]] + [across(result[s], -s) for s in slots[1:]], result[grp:]
 
-    def sent_rows(s, table):
-        return within(pack(table, (query_rows, grad_out), part, 1, heads * hd))
+    def sent_rows(s, *earlier):
+        packed = pack(
+            after(table, *earlier),
+            base["owner"] + s * part,
+            (query_rows, grad_out),
+            part,
+            1,
+            heads * hd,
+        )
+        return within(packed)
 
     first, others = order[0], order[1:]
-    rows = {first: sent_rows(first, ints(owner[first]))}
+    rows = {first: sent_rows(first, kv)}
     partial, norm = {}, {}
     for s in order:
         partial[s], norm[s] = call(
@@ -573,15 +592,16 @@
             "states",
             unit * 2 * hd,
         )
-    norms = gathered(jnp.concatenate([norm[i] for i in slots] + [prefix_norm], axis=0))
+    halves = both_halves(jnp.concatenate([norm[i] for i in slots] + [prefix_norm], axis=0))
     parts, total = totals_of(partial)
     for s in others:
-        rows[s] = sent_rows(s, after(ints(owner[s]), *parts))
-    state, _ = spread(parts, total, lambda a, b: a < b, [prefix_state], False)
+        rows[s] = sent_rows(s, halves, *parts)
+    norms = lax.all_gather(halves, "fsdp")
+    state, _ = spread(parts, total, "before", [prefix_state], False)
 
     def front_of(s, norms):
         return call(
-            front_kernel,
+            functools.partial(front_kernel, (s, base["block"], base["places before"])),
             s,
             [
                 wide_shape,
@@ -592,7 +612,7 @@
                 row_shape,
                 state_shape,
             ],
-            [k_spec(s), q_spec, g_spec, map_spec(s), fixed_spec(*norms.shape), in_smem],
+            [k_spec(s), q_spec, g_spec, map_spec(s), fixed_spec(*norms.shape)],
             [
                 wide_spec,
                 wide_spec,
@@ -602,7 +622,7 @@
                 row_spec,
                 state_spec,
             ],
-            [kv, rows[s], rows[s], maps, norms, earlier],
+            [kv, rows[s], rows[s], maps, norms],
             [],
             "front",
             unit * 3 * BLK,
@@ -641,18 +661,22 @@
     sent = {s: across(fronts[first][6], s) for s in (first,) if s}
     for s in others:
         fronts[s] = front_of(s, after(norms, state[0], *sent.values()))
+    sent = {s: after(sent[s], *state[1:]) for s in sent}
     parts, total = totals_of({s: fronts[s][6] for s in slots}, sent)
     state[0] = after(state[0], total)
-    suffix, (grad_prefix,) = spread(parts, total, lambda a, b: a > b, [], True)
-    backs, returned, q_maps = {}, {}, []
+    backs = {0: back_of(0)}
+    parts[0] = after(parts[0], backs[0][3])
+    suffix, (grad_prefix,) = spread(parts, total, "after", [], True)
+    returned, q_maps = {}, []
     for s in slots:
         if s:
             state[s] = after(state[s], suffix[0])
-        backs[s] = back_of(s)
-        returned[s] = within(backs[s][0])
-        if s:
+            backs[s] = back_of(s)
             q_maps += [apart(rows_for(backs[s][4], seq + r), s, r) for r in range(fsdp)]
-    suffix_norms = gathered(jnp.concatenate([backs[s][3] for s in slots], axis=0))
+        returned[s] = within(after(backs[s][0], suffix[0]))
+    suffix_norms = jnp.concatenate([backs[s][3] for s in slots], axis=0)
+    suffix_norms = both_halves(after(suffix_norms, *suffix[1:]))
+    suffix_norms = lax.all_gather(suffix_norms, "fsdp")
 
     kv_type = BF16 if replicas == 1 else F32
     pairs = jnp.zeros((part, tok, grp * 2 * hd), kv_type)
@@ -661,13 +685,13 @@
         if s:
             suffix[s] = after(suffix[s], returned[0], *q_maps, *both_maps)
         pairs, key_gm[s] = call(
-            key_kernel,
+            functools.partial(key_kernel, (s, base["block"], base["places after"])),
             s,
             [of(kv_type, *pairs.shape), gm_shape],
             [k_spec(s), v_spec(s), map_spec(s), state_spec, wide_spec, dv_spec]
-            + [fixed_spec(*suffix_norms.shape), in_smem, anywhere],
+            + [fixed_spec(*suffix_norms.shape), anywhere],
             [piece_spec(lambda h: s, 2), gm_spec],
-            [kv, kv, maps, suffix[s], backs[s][1], backs[s][2], suffix_norms, later, pairs],
+            [kv, kv, maps, suffix[s], backs[s][1], backs[s][2], suffix_norms, pairs],
             [
                 pltpu.VMEM((hd, BLK), BF16),
                 pltpu.VMEM((hd, BLK), F32),
@@ -677,7 +701,7 @@
             ],
             "keys",
             unit * 4 * hd,
-            {9: 0},
+            {8: 0},
         )
         if s == 0:
             two = jnp.stack([backs[s][4], key_gm[s]])
@@ -685,12 +709,11 @@
         else:
             k_maps += [apart(rows_for(key_gm[s], seq + r), s, r) for r in range(fsdp)]
 
-    table = ints([c for s in slots for c in owner[s]])
     pairs = after(pairs, *returned.values())
     pairs = within(pairs)
-    (grad_queries,) = unpack(table, [returned[s] for s in slots], 1, heads * hd)
+    (grad_queries,) = unpack(table, base["owner"], [returned[s] for s in slots], 1, heads * hd)
     pairs = [pairs[:, :, s * 2 * hd : (s + 1) * 2 * hd] for s in slots]
-    grad_keys, grad_values = unpack(table, pairs, 2, hd)
+    grad_keys, grad_values = unpack(table, base["owner"], pairs, 2, hd)
     if replicas > 1:
         grad_keys, grad_values = (
             jnp.sum(a.reshape(tok, kv_heads, replicas, hd), axis=2)
@@ -699,9 +722,9 @@
             for a in (grad_keys, grad_values)
         )
     query_map_grad, key_map_grad = whole_call(
-        functools.partial(close_kernel, len(both_maps), len(q_maps)),
+        functools.partial(close_kernel, len(both_maps), len(q_maps), base["seq"]),
         [of(F32, heads, map_rows, half)] * 2,
-        [ints([seq])],
+        table,
         [backs[0][4], key_gm[0]] + both_maps + q_maps + k_maps,
         "close",
     )

time: 279 us -> 265 us (0.950)
  Pallas kernels: 95.1 us -> 65.8 us
  local copies, waits for them, and re-layouts: 9.87 us -> 29 us
  other arithmetic: 7.48 us -> 0.23 us
  waiting for transfers between devices: 74.7 us -> 80.7 us
  starting transfers between devices: 63.3 us -> 58.3 us
  blocking collectives: 25.2 us -> 28.3 us
    unnamed x81 -> x90, local copies, waits for them, and re-layouts: 5.88 us -> 28 us
    pallas_call x8, Pallas kernels: 66.6 us -> 53.6 us  [call(): pl.pallas_call(kernel, out_shape=outs, grid_spec=pltpu.PrefetchScalarGrid...]
    ppermute x7, waiting for transfers between devices: 58 us -> 68.8 us  [across(): lax.ppermute(array, 'ctx', [(d, (d + shift * part) % ctx) for d in range(...]
    ppermute x9, waiting for transfers between devices: 8.58 us -> 0.65 us  [along(): lax.ppermute(array, 'fsdp', [(d, (d + shift) % fsdp) for d in range(fsdp)])]
    pallas_call x6, Pallas kernels: 12.5 us -> 5.54 us  [whole_call(): pl.pallas_call(kernel, out_shape=outs, in_specs=[pl.BlockSpec(memory_spac...]
    pallas_call x2, Pallas kernels: 8.88 us -> 1.95 us  [pack(): pl.pallas_call(functools.partial(pack_kernel, columns), out_shape=jax.Sha...]
    another operation x13 -> x2, other arithmetic: 6.46 us -> 0.01 us  [both_halves(): return jnp.stack([array] + [across(array, s) for s in slots[1:]])]
    ppermute x3, waiting for transfers between devices: 0.01 us -> 4.65 us  [shards(): lax.ppermute(dealt[r], 'ctx', moves[r])]
  transfers between devices with their start and end apart: 32 -> 32, of which waited for: 11 -> 11; matrix products, arithmetic and copies ran while one was open for 4% -> 0% of each run, Pallas kernels for 24% -> 20%
where the time goes in v5:
time: 265 us; the launch traced here: 264 us
  waiting for transfers between devices  80.7 us (30%)
  Pallas kernels  65.8 us (25%)
  starting transfers between devices  58.3 us (22%)
  local copies, waits for them, and re-layouts  29 us (11%)
  blocking collectives  28.3 us (11%)
    ppermute x7, waiting for transfers between devices, across(): lax.ppermute(array, 'ctx', [(d, (d + shift * part) % ctx) for d in range(...  68.8 us
    pallas_call x8, Pallas kernels, call(): pl.pallas_call(kernel, out_shape=outs, grid_spec=pltpu.PrefetchScalarGrid...  53.6 us
    unnamed x90, local copies, waits for them, and re-layouts  28 us
    all_to_all x5, starting transfers between devices, within(): lax.all_to_all(array, 'ctx', 0, 0, axis_index_groups=blocks_of, tiled=True)  20.1 us
    ppermute x8, starting transfers between devices, apart(): return lax.ppermute(array, ('ctx', 'fsdp'), moves)  14.7 us
    all_gather x1, blocking collectives, shards(): norms = lax.all_gather(halves, 'fsdp')  14.1 us
    ppermute x7, starting transfers between devices, across(): lax.ppermute(array, 'ctx', [(d, (d + shift * part) % ctx) for d in range(...  13 us
    all_gather x1, blocking collectives, shards(): maps = lax.all_gather(maps, 'fsdp')  9.44 us
  transfers between devices with their start and end apart: 32, of which 11 were waited for; matrix products, arithmetic and copies ran while one was open for 0% of the time, Pallas kernels for 20%

profile of v5, /device:TPU:1, one launch (start us, length us, event | category | flops | bytes accessed | tf_op | source)
XLA Modules:
  0.0 263.7 jit_solution(5242531436637713488)
XLA Ops:
  15.9 3.7 %all-to-all-start.1 = ((bf16[4,128,2048]{2,1,0:T(8,128)(2,1)}), bf16[4,128,2048]{2,1,0:T(8,128)(2,1)S(1)}, u32[]{:S(2)}, u32[]{:S(2)}) async-start(bf16[4,128,2048]{2,1,0:T(8,128)(2,1)} %copy-done.7), calls=%async_computation.1 | async-start | bytes 4194304 | tf_op jit(solution)/shard_map/all_to_all | solution.py:431
  22.2 20.0 %collective-permute-done.3 = bf16[8,32,128]{2,1,0:T(8,128)(2,1)S(1)} collective-permute-done((bf16[8,32,128]{2,1,0:T(8,128)(2,1)S(1)}, bf16[8,32,128]{2,1,0:T(8,128)(2,1)S(1)}, u32[]{:S(2)}, u32[]{:S(2)}) %collective-permute-start.3) | collective-permute-done | bytes 65568 | tf_op jit(solution)/shard_map/ppermute | solution.py:434
  42.2 9.4 %all-gather = bf16[8,8,32,128]{3,2,1,0:T(8,128)(2,1)S(1)} all-gather(bf16[2,8,32,128]{3,2,1,0:T(8,128)(2,1)S(1)} %pad_maximum_fusion), channel_id=2, replica_groups=mesh['ctx'=8,'fsdp'=4] {'fsdp'}, dimensions={0}, use_global_device_ids=true | all-gather | bytes 655360 | tf_op jit(solution)/shard_map/all_gather | solution.py:484
  51.7 3.4 %states.3 = (bf16[8,128,128]{2,1,0:T(8,128)(2,1)S(1)}, f32[8,128]{1,0:T(8,128)S(1)}) custom-call(s32[54]{0:T(128)S(1)} %stack.343.table.slot, bf16[4,128,512]{2,1,0:T(8,128)(2,1)S(1)} %sort.1.k_ref.v_ref, bf16[4,128,512]{2,1,0:T(8,128)(2,1)S(1)} %sort.1.k_ref.v_ref, bf16[4,2,8,32,128]{4,3,2,1,0:T(8,128)(2,1)S(1)} %bitcast.108), custom_call_target="tpu_custom_call" | custom-call | flops 1000 | bytes 1000 | tf_op jit(solution)/shard_map/states/pallas_call | solution.py:533
  55.1 3.4 %states.2 = (bf16[8,128,128]{2,1,0:T(8,128)(2,1)S(1)}, f32[8,128]{1,0:T(8,128)S(1)}) custom-call(s32[54]{0:T(128)S(1)} %stack.343.table.slot, bf16[4,128,512]{2,1,0:T(8,128)(2,1)S(1)} %sort.1.k_ref.v_ref, bf16[4,128,512]{2,1,0:T(8,128)(2,1)S(1)} %sort.1.k_ref.v_ref, bf16[4,2,8,32,128]{4,3,2,1,0:T(8,128)(2,1)S(1)} %bitcast.109), custom_call_target="tpu_custom_call" | custom-call | flops 1000 | bytes 1000 | tf_op jit(solution)/shard_map/states/pallas_call | solution.py:533
  58.5 3.2 %collective-permute-start.5 = (bf16[8,128,128]{2,1,0:T(8,128)(2,1)S(1)}, bf16[8,128,128]{2,1,0:T(8,128)(2,1)S(1)}, u32[]{:S(2)}, u32[]{:S(2)}) collective-permute-start(bf16[8,128,128]{2,1,0:T(8,128)(2,1)S(1)} %get-tuple-element.70), channel_id=1, source_target_pairs={{0,16},{4,20},{8,24},{12,28},{16,0},{20,4},{24,8},{28,12},{1,17},{... | collective-permute-start | bytes 786440 | tf_op jit(solution)/shard_map/ppermute | solution.py:434
  61.7 12.6 %collective-permute-done.4 = f32[24,128]{1,0:T(8,128)S(1)} collective-permute-done((f32[24,128]{1,0:T(8,128)S(1)}, f32[24,128]{1,0:T(8,128)S(1)}, u32[]{:S(2)}, u32[]{:S(2)}) %collective-permute-start.4) | collective-permute-done | bytes 12320 | tf_op jit(solution)/shard_map/ppermute | solution.py:434
  77.4 4.5 %all-to-all-start = ((bf16[4,128,2048]{2,1,0:T(8,128)(2,1)}), bf16[4,128,2048]{2,1,0:T(8,128)(2,1)}, u32[]{:S(2)}, u32[]{:S(2)}) async-start(bf16[4,128,2048]{2,1,0:T(8,128)(2,1)} %copy-done.6), calls=%async_computation | async-start | bytes 4194304 | tf_op jit(solution)/shard_map/all_to_all | solution.py:431
  85.5 14.1 %all-gather.1 = f32[8,24,128]{2,1,0:T(8,128)S(1)} all-gather(f32[2,24,128]{2,1,0:T(8,128)S(1)} %pad_maximum_fusion.2), channel_id=3, replica_groups=mesh['ctx'=8,'fsdp'=4] {'fsdp'}, dimensions={0}, use_global_device_ids=true | all-gather | bytes 122880 | tf_op jit(solution)/shard_map/all_gather | solution.py:599
  99.6 7.5 %front.2 = (f32[8,128,512]{2,1,0:T(8,128)S(1)}, bf16[8,128,512]{2,1,0:T(8,128)(2,1)S(1)}, f32[8,128,512]{2,1,0:T(8,128)S(1)}, bf16[8,3,256,256]{3,2,1,0:T(8,128)...) custom-call(s32[54]{0:T(128)S(1)} %stack.343.table.slot, ...), custom_call_target="tpu_custom_call" | custom-call | flops 1000 | bytes 1000 | tf_op jit(solution)/shard_map/front/pallas_call | solution.py:533
  116.3 15.9 %collective-permute-done.9.refs_1_ = bf16[8,128,128]{2,1,0:T(8,128)(2,1)S(1)} collective-permute-done((bf16[8,128,128]{2,1,0:T(8,128)(2,1)S(1)}, bf16[8,128,128]{2,1,0:T(8,128)(2,1)S(1)}, u32[]{:S(2)}, u32[]{:S(2)}) %collective-permute-start.9) | collective-permute-done | bytes 262176 | tf_op jit(solution)/shard_map/ppermute | solution.py:434
  132.3 5.6 %collective-permute-done.10.st_ref = bf16[8,128,128]{2,1,0:T(8,128)(2,1)S(1)} collective-permute-done((bf16[8,128,128]{2,1,0:T(8,128)(2,1)S(1)}, bf16[8,128,128]{2,1,0:T(8,128)(2,1)S(1)}, u32[]{:S(2)}, u32[]{:S(2)}) %collective-permute-start.10) | collective-permute-done | bytes 262176 | tf_op jit(solution)/shard_map/ppermute | solution.py:434
  138.6 8.2 %front.3 = (f32[8,128,512]{2,1,0:T(8,128)S(1)}, bf16[8,128,512]{2,1,0:T(8,128)(2,1)S(1)}, f32[8,128,512]{2,1,0:T(8,128)S(1)}, bf16[8,3,256,256]{3,2,1,0:T(8,128)...) custom-call(s32[54]{0:T(128)S(1)} %stack.343.table.slot, ...), custom_call_target="tpu_custom_call" | custom-call | flops 1000 | bytes 1000 | tf_op jit(solution)/shard_map/front/pallas_call | solution.py:533
  151.5 10.1 %back.2 = (bf16[4,128,1024]{2,1,0:T(8,128)(2,1)S(1)}, f32[8,128,512]{2,1,0:T(8,128)S(1)}, f32[128,512]{1,0:T(8,128)S(1)}, f32[8,128]{1,0:T(8,128)S(1)}, bf16[4,128,128]{2,1,0:T(8,128)(2,1)S(1)}) custom-call(s32[54]{0:T(128)S(1)} %stack.343.table.slot, bf16[4,128,512]{2,1,0:T(8,128)(2,1)S(1)} %sort.1.k_ref.v_ref, bf16[4,128,512]{2,1,0:T(8,128)(2,1)S(1)} %sort.1.k_ref.v_ref, ...), custom_call_target="tpu_custom_call" | custom-call | flops 1000 | bytes 1000 | tf_op jit(solution)/shard_map/back/pallas_call | solution.py:533
  166.6 4.3 %all-to-all-start.2 = ((bf16[4,128,1024]{2,1,0:T(8,128)(2,1)}), bf16[4,128,1024]{2,1,0:T(8,128)(2,1)}, u32[]{:S(2)}, u32[]{:S(2)}) async-start(bf16[4,128,1024]{2,1,0:T(8,128)(2,1)} %copy-done.21), calls=%async_computation.2 | async-start | bytes 2097152 | tf_op jit(solution)/shard_map/all_to_all | solution.py:431
  177.0 10.2 %back.3 = (bf16[4,128,1024]{2,1,0:T(8,128)(2,1)S(1)}, f32[8,128,512]{2,1,0:T(8,128)S(1)}, f32[128,512]{1,0:T(8,128)S(1)}, f32[8,128]{1,0:T(8,128)S(1)}, bf16[4,128,128]{2,1,0:T(8,128)(2,1)S(1)}) custom-call(s32[54]{0:T(128)S(1)} %stack.343.table.slot, bf16[4,128,512]{2,1,0:T(8,128)(2,1)S(1)} %sort.1.k_ref.v_ref, bf16[4,128,512]{2,1,0:T(8,128)(2,1)S(1)} %sort.1.k_ref.v_ref, ...), custom_call_target="tpu_custom_call" | custom-call | flops 1000 | bytes 1000 | tf_op jit(solution)/shard_map/back/pallas_call | solution.py:533
  190.1 3.7 %all-to-all-start.3 = ((bf16[4,128,1024]{2,1,0:T(8,128)(2,1)}), bf16[4,128,1024]{2,1,0:T(8,128)(2,1)S(1)}, u32[]{:S(2)}, u32[]{:S(2)}) async-start(bf16[4,128,1024]{2,1,0:T(8,128)(2,1)} %copy-done.20), calls=%async_computation.3 | async-start | bytes 2097152 | tf_op jit(solution)/shard_map/all_to_all | solution.py:431
  195.9 14.6 %collective-permute-done.14.sx_ref = bf16[8,128,128]{2,1,0:T(8,128)(2,1)S(1)} collective-permute-done((bf16[8,128,128]{2,1,0:T(8,128)(2,1)}, bf16[8,128,128]{2,1,0:T(8,128)(2,1)S(1)}, u32[]{:S(2)}, u32[]{:S(2)}) %collective-permute-start.14) | collective-permute-done | bytes 262176 | tf_op jit(solution)/shard_map/ppermute | solution.py:434
  213.6 4.6 %collective-permute-start.16 = (bf16[4,32,128]{2,1,0:T(8,128)(2,1)S(1)}, bf16[4,32,128]{2,1,0:T(8,128)(2,1)S(1)}, u32[]{:S(2)}, u32[]{:S(2)}) collective-permute-start(bf16[4,32,128]{2,1,0:T(8,128)(2,1)S(1)} %get-tuple-element.131), channel_id=1, source_target_pairs={{0,17},{1,18},{2,19},{3,16},{4,21},{5,22},{6,23},{7,20},{8,25},{9,... | collective-permute-start | bytes 98312 | tf_op jit(solution)/shard_map/ppermute | solution.py:445
  218.2 4.8 %all-gather.2 = f32[8,16,128]{2,1,0:T(8,128)S(1)} all-gather(f32[2,16,128]{2,1,0:T(8,128)S(1)} %pad_maximum_fusion.3), channel_id=4, replica_groups=mesh['ctx'=8,'fsdp'=4] {'fsdp'}, dimensions={0}, use_global_device_ids=true | all-gather | bytes 81920 | tf_op jit(solution)/shard_map/all_gather | solution.py:679
  225.4 5.4 %keys.2 = (bf16[4,128,512]{2,1,0:T(8,128)(2,1)}, bf16[4,128,128]{2,1,0:T(8,128)(2,1)S(1)}) custom-call(s32[54]{0:T(128)S(1)} %stack.343.table.slot, bf16[4,128,512]{2,1,0:T(8,128)(2,1)S(1)} %sort.1.k_ref.v_ref, bf16[4,128,512]{2,1,0:T(8,128)(2,1)S(1)} %sort.1.k_ref.v_ref, bf16[4,2,8,32,128]{4,3,2,1,0:T(8,128)(2,1)S(1)} %bitcast.114, ...), custom_call_target="tpu_custom_call", output_to_operand_aliasing={{0}: (8, {})} | custom-call | flops 1000 | bytes 1000 | tf_op jit(solution)/shard_map/keys/pallas_call | solution.py:533
  237.0 3.4 %collective-permute-done.18.refs_6_ = bf16[4,32,128]{2,1,0:T(8,128)(2,1)S(1)} collective-permute-done((bf16[4,32,128]{2,1,0:T(8,128)(2,1)S(1)}, bf16[4,32,128]{2,1,0:T(8,128)(2,1)S(1)}, u32[]{:S(2)}, u32[]{:S(2)}) %collective-permute-start.18) | collective-permute-done | bytes 32800 | tf_op jit(solution)/shard_map/ppermute | solution.py:445
  240.4 5.4 %keys.3 = (bf16[4,128,512]{2,1,0:T(8,128)(2,1)}, bf16[4,128,128]{2,1,0:T(8,128)(2,1)S(1)}) custom-call(s32[54]{0:T(128)S(1)} %stack.343.table.slot, bf16[4,128,512]{2,1,0:T(8,128)(2,1)S(1)} %sort.1.k_ref.v_ref, bf16[4,128,512]{2,1,0:T(8,128)(2,1)S(1)} %sort.1.k_ref.v_ref, bf16[4,2,8,32,128]{4,3,2,1,0:T(8,128)(2,1)S(1)} %bitcast.115, ...), custom_call_target="tpu_custom_call", output_to_operand_aliasing={{0}: (8, {})} | custom-call | flops 1000 | bytes 1000 | tf_op jit(solution)/shard_map/keys/pallas_call | solution.py:533
  245.8 3.9 %all-to-all-start.4 = ((bf16[4,128,512]{2,1,0:T(8,128)(2,1)}), bf16[4,128,512]{2,1,0:T(8,128)(2,1)S(1)}, u32[]{:S(2)}, u32[]{:S(2)}) async-start(bf16[4,128,512]{2,1,0:T(8,128)(2,1)} %get-tuple-element.113), calls=%async_computation.4 | async-start | bytes 1048576 | tf_op jit(solution)/shard_map/all_to_all | solution.py:431
  (166 shorter events, 80.5 us)
Async XLA Ops:
  15.9 61.5 %all-to-all-start.1 = ((bf16[4,128,2048]{2,1,0:T(8,128)(2,1)}), bf16[4,128,2048]{2,1,0:T(8,128)(2,1)S(1)}, u32[]{:S(2)}, u32[]{:S(2)}) async-start(bf16[4,128,2048]{2,1,0:T(8,128)(2,1)} %copy-done.7), calls=%async_computation.1 | async-start | bytes 4194304 | tf_op jit(solution)/shard_map/all_to_all | solution.py:431
  19.8 22.5 %collective-permute-start.3 = (bf16[8,32,128]{2,1,0:T(8,128)(2,1)S(1)}, bf16[8,32,128]{2,1,0:T(8,128)(2,1)S(1)}, u32[]{:S(2)}, u32[]{:S(2)}) collective-permute-start(bf16[8,32,128]{2,1,0:T(8,128)(2,1)S(1)} %pad_maximum_fusion.1), channel_id=1, source_target_pairs={{0,16},{4,20},{8,24},{12,28},{16,0},{20,4},{24,8},{28,12},{1,17},{... | collective-permute-start | bytes 196616 | tf_op jit(solution)/shard_map/ppermute | solution.py:434
  58.5 15.9 %collective-permute-start.5 = (bf16[8,128,128]{2,1,0:T(8,128)(2,1)S(1)}, bf16[8,128,128]{2,1,0:T(8,128)(2,1)S(1)}, u32[]{:S(2)}, u32[]{:S(2)}) collective-permute-start(bf16[8,128,128]{2,1,0:T(8,128)(2,1)S(1)} %get-tuple-element.70), channel_id=1, source_target_pairs={{0,16},{4,20},{8,24},{12,28},{16,0},{20,4},{24,8},{28,12},{1,17},{... | collective-permute-start | bytes 786440 | tf_op jit(solution)/shard_map/ppermute | solution.py:434
  61.6 12.7 %collective-permute-start.4 = (f32[24,128]{1,0:T(8,128)S(1)}, f32[24,128]{1,0:T(8,128)S(1)}, u32[]{:S(2)}, u32[]{:S(2)}) collective-permute-start(f32[24,128]{1,0:T(8,128)S(1)} %constant_dynamic-update-slice_fusion), channel_id=1, source_target_pairs={{0,16},{4,20},{8,24},{12,28},{16,0},{20,4},{24,8},{28,12},{1,17},{... | collective-permute-start | bytes 36872 | tf_op jit(solution)/shard_map/ppermute | solution.py:434
  77.4 61.2 %all-to-all-start = ((bf16[4,128,2048]{2,1,0:T(8,128)(2,1)}), bf16[4,128,2048]{2,1,0:T(8,128)(2,1)}, u32[]{:S(2)}, u32[]{:S(2)}) async-start(bf16[4,128,2048]{2,1,0:T(8,128)(2,1)} %copy-done.6), calls=%async_computation | async-start | bytes 4194304 | tf_op jit(solution)/shard_map/all_to_all | solution.py:431
  83.4 30.7 %collective-permute-start.6 = (bf16[8,128,128]{2,1,0:T(8,128)(2,1)S(1)}, bf16[8,128,128]{2,1,0:T(8,128)(2,1)S(1)}, u32[]{:S(2)}, u32[]{:S(2)}) collective-permute-start(bf16[8,128,128]{2,1,0:T(8,128)(2,1)S(1)} %totals.2), channel_id=1, source_target_pairs={{0,1},{1,2},{2,3},{3,0},{4,5},{5,6},{6,7},{7,4},{8,9},{9,10},{10,1... | collective-permute-start | bytes 786440 | tf_op jit(solution)/shard_map/ppermute | solution.py:437
  84.6 29.6 %collective-permute-start.7 = (bf16[8,128,128]{2,1,0:T(8,128)(2,1)S(1)}, bf16[8,128,128]{2,1,0:T(8,128)(2,1)S(1)}, u32[]{:S(2)}, u32[]{:S(2)}) collective-permute-start(bf16[8,128,128]{2,1,0:T(8,128)(2,1)S(1)} %totals.2), channel_id=1, source_target_pairs={{0,2},{1,3},{2,0},{3,1},{4,6},{5,7},{6,4},{7,5},{8,10},{9,11},{10,... | collective-permute-start | bytes 786440 | tf_op jit(solution)/shard_map/ppermute | solution.py:437
  85.5 28.6 %collective-permute-start.8 = (bf16[8,128,128]{2,1,0:T(8,128)(2,1)S(1)}, bf16[8,128,128]{2,1,0:T(8,128)(2,1)S(1)}, u32[]{:S(2)}, u32[]{:S(2)}) collective-permute-start(bf16[8,128,128]{2,1,0:T(8,128)(2,1)S(1)} %totals.2), channel_id=1, source_target_pairs={{0,3},{1,0},{2,1},{3,2},{4,7},{5,4},{6,5},{7,6},{8,11},{9,8},{10,9... | collective-permute-start | bytes 786440 | tf_op jit(solution)/shard_map/ppermute | solution.py:437
  112.4 19.9 %collective-permute-start.9 = (bf16[8,128,128]{2,1,0:T(8,128)(2,1)S(1)}, bf16[8,128,128]{2,1,0:T(8,128)(2,1)S(1)}, u32[]{:S(2)}, u32[]{:S(2)}) collective-permute-start(bf16[8,128,128]{2,1,0:T(8,128)(2,1)S(1)} %get-tuple-element.74), channel_id=1, source_target_pairs={{0,16},{4,20},{8,24},{12,28},{16,0},{20,4},{24,8},{28,12},{1,17},{... | collective-permute-start | bytes 786440 | tf_op jit(solution)/shard_map/ppermute | solution.py:434
  115.7 22.2 %collective-permute-start.10 = (bf16[8,128,128]{2,1,0:T(8,128)(2,1)S(1)}, bf16[8,128,128]{2,1,0:T(8,128)(2,1)S(1)}, u32[]{:S(2)}, u32[]{:S(2)}) collective-permute-start(bf16[8,128,128]{2,1,0:T(8,128)(2,1)S(1)} %get-tuple-element.83), channel_id=1, source_target_pairs={{0,16},{4,20},{8,24},{12,28},{16,0},{20,4},{24,8},{28,12},{1,17},{... | collective-permute-start | bytes 786440 | tf_op jit(solution)/shard_map/ppermute | solution.py:434
  149.1 13.9 %collective-permute-start.11 = (bf16[8,128,128]{2,1,0:T(8,128)(2,1)S(1)}, bf16[8,128,128]{2,1,0:T(8,128)(2,1)S(1)}, u32[]{:S(2)}, u32[]{:S(2)}) collective-permute-start(bf16[8,128,128]{2,1,0:T(8,128)(2,1)S(1)} %totals.3), channel_id=1, source_target_pairs={{0,1},{1,2},{2,3},{3,0},{4,5},{5,6},{6,7},{7,4},{8,9},{9,10},{10,1... | collective-permute-start | bytes 786440 | tf_op jit(solution)/shard_map/ppermute | solution.py:437
  150.5 12.5 %collective-permute-start.12 = (bf16[8,128,128]{2,1,0:T(8,128)(2,1)S(1)}, bf16[8,128,128]{2,1,0:T(8,128)(2,1)S(1)}, u32[]{:S(2)}, u32[]{:S(2)}) collective-permute-start(bf16[8,128,128]{2,1,0:T(8,128)(2,1)S(1)} %totals.3), channel_id=1, source_target_pairs={{0,2},{1,3},{2,0},{3,1},{4,6},{5,7},{6,4},{7,5},{8,10},{9,11},{10,... | collective-permute-start | bytes 786440 | tf_op jit(solution)/shard_map/ppermute | solution.py:437
  151.5 12.2 %collective-permute-start.13 = (bf16[8,128,128]{2,1,0:T(8,128)(2,1)S(1)}, bf16[8,128,128]{2,1,0:T(8,128)(2,1)S(1)}, u32[]{:S(2)}, u32[]{:S(2)}) collective-permute-start(bf16[8,128,128]{2,1,0:T(8,128)(2,1)S(1)} %totals.3), channel_id=1, source_target_pairs={{0,3},{1,0},{2,1},{3,2},{4,7},{5,4},{6,5},{7,6},{8,11},{9,8},{10,9... | collective-permute-start | bytes 786440 | tf_op jit(solution)/shard_map/ppermute | solution.py:437
  166.6 23.5 %all-to-all-start.2 = ((bf16[4,128,1024]{2,1,0:T(8,128)(2,1)}), bf16[4,128,1024]{2,1,0:T(8,128)(2,1)}, u32[]{:S(2)}, u32[]{:S(2)}) async-start(bf16[4,128,1024]{2,1,0:T(8,128)(2,1)} %copy-done.21), calls=%async_computation.2 | async-start | bytes 2097152 | tf_op jit(solution)/shard_map/all_to_all | solution.py:431
  190.1 55.7 %all-to-all-start.3 = ((bf16[4,128,1024]{2,1,0:T(8,128)(2,1)}), bf16[4,128,1024]{2,1,0:T(8,128)(2,1)S(1)}, u32[]{:S(2)}, u32[]{:S(2)}) async-start(bf16[4,128,1024]{2,1,0:T(8,128)(2,1)} %copy-done.20), calls=%async_computation.3 | async-start | bytes 2097152 | tf_op jit(solution)/shard_map/all_to_all | solution.py:431
  193.9 16.6 %collective-permute-start.14 = (bf16[8,128,128]{2,1,0:T(8,128)(2,1)}, bf16[8,128,128]{2,1,0:T(8,128)(2,1)S(1)}, u32[]{:S(2)}, u32[]{:S(2)}) collective-permute-start(bf16[8,128,128]{2,1,0:T(8,128)(2,1)} %copy-done.40), channel_id=1, source_target_pairs={{0,16},{4,20},{8,24},{12,28},{16,0},{20,4},{24,8},{28,12},{1,17},{... | collective-permute-start | bytes 786440 | tf_op jit(solution)/shard_map/ppermute | solution.py:434
  210.5 7.6 %collective-permute-start.19 = (f32[16,128]{1,0:T(8,128)S(1)}, f32[16,128]{1,0:T(8,128)S(1)}, u32[]{:S(2)}, u32[]{:S(2)}) collective-permute-start(f32[16,128]{1,0:T(8,128)S(1)} %pad_maximum_fusion.4), channel_id=1, source_target_pairs={{0,16},{4,20},{8,24},{12,28},{16,0},{20,4},{24,8},{28,12},{1,17},{... | collective-permute-start | bytes 24584 | tf_op jit(solution)/shard_map/ppermute | solution.py:434
  213.5 18.9 %collective-permute-start.15 = (bf16[4,32,128]{2,1,0:T(8,128)(2,1)S(1)}, bf16[4,32,128]{2,1,0:T(8,128)(2,1)S(1)}, u32[]{:S(2)}, u32[]{:S(2)}) collective-permute-start(bf16[4,32,128]{2,1,0:T(8,128)(2,1)S(1)} %get-tuple-element.132), channel_id=1, source_target_pairs={{0,16},{1,17},{2,18},{3,19},{4,20},{5,21},{6,22},{7,23},{8,24},{9,... | collective-permute-start | bytes 98312 | tf_op jit(solution)/shard_map/ppermute | solution.py:445
  213.6 20.9 %collective-permute-start.16 = (bf16[4,32,128]{2,1,0:T(8,128)(2,1)S(1)}, bf16[4,32,128]{2,1,0:T(8,128)(2,1)S(1)}, u32[]{:S(2)}, u32[]{:S(2)}) collective-permute-start(bf16[4,32,128]{2,1,0:T(8,128)(2,1)S(1)} %get-tuple-element.131), channel_id=1, source_target_pairs={{0,17},{1,18},{2,19},{3,16},{4,21},{5,22},{6,23},{7,20},{8,25},{9,... | collective-permute-start | bytes 98312 | tf_op jit(solution)/shard_map/ppermute | solution.py:445
  230.8 9.5 %collective-permute-start.20 = (bf16[2,4,32,128]{3,2,1,0:T(8,128)(2,1)S(1)}, bf16[2,4,32,128]{3,2,1,0:T(8,128)(2,1)S(1)}, u32[]{:S(2)}, u32[]{:S(2)}) collective-permute-start(bf16[2,4,32,128]{3,2,1,0:T(8,128)(2,1)S(1)} %get-tuple-element.123), channel_id=1, source_target_pairs={{0,1},{1,2},{2,3},{3,0},{4,5},{5,6},{6,7},{7,4},{8,9},{9,10},{10,1... | collective-permute-start | bytes 196616 | tf_op jit(solution)/shard_map/ppermute | solution.py:437
  231.4 8.9 %collective-permute-start.21 = (bf16[2,4,32,128]{3,2,1,0:T(8,128)(2,1)S(1)}, bf16[2,4,32,128]{3,2,1,0:T(8,128)(2,1)S(1)}, u32[]{:S(2)}, u32[]{:S(2)}) collective-permute-start(bf16[2,4,32,128]{3,2,1,0:T(8,128)(2,1)S(1)} %get-tuple-element.124), channel_id=1, source_target_pairs={{0,2},{1,3},{2,0},{3,1},{4,6},{5,7},{6,4},{7,5},{8,10},{9,11},{10,... | collective-permute-start | bytes 196616 | tf_op jit(solution)/shard_map/ppermute | solution.py:437
  232.4 7.9 %collective-permute-start.22 = (bf16[2,4,32,128]{3,2,1,0:T(8,128)(2,1)S(1)}, bf16[2,4,32,128]{3,2,1,0:T(8,128)(2,1)S(1)}, u32[]{:S(2)}, u32[]{:S(2)}) collective-permute-start(bf16[2,4,32,128]{3,2,1,0:T(8,128)(2,1)S(1)} %get-tuple-element.122), channel_id=1, source_target_pairs={{0,3},{1,0},{2,1},{3,2},{4,7},{5,4},{6,5},{7,6},{8,11},{9,8},{10,9... | collective-permute-start | bytes 196616 | tf_op jit(solution)/shard_map/ppermute | solution.py:437
  245.8 16.4 %all-to-all-start.4 = ((bf16[4,128,512]{2,1,0:T(8,128)(2,1)}), bf16[4,128,512]{2,1,0:T(8,128)(2,1)S(1)}, u32[]{:S(2)}, u32[]{:S(2)}) async-start(bf16[4,128,512]{2,1,0:T(8,128)(2,1)} %get-tuple-element.113), calls=%async_computation.4 | async-start | bytes 1048576 | tf_op jit(solution)/shard_map/all_to_all | solution.py:431
  249.7 8.4 %collective-permute-start.23 = (bf16[4,32,128]{2,1,0:T(8,128)(2,1)S(1)}, bf16[4,32,128]{2,1,0:T(8,128)(2,1)S(1)}, u32[]{:S(2)}, u32[]{:S(2)}) collective-permute-start(bf16[4,32,128]{2,1,0:T(8,128)(2,1)S(1)} %get-tuple-element.128), channel_id=1, source_target_pairs={{0,16},{1,17},{2,18},{3,19},{4,20},{5,21},{6,22},{7,23},{8,24},{9,... | collective-permute-start | bytes 98312 | tf_op jit(solution)/shard_map/ppermute | solution.py:445
  (52 other events, 474.5 us)

commit v6 on v5

--- a/solution.py
+++ b/solution.py
@@ -10,7 +10,7 @@
 BLK = 512
 TILE = 256
 PAIR = 2
-LIMIT = 40 * 1024 * 1024
+LIMIT = 24 * 1024 * 1024
 
 LITTLE = pl.CostEstimate(flops=1000, bytes_accessed=1000, transcendentals=0)
 
@@ -37,9 +37,9 @@
     return jnp.concatenate([square] * (width // n), axis=1)
 
 
-def pick(ref, table, slot, block, weights, before):
+def pick(ref, table, slot, block, weights):
     blocks, groups = ref.shape[:2]
-    heads = ref.shape[2] // (groups + before)
+    heads = ref.shape[2] // groups
     total = jnp.zeros((heads, ref.shape[3]), F32)
     slot, block = table[slot], table[block]
     for r in range(groups):
@@ -47,8 +47,6 @@
         rows = pl.ds(pl.multiple_of(at, heads), heads)
         for i in range(blocks):
             total = total + table[weights + i * groups + r].astype(F32) * ref[i, r, rows, :]
-    if before:
-        total = total + ref[0, lax.rem(block - slot + groups, groups), groups * heads :, :]
     return total
 
 
@@ -106,46 +104,6 @@
         cost_estimate=LITTLE,
         name="pack",
     )(table, *(list(sources) * columns))
-
-
-def deal_kernel(columns, inputs, table, *refs):
-    count = columns * inputs
-    for r, out in enumerate(refs[-(len(refs) // (count + 1)) :]):
-        width = out.shape[1] // count
-        for i in range(count):
-            out[:, i * width : (i + 1) * width] = refs[r * count + i][...]
-
-
-def deal(table, base, sources, pieces, columns, width):
-    rows = sources[0].shape[0]
-    count = columns * len(sources)
-
-    def take(at):
-        return pl.BlockSpec((rows, width), lambda i, t: (0, t[base + at]))
-
-    return pl.pallas_call(
-        functools.partial(deal_kernel, columns, len(sources)),
-        out_shape=[jax.ShapeDtypeStruct((rows, count * width), sources[0].dtype)] * pieces,
-        grid_spec=pltpu.PrefetchScalarGridSpec(
-            num_scalar_prefetch=1,
-            grid=(1,),
-            in_specs=[
-                take(r * columns + s)
-                for r in range(pieces)
-                for s in range(columns)
-                for _ in sources
-            ],
-            out_specs=[pl.BlockSpec((rows, count * width), lambda i, t: (0, 0))] * pieces,
-        ),
-        compiler_params=pltpu.CompilerParams(vmem_limit_bytes=LIMIT),
-        cost_estimate=LITTLE,
-        name="deal",
-    )(table, *(list(sources) * (pieces * columns)))
-
-
-def sort_kernel(base, table, *refs):
-    for r, ref in enumerate(refs[:-1]):
-        refs[-1][table[base + r]] = ref[...]
 
 
 def unpack_kernel(outputs, base, table, *refs):
@@ -180,15 +138,28 @@
     return pl.ds(step * PAIR + u, 1)
 
 
-def state_kernel(slot, k_ref, v_ref, w_ref, out, norm_ref):
+def state_kernel(
+    near, table, k_ref, v_ref, w_ref, total_ref, before_ref, norm_ref, norm_before_ref
+):
     k_all, v_all = flat(k_ref), flat(v_ref)
     step = pl.program_id(0)
     for u in range(PAIR):
         weight = weight_rows(w_ref, u)
         feats = features(weight[weight.shape[0] // 2 :], k_all).astype(BF16)
-        out[u] = nn(feats, v_all).astype(BF16)
-        ones = jnp.ones((8, feats.shape[1]), BF16)
-        norm_ref[place(step, u), :] = nt(ones, feats)[:1]
+        ones = jnp.ones((8, BLK), BF16)
+        sums = [jnp.zeros((feats.shape[0], v_all.shape[1]), F32)] * 2
+        norms = [jnp.zeros((1, feats.shape[0]), F32)] * 2
+        for g in range(k_all.shape[0] // BLK):
+            rows = slice(g * BLK, (g + 1) * BLK)
+            part = nn(feats[:, rows], v_all[rows])
+            norm = nt(ones, feats[:, rows])[:1]
+            weight = table[near + g].astype(F32)
+            sums = [sums[0] + part, sums[1] + weight * part]
+            norms = [norms[0] + norm, norms[1] + weight * norm]
+        total_ref[u] = sums[0].astype(BF16)
+        before_ref[u] = sums[1]
+        norm_ref[place(step, u), :] = norms[0]
+        norm_before_ref[place(step, u), :] = norms[1]
 
 
 def tiles_of(j):
@@ -204,7 +175,7 @@
 
 
 def front_kernel(
-    where, table, k_ref, q_ref, g_ref, w_ref, norms_ref,
+    far, slot, table, k_ref, q_ref, g_ref, w_ref, norms_ref, before_ref, prefix_ref,
     qf_ref, kf_ref, scaled_ref, sc_ref, inv_ref, norm_ref, sx_ref,
 ):
     k_all, q_all, g_all = flat(k_ref), flat(q_ref), flat(g_ref)
@@ -213,7 +184,10 @@
 
     @pl.when(step == 0)
     def _():
-        norm_ref[...] = pick(norms_ref, table, *where, True)
+        norm = prefix_ref[...] + before_ref[...]
+        for i in range(norms_ref.shape[0]):
+            norm = norm + table[far + i].astype(F32) * norms_ref[i, slot]
+        norm_ref[...] = norm
 
     for u in range(PAIR):
         weight = weight_rows(w_ref, u)
@@ -314,7 +288,7 @@
     def _():
         vt_all[...] = turned(v_all)
         total[...] = dv_ref[...]
-        norm_all[...] = pick(norms_ref, table, *where, False)
+        norm_all[...] = pick(norms_ref, table, *where)
 
     maps = []
     for u in range(PAIR):
@@ -343,22 +317,25 @@
         refs[-1][h] = sum(ref[h].astype(F32) for ref in refs[:-1]).astype(BF16)
 
 
-def spread_kernel(grp, others, closing, block_weight, total_weight, at, table, *refs):
+def prefix_kernel(others, total_weight, table, *refs):
+    totals, (before_ref, state_ref, out) = refs[:others], refs[others:]
+    for h in range(out.shape[0]):
+        state = state_ref[h].astype(F32) + before_ref[h]
+        for i, ref in enumerate(totals):
+            state = state + table[total_weight + i].astype(F32) * ref[h].astype(F32)
+        out[h] = state.astype(BF16)
+
+
+def suffix_kernel(grp, others, block_weight, total_weight, at, table, *refs):
     parts, totals, refs = refs[:grp], refs[grp : grp + others], refs[grp + others :]
-    if closing:
-        outs, grad, scratch = refs[:grp], refs[grp], refs[grp + 1]
-    else:
-        state_ref, outs = refs[0], refs[1:]
+    outs, grad, scratch = refs[:grp], refs[grp], refs[grp + 1]
+    rows = grad.shape[1]
     for h in range(parts[0].shape[0]):
         states = [ref[h].astype(F32) for ref in parts]
         others_state = [ref[h].astype(F32) for ref in totals]
-        if closing:
-            base = jnp.zeros_like(states[0])
-            scratch[...] = sum(states) + sum(others_state)
-            rows = grad.shape[1]
-            grad[h] = scratch[pl.ds(pl.multiple_of(table[at] * rows, rows), rows), :]
-        else:
-            base = state_ref[h]
+        scratch[...] = sum(states) + sum(others_state)
+        grad[h] = scratch[pl.ds(pl.multiple_of(table[at] * rows, rows), rows), :]
+        base = jnp.zeros_like(states[0])
         for i, state in enumerate(others_state):
             base = base + table[total_weight + i].astype(F32) * state
         for r, out in enumerate(outs):
@@ -452,7 +429,6 @@
 
     slot = [(block + s) % grp for s in slots]
     owner = [slot[s] * part + p for s in slots for p in range(part)]
-    at = mine % part
     here = seq * grp + block
     places = [i * grp + (block - r) % grp for i in range(fsdp) for r in slots]
     near = [(block - r) % grp for r in slots]
@@ -463,12 +439,14 @@
         "seq": [seq],
         "owner": owner,
         "kv": [
-            (slot[s] * part + (at + r) % part) // replicas for r in range(part) for s in slots
+            ((g + s) % grp * part + p) // replicas
+            for s in slots
+            for g in slots
+            for p in range(part)
         ],
-        "sorted": [(at - r) % part for r in range(part)],
-        "places before": [other < here for other in places],
         "places after": [other > here for other in places],
-        "near before": [b < a for a in near for b in near],
+        "before": [g < block for g in slots],
+        "seq before": [i < seq for i in range(fsdp)],
         "near after": [b > a for a in near for b in near],
         "far before": [other < seq for other in far],
         "far after": [other > seq for other in far],
@@ -481,17 +459,15 @@
 
     own_maps = jnp.concatenate((query_map, key_map), axis=-1)
     maps = jnp.stack([own_maps] + [across(own_maps, -s) for s in slots[1:]])
+    kv = pack(
+        after(table, maps), base["kv"], (key_rows, value_rows), ctx, grp, hd
+    )
+    kv = lax.all_to_all(kv, "ctx", 0, 0, tiled=True)
     maps = lax.all_gather(maps, "fsdp")
-    dealt = deal(table, base["kv"], (key_rows, value_rows), part, grp, hd)
-    moves = [[(d, d // part * part + (d + r) % part) for d in range(ctx)] for r in range(part)]
-    kv = [dealt[0]] + [lax.ppermute(dealt[r], "ctx", moves[r]) for r in range(1, part)]
-    (kv,) = whole_call(
-        functools.partial(sort_kernel, base["sorted"]),
-        [jax.ShapeDtypeStruct((part, *dealt[0].shape), BF16)],
-        table,
-        kv,
-        "sort",
-    )
+    prefix_states = [prefix_state] + [
+        across(prefix_state.astype(BF16), -s) for s in slots[1:]
+    ]
+    prefix_norms = [prefix_norm] + [across(prefix_norm, -s) for s in slots[1:]]
 
     params = pltpu.CompilerParams(
         dimension_semantics=("arbitrary",), vmem_limit_bytes=LIMIT
@@ -511,10 +487,13 @@
         return jax.ShapeDtypeStruct(shape, dtype)
 
     def k_spec(s):
-        return piece_spec(lambda h: 2 * s, 1)
+        return pl.BlockSpec((part, tok, hd), lambda h, t: (t[base["block"]], 0, 2 * s))
 
     def v_spec(s):
-        return piece_spec(lambda h: 2 * s + 1, 1)
+        return pl.BlockSpec((part, tok, hd), lambda h, t: (t[base["block"]], 0, 2 * s + 1))
+
+    def all_spec(column):
+        return pl.BlockSpec((ctx, tok, hd), lambda h, t: (0, 0, column))
 
     def map_spec(s):
         return pl.BlockSpec((fsdp, None, PAIR, map_rows, 2 * half), lambda h, t: (0, s, h, 0, 0))
@@ -553,18 +532,28 @@
         ]
         return parts, whole_call(total_kernel, [state_shape], table, parts, "totals")[0]
 
-    def spread(parts, total, when, extra, closing):
+    def prefix_of(s, total, before):
         others = [along(total, r) for r in range(1, fsdp)]
-        weights = [base["near " + when], base["far " + when], base["seq"]]
+        return whole_call(
+            functools.partial(prefix_kernel, fsdp - 1, base["far before"]),
+            [state_shape],
+            table,
+            [*others, before, prefix_states[s]],
+            "prefix",
+        )[0]
+
+    def suffixes_of(parts, total):
+        others = [along(total, r) for r in range(1, fsdp)]
+        weights = [base["near after"], base["far after"], base["seq"]]
         result = whole_call(
-            functools.partial(spread_kernel, grp, fsdp - 1, closing, *weights),
-            [state_shape] * grp + [of(F32, heads, map_rows, hd)] * closing,
+            functools.partial(suffix_kernel, grp, fsdp - 1, *weights),
+            [state_shape] * grp + [of(F32, heads, map_rows, hd)],
             table,
-            parts + others + extra,
-            "spread",
-            [pltpu.VMEM((hd, hd), F32)] * closing,
+            parts + others,
+            "suffix",
+            [pltpu.VMEM((hd, hd), F32)],
         )
-        return [result[0]] + [across(result[s], -s) for s in slots[1:]], result[grp:]
+        return [result[0]] + [across(result[s], -s) for s in slots[1:]], result[grp]
 
     def sent_rows(s, *earlier):
         packed = pack(
@@ -579,29 +568,27 @@
 
     first, others = order[0], order[1:]
     rows = {first: sent_rows(first, kv)}
-    partial, norm = {}, {}
+    partial = {}
     for s in order:
-        partial[s], norm[s] = call(
-            state_kernel,
+        partial[s] = call(
+            functools.partial(state_kernel, base["before"]),
             s,
-            [state_shape, row_shape],
-            [k_spec(s), v_spec(s), map_spec(s)],
-            [state_spec, row_spec],
+            [state_shape, of(F32, heads, hd, hd), row_shape, row_shape],
+            [all_spec(2 * s), all_spec(2 * s + 1), map_spec(s)],
+            [state_spec, head_spec(hd, hd), row_spec, row_spec],
             [kv, kv, maps],
             [],
             "states",
             unit * 2 * hd,
         )
-    halves = both_halves(jnp.concatenate([norm[i] for i in slots] + [prefix_norm], axis=0))
-    parts, total = totals_of(partial)
+    norms = lax.all_gather(jnp.stack([partial[s][2] for s in slots]), "fsdp")
+    state = {s: prefix_of(s, after(partial[s][0], norms), partial[s][1]) for s in order}
     for s in others:
-        rows[s] = sent_rows(s, halves, *parts)
-    norms = lax.all_gather(halves, "fsdp")
-    state, _ = spread(parts, total, "before", [prefix_state], False)
+        rows[s] = sent_rows(s, norms)
 
     def front_of(s, norms):
         return call(
-            functools.partial(front_kernel, (s, base["block"], base["places before"])),
+            functools.partial(front_kernel, base["seq before"], s),
             s,
             [
                 wide_shape,
@@ -612,7 +599,7 @@
                 row_shape,
                 state_shape,
             ],
-            [k_spec(s), q_spec, g_spec, map_spec(s), fixed_spec(*norms.shape)],
+            [k_spec(s), q_spec, g_spec, map_spec(s), fixed_spec(*norms.shape), row_spec, row_spec],
             [
                 wide_spec,
                 wide_spec,
@@ -622,7 +609,7 @@
                 row_spec,
                 state_spec,
             ],
-            [kv, rows[s], rows[s], maps, norms],
+            [kv, rows[s], rows[s], maps, norms, partial[s][3], prefix_norms[s]],
             [],
             "front",
             unit * 3 * BLK,
@@ -657,25 +644,22 @@
         pieces = array.reshape(*array.shape[:-2], fsdp, map_rows, array.shape[-1])
         return lax.dynamic_index_in_dim(pieces, device % fsdp, array.ndim - 2, keepdims=False)
 
-    fronts = {first: front_of(first, norms)}
-    sent = {s: across(fronts[first][6], s) for s in (first,) if s}
-    for s in others:
-        fronts[s] = front_of(s, after(norms, state[0], *sent.values()))
-    sent = {s: after(sent[s], *state[1:]) for s in sent}
+    fronts, backs, sent, returned, q_maps = {}, {}, {}, {}, []
+    for s in order:
+        fronts[s] = front_of(s, after(norms, *q_maps))
+        if s:
+            sent[s] = across(fronts[s][6], s)
+            backs[s] = back_of(s)
+            q_maps += [apart(rows_for(backs[s][4], seq + r), s, r) for r in range(fsdp)]
     parts, total = totals_of({s: fronts[s][6] for s in slots}, sent)
     state[0] = after(state[0], total)
-    backs = {0: back_of(0)}
+    backs[0] = back_of(0)
     parts[0] = after(parts[0], backs[0][3])
-    suffix, (grad_prefix,) = spread(parts, total, "after", [], True)
-    returned, q_maps = {}, []
-    for s in slots:
-        if s:
-            state[s] = after(state[s], suffix[0])
-            backs[s] = back_of(s)
-            q_maps += [apart(rows_for(backs[s][4], seq + r), s, r) for r in range(fsdp)]
-        returned[s] = within(after(backs[s][0], suffix[0]))
+    suffix, grad_prefix = suffixes_of(parts, total)
+    for s in order:
+        returned[s] = within(after(backs[s][0], total if s else suffix[0]))
     suffix_norms = jnp.concatenate([backs[s][3] for s in slots], axis=0)
-    suffix_norms = both_halves(after(suffix_norms, *suffix[1:]))
+    suffix_norms = both_halves(suffix_norms)
     suffix_norms = lax.all_gather(suffix_norms, "fsdp")
 
     kv_type = BF16 if replicas == 1 else F32
@@ -683,7 +667,7 @@
     k_maps, both_maps, key_gm = [], [], {}
     for s in slots:
         if s:
-            suffix[s] = after(suffix[s], returned[0], *q_maps, *both_maps)
+            suffix[s] = after(suffix[s], *both_maps)
         pairs, key_gm[s] = call(
             functools.partial(key_kernel, (s, base["block"], base["places after"])),
             s,

time: 265 us -> 284 us (1.072)
  waiting for transfers between devices: 80.7 us -> 56 us
  blocking collectives: 28.3 us -> 50.6 us
  local copies, waits for them, and re-layouts: 29 us -> 45.5 us
  Pallas kernels: 65.8 us -> 71.1 us
  starting transfers between devices: 58.3 us -> 53.9 us
    ppermute x7 -> x6, waiting for transfers between devices: 68.8 us -> 34 us  [across(): lax.ppermute(array, 'ctx', [(d, (d + shift * part) % ctx) for d in range(...]
    all_to_all x0 -> x1, blocking collectives: none -> 32.2 us  [shards(): kv = lax.all_to_all(kv, 'ctx', 0, 0, tiled=True)]
    unnamed x90 -> x123, local copies, waits for them, and re-layouts: 28 us -> 44.5 us
    ppermute x9 -> x12, waiting for transfers between devices: 0.65 us -> 12.9 us  [along(): lax.ppermute(array, 'fsdp', [(d, (d + shift) % fsdp) for d in range(fsdp)])]
    all_gather x1, blocking collectives: 14.1 us -> 5.15 us  [shards(): norms = lax.all_gather(jnp.stack([partial[s][2] for s in slots]), 'fsdp')]
    ppermute x3 -> x0, waiting for transfers between devices: 4.65 us -> none  [shards(): lax.ppermute(dealt[r], 'ctx', moves[r])]
    ppermute x3 -> x0, starting transfers between devices: 4.54 us -> none  [shards(): lax.ppermute(dealt[r], 'ctx', moves[r])]
    ppermute x8, starting transfers between devices: 14.7 us -> 11.3 us  [apart(): return lax.ppermute(array, ('ctx', 'fsdp'), moves)]
  transfers between devices with their start and end apart: 32 -> 31, of which waited for: 11 -> 15; matrix products, arithmetic and copies ran while one was open for 0% -> 1% of each run, Pallas kernels for 20% -> 23%
where the time goes in v6:
time: 284 us; the launch traced here: 281 us
  Pallas kernels  71.1 us (25%)
  waiting for transfers between devices  56 us (20%)
  starting transfers between devices  53.9 us (19%)
  blocking collectives  50.6 us (18%)
  local copies, waits for them, and re-layouts  45.5 us (16%)
    pallas_call x8, Pallas kernels, call(): pl.pallas_call(kernel, out_shape=outs, grid_spec=pltpu.PrefetchScalarGrid...  56.5 us
    unnamed x123, local copies, waits for them, and re-layouts  44.5 us
    ppermute x6, waiting for transfers between devices, across(): lax.ppermute(array, 'ctx', [(d, (d + shift * part) % ctx) for d in range(...  34 us
    all_to_all x1, blocking collectives, shards(): kv = lax.all_to_all(kv, 'ctx', 0, 0, tiled=True)  32.2 us
    all_to_all x5, starting transfers between devices, within(): lax.all_to_all(array, 'ctx', 0, 0, axis_index_groups=blocks_of, tiled=True)  22.8 us
    ppermute x12, waiting for transfers between devices, along(): lax.ppermute(array, 'fsdp', [(d, (d + shift) % fsdp) for d in range(fsdp)])  12.9 us
    ppermute x8, starting transfers between devices, apart(): return lax.ppermute(array, ('ctx', 'fsdp'), moves)  11.3 us
    ppermute x6, starting transfers between devices, across(): lax.ppermute(array, 'ctx', [(d, (d + shift * part) % ctx) for d in range(...  11.2 us
  transfers between devices with their start and end apart: 31, of which 15 were waited for; matrix products, arithmetic and copies ran while one was open for 1% of the time, Pallas kernels for 23%

profile of v6, /device:TPU:1, one launch (start us, length us, event | category | flops | bytes accessed | tf_op | source)
XLA Modules:
  0.0 280.9 jit_solution(16868829189483448135)
XLA Ops:
  1.6 3.2 %collective-permute-start = (bf16[8,32,128]{2,1,0:T(8,128)(2,1)S(1)}, bf16[8,32,128]{2,1,0:T(8,128)(2,1)S(1)}, u32[]{:S(2)}, u32[]{:S(2)}) collective-permute-start(bf16[8,32,128]{2,1,0:T(8,128)(2,1)S(1)} %pad_maximum_fusion.1), channel_id=1, source_target_pairs={{0,16},{4,20},{8,24},{12,28},{16,0},{20,4},{24,8},{28,12},{1,17},{... | collective-permute-start | bytes 196616 | tf_op jit(solution)/shard_map/ppermute | solution.py:411
  9.8 32.2 %all_to_all.30.k_ref.v_ref = bf16[8,128,512]{2,1,0:T(8,128)(2,1)S(1)} all-to-all(bf16[8,128,512]{2,1,0:T(8,128)(2,1)S(1)} %pack.3), channel_id=1, replica_groups=mesh['ctx'=8,'fsdp'=4] {'ctx'}, dimensions={0} | all-to-all | bytes 2097152 | tf_op jit(solution)/shard_map/all_to_all | solution.py:465
  44.6 4.4 %all-to-all-start.2 = ((bf16[4,128,2048]{2,1,0:T(8,128)(2,1)}), bf16[4,128,2048]{2,1,0:T(8,128)(2,1)}, u32[]{:S(2)}, u32[]{:S(2)}) async-start(bf16[4,128,2048]{2,1,0:T(8,128)(2,1)} %pack.5), calls=%async_computation.2 | async-start | bytes 4194304 | tf_op jit(solution)/shard_map/all_to_all | solution.py:408
  49.0 8.8 %all-gather = bf16[8,8,32,128]{3,2,1,0:T(8,128)(2,1)S(1)} all-gather(bf16[2,8,32,128]{3,2,1,0:T(8,128)(2,1)S(1)} %pad_maximum_fusion), channel_id=2, replica_groups=mesh['ctx'=8,'fsdp'=4] {'fsdp'}, dimensions={0}, use_global_device_ids=true | all-gather | bytes 655360 | tf_op jit(solution)/shard_map/all_gather | solution.py:466
  57.9 4.1 %states.2 = (bf16[8,128,128]{2,1,0:T(8,128)(2,1)S(1)}, f32[8,128,128]{2,1,0:T(8,128)S(1)}, f32[8,128]{1,0:T(8,128)S(1)}, f32[8,128]{1,0:T(8,128)S(1)}) custom-call(s32[52]{0:T(128)S(1)} %stack.263.table.slot, bf16[8,128,512]{2,1,0:T(8,128)(2,1)S(1)} %all_to_all.30.k_ref.v_ref, bf16[8,128,512]{2,1,0:T(8,128)(2,1)S(1)} %all_to_all.30.k_ref.v_ref, ...), custom_call_target="tpu_custom_call" | custom-call | flops 1000 | bytes 1000 | tf_op jit(solution)/shard_map/states/pallas_call | solution.py:512
  63.5 4.8 %states.3 = (bf16[8,128,128]{2,1,0:T(8,128)(2,1)}, f32[8,128,128]{2,1,0:T(8,128)S(1)}, f32[8,128]{1,0:T(8,128)S(1)}, f32[8,128]{1,0:T(8,128)S(1)}) custom-call(s32[52]{0:T(128)S(1)} %stack.263.table.slot, bf16[8,128,512]{2,1,0:T(8,128)(2,1)S(1)} %all_to_all.30.k_ref.v_ref, bf16[8,128,512]{2,1,0:T(8,128)(2,1)S(1)} %all_to_all.30.k_ref.v_ref, ...), custom_call_target="tpu_custom_call" | custom-call | flops 1000 | bytes 1000 | tf_op jit(solution)/shard_map/states/pallas_call | solution.py:512
  69.1 5.1 %all-gather.1 = f32[8,8,128]{2,1,0:T(8,128)S(1)} all-gather(f32[2,8,128]{2,1,0:T(8,128)S(1)} %pad_maximum_fusion.3), channel_id=3, replica_groups=mesh['ctx'=8,'fsdp'=4] {'fsdp'}, dimensions={0}, use_global_device_ids=true | all-gather | bytes 40960 | tf_op jit(solution)/shard_map/all_gather | solution.py:584
  76.6 4.6 %all-to-all-start.1 = ((bf16[4,128,2048]{2,1,0:T(8,128)(2,1)}), bf16[4,128,2048]{2,1,0:T(8,128)(2,1)}, u32[]{:S(2)}, u32[]{:S(2)}) async-start(bf16[4,128,2048]{2,1,0:T(8,128)(2,1)} %copy-done.4), calls=%async_computation.1 | async-start | bytes 4194304 | tf_op jit(solution)/shard_map/all_to_all | solution.py:408
  86.1 23.7 %collective-permute-done.1.prefix_ref = f32[8,128]{1,0:T(8,128)S(1)} collective-permute-done((f32[8,128]{1,0:T(8,128)S(1)}, f32[8,128]{1,0:T(8,128)S(1)}, u32[]{:S(2)}, u32[]{:S(2)}) %collective-permute-start.1) | collective-permute-done | bytes 4128 | tf_op jit(solution)/shard_map/ppermute | solution.py:411
  109.8 8.8 %front.2 = (f32[8,128,512]{2,1,0:T(8,128)S(1)}, bf16[8,128,512]{2,1,0:T(8,128)(2,1)S(1)}, f32[8,128,512]{2,1,0:T(8,128)S(1)}, bf16[8,3,256,256]{3,2,1,0:T(8,128)...) custom-call(s32[52]{0:T(128)S(1)} %stack.263.table.slot, ...), custom_call_target="tpu_custom_call" | custom-call | flops 1000 | bytes 1000 | tf_op jit(solution)/shard_map/front/pallas_call | solution.py:512
  123.0 3.2 %collective-permute-start.13 = (bf16[8,128,128]{2,1,0:T(8,128)(2,1)}, bf16[8,128,128]{2,1,0:T(8,128)(2,1)S(1)}, u32[]{:S(2)}, u32[]{:S(2)}) collective-permute-start(bf16[8,128,128]{2,1,0:T(8,128)(2,1)} %get-tuple-element.89), channel_id=1, source_target_pairs={{0,16},{4,20},{8,24},{12,28},{16,0},{20,4},{24,8},{28,12},{1,17},{... | collective-permute-start | bytes 786440 | tf_op jit(solution)/shard_map/ppermute | solution.py:411
  133.7 9.9 %back.2 = (bf16[4,128,1024]{2,1,0:T(8,128)(2,1)S(1)}, f32[8,128,512]{2,1,0:T(8,128)S(1)}, f32[128,512]{1,0:T(8,128)S(1)}, f32[8,128]{1,0:T(8,128)S(1)}, bf16[4,128,128]{2,1,0:T(8,128)(2,1)S(1)}) custom-call(s32[52]{0:T(128)S(1)} %stack.263.table.slot, bf16[8,128,512]{2,1,0:T(8,128)(2,1)S(1)} %all_to_all.30.k_ref.v_ref, ...), custom_call_target="tpu_custom_call" | custom-call | flops 1000 | bytes 1000 | tf_op jit(solution)/shard_map/back/pallas_call | solution.py:512
  146.7 3.7 %collective-permute-start.7 = (bf16[4,32,128]{2,1,0:T(8,128)(2,1)S(1)}, bf16[4,32,128]{2,1,0:T(8,128)(2,1)S(1)}, u32[]{:S(2)}, u32[]{:S(2)}) collective-permute-start(bf16[4,32,128]{2,1,0:T(8,128)(2,1)S(1)} %get-tuple-element.127), channel_id=1, source_target_pairs={{0,17},{1,18},{2,19},{3,16},{4,21},{5,22},{6,23},{7,20},{8,25},{9,... | collective-permute-start | bytes 98312 | tf_op jit(solution)/shard_map/ppermute | solution.py:422
  152.6 3.5 %collective-permute-done.8.refs_5_ = bf16[4,32,128]{2,1,0:T(8,128)(2,1)S(1)} collective-permute-done((bf16[4,32,128]{2,1,0:T(8,128)(2,1)S(1)}, bf16[4,32,128]{2,1,0:T(8,128)(2,1)S(1)}, u32[]{:S(2)}, u32[]{:S(2)}) %collective-permute-start.8) | collective-permute-done | bytes 32800 | tf_op jit(solution)/shard_map/ppermute | solution.py:422
  156.9 8.2 %front.3 = (f32[8,128,512]{2,1,0:T(8,128)S(1)}, bf16[8,128,512]{2,1,0:T(8,128)(2,1)S(1)}, f32[8,128,512]{2,1,0:T(8,128)S(1)}, bf16[8,3,256,256]{3,2,1,0:T(8,128)...) custom-call(s32[52]{0:T(128)S(1)} %stack.263.table.slot, ...), custom_call_target="tpu_custom_call" | custom-call | flops 1000 | bytes 1000 | tf_op jit(solution)/shard_map/front/pallas_call | solution.py:512
  172.5 3.9 %all-to-all-start.4 = ((bf16[4,128,1024]{2,1,0:T(8,128)(2,1)}), bf16[4,128,1024]{2,1,0:T(8,128)(2,1)S(1)}, u32[]{:S(2)}, u32[]{:S(2)}) async-start(bf16[4,128,1024]{2,1,0:T(8,128)(2,1)} %copy-done.26), calls=%async_computation.4 | async-start | bytes 2097152 | tf_op jit(solution)/shard_map/all_to_all | solution.py:408
  183.7 5.2 %collective-permute-done.11.refs_1_ = bf16[8,128,128]{2,1,0:T(8,128)(2,1)S(1)} collective-permute-done((bf16[8,128,128]{2,1,0:T(8,128)(2,1)}, bf16[8,128,128]{2,1,0:T(8,128)(2,1)S(1)}, u32[]{:S(2)}, u32[]{:S(2)}) %collective-permute-start.11) | collective-permute-done | bytes 262176 | tf_op jit(solution)/shard_map/ppermute | solution.py:414
  198.7 9.9 %back.3 = (bf16[4,128,1024]{2,1,0:T(8,128)(2,1)S(1)}, f32[8,128,512]{2,1,0:T(8,128)S(1)}, f32[128,512]{1,0:T(8,128)S(1)}, f32[8,128]{1,0:T(8,128)S(1)}, bf16[4,128,128]{2,1,0:T(8,128)(2,1)S(1)}) custom-call(s32[52]{0:T(128)S(1)} %stack.263.table.slot, bf16[8,128,512]{2,1,0:T(8,128)(2,1)S(1)} %all_to_all.30.k_ref.v_ref, ...), custom_call_target="tpu_custom_call" | custom-call | flops 1000 | bytes 1000 | tf_op jit(solution)/shard_map/back/pallas_call | solution.py:512
  211.7 4.3 %all-to-all-start.3 = ((bf16[4,128,1024]{2,1,0:T(8,128)(2,1)}), bf16[4,128,1024]{2,1,0:T(8,128)(2,1)}, u32[]{:S(2)}, u32[]{:S(2)}) async-start(bf16[4,128,1024]{2,1,0:T(8,128)(2,1)} %copy-done.27), calls=%async_computation.3 | async-start | bytes 2097152 | tf_op jit(solution)/shard_map/all_to_all | solution.py:408
  218.4 9.7 %collective-permute-done.18 = f32[16,128]{1,0:T(8,128)S(1)} collective-permute-done((f32[16,128]{1,0:T(8,128)S(1)}, f32[16,128]{1,0:T(8,128)S(1)}, u32[]{:S(2)}, u32[]{:S(2)}) %collective-permute-start.18) | collective-permute-done | bytes 8224 | tf_op jit(solution)/shard_map/ppermute | solution.py:411
  228.1 4.5 %all-gather.2 = f32[8,16,128]{2,1,0:T(8,128)S(1)} all-gather(f32[2,16,128]{2,1,0:T(8,128)S(1)} %pad_maximum_fusion.2), channel_id=4, replica_groups=mesh['ctx'=8,'fsdp'=4] {'fsdp'}, dimensions={0}, use_global_device_ids=true | all-gather | bytes 81920 | tf_op jit(solution)/shard_map/all_gather | solution.py:663
  236.9 5.5 %keys.2 = (bf16[4,128,512]{2,1,0:T(8,128)(2,1)}, bf16[4,128,128]{2,1,0:T(8,128)(2,1)S(1)}) custom-call(s32[52]{0:T(128)S(1)} %stack.263.table.slot, bf16[8,128,512]{2,1,0:T(8,128)(2,1)S(1)} %all_to_all.30.k_ref.v_ref, bf16[8,128,512]{2,1,0:T(8,128)(2,1)S(1)} %all_to_all.30.k_ref.v_ref, ...), custom_call_target="tpu_custom_call", output_to_operand_aliasing={{0}: (8, {})} | custom-call | flops 1000 | bytes 1000 | tf_op jit(solution)/shard_map/keys/pallas_call | solution.py:512
  248.8 5.5 %keys.3 = (bf16[4,128,512]{2,1,0:T(8,128)(2,1)}, bf16[4,128,128]{2,1,0:T(8,128)(2,1)S(1)}) custom-call(s32[52]{0:T(128)S(1)} %stack.263.table.slot, bf16[8,128,512]{2,1,0:T(8,128)(2,1)S(1)} %all_to_all.30.k_ref.v_ref, bf16[8,128,512]{2,1,0:T(8,128)(2,1)S(1)} %all_to_all.30.k_ref.v_ref, ...), custom_call_target="tpu_custom_call", output_to_operand_aliasing={{0}: (8, {})} | custom-call | flops 1000 | bytes 1000 | tf_op jit(solution)/shard_map/keys/pallas_call | solution.py:512
  254.2 5.6 %all-to-all-start.5 = ((bf16[4,128,512]{2,1,0:T(8,128)(2,1)}), bf16[4,128,512]{2,1,0:T(8,128)(2,1)S(1)}, u32[]{:S(2)}, u32[]{:S(2)}) async-start(bf16[4,128,512]{2,1,0:T(8,128)(2,1)} %get-tuple-element.109), calls=%async_computation.5 | async-start | bytes 1048576 | tf_op jit(solution)/shard_map/all_to_all | solution.py:408
  (196 shorter events, 97.7 us)
Async XLA Ops:
  44.6 32.0 %all-to-all-start.2 = ((bf16[4,128,2048]{2,1,0:T(8,128)(2,1)}), bf16[4,128,2048]{2,1,0:T(8,128)(2,1)}, u32[]{:S(2)}, u32[]{:S(2)}) async-start(bf16[4,128,2048]{2,1,0:T(8,128)(2,1)} %pack.5), calls=%async_computation.2 | async-start | bytes 4194304 | tf_op jit(solution)/shard_map/all_to_all | solution.py:408
  76.6 80.3 %all-to-all-start.1 = ((bf16[4,128,2048]{2,1,0:T(8,128)(2,1)}), bf16[4,128,2048]{2,1,0:T(8,128)(2,1)}, u32[]{:S(2)}, u32[]{:S(2)}) async-start(bf16[4,128,2048]{2,1,0:T(8,128)(2,1)} %copy-done.4), calls=%async_computation.1 | async-start | bytes 4194304 | tf_op jit(solution)/shard_map/all_to_all | solution.py:408
  81.9 44.3 %collective-permute-start.5 = (bf16[8,128,128]{2,1,0:T(8,128)(2,1)}, bf16[8,128,128]{2,1,0:T(8,128)(2,1)}, u32[]{:S(2)}, u32[]{:S(2)}) collective-permute-start(bf16[8,128,128]{2,1,0:T(8,128)(2,1)} %convert_element_type.2), channel_id=1, source_target_pairs={{0,16},{4,20},{8,24},{12,28},{16,0},{20,4},{24,8},{28,12},{1,17},{... | collective-permute-start | bytes 786440 | tf_op jit(solution)/shard_map/ppermute | solution.py:411
  82.7 43.5 %collective-permute-start.2 = (bf16[8,128,128]{2,1,0:T(8,128)(2,1)}, bf16[8,128,128]{2,1,0:T(8,128)(2,1)}, u32[]{:S(2)}, u32[]{:S(2)}) collective-permute-start(bf16[8,128,128]{2,1,0:T(8,128)(2,1)} %get-tuple-element.74), channel_id=1, source_target_pairs={{0,1},{1,2},{2,3},{3,0},{4,5},{5,6},{6,7},{7,4},{8,9},{9,10},{10,1... | collective-permute-start | bytes 786440 | tf_op jit(solution)/shard_map/ppermute | solution.py:414
  83.6 42.6 %collective-permute-start.3 = (bf16[8,128,128]{2,1,0:T(8,128)(2,1)}, bf16[8,128,128]{2,1,0:T(8,128)(2,1)}, u32[]{:S(2)}, u32[]{:S(2)}) collective-permute-start(bf16[8,128,128]{2,1,0:T(8,128)(2,1)} %get-tuple-element.74), channel_id=1, source_target_pairs={{0,2},{1,3},{2,0},{3,1},{4,6},{5,7},{6,4},{7,5},{8,10},{9,11},{10,... | collective-permute-start | bytes 786440 | tf_op jit(solution)/shard_map/ppermute | solution.py:414
  84.5 41.7 %collective-permute-start.4 = (bf16[8,128,128]{2,1,0:T(8,128)(2,1)}, bf16[8,128,128]{2,1,0:T(8,128)(2,1)}, u32[]{:S(2)}, u32[]{:S(2)}) collective-permute-start(bf16[8,128,128]{2,1,0:T(8,128)(2,1)} %get-tuple-element.74), channel_id=1, source_target_pairs={{0,3},{1,0},{2,1},{3,2},{4,7},{5,4},{6,5},{7,6},{8,11},{9,8},{10,9... | collective-permute-start | bytes 786440 | tf_op jit(solution)/shard_map/ppermute | solution.py:414
  84.5 25.3 %collective-permute-start.1 = (f32[8,128]{1,0:T(8,128)S(1)}, f32[8,128]{1,0:T(8,128)S(1)}, u32[]{:S(2)}, u32[]{:S(2)}) collective-permute-start(f32[8,128]{1,0:T(8,128)S(1)} %copy-done.57), channel_id=1, source_target_pairs={{0,16},{4,20},{8,24},{12,28},{16,0},{20,4},{24,8},{28,12},{1,17},{... | collective-permute-start | bytes 12296 | tf_op jit(solution)/shard_map/ppermute | solution.py:411
  123.0 47.5 %collective-permute-start.13 = (bf16[8,128,128]{2,1,0:T(8,128)(2,1)}, bf16[8,128,128]{2,1,0:T(8,128)(2,1)S(1)}, u32[]{:S(2)}, u32[]{:S(2)}) collective-permute-start(bf16[8,128,128]{2,1,0:T(8,128)(2,1)} %get-tuple-element.89), channel_id=1, source_target_pairs={{0,16},{4,20},{8,24},{12,28},{16,0},{20,4},{24,8},{28,12},{1,17},{... | collective-permute-start | bytes 786440 | tf_op jit(solution)/shard_map/ppermute | solution.py:411
  146.7 5.9 %collective-permute-start.7 = (bf16[4,32,128]{2,1,0:T(8,128)(2,1)S(1)}, bf16[4,32,128]{2,1,0:T(8,128)(2,1)S(1)}, u32[]{:S(2)}, u32[]{:S(2)}) collective-permute-start(bf16[4,32,128]{2,1,0:T(8,128)(2,1)S(1)} %get-tuple-element.127), channel_id=1, source_target_pairs={{0,17},{1,18},{2,19},{3,16},{4,21},{5,22},{6,23},{7,20},{8,25},{9,... | collective-permute-start | bytes 98312 | tf_op jit(solution)/shard_map/ppermute | solution.py:422
  150.4 5.7 %collective-permute-start.8 = (bf16[4,32,128]{2,1,0:T(8,128)(2,1)S(1)}, bf16[4,32,128]{2,1,0:T(8,128)(2,1)S(1)}, u32[]{:S(2)}, u32[]{:S(2)}) collective-permute-start(bf16[4,32,128]{2,1,0:T(8,128)(2,1)S(1)} %get-tuple-element.126), channel_id=1, source_target_pairs={{0,18},{1,19},{2,16},{3,17},{4,22},{5,23},{6,20},{7,21},{8,26},{9,... | collective-permute-start | bytes 98312 | tf_op jit(solution)/shard_map/ppermute | solution.py:422
  150.9 6.1 %collective-permute-start.9 = (bf16[4,32,128]{2,1,0:T(8,128)(2,1)S(1)}, bf16[4,32,128]{2,1,0:T(8,128)(2,1)S(1)}, u32[]{:S(2)}, u32[]{:S(2)}) collective-permute-start(bf16[4,32,128]{2,1,0:T(8,128)(2,1)S(1)} %get-tuple-element.125), channel_id=1, source_target_pairs={{0,19},{1,16},{2,17},{3,18},{4,23},{5,20},{6,21},{7,22},{8,27},{9,... | collective-permute-start | bytes 98312 | tf_op jit(solution)/shard_map/ppermute | solution.py:422
  172.5 39.2 %all-to-all-start.4 = ((bf16[4,128,1024]{2,1,0:T(8,128)(2,1)}), bf16[4,128,1024]{2,1,0:T(8,128)(2,1)S(1)}, u32[]{:S(2)}, u32[]{:S(2)}) async-start(bf16[4,128,1024]{2,1,0:T(8,128)(2,1)} %copy-done.26), calls=%async_computation.4 | async-start | bytes 2097152 | tf_op jit(solution)/shard_map/all_to_all | solution.py:408
  176.4 6.2 %collective-permute-start.10 = (bf16[8,128,128]{2,1,0:T(8,128)(2,1)}, bf16[8,128,128]{2,1,0:T(8,128)(2,1)S(1)}, u32[]{:S(2)}, u32[]{:S(2)}) collective-permute-start(bf16[8,128,128]{2,1,0:T(8,128)(2,1)} %copy-done.60), channel_id=1, source_target_pairs={{0,1},{1,2},{2,3},{3,0},{4,5},{5,6},{6,7},{7,4},{8,9},{9,10},{10,1... | collective-permute-start | bytes 786440 | tf_op jit(solution)/shard_map/ppermute | solution.py:414
  177.0 12.0 %collective-permute-start.11 = (bf16[8,128,128]{2,1,0:T(8,128)(2,1)}, bf16[8,128,128]{2,1,0:T(8,128)(2,1)S(1)}, u32[]{:S(2)}, u32[]{:S(2)}) collective-permute-start(bf16[8,128,128]{2,1,0:T(8,128)(2,1)} %copy-done.60), channel_id=1, source_target_pairs={{0,2},{1,3},{2,0},{3,1},{4,6},{5,7},{6,4},{7,5},{8,10},{9,11},{10,... | collective-permute-start | bytes 786440 | tf_op jit(solution)/shard_map/ppermute | solution.py:414
  177.5 14.0 %collective-permute-start.12 = (bf16[8,128,128]{2,1,0:T(8,128)(2,1)}, bf16[8,128,128]{2,1,0:T(8,128)(2,1)S(1)}, u32[]{:S(2)}, u32[]{:S(2)}) collective-permute-start(bf16[8,128,128]{2,1,0:T(8,128)(2,1)} %copy-done.60), channel_id=1, source_target_pairs={{0,3},{1,0},{2,1},{3,2},{4,7},{5,4},{6,5},{7,6},{8,11},{9,8},{10,9... | collective-permute-start | bytes 786440 | tf_op jit(solution)/shard_map/ppermute | solution.py:414
  177.7 32.2 %collective-permute-start.14 = (bf16[8,128,128]{2,1,0:T(8,128)(2,1)}, bf16[8,128,128]{2,1,0:T(8,128)(2,1)S(1)}, u32[]{:S(2)}, u32[]{:S(2)}) collective-permute-start(bf16[8,128,128]{2,1,0:T(8,128)(2,1)} %copy-done.40), channel_id=1, source_target_pairs={{0,1},{1,2},{2,3},{3,0},{4,5},{5,6},{6,7},{7,4},{8,9},{9,10},{10,1... | collective-permute-start | bytes 786440 | tf_op jit(solution)/shard_map/ppermute | solution.py:414
  179.3 30.6 %collective-permute-start.15 = (bf16[8,128,128]{2,1,0:T(8,128)(2,1)}, bf16[8,128,128]{2,1,0:T(8,128)(2,1)S(1)}, u32[]{:S(2)}, u32[]{:S(2)}) collective-permute-start(bf16[8,128,128]{2,1,0:T(8,128)(2,1)} %copy-done.40), channel_id=1, source_target_pairs={{0,2},{1,3},{2,0},{3,1},{4,6},{5,7},{6,4},{7,5},{8,10},{9,11},{10,... | collective-permute-start | bytes 786440 | tf_op jit(solution)/shard_map/ppermute | solution.py:414
  182.5 27.4 %collective-permute-start.16 = (bf16[8,128,128]{2,1,0:T(8,128)(2,1)}, bf16[8,128,128]{2,1,0:T(8,128)(2,1)S(1)}, u32[]{:S(2)}, u32[]{:S(2)}) collective-permute-start(bf16[8,128,128]{2,1,0:T(8,128)(2,1)} %copy-done.40), channel_id=1, source_target_pairs={{0,3},{1,0},{2,1},{3,2},{4,7},{5,4},{6,5},{7,6},{8,11},{9,8},{10,9... | collective-permute-start | bytes 786440 | tf_op jit(solution)/shard_map/ppermute | solution.py:414
  211.7 42.6 %all-to-all-start.3 = ((bf16[4,128,1024]{2,1,0:T(8,128)(2,1)}), bf16[4,128,1024]{2,1,0:T(8,128)(2,1)}, u32[]{:S(2)}, u32[]{:S(2)}) async-start(bf16[4,128,1024]{2,1,0:T(8,128)(2,1)} %copy-done.27), calls=%async_computation.3 | async-start | bytes 2097152 | tf_op jit(solution)/shard_map/all_to_all | solution.py:408
  216.0 12.1 %collective-permute-start.18 = (f32[16,128]{1,0:T(8,128)S(1)}, f32[16,128]{1,0:T(8,128)S(1)}, u32[]{:S(2)}, u32[]{:S(2)}) collective-permute-start(f32[16,128]{1,0:T(8,128)S(1)} %constant_dynamic-update-slice_fusion), channel_id=1, source_target_pairs={{0,16},{4,20},{8,24},{12,28},{16,0},{20,4},{24,8},{28,12},{1,17},{... | collective-permute-start | bytes 24584 | tf_op jit(solution)/shard_map/ppermute | solution.py:411
  217.4 31.3 %collective-permute-start.17 = (bf16[8,128,128]{2,1,0:T(8,128)(2,1)}, bf16[8,128,128]{2,1,0:T(8,128)(2,1)S(1)}, u32[]{:S(2)}, u32[]{:S(2)}) collective-permute-start(bf16[8,128,128]{2,1,0:T(8,128)(2,1)} %get-tuple-element.98), channel_id=1, source_target_pairs={{0,16},{4,20},{8,24},{12,28},{16,0},{20,4},{24,8},{28,12},{1,17},{... | collective-permute-start | bytes 786440 | tf_op jit(solution)/shard_map/ppermute | solution.py:411
  254.2 25.2 %all-to-all-start.5 = ((bf16[4,128,512]{2,1,0:T(8,128)(2,1)}), bf16[4,128,512]{2,1,0:T(8,128)(2,1)S(1)}, u32[]{:S(2)}, u32[]{:S(2)}) async-start(bf16[4,128,512]{2,1,0:T(8,128)(2,1)} %get-tuple-element.109), calls=%async_computation.5 | async-start | bytes 1048576 | tf_op jit(solution)/shard_map/all_to_all | solution.py:408
  259.9 6.2 %collective-permute-start.22 = (bf16[4,32,128]{2,1,0:T(8,128)(2,1)S(1)}, bf16[4,32,128]{2,1,0:T(8,128)(2,1)S(1)}, u32[]{:S(2)}, u32[]{:S(2)}) collective-permute-start(bf16[4,32,128]{2,1,0:T(8,128)(2,1)S(1)} %get-tuple-element.124), channel_id=1, source_target_pairs={{0,16},{1,17},{2,18},{3,19},{4,20},{5,21},{6,22},{7,23},{8,24},{9,... | collective-permute-start | bytes 98312 | tf_op jit(solution)/shard_map/ppermute | solution.py:422
  260.8 6.0 %collective-permute-start.23 = (bf16[4,32,128]{2,1,0:T(8,128)(2,1)S(1)}, bf16[4,32,128]{2,1,0:T(8,128)(2,1)S(1)}, u32[]{:S(2)}, u32[]{:S(2)}) collective-permute-start(bf16[4,32,128]{2,1,0:T(8,128)(2,1)S(1)} %get-tuple-element.123), channel_id=1, source_target_pairs={{0,17},{1,18},{2,19},{3,16},{4,21},{5,22},{6,23},{7,20},{8,25},{9,... | collective-permute-start | bytes 98312 | tf_op jit(solution)/shard_map/ppermute | solution.py:422
  (68 other events, 344.8 us)

commit v7 on v2

v7 whole, which is shorter than its diff:
```python
import functools

import jax
import jax.numpy as jnp
from jax import lax
from jax.experimental import pallas as pl
from jax.experimental.pallas import tpu as pltpu
from jax.sharding import PartitionSpec as P

BLK = 512
TILE = 256
PAIR = 2
EXT = 16
LIMIT = 40 * 1024 * 1024

LITTLE = pl.CostEstimate(flops=1000, bytes_accessed=1000, transcendentals=0)

F32 = jnp.float32
BF16 = jnp.bfloat16
SMEM = pltpu.SMEM


def nn(left, right):
    return lax.dot_general(left, right, (((1,), (0,)), ((), ())), preferred_element_type=F32)


def nt(left, right):
    return lax.dot_general(left, right, (((1,), (1,)), ((), ())), preferred_element_type=F32)


def turned(array):
    return array.astype(F32).T.astype(array.dtype)


def column(row, width):
    n = row.shape[1]
    square = jnp.broadcast_to(row, (n, n)).T
    return jnp.concatenate([square] * (width // n), axis=1)


def thirds(row):
    rows = jnp.broadcast_to(row, (EXT, row.shape[1]))
    high = rows.astype(BF16).astype(F32)
    middle = (rows - high).astype(BF16).astype(F32)
    low = rows - high - middle
    place = lax.broadcasted_iota(jnp.int32, rows.shape, 0)
    picked = jnp.where(place == 0, high, jnp.where(place == 1, middle, low))
    return jnp.where(place < 3, picked, 0.0).astype(BF16)


def whole_row(block):
    return jnp.sum(block.astype(F32), axis=0, keepdims=True)


def weight_rows(ref, u):
    whole = jnp.concatenate([ref[i, u] for i in range(ref.shape[0])], axis=0)
    return turned(whole)


def features(weight, rows):
    logits = nt(weight, rows).astype(BF16).astype(F32)
    upper = jnp.exp(logits)
    lower = jnp.exp(-logits)
    upper = upper * (1.0 / jnp.sum(upper, axis=0, keepdims=True))
    lower = lower * (1.0 / jnp.sum(lower, axis=0, keepdims=True))
    return jnp.concatenate([upper, lower], axis=0)


def feature_back(feats, upstream):
    half = feats.shape[0] // 2
    weighted = feats * upstream
    first, second = weighted[:half], weighted[half:]
    first = first - feats[:half] * jnp.sum(first, axis=0, keepdims=True)
    second = second - feats[half:] * jnp.sum(second, axis=0, keepdims=True)
    return (first - second).astype(BF16)


def gather(table, base, refs, out):
    rows = refs[0].shape[0]
    for r, ref in enumerate(refs):
        out[pl.ds(pl.multiple_of(table[base + r] * rows, rows), rows), :] = ref[...]


def pack_kernel(columns, inputs, table, *refs):
    count = columns * inputs
    for r, out in enumerate(refs[-(len(refs) // (count + 1)) :]):
        width = out.shape[1] // count
        for i in range(count):
            out[:, i * width : (i + 1) * width] = refs[r * count + i][...]


def pack(table, base, sources, pieces, columns, width):
    rows = sources[0].shape[0]
    count = columns * len(sources)
    step = rows // 2

    def take(at):
        return pl.BlockSpec((step, width), lambda i, t: (i, t[base + at]))

    return pl.pallas_call(
        functools.partial(pack_kernel, columns, len(sources)),
        out_shape=[jax.ShapeDtypeStruct((rows, count * width), sources[0].dtype)] * pieces,
        grid_spec=pltpu.PrefetchScalarGridSpec(
            num_scalar_prefetch=1,
            grid=(rows // step,),
            in_specs=[
                take(r * columns + s)
                for r in range(pieces)
                for s in range(columns)
                for _ in sources
            ],
            out_specs=[pl.BlockSpec((step, count * width), lambda i, t: (i, 0))] * pieces,
        ),
        compiler_params=pltpu.CompilerParams(vmem_limit_bytes=LIMIT),
        cost_estimate=LITTLE,
        name="pack",
    )(table, *(list(sources) * (pieces * columns)))


def unpack_kernel(outputs, base, table, *refs):
    sources, outs = refs[:-outputs], refs[-outputs:]
    for s, source in enumerate(sources):
        pieces = source.shape[0]
        width = source.shape[2] // outputs
        for r in range(pieces):
            at = pl.ds(pl.multiple_of(table[base + s * pieces + r] * width, width), width)
            for i, out in enumerate(outs):
                out[:, at] = source[r, :, i * width : (i + 1) * width]


def unpack(table, base, sources, outputs, width):
    pieces, rows = sources[0].shape[:2]
    total = len(sources) * pieces * width
    step = rows // 2
    return pl.pallas_call(
        functools.partial(unpack_kernel, outputs, base),
        out_shape=[jax.ShapeDtypeStruct((rows, total), sources[0].dtype)] * outputs,
        grid=(rows // step,),
        in_specs=[pl.BlockSpec(memory_space=SMEM)]
        + [pl.BlockSpec((pieces, step, outputs * width), lambda i: (0, i, 0))] * len(sources),
        out_specs=[pl.BlockSpec((step, total), lambda i: (i, 0))] * outputs,
        compiler_params=pltpu.CompilerParams(vmem_limit_bytes=LIMIT),
        cost_estimate=LITTLE,
        name="unpack",
    )(table, *sources)


def state_kernel(part, base, table, *refs):
    k_refs, v_refs, (w_ref, out, k_all, v_all) = refs[:part], refs[part : 2 * part], refs[2 * part :]
    hd = k_all.shape[1]

    @pl.when(pl.program_id(0) == 0)
    def _():
        gather(table, base, k_refs, k_all)
        gather(table, base, v_refs, v_all)

    for u in range(out.shape[0]):
        weight = weight_rows(w_ref, u)
        feats = features(weight[weight.shape[0] // 2 :], k_all[...]).astype(BF16)
        out[u, :hd, :] = nn(feats, v_all[...]).astype(BF16)
        ones = jnp.ones((EXT, feats.shape[1]), BF16)
        out[u, hd:, :] = thirds(nt(ones, feats)[:1])


def block_kernel(part, base, table, *refs):
    k_refs, v_refs = refs[:part], refs[part : 2 * part]
    q_refs, g_refs = refs[2 * part : 3 * part], refs[3 * part : 4 * part]
    w_ref, st_ref = refs[4 * part : 4 * part + 2]
    gq_ref, dk_ref, dv_ref, sx_ref, gm_ref, k_all, v_all, vt_all, q_all, g_all = refs[4 * part + 2 :]
    hd = k_all.shape[1]

    @pl.when(pl.program_id(0) == 0)
    def _():
        gather(table, base, k_refs, k_all)
        gather(table, base, v_refs, v_all)
        vt_all[...] = turned(v_all[...])
        dv_ref[...] = jnp.zeros_like(dv_ref)

    gather(table, base, q_refs, q_all)
    gather(table, base, g_refs, g_all)
    maps = []
    earlier = lax.broadcasted_iota(jnp.int32, (TILE, TILE), 0) <= lax.broadcasted_iota(
        jnp.int32, (TILE, TILE), 1
    )

    def causal(array, begin):
        masked = jnp.where(earlier, array[begin:], 0.0)
        return masked if begin == 0 else jnp.concatenate([array[:begin], masked], axis=0)

    for u in range(PAIR):
        weight = weight_rows(w_ref, u)
        half = weight.shape[0] // 2
        lanes = slice(u * hd, (u + 1) * hd)
        q_feat = features(weight[:half], q_all[:, lanes])
        k_low = features(weight[half:], k_all[...]).astype(BF16)
        q_low = q_feat.astype(BF16)
        k_turned = turned(k_low)
        state = st_ref[u, :hd, :]
        state_turned = turned(state)
        norm = column(whole_row(st_ref[u, hd:, :]), TILE)
        g_turned = g_all[:, lanes].astype(F32).T
        back = []
        dkey = [jnp.zeros((2 * half, TILE), F32) for _ in range(BLK // TILE)]
        dvalue = [jnp.zeros((hd, TILE), F32) for _ in range(BLK // TILE)]
        suffix = jnp.zeros((2 * half, hd), F32)
        suffix_norm = jnp.zeros((2 * half, 1), F32)
        for j in range(BLK // TILE):
            begin, end = j * TILE, (j + 1) * TILE
            own = q_low[:, begin:end]
            own_wide = own.astype(F32)
            scores = causal(nn(k_turned[:end], own), begin)
            scores_low = scores.astype(BF16)
            numerator = nn(state_turned, own) + nn(vt_all[:, :end], scores_low)
            denominator = jnp.sum(own_wide * norm, axis=0, keepdims=True) + jnp.sum(
                scores, axis=0, keepdims=True
            )
            inverse = 1.0 / denominator
            scaled = g_turned[:, begin:end] * inverse
            scaled_low = scaled.astype(BF16)
            norm_grad = -jnp.sum(scaled * (numerator * inverse), axis=0, keepdims=True)
            dscores = causal(nn(v_all[:end, :], scaled_low) + norm_grad, begin).astype(BF16)
            dquery = nn(state, scaled_low) + norm * norm_grad + nn(k_low[:, :end], dscores)
            back.append(feature_back(q_feat[:, begin:end], dquery))
            for i in range(j + 1):
                rows = slice(i * TILE, (i + 1) * TILE)
                dkey[i] = dkey[i] + nt(own, dscores[rows])
                dvalue[i] = dvalue[i] + nt(scaled_low, scores_low[rows])
            suffix = suffix + nt(own, scaled_low)
            suffix_norm = suffix_norm + jnp.sum(own_wide * norm_grad, axis=1, keepdims=True)
        dlog = jnp.concatenate(back, axis=1)
        grads = nn(turned(dlog), weight[:half]).astype(BF16)
        gq_ref[:, :, lanes] = grads.reshape(gq_ref.shape[0], -1, hd)
        maps.append(nn(dlog, q_all[:, lanes]))
        dk_ref[u] = jnp.concatenate(dkey, axis=1)
        dv_ref[...] += jnp.concatenate(dvalue, axis=1)
        sx_ref[u, :hd, :] = suffix.astype(BF16)
        sx_ref[u, hd:, :] = thirds(jnp.broadcast_to(suffix_norm, (2 * half, 2 * half)).T[:1])
    gm_ref[0] = jnp.concatenate(maps, axis=0).T.astype(gm_ref.dtype)


def key_kernel(part, base, table, *refs):
    k_refs, v_refs = refs[:part], refs[part : 2 * part]
    w_ref, sx_ref, dk_ref, dv_ref = refs[2 * part : 2 * part + 4]
    out, gm_ref, k_all, v_all, vt_all, total, logs, weights = refs[2 * part + 5 :]
    hd = k_all.shape[1]
    step = pl.program_id(0)

    @pl.when(step == 0)
    def _():
        gather(table, base, k_refs, k_all)
        gather(table, base, v_refs, v_all)
        vt_all[...] = turned(v_all[...])
        total[...] = dv_ref[...]

    maps = []
    for u in range(PAIR):
        weight = weight_rows(w_ref, u)
        half = weight.shape[0] // 2
        weight = weight[half:]
        feats = features(weight, k_all[...])
        suffix = sx_ref[u, :hd, :]
        norm = column(whole_row(sx_ref[u, hd:, :]), BLK)
        dlog = feature_back(feats, dk_ref[u] + nn(suffix, vt_all[...]) + norm)
        at = pl.ds(pl.multiple_of((step * PAIR + u) * half, half), half)
        logs[at, :] = dlog
        weights[at, :] = weight
        maps.append(nn(dlog, k_all[...]))
        total[...] += nn(turned(suffix), feats.astype(BF16))
    gm_ref[0] = jnp.concatenate(maps, axis=0).T.astype(gm_ref.dtype)

    @pl.when(step == pl.num_programs(0) - 1)
    def _():
        pair = jnp.concatenate([nn(turned(logs[...]), weights[...]), total[...].T], axis=1)
        out[...] = pair.astype(out.dtype).reshape(out.shape)


def total_kernel(table, *refs):
    out = refs[-1]
    heads, hd = out.shape[0], out.shape[2]
    for h in range(heads):
        out[h, :hd, :] = sum(ref[h, :hd, :].astype(F32) for ref in refs[:-1]).astype(BF16)
        out[h, hd:, :] = thirds(sum(whole_row(ref[h, hd:, :]) for ref in refs[:-1]))


def spread_kernel(grp, others, closing, block_weight, total_weight, at, table, *refs):
    parts, totals, refs = refs[:grp], refs[grp : grp + others], refs[grp + others :]
    if closing:
        outs, grad, scratch = refs[:grp], refs[grp], refs[grp + 1]
    else:
        state_ref, norm_ref, outs = refs[0], refs[1], refs[2:]
    heads, hd = parts[0].shape[0], parts[0].shape[2]
    for h in range(heads):
        states = [ref[h, :hd, :].astype(F32) for ref in parts]
        norms = [whole_row(ref[h, hd:, :]) for ref in parts]
        others_state = [ref[h, :hd, :].astype(F32) for ref in totals]
        others_norm = [whole_row(ref[h, hd:, :]) for ref in totals]
        if closing:
            base, base_norm = jnp.zeros_like(states[0]), jnp.zeros_like(norms[0])
            scratch[...] = sum(states) + sum(others_state)
            rows = grad.shape[1]
            grad[h] = scratch[pl.ds(pl.multiple_of(table[at] * rows, rows), rows), :]
        else:
            base, base_norm = state_ref[h], norm_ref[pl.ds(h, 1), :]
        for i, (state, norm) in enumerate(zip(others_state, others_norm)):
            base = base + table[total_weight + i].astype(F32) * state
            base_norm = base_norm + table[total_weight + i].astype(F32) * norm
        for r, out in enumerate(outs):
            state, norm = base, base_norm
            for i in range(grp):
                if i != r:
                    state = state + table[block_weight + r * grp + i].astype(F32) * states[i]
                    norm = norm + table[block_weight + r * grp + i].astype(F32) * norms[i]
            out[h, :hd, :] = state.astype(BF16)
            out[h, hd:, :] = thirds(norm)


def close_kernel(pairs, singles, at, table, q_ref, k_ref, *refs):
    both, q_parts, k_parts = (
        refs[:pairs],
        refs[pairs : pairs + singles],
        refs[pairs + singles : pairs + 2 * singles],
    )
    for i, (own, parts, out) in enumerate(
        ((q_ref, q_parts, refs[-2]), (k_ref, k_parts, refs[-1]))
    ):
        rows, half = out.shape[1:]
        mine = pl.ds(pl.multiple_of(table[at] * rows, rows), rows)
        for h in range(own.shape[0]):
            total = own[h, mine, :].astype(F32)
            for ref in both:
                total = total + ref[i, h].astype(F32)
            for ref in parts:
                total = total + ref[h].astype(F32)
            for u in range(PAIR):
                out[h * PAIR + u] = total[:, u * half : (u + 1) * half]


def whole_call(kernel, outs, table, arrays, name, scratch=()):
    return pl.pallas_call(
        kernel,
        out_shape=outs,
        in_specs=[pl.BlockSpec(memory_space=SMEM)]
        + [pl.BlockSpec(memory_space=pltpu.VMEM)] * len(arrays),
        out_specs=[pl.BlockSpec(memory_space=pltpu.VMEM)] * len(outs),
        scratch_shapes=list(scratch),
        compiler_params=pltpu.CompilerParams(vmem_limit_bytes=LIMIT),
        cost_estimate=LITTLE,
        name=name,
    )(table, *arrays)


def after(value, *others):
    return lax.optimization_barrier((value, *others))[0]


def shards(
    query_rows, key_rows, value_rows, grad_out, query_map, key_map, prefix_state, prefix_norm
):
    ctx, fsdp = lax.axis_size("ctx"), lax.axis_size("fsdp")
    tok = query_rows.shape[0]
    heads, map_rows, half = query_map.shape
    hd = map_rows * fsdp
    kv_heads = key_rows.shape[1] // hd
    replicas = ctx // kv_heads
    part = BLK // tok
    grp = ctx // part
    mine = lax.axis_index("ctx")
    at, block, seq = mine % part, mine // part, lax.axis_index("fsdp")
    shifts, slots = range(part), range(grp)
    order = list(reversed(slots))
    grid = (heads // PAIR,)
    blocks_of = [[g * part + p for p in range(part)] for g in slots]

    def within(array):
        return lax.all_to_all(array, "ctx", 0, 0, axis_index_groups=blocks_of, tiled=True)

    def around(array, shift):
        return lax.ppermute(
            array, "ctx", [(d, d // part * part + (d + shift) % part) for d in range(ctx)]
        )

    def across(array, shift):
        return lax.ppermute(array, "ctx", [(d, (d + shift * part) % ctx) for d in range(ctx)])

    def along(array, shift):
        return lax.ppermute(array, "fsdp", [(d, (d + shift) % fsdp) for d in range(fsdp)])

    def apart(array, s, r):
        moves = [
            (d * fsdp + i, (d + s * part) % ctx * fsdp + (i + r) % fsdp)
            for d in range(ctx)
            for i in range(fsdp)
        ]
        return lax.ppermute(array, ("ctx", "fsdp"), moves)

    slot = [(block + s) % grp for s in slots]
    near = [(block - r) % grp for r in slots]
    far = [(seq - r) % fsdp for r in range(1, fsdp)]
    lists = {
        "seq": [seq],
        "owner": [slot[s] * part + p for s in slots for p in range(part)],
        "sent": [slot[s] * part + (at + r) % part for s in slots for r in shifts],
        "kv": [
            (slot[s] * part + (at + r) % part) // replicas for r in shifts for s in slots
        ],
        "sorted": [(at - r) % part for r in shifts],
        "near before": [b < a for a in near for b in near],
        "near after": [b > a for a in near for b in near],
        "far before": [other < seq for other in far],
        "far after": [other > seq for other in far],
    }
    base, values = {}, []
    for name, entries in lists.items():
        base[name] = len(values)
        values += entries
    table = jnp.stack([jnp.asarray(v, jnp.int32) for v in values])

    own_maps = jnp.concatenate((query_map, key_map), axis=-1)
    maps = jnp.stack([own_maps] + [across(own_maps, -s) for s in slots[1:]])
    kv_sent = pack(table, base["kv"], (key_rows, value_rows), part, grp, hd)
    kv = [kv_sent[0]] + [around(kv_sent[r], r) for r in shifts[1:]]
    maps = lax.all_gather(maps, "fsdp")

    rows = {}
    for s in order:
        sent = pack(
            after(table, maps),
            base["sent"] + s * part,
            (query_rows, grad_out),
            part,
            1,
            heads * hd,
        )
        rows[s] = [sent[0]] + [around(sent[r], r) for r in shifts[1:]]

    params = pltpu.CompilerParams(
        dimension_semantics=("arbitrary",), vmem_limit_bytes=LIMIT
    )

    def piece_specs(column, count):
        return [pl.BlockSpec((tok, count * hd), lambda h, t: (0, column(h)))] * part

    def kv_specs(s):
        return piece_specs(lambda h: 2 * s, 1) + piece_specs(lambda h: 2 * s + 1, 1)

    def map_spec(s):
        return pl.BlockSpec((fsdp, None, PAIR, map_rows, 2 * half), lambda h, t: (0, s, h, 0, 0))

    def head_spec(*shape):
        return pl.BlockSpec((PAIR, *shape), lambda h, t: (h,) + (0,) * len(shape))

    def of(dtype, *shape):
        return jax.ShapeDtypeStruct(shape, dtype)

    ext_spec, ext_shape = head_spec(hd + EXT, hd), of(BF16, heads, hd + EXT, hd)
    gm_spec = pl.BlockSpec((1, hd, PAIR * half), lambda h, t: (h, 0, 0))
    gm_shape = of(BF16, heads // PAIR, hd, PAIR * half)
    dk_spec, dk_shape = head_spec(2 * half, BLK), of(F32, heads, 2 * half, BLK)
    dv_spec, dv_shape = pl.BlockSpec((hd, BLK), lambda h, t: (0, 0)), of(F32, hd, BLK)
    low, wide = pltpu.VMEM((BLK, hd), BF16), pltpu.VMEM((BLK, PAIR * hd), BF16)

    def call(kernel, outs, specs, out_specs, arrays, scratch, name, alias=()):
        return pl.pallas_call(
            functools.partial(kernel, part, base["sorted"]),
            out_shape=outs,
            grid_spec=pltpu.PrefetchScalarGridSpec(
                num_scalar_prefetch=1,
                grid=grid,
                in_specs=specs,
                out_specs=out_specs,
                scratch_shapes=scratch,
            ),
            compiler_params=params,
            cost_estimate=LITTLE,
            input_output_aliases=dict(alias),
            name=name,
        )(table, *arrays)

    def states_of(s):
        return call(
            state_kernel,
            [ext_shape],
            kv_specs(s) + [map_spec(s)],
            [ext_spec],
            [*kv, *kv, maps],
            [low, low],
            "states",
        )[0]

    def spread(parts, total, when, extra, closing):
        others = [along(total, r) for r in range(1, fsdp)]
        weights = [base["near " + when], base["far " + when], base["seq"]]
        result = whole_call(
            functools.partial(spread_kernel, grp, fsdp - 1, closing, *weights),
            [ext_shape] * grp + [of(F32, heads, map_rows, hd)] * closing,
            table,
            parts + others + extra,
            "spread",
            [pltpu.VMEM((hd, hd), F32)] * closing,
        )
        return [result[0]] + [across(result[s], -s) for s in slots[1:]], result[grp:]

    def totals_of(parts):
        return whole_call(total_kernel, [ext_shape], table, parts, "totals")[0]

    partial = {s: states_of(s) for s in order}
    parts = [after(partial[0], *rows[order[0]])] + [across(partial[s], s) for s in slots[1:]]
    state, _ = spread(parts, totals_of(parts), "before", [prefix_state, prefix_norm], False)

    def block_of(s):
        return call(
            block_kernel,
            [of(BF16, part, tok, heads * hd), dk_shape, dv_shape, ext_shape, gm_shape],
            kv_specs(s)
            + piece_specs(lambda h: h, PAIR)
            + piece_specs(lambda h: grid[0] + h, PAIR)
            + [map_spec(s), ext_spec],
            [
                pl.BlockSpec((part, tok, PAIR * hd), lambda h, t: (0, 0, h)),
                dk_spec,
                dv_spec,
                ext_spec,
                gm_spec,
            ],
            [*kv, *kv, *rows[s], *rows[s], maps, state[s]],
            [low, low, pltpu.VMEM((hd, BLK), BF16), wide, wide],
            "blocks",
        )

    def rows_for(array, device):
        pieces = array.reshape(*array.shape[:-2], fsdp, map_rows, array.shape[-1])
        return lax.dynamic_index_in_dim(pieces, device % fsdp, array.ndim - 2, keepdims=False)

    blocks, parts, q_maps = {}, {}, []
    for s in order:
        blocks[s] = block_of(s)
        parts[s] = across(blocks[s][3], s) if s else blocks[s][3]
        if s:
            q_maps += [apart(rows_for(blocks[s][4], seq + r), s, r) for r in range(fsdp)]
    parts = [after(parts[0], *q_maps)] + [parts[s] for s in slots[1:]]
    total = totals_of(parts)
    suffix, (grad_prefix,) = spread(parts, total, "after", [], True)
    returned = {s: within(after(blocks[s][0], total if s else suffix[0])) for s in order}

    kv_type = BF16 if replicas == 1 else F32
    pairs = jnp.zeros((part, tok, grp * 2 * hd), kv_type)
    k_maps, both_maps, key_gm = [], [], {}
    for s in slots:
        pairs, key_gm[s] = call(
            key_kernel,
            [of(kv_type, *pairs.shape), gm_shape],
            kv_specs(s)
            + [map_spec(s), ext_spec, dk_spec, dv_spec, pl.BlockSpec(memory_space=pl.ANY)],
            [pl.BlockSpec((part, tok, 2 * hd), lambda h, t: (0, 0, s)), gm_spec],
            [*kv, *kv, maps, suffix[s], blocks[s][1], blocks[s][2], pairs],
            [
                low,
                low,
                pltpu.VMEM((hd, BLK), BF16),
                pltpu.VMEM((hd, BLK), F32),
                pltpu.VMEM((heads * half, BLK), BF16),
                pltpu.VMEM((heads * half, hd), BF16),
            ],
            "keys",
            {2 * part + 5: 0},
        )
        if s == 0:
            two = after(jnp.stack([blocks[s][4], key_gm[s]]), *suffix[1:])
            both_maps = [along(rows_for(two, seq + r), r) for r in range(1, fsdp)]
        else:
            k_maps += [apart(rows_for(key_gm[s], seq + r), s, r) for r in range(fsdp)]

    pairs = within(after(pairs, *returned.values()))
    (grad_queries,) = unpack(table, base["owner"], [returned[s] for s in slots], 1, heads * hd)
    pairs = [pairs[:, :, s * 2 * hd : (s + 1) * 2 * hd] for s in slots]
    grad_keys, grad_values = unpack(table, base["owner"], pairs, 2, hd)
    if replicas > 1:
        grad_keys, grad_values = (
            jnp.sum(a.reshape(tok, kv_heads, replicas, hd), axis=2)
            .astype(BF16)
            .reshape(tok, kv_heads * hd)
            for a in (grad_keys, grad_values)
        )
    query_map_grad, key_map_grad = whole_call(
        functools.partial(close_kernel, len(both_maps), len(q_maps), base["seq"]),
        [of(F32, heads, map_rows, half)] * 2,
        table,
        [blocks[0][4], key_gm[0]] + both_maps + q_maps + k_maps,
        "close",
    )
    return grad_queries, grad_keys, grad_values, query_map_grad, key_map_grad, grad_prefix


def solution(mesh):
    rows, maps = P(("fsdp", "ctx"), None), P("ctx", "fsdp", None)
    return jax.shard_map(
        shards,
        mesh=mesh,
        in_specs=(rows,) * 4 + (maps, maps, P("ctx", None, None), P("ctx", None)),
        out_specs=(rows,) * 3 + (maps,) * 3,
        check_vma=False,
    )
```

time: 279 us -> 230 us (0.82)
  blocking collectives: 42.7 us -> 9.12 us
  waiting for transfers between devices: 105 us -> 83.2 us
  starting transfers between devices: 43.1 us -> 54.7 us
  local copies, waits for them, and re-layouts: 27.1 us -> 17.1 us
  Pallas kernels: 54.3 us -> 61.4 us
    ppermute x0 -> x17, waiting for transfers between devices: none -> 28.7 us  [the longest x9 25.1 us: around(): lax.ppermute(array, 'ctx', [(d, d // part * part + (d + shift) % part) fo...]
    ppermute x0 -> x17, starting transfers between devices: none -> 28.2 us  [the longest x8 15.3 us: apart(): return lax.ppermute(array, ('ctx', 'fsdp'), moves)]
    all_to_all x6 -> x3, waiting for transfers between devices: 27.5 us -> 0.01 us  [within(): lax.all_to_all(array, 'ctx', 0, 0, axis_index_groups=blocks_of, tiled=True)]
    all_gather x1, blocking collectives: 34.6 us -> 9.12 us  [shards(): maps = lax.all_gather(maps, 'fsdp')]
    ppermute x6 -> x5, waiting for transfers between devices: 42.1 us -> 27.3 us  [across(): lax.ppermute(array, 'ctx', [(d, (d + shift * part) % ctx) for d in range(...]
    unnamed x74 -> x64, local copies, waits for them, and re-layouts: 26.9 us -> 14.2 us
    all_to_all x6 -> x3, starting transfers between devices: 23.2 us -> 14.4 us  [within(): lax.all_to_all(array, 'ctx', 0, 0, axis_index_groups=blocks_of, tiled=True)]
    all_to_all x1 -> x0, blocking collectives: 8.14 us -> none  [within(): lax.all_to_all(array, 'ctx', 0, 0, axis_index_groups=blocks_of, tiled=True)]
  transfers between devices with their start and end apart: 24 -> 34, of which waited for: 19 -> 14; matrix products, arithmetic and copies ran while one was open for 1% -> 1% of each run, Pallas kernels for 17% -> 25%
where the time goes in v7:
time: 230 us; the launch traced here: 228 us
  waiting for transfers between devices  83.2 us (36%)
  Pallas kernels  61.4 us (27%)
  starting transfers between devices  54.7 us (24%)
  local copies, waits for them, and re-layouts  17.1 us (7%)
  blocking collectives  9.12 us (4%)
    pallas_call x6, Pallas kernels, call(): pl.pallas_call(functools.partial(kernel, part, base['sorted']), out_shape...  48.3 us
    ppermute x5, waiting for transfers between devices, across(): lax.ppermute(array, 'ctx', [(d, (d + shift * part) % ctx) for d in range(...  27.3 us
    ppermute x9, waiting for transfers between devices, along(): lax.ppermute(array, 'fsdp', [(d, (d + shift) % fsdp) for d in range(fsdp)])  27.2 us
    ppermute x9, waiting for transfers between devices, around(): lax.ppermute(array, 'ctx', [(d, d // part * part + (d + shift) % part) fo...  25.1 us
    ppermute x8, starting transfers between devices, apart(): return lax.ppermute(array, ('ctx', 'fsdp'), moves)  15.3 us
    all_to_all x3, starting transfers between devices, within(): lax.all_to_all(array, 'ctx', 0, 0, axis_index_groups=blocks_of, tiled=True)  14.4 us
    unnamed x64, local copies, waits for them, and re-layouts  14.2 us
    ppermute x9, starting transfers between devices, around(): lax.ppermute(array, 'ctx', [(d, d // part * part + (d + shift) % part) fo...  12.8 us
  transfers between devices with their start and end apart: 34, of which 14 were waited for; matrix products, arithmetic and copies ran while one was open for 1% of the time, Pallas kernels for 25%

profile of v7, /device:TPU:1, one launch (start us, length us, event | category | flops | bytes accessed | tf_op | source)
XLA Modules:
  0.0 228.0 jit_solution(9093564296763018393)
XLA Ops:
  10.9 9.1 %all-gather = bf16[8,8,32,128]{3,2,1,0:T(8,128)(2,1)S(1)} all-gather(bf16[2,8,32,128]{3,2,1,0:T(8,128)(2,1)S(1)} %pad_maximum_fusion.1), channel_id=2, replica_groups=mesh['ctx'=8,'fsdp'=4] {'fsdp'}, dimensions={0}, use_global_device_ids=true | all-gather | bytes 655360 | tf_op jit(solution)/shard_map/all_gather | solution.py:422
  26.7 23.1 %collective-permute-done.1.refs_2_.refs_6_ = bf16[128,512]{1,0:T(8,128)(2,1)S(1)} collective-permute-done((bf16[128,512]{1,0:T(8,128)(2,1)S(1)}, bf16[128,512]{1,0:T(8,128)(2,1)S(1)}, u32[]{:S(2)}, u32[]{:S(2)}) %collective-permute-start.1) | collective-permute-done | bytes 131104 | tf_op jit(solution)/shard_map/ppermute | solution.py:378
  51.8 3.5 %states.3 = bf16[8,144,128]{2,1,0:T(8,128)(2,1)S(1)} custom-call(s32[43]{0:T(128)S(1)} %stack.193.table, bf16[128,512]{1,0:T(8,128)(2,1)S(1)} %get-tuple-element.48.refs_0_.refs_4_, bf16[128,512]{1,0:T(8,128)(2,1)S(1)} %collective-permute-done.refs_1_.refs_5_, bf16[128,512]{1,0:T(8,128)(2,1)S(1)} %collective-permute-done.1.refs_2_.refs_6_, ...), custom_call_target="tpu_custom_call" | custom-call | flops 1000 | bytes 1000 | tf_op jit(solution)/shard_map/states/pallas_call | solution.py:463
  57.0 3.5 %states.2.refs_0_ = bf16[8,144,128]{2,1,0:T(8,128)(2,1)S(1)} custom-call(s32[43]{0:T(128)S(1)} %stack.193.table, bf16[128,512]{1,0:T(8,128)(2,1)S(1)} %get-tuple-element.48.refs_0_.refs_4_, bf16[128,512]{1,0:T(8,128)(2,1)S(1)} %collective-permute-done.refs_1_.refs_5_, bf16[128,512]{1,0:T(8,128)(2,1)S(1)} %collective-permute-done.1.refs_2_.refs_6_, ...), custom_call_target="tpu_custom_call" | custom-call | flops 1000 | bytes 1000 | tf_op jit(solution)/shard_map/states/pallas_call | solution.py:463
  60.6 10.7 %collective-permute-done.10.refs_1_ = bf16[8,144,128]{2,1,0:T(8,128)(2,1)S(1)} collective-permute-done((bf16[8,144,128]{2,1,0:T(8,128)(2,1)S(1)}, bf16[8,144,128]{2,1,0:T(8,128)(2,1)S(1)}, u32[]{:S(2)}, u32[]{:S(2)}) %collective-permute-start.10) | collective-permute-done | bytes 294944 | tf_op jit(solution)/shard_map/ppermute | solution.py:383
  73.9 5.3 %collective-permute-done.11.refs_2_ = bf16[8,144,128]{2,1,0:T(8,128)(2,1)S(1)} collective-permute-done((bf16[8,144,128]{2,1,0:T(8,128)(2,1)S(1)}, bf16[8,144,128]{2,1,0:T(8,128)(2,1)S(1)}, u32[]{:S(2)}, u32[]{:S(2)}) %collective-permute-start.11) | collective-permute-done | bytes 294944 | tf_op jit(solution)/shard_map/ppermute | solution.py:386
  79.2 7.7 %collective-permute-done.12.refs_3_ = bf16[8,144,128]{2,1,0:T(8,128)(2,1)S(1)} collective-permute-done((bf16[8,144,128]{2,1,0:T(8,128)(2,1)S(1)}, bf16[8,144,128]{2,1,0:T(8,128)(2,1)S(1)}, u32[]{:S(2)}, u32[]{:S(2)}) %collective-permute-start.12) | collective-permute-done | bytes 294944 | tf_op jit(solution)/shard_map/ppermute | solution.py:386
  92.7 2.8 %collective-permute-start.5 = (bf16[128,2048]{1,0:T(8,128)(2,1)}, bf16[128,2048]{1,0:T(8,128)(2,1)S(1)}, u32[]{:S(2)}, u32[]{:S(2)}) collective-permute-start(bf16[128,2048]{1,0:T(8,128)(2,1)} %get-tuple-element.55), channel_id=1, source_target_pairs={{0,8},{4,12},{8,0},{12,4},{16,24},{20,28},{24,16},{28,20},{1,9},{5... | collective-permute-start | bytes 1572872 | tf_op jit(solution)/shard_map/ppermute | solution.py:378
  95.6 8.0 %collective-permute-done.14.refs_17_ = bf16[8,144,128]{2,1,0:T(8,128)(2,1)S(1)} collective-permute-done((bf16[8,144,128]{2,1,0:T(8,128)(2,1)S(1)}, bf16[8,144,128]{2,1,0:T(8,128)(2,1)S(1)}, u32[]{:S(2)}, u32[]{:S(2)}) %collective-permute-start.14) | collective-permute-done | bytes 294944 | tf_op jit(solution)/shard_map/ppermute | solution.py:383
  103.5 15.5 %blocks.3 = (bf16[4,128,1024]{2,1,0:T(8,128)(2,1)S(1)}, f32[8,128,512]{2,1,0:T(8,128)S(1)}, f32[128,512]{1,0:T(8,128)S(1)}, bf16[8,144,128]{2,1,0:T(8,128)(2,1)}, bf16[4,128,128]{2,1,0:T(8,128)(2,1)S(1)}) custom-call(s32[43]{0:T(128)S(1)} %stack.193.table, bf16[128,512]{1,0:T(8,128)(2,1)S(1)} %get-tuple-element.48.refs_0_.refs_4_, ...), custom_call_target="tpu_custom_call" | custom-call | flops 1000 | bytes 1000 | tf_op jit(solution)/shard_map/blocks/pallas_call | solution.py:463
  123.5 2.4 %collective-permute-start.15 = (bf16[4,32,128]{2,1,0:T(8,128)(2,1)S(1)}, bf16[4,32,128]{2,1,0:T(8,128)(2,1)S(1)}, u32[]{:S(2)}, u32[]{:S(2)}) collective-permute-start(bf16[4,32,128]{2,1,0:T(8,128)(2,1)S(1)} %get-tuple-element.102), channel_id=1, source_target_pairs={{0,16},{1,17},{2,18},{3,19},{4,20},{5,21},{6,22},{7,23},{8,24},{9,... | collective-permute-start | bytes 98312 | tf_op jit(solution)/shard_map/ppermute | solution.py:394
  127.2 2.8 %collective-permute-start.17 = (bf16[4,32,128]{2,1,0:T(8,128)(2,1)S(1)}, bf16[4,32,128]{2,1,0:T(8,128)(2,1)S(1)}, u32[]{:S(2)}, u32[]{:S(2)}) collective-permute-start(bf16[4,32,128]{2,1,0:T(8,128)(2,1)S(1)} %get-tuple-element.100), channel_id=1, source_target_pairs={{0,18},{1,19},{2,16},{3,17},{4,22},{5,23},{6,20},{7,21},{8,26},{9,... | collective-permute-start | bytes 98312 | tf_op jit(solution)/shard_map/ppermute | solution.py:394
  131.1 14.9 %blocks.2 = (bf16[4,128,1024]{2,1,0:T(8,128)(2,1)S(1)}, f32[8,128,512]{2,1,0:T(8,128)S(1)}, f32[128,512]{1,0:T(8,128)S(1)}, bf16[8,144,128]{2,1,0:T(8,128)(2,1)S(1)}, bf16[4,128,128]{2,1,0:T(8,128)(2,1)S(1)}) custom-call(s32[43]{0:T(128)S(1)} %stack.193.table, bf16[128,512]{1,0:T(8,128)(2,1)S(1)} %get-tuple-element.48.refs_0_.refs_4_, ...), custom_call_target="tpu_custom_call" | custom-call | flops 1000 | bytes 1000 | tf_op jit(solution)/shard_map/blocks/pallas_call | solution.py:463
  149.8 4.2 %all-to-all-start.1 = ((bf16[4,128,1024]{2,1,0:T(8,128)(2,1)}), bf16[4,128,1024]{2,1,0:T(8,128)(2,1)S(1)}, u32[]{:S(2)}, u32[]{:S(2)}) async-start(bf16[4,128,1024]{2,1,0:T(8,128)(2,1)} %copy-done.10), calls=%async_computation.1 | async-start | bytes 2097152 | tf_op jit(solution)/shard_map/all_to_all | solution.py:375
  157.3 5.3 %collective-permute-done.20.refs_2_ = bf16[8,144,128]{2,1,0:T(8,128)(2,1)S(1)} collective-permute-done((bf16[8,144,128]{2,1,0:T(8,128)(2,1)S(1)}, bf16[8,144,128]{2,1,0:T(8,128)(2,1)S(1)}, u32[]{:S(2)}, u32[]{:S(2)}) %collective-permute-start.20) | collective-permute-done | bytes 294944 | tf_op jit(solution)/shard_map/ppermute | solution.py:386
  162.6 7.7 %collective-permute-done.21.refs_3_ = bf16[8,144,128]{2,1,0:T(8,128)(2,1)S(1)} collective-permute-done((bf16[8,144,128]{2,1,0:T(8,128)(2,1)S(1)}, bf16[8,144,128]{2,1,0:T(8,128)(2,1)S(1)}, u32[]{:S(2)}, u32[]{:S(2)}) %collective-permute-start.21) | collective-permute-done | bytes 294944 | tf_op jit(solution)/shard_map/ppermute | solution.py:386
  174.0 4.0 %all-to-all-start = ((bf16[4,128,1024]{2,1,0:T(8,128)(2,1)}), bf16[4,128,1024]{2,1,0:T(8,128)(2,1)S(1)}, u32[]{:S(2)}, u32[]{:S(2)}) async-start(bf16[4,128,1024]{2,1,0:T(8,128)(2,1)} %copy-done.11), calls=%async_computation | async-start | bytes 2097152 | tf_op jit(solution)/shard_map/all_to_all | solution.py:375
  183.1 5.4 %keys.2 = (bf16[4,128,512]{2,1,0:T(8,128)(2,1)}, bf16[4,128,128]{2,1,0:T(8,128)(2,1)S(1)}) custom-call(s32[43]{0:T(128)S(1)} %stack.193.table, bf16[128,512]{1,0:T(8,128)(2,1)S(1)} %get-tuple-element.48.refs_0_.refs_4_, bf16[128,512]{1,0:T(8,128)(2,1)S(1)} %collective-permute-done.refs_1_.refs_5_, ...), custom_call_target="tpu_custom_call", output_to_operand_aliasing={{0}: (13, {})} | custom-call | flops 1000 | bytes 1000 | tf_op jit(solution)/shard_map/keys/pallas_call | solution.py:463
  189.2 6.7 %collective-permute-done.23.refs_9_ = bf16[8,144,128]{2,1,0:T(8,128)(2,1)S(1)} collective-permute-done((bf16[8,144,128]{2,1,0:T(8,128)(2,1)}, bf16[8,144,128]{2,1,0:T(8,128)(2,1)S(1)}, u32[]{:S(2)}, u32[]{:S(2)}) %collective-permute-start.23) | collective-permute-done | bytes 294944 | tf_op jit(solution)/shard_map/ppermute | solution.py:383
  195.9 5.5 %keys.3 = (bf16[4,128,512]{2,1,0:T(8,128)(2,1)}, bf16[4,128,128]{2,1,0:T(8,128)(2,1)S(1)}) custom-call(s32[43]{0:T(128)S(1)} %stack.193.table, bf16[128,512]{1,0:T(8,128)(2,1)S(1)} %get-tuple-element.48.refs_0_.refs_4_, bf16[128,512]{1,0:T(8,128)(2,1)S(1)} %collective-permute-done.refs_1_.refs_5_, ...), custom_call_target="tpu_custom_call", output_to_operand_aliasing={{0}: (13, {})} | custom-call | flops 1000 | bytes 1000 | tf_op jit(solution)/shard_map/keys/pallas_call | solution.py:463
  201.4 6.1 %all-to-all-start.2 = ((bf16[4,128,512]{2,1,0:T(8,128)(2,1)}), bf16[4,128,512]{2,1,0:T(8,128)(2,1)}, u32[]{:S(2)}, u32[]{:S(2)}) async-start(bf16[4,128,512]{2,1,0:T(8,128)(2,1)} %get-tuple-element.80), calls=%async_computation.2 | async-start | bytes 1048576 | tf_op jit(solution)/shard_map/all_to_all | solution.py:375
  209.5 3.1 %collective-permute-start.28 = (bf16[4,32,128]{2,1,0:T(8,128)(2,1)S(1)}, bf16[4,32,128]{2,1,0:T(8,128)(2,1)S(1)}, u32[]{:S(2)}, u32[]{:S(2)}) collective-permute-start(bf16[4,32,128]{2,1,0:T(8,128)(2,1)S(1)} %get-tuple-element.97), channel_id=1, source_target_pairs={{0,17},{1,18},{2,19},{3,16},{4,21},{5,22},{6,23},{7,20},{8,25},{9,... | collective-permute-start | bytes 98312 | tf_op jit(solution)/shard_map/ppermute | solution.py:394
  213.8 3.0 %collective-permute-start.29 = (bf16[4,32,128]{2,1,0:T(8,128)(2,1)S(1)}, bf16[4,32,128]{2,1,0:T(8,128)(2,1)S(1)}, u32[]{:S(2)}, u32[]{:S(2)}) collective-permute-start(bf16[4,32,128]{2,1,0:T(8,128)(2,1)S(1)} %get-tuple-element.96), channel_id=1, source_target_pairs={{0,18},{1,19},{2,16},{3,17},{4,22},{5,23},{6,20},{7,21},{8,26},{9,... | collective-permute-start | bytes 98312 | tf_op jit(solution)/shard_map/ppermute | solution.py:394
  219.0 3.0 %collective-permute-done.30.refs_10_ = bf16[4,32,128]{2,1,0:T(8,128)(2,1)S(1)} collective-permute-done((bf16[4,32,128]{2,1,0:T(8,128)(2,1)S(1)}, bf16[4,32,128]{2,1,0:T(8,128)(2,1)S(1)}, u32[]{:S(2)}, u32[]{:S(2)}) %collective-permute-start.30) | collective-permute-done | bytes 32800 | tf_op jit(solution)/shard_map/ppermute | solution.py:394
  (136 shorter events, 63.3 us)
Async XLA Ops:
  4.2 21.1 %collective-permute-start = (bf16[128,512]{1,0:T(8,128)(2,1)S(1)}, bf16[128,512]{1,0:T(8,128)(2,1)S(1)}, u32[]{:S(2)}, u32[]{:S(2)}) collective-permute-start(bf16[128,512]{1,0:T(8,128)(2,1)S(1)} %get-tuple-element.49), channel_id=1, source_target_pairs={{0,4},{4,8},{8,12},{12,0},{16,20},{20,24},{24,28},{28,16},{1,5},{5... | collective-permute-start | bytes 393224 | tf_op jit(solution)/shard_map/ppermute | solution.py:378
  21.0 39.5 %collective-permute-start.7 = (bf16[128,2048]{1,0:T(8,128)(2,1)S(1)}, bf16[128,2048]{1,0:T(8,128)(2,1)S(1)}, u32[]{:S(2)}, u32[]{:S(2)}) collective-permute-start(bf16[128,2048]{1,0:T(8,128)(2,1)S(1)} %get-tuple-element.58), channel_id=1, source_target_pairs={{0,4},{4,8},{8,12},{12,0},{16,20},{20,24},{24,28},{28,16},{1,5},{5... | collective-permute-start | bytes 1572872 | tf_op jit(solution)/shard_map/ppermute | solution.py:378
  22.7 37.9 %collective-permute-start.8 = (bf16[128,2048]{1,0:T(8,128)(2,1)S(1)}, bf16[128,2048]{1,0:T(8,128)(2,1)S(1)}, u32[]{:S(2)}, u32[]{:S(2)}) collective-permute-start(bf16[128,2048]{1,0:T(8,128)(2,1)S(1)} %get-tuple-element.59), channel_id=1, source_target_pairs={{0,8},{4,12},{8,0},{12,4},{16,24},{20,28},{24,16},{28,20},{1,9},{5... | collective-permute-start | bytes 1572872 | tf_op jit(solution)/shard_map/ppermute | solution.py:378
  24.1 36.5 %collective-permute-start.9 = (bf16[128,2048]{1,0:T(8,128)(2,1)S(1)}, bf16[128,2048]{1,0:T(8,128)(2,1)S(1)}, u32[]{:S(2)}, u32[]{:S(2)}) collective-permute-start(bf16[128,2048]{1,0:T(8,128)(2,1)S(1)} %get-tuple-element.60), channel_id=1, source_target_pairs={{0,12},{4,0},{8,4},{12,8},{16,28},{20,16},{24,20},{28,24},{1,13},{... | collective-permute-start | bytes 1572872 | tf_op jit(solution)/shard_map/ppermute | solution.py:378
  24.5 25.3 %collective-permute-start.1 = (bf16[128,512]{1,0:T(8,128)(2,1)S(1)}, bf16[128,512]{1,0:T(8,128)(2,1)S(1)}, u32[]{:S(2)}, u32[]{:S(2)}) collective-permute-start(bf16[128,512]{1,0:T(8,128)(2,1)S(1)} %get-tuple-element.50), channel_id=1, source_target_pairs={{0,8},{4,12},{8,0},{12,4},{16,24},{20,28},{24,16},{28,20},{1,9},{5... | collective-permute-start | bytes 393224 | tf_op jit(solution)/shard_map/ppermute | solution.py:378
  25.3 26.4 %collective-permute-start.2 = (bf16[128,512]{1,0:T(8,128)(2,1)S(1)}, bf16[128,512]{1,0:T(8,128)(2,1)S(1)}, u32[]{:S(2)}, u32[]{:S(2)}) collective-permute-start(bf16[128,512]{1,0:T(8,128)(2,1)S(1)} %get-tuple-element.51), channel_id=1, source_target_pairs={{0,12},{4,0},{8,4},{12,8},{16,28},{20,16},{24,20},{28,24},{1,13},{... | collective-permute-start | bytes 393224 | tf_op jit(solution)/shard_map/ppermute | solution.py:378
  55.3 16.0 %collective-permute-start.10 = (bf16[8,144,128]{2,1,0:T(8,128)(2,1)S(1)}, bf16[8,144,128]{2,1,0:T(8,128)(2,1)S(1)}, u32[]{:S(2)}, u32[]{:S(2)}) collective-permute-start(bf16[8,144,128]{2,1,0:T(8,128)(2,1)S(1)} %states.3), channel_id=1, source_target_pairs={{0,16},{4,20},{8,24},{12,28},{16,0},{20,4},{24,8},{28,12},{1,17},{... | collective-permute-start | bytes 884744 | tf_op jit(solution)/shard_map/ppermute | solution.py:383
  73.0 13.9 %collective-permute-start.12 = (bf16[8,144,128]{2,1,0:T(8,128)(2,1)S(1)}, bf16[8,144,128]{2,1,0:T(8,128)(2,1)S(1)}, u32[]{:S(2)}, u32[]{:S(2)}) collective-permute-start(bf16[8,144,128]{2,1,0:T(8,128)(2,1)S(1)} %totals.2), channel_id=1, source_target_pairs={{0,2},{1,3},{2,0},{3,1},{4,6},{5,7},{6,4},{7,5},{8,10},{9,11},{10,... | collective-permute-start | bytes 884744 | tf_op jit(solution)/shard_map/ppermute | solution.py:386
  73.9 13.6 %collective-permute-start.13 = (bf16[8,144,128]{2,1,0:T(8,128)(2,1)S(1)}, bf16[8,144,128]{2,1,0:T(8,128)(2,1)S(1)}, u32[]{:S(2)}, u32[]{:S(2)}) collective-permute-start(bf16[8,144,128]{2,1,0:T(8,128)(2,1)S(1)} %totals.2), channel_id=1, source_target_pairs={{0,3},{1,0},{2,1},{3,2},{4,7},{5,4},{6,5},{7,6},{8,11},{9,8},{10,9... | collective-permute-start | bytes 884744 | tf_op jit(solution)/shard_map/ppermute | solution.py:386
  88.4 15.1 %collective-permute-start.14 = (bf16[8,144,128]{2,1,0:T(8,128)(2,1)S(1)}, bf16[8,144,128]{2,1,0:T(8,128)(2,1)S(1)}, u32[]{:S(2)}, u32[]{:S(2)}) collective-permute-start(bf16[8,144,128]{2,1,0:T(8,128)(2,1)S(1)} %get-tuple-element.65), channel_id=1, source_target_pairs={{0,16},{4,20},{8,24},{12,28},{16,0},{20,4},{24,8},{28,12},{1,17},{... | collective-permute-start | bytes 884744 | tf_op jit(solution)/shard_map/ppermute | solution.py:383
  90.5 35.4 %collective-permute-start.4 = (bf16[128,2048]{1,0:T(8,128)(2,1)}, bf16[128,2048]{1,0:T(8,128)(2,1)S(1)}, u32[]{:S(2)}, u32[]{:S(2)}) collective-permute-start(bf16[128,2048]{1,0:T(8,128)(2,1)} %get-tuple-element.54), channel_id=1, source_target_pairs={{0,4},{4,8},{8,12},{12,0},{16,20},{20,24},{24,28},{28,16},{1,5},{5... | collective-permute-start | bytes 1572872 | tf_op jit(solution)/shard_map/ppermute | solution.py:378
  92.7 34.5 %collective-permute-start.5 = (bf16[128,2048]{1,0:T(8,128)(2,1)}, bf16[128,2048]{1,0:T(8,128)(2,1)S(1)}, u32[]{:S(2)}, u32[]{:S(2)}) collective-permute-start(bf16[128,2048]{1,0:T(8,128)(2,1)} %get-tuple-element.55), channel_id=1, source_target_pairs={{0,8},{4,12},{8,0},{12,4},{16,24},{20,28},{24,16},{28,20},{1,9},{5... | collective-permute-start | bytes 1572872 | tf_op jit(solution)/shard_map/ppermute | solution.py:378
  95.6 34.5 %collective-permute-start.6 = (bf16[128,2048]{1,0:T(8,128)(2,1)}, bf16[128,2048]{1,0:T(8,128)(2,1)S(1)}, u32[]{:S(2)}, u32[]{:S(2)}) collective-permute-start(bf16[128,2048]{1,0:T(8,128)(2,1)} %get-tuple-element.56), channel_id=1, source_target_pairs={{0,12},{4,0},{8,4},{12,8},{16,28},{20,16},{24,20},{28,24},{1,13},{... | collective-permute-start | bytes 1572872 | tf_op jit(solution)/shard_map/ppermute | solution.py:378
  122.6 25.7 %collective-permute-start.19 = (bf16[8,144,128]{2,1,0:T(8,128)(2,1)}, bf16[8,144,128]{2,1,0:T(8,128)(2,1)S(1)}, u32[]{:S(2)}, u32[]{:S(2)}) collective-permute-start(bf16[8,144,128]{2,1,0:T(8,128)(2,1)} %get-tuple-element.68), channel_id=1, source_target_pairs={{0,16},{4,20},{8,24},{12,28},{16,0},{20,4},{24,8},{28,12},{1,17},{... | collective-permute-start | bytes 884744 | tf_op jit(solution)/shard_map/ppermute | solution.py:383
  123.5 24.8 %collective-permute-start.15 = (bf16[4,32,128]{2,1,0:T(8,128)(2,1)S(1)}, bf16[4,32,128]{2,1,0:T(8,128)(2,1)S(1)}, u32[]{:S(2)}, u32[]{:S(2)}) collective-permute-start(bf16[4,32,128]{2,1,0:T(8,128)(2,1)S(1)} %get-tuple-element.102), channel_id=1, source_target_pairs={{0,16},{1,17},{2,18},{3,19},{4,20},{5,21},{6,22},{7,23},{8,24},{9,... | collective-permute-start | bytes 98312 | tf_op jit(solution)/shard_map/ppermute | solution.py:394
  125.9 22.4 %collective-permute-start.16 = (bf16[4,32,128]{2,1,0:T(8,128)(2,1)S(1)}, bf16[4,32,128]{2,1,0:T(8,128)(2,1)S(1)}, u32[]{:S(2)}, u32[]{:S(2)}) collective-permute-start(bf16[4,32,128]{2,1,0:T(8,128)(2,1)S(1)} %get-tuple-element.101), channel_id=1, source_target_pairs={{0,17},{1,18},{2,19},{3,16},{4,21},{5,22},{6,23},{7,20},{8,25},{9,... | collective-permute-start | bytes 98312 | tf_op jit(solution)/shard_map/ppermute | solution.py:394
  127.2 21.1 %collective-permute-start.17 = (bf16[4,32,128]{2,1,0:T(8,128)(2,1)S(1)}, bf16[4,32,128]{2,1,0:T(8,128)(2,1)S(1)}, u32[]{:S(2)}, u32[]{:S(2)}) collective-permute-start(bf16[4,32,128]{2,1,0:T(8,128)(2,1)S(1)} %get-tuple-element.100), channel_id=1, source_target_pairs={{0,18},{1,19},{2,16},{3,17},{4,22},{5,23},{6,20},{7,21},{8,26},{9,... | collective-permute-start | bytes 98312 | tf_op jit(solution)/shard_map/ppermute | solution.py:394
  130.0 18.3 %collective-permute-start.18 = (bf16[4,32,128]{2,1,0:T(8,128)(2,1)S(1)}, bf16[4,32,128]{2,1,0:T(8,128)(2,1)S(1)}, u32[]{:S(2)}, u32[]{:S(2)}) collective-permute-start(bf16[4,32,128]{2,1,0:T(8,128)(2,1)S(1)} %get-tuple-element.99), channel_id=1, source_target_pairs={{0,19},{1,16},{2,17},{3,18},{4,23},{5,20},{6,21},{7,22},{8,27},{9,... | collective-permute-start | bytes 98312 | tf_op jit(solution)/shard_map/ppermute | solution.py:394
  149.8 24.2 %all-to-all-start.1 = ((bf16[4,128,1024]{2,1,0:T(8,128)(2,1)}), bf16[4,128,1024]{2,1,0:T(8,128)(2,1)S(1)}, u32[]{:S(2)}, u32[]{:S(2)}) async-start(bf16[4,128,1024]{2,1,0:T(8,128)(2,1)} %copy-done.10), calls=%async_computation.1 | async-start | bytes 2097152 | tf_op jit(solution)/shard_map/all_to_all | solution.py:375
  156.3 14.0 %collective-permute-start.21 = (bf16[8,144,128]{2,1,0:T(8,128)(2,1)S(1)}, bf16[8,144,128]{2,1,0:T(8,128)(2,1)S(1)}, u32[]{:S(2)}, u32[]{:S(2)}) collective-permute-start(bf16[8,144,128]{2,1,0:T(8,128)(2,1)S(1)} %totals.3), channel_id=1, source_target_pairs={{0,2},{1,3},{2,0},{3,1},{4,6},{5,7},{6,4},{7,5},{8,10},{9,11},{10,... | collective-permute-start | bytes 884744 | tf_op jit(solution)/shard_map/ppermute | solution.py:386
  157.3 13.6 %collective-permute-start.22 = (bf16[8,144,128]{2,1,0:T(8,128)(2,1)S(1)}, bf16[8,144,128]{2,1,0:T(8,128)(2,1)S(1)}, u32[]{:S(2)}, u32[]{:S(2)}) collective-permute-start(bf16[8,144,128]{2,1,0:T(8,128)(2,1)S(1)} %totals.3), channel_id=1, source_target_pairs={{0,3},{1,0},{2,1},{3,2},{4,7},{5,4},{6,5},{7,6},{8,11},{9,8},{10,9... | collective-permute-start | bytes 884744 | tf_op jit(solution)/shard_map/ppermute | solution.py:386
  174.0 27.4 %all-to-all-start = ((bf16[4,128,1024]{2,1,0:T(8,128)(2,1)}), bf16[4,128,1024]{2,1,0:T(8,128)(2,1)S(1)}, u32[]{:S(2)}, u32[]{:S(2)}) async-start(bf16[4,128,1024]{2,1,0:T(8,128)(2,1)} %copy-done.11), calls=%async_computation | async-start | bytes 2097152 | tf_op jit(solution)/shard_map/all_to_all | solution.py:375
  178.1 17.9 %collective-permute-start.23 = (bf16[8,144,128]{2,1,0:T(8,128)(2,1)}, bf16[8,144,128]{2,1,0:T(8,128)(2,1)S(1)}, u32[]{:S(2)}, u32[]{:S(2)}) collective-permute-start(bf16[8,144,128]{2,1,0:T(8,128)(2,1)} %copy-done.29), channel_id=1, source_target_pairs={{0,16},{4,20},{8,24},{12,28},{16,0},{20,4},{24,8},{28,12},{1,17},{... | collective-permute-start | bytes 884744 | tf_op jit(solution)/shard_map/ppermute | solution.py:383
  201.4 24.0 %all-to-all-start.2 = ((bf16[4,128,512]{2,1,0:T(8,128)(2,1)}), bf16[4,128,512]{2,1,0:T(8,128)(2,1)}, u32[]{:S(2)}, u32[]{:S(2)}) async-start(bf16[4,128,512]{2,1,0:T(8,128)(2,1)} %get-tuple-element.80), calls=%async_computation.2 | async-start | bytes 1048576 | tf_op jit(solution)/shard_map/all_to_all | solution.py:375
  (42 other events, 321.0 us)

commit v8 on v7

--- a/solution.py
+++ b/solution.py
@@ -12,6 +12,7 @@
 PAIR = 2
 EXT = 16
 LIMIT = 40 * 1024 * 1024
+LARGE = 56 * 1024 * 1024
 
 LITTLE = pl.CostEstimate(flops=1000, bytes_accessed=1000, transcendentals=0)
 
@@ -117,27 +118,30 @@
     )(table, *(list(sources) * (pieces * columns)))
 
 
-def unpack_kernel(outputs, base, table, *refs):
+def unpack_kernel(outputs, inner, base, table, *refs):
     sources, outs = refs[:-outputs], refs[-outputs:]
     for s, source in enumerate(sources):
         pieces = source.shape[0]
-        width = source.shape[2] // outputs
+        width = source.shape[2] // (outputs * inner)
         for r in range(pieces):
-            at = pl.ds(pl.multiple_of(table[base + s * pieces + r] * width, width), width)
-            for i, out in enumerate(outs):
-                out[:, at] = source[r, :, i * width : (i + 1) * width]
-
-
-def unpack(table, base, sources, outputs, width):
+            for j in range(inner):
+                slot = s * inner + j
+                at = table[base + slot * pieces + r] * width
+                for i, out in enumerate(outs):
+                    lanes = slice((j * outputs + i) * width, (j * outputs + i + 1) * width)
+                    out[:, pl.ds(pl.multiple_of(at, width), width)] = source[r, :, lanes]
+
+
+def unpack(table, base, sources, inner, outputs, width):
     pieces, rows = sources[0].shape[:2]
-    total = len(sources) * pieces * width
+    total = len(sources) * inner * pieces * width
     step = rows // 2
+    taken = pl.BlockSpec((pieces, step, inner * outputs * width), lambda i: (0, i, 0))
     return pl.pallas_call(
-        functools.partial(unpack_kernel, outputs, base),
+        functools.partial(unpack_kernel, outputs, inner, base),
         out_shape=[jax.ShapeDtypeStruct((rows, total), sources[0].dtype)] * outputs,
         grid=(rows // step,),
-        in_specs=[pl.BlockSpec(memory_space=SMEM)]
-        + [pl.BlockSpec((pieces, step, outputs * width), lambda i: (0, i, 0))] * len(sources),
+        in_specs=[pl.BlockSpec(memory_space=SMEM)] + [taken] * len(sources),
         out_specs=[pl.BlockSpec((step, total), lambda i: (i, 0))] * outputs,
         compiler_params=pltpu.CompilerParams(vmem_limit_bytes=LIMIT),
         cost_estimate=LITTLE,
@@ -238,10 +242,10 @@
     gm_ref[0] = jnp.concatenate(maps, axis=0).T.astype(gm_ref.dtype)
 
 
-def key_kernel(part, base, table, *refs):
+def key_kernel(begun, part, base, table, *refs):
     k_refs, v_refs = refs[:part], refs[part : 2 * part]
     w_ref, sx_ref, dk_ref, dv_ref = refs[2 * part : 2 * part + 4]
-    out, gm_ref, k_all, v_all, vt_all, total, logs, weights = refs[2 * part + 5 :]
+    out, gm_ref, k_all, v_all, vt_all, total, logs, weights = refs[2 * part + 4 + begun :]
     hd = k_all.shape[1]
     step = pl.program_id(0)
 
@@ -416,15 +420,15 @@
     table = jnp.stack([jnp.asarray(v, jnp.int32) for v in values])
 
     own_maps = jnp.concatenate((query_map, key_map), axis=-1)
-    maps = jnp.stack([own_maps] + [across(own_maps, -s) for s in slots[1:]])
+    near_maps = jnp.stack([own_maps] + [across(own_maps, -s) for s in slots[1:]])
     kv_sent = pack(table, base["kv"], (key_rows, value_rows), part, grp, hd)
     kv = [kv_sent[0]] + [around(kv_sent[r], r) for r in shifts[1:]]
-    maps = lax.all_gather(maps, "fsdp")
+    maps = lax.all_gather(near_maps, "fsdp")
 
     rows = {}
     for s in order:
         sent = pack(
-            after(table, maps),
+            after(table, near_maps, *kv),
             base["sent"] + s * part,
             (query_rows, grad_out),
             part,
@@ -433,10 +437,6 @@
         )
         rows[s] = [sent[0]] + [around(sent[r], r) for r in shifts[1:]]
 
-    params = pltpu.CompilerParams(
-        dimension_semantics=("arbitrary",), vmem_limit_bytes=LIMIT
-    )
-
     def piece_specs(column, count):
         return [pl.BlockSpec((tok, count * hd), lambda h, t: (0, column(h)))] * part
 
@@ -459,7 +459,7 @@
     dv_spec, dv_shape = pl.BlockSpec((hd, BLK), lambda h, t: (0, 0)), of(F32, hd, BLK)
     low, wide = pltpu.VMEM((BLK, hd), BF16), pltpu.VMEM((BLK, PAIR * hd), BF16)
 
-    def call(kernel, outs, specs, out_specs, arrays, scratch, name, alias=()):
+    def call(kernel, outs, specs, out_specs, arrays, scratch, name, alias=(), limit=LIMIT):
         return pl.pallas_call(
             functools.partial(kernel, part, base["sorted"]),
             out_shape=outs,
@@ -470,7 +470,9 @@
                 out_specs=out_specs,
                 scratch_shapes=scratch,
             ),
-            compiler_params=params,
+            compiler_params=pltpu.CompilerParams(
+                dimension_semantics=("arbitrary",), vmem_limit_bytes=limit
+            ),
             cost_estimate=LITTLE,
             input_output_aliases=dict(alias),
             name=name,
@@ -487,8 +489,7 @@
             "states",
         )[0]
 
-    def spread(parts, total, when, extra, closing):
-        others = [along(total, r) for r in range(1, fsdp)]
+    def spread(parts, others, when, extra, closing):
         weights = [base["near " + when], base["far " + when], base["seq"]]
         result = whole_call(
             functools.partial(spread_kernel, grp, fsdp - 1, closing, *weights),
@@ -500,12 +501,16 @@
         )
         return [result[0]] + [across(result[s], -s) for s in slots[1:]], result[grp:]
 
+    def around_all(total):
+        return [along(total, r) for r in range(1, fsdp)]
+
     def totals_of(parts):
         return whole_call(total_kernel, [ext_shape], table, parts, "totals")[0]
 
     partial = {s: states_of(s) for s in order}
     parts = [after(partial[0], *rows[order[0]])] + [across(partial[s], s) for s in slots[1:]]
-    state, _ = spread(parts, totals_of(parts), "before", [prefix_state, prefix_norm], False)
+    others = around_all(totals_of(parts))
+    state, _ = spread(parts, others, "before", [prefix_state, prefix_norm], False)
 
     def block_of(s):
         return call(
@@ -525,6 +530,7 @@
             [*kv, *kv, *rows[s], *rows[s], maps, state[s]],
             [low, low, pltpu.VMEM((hd, BLK), BF16), wide, wide],
             "blocks",
+            limit=LARGE,
         )
 
     def rows_for(array, device):
@@ -535,24 +541,28 @@
     for s in order:
         blocks[s] = block_of(s)
         parts[s] = across(blocks[s][3], s) if s else blocks[s][3]
-        if s:
-            q_maps += [apart(rows_for(blocks[s][4], seq + r), s, r) for r in range(fsdp)]
-    parts = [after(parts[0], *q_maps)] + [parts[s] for s in slots[1:]]
+    parts = [parts[s] for s in slots]
     total = totals_of(parts)
-    suffix, (grad_prefix,) = spread(parts, total, "after", [], True)
-    returned = {s: within(after(blocks[s][0], total if s else suffix[0])) for s in order}
+    for s in slots[1:]:
+        late = after(blocks[s][4], total)
+        q_maps += [apart(rows_for(late, seq + r), s, r) for r in range(fsdp)]
+    others = around_all(total)
+    suffix, (grad_prefix,) = spread(parts, others, "after", [], True)
+    returned = {s: within(after(blocks[s][0], others[0])) for s in order if s}
 
     kv_type = BF16 if replicas == 1 else F32
-    pairs = jnp.zeros((part, tok, grp * 2 * hd), kv_type)
+    pairs = of(kv_type, part, tok, grp * 2 * hd)
     k_maps, both_maps, key_gm = [], [], {}
     for s in slots:
+        begun = [] if s == 0 else [pairs]
         pairs, key_gm[s] = call(
-            key_kernel,
+            functools.partial(key_kernel, bool(begun)),
             [of(kv_type, *pairs.shape), gm_shape],
             kv_specs(s)
-            + [map_spec(s), ext_spec, dk_spec, dv_spec, pl.BlockSpec(memory_space=pl.ANY)],
+            + [map_spec(s), ext_spec, dk_spec, dv_spec]
+            + [pl.BlockSpec(memory_space=pl.ANY)] * len(begun),
             [pl.BlockSpec((part, tok, 2 * hd), lambda h, t: (0, 0, s)), gm_spec],
-            [*kv, *kv, maps, suffix[s], blocks[s][1], blocks[s][2], pairs],
+            [*kv, *kv, maps, suffix[s], blocks[s][1], blocks[s][2], *begun],
             [
                 low,
                 low,
@@ -562,18 +572,18 @@
                 pltpu.VMEM((heads * half, hd), BF16),
             ],
             "keys",
-            {2 * part + 5: 0},
+            {2 * part + 5: 0} if begun else {},
         )
         if s == 0:
-            two = after(jnp.stack([blocks[s][4], key_gm[s]]), *suffix[1:])
+            two = after(jnp.stack([blocks[s][4], key_gm[s]]), *suffix[1:], *q_maps)
             both_maps = [along(rows_for(two, seq + r), r) for r in range(1, fsdp)]
+            returned[s] = within(after(blocks[s][0], key_gm[s]))
         else:
             k_maps += [apart(rows_for(key_gm[s], seq + r), s, r) for r in range(fsdp)]
 
-    pairs = within(after(pairs, *returned.values()))
-    (grad_queries,) = unpack(table, base["owner"], [returned[s] for s in slots], 1, heads * hd)
-    pairs = [pairs[:, :, s * 2 * hd : (s + 1) * 2 * hd] for s in slots]
-    grad_keys, grad_values = unpack(table, base["owner"], pairs, 2, hd)
+    pairs = within(pairs)
+    (grad_queries,) = unpack(table, base["owner"], [returned[s] for s in slots], 1, 1, heads * hd)
+    grad_keys, grad_values = unpack(table, base["owner"], [pairs], grp, 2, hd)
     if replicas > 1:
         grad_keys, grad_values = (
             jnp.sum(a.reshape(tok, kv_heads, replicas, hd), axis=2)

time: 230 us -> 225 us (0.978)
  local copies, waits for them, and re-layouts: 17.1 us -> 7.46 us
  waiting for transfers between devices: 83.2 us -> 85.6 us
    all_to_all x3, waiting for transfers between devices: 0.01 us -> 22.1 us  [within(): lax.all_to_all(array, 'ctx', 0, 0, axis_index_groups=blocks_of, tiled=True)]
    ppermute x9, waiting for transfers between devices: 25.1 us -> 4.32 us  [around(): lax.ppermute(array, 'ctx', [(d, d // part * part + (d + shift) % part) fo...]
    ppermute x8, waiting for transfers between devices: 3.63 us -> 12 us  [apart(): return lax.ppermute(array, ('ctx', 'fsdp'), moves)]
    unnamed x64 -> x74, local copies, waits for them, and re-layouts: 14.2 us -> 7.27 us
    ppermute x5, waiting for transfers between devices: 27.3 us -> 21.6 us  [across(): lax.ppermute(array, 'ctx', [(d, (d + shift * part) % ctx) for d in range(...]
    ppermute x9, starting transfers between devices: 6.36 us -> 9.72 us  [along(): lax.ppermute(array, 'fsdp', [(d, (d + shift) % fsdp) for d in range(fsdp)])]
    pallas_call x6, Pallas kernels: 48.3 us -> 50.6 us  [call(): pl.pallas_call(functools.partial(kernel, part, base['sorted']), out_shape...]
  transfers between devices with their start and end apart: 34 -> 34, of which waited for: 14 -> 18; matrix products, arithmetic and copies ran while one was open for 1% -> 0% of each run, Pallas kernels for 25% -> 22%
where the time goes in v8:
time: 225 us; the launch traced here: 224 us
  waiting for transfers between devices  85.6 us (38%)
  Pallas kernels  62.7 us (28%)
  starting transfers between devices  56.1 us (25%)
  blocking collectives  9.99 us (4%)
  local copies, waits for them, and re-layouts  7.46 us (3%)
    pallas_call x6, Pallas kernels, call(): pl.pallas_call(functools.partial(kernel, part, base['sorted']), out_shape...  50.6 us
    ppermute x9, waiting for transfers between devices, along(): lax.ppermute(array, 'fsdp', [(d, (d + shift) % fsdp) for d in range(fsdp)])  25.7 us
    all_to_all x3, waiting for transfers between devices, within(): lax.all_to_all(array, 'ctx', 0, 0, axis_index_groups=blocks_of, tiled=True)  22.1 us
    ppermute x5, waiting for transfers between devices, across(): lax.ppermute(array, 'ctx', [(d, (d + shift * part) % ctx) for d in range(...  21.6 us
    ppermute x8, starting transfers between devices, apart(): return lax.ppermute(array, ('ctx', 'fsdp'), moves)  15.3 us
    all_to_all x3, starting transfers between devices, within(): lax.all_to_all(array, 'ctx', 0, 0, axis_index_groups=blocks_of, tiled=True)  12.9 us
    ppermute x9, starting transfers between devices, around(): lax.ppermute(array, 'ctx', [(d, d // part * part + (d + shift) % part) fo...  12.2 us
    ppermute x8, waiting for transfers between devices, apart(): return lax.ppermute(array, ('ctx', 'fsdp'), moves)  12 us
  transfers between devices with their start and end apart: 34, of which 18 were waited for; matrix products, arithmetic and copies ran while one was open for 0% of the time, Pallas kernels for 22%

profile of v8, /device:TPU:1, one launch (start us, length us, event | category | flops | bytes accessed | tf_op | source)
XLA Modules:
  0.0 223.6 jit_solution(2769132745268722983)
XLA Ops:
  20.2 10.0 %all-gather = bf16[8,8,32,128]{3,2,1,0:T(8,128)(2,1)S(1)} all-gather(bf16[2,8,32,128]{3,2,1,0:T(8,128)(2,1)S(1)} %pad_maximum_fusion.1), channel_id=2, replica_groups=mesh['ctx'=8,'fsdp'=4] {'fsdp'}, dimensions={0}, use_global_device_ids=true | all-gather | bytes 655360 | tf_op jit(solution)/shard_map/all_gather | solution.py:426
  30.2 3.5 %states.3 = bf16[8,144,128]{2,1,0:T(8,128)(2,1)S(1)} custom-call(s32[43]{0:T(128)S(1)} %stack.193.table, bf16[128,512]{1,0:T(8,128)(2,1)S(1)} %get-tuple-element.47.refs_0_.refs_4_, bf16[128,512]{1,0:T(8,128)(2,1)S(1)} %collective-permute-done.refs_1_.refs_5_, bf16[128,512]{1,0:T(8,128)(2,1)S(1)} %collective-permute-done.1.refs_2_.refs_6_, ...), custom_call_target="tpu_custom_call" | custom-call | flops 1000 | bytes 1000 | tf_op jit(solution)/shard_map/states/pallas_call | solution.py:463
  33.9 3.5 %states.2.refs_0_ = bf16[8,144,128]{2,1,0:T(8,128)(2,1)S(1)} custom-call(s32[43]{0:T(128)S(1)} %stack.193.table, bf16[128,512]{1,0:T(8,128)(2,1)S(1)} %get-tuple-element.47.refs_0_.refs_4_, bf16[128,512]{1,0:T(8,128)(2,1)S(1)} %collective-permute-done.refs_1_.refs_5_, bf16[128,512]{1,0:T(8,128)(2,1)S(1)} %collective-permute-done.1.refs_2_.refs_6_, ...), custom_call_target="tpu_custom_call" | custom-call | flops 1000 | bytes 1000 | tf_op jit(solution)/shard_map/states/pallas_call | solution.py:463
  37.5 4.3 %collective-permute-done.9.refs_11_.refs_15_ = bf16[128,2048]{1,0:T(8,128)(2,1)S(1)} collective-permute-done((bf16[128,2048]{1,0:T(8,128)(2,1)S(1)}, bf16[128,2048]{1,0:T(8,128)(2,1)S(1)}, u32[]{:S(2)}, u32[]{:S(2)}) %collective-permute-start.9) | collective-permute-done | bytes 524320 | tf_op jit(solution)/shard_map/ppermute | solution.py:382
  41.8 4.1 %collective-permute-done.10.refs_1_ = bf16[8,144,128]{2,1,0:T(8,128)(2,1)S(1)} collective-permute-done((bf16[8,144,128]{2,1,0:T(8,128)(2,1)S(1)}, bf16[8,144,128]{2,1,0:T(8,128)(2,1)S(1)}, u32[]{:S(2)}, u32[]{:S(2)}) %collective-permute-start.10) | collective-permute-done | bytes 294944 | tf_op jit(solution)/shard_map/ppermute | solution.py:387
  46.5 3.4 %collective-permute-start.11 = (bf16[8,144,128]{2,1,0:T(8,128)(2,1)S(1)}, bf16[8,144,128]{2,1,0:T(8,128)(2,1)S(1)}, u32[]{:S(2)}, u32[]{:S(2)}) collective-permute-start(bf16[8,144,128]{2,1,0:T(8,128)(2,1)S(1)} %totals.2), channel_id=1, source_target_pairs={{0,1},{1,2},{2,3},{3,0},{4,5},{5,6},{6,7},{7,4},{8,9},{9,10},{10,1... | collective-permute-start | bytes 884744 | tf_op jit(solution)/shard_map/ppermute | solution.py:390
  55.1 10.4 %collective-permute-done.12.refs_3_ = bf16[8,144,128]{2,1,0:T(8,128)(2,1)S(1)} collective-permute-done((bf16[8,144,128]{2,1,0:T(8,128)(2,1)S(1)}, bf16[8,144,128]{2,1,0:T(8,128)(2,1)S(1)}, u32[]{:S(2)}, u32[]{:S(2)}) %collective-permute-start.12) | collective-permute-done | bytes 294944 | tf_op jit(solution)/shard_map/ppermute | solution.py:390
  72.2 9.5 %collective-permute-done.14.refs_17_ = bf16[8,144,128]{2,1,0:T(8,128)(2,1)S(1)} collective-permute-done((bf16[8,144,128]{2,1,0:T(8,128)(2,1)S(1)}, bf16[8,144,128]{2,1,0:T(8,128)(2,1)S(1)}, u32[]{:S(2)}, u32[]{:S(2)}) %collective-permute-start.14) | collective-permute-done | bytes 294944 | tf_op jit(solution)/shard_map/ppermute | solution.py:387
  82.4 16.3 %blocks.3 = (bf16[4,128,1024]{2,1,0:T(8,128)(2,1)}, f32[8,128,512]{2,1,0:T(8,128)}, f32[128,512]{1,0:T(8,128)}, bf16[8,144,128]{2,1,0:T(8,128)(2,1)}, bf16[4,128,128]{2,1,0:T(8,128)(2,1)}) custom-call(s32[43]{0:T(128)} %copy-done.24, bf16[128,512]{1,0:T(8,128)(2,1)} %copy-done.4, bf16[128,512]{1,0:T(8,128)(2,1)} %copy-done.6, bf16[128,512]{1,0:T(8,128)(2,1)} %copy-done.8, ...), custom_call_target="tpu_custom_call" | custom-call | flops 1000 | bytes 1000 | tf_op jit(solution)/shard_map/blocks/pallas_call | solution.py:463
  100.0 16.4 %blocks.2 = (bf16[4,128,1024]{2,1,0:T(8,128)(2,1)}, f32[8,128,512]{2,1,0:T(8,128)}, f32[128,512]{1,0:T(8,128)}, bf16[8,144,128]{2,1,0:T(8,128)(2,1)}, bf16[4,128,128]{2,1,0:T(8,128)(2,1)}) custom-call(s32[43]{0:T(128)} %copy-done.24, bf16[128,512]{1,0:T(8,128)(2,1)} %copy-done.4, bf16[128,512]{1,0:T(8,128)(2,1)} %copy-done.6, bf16[128,512]{1,0:T(8,128)(2,1)} %copy-done.8, ...), custom_call_target="tpu_custom_call" | custom-call | flops 1000 | bytes 1000 | tf_op jit(solution)/shard_map/blocks/pallas_call | solution.py:463
  120.4 5.7 %collective-permute-done.16.refs_2_ = bf16[8,144,128]{2,1,0:T(8,128)(2,1)S(1)} collective-permute-done((bf16[8,144,128]{2,1,0:T(8,128)(2,1)S(1)}, bf16[8,144,128]{2,1,0:T(8,128)(2,1)S(1)}, u32[]{:S(2)}, u32[]{:S(2)}) %collective-permute-start.16) | collective-permute-done | bytes 294944 | tf_op jit(solution)/shard_map/ppermute | solution.py:390
  126.1 6.3 %collective-permute-done.17.refs_3_ = bf16[8,144,128]{2,1,0:T(8,128)(2,1)S(1)} collective-permute-done((bf16[8,144,128]{2,1,0:T(8,128)(2,1)S(1)}, bf16[8,144,128]{2,1,0:T(8,128)(2,1)S(1)}, u32[]{:S(2)}, u32[]{:S(2)}) %collective-permute-start.17) | collective-permute-done | bytes 294944 | tf_op jit(solution)/shard_map/ppermute | solution.py:390
  138.4 5.4 %keys.2 = (bf16[4,128,512]{2,1,0:T(8,128)(2,1)}, bf16[4,128,128]{2,1,0:T(8,128)(2,1)S(1)}) custom-call(s32[43]{0:T(128)S(1)} %copy-done.25, bf16[128,512]{1,0:T(8,128)(2,1)S(1)} %copy-done.5, bf16[128,512]{1,0:T(8,128)(2,1)S(1)} %copy-done.7, bf16[128,512]{1,0:T(8,128)(2,1)S(1)} %copy-done.9, bf16[128,512]{1,0:T(8,128)(2,1)S(1)} %copy-done.11, ...), custom_call_target="tpu_custom_call" | custom-call | flops 1000 | bytes 1000 | tf_op jit(solution)/shard_map/keys/pallas_call | solution.py:463
  143.8 5.6 %collective-permute-done.19.refs_9_ = bf16[8,144,128]{2,1,0:T(8,128)(2,1)S(1)} collective-permute-done((bf16[8,144,128]{2,1,0:T(8,128)(2,1)S(1)}, bf16[8,144,128]{2,1,0:T(8,128)(2,1)S(1)}, u32[]{:S(2)}, u32[]{:S(2)}) %collective-permute-start.19) | collective-permute-done | bytes 294944 | tf_op jit(solution)/shard_map/ppermute | solution.py:387
  149.4 5.5 %keys.3 = (bf16[4,128,512]{2,1,0:T(8,128)(2,1)}, bf16[4,128,128]{2,1,0:T(8,128)(2,1)S(1)}) custom-call(s32[43]{0:T(128)S(1)} %copy-done.25, bf16[128,512]{1,0:T(8,128)(2,1)S(1)} %copy-done.5, bf16[128,512]{1,0:T(8,128)(2,1)S(1)} %copy-done.7, bf16[128,512]{1,0:T(8,128)(2,1)S(1)} %copy-done.9, ...), custom_call_target="tpu_custom_call", output_to_operand_aliasing={{0}: (13, {})} | custom-call | flops 1000 | bytes 1000 | tf_op jit(solution)/shard_map/keys/pallas_call | solution.py:463
  154.9 5.9 %all-to-all-start.2 = ((bf16[4,128,512]{2,1,0:T(8,128)(2,1)}), bf16[4,128,512]{2,1,0:T(8,128)(2,1)S(1)}, u32[]{:S(2)}, u32[]{:S(2)}) async-start(bf16[4,128,512]{2,1,0:T(8,128)(2,1)} %get-tuple-element.77), calls=%async_computation.2 | async-start | bytes 1048576 | tf_op jit(solution)/shard_map/all_to_all | solution.py:379
  160.8 9.0 %all-to-all-done.2.refs_0_ = bf16[4,128,512]{2,1,0:T(8,128)(2,1)S(1)} async-done(((bf16[4,128,512]{2,1,0:T(8,128)(2,1)}), bf16[4,128,512]{2,1,0:T(8,128)(2,1)S(1)}, u32[]{:S(2)}, u32[]{:S(2)}) %all-to-all-start.2) | async-done | bytes 524320 | tf_op jit(solution)/shard_map/all_to_all | solution.py:379
  169.7 3.5 %all-to-all-start.1 = ((bf16[4,128,1024]{2,1,0:T(8,128)(2,1)}), bf16[4,128,1024]{2,1,0:T(8,128)(2,1)S(1)}, u32[]{:S(2)}, u32[]{:S(2)}) async-start(bf16[4,128,1024]{2,1,0:T(8,128)(2,1)} %get-tuple-element.72), calls=%async_computation.1 | async-start | bytes 2097152 | tf_op jit(solution)/shard_map/all_to_all | solution.py:379
  173.3 13.1 %all-to-all-done.1.refs_1_ = bf16[4,128,1024]{2,1,0:T(8,128)(2,1)S(1)} async-done(((bf16[4,128,1024]{2,1,0:T(8,128)(2,1)}), bf16[4,128,1024]{2,1,0:T(8,128)(2,1)S(1)}, u32[]{:S(2)}, u32[]{:S(2)}) %all-to-all-start.1) | async-done | bytes 1048608 | tf_op jit(solution)/shard_map/all_to_all | solution.py:379
  186.3 3.5 %all-to-all-start = ((bf16[4,128,1024]{2,1,0:T(8,128)(2,1)}), bf16[4,128,1024]{2,1,0:T(8,128)(2,1)S(1)}, u32[]{:S(2)}, u32[]{:S(2)}) async-start(bf16[4,128,1024]{2,1,0:T(8,128)(2,1)} %get-tuple-element.70), calls=%async_computation | async-start | bytes 2097152 | tf_op jit(solution)/shard_map/all_to_all | solution.py:379
  190.0 4.2 %collective-permute-start.21 = (bf16[4,32,128]{2,1,0:T(8,128)(2,1)S(1)}, bf16[4,32,128]{2,1,0:T(8,128)(2,1)S(1)}, u32[]{:S(2)}, u32[]{:S(2)}) collective-permute-start(bf16[4,32,128]{2,1,0:T(8,128)(2,1)S(1)} %get-tuple-element.97), channel_id=1, source_target_pairs={{0,17},{1,18},{2,19},{3,16},{4,21},{5,22},{6,23},{7,20},{8,25},{9,... | collective-permute-start | bytes 98312 | tf_op jit(solution)/shard_map/ppermute | solution.py:398
  195.7 5.1 %collective-permute-done.20.refs_3_ = bf16[4,32,128]{2,1,0:T(8,128)(2,1)S(1)} collective-permute-done((bf16[4,32,128]{2,1,0:T(8,128)(2,1)S(1)}, bf16[4,32,128]{2,1,0:T(8,128)(2,1)S(1)}, u32[]{:S(2)}, u32[]{:S(2)}) %collective-permute-start.20) | collective-permute-done | bytes 32800 | tf_op jit(solution)/shard_map/ppermute | solution.py:398
  203.0 5.0 %collective-permute-start.27 = (bf16[4,32,128]{2,1,0:T(8,128)(2,1)S(1)}, bf16[4,32,128]{2,1,0:T(8,128)(2,1)S(1)}, u32[]{:S(2)}, u32[]{:S(2)}) collective-permute-start(bf16[4,32,128]{2,1,0:T(8,128)(2,1)S(1)} %get-tuple-element.94), channel_id=1, source_target_pairs={{0,16},{1,17},{2,18},{3,19},{4,20},{5,21},{6,22},{7,23},{8,24},{9,... | collective-permute-start | bytes 98312 | tf_op jit(solution)/shard_map/ppermute | solution.py:398
  214.8 4.0 %collective-permute-done.30.refs_10_ = bf16[4,32,128]{2,1,0:T(8,128)(2,1)S(1)} collective-permute-done((bf16[4,32,128]{2,1,0:T(8,128)(2,1)S(1)}, bf16[4,32,128]{2,1,0:T(8,128)(2,1)S(1)}, u32[]{:S(2)}, u32[]{:S(2)}) %collective-permute-start.30) | collective-permute-done | bytes 32800 | tf_op jit(solution)/shard_map/ppermute | solution.py:398
  (144 shorter events, 58.8 us)
Async XLA Ops:
  4.3 9.5 %collective-permute-start = (bf16[128,512]{1,0:T(8,128)(2,1)S(1)}, bf16[128,512]{1,0:T(8,128)(2,1)S(1)}, u32[]{:S(2)}, u32[]{:S(2)}) collective-permute-start(bf16[128,512]{1,0:T(8,128)(2,1)S(1)} %get-tuple-element.48), channel_id=1, source_target_pairs={{0,4},{4,8},{8,12},{12,0},{16,20},{20,24},{24,28},{28,16},{1,5},{5... | collective-permute-start | bytes 393224 | tf_op jit(solution)/shard_map/ppermute | solution.py:382
  14.9 22.5 %collective-permute-start.7 = (bf16[128,2048]{1,0:T(8,128)(2,1)S(1)}, bf16[128,2048]{1,0:T(8,128)(2,1)S(1)}, u32[]{:S(2)}, u32[]{:S(2)}) collective-permute-start(bf16[128,2048]{1,0:T(8,128)(2,1)S(1)} %get-tuple-element.57), channel_id=1, source_target_pairs={{0,4},{4,8},{8,12},{12,0},{16,20},{20,24},{24,28},{28,16},{1,5},{5... | collective-permute-start | bytes 1572872 | tf_op jit(solution)/shard_map/ppermute | solution.py:382
  16.3 21.2 %collective-permute-start.8 = (bf16[128,2048]{1,0:T(8,128)(2,1)S(1)}, bf16[128,2048]{1,0:T(8,128)(2,1)S(1)}, u32[]{:S(2)}, u32[]{:S(2)}) collective-permute-start(bf16[128,2048]{1,0:T(8,128)(2,1)S(1)} %get-tuple-element.58), channel_id=1, source_target_pairs={{0,8},{4,12},{8,0},{12,4},{16,24},{20,28},{24,16},{28,20},{1,9},{5... | collective-permute-start | bytes 1572872 | tf_op jit(solution)/shard_map/ppermute | solution.py:382
  18.4 23.3 %collective-permute-start.9 = (bf16[128,2048]{1,0:T(8,128)(2,1)S(1)}, bf16[128,2048]{1,0:T(8,128)(2,1)S(1)}, u32[]{:S(2)}, u32[]{:S(2)}) collective-permute-start(bf16[128,2048]{1,0:T(8,128)(2,1)S(1)} %get-tuple-element.59), channel_id=1, source_target_pairs={{0,12},{4,0},{8,4},{12,8},{16,28},{20,16},{24,20},{28,24},{1,13},{... | collective-permute-start | bytes 1572872 | tf_op jit(solution)/shard_map/ppermute | solution.py:382
  33.8 12.1 %collective-permute-start.10 = (bf16[8,144,128]{2,1,0:T(8,128)(2,1)S(1)}, bf16[8,144,128]{2,1,0:T(8,128)(2,1)S(1)}, u32[]{:S(2)}, u32[]{:S(2)}) collective-permute-start(bf16[8,144,128]{2,1,0:T(8,128)(2,1)S(1)} %states.3), channel_id=1, source_target_pairs={{0,16},{4,20},{8,24},{12,28},{16,0},{20,4},{24,8},{28,12},{1,17},{... | collective-permute-start | bytes 884744 | tf_op jit(solution)/shard_map/ppermute | solution.py:387
  46.5 8.6 %collective-permute-start.11 = (bf16[8,144,128]{2,1,0:T(8,128)(2,1)S(1)}, bf16[8,144,128]{2,1,0:T(8,128)(2,1)S(1)}, u32[]{:S(2)}, u32[]{:S(2)}) collective-permute-start(bf16[8,144,128]{2,1,0:T(8,128)(2,1)S(1)} %totals.2), channel_id=1, source_target_pairs={{0,1},{1,2},{2,3},{3,0},{4,5},{5,6},{6,7},{7,4},{8,9},{9,10},{10,1... | collective-permute-start | bytes 884744 | tf_op jit(solution)/shard_map/ppermute | solution.py:390
  49.9 15.6 %collective-permute-start.12 = (bf16[8,144,128]{2,1,0:T(8,128)(2,1)S(1)}, bf16[8,144,128]{2,1,0:T(8,128)(2,1)S(1)}, u32[]{:S(2)}, u32[]{:S(2)}) collective-permute-start(bf16[8,144,128]{2,1,0:T(8,128)(2,1)S(1)} %totals.2), channel_id=1, source_target_pairs={{0,2},{1,3},{2,0},{3,1},{4,6},{5,7},{6,4},{7,5},{8,10},{9,11},{10,... | collective-permute-start | bytes 884744 | tf_op jit(solution)/shard_map/ppermute | solution.py:390
  52.6 13.6 %collective-permute-start.13 = (bf16[8,144,128]{2,1,0:T(8,128)(2,1)S(1)}, bf16[8,144,128]{2,1,0:T(8,128)(2,1)S(1)}, u32[]{:S(2)}, u32[]{:S(2)}) collective-permute-start(bf16[8,144,128]{2,1,0:T(8,128)(2,1)S(1)} %totals.2), channel_id=1, source_target_pairs={{0,3},{1,0},{2,1},{3,2},{4,7},{5,4},{6,5},{7,6},{8,11},{9,8},{10,9... | collective-permute-start | bytes 884744 | tf_op jit(solution)/shard_map/ppermute | solution.py:390
  67.1 14.6 %collective-permute-start.14 = (bf16[8,144,128]{2,1,0:T(8,128)(2,1)S(1)}, bf16[8,144,128]{2,1,0:T(8,128)(2,1)S(1)}, u32[]{:S(2)}, u32[]{:S(2)}) collective-permute-start(bf16[8,144,128]{2,1,0:T(8,128)(2,1)S(1)} %get-tuple-element.64), channel_id=1, source_target_pairs={{0,16},{4,20},{8,24},{12,28},{16,0},{20,4},{24,8},{28,12},{1,17},{... | collective-permute-start | bytes 884744 | tf_op jit(solution)/shard_map/ppermute | solution.py:387
  69.8 29.0 %collective-permute-start.4 = (bf16[128,2048]{1,0:T(8,128)(2,1)S(1)}, bf16[128,2048]{1,0:T(8,128)(2,1)S(1)}, u32[]{:S(2)}, u32[]{:S(2)}) collective-permute-start(bf16[128,2048]{1,0:T(8,128)(2,1)S(1)} %get-tuple-element.53), channel_id=1, source_target_pairs={{0,4},{4,8},{8,12},{12,0},{16,20},{20,24},{24,28},{28,16},{1,5},{5... | collective-permute-start | bytes 1572872 | tf_op jit(solution)/shard_map/ppermute | solution.py:382
  70.5 28.4 %collective-permute-start.5 = (bf16[128,2048]{1,0:T(8,128)(2,1)S(1)}, bf16[128,2048]{1,0:T(8,128)(2,1)S(1)}, u32[]{:S(2)}, u32[]{:S(2)}) collective-permute-start(bf16[128,2048]{1,0:T(8,128)(2,1)S(1)} %get-tuple-element.54), channel_id=1, source_target_pairs={{0,8},{4,12},{8,0},{12,4},{16,24},{20,28},{24,16},{28,20},{1,9},{5... | collective-permute-start | bytes 1572872 | tf_op jit(solution)/shard_map/ppermute | solution.py:382
  71.7 27.1 %collective-permute-start.6 = (bf16[128,2048]{1,0:T(8,128)(2,1)S(1)}, bf16[128,2048]{1,0:T(8,128)(2,1)S(1)}, u32[]{:S(2)}, u32[]{:S(2)}) collective-permute-start(bf16[128,2048]{1,0:T(8,128)(2,1)S(1)} %get-tuple-element.55), channel_id=1, source_target_pairs={{0,12},{4,0},{8,4},{12,8},{16,28},{20,16},{24,20},{28,24},{1,13},{... | collective-permute-start | bytes 1572872 | tf_op jit(solution)/shard_map/ppermute | solution.py:382
  98.7 17.7 %collective-permute-start.15 = (bf16[8,144,128]{2,1,0:T(8,128)(2,1)}, bf16[8,144,128]{2,1,0:T(8,128)(2,1)S(1)}, u32[]{:S(2)}, u32[]{:S(2)}) collective-permute-start(bf16[8,144,128]{2,1,0:T(8,128)(2,1)} %get-tuple-element.65), channel_id=1, source_target_pairs={{0,16},{4,20},{8,24},{12,28},{16,0},{20,4},{24,8},{28,12},{1,17},{... | collective-permute-start | bytes 884744 | tf_op jit(solution)/shard_map/ppermute | solution.py:387
  119.9 12.5 %collective-permute-start.17 = (bf16[8,144,128]{2,1,0:T(8,128)(2,1)S(1)}, bf16[8,144,128]{2,1,0:T(8,128)(2,1)S(1)}, u32[]{:S(2)}, u32[]{:S(2)}) collective-permute-start(bf16[8,144,128]{2,1,0:T(8,128)(2,1)S(1)} %totals.3), channel_id=1, source_target_pairs={{0,2},{1,3},{2,0},{3,1},{4,6},{5,7},{6,4},{7,5},{8,10},{9,11},{10,... | collective-permute-start | bytes 884744 | tf_op jit(solution)/shard_map/ppermute | solution.py:390
  119.9 12.5 %collective-permute-start.18 = (bf16[8,144,128]{2,1,0:T(8,128)(2,1)S(1)}, bf16[8,144,128]{2,1,0:T(8,128)(2,1)S(1)}, u32[]{:S(2)}, u32[]{:S(2)}) collective-permute-start(bf16[8,144,128]{2,1,0:T(8,128)(2,1)S(1)} %totals.3), channel_id=1, source_target_pairs={{0,3},{1,0},{2,1},{3,2},{4,7},{5,4},{6,5},{7,6},{8,11},{9,8},{10,9... | collective-permute-start | bytes 884744 | tf_op jit(solution)/shard_map/ppermute | solution.py:390
  134.1 15.3 %collective-permute-start.19 = (bf16[8,144,128]{2,1,0:T(8,128)(2,1)S(1)}, bf16[8,144,128]{2,1,0:T(8,128)(2,1)S(1)}, u32[]{:S(2)}, u32[]{:S(2)}) collective-permute-start(bf16[8,144,128]{2,1,0:T(8,128)(2,1)S(1)} %get-tuple-element.73), channel_id=1, source_target_pairs={{0,16},{4,20},{8,24},{12,28},{16,0},{20,4},{24,8},{28,12},{1,17},{... | collective-permute-start | bytes 884744 | tf_op jit(solution)/shard_map/ppermute | solution.py:387
  154.9 14.9 %all-to-all-start.2 = ((bf16[4,128,512]{2,1,0:T(8,128)(2,1)}), bf16[4,128,512]{2,1,0:T(8,128)(2,1)S(1)}, u32[]{:S(2)}, u32[]{:S(2)}) async-start(bf16[4,128,512]{2,1,0:T(8,128)(2,1)} %get-tuple-element.77), calls=%async_computation.2 | async-start | bytes 1048576 | tf_op jit(solution)/shard_map/all_to_all | solution.py:379
  169.7 16.6 %all-to-all-start.1 = ((bf16[4,128,1024]{2,1,0:T(8,128)(2,1)}), bf16[4,128,1024]{2,1,0:T(8,128)(2,1)S(1)}, u32[]{:S(2)}, u32[]{:S(2)}) async-start(bf16[4,128,1024]{2,1,0:T(8,128)(2,1)} %get-tuple-element.72), calls=%async_computation.1 | async-start | bytes 2097152 | tf_op jit(solution)/shard_map/all_to_all | solution.py:379
  186.3 35.2 %all-to-all-start = ((bf16[4,128,1024]{2,1,0:T(8,128)(2,1)}), bf16[4,128,1024]{2,1,0:T(8,128)(2,1)S(1)}, u32[]{:S(2)}, u32[]{:S(2)}) async-start(bf16[4,128,1024]{2,1,0:T(8,128)(2,1)} %get-tuple-element.70), calls=%async_computation | async-start | bytes 2097152 | tf_op jit(solution)/shard_map/all_to_all | solution.py:379
  190.0 10.9 %collective-permute-start.20 = (bf16[4,32,128]{2,1,0:T(8,128)(2,1)S(1)}, bf16[4,32,128]{2,1,0:T(8,128)(2,1)S(1)}, u32[]{:S(2)}, u32[]{:S(2)}) collective-permute-start(bf16[4,32,128]{2,1,0:T(8,128)(2,1)S(1)} %get-tuple-element.98), channel_id=1, source_target_pairs={{0,16},{1,17},{2,18},{3,19},{4,20},{5,21},{6,22},{7,23},{8,24},{9,... | collective-permute-start | bytes 98312 | tf_op jit(solution)/shard_map/ppermute | solution.py:398
  190.0 11.5 %collective-permute-start.21 = (bf16[4,32,128]{2,1,0:T(8,128)(2,1)S(1)}, bf16[4,32,128]{2,1,0:T(8,128)(2,1)S(1)}, u32[]{:S(2)}, u32[]{:S(2)}) collective-permute-start(bf16[4,32,128]{2,1,0:T(8,128)(2,1)S(1)} %get-tuple-element.97), channel_id=1, source_target_pairs={{0,17},{1,18},{2,19},{3,16},{4,21},{5,22},{6,23},{7,20},{8,25},{9,... | collective-permute-start | bytes 98312 | tf_op jit(solution)/shard_map/ppermute | solution.py:398
  208.8 10.0 %collective-permute-start.24 = (bf16[2,4,32,128]{3,2,1,0:T(8,128)(2,1)S(1)}, bf16[2,4,32,128]{3,2,1,0:T(8,128)(2,1)S(1)}, u32[]{:S(2)}, u32[]{:S(2)}) collective-permute-start(bf16[2,4,32,128]{3,2,1,0:T(8,128)(2,1)S(1)} %get-tuple-element.90), channel_id=1, source_target_pairs={{0,1},{1,2},{2,3},{3,0},{4,5},{5,6},{6,7},{7,4},{8,9},{9,10},{10,1... | collective-permute-start | bytes 196616 | tf_op jit(solution)/shard_map/ppermute | solution.py:390
  209.3 9.5 %collective-permute-start.25 = (bf16[2,4,32,128]{3,2,1,0:T(8,128)(2,1)S(1)}, bf16[2,4,32,128]{3,2,1,0:T(8,128)(2,1)S(1)}, u32[]{:S(2)}, u32[]{:S(2)}) collective-permute-start(bf16[2,4,32,128]{3,2,1,0:T(8,128)(2,1)S(1)} %get-tuple-element.89), channel_id=1, source_target_pairs={{0,2},{1,3},{2,0},{3,1},{4,6},{5,7},{6,4},{7,5},{8,10},{9,11},{10,... | collective-permute-start | bytes 196616 | tf_op jit(solution)/shard_map/ppermute | solution.py:390
  209.9 8.9 %collective-permute-start.26 = (bf16[2,4,32,128]{3,2,1,0:T(8,128)(2,1)S(1)}, bf16[2,4,32,128]{3,2,1,0:T(8,128)(2,1)S(1)}, u32[]{:S(2)}, u32[]{:S(2)}) collective-permute-start(bf16[2,4,32,128]{3,2,1,0:T(8,128)(2,1)S(1)} %get-tuple-element.88), channel_id=1, source_target_pairs={{0,3},{1,0},{2,1},{3,2},{4,7},{5,4},{6,5},{7,6},{8,11},{9,8},{10,9... | collective-permute-start | bytes 196616 | tf_op jit(solution)/shard_map/ppermute | solution.py:390
  (47 other events, 692.6 us)

commit v9 on v8

--- a/solution.py
+++ b/solution.py
@@ -318,23 +318,15 @@
             out[h, hd:, :] = thirds(norm)
 
 
-def close_kernel(pairs, singles, at, table, q_ref, k_ref, *refs):
-    both, q_parts, k_parts = (
-        refs[:pairs],
-        refs[pairs : pairs + singles],
-        refs[pairs + singles : pairs + 2 * singles],
-    )
-    for i, (own, parts, out) in enumerate(
-        ((q_ref, q_parts, refs[-2]), (k_ref, k_parts, refs[-1]))
-    ):
+def close_kernel(at, table, q_ref, k_ref, *refs):
+    pieces, outs = refs[:-2], refs[-2:]
+    for i, (own, out) in enumerate(zip((q_ref, k_ref), outs)):
         rows, half = out.shape[1:]
         mine = pl.ds(pl.multiple_of(table[at] * rows, rows), rows)
         for h in range(own.shape[0]):
             total = own[h, mine, :].astype(F32)
-            for ref in both:
+            for ref in pieces:
                 total = total + ref[i, h].astype(F32)
-            for ref in parts:
-                total = total + ref[h].astype(F32)
             for u in range(PAIR):
                 out[h * PAIR + u] = total[:, u * half : (u + 1) * half]
 
@@ -389,6 +381,9 @@
     def along(array, shift):
         return lax.ppermute(array, "fsdp", [(d, (d + shift) % fsdp) for d in range(fsdp)])
 
+    def twin(array, bit):
+        return lax.ppermute(array, "fsdp", [(d, d ^ bit) for d in range(fsdp)])
+
     def apart(array, s, r):
         moves = [
             (d * fsdp + i, (d + s * part) % ctx * fsdp + (i + r) % fsdp)
@@ -399,7 +394,7 @@
 
     slot = [(block + s) % grp for s in slots]
     near = [(block - r) % grp for r in slots]
-    far = [(seq - r) % fsdp for r in range(1, fsdp)]
+    bits = [1 << i for i in range(fsdp.bit_length() - 1)]
     lists = {
         "seq": [seq],
         "owner": [slot[s] * part + p for s in slots for p in range(part)],
@@ -410,8 +405,8 @@
         "sorted": [(at - r) % part for r in shifts],
         "near before": [b < a for a in near for b in near],
         "near after": [b > a for a in near for b in near],
-        "far before": [other < seq for other in far],
-        "far after": [other > seq for other in far],
+        "far before": [(seq ^ bit) < seq for bit in bits],
+        "far after": [(seq ^ bit) > seq for bit in bits],
     }
     base, values = {}, []
     for name, entries in lists.items():
@@ -425,17 +420,16 @@
     kv = [kv_sent[0]] + [around(kv_sent[r], r) for r in shifts[1:]]
     maps = lax.all_gather(near_maps, "fsdp")
 
-    rows = {}
-    for s in order:
+    def sent_rows(s, *earlier):
         sent = pack(
-            after(table, near_maps, *kv),
+            after(table, *earlier),
             base["sent"] + s * part,
             (query_rows, grad_out),
             part,
             1,
             heads * hd,
         )
-        rows[s] = [sent[0]] + [around(sent[r], r) for r in shifts[1:]]
+        return [sent[0]] + [around(sent[r], r) for r in shifts[1:]]
 
     def piece_specs(column, count):
         return [pl.BlockSpec((tok, count * hd), lambda h, t: (0, column(h)))] * part
@@ -492,7 +486,7 @@
     def spread(parts, others, when, extra, closing):
         weights = [base["near " + when], base["far " + when], base["seq"]]
         result = whole_call(
-            functools.partial(spread_kernel, grp, fsdp - 1, closing, *weights),
+            functools.partial(spread_kernel, grp, len(bits), closing, *weights),
             [ext_shape] * grp + [of(F32, heads, map_rows, hd)] * closing,
             table,
             parts + others + extra,
@@ -501,16 +495,28 @@
         )
         return [result[0]] + [across(result[s], -s) for s in slots[1:]], result[grp:]
 
-    def around_all(total):
-        return [along(total, r) for r in range(1, fsdp)]
-
     def totals_of(parts):
         return whole_call(total_kernel, [ext_shape], table, parts, "totals")[0]
 
+    def around_all(total, waits=()):
+        others = []
+        for i, bit in enumerate(bits):
+            if others:
+                last = after(others[-1], waits[i - 1]) if i <= len(waits) else others[-1]
+                total = totals_of([total, last])
+            others.append(twin(total, bit))
+        return others
+
     partial = {s: states_of(s) for s in order}
-    parts = [after(partial[0], *rows[order[0]])] + [across(partial[s], s) for s in slots[1:]]
-    others = around_all(totals_of(parts))
+    parts = [partial[0]] + [across(partial[s], s) for s in slots[1:]]
+    bulk = sent_rows(order[0], partial[order[0]])
+    rows = {order[0]: bulk}
+    parts[0] = after(parts[0], bulk[1])
+    others = around_all(totals_of(parts), bulk[2:-1])
+    others[-1] = after(others[-1], bulk[-1])
     state, _ = spread(parts, others, "before", [prefix_state, prefix_norm], False)
+    for s in order[1:]:
+        rows[s] = sent_rows(s, state[0])
 
     def block_of(s):
         return call(
@@ -537,22 +543,20 @@
         pieces = array.reshape(*array.shape[:-2], fsdp, map_rows, array.shape[-1])
         return lax.dynamic_index_in_dim(pieces, device % fsdp, array.ndim - 2, keepdims=False)
 
-    blocks, parts, q_maps = {}, {}, []
+    blocks, parts = {}, {}
     for s in order:
         blocks[s] = block_of(s)
         parts[s] = across(blocks[s][3], s) if s else blocks[s][3]
     parts = [parts[s] for s in slots]
     total = totals_of(parts)
-    for s in slots[1:]:
-        late = after(blocks[s][4], total)
-        q_maps += [apart(rows_for(late, seq + r), s, r) for r in range(fsdp)]
     others = around_all(total)
     suffix, (grad_prefix,) = spread(parts, others, "after", [], True)
     returned = {s: within(after(blocks[s][0], others[0])) for s in order if s}
+    suffix[0] = after(suffix[0], *returned.values())
 
     kv_type = BF16 if replicas == 1 else F32
     pairs = of(kv_type, part, tok, grp * 2 * hd)
-    k_maps, both_maps, key_gm = [], [], {}
+    moved, key_gm = [], {}
     for s in slots:
         begun = [] if s == 0 else [pairs]
         pairs, key_gm[s] = call(
@@ -574,14 +578,15 @@
             "keys",
             {2 * part + 5: 0} if begun else {},
         )
-        if s == 0:
-            two = after(jnp.stack([blocks[s][4], key_gm[s]]), *suffix[1:], *q_maps)
-            both_maps = [along(rows_for(two, seq + r), r) for r in range(1, fsdp)]
+        two = jnp.stack([blocks[s][4], key_gm[s]])
+        if s:
+            moved += [apart(rows_for(two, seq + r), s, r) for r in range(fsdp)]
+        else:
+            two = after(two, *suffix[1:])
+            moved += [along(rows_for(two, seq + r), r) for r in range(1, fsdp)]
             returned[s] = within(after(blocks[s][0], key_gm[s]))
-        else:
-            k_maps += [apart(rows_for(key_gm[s], seq + r), s, r) for r in range(fsdp)]
-
-    pairs = within(pairs)
+
+    pairs = within(after(pairs, returned[0]))
     (grad_queries,) = unpack(table, base["owner"], [returned[s] for s in slots], 1, 1, heads * hd)
     grad_keys, grad_values = unpack(table, base["owner"], [pairs], grp, 2, hd)
     if replicas > 1:
@@ -592,10 +597,10 @@
             for a in (grad_keys, grad_values)
         )
     query_map_grad, key_map_grad = whole_call(
-        functools.partial(close_kernel, len(both_maps), len(q_maps), base["seq"]),
+        functools.partial(close_kernel, base["seq"]),
         [of(F32, heads, map_rows, half)] * 2,
         table,
-        [blocks[0][4], key_gm[0]] + both_maps + q_maps + k_maps,
+        [blocks[0][4], key_gm[0]] + moved,
         "close",
     )
     return grad_queries, grad_keys, grad_values, query_map_grad, key_map_grad, grad_prefix

time: 225 us -> 212 us (0.942)
  waiting for transfers between devices: 85.6 us -> 64.6 us
  local copies, waits for them, and re-layouts: 7.46 us -> 19.3 us
  starting transfers between devices: 56.1 us -> 51.8 us
    ppermute x9 -> x3, waiting for transfers between devices: 25.7 us -> 0.01 us  [along(): lax.ppermute(array, 'fsdp', [(d, (d + shift) % fsdp) for d in range(fsdp)])]
    all_to_all x3, waiting for transfers between devices: 22.1 us -> 0.96 us  [within(): lax.all_to_all(array, 'ctx', 0, 0, axis_index_groups=blocks_of, tiled=True)]
    ppermute x9, waiting for transfers between devices: 4.32 us -> 24.4 us  [around(): lax.ppermute(array, 'ctx', [(d, d // part * part + (d + shift) % part) fo...]
    unnamed x74 -> x98, local copies, waits for them, and re-layouts: 7.27 us -> 19.1 us
    ppermute x0 -> x4, waiting for transfers between devices: none -> 8.56 us  [twin(): return lax.ppermute(array, 'fsdp', [(d, d ^ bit) for d in range(fsdp)])]
    ppermute x8 -> x4, starting transfers between devices: 15.3 us -> 7.79 us  [apart(): return lax.ppermute(array, ('ctx', 'fsdp'), moves)]
    ppermute x9 -> x3, starting transfers between devices: 9.72 us -> 3.45 us  [along(): lax.ppermute(array, 'fsdp', [(d, (d + shift) % fsdp) for d in range(fsdp)])]
    ppermute x8 -> x4, waiting for transfers between devices: 12 us -> 6.26 us  [apart(): return lax.ppermute(array, ('ctx', 'fsdp'), moves)]
  transfers between devices with their start and end apart: 34 -> 28, of which waited for: 18 -> 10; matrix products, arithmetic and copies ran while one was open for 0% -> 1% of each run, Pallas kernels for 22% -> 23%
where the time goes in v9:
time: 212 us; the launch traced here: 210 us
  waiting for transfers between devices  64.6 us (30%)
  Pallas kernels  62.6 us (30%)
  starting transfers between devices  51.8 us (24%)
  local copies, waits for them, and re-layouts  19.3 us (9%)
  blocking collectives  9.03 us (4%)
    pallas_call x6, Pallas kernels, call(): pl.pallas_call(functools.partial(kernel, part, base['sorted']), out_shape...  49.3 us
    ppermute x5, waiting for transfers between devices, across(): lax.ppermute(array, 'ctx', [(d, (d + shift * part) % ctx) for d in range(...  24.4 us
    ppermute x9, waiting for transfers between devices, around(): lax.ppermute(array, 'ctx', [(d, d // part * part + (d + shift) % part) fo...  24.4 us
    unnamed x98, local copies, waits for them, and re-layouts  19.1 us
    all_to_all x3, starting transfers between devices, within(): lax.all_to_all(array, 'ctx', 0, 0, axis_index_groups=blocks_of, tiled=True)  15 us
    ppermute x9, starting transfers between devices, around(): lax.ppermute(array, 'ctx', [(d, d // part * part + (d + shift) % part) fo...  13.2 us
    all_gather x1, blocking collectives, shards(): maps = lax.all_gather(near_maps, 'fsdp')  9.03 us
    ppermute x4, waiting for transfers between devices, twin(): return lax.ppermute(array, 'fsdp', [(d, d ^ bit) for d in range(fsdp)])  8.56 us
  transfers between devices with their start and end apart: 28, of which 10 were waited for; matrix products, arithmetic and copies ran while one was open for 1% of the time, Pallas kernels for 23%

profile of v9, /device:TPU:1, one launch (start us, length us, event | category | flops | bytes accessed | tf_op | source)
XLA Modules:
  0.0 209.6 jit_solution(6916932044319340290)
XLA Ops:
  8.9 2.4 %collective-permute-start.3 = (bf16[8,32,128]{2,1,0:T(8,128)(2,1)S(1)}, bf16[8,32,128]{2,1,0:T(8,128)(2,1)S(1)}, u32[]{:S(2)}, u32[]{:S(2)}) collective-permute-start(bf16[8,32,128]{2,1,0:T(8,128)(2,1)S(1)} %pad_maximum_fusion.2), channel_id=1, source_target_pairs={{0,16},{4,20},{8,24},{12,28},{16,0},{20,4},{24,8},{28,12},{1,17},{... | collective-permute-start | bytes 196616 | tf_op jit(solution)/shard_map/ppermute | solution.py:379
  11.3 2.4 %collective-permute-done.3 = bf16[8,32,128]{2,1,0:T(8,128)(2,1)S(1)} collective-permute-done((bf16[8,32,128]{2,1,0:T(8,128)(2,1)S(1)}, bf16[8,32,128]{2,1,0:T(8,128)(2,1)S(1)}, u32[]{:S(2)}, u32[]{:S(2)}) %collective-permute-start.3) | collective-permute-done | bytes 65568 | tf_op jit(solution)/shard_map/ppermute | solution.py:379
  13.7 9.0 %all-gather = bf16[8,8,32,128]{3,2,1,0:T(8,128)(2,1)S(1)} all-gather(bf16[2,8,32,128]{3,2,1,0:T(8,128)(2,1)S(1)} %pad_maximum_fusion.1), channel_id=2, replica_groups=mesh['ctx'=8,'fsdp'=4] {'fsdp'}, dimensions={0}, use_global_device_ids=true | all-gather | bytes 655360 | tf_op jit(solution)/shard_map/all_gather | solution.py:421
  22.8 3.5 %states.3 = bf16[8,144,128]{2,1,0:T(8,128)(2,1)S(1)} custom-call(s32[41]{0:T(128)S(1)} %stack.186.table, bf16[128,512]{1,0:T(8,128)(2,1)S(1)} %get-tuple-element.51.refs_0_.refs_4_, bf16[128,512]{1,0:T(8,128)(2,1)S(1)} %collective-permute-done.refs_1_.refs_5_, bf16[128,512]{1,0:T(8,128)(2,1)S(1)} %collective-permute-done.1.refs_2_.refs_6_, ...), custom_call_target="tpu_custom_call" | custom-call | flops 1000 | bytes 1000 | tf_op jit(solution)/shard_map/states/pallas_call | solution.py:457
  27.8 2.7 %collective-permute-start.5 = (bf16[8,144,128]{2,1,0:T(8,128)(2,1)S(1)}, bf16[8,144,128]{2,1,0:T(8,128)(2,1)S(1)}, u32[]{:S(2)}, u32[]{:S(2)}) collective-permute-start(bf16[8,144,128]{2,1,0:T(8,128)(2,1)S(1)} %states.3), channel_id=1, source_target_pairs={{0,16},{4,20},{8,24},{12,28},{16,0},{20,4},{24,8},{28,12},{1,17},{... | collective-permute-start | bytes 884744 | tf_op jit(solution)/shard_map/ppermute | solution.py:379
  30.8 3.5 %states.2.refs_0_ = bf16[8,144,128]{2,1,0:T(8,128)(2,1)S(1)} custom-call(s32[41]{0:T(128)S(1)} %stack.186.table, bf16[128,512]{1,0:T(8,128)(2,1)S(1)} %get-tuple-element.51.refs_0_.refs_4_, bf16[128,512]{1,0:T(8,128)(2,1)S(1)} %collective-permute-done.refs_1_.refs_5_, bf16[128,512]{1,0:T(8,128)(2,1)S(1)} %collective-permute-done.1.refs_2_.refs_6_, ...), custom_call_target="tpu_custom_call" | custom-call | flops 1000 | bytes 1000 | tf_op jit(solution)/shard_map/states/pallas_call | solution.py:457
  34.3 14.3 %collective-permute-done.4.refs_9_.refs_13_ = bf16[128,2048]{1,0:T(8,128)(2,1)S(1)} collective-permute-done((bf16[128,2048]{1,0:T(8,128)(2,1)S(1)}, bf16[128,2048]{1,0:T(8,128)(2,1)S(1)}, u32[]{:S(2)}, u32[]{:S(2)}) %collective-permute-start.4) | collective-permute-done | bytes 524320 | tf_op jit(solution)/shard_map/ppermute | solution.py:374
  50.5 2.8 %collective-permute-start.9 = (bf16[128,2048]{1,0:T(8,128)(2,1)S(1)}, bf16[128,2048]{1,0:T(8,128)(2,1)S(1)}, u32[]{:S(2)}, u32[]{:S(2)}) collective-permute-start(bf16[128,2048]{1,0:T(8,128)(2,1)S(1)} %get-tuple-element.60), channel_id=1, source_target_pairs={{0,12},{4,0},{8,4},{12,8},{16,28},{20,16},{24,20},{28,24},{1,13},{... | collective-permute-start | bytes 1572872 | tf_op jit(solution)/shard_map/ppermute | solution.py:374
  54.5 10.0 %collective-permute-done.9.refs_11_.refs_15_ = bf16[128,2048]{1,0:T(8,128)(2,1)S(1)} collective-permute-done((bf16[128,2048]{1,0:T(8,128)(2,1)S(1)}, bf16[128,2048]{1,0:T(8,128)(2,1)S(1)}, u32[]{:S(2)}, u32[]{:S(2)}) %collective-permute-start.9) | collective-permute-done | bytes 524320 | tf_op jit(solution)/shard_map/ppermute | solution.py:374
  70.3 4.0 %collective-permute-start.10 = (bf16[128,2048]{1,0:T(8,128)(2,1)S(1)}, bf16[128,2048]{1,0:T(8,128)(2,1)S(1)}, u32[]{:S(2)}, u32[]{:S(2)}) collective-permute-start(bf16[128,2048]{1,0:T(8,128)(2,1)S(1)} %get-tuple-element.65), channel_id=1, source_target_pairs={{0,4},{4,8},{8,12},{12,0},{16,20},{20,24},{24,28},{28,16},{1,5},{5... | collective-permute-start | bytes 1572872 | tf_op jit(solution)/shard_map/ppermute | solution.py:374
  75.5 5.9 %collective-permute-done.13.refs_17_ = bf16[8,144,128]{2,1,0:T(8,128)(2,1)S(1)} collective-permute-done((bf16[8,144,128]{2,1,0:T(8,128)(2,1)S(1)}, bf16[8,144,128]{2,1,0:T(8,128)(2,1)S(1)}, u32[]{:S(2)}, u32[]{:S(2)}) %collective-permute-start.13) | collective-permute-done | bytes 294944 | tf_op jit(solution)/shard_map/ppermute | solution.py:379
  82.1 16.3 %blocks.3 = (bf16[4,128,1024]{2,1,0:T(8,128)(2,1)}, f32[8,128,512]{2,1,0:T(8,128)}, f32[128,512]{1,0:T(8,128)}, bf16[8,144,128]{2,1,0:T(8,128)(2,1)}, bf16[4,128,128]{2,1,0:T(8,128)(2,1)}) custom-call(s32[41]{0:T(128)} %copy-done.34, bf16[128,512]{1,0:T(8,128)(2,1)} %copy-done.4, bf16[128,512]{1,0:T(8,128)(2,1)} %copy-done.6, bf16[128,512]{1,0:T(8,128)(2,1)} %copy-done.8, ...), custom_call_target="tpu_custom_call" | custom-call | flops 1000 | bytes 1000 | tf_op jit(solution)/shard_map/blocks/pallas_call | solution.py:457
  99.7 16.4 %blocks.2 = (bf16[4,128,1024]{2,1,0:T(8,128)(2,1)}, f32[8,128,512]{2,1,0:T(8,128)}, f32[128,512]{1,0:T(8,128)}, bf16[8,144,128]{2,1,0:T(8,128)(2,1)}, bf16[4,128,128]{2,1,0:T(8,128)(2,1)}) custom-call(s32[41]{0:T(128)} %copy-done.34, bf16[128,512]{1,0:T(8,128)(2,1)} %copy-done.4, bf16[128,512]{1,0:T(8,128)(2,1)} %copy-done.6, bf16[128,512]{1,0:T(8,128)(2,1)} %copy-done.8, ...), custom_call_target="tpu_custom_call" | custom-call | flops 1000 | bytes 1000 | tf_op jit(solution)/shard_map/blocks/pallas_call | solution.py:457
  120.7 7.6 %all-to-all-start = ((bf16[4,128,1024]{2,1,0:T(8,128)(2,1)}), bf16[4,128,1024]{2,1,0:T(8,128)(2,1)S(1)}, u32[]{:S(2)}, u32[]{:S(2)}) async-start(bf16[4,128,1024]{2,1,0:T(8,128)(2,1)} %get-tuple-element.75), calls=%async_computation | async-start | bytes 2097152 | tf_op jit(solution)/shard_map/all_to_all | solution.py:371
  129.6 7.3 %collective-permute-done.16.refs_3_ = bf16[8,144,128]{2,1,0:T(8,128)(2,1)S(1)} collective-permute-done((bf16[8,144,128]{2,1,0:T(8,128)(2,1)S(1)}, bf16[8,144,128]{2,1,0:T(8,128)(2,1)S(1)}, u32[]{:S(2)}, u32[]{:S(2)}) %collective-permute-start.16) | collective-permute-done | bytes 294944 | tf_op jit(solution)/shard_map/ppermute | solution.py:385
  146.4 4.8 %keys.2 = (bf16[4,128,512]{2,1,0:T(8,128)(2,1)S(1)}, bf16[4,128,128]{2,1,0:T(8,128)(2,1)S(1)}) custom-call(s32[41]{0:T(128)S(1)} %copy-done.35, bf16[128,512]{1,0:T(8,128)(2,1)S(1)} %copy-done.5, bf16[128,512]{1,0:T(8,128)(2,1)S(1)} %copy-done.7, bf16[128,512]{1,0:T(8,128)(2,1)S(1)} %copy-done.9, bf16[128,512]{1,0:T(8,128)(2,1)S(1)} %copy-done.11, ...), custom_call_target="tpu_custom_call" | custom-call | flops 1000 | bytes 1000 | tf_op jit(solution)/shard_map/keys/pallas_call | solution.py:457
  152.0 3.5 %all-to-all-start.1 = ((bf16[4,128,1024]{2,1,0:T(8,128)(2,1)}), bf16[4,128,1024]{2,1,0:T(8,128)(2,1)S(1)}, u32[]{:S(2)}, u32[]{:S(2)}) async-start(bf16[4,128,1024]{2,1,0:T(8,128)(2,1)} %get-tuple-element.80), calls=%async_computation.1 | async-start | bytes 2097152 | tf_op jit(solution)/shard_map/all_to_all | solution.py:371
  156.5 16.2 %collective-permute-done.17.refs_9_ = bf16[8,144,128]{2,1,0:T(8,128)(2,1)S(1)} collective-permute-done((bf16[8,144,128]{2,1,0:T(8,128)(2,1)}, bf16[8,144,128]{2,1,0:T(8,128)(2,1)S(1)}, u32[]{:S(2)}, u32[]{:S(2)}) %collective-permute-start.17) | collective-permute-done | bytes 294944 | tf_op jit(solution)/shard_map/ppermute | solution.py:379
  176.3 4.8 %keys.3 = (bf16[4,128,512]{2,1,0:T(8,128)(2,1)S(1)}, bf16[4,128,128]{2,1,0:T(8,128)(2,1)S(1)}) custom-call(s32[41]{0:T(128)S(1)} %copy-done.35, bf16[128,512]{1,0:T(8,128)(2,1)S(1)} %copy-done.5, bf16[128,512]{1,0:T(8,128)(2,1)S(1)} %copy-done.7, bf16[128,512]{1,0:T(8,128)(2,1)S(1)} %copy-done.9, ...), custom_call_target="tpu_custom_call", output_to_operand_aliasing={{0}: (13, {})} | custom-call | flops 1000 | bytes 1000 | tf_op jit(solution)/shard_map/keys/pallas_call | solution.py:457
  182.5 3.9 %all-to-all-start.2 = ((bf16[4,128,512]{2,1,0:T(8,128)(2,1)}), bf16[4,128,512]{2,1,0:T(8,128)(2,1)S(1)}, u32[]{:S(2)}, u32[]{:S(2)}) async-start(bf16[4,128,512]{2,1,0:T(8,128)(2,1)} %copy-done.19), calls=%async_computation.2 | async-start | bytes 1048576 | tf_op jit(solution)/shard_map/all_to_all | solution.py:371
  187.2 2.7 %collective-permute-start.21 = (bf16[2,4,32,128]{3,2,1,0:T(8,128)(2,1)S(1)}, bf16[2,4,32,128]{3,2,1,0:T(8,128)(2,1)S(1)}, u32[]{:S(2)}, u32[]{:S(2)}) collective-permute-start(bf16[2,4,32,128]{3,2,1,0:T(8,128)(2,1)S(1)} %get-tuple-element.97), channel_id=1, source_target_pairs={{0,16},{1,17},{2,18},{3,19},{4,20},{5,21},{6,22},{7,23},{8,24},{9,... | collective-permute-start | bytes 196616 | tf_op jit(solution)/shard_map/ppermute | solution.py:393
  189.9 3.4 %collective-permute-start.22 = (bf16[2,4,32,128]{3,2,1,0:T(8,128)(2,1)S(1)}, bf16[2,4,32,128]{3,2,1,0:T(8,128)(2,1)S(1)}, u32[]{:S(2)}, u32[]{:S(2)}) collective-permute-start(bf16[2,4,32,128]{3,2,1,0:T(8,128)(2,1)S(1)} %get-tuple-element.98), channel_id=1, source_target_pairs={{0,17},{1,18},{2,19},{3,16},{4,21},{5,22},{6,23},{7,20},{8,25},{9,... | collective-permute-start | bytes 196616 | tf_op jit(solution)/shard_map/ppermute | solution.py:393
  195.1 2.8 %collective-permute-start.18 = (bf16[2,4,32,128]{3,2,1,0:T(8,128)(2,1)S(1)}, bf16[2,4,32,128]{3,2,1,0:T(8,128)(2,1)S(1)}, u32[]{:S(2)}, u32[]{:S(2)}) collective-permute-start(bf16[2,4,32,128]{3,2,1,0:T(8,128)(2,1)S(1)} %get-tuple-element.102), channel_id=1, source_target_pairs={{0,1},{1,2},{2,3},{3,0},{4,5},{5,6},{6,7},{7,4},{8,9},{9,10},{10,1... | collective-permute-start | bytes 196616 | tf_op jit(solution)/shard_map/ppermute | solution.py:382
  198.6 5.4 %collective-permute-done.23.refs_5_ = bf16[2,4,32,128]{3,2,1,0:T(8,128)(2,1)S(1)} collective-permute-done((bf16[2,4,32,128]{3,2,1,0:T(8,128)(2,1)S(1)}, bf16[2,4,32,128]{3,2,1,0:T(8,128)(2,1)S(1)}, u32[]{:S(2)}, u32[]{:S(2)}) %collective-permute-start.23) | collective-permute-done | bytes 65568 | tf_op jit(solution)/shard_map/ppermute | solution.py:393
  (157 shorter events, 52.7 us)
Async XLA Ops:
  4.2 18.5 %collective-permute-start = (bf16[128,512]{1,0:T(8,128)(2,1)S(1)}, bf16[128,512]{1,0:T(8,128)(2,1)S(1)}, u32[]{:S(2)}, u32[]{:S(2)}) collective-permute-start(bf16[128,512]{1,0:T(8,128)(2,1)S(1)} %get-tuple-element.52), channel_id=1, source_target_pairs={{0,4},{4,8},{8,12},{12,0},{16,20},{20,24},{24,28},{28,16},{1,5},{5... | collective-permute-start | bytes 393224 | tf_op jit(solution)/shard_map/ppermute | solution.py:374
  6.3 16.4 %collective-permute-start.1 = (bf16[128,512]{1,0:T(8,128)(2,1)S(1)}, bf16[128,512]{1,0:T(8,128)(2,1)S(1)}, u32[]{:S(2)}, u32[]{:S(2)}) collective-permute-start(bf16[128,512]{1,0:T(8,128)(2,1)S(1)} %get-tuple-element.53), channel_id=1, source_target_pairs={{0,8},{4,12},{8,0},{12,4},{16,24},{20,28},{24,16},{28,20},{1,9},{5... | collective-permute-start | bytes 393224 | tf_op jit(solution)/shard_map/ppermute | solution.py:374
  7.6 15.1 %collective-permute-start.2 = (bf16[128,512]{1,0:T(8,128)(2,1)S(1)}, bf16[128,512]{1,0:T(8,128)(2,1)S(1)}, u32[]{:S(2)}, u32[]{:S(2)}) collective-permute-start(bf16[128,512]{1,0:T(8,128)(2,1)S(1)} %get-tuple-element.54), channel_id=1, source_target_pairs={{0,12},{4,0},{8,4},{12,8},{16,28},{20,16},{24,20},{28,24},{1,13},{... | collective-permute-start | bytes 393224 | tf_op jit(solution)/shard_map/ppermute | solution.py:374
  27.4 21.2 %collective-permute-start.4 = (bf16[128,2048]{1,0:T(8,128)(2,1)S(1)}, bf16[128,2048]{1,0:T(8,128)(2,1)S(1)}, u32[]{:S(2)}, u32[]{:S(2)}) collective-permute-start(bf16[128,2048]{1,0:T(8,128)(2,1)S(1)} %get-tuple-element.56), channel_id=1, source_target_pairs={{0,4},{4,8},{8,12},{12,0},{16,20},{20,24},{24,28},{28,16},{1,5},{5... | collective-permute-start | bytes 1572872 | tf_op jit(solution)/shard_map/ppermute | solution.py:374
  27.8 20.8 %collective-permute-start.5 = (bf16[8,144,128]{2,1,0:T(8,128)(2,1)S(1)}, bf16[8,144,128]{2,1,0:T(8,128)(2,1)S(1)}, u32[]{:S(2)}, u32[]{:S(2)}) collective-permute-start(bf16[8,144,128]{2,1,0:T(8,128)(2,1)S(1)} %states.3), channel_id=1, source_target_pairs={{0,16},{4,20},{8,24},{12,28},{16,0},{20,4},{24,8},{28,12},{1,17},{... | collective-permute-start | bytes 884744 | tf_op jit(solution)/shard_map/ppermute | solution.py:379
  30.5 22.8 %collective-permute-start.7 = (bf16[128,2048]{1,0:T(8,128)(2,1)S(1)}, bf16[128,2048]{1,0:T(8,128)(2,1)S(1)}, u32[]{:S(2)}, u32[]{:S(2)}) collective-permute-start(bf16[128,2048]{1,0:T(8,128)(2,1)S(1)} %get-tuple-element.58), channel_id=1, source_target_pairs={{0,8},{4,12},{8,0},{12,4},{16,24},{20,28},{24,16},{28,20},{1,9},{5... | collective-permute-start | bytes 1572872 | tf_op jit(solution)/shard_map/ppermute | solution.py:374
  50.5 14.1 %collective-permute-start.9 = (bf16[128,2048]{1,0:T(8,128)(2,1)S(1)}, bf16[128,2048]{1,0:T(8,128)(2,1)S(1)}, u32[]{:S(2)}, u32[]{:S(2)}) collective-permute-start(bf16[128,2048]{1,0:T(8,128)(2,1)S(1)} %get-tuple-element.60), channel_id=1, source_target_pairs={{0,12},{4,0},{8,4},{12,8},{16,28},{20,16},{24,20},{28,24},{1,13},{... | collective-permute-start | bytes 1572872 | tf_op jit(solution)/shard_map/ppermute | solution.py:374
  53.9 10.6 %collective-permute-start.8 = (bf16[8,144,128]{2,1,0:T(8,128)(2,1)S(1)}, bf16[8,144,128]{2,1,0:T(8,128)(2,1)S(1)}, u32[]{:S(2)}, u32[]{:S(2)}) collective-permute-start(bf16[8,144,128]{2,1,0:T(8,128)(2,1)S(1)} %totals.5), channel_id=1, source_target_pairs={{0,2},{1,3},{2,0},{3,1},{4,6},{5,7},{6,4},{7,5},{8,10},{9,11},{10,... | collective-permute-start | bytes 884744 | tf_op jit(solution)/shard_map/ppermute | solution.py:385
  66.2 15.2 %collective-permute-start.13 = (bf16[8,144,128]{2,1,0:T(8,128)(2,1)S(1)}, bf16[8,144,128]{2,1,0:T(8,128)(2,1)S(1)}, u32[]{:S(2)}, u32[]{:S(2)}) collective-permute-start(bf16[8,144,128]{2,1,0:T(8,128)(2,1)S(1)} %get-tuple-element.71), channel_id=1, source_target_pairs={{0,16},{4,20},{8,24},{12,28},{16,0},{20,4},{24,8},{28,12},{1,17},{... | collective-permute-start | bytes 884744 | tf_op jit(solution)/shard_map/ppermute | solution.py:379
  70.3 28.2 %collective-permute-start.10 = (bf16[128,2048]{1,0:T(8,128)(2,1)S(1)}, bf16[128,2048]{1,0:T(8,128)(2,1)S(1)}, u32[]{:S(2)}, u32[]{:S(2)}) collective-permute-start(bf16[128,2048]{1,0:T(8,128)(2,1)S(1)} %get-tuple-element.65), channel_id=1, source_target_pairs={{0,4},{4,8},{8,12},{12,0},{16,20},{20,24},{24,28},{28,16},{1,5},{5... | collective-permute-start | bytes 1572872 | tf_op jit(solution)/shard_map/ppermute | solution.py:374
  74.3 24.2 %collective-permute-start.11 = (bf16[128,2048]{1,0:T(8,128)(2,1)S(1)}, bf16[128,2048]{1,0:T(8,128)(2,1)S(1)}, u32[]{:S(2)}, u32[]{:S(2)}) collective-permute-start(bf16[128,2048]{1,0:T(8,128)(2,1)S(1)} %get-tuple-element.66), channel_id=1, source_target_pairs={{0,8},{4,12},{8,0},{12,4},{16,24},{20,28},{24,16},{28,20},{1,9},{5... | collective-permute-start | bytes 1572872 | tf_op jit(solution)/shard_map/ppermute | solution.py:374
  74.4 24.1 %collective-permute-start.12 = (bf16[128,2048]{1,0:T(8,128)(2,1)S(1)}, bf16[128,2048]{1,0:T(8,128)(2,1)S(1)}, u32[]{:S(2)}, u32[]{:S(2)}) collective-permute-start(bf16[128,2048]{1,0:T(8,128)(2,1)S(1)} %get-tuple-element.67), channel_id=1, source_target_pairs={{0,12},{4,0},{8,4},{12,8},{16,28},{20,16},{24,20},{28,24},{1,13},{... | collective-permute-start | bytes 1572872 | tf_op jit(solution)/shard_map/ppermute | solution.py:374
  98.4 17.7 %collective-permute-start.14 = (bf16[8,144,128]{2,1,0:T(8,128)(2,1)}, bf16[8,144,128]{2,1,0:T(8,128)(2,1)S(1)}, u32[]{:S(2)}, u32[]{:S(2)}) collective-permute-start(bf16[8,144,128]{2,1,0:T(8,128)(2,1)} %get-tuple-element.72), channel_id=1, source_target_pairs={{0,16},{4,20},{8,24},{12,28},{16,0},{20,4},{24,8},{28,12},{1,17},{... | collective-permute-start | bytes 884744 | tf_op jit(solution)/shard_map/ppermute | solution.py:379
  120.7 22.1 %all-to-all-start = ((bf16[4,128,1024]{2,1,0:T(8,128)(2,1)}), bf16[4,128,1024]{2,1,0:T(8,128)(2,1)S(1)}, u32[]{:S(2)}, u32[]{:S(2)}) async-start(bf16[4,128,1024]{2,1,0:T(8,128)(2,1)} %get-tuple-element.75), calls=%async_computation | async-start | bytes 2097152 | tf_op jit(solution)/shard_map/all_to_all | solution.py:371
  129.0 8.0 %collective-permute-start.16 = (bf16[8,144,128]{2,1,0:T(8,128)(2,1)S(1)}, bf16[8,144,128]{2,1,0:T(8,128)(2,1)S(1)}, u32[]{:S(2)}, u32[]{:S(2)}) collective-permute-start(bf16[8,144,128]{2,1,0:T(8,128)(2,1)S(1)} %totals.7), channel_id=1, source_target_pairs={{0,2},{1,3},{2,0},{3,1},{4,6},{5,7},{6,4},{7,5},{8,10},{9,11},{10,... | collective-permute-start | bytes 884744 | tf_op jit(solution)/shard_map/ppermute | solution.py:385
  152.0 30.5 %all-to-all-start.1 = ((bf16[4,128,1024]{2,1,0:T(8,128)(2,1)}), bf16[4,128,1024]{2,1,0:T(8,128)(2,1)S(1)}, u32[]{:S(2)}, u32[]{:S(2)}) async-start(bf16[4,128,1024]{2,1,0:T(8,128)(2,1)} %get-tuple-element.80), calls=%async_computation.1 | async-start | bytes 2097152 | tf_op jit(solution)/shard_map/all_to_all | solution.py:371
  155.5 17.2 %collective-permute-start.17 = (bf16[8,144,128]{2,1,0:T(8,128)(2,1)}, bf16[8,144,128]{2,1,0:T(8,128)(2,1)S(1)}, u32[]{:S(2)}, u32[]{:S(2)}) collective-permute-start(bf16[8,144,128]{2,1,0:T(8,128)(2,1)} %copy-done.38), channel_id=1, source_target_pairs={{0,16},{4,20},{8,24},{12,28},{16,0},{20,4},{24,8},{28,12},{1,17},{... | collective-permute-start | bytes 884744 | tf_op jit(solution)/shard_map/ppermute | solution.py:379
  182.5 25.7 %all-to-all-start.2 = ((bf16[4,128,512]{2,1,0:T(8,128)(2,1)}), bf16[4,128,512]{2,1,0:T(8,128)(2,1)S(1)}, u32[]{:S(2)}, u32[]{:S(2)}) async-start(bf16[4,128,512]{2,1,0:T(8,128)(2,1)} %copy-done.19), calls=%async_computation.2 | async-start | bytes 1048576 | tf_op jit(solution)/shard_map/all_to_all | solution.py:371
  187.2 10.6 %collective-permute-start.21 = (bf16[2,4,32,128]{3,2,1,0:T(8,128)(2,1)S(1)}, bf16[2,4,32,128]{3,2,1,0:T(8,128)(2,1)S(1)}, u32[]{:S(2)}, u32[]{:S(2)}) collective-permute-start(bf16[2,4,32,128]{3,2,1,0:T(8,128)(2,1)S(1)} %get-tuple-element.97), channel_id=1, source_target_pairs={{0,16},{1,17},{2,18},{3,19},{4,20},{5,21},{6,22},{7,23},{8,24},{9,... | collective-permute-start | bytes 196616 | tf_op jit(solution)/shard_map/ppermute | solution.py:393
  189.9 8.5 %collective-permute-start.22 = (bf16[2,4,32,128]{3,2,1,0:T(8,128)(2,1)S(1)}, bf16[2,4,32,128]{3,2,1,0:T(8,128)(2,1)S(1)}, u32[]{:S(2)}, u32[]{:S(2)}) collective-permute-start(bf16[2,4,32,128]{3,2,1,0:T(8,128)(2,1)S(1)} %get-tuple-element.98), channel_id=1, source_target_pairs={{0,17},{1,18},{2,19},{3,16},{4,21},{5,22},{6,23},{7,20},{8,25},{9,... | collective-permute-start | bytes 196616 | tf_op jit(solution)/shard_map/ppermute | solution.py:393
  193.3 10.6 %collective-permute-start.23 = (bf16[2,4,32,128]{3,2,1,0:T(8,128)(2,1)S(1)}, bf16[2,4,32,128]{3,2,1,0:T(8,128)(2,1)S(1)}, u32[]{:S(2)}, u32[]{:S(2)}) collective-permute-start(bf16[2,4,32,128]{3,2,1,0:T(8,128)(2,1)S(1)} %get-tuple-element.99), channel_id=1, source_target_pairs={{0,18},{1,19},{2,16},{3,17},{4,22},{5,23},{6,20},{7,21},{8,26},{9,... | collective-permute-start | bytes 196616 | tf_op jit(solution)/shard_map/ppermute | solution.py:393
  195.0 9.8 %collective-permute-start.24 = (bf16[2,4,32,128]{3,2,1,0:T(8,128)(2,1)S(1)}, bf16[2,4,32,128]{3,2,1,0:T(8,128)(2,1)S(1)}, u32[]{:S(2)}, u32[]{:S(2)}) collective-permute-start(bf16[2,4,32,128]{3,2,1,0:T(8,128)(2,1)S(1)} %get-tuple-element.96), channel_id=1, source_target_pairs={{0,19},{1,16},{2,17},{3,18},{4,23},{5,20},{6,21},{7,22},{8,27},{9,... | collective-permute-start | bytes 196616 | tf_op jit(solution)/shard_map/ppermute | solution.py:393
  195.1 9.7 %collective-permute-start.18 = (bf16[2,4,32,128]{3,2,1,0:T(8,128)(2,1)S(1)}, bf16[2,4,32,128]{3,2,1,0:T(8,128)(2,1)S(1)}, u32[]{:S(2)}, u32[]{:S(2)}) collective-permute-start(bf16[2,4,32,128]{3,2,1,0:T(8,128)(2,1)S(1)} %get-tuple-element.102), channel_id=1, source_target_pairs={{0,1},{1,2},{2,3},{3,0},{4,5},{5,6},{6,7},{7,4},{8,9},{9,10},{10,1... | collective-permute-start | bytes 196616 | tf_op jit(solution)/shard_map/ppermute | solution.py:382
  197.9 6.9 %collective-permute-start.19 = (bf16[2,4,32,128]{3,2,1,0:T(8,128)(2,1)S(1)}, bf16[2,4,32,128]{3,2,1,0:T(8,128)(2,1)S(1)}, u32[]{:S(2)}, u32[]{:S(2)}) collective-permute-start(bf16[2,4,32,128]{3,2,1,0:T(8,128)(2,1)S(1)} %get-tuple-element.101), channel_id=1, source_target_pairs={{0,2},{1,3},{2,0},{3,1},{4,6},{5,7},{6,4},{7,5},{8,10},{9,11},{10,... | collective-permute-start | bytes 196616 | tf_op jit(solution)/shard_map/ppermute | solution.py:382
  (53 other events, 547.1 us)

commit v10 on v9

--- a/solution.py
+++ b/solution.py
@@ -170,7 +170,8 @@
     k_refs, v_refs = refs[:part], refs[part : 2 * part]
     q_refs, g_refs = refs[2 * part : 3 * part], refs[3 * part : 4 * part]
     w_ref, st_ref = refs[4 * part : 4 * part + 2]
-    gq_ref, dk_ref, dv_ref, sx_ref, gm_ref, k_all, v_all, vt_all, q_all, g_all = refs[4 * part + 2 :]
+    gq_refs = refs[4 * part + 2 : 5 * part + 2]
+    dk_ref, dv_ref, sx_ref, gm_ref, k_all, v_all, vt_all, q_all, g_all, gq_all = refs[5 * part + 2 :]
     hd = k_all.shape[1]
 
     @pl.when(pl.program_id(0) == 0)
@@ -232,14 +233,16 @@
             suffix = suffix + nt(own, scaled_low)
             suffix_norm = suffix_norm + jnp.sum(own_wide * norm_grad, axis=1, keepdims=True)
         dlog = jnp.concatenate(back, axis=1)
-        grads = nn(turned(dlog), weight[:half]).astype(BF16)
-        gq_ref[:, :, lanes] = grads.reshape(gq_ref.shape[0], -1, hd)
+        gq_all[:, lanes] = nn(turned(dlog), weight[:half]).astype(BF16)
         maps.append(nn(dlog, q_all[:, lanes]))
         dk_ref[u] = jnp.concatenate(dkey, axis=1)
         dv_ref[...] += jnp.concatenate(dvalue, axis=1)
         sx_ref[u, :hd, :] = suffix.astype(BF16)
         sx_ref[u, hd:, :] = thirds(jnp.broadcast_to(suffix_norm, (2 * half, 2 * half)).T[:1])
     gm_ref[0] = jnp.concatenate(maps, axis=0).T.astype(gm_ref.dtype)
+    for r, ref in enumerate(gq_refs):
+        rows = ref.shape[0]
+        ref[...] = gq_all[pl.ds(pl.multiple_of(table[base + r] * rows, rows), rows), :]
 
 
 def key_kernel(begun, part, base, table, *refs):
@@ -399,6 +402,7 @@
         "seq": [seq],
         "owner": [slot[s] * part + p for s in slots for p in range(part)],
         "sent": [slot[s] * part + (at + r) % part for s in slots for r in shifts],
+        "back": [slot[s] * part + (at + r) % part for s in slots for r in shifts],
         "kv": [
             (slot[s] * part + (at + r) % part) // replicas for r in shifts for s in slots
         ],
@@ -498,22 +502,18 @@
     def totals_of(parts):
         return whole_call(total_kernel, [ext_shape], table, parts, "totals")[0]
 
-    def around_all(total, waits=()):
+    def around_all(total):
         others = []
-        for i, bit in enumerate(bits):
-            if others:
-                last = after(others[-1], waits[i - 1]) if i <= len(waits) else others[-1]
-                total = totals_of([total, last])
+        for bit in bits:
+            total = totals_of([total, others[-1]]) if others else total
             others.append(twin(total, bit))
         return others
 
     partial = {s: states_of(s) for s in order}
     parts = [partial[0]] + [across(partial[s], s) for s in slots[1:]]
-    bulk = sent_rows(order[0], partial[order[0]])
-    rows = {order[0]: bulk}
-    parts[0] = after(parts[0], bulk[1])
-    others = around_all(totals_of(parts), bulk[2:-1])
-    others[-1] = after(others[-1], bulk[-1])
+    rows = {order[0]: sent_rows(order[0], near_maps, *kv)}
+    parts[0] = after(parts[0], *rows[order[0]])
+    others = around_all(totals_of(parts))
     state, _ = spread(parts, others, "before", [prefix_state, prefix_norm], False)
     for s in order[1:]:
         rows[s] = sent_rows(s, state[0])
@@ -521,20 +521,14 @@
     def block_of(s):
         return call(
             block_kernel,
-            [of(BF16, part, tok, heads * hd), dk_shape, dv_shape, ext_shape, gm_shape],
+            [of(BF16, tok, heads * hd)] * part + [dk_shape, dv_shape, ext_shape, gm_shape],
             kv_specs(s)
             + piece_specs(lambda h: h, PAIR)
             + piece_specs(lambda h: grid[0] + h, PAIR)
             + [map_spec(s), ext_spec],
-            [
-                pl.BlockSpec((part, tok, PAIR * hd), lambda h, t: (0, 0, h)),
-                dk_spec,
-                dv_spec,
-                ext_spec,
-                gm_spec,
-            ],
+            piece_specs(lambda h: h, PAIR) + [dk_spec, dv_spec, ext_spec, gm_spec],
             [*kv, *kv, *rows[s], *rows[s], maps, state[s]],
-            [low, low, pltpu.VMEM((hd, BLK), BF16), wide, wide],
+            [low, low, pltpu.VMEM((hd, BLK), BF16), wide, wide, wide],
             "blocks",
             limit=LARGE,
         )
@@ -545,14 +539,19 @@
 
     blocks, parts = {}, {}
     for s in order:
-        blocks[s] = block_of(s)
+        result = block_of(s)
+        blocks[s] = (result[:part], *result[part:])
         parts[s] = across(blocks[s][3], s) if s else blocks[s][3]
     parts = [parts[s] for s in slots]
     total = totals_of(parts)
     others = around_all(total)
     suffix, (grad_prefix,) = spread(parts, others, "after", [], True)
-    returned = {s: within(after(blocks[s][0], others[0])) for s in order if s}
-    suffix[0] = after(suffix[0], *returned.values())
+    def brought_back(s, begin):
+        pieces = [after(piece, begin) for piece in blocks[s][0]]
+        return [pieces[0]] + [around(pieces[r], -r) for r in shifts[1:]]
+
+    returned = {s: brought_back(s, others[0]) for s in order if s}
+    suffix[0] = after(suffix[0], *[piece for s in returned for piece in returned[s]])
 
     kv_type = BF16 if replicas == 1 else F32
     pairs = of(kv_type, part, tok, grp * 2 * hd)
@@ -584,10 +583,11 @@
         else:
             two = after(two, *suffix[1:])
             moved += [along(rows_for(two, seq + r), r) for r in range(1, fsdp)]
-            returned[s] = within(after(blocks[s][0], key_gm[s]))
-
-    pairs = within(after(pairs, returned[0]))
-    (grad_queries,) = unpack(table, base["owner"], [returned[s] for s in slots], 1, 1, heads * hd)
+            returned[s] = brought_back(s, key_gm[s])
+
+    pairs = within(after(pairs, *returned[0]))
+    back = [piece[None] for s in slots for piece in returned[s]]
+    (grad_queries,) = unpack(table, base["back"], back, 1, 1, heads * hd)
     grad_keys, grad_values = unpack(table, base["owner"], [pairs], grp, 2, hd)
     if replicas > 1:
         grad_keys, grad_values = (

time: 212 us -> 182 us (0.86); the launches traced: 210 us -> 182 us
  waiting for transfers between devices: 64.6 us -> 49 us
  local copies, waits for them, and re-layouts: 19.3 us -> 7.47 us
  starting transfers between devices: 51.8 us -> 49.2 us
    ppermute x9 -> x15, waiting for transfers between devices: 24.4 us -> 12.2 us  [around(): lax.ppermute(array, 'ctx', [(d, d // part * part + (d + shift) % part) fo...]
    unnamed x98 -> x90, local copies, waits for them, and re-layouts: 19.1 us -> 7.33 us
    all_to_all x3 -> x1, starting transfers between devices: 15 us -> 3.74 us  [within(): lax.all_to_all(array, 'ctx', 0, 0, axis_index_groups=blocks_of, tiled=True)]
    ppermute x9 -> x15, starting transfers between devices: 13.2 us -> 21.2 us  [around(): lax.ppermute(array, 'ctx', [(d, d // part * part + (d + shift) % part) fo...]
    ppermute x5, waiting for transfers between devices: 24.4 us -> 17.5 us  [across(): lax.ppermute(array, 'ctx', [(d, (d + shift * part) % ctx) for d in range(...]
    ppermute x4, waiting for transfers between devices: 8.56 us -> 14.6 us  [twin(): return lax.ppermute(array, 'fsdp', [(d, d ^ bit) for d in range(fsdp)])]
    ppermute x5, starting transfers between devices: 8.36 us -> 5.9 us  [across(): lax.ppermute(array, 'ctx', [(d, (d + shift * part) % ctx) for d in range(...]
  transfers between devices with their start and end apart: 28 -> 32, of which waited for: 10 -> 12; matrix products, arithmetic and copies ran while one was open for 1% -> 0% of each run, Pallas kernels for 23% -> 31%
where the time goes in v10:
time: 182 us
  Pallas kernels  64.5 us (35%)
  starting transfers between devices  49.2 us (27%)
  waiting for transfers between devices  49 us (27%)
  blocking collectives  9.99 us (5%)
  local copies, waits for them, and re-layouts  7.47 us (4%)
    pallas_call x6, Pallas kernels, call(): pl.pallas_call(functools.partial(kernel, part, base['sorted']), out_shape...  51.3 us
    ppermute x15, starting transfers between devices, around(): lax.ppermute(array, 'ctx', [(d, d // part * part + (d + shift) % part) fo...  21.2 us
    ppermute x5, waiting for transfers between devices, across(): lax.ppermute(array, 'ctx', [(d, (d + shift * part) % ctx) for d in range(...  17.5 us
    ppermute x4, waiting for transfers between devices, twin(): return lax.ppermute(array, 'fsdp', [(d, d ^ bit) for d in range(fsdp)])  14.6 us
    ppermute x15, waiting for transfers between devices, around(): lax.ppermute(array, 'ctx', [(d, d // part * part + (d + shift) % part) fo...  12.2 us
    all_gather x1, blocking collectives, shards(): maps = lax.all_gather(near_maps, 'fsdp')  9.99 us
    ppermute x4, starting transfers between devices, apart(): return lax.ppermute(array, ('ctx', 'fsdp'), moves)  9.71 us
    unnamed x90, local copies, waits for them, and re-layouts  7.33 us
  transfers between devices with their start and end apart: 32, of which 12 were waited for; matrix products, arithmetic and copies ran while one was open for 0% of the time, Pallas kernels for 31%

profile of v10, /device:TPU:1, one launch (start us, length us, event | category | flops | bytes accessed | tf_op | source)
XLA Modules:
  0.0 181.8 jit_solution(17869303709884841534)
XLA Ops:
  8.9 2.4 %collective-permute-start.3 = (bf16[8,32,128]{2,1,0:T(8,128)(2,1)S(1)}, bf16[8,32,128]{2,1,0:T(8,128)(2,1)S(1)}, u32[]{:S(2)}, u32[]{:S(2)}) collective-permute-start(bf16[8,32,128]{2,1,0:T(8,128)(2,1)S(1)} %pad_maximum_fusion.2), channel_id=1, source_target_pairs={{0,16},{4,20},{8,24},{12,28},{16,0},{20,4},{24,8},{28,12},{1,17},{... | collective-permute-start | bytes 196616 | tf_op jit(solution)/shard_map/ppermute | solution.py:382
  11.3 2.4 %collective-permute-done.3 = bf16[8,32,128]{2,1,0:T(8,128)(2,1)S(1)} collective-permute-done((bf16[8,32,128]{2,1,0:T(8,128)(2,1)S(1)}, bf16[8,32,128]{2,1,0:T(8,128)(2,1)S(1)}, u32[]{:S(2)}, u32[]{:S(2)}) %collective-permute-start.3) | collective-permute-done | bytes 65568 | tf_op jit(solution)/shard_map/ppermute | solution.py:382
  16.2 2.2 %collective-permute-start.5 = (bf16[128,2048]{1,0:T(8,128)(2,1)S(1)}, bf16[128,2048]{1,0:T(8,128)(2,1)S(1)}, u32[]{:S(2)}, u32[]{:S(2)}) collective-permute-start(bf16[128,2048]{1,0:T(8,128)(2,1)S(1)} %get-tuple-element.68), channel_id=1, source_target_pairs={{0,8},{4,12},{8,0},{12,4},{16,24},{20,28},{24,16},{28,20},{1,9},{5... | collective-permute-start | bytes 1572872 | tf_op jit(solution)/shard_map/ppermute | solution.py:377
  20.2 10.0 %all-gather = bf16[8,8,32,128]{3,2,1,0:T(8,128)(2,1)S(1)} all-gather(bf16[2,8,32,128]{3,2,1,0:T(8,128)(2,1)S(1)} %pad_maximum_fusion.1), channel_id=2, replica_groups=mesh['ctx'=8,'fsdp'=4] {'fsdp'}, dimensions={0}, use_global_device_ids=true | all-gather | bytes 655360 | tf_op jit(solution)/shard_map/all_gather | solution.py:425
  30.2 3.5 %states.3 = bf16[8,144,128]{2,1,0:T(8,128)(2,1)S(1)} custom-call(s32[49]{0:T(128)S(1)} %stack.194.table, bf16[128,512]{1,0:T(8,128)(2,1)S(1)} %get-tuple-element.61.refs_0_.refs_4_, bf16[128,512]{1,0:T(8,128)(2,1)S(1)} %collective-permute-done.refs_1_.refs_5_, bf16[128,512]{1,0:T(8,128)(2,1)S(1)} %collective-permute-done.1.refs_2_.refs_6_, ...), custom_call_target="tpu_custom_call" | custom-call | flops 1000 | bytes 1000 | tf_op jit(solution)/shard_map/states/pallas_call | solution.py:461
  33.9 3.5 %states.2.refs_0_ = bf16[8,144,128]{2,1,0:T(8,128)(2,1)S(1)} custom-call(s32[49]{0:T(128)S(1)} %stack.194.table, bf16[128,512]{1,0:T(8,128)(2,1)S(1)} %get-tuple-element.61.refs_0_.refs_4_, bf16[128,512]{1,0:T(8,128)(2,1)S(1)} %collective-permute-done.refs_1_.refs_5_, bf16[128,512]{1,0:T(8,128)(2,1)S(1)} %collective-permute-done.1.refs_2_.refs_6_, ...), custom_call_target="tpu_custom_call" | custom-call | flops 1000 | bytes 1000 | tf_op jit(solution)/shard_map/states/pallas_call | solution.py:461
  37.5 4.3 %collective-permute-done.6.refs_11_.refs_15_ = bf16[128,2048]{1,0:T(8,128)(2,1)S(1)} collective-permute-done((bf16[128,2048]{1,0:T(8,128)(2,1)S(1)}, bf16[128,2048]{1,0:T(8,128)(2,1)S(1)}, u32[]{:S(2)}, u32[]{:S(2)}) %collective-permute-start.6) | collective-permute-done | bytes 524320 | tf_op jit(solution)/shard_map/ppermute | solution.py:377
  41.7 4.1 %collective-permute-done.7.refs_1_ = bf16[8,144,128]{2,1,0:T(8,128)(2,1)S(1)} collective-permute-done((bf16[8,144,128]{2,1,0:T(8,128)(2,1)S(1)}, bf16[8,144,128]{2,1,0:T(8,128)(2,1)S(1)}, u32[]{:S(2)}, u32[]{:S(2)}) %collective-permute-start.7) | collective-permute-done | bytes 294944 | tf_op jit(solution)/shard_map/ppermute | solution.py:382
  46.5 4.7 %collective-permute-start.8 = (bf16[8,144,128]{2,1,0:T(8,128)(2,1)S(1)}, bf16[8,144,128]{2,1,0:T(8,128)(2,1)S(1)}, u32[]{:S(2)}, u32[]{:S(2)}) collective-permute-start(bf16[8,144,128]{2,1,0:T(8,128)(2,1)S(1)} %totals.4.refs_0_), channel_id=1, source_target_pairs={{0,1},{1,0},{2,3},{3,2},{4,5},{5,4},{6,7},{7,6},{8,9},{9,8},{10,11... | collective-permute-start | bytes 884744 | tf_op jit(solution)/shard_map/ppermute | solution.py:388
  53.2 8.2 %collective-permute-done.9.refs_3_ = bf16[8,144,128]{2,1,0:T(8,128)(2,1)S(1)} collective-permute-done((bf16[8,144,128]{2,1,0:T(8,128)(2,1)S(1)}, bf16[8,144,128]{2,1,0:T(8,128)(2,1)S(1)}, u32[]{:S(2)}, u32[]{:S(2)}) %collective-permute-start.9) | collective-permute-done | bytes 294944 | tf_op jit(solution)/shard_map/ppermute | solution.py:388
  67.2 11.0 %collective-permute-done.13.refs_17_ = bf16[8,144,128]{2,1,0:T(8,128)(2,1)S(1)} collective-permute-done((bf16[8,144,128]{2,1,0:T(8,128)(2,1)S(1)}, bf16[8,144,128]{2,1,0:T(8,128)(2,1)S(1)}, u32[]{:S(2)}, u32[]{:S(2)}) %collective-permute-start.13) | collective-permute-done | bytes 294944 | tf_op jit(solution)/shard_map/ppermute | solution.py:382
  79.0 16.6 %blocks.3 = (bf16[128,1024]{1,0:T(8,128)(2,1)}, bf16[128,1024]{1,0:T(8,128)(2,1)}, bf16[128,1024]{1,0:T(8,128)(2,1)}, bf16[128,1024]{1,0:T(8,128)(2,1)}, f32[8,1...) custom-call(s32[49]{0:T(128)} %copy-done.26, ...), custom_call_target="tpu_custom_call" | custom-call | flops 1000 | bytes 1000 | tf_op jit(solution)/shard_map/blocks/pallas_call | solution.py:461
  96.9 16.7 %blocks.2 = (bf16[128,1024]{1,0:T(8,128)(2,1)}, bf16[128,1024]{1,0:T(8,128)(2,1)}, bf16[128,1024]{1,0:T(8,128)(2,1)}, bf16[128,1024]{1,0:T(8,128)(2,1)}, f32[8,1...) custom-call(s32[49]{0:T(128)} %copy-done.26, ...), custom_call_target="tpu_custom_call" | custom-call | flops 1000 | bytes 1000 | tf_op jit(solution)/shard_map/blocks/pallas_call | solution.py:461
  122.2 3.9 %collective-permute-done.16.refs_3_ = bf16[8,144,128]{2,1,0:T(8,128)(2,1)S(1)} collective-permute-done((bf16[8,144,128]{2,1,0:T(8,128)(2,1)S(1)}, bf16[8,144,128]{2,1,0:T(8,128)(2,1)S(1)}, u32[]{:S(2)}, u32[]{:S(2)}) %collective-permute-start.16) | collective-permute-done | bytes 294944 | tf_op jit(solution)/shard_map/ppermute | solution.py:388
  127.7 2.6 %collective-permute-start.23 = (bf16[8,144,128]{2,1,0:T(8,128)(2,1)S(1)}, bf16[8,144,128]{2,1,0:T(8,128)(2,1)S(1)}, u32[]{:S(2)}, u32[]{:S(2)}) collective-permute-start(bf16[8,144,128]{2,1,0:T(8,128)(2,1)S(1)} %get-tuple-element.101), channel_id=1, source_target_pairs={{0,16},{4,20},{8,24},{12,28},{16,0},{20,4},{24,8},{28,12},{1,17},{... | collective-permute-start | bytes 884744 | tf_op jit(solution)/shard_map/ppermute | solution.py:382
  130.3 3.9 %collective-permute-done.17 = bf16[128,1024]{1,0:T(8,128)(2,1)S(1)} collective-permute-done((bf16[128,1024]{1,0:T(8,128)(2,1)S(1)}, bf16[128,1024]{1,0:T(8,128)(2,1)S(1)}, u32[]{:S(2)}, u32[]{:S(2)}) %collective-permute-start.17) | collective-permute-done | bytes 262176 | tf_op jit(solution)/shard_map/ppermute | solution.py:377
  135.9 5.5 %keys.2 = (bf16[4,128,512]{2,1,0:T(8,128)(2,1)}, bf16[4,128,128]{2,1,0:T(8,128)(2,1)S(1)}) custom-call(s32[49]{0:T(128)S(1)} %copy-done.27, bf16[128,512]{1,0:T(8,128)(2,1)S(1)} %copy-done.5, bf16[128,512]{1,0:T(8,128)(2,1)S(1)} %copy-done.7, bf16[128,512]{1,0:T(8,128)(2,1)S(1)} %copy-done.9, bf16[128,512]{1,0:T(8,128)(2,1)S(1)} %copy-done.11, ...), custom_call_target="tpu_custom_call" | custom-call | flops 1000 | bytes 1000 | tf_op jit(solution)/shard_map/keys/pallas_call | solution.py:461
  141.4 4.0 %collective-permute-start.22 = (bf16[128,1024]{1,0:T(8,128)(2,1)S(1)}, bf16[128,1024]{1,0:T(8,128)(2,1)S(1)}, u32[]{:S(2)}, u32[]{:S(2)}) collective-permute-start(bf16[128,1024]{1,0:T(8,128)(2,1)S(1)} %copy-done.41), channel_id=1, source_target_pairs={{0,4},{4,8},{8,12},{12,0},{16,20},{20,24},{24,28},{28,16},{1,5},{5... | collective-permute-start | bytes 786440 | tf_op jit(solution)/shard_map/ppermute | solution.py:377
  146.6 5.5 %keys.3 = (bf16[4,128,512]{2,1,0:T(8,128)(2,1)}, bf16[4,128,128]{2,1,0:T(8,128)(2,1)S(1)}) custom-call(s32[49]{0:T(128)S(1)} %copy-done.27, bf16[128,512]{1,0:T(8,128)(2,1)S(1)} %copy-done.5, bf16[128,512]{1,0:T(8,128)(2,1)S(1)} %copy-done.7, bf16[128,512]{1,0:T(8,128)(2,1)S(1)} %copy-done.9, ...), custom_call_target="tpu_custom_call", output_to_operand_aliasing={{0}: (13, {})} | custom-call | flops 1000 | bytes 1000 | tf_op jit(solution)/shard_map/keys/pallas_call | solution.py:461
  152.2 4.1 %collective-permute-done.20 = bf16[128,1024]{1,0:T(8,128)(2,1)S(1)} collective-permute-done((bf16[128,1024]{1,0:T(8,128)(2,1)S(1)}, bf16[128,1024]{1,0:T(8,128)(2,1)S(1)}, u32[]{:S(2)}, u32[]{:S(2)}) %collective-permute-start.20) | collective-permute-done | bytes 262176 | tf_op jit(solution)/shard_map/ppermute | solution.py:377
  156.2 3.7 %all-to-all-start = ((bf16[4,128,512]{2,1,0:T(8,128)(2,1)}), bf16[4,128,512]{2,1,0:T(8,128)(2,1)S(1)}, u32[]{:S(2)}, u32[]{:S(2)}) async-start(bf16[4,128,512]{2,1,0:T(8,128)(2,1)} %get-tuple-element.106), calls=%async_computation | async-start | bytes 1048576 | tf_op jit(solution)/shard_map/all_to_all | solution.py:374
  160.0 4.6 %collective-permute-start.27 = (bf16[2,4,32,128]{3,2,1,0:T(8,128)(2,1)S(1)}, bf16[2,4,32,128]{3,2,1,0:T(8,128)(2,1)S(1)}, u32[]{:S(2)}, u32[]{:S(2)}) collective-permute-start(bf16[2,4,32,128]{3,2,1,0:T(8,128)(2,1)S(1)} %get-tuple-element.117), channel_id=1, source_target_pairs={{0,16},{1,17},{2,18},{3,19},{4,20},{5,21},{6,22},{7,23},{8,24},{9,... | collective-permute-start | bytes 196616 | tf_op jit(solution)/shard_map/ppermute | solution.py:396
  165.5 4.2 %collective-permute-start.29 = (bf16[2,4,32,128]{3,2,1,0:T(8,128)(2,1)S(1)}, bf16[2,4,32,128]{3,2,1,0:T(8,128)(2,1)S(1)}, u32[]{:S(2)}, u32[]{:S(2)}) collective-permute-start(bf16[2,4,32,128]{3,2,1,0:T(8,128)(2,1)S(1)} %get-tuple-element.119), channel_id=1, source_target_pairs={{0,18},{1,19},{2,16},{3,17},{4,22},{5,23},{6,20},{7,21},{8,26},{9,... | collective-permute-start | bytes 196616 | tf_op jit(solution)/shard_map/ppermute | solution.py:396
  174.4 3.6 %collective-permute-done.29.refs_5_ = bf16[2,4,32,128]{3,2,1,0:T(8,128)(2,1)S(1)} collective-permute-done((bf16[2,4,32,128]{3,2,1,0:T(8,128)(2,1)S(1)}, bf16[2,4,32,128]{3,2,1,0:T(8,128)(2,1)S(1)}, u32[]{:S(2)}, u32[]{:S(2)}) %collective-permute-start.29) | collective-permute-done | bytes 65568 | tf_op jit(solution)/shard_map/ppermute | solution.py:396
  (157 shorter events, 45.1 us)
Async XLA Ops:
  4.2 9.5 %collective-permute-start = (bf16[128,512]{1,0:T(8,128)(2,1)S(1)}, bf16[128,512]{1,0:T(8,128)(2,1)S(1)}, u32[]{:S(2)}, u32[]{:S(2)}) collective-permute-start(bf16[128,512]{1,0:T(8,128)(2,1)S(1)} %get-tuple-element.62), channel_id=1, source_target_pairs={{0,4},{4,8},{8,12},{12,0},{16,20},{20,24},{24,28},{28,16},{1,5},{5... | collective-permute-start | bytes 393224 | tf_op jit(solution)/shard_map/ppermute | solution.py:377
  14.9 22.5 %collective-permute-start.4 = (bf16[128,2048]{1,0:T(8,128)(2,1)S(1)}, bf16[128,2048]{1,0:T(8,128)(2,1)S(1)}, u32[]{:S(2)}, u32[]{:S(2)}) collective-permute-start(bf16[128,2048]{1,0:T(8,128)(2,1)S(1)} %get-tuple-element.67), channel_id=1, source_target_pairs={{0,4},{4,8},{8,12},{12,0},{16,20},{20,24},{24,28},{28,16},{1,5},{5... | collective-permute-start | bytes 1572872 | tf_op jit(solution)/shard_map/ppermute | solution.py:377
  16.2 21.2 %collective-permute-start.5 = (bf16[128,2048]{1,0:T(8,128)(2,1)S(1)}, bf16[128,2048]{1,0:T(8,128)(2,1)S(1)}, u32[]{:S(2)}, u32[]{:S(2)}) collective-permute-start(bf16[128,2048]{1,0:T(8,128)(2,1)S(1)} %get-tuple-element.68), channel_id=1, source_target_pairs={{0,8},{4,12},{8,0},{12,4},{16,24},{20,28},{24,16},{28,20},{1,9},{5... | collective-permute-start | bytes 1572872 | tf_op jit(solution)/shard_map/ppermute | solution.py:377
  18.4 23.3 %collective-permute-start.6 = (bf16[128,2048]{1,0:T(8,128)(2,1)S(1)}, bf16[128,2048]{1,0:T(8,128)(2,1)S(1)}, u32[]{:S(2)}, u32[]{:S(2)}) collective-permute-start(bf16[128,2048]{1,0:T(8,128)(2,1)S(1)} %get-tuple-element.69), channel_id=1, source_target_pairs={{0,12},{4,0},{8,4},{12,8},{16,28},{20,16},{24,20},{28,24},{1,13},{... | collective-permute-start | bytes 1572872 | tf_op jit(solution)/shard_map/ppermute | solution.py:377
  33.8 12.1 %collective-permute-start.7 = (bf16[8,144,128]{2,1,0:T(8,128)(2,1)S(1)}, bf16[8,144,128]{2,1,0:T(8,128)(2,1)S(1)}, u32[]{:S(2)}, u32[]{:S(2)}) collective-permute-start(bf16[8,144,128]{2,1,0:T(8,128)(2,1)S(1)} %states.3), channel_id=1, source_target_pairs={{0,16},{4,20},{8,24},{12,28},{16,0},{20,4},{24,8},{28,12},{1,17},{... | collective-permute-start | bytes 884744 | tf_op jit(solution)/shard_map/ppermute | solution.py:382
  53.1 8.3 %collective-permute-start.9 = (bf16[8,144,128]{2,1,0:T(8,128)(2,1)S(1)}, bf16[8,144,128]{2,1,0:T(8,128)(2,1)S(1)}, u32[]{:S(2)}, u32[]{:S(2)}) collective-permute-start(bf16[8,144,128]{2,1,0:T(8,128)(2,1)S(1)} %totals.5), channel_id=1, source_target_pairs={{0,2},{1,3},{2,0},{3,1},{4,6},{5,7},{6,4},{7,5},{8,10},{9,11},{10,... | collective-permute-start | bytes 884744 | tf_op jit(solution)/shard_map/ppermute | solution.py:388
  62.2 16.0 %collective-permute-start.13 = (bf16[8,144,128]{2,1,0:T(8,128)(2,1)S(1)}, bf16[8,144,128]{2,1,0:T(8,128)(2,1)S(1)}, u32[]{:S(2)}, u32[]{:S(2)}) collective-permute-start(bf16[8,144,128]{2,1,0:T(8,128)(2,1)S(1)} %get-tuple-element.79), channel_id=1, source_target_pairs={{0,16},{4,20},{8,24},{12,28},{16,0},{20,4},{24,8},{28,12},{1,17},{... | collective-permute-start | bytes 884744 | tf_op jit(solution)/shard_map/ppermute | solution.py:382
  64.9 30.8 %collective-permute-start.10 = (bf16[128,2048]{1,0:T(8,128)(2,1)S(1)}, bf16[128,2048]{1,0:T(8,128)(2,1)S(1)}, u32[]{:S(2)}, u32[]{:S(2)}) collective-permute-start(bf16[128,2048]{1,0:T(8,128)(2,1)S(1)} %get-tuple-element.74), channel_id=1, source_target_pairs={{0,4},{4,8},{8,12},{12,0},{16,20},{20,24},{24,28},{28,16},{1,5},{5... | collective-permute-start | bytes 1572872 | tf_op jit(solution)/shard_map/ppermute | solution.py:377
  65.5 30.2 %collective-permute-start.11 = (bf16[128,2048]{1,0:T(8,128)(2,1)S(1)}, bf16[128,2048]{1,0:T(8,128)(2,1)S(1)}, u32[]{:S(2)}, u32[]{:S(2)}) collective-permute-start(bf16[128,2048]{1,0:T(8,128)(2,1)S(1)} %get-tuple-element.75), channel_id=1, source_target_pairs={{0,8},{4,12},{8,0},{12,4},{16,24},{20,28},{24,16},{28,20},{1,9},{5... | collective-permute-start | bytes 1572872 | tf_op jit(solution)/shard_map/ppermute | solution.py:377
  66.8 29.0 %collective-permute-start.12 = (bf16[128,2048]{1,0:T(8,128)(2,1)S(1)}, bf16[128,2048]{1,0:T(8,128)(2,1)S(1)}, u32[]{:S(2)}, u32[]{:S(2)}) collective-permute-start(bf16[128,2048]{1,0:T(8,128)(2,1)S(1)} %get-tuple-element.76), channel_id=1, source_target_pairs={{0,12},{4,0},{8,4},{12,8},{16,28},{20,16},{24,20},{28,24},{1,13},{... | collective-permute-start | bytes 1572872 | tf_op jit(solution)/shard_map/ppermute | solution.py:377
  95.6 18.0 %collective-permute-start.14 = (bf16[8,144,128]{2,1,0:T(8,128)(2,1)}, bf16[8,144,128]{2,1,0:T(8,128)(2,1)S(1)}, u32[]{:S(2)}, u32[]{:S(2)}) collective-permute-start(bf16[8,144,128]{2,1,0:T(8,128)(2,1)} %get-tuple-element.80), channel_id=1, source_target_pairs={{0,16},{4,20},{8,24},{12,28},{16,0},{20,4},{24,8},{28,12},{1,17},{... | collective-permute-start | bytes 884744 | tf_op jit(solution)/shard_map/ppermute | solution.py:382
  117.8 8.3 %collective-permute-start.16 = (bf16[8,144,128]{2,1,0:T(8,128)(2,1)S(1)}, bf16[8,144,128]{2,1,0:T(8,128)(2,1)S(1)}, u32[]{:S(2)}, u32[]{:S(2)}) collective-permute-start(bf16[8,144,128]{2,1,0:T(8,128)(2,1)S(1)} %totals.7), channel_id=1, source_target_pairs={{0,2},{1,3},{2,0},{3,1},{4,6},{5,7},{6,4},{7,5},{8,10},{9,11},{10,... | collective-permute-start | bytes 884744 | tf_op jit(solution)/shard_map/ppermute | solution.py:388
  118.5 11.9 %collective-permute-start.19 = (bf16[128,1024]{1,0:T(8,128)(2,1)S(1)}, bf16[128,1024]{1,0:T(8,128)(2,1)S(1)}, u32[]{:S(2)}, u32[]{:S(2)}) collective-permute-start(bf16[128,1024]{1,0:T(8,128)(2,1)S(1)} %copy-done.44), channel_id=1, source_target_pairs={{0,4},{4,8},{8,12},{12,0},{16,20},{20,24},{24,28},{28,16},{1,5},{5... | collective-permute-start | bytes 786440 | tf_op jit(solution)/shard_map/ppermute | solution.py:377
  120.5 9.9 %collective-permute-start.18 = (bf16[128,1024]{1,0:T(8,128)(2,1)S(1)}, bf16[128,1024]{1,0:T(8,128)(2,1)S(1)}, u32[]{:S(2)}, u32[]{:S(2)}) collective-permute-start(bf16[128,1024]{1,0:T(8,128)(2,1)S(1)} %copy-done.43), channel_id=1, source_target_pairs={{0,8},{4,12},{8,0},{12,4},{16,24},{20,28},{24,16},{28,20},{1,9},{5... | collective-permute-start | bytes 786440 | tf_op jit(solution)/shard_map/ppermute | solution.py:377
  122.1 12.1 %collective-permute-start.17 = (bf16[128,1024]{1,0:T(8,128)(2,1)S(1)}, bf16[128,1024]{1,0:T(8,128)(2,1)S(1)}, u32[]{:S(2)}, u32[]{:S(2)}) collective-permute-start(bf16[128,1024]{1,0:T(8,128)(2,1)S(1)} %copy-done.42), channel_id=1, source_target_pairs={{0,12},{4,0},{8,4},{12,8},{16,28},{20,16},{24,20},{28,24},{1,13},{... | collective-permute-start | bytes 786440 | tf_op jit(solution)/shard_map/ppermute | solution.py:377
  127.7 18.9 %collective-permute-start.23 = (bf16[8,144,128]{2,1,0:T(8,128)(2,1)S(1)}, bf16[8,144,128]{2,1,0:T(8,128)(2,1)S(1)}, u32[]{:S(2)}, u32[]{:S(2)}) collective-permute-start(bf16[8,144,128]{2,1,0:T(8,128)(2,1)S(1)} %get-tuple-element.101), channel_id=1, source_target_pairs={{0,16},{4,20},{8,24},{12,28},{16,0},{20,4},{24,8},{28,12},{1,17},{... | collective-permute-start | bytes 884744 | tf_op jit(solution)/shard_map/ppermute | solution.py:382
  141.4 10.8 %collective-permute-start.22 = (bf16[128,1024]{1,0:T(8,128)(2,1)S(1)}, bf16[128,1024]{1,0:T(8,128)(2,1)S(1)}, u32[]{:S(2)}, u32[]{:S(2)}) collective-permute-start(bf16[128,1024]{1,0:T(8,128)(2,1)S(1)} %copy-done.41), channel_id=1, source_target_pairs={{0,4},{4,8},{8,12},{12,0},{16,20},{20,24},{24,28},{28,16},{1,5},{5... | collective-permute-start | bytes 786440 | tf_op jit(solution)/shard_map/ppermute | solution.py:377
  145.4 10.9 %collective-permute-start.20 = (bf16[128,1024]{1,0:T(8,128)(2,1)S(1)}, bf16[128,1024]{1,0:T(8,128)(2,1)S(1)}, u32[]{:S(2)}, u32[]{:S(2)}) collective-permute-start(bf16[128,1024]{1,0:T(8,128)(2,1)S(1)} %copy-done.39), channel_id=1, source_target_pairs={{0,12},{4,0},{8,4},{12,8},{16,28},{20,16},{24,20},{28,24},{1,13},{... | collective-permute-start | bytes 786440 | tf_op jit(solution)/shard_map/ppermute | solution.py:377
  156.2 24.2 %all-to-all-start = ((bf16[4,128,512]{2,1,0:T(8,128)(2,1)}), bf16[4,128,512]{2,1,0:T(8,128)(2,1)S(1)}, u32[]{:S(2)}, u32[]{:S(2)}) async-start(bf16[4,128,512]{2,1,0:T(8,128)(2,1)} %get-tuple-element.106), calls=%async_computation | async-start | bytes 1048576 | tf_op jit(solution)/shard_map/all_to_all | solution.py:374
  160.0 11.0 %collective-permute-start.27 = (bf16[2,4,32,128]{3,2,1,0:T(8,128)(2,1)S(1)}, bf16[2,4,32,128]{3,2,1,0:T(8,128)(2,1)S(1)}, u32[]{:S(2)}, u32[]{:S(2)}) collective-permute-start(bf16[2,4,32,128]{3,2,1,0:T(8,128)(2,1)S(1)} %get-tuple-element.117), channel_id=1, source_target_pairs={{0,16},{1,17},{2,18},{3,19},{4,20},{5,21},{6,22},{7,23},{8,24},{9,... | collective-permute-start | bytes 196616 | tf_op jit(solution)/shard_map/ppermute | solution.py:396
  165.5 12.4 %collective-permute-start.29 = (bf16[2,4,32,128]{3,2,1,0:T(8,128)(2,1)S(1)}, bf16[2,4,32,128]{3,2,1,0:T(8,128)(2,1)S(1)}, u32[]{:S(2)}, u32[]{:S(2)}) collective-permute-start(bf16[2,4,32,128]{3,2,1,0:T(8,128)(2,1)S(1)} %get-tuple-element.119), channel_id=1, source_target_pairs={{0,18},{1,19},{2,16},{3,17},{4,22},{5,23},{6,20},{7,21},{8,26},{9,... | collective-permute-start | bytes 196616 | tf_op jit(solution)/shard_map/ppermute | solution.py:396
  169.8 9.2 %collective-permute-start.30 = (bf16[2,4,32,128]{3,2,1,0:T(8,128)(2,1)S(1)}, bf16[2,4,32,128]{3,2,1,0:T(8,128)(2,1)S(1)}, u32[]{:S(2)}, u32[]{:S(2)}) collective-permute-start(bf16[2,4,32,128]{3,2,1,0:T(8,128)(2,1)S(1)} %get-tuple-element.116), channel_id=1, source_target_pairs={{0,19},{1,16},{2,17},{3,18},{4,23},{5,20},{6,21},{7,22},{8,27},{9,... | collective-permute-start | bytes 196616 | tf_op jit(solution)/shard_map/ppermute | solution.py:396
  169.8 9.2 %collective-permute-start.24 = (bf16[2,4,32,128]{3,2,1,0:T(8,128)(2,1)S(1)}, bf16[2,4,32,128]{3,2,1,0:T(8,128)(2,1)S(1)}, u32[]{:S(2)}, u32[]{:S(2)}) collective-permute-start(bf16[2,4,32,128]{3,2,1,0:T(8,128)(2,1)S(1)} %get-tuple-element.122), channel_id=1, source_target_pairs={{0,1},{1,2},{2,3},{3,0},{4,5},{5,6},{6,7},{7,4},{8,9},{9,10},{10,1... | collective-permute-start | bytes 196616 | tf_op jit(solution)/shard_map/ppermute | solution.py:385
  171.1 7.9 %collective-permute-start.25 = (bf16[2,4,32,128]{3,2,1,0:T(8,128)(2,1)S(1)}, bf16[2,4,32,128]{3,2,1,0:T(8,128)(2,1)S(1)}, u32[]{:S(2)}, u32[]{:S(2)}) collective-permute-start(bf16[2,4,32,128]{3,2,1,0:T(8,128)(2,1)S(1)} %get-tuple-element.121), channel_id=1, source_target_pairs={{0,2},{1,3},{2,0},{3,1},{4,6},{5,7},{6,4},{7,5},{8,10},{9,11},{10,... | collective-permute-start | bytes 196616 | tf_op jit(solution)/shard_map/ppermute | solution.py:385
  (53 other events, 738.5 us)

commit v11 on v10

--- a/solution.py
+++ b/solution.py
@@ -30,7 +30,7 @@
 
 
 def turned(array):
-    return array.astype(F32).T.astype(array.dtype)
+    return array.T
 
 
 def column(row, width):
@@ -203,7 +203,7 @@
         state = st_ref[u, :hd, :]
         state_turned = turned(state)
         norm = column(whole_row(st_ref[u, hd:, :]), TILE)
-        g_turned = g_all[:, lanes].astype(F32).T
+        g_turned = g_all[:, lanes].T.astype(F32)
         back = []
         dkey = [jnp.zeros((2 * half, TILE), F32) for _ in range(BLK // TILE)]
         dvalue = [jnp.zeros((hd, TILE), F32) for _ in range(BLK // TILE)]
@@ -511,8 +511,7 @@
 
     partial = {s: states_of(s) for s in order}
     parts = [partial[0]] + [across(partial[s], s) for s in slots[1:]]
-    rows = {order[0]: sent_rows(order[0], near_maps, *kv)}
-    parts[0] = after(parts[0], *rows[order[0]])
+    rows = {order[0]: sent_rows(order[0], partial[order[0]])}
     others = around_all(totals_of(parts))
     state, _ = spread(parts, others, "before", [prefix_state, prefix_norm], False)
     for s in order[1:]:
@@ -585,7 +584,7 @@
             moved += [along(rows_for(two, seq + r), r) for r in range(1, fsdp)]
             returned[s] = brought_back(s, key_gm[s])
 
-    pairs = within(after(pairs, *returned[0]))
+    pairs = within(pairs)
     back = [piece[None] for s in slots for piece in returned[s]]
     (grad_queries,) = unpack(table, base["back"], back, 1, 1, heads * hd)
     grad_keys, grad_values = unpack(table, base["owner"], [pairs], grp, 2, hd)

time: 182 us -> 201 us (1.10)
  starting transfers between devices: 49.2 us -> 71 us
    ppermute x15, starting transfers between devices: 21.2 us -> 31.3 us  [around(): lax.ppermute(array, 'ctx', [(d, d // part * part + (d + shift) % part) fo...]
    ppermute x15, waiting for transfers between devices: 12.2 us -> 20.2 us  [around(): lax.ppermute(array, 'ctx', [(d, d // part * part + (d + shift) % part) fo...]
    ppermute x4, starting transfers between devices: 9.71 us -> 16.9 us  [apart(): return lax.ppermute(array, ('ctx', 'fsdp'), moves)]
    ppermute x5, starting transfers between devices: 5.9 us -> 12.6 us  [across(): lax.ppermute(array, 'ctx', [(d, (d + shift * part) % ctx) for d in range(...]
    ppermute x5, waiting for transfers between devices: 17.5 us -> 12.5 us  [across(): lax.ppermute(array, 'ctx', [(d, (d + shift * part) % ctx) for d in range(...]
    ppermute x4, waiting for transfers between devices: 4.65 us -> 0.44 us  [apart(): return lax.ppermute(array, ('ctx', 'fsdp'), moves)]
    ppermute x4, starting transfers between devices: 6.01 us -> 2.6 us  [twin(): return lax.ppermute(array, 'fsdp', [(d, d ^ bit) for d in range(fsdp)])]
    all_to_all x1, starting transfers between devices: 3.74 us -> 5.97 us  [within(): lax.all_to_all(array, 'ctx', 0, 0, axis_index_groups=blocks_of, tiled=True)]
  transfers between devices with their start and end apart: 32 -> 32, of which waited for: 12 -> 13; matrix products, arithmetic and copies ran while one was open for 0% -> 0% of each run, Pallas kernels for 31% -> 24%
where the time goes in v11:
time: 201 us
  starting transfers between devices  71 us (35%)
  Pallas kernels  62.6 us (31%)
  waiting for transfers between devices  49.4 us (25%)
  blocking collectives  9.03 us (4%)
  local copies, waits for them, and re-layouts  7.27 us (4%)
    pallas_call x6, Pallas kernels, call(): pl.pallas_call(functools.partial(kernel, part, base['sorted']), out_shape...  49.5 us
    ppermute x15, starting transfers between devices, around(): lax.ppermute(array, 'ctx', [(d, d // part * part + (d + shift) % part) fo...  31.3 us
    ppermute x15, waiting for transfers between devices, around(): lax.ppermute(array, 'ctx', [(d, d // part * part + (d + shift) % part) fo...  20.2 us
    ppermute x4, starting transfers between devices, apart(): return lax.ppermute(array, ('ctx', 'fsdp'), moves)  16.9 us
    ppermute x4, waiting for transfers between devices, twin(): return lax.ppermute(array, 'fsdp', [(d, d ^ bit) for d in range(fsdp)])  14.3 us
    ppermute x5, starting transfers between devices, across(): lax.ppermute(array, 'ctx', [(d, (d + shift * part) % ctx) for d in range(...  12.6 us
    ppermute x5, waiting for transfers between devices, across(): lax.ppermute(array, 'ctx', [(d, (d + shift * part) % ctx) for d in range(...  12.5 us
    all_gather x1, blocking collectives, shards(): maps = lax.all_gather(near_maps, 'fsdp')  9.03 us
  transfers between devices with their start and end apart: 32, of which 13 were waited for; matrix products, arithmetic and copies ran while one was open for 0% of the time, Pallas kernels for 24%

profile of v11, /device:TPU:1, one launch (start us, length us, event | category | flops | bytes accessed | tf_op | source)
XLA Modules:
  0.0 201.0 jit_solution(10964525852270375568)
XLA Ops:
  8.8 2.4 %collective-permute-start.3 = (bf16[8,32,128]{2,1,0:T(8,128)(2,1)S(1)}, bf16[8,32,128]{2,1,0:T(8,128)(2,1)S(1)}, u32[]{:S(2)}, u32[]{:S(2)}) collective-permute-start(bf16[8,32,128]{2,1,0:T(8,128)(2,1)S(1)} %pad_maximum_fusion.2), channel_id=1, source_target_pairs={{0,16},{4,20},{8,24},{12,28},{16,0},{20,4},{24,8},{28,12},{1,17},{... | collective-permute-start | bytes 196616 | tf_op jit(solution)/shard_map/ppermute | solution.py:382
  11.3 2.4 %collective-permute-done.3 = bf16[8,32,128]{2,1,0:T(8,128)(2,1)S(1)} collective-permute-done((bf16[8,32,128]{2,1,0:T(8,128)(2,1)S(1)}, bf16[8,32,128]{2,1,0:T(8,128)(2,1)S(1)}, u32[]{:S(2)}, u32[]{:S(2)}) %collective-permute-start.3) | collective-permute-done | bytes 65568 | tf_op jit(solution)/shard_map/ppermute | solution.py:382
  13.7 9.0 %all-gather = bf16[8,8,32,128]{3,2,1,0:T(8,128)(2,1)S(1)} all-gather(bf16[2,8,32,128]{3,2,1,0:T(8,128)(2,1)S(1)} %pad_maximum_fusion.1), channel_id=2, replica_groups=mesh['ctx'=8,'fsdp'=4] {'fsdp'}, dimensions={0}, use_global_device_ids=true | all-gather | bytes 655360 | tf_op jit(solution)/shard_map/all_gather | solution.py:425
  22.8 3.4 %states.3 = bf16[8,144,128]{2,1,0:T(8,128)(2,1)S(1)} custom-call(s32[49]{0:T(128)S(1)} %stack.194.table, bf16[128,512]{1,0:T(8,128)(2,1)S(1)} %get-tuple-element.59.refs_0_.refs_4_, bf16[128,512]{1,0:T(8,128)(2,1)S(1)} %collective-permute-done.refs_1_.refs_5_, bf16[128,512]{1,0:T(8,128)(2,1)S(1)} %collective-permute-done.1.refs_2_.refs_6_, ...), custom_call_target="tpu_custom_call" | custom-call | flops 1000 | bytes 1000 | tf_op jit(solution)/shard_map/states/pallas_call | solution.py:461
  26.2 3.0 %collective-permute-start.4 = (bf16[8,144,128]{2,1,0:T(8,128)(2,1)S(1)}, bf16[8,144,128]{2,1,0:T(8,128)(2,1)S(1)}, u32[]{:S(2)}, u32[]{:S(2)}) collective-permute-start(bf16[8,144,128]{2,1,0:T(8,128)(2,1)S(1)} %states.3), channel_id=1, source_target_pairs={{0,16},{4,20},{8,24},{12,28},{16,0},{20,4},{24,8},{28,12},{1,17},{... | collective-permute-start | bytes 884744 | tf_op jit(solution)/shard_map/ppermute | solution.py:382
  29.2 3.4 %states.2.refs_0_ = bf16[8,144,128]{2,1,0:T(8,128)(2,1)S(1)} custom-call(s32[49]{0:T(128)S(1)} %stack.194.table, bf16[128,512]{1,0:T(8,128)(2,1)S(1)} %get-tuple-element.59.refs_0_.refs_4_, bf16[128,512]{1,0:T(8,128)(2,1)S(1)} %collective-permute-done.refs_1_.refs_5_, bf16[128,512]{1,0:T(8,128)(2,1)S(1)} %collective-permute-done.1.refs_2_.refs_6_, ...), custom_call_target="tpu_custom_call" | custom-call | flops 1000 | bytes 1000 | tf_op jit(solution)/shard_map/states/pallas_call | solution.py:461
  32.6 10.1 %collective-permute-done.4.refs_1_ = bf16[8,144,128]{2,1,0:T(8,128)(2,1)S(1)} collective-permute-done((bf16[8,144,128]{2,1,0:T(8,128)(2,1)S(1)}, bf16[8,144,128]{2,1,0:T(8,128)(2,1)S(1)}, u32[]{:S(2)}, u32[]{:S(2)}) %collective-permute-start.4) | collective-permute-done | bytes 294944 | tf_op jit(solution)/shard_map/ppermute | solution.py:382
  49.0 5.4 %collective-permute-done.6.refs_3_ = bf16[8,144,128]{2,1,0:T(8,128)(2,1)S(1)} collective-permute-done((bf16[8,144,128]{2,1,0:T(8,128)(2,1)S(1)}, bf16[8,144,128]{2,1,0:T(8,128)(2,1)S(1)}, u32[]{:S(2)}, u32[]{:S(2)}) %collective-permute-start.6) | collective-permute-done | bytes 294944 | tf_op jit(solution)/shard_map/ppermute | solution.py:388
  55.3 2.4 %collective-permute-start.13 = (bf16[8,144,128]{2,1,0:T(8,128)(2,1)S(1)}, bf16[8,144,128]{2,1,0:T(8,128)(2,1)S(1)}, u32[]{:S(2)}, u32[]{:S(2)}) collective-permute-start(bf16[8,144,128]{2,1,0:T(8,128)(2,1)S(1)} %get-tuple-element.76), channel_id=1, source_target_pairs={{0,16},{4,20},{8,24},{12,28},{16,0},{20,4},{24,8},{28,12},{1,17},{... | collective-permute-start | bytes 884744 | tf_op jit(solution)/shard_map/ppermute | solution.py:382
  62.0 14.7 %collective-permute-start.9 = (bf16[128,2048]{1,0:T(8,128)(2,1)S(1)}, bf16[128,2048]{1,0:T(8,128)(2,1)S(1)}, u32[]{:S(2)}, u32[]{:S(2)}) collective-permute-start(bf16[128,2048]{1,0:T(8,128)(2,1)S(1)} %get-tuple-element.68), channel_id=1, source_target_pairs={{0,12},{4,0},{8,4},{12,8},{16,28},{20,16},{24,20},{28,24},{1,13},{... | collective-permute-start | bytes 1572872 | tf_op jit(solution)/shard_map/ppermute | solution.py:377
  77.6 15.9 %blocks.3 = (bf16[128,1024]{1,0:T(8,128)(2,1)}, bf16[128,1024]{1,0:T(8,128)(2,1)}, bf16[128,1024]{1,0:T(8,128)(2,1)}, bf16[128,1024]{1,0:T(8,128)(2,1)}, f32[8,1...) custom-call(s32[49]{0:T(128)} %copy-done.26, ...), custom_call_target="tpu_custom_call" | custom-call | flops 1000 | bytes 1000 | tf_op jit(solution)/shard_map/blocks/pallas_call | solution.py:461
  93.6 3.3 %collective-permute-start.14 = (bf16[8,144,128]{2,1,0:T(8,128)(2,1)}, bf16[8,144,128]{2,1,0:T(8,128)(2,1)S(1)}, u32[]{:S(2)}, u32[]{:S(2)}) collective-permute-start(bf16[8,144,128]{2,1,0:T(8,128)(2,1)} %get-tuple-element.77), channel_id=1, source_target_pairs={{0,16},{4,20},{8,24},{12,28},{16,0},{20,4},{24,8},{28,12},{1,17},{... | collective-permute-start | bytes 884744 | tf_op jit(solution)/shard_map/ppermute | solution.py:382
  96.9 3.4 %collective-permute-done.9.refs_11_.refs_15_ = bf16[128,2048]{1,0:T(8,128)(2,1)S(1)} collective-permute-done((bf16[128,2048]{1,0:T(8,128)(2,1)S(1)}, bf16[128,2048]{1,0:T(8,128)(2,1)S(1)}, u32[]{:S(2)}, u32[]{:S(2)}) %collective-permute-start.9) | collective-permute-done | bytes 524320 | tf_op jit(solution)/shard_map/ppermute | solution.py:377
  101.0 16.0 %blocks.2 = (bf16[128,1024]{1,0:T(8,128)(2,1)}, bf16[128,1024]{1,0:T(8,128)(2,1)}, bf16[128,1024]{1,0:T(8,128)(2,1)}, bf16[128,1024]{1,0:T(8,128)(2,1)}, f32[8,1...) custom-call(s32[49]{0:T(128)} %copy-done.26, ...), custom_call_target="tpu_custom_call" | custom-call | flops 1000 | bytes 1000 | tf_op jit(solution)/shard_map/blocks/pallas_call | solution.py:461
  121.9 7.7 %collective-permute-done.16.refs_3_ = bf16[8,144,128]{2,1,0:T(8,128)(2,1)S(1)} collective-permute-done((bf16[8,144,128]{2,1,0:T(8,128)(2,1)S(1)}, bf16[8,144,128]{2,1,0:T(8,128)(2,1)S(1)}, u32[]{:S(2)}, u32[]{:S(2)}) %collective-permute-start.16) | collective-permute-done | bytes 294944 | tf_op jit(solution)/shard_map/ppermute | solution.py:388
  133.6 2.5 %collective-permute-start.18 = (bf16[128,1024]{1,0:T(8,128)(2,1)S(1)}, bf16[128,1024]{1,0:T(8,128)(2,1)S(1)}, u32[]{:S(2)}, u32[]{:S(2)}) collective-permute-start(bf16[128,1024]{1,0:T(8,128)(2,1)S(1)} %copy-done.43), channel_id=1, source_target_pairs={{0,8},{4,12},{8,0},{12,4},{16,24},{20,28},{24,16},{28,20},{1,9},{5... | collective-permute-start | bytes 786440 | tf_op jit(solution)/shard_map/ppermute | solution.py:377
  136.2 5.0 %collective-permute-done.19 = bf16[128,1024]{1,0:T(8,128)(2,1)S(1)} collective-permute-done((bf16[128,1024]{1,0:T(8,128)(2,1)S(1)}, bf16[128,1024]{1,0:T(8,128)(2,1)S(1)}, u32[]{:S(2)}, u32[]{:S(2)}) %collective-permute-start.19) | collective-permute-done | bytes 262176 | tf_op jit(solution)/shard_map/ppermute | solution.py:377
  143.5 5.6 %collective-permute-done.17 = bf16[128,1024]{1,0:T(8,128)(2,1)S(1)} collective-permute-done((bf16[128,1024]{1,0:T(8,128)(2,1)S(1)}, bf16[128,1024]{1,0:T(8,128)(2,1)S(1)}, u32[]{:S(2)}, u32[]{:S(2)}) %collective-permute-start.17) | collective-permute-done | bytes 262176 | tf_op jit(solution)/shard_map/ppermute | solution.py:377
  150.8 5.3 %keys.2 = (bf16[4,128,512]{2,1,0:T(8,128)(2,1)}, bf16[4,128,128]{2,1,0:T(8,128)(2,1)S(1)}) custom-call(s32[49]{0:T(128)S(1)} %copy-done.27, bf16[128,512]{1,0:T(8,128)(2,1)S(1)} %copy-done.5, bf16[128,512]{1,0:T(8,128)(2,1)S(1)} %copy-done.7, bf16[128,512]{1,0:T(8,128)(2,1)S(1)} %copy-done.9, bf16[128,512]{1,0:T(8,128)(2,1)S(1)} %copy-done.11, ...), custom_call_target="tpu_custom_call" | custom-call | flops 1000 | bytes 1000 | tf_op jit(solution)/shard_map/keys/pallas_call | solution.py:461
  156.2 5.3 %keys.3 = (bf16[4,128,512]{2,1,0:T(8,128)(2,1)}, bf16[4,128,128]{2,1,0:T(8,128)(2,1)S(1)}) custom-call(s32[49]{0:T(128)S(1)} %copy-done.27, bf16[128,512]{1,0:T(8,128)(2,1)S(1)} %copy-done.5, bf16[128,512]{1,0:T(8,128)(2,1)S(1)} %copy-done.7, bf16[128,512]{1,0:T(8,128)(2,1)S(1)} %copy-done.9, ...), custom_call_target="tpu_custom_call", output_to_operand_aliasing={{0}: (13, {})} | custom-call | flops 1000 | bytes 1000 | tf_op jit(solution)/shard_map/keys/pallas_call | solution.py:461
  161.5 6.0 %all-to-all-start = ((bf16[4,128,512]{2,1,0:T(8,128)(2,1)}), bf16[4,128,512]{2,1,0:T(8,128)(2,1)S(1)}, u32[]{:S(2)}, u32[]{:S(2)}) async-start(bf16[4,128,512]{2,1,0:T(8,128)(2,1)} %get-tuple-element.102), calls=%async_computation | async-start | bytes 1048576 | tf_op jit(solution)/shard_map/all_to_all | solution.py:374
  172.7 5.4 %collective-permute-start.28 = (bf16[2,4,32,128]{3,2,1,0:T(8,128)(2,1)S(1)}, bf16[2,4,32,128]{3,2,1,0:T(8,128)(2,1)S(1)}, u32[]{:S(2)}, u32[]{:S(2)}) collective-permute-start(bf16[2,4,32,128]{3,2,1,0:T(8,128)(2,1)S(1)} %get-tuple-element.114), channel_id=1, source_target_pairs={{0,17},{1,18},{2,19},{3,16},{4,21},{5,22},{6,23},{7,20},{8,25},{9,... | collective-permute-start | bytes 196616 | tf_op jit(solution)/shard_map/ppermute | solution.py:396
  178.1 3.9 %collective-permute-done.22 = bf16[128,1024]{1,0:T(8,128)(2,1)S(1)} collective-permute-done((bf16[128,1024]{1,0:T(8,128)(2,1)S(1)}, bf16[128,1024]{1,0:T(8,128)(2,1)S(1)}, u32[]{:S(2)}, u32[]{:S(2)}) %collective-permute-start.22) | collective-permute-done | bytes 262176 | tf_op jit(solution)/shard_map/ppermute | solution.py:377
  182.0 10.2 %collective-permute-start.30 = (bf16[2,4,32,128]{3,2,1,0:T(8,128)(2,1)S(1)}, bf16[2,4,32,128]{3,2,1,0:T(8,128)(2,1)S(1)}, u32[]{:S(2)}, u32[]{:S(2)}) collective-permute-start(bf16[2,4,32,128]{3,2,1,0:T(8,128)(2,1)S(1)} %get-tuple-element.112), channel_id=1, source_target_pairs={{0,19},{1,16},{2,17},{3,18},{4,23},{5,20},{6,21},{7,22},{8,27},{9,... | collective-permute-start | bytes 196616 | tf_op jit(solution)/shard_map/ppermute | solution.py:396
  (157 shorter events, 47.9 us)
Async XLA Ops:
  4.2 18.5 %collective-permute-start = (bf16[128,512]{1,0:T(8,128)(2,1)S(1)}, bf16[128,512]{1,0:T(8,128)(2,1)S(1)}, u32[]{:S(2)}, u32[]{:S(2)}) collective-permute-start(bf16[128,512]{1,0:T(8,128)(2,1)S(1)} %get-tuple-element.60), channel_id=1, source_target_pairs={{0,4},{4,8},{8,12},{12,0},{16,20},{20,24},{24,28},{28,16},{1,5},{5... | collective-permute-start | bytes 393224 | tf_op jit(solution)/shard_map/ppermute | solution.py:377
  6.3 16.4 %collective-permute-start.1 = (bf16[128,512]{1,0:T(8,128)(2,1)S(1)}, bf16[128,512]{1,0:T(8,128)(2,1)S(1)}, u32[]{:S(2)}, u32[]{:S(2)}) collective-permute-start(bf16[128,512]{1,0:T(8,128)(2,1)S(1)} %get-tuple-element.61), channel_id=1, source_target_pairs={{0,8},{4,12},{8,0},{12,4},{16,24},{20,28},{24,16},{28,20},{1,9},{5... | collective-permute-start | bytes 393224 | tf_op jit(solution)/shard_map/ppermute | solution.py:377
  7.6 15.1 %collective-permute-start.2 = (bf16[128,512]{1,0:T(8,128)(2,1)S(1)}, bf16[128,512]{1,0:T(8,128)(2,1)S(1)}, u32[]{:S(2)}, u32[]{:S(2)}) collective-permute-start(bf16[128,512]{1,0:T(8,128)(2,1)S(1)} %get-tuple-element.62), channel_id=1, source_target_pairs={{0,12},{4,0},{8,4},{12,8},{16,28},{20,16},{24,20},{28,24},{1,13},{... | collective-permute-start | bytes 393224 | tf_op jit(solution)/shard_map/ppermute | solution.py:377
  26.2 16.6 %collective-permute-start.4 = (bf16[8,144,128]{2,1,0:T(8,128)(2,1)S(1)}, bf16[8,144,128]{2,1,0:T(8,128)(2,1)S(1)}, u32[]{:S(2)}, u32[]{:S(2)}) collective-permute-start(bf16[8,144,128]{2,1,0:T(8,128)(2,1)S(1)} %states.3), channel_id=1, source_target_pairs={{0,16},{4,20},{8,24},{12,28},{16,0},{20,4},{24,8},{28,12},{1,17},{... | collective-permute-start | bytes 884744 | tf_op jit(solution)/shard_map/ppermute | solution.py:382
  45.4 15.5 %collective-permute-start.10 = (bf16[128,2048]{1,0:T(8,128)(2,1)S(1)}, bf16[128,2048]{1,0:T(8,128)(2,1)S(1)}, u32[]{:S(2)}, u32[]{:S(2)}) collective-permute-start(bf16[128,2048]{1,0:T(8,128)(2,1)S(1)} %get-tuple-element.73), channel_id=1, source_target_pairs={{0,4},{4,8},{8,12},{12,0},{16,20},{20,24},{24,28},{28,16},{1,5},{5... | collective-permute-start | bytes 1572872 | tf_op jit(solution)/shard_map/ppermute | solution.py:377
  45.4 16.6 %collective-permute-start.11 = (bf16[128,2048]{1,0:T(8,128)(2,1)S(1)}, bf16[128,2048]{1,0:T(8,128)(2,1)S(1)}, u32[]{:S(2)}, u32[]{:S(2)}) collective-permute-start(bf16[128,2048]{1,0:T(8,128)(2,1)S(1)} %get-tuple-element.74), channel_id=1, source_target_pairs={{0,8},{4,12},{8,0},{12,4},{16,24},{20,28},{24,16},{28,20},{1,9},{5... | collective-permute-start | bytes 1572872 | tf_op jit(solution)/shard_map/ppermute | solution.py:377
  46.8 29.9 %collective-permute-start.12 = (bf16[128,2048]{1,0:T(8,128)(2,1)S(1)}, bf16[128,2048]{1,0:T(8,128)(2,1)S(1)}, u32[]{:S(2)}, u32[]{:S(2)}) collective-permute-start(bf16[128,2048]{1,0:T(8,128)(2,1)S(1)} %get-tuple-element.75), channel_id=1, source_target_pairs={{0,12},{4,0},{8,4},{12,8},{16,28},{20,16},{24,20},{28,24},{1,13},{... | collective-permute-start | bytes 1572872 | tf_op jit(solution)/shard_map/ppermute | solution.py:377
  55.3 21.4 %collective-permute-start.13 = (bf16[8,144,128]{2,1,0:T(8,128)(2,1)S(1)}, bf16[8,144,128]{2,1,0:T(8,128)(2,1)S(1)}, u32[]{:S(2)}, u32[]{:S(2)}) collective-permute-start(bf16[8,144,128]{2,1,0:T(8,128)(2,1)S(1)} %get-tuple-element.76), channel_id=1, source_target_pairs={{0,16},{4,20},{8,24},{12,28},{16,0},{20,4},{24,8},{28,12},{1,17},{... | collective-permute-start | bytes 884744 | tf_op jit(solution)/shard_map/ppermute | solution.py:382
  59.6 37.3 %collective-permute-start.7 = (bf16[128,2048]{1,0:T(8,128)(2,1)S(1)}, bf16[128,2048]{1,0:T(8,128)(2,1)S(1)}, u32[]{:S(2)}, u32[]{:S(2)}) collective-permute-start(bf16[128,2048]{1,0:T(8,128)(2,1)S(1)} %get-tuple-element.66), channel_id=1, source_target_pairs={{0,4},{4,8},{8,12},{12,0},{16,20},{20,24},{24,28},{28,16},{1,5},{5... | collective-permute-start | bytes 1572872 | tf_op jit(solution)/shard_map/ppermute | solution.py:377
  60.9 36.0 %collective-permute-start.8 = (bf16[128,2048]{1,0:T(8,128)(2,1)S(1)}, bf16[128,2048]{1,0:T(8,128)(2,1)S(1)}, u32[]{:S(2)}, u32[]{:S(2)}) collective-permute-start(bf16[128,2048]{1,0:T(8,128)(2,1)S(1)} %get-tuple-element.67), channel_id=1, source_target_pairs={{0,8},{4,12},{8,0},{12,4},{16,24},{20,28},{24,16},{28,20},{1,9},{5... | collective-permute-start | bytes 1572872 | tf_op jit(solution)/shard_map/ppermute | solution.py:377
  62.0 38.2 %collective-permute-start.9 = (bf16[128,2048]{1,0:T(8,128)(2,1)S(1)}, bf16[128,2048]{1,0:T(8,128)(2,1)S(1)}, u32[]{:S(2)}, u32[]{:S(2)}) collective-permute-start(bf16[128,2048]{1,0:T(8,128)(2,1)S(1)} %get-tuple-element.68), channel_id=1, source_target_pairs={{0,12},{4,0},{8,4},{12,8},{16,28},{20,16},{24,20},{28,24},{1,13},{... | collective-permute-start | bytes 1572872 | tf_op jit(solution)/shard_map/ppermute | solution.py:377
  93.6 23.6 %collective-permute-start.14 = (bf16[8,144,128]{2,1,0:T(8,128)(2,1)}, bf16[8,144,128]{2,1,0:T(8,128)(2,1)S(1)}, u32[]{:S(2)}, u32[]{:S(2)}) collective-permute-start(bf16[8,144,128]{2,1,0:T(8,128)(2,1)} %get-tuple-element.77), channel_id=1, source_target_pairs={{0,16},{4,20},{8,24},{12,28},{16,0},{20,4},{24,8},{28,12},{1,17},{... | collective-permute-start | bytes 884744 | tf_op jit(solution)/shard_map/ppermute | solution.py:382
  131.1 25.0 %collective-permute-start.23 = (bf16[8,144,128]{2,1,0:T(8,128)(2,1)S(1)}, bf16[8,144,128]{2,1,0:T(8,128)(2,1)S(1)}, u32[]{:S(2)}, u32[]{:S(2)}) collective-permute-start(bf16[8,144,128]{2,1,0:T(8,128)(2,1)S(1)} %get-tuple-element.98), channel_id=1, source_target_pairs={{0,16},{4,20},{8,24},{12,28},{16,0},{20,4},{24,8},{28,12},{1,17},{... | collective-permute-start | bytes 884744 | tf_op jit(solution)/shard_map/ppermute | solution.py:382
  132.7 8.5 %collective-permute-start.19 = (bf16[128,1024]{1,0:T(8,128)(2,1)S(1)}, bf16[128,1024]{1,0:T(8,128)(2,1)S(1)}, u32[]{:S(2)}, u32[]{:S(2)}) collective-permute-start(bf16[128,1024]{1,0:T(8,128)(2,1)S(1)} %copy-done.44), channel_id=1, source_target_pairs={{0,4},{4,8},{8,12},{12,0},{16,20},{20,24},{24,28},{28,16},{1,5},{5... | collective-permute-start | bytes 786440 | tf_op jit(solution)/shard_map/ppermute | solution.py:377
  133.6 9.9 %collective-permute-start.18 = (bf16[128,1024]{1,0:T(8,128)(2,1)S(1)}, bf16[128,1024]{1,0:T(8,128)(2,1)S(1)}, u32[]{:S(2)}, u32[]{:S(2)}) collective-permute-start(bf16[128,1024]{1,0:T(8,128)(2,1)S(1)} %copy-done.43), channel_id=1, source_target_pairs={{0,8},{4,12},{8,0},{12,4},{16,24},{20,28},{24,16},{28,20},{1,9},{5... | collective-permute-start | bytes 786440 | tf_op jit(solution)/shard_map/ppermute | solution.py:377
  136.1 13.0 %collective-permute-start.17 = (bf16[128,1024]{1,0:T(8,128)(2,1)S(1)}, bf16[128,1024]{1,0:T(8,128)(2,1)S(1)}, u32[]{:S(2)}, u32[]{:S(2)}) collective-permute-start(bf16[128,1024]{1,0:T(8,128)(2,1)S(1)} %copy-done.42), channel_id=1, source_target_pairs={{0,12},{4,0},{8,4},{12,8},{16,28},{20,16},{24,20},{28,24},{1,13},{... | collective-permute-start | bytes 786440 | tf_op jit(solution)/shard_map/ppermute | solution.py:377
  161.5 38.1 %all-to-all-start = ((bf16[4,128,512]{2,1,0:T(8,128)(2,1)}), bf16[4,128,512]{2,1,0:T(8,128)(2,1)S(1)}, u32[]{:S(2)}, u32[]{:S(2)}) async-start(bf16[4,128,512]{2,1,0:T(8,128)(2,1)} %get-tuple-element.102), calls=%async_computation | async-start | bytes 1048576 | tf_op jit(solution)/shard_map/all_to_all | solution.py:374
  167.5 14.5 %collective-permute-start.22 = (bf16[128,1024]{1,0:T(8,128)(2,1)S(1)}, bf16[128,1024]{1,0:T(8,128)(2,1)S(1)}, u32[]{:S(2)}, u32[]{:S(2)}) collective-permute-start(bf16[128,1024]{1,0:T(8,128)(2,1)S(1)} %copy-done.41), channel_id=1, source_target_pairs={{0,4},{4,8},{8,12},{12,0},{16,20},{20,24},{24,28},{28,16},{1,5},{5... | collective-permute-start | bytes 786440 | tf_op jit(solution)/shard_map/ppermute | solution.py:377
  169.8 12.2 %collective-permute-start.21 = (bf16[128,1024]{1,0:T(8,128)(2,1)S(1)}, bf16[128,1024]{1,0:T(8,128)(2,1)S(1)}, u32[]{:S(2)}, u32[]{:S(2)}) collective-permute-start(bf16[128,1024]{1,0:T(8,128)(2,1)S(1)} %copy-done.40), channel_id=1, source_target_pairs={{0,8},{4,12},{8,0},{12,4},{16,24},{20,28},{24,16},{28,20},{1,9},{5... | collective-permute-start | bytes 786440 | tf_op jit(solution)/shard_map/ppermute | solution.py:377
  170.1 22.0 %collective-permute-start.20 = (bf16[128,1024]{1,0:T(8,128)(2,1)S(1)}, bf16[128,1024]{1,0:T(8,128)(2,1)S(1)}, u32[]{:S(2)}, u32[]{:S(2)}) collective-permute-start(bf16[128,1024]{1,0:T(8,128)(2,1)S(1)} %copy-done.39), channel_id=1, source_target_pairs={{0,12},{4,0},{8,4},{12,8},{16,28},{20,16},{24,20},{28,24},{1,13},{... | collective-permute-start | bytes 786440 | tf_op jit(solution)/shard_map/ppermute | solution.py:377
  171.4 20.8 %collective-permute-start.27 = (bf16[2,4,32,128]{3,2,1,0:T(8,128)(2,1)S(1)}, bf16[2,4,32,128]{3,2,1,0:T(8,128)(2,1)S(1)}, u32[]{:S(2)}, u32[]{:S(2)}) collective-permute-start(bf16[2,4,32,128]{3,2,1,0:T(8,128)(2,1)S(1)} %get-tuple-element.113), channel_id=1, source_target_pairs={{0,16},{1,17},{2,18},{3,19},{4,20},{5,21},{6,22},{7,23},{8,24},{9,... | collective-permute-start | bytes 196616 | tf_op jit(solution)/shard_map/ppermute | solution.py:396
  172.7 20.5 %collective-permute-start.28 = (bf16[2,4,32,128]{3,2,1,0:T(8,128)(2,1)S(1)}, bf16[2,4,32,128]{3,2,1,0:T(8,128)(2,1)S(1)}, u32[]{:S(2)}, u32[]{:S(2)}) collective-permute-start(bf16[2,4,32,128]{3,2,1,0:T(8,128)(2,1)S(1)} %get-tuple-element.114), channel_id=1, source_target_pairs={{0,17},{1,18},{2,19},{3,16},{4,21},{5,22},{6,23},{7,20},{8,25},{9,... | collective-permute-start | bytes 196616 | tf_op jit(solution)/shard_map/ppermute | solution.py:396
  182.0 13.8 %collective-permute-start.29 = (bf16[2,4,32,128]{3,2,1,0:T(8,128)(2,1)S(1)}, bf16[2,4,32,128]{3,2,1,0:T(8,128)(2,1)S(1)}, u32[]{:S(2)}, u32[]{:S(2)}) collective-permute-start(bf16[2,4,32,128]{3,2,1,0:T(8,128)(2,1)S(1)} %get-tuple-element.115), channel_id=1, source_target_pairs={{0,18},{1,19},{2,16},{3,17},{4,22},{5,23},{6,20},{7,21},{8,26},{9,... | collective-permute-start | bytes 196616 | tf_op jit(solution)/shard_map/ppermute | solution.py:396
  182.0 14.3 %collective-permute-start.30 = (bf16[2,4,32,128]{3,2,1,0:T(8,128)(2,1)S(1)}, bf16[2,4,32,128]{3,2,1,0:T(8,128)(2,1)S(1)}, u32[]{:S(2)}, u32[]{:S(2)}) collective-permute-start(bf16[2,4,32,128]{3,2,1,0:T(8,128)(2,1)S(1)} %get-tuple-element.112), channel_id=1, source_target_pairs={{0,19},{1,16},{2,17},{3,18},{4,23},{5,20},{6,21},{7,22},{8,27},{9,... | collective-permute-start | bytes 196616 | tf_op jit(solution)/shard_map/ppermute | solution.py:396
  (53 other events, 796.3 us)

commit v12 on v11

--- a/solution.py
+++ b/solution.py
@@ -116,6 +116,31 @@
         cost_estimate=LITTLE,
         name="pack",
     )(table, *(list(sources) * (pieces * columns)))
+
+
+def stack_kernel(table, *refs):
+    sources, out = refs[:-1], refs[-1]
+    width = sources[0].shape[1]
+    for i, source in enumerate(sources):
+        out[:, i * width : (i + 1) * width] = source[...]
+
+
+def stacked(table, base, sources, pieces, width):
+    rows = sources[0].shape[0]
+    total = len(sources) * width
+    return pl.pallas_call(
+        stack_kernel,
+        out_shape=jax.ShapeDtypeStruct((pieces, rows, total), sources[0].dtype),
+        grid_spec=pltpu.PrefetchScalarGridSpec(
+            num_scalar_prefetch=1,
+            grid=(pieces,),
+            in_specs=[pl.BlockSpec((rows, width), lambda i, t: (0, t[base + i]))] * len(sources),
+            out_specs=pl.BlockSpec((None, rows, total), lambda i, t: (i, 0, 0)),
+        ),
+        compiler_params=pltpu.CompilerParams(vmem_limit_bytes=LIMIT),
+        cost_estimate=LITTLE,
+        name="stacked",
+    )(table, *sources)
 
 
 def unpack_kernel(outputs, inner, base, table, *refs):
@@ -511,19 +536,38 @@
 
     partial = {s: states_of(s) for s in order}
     parts = [partial[0]] + [across(partial[s], s) for s in slots[1:]]
-    rows = {order[0]: sent_rows(order[0], partial[order[0]])}
+    bulk = stacked(
+        after(table, partial[0]),
+        base["owner"] + order[0] * part,
+        (query_rows, grad_out),
+        part,
+        heads * hd,
+    )
+    bulk = lax.all_to_all(bulk, "ctx", 0, 0, axis_index_groups=blocks_of, tiled=True)
+    rows = {order[0]: [bulk] * part}
     others = around_all(totals_of(parts))
     state, _ = spread(parts, others, "before", [prefix_state, prefix_norm], False)
     for s in order[1:]:
         rows[s] = sent_rows(s, state[0])
+
+    def row_specs(s, column):
+        if rows[s][0].ndim == 2:
+            return piece_specs(column, PAIR)
+
+        def spec(r):
+            return pl.BlockSpec(
+                (None, tok, PAIR * hd), lambda h, t: (t[base["sorted"] + r], 0, column(h))
+            )
+
+        return [spec(r) for r in shifts]
 
     def block_of(s):
         return call(
             block_kernel,
             [of(BF16, tok, heads * hd)] * part + [dk_shape, dv_shape, ext_shape, gm_shape],
             kv_specs(s)
-            + piece_specs(lambda h: h, PAIR)
-            + piece_specs(lambda h: grid[0] + h, PAIR)
+            + row_specs(s, lambda h: h)
+            + row_specs(s, lambda h: grid[0] + h)
             + [map_spec(s), ext_spec],
             piece_specs(lambda h: h, PAIR) + [dk_spec, dv_spec, ext_spec, gm_spec],
             [*kv, *kv, *rows[s], *rows[s], maps, state[s]],
@@ -578,6 +622,7 @@
         )
         two = jnp.stack([blocks[s][4], key_gm[s]])
         if s:
+            two = after(two, *returned[0])
             moved += [apart(rows_for(two, seq + r), s, r) for r in range(fsdp)]
         else:
             two = after(two, *suffix[1:])

time: 201 us -> 222 us (1.10)
  waiting for transfers between devices: 49.4 us -> 82.2 us
  starting transfers between devices: 71 us -> 55.6 us
    ppermute x5, waiting for transfers between devices: 12.5 us -> 29.5 us  [across(): lax.ppermute(array, 'ctx', [(d, (d + shift * part) % ctx) for d in range(...]
    ppermute x15 -> x12, starting transfers between devices: 31.3 us -> 16.2 us  [around(): lax.ppermute(array, 'ctx', [(d, d // part * part + (d + shift) % part) fo...]
    ppermute x4, starting transfers between devices: 16.9 us -> 5.64 us  [apart(): return lax.ppermute(array, ('ctx', 'fsdp'), moves)]
    ppermute x15 -> x12, waiting for transfers between devices: 20.2 us -> 29.3 us  [around(): lax.ppermute(array, 'ctx', [(d, d // part * part + (d + shift) % part) fo...]
    all_to_all x0 -> x1, starting transfers between devices: none -> 4.45 us  [shards(): lax.all_to_all(bulk, 'ctx', 0, 0, axis_index_groups=blocks_of, tiled=True)]
    ppermute x4, waiting for transfers between devices: 0.44 us -> 4.04 us  [apart(): return lax.ppermute(array, ('ctx', 'fsdp'), moves)]
    ppermute x4, waiting for transfers between devices: 14.3 us -> 17.8 us  [twin(): return lax.ppermute(array, 'fsdp', [(d, d ^ bit) for d in range(fsdp)])]
    unnamed x90 -> x82, local copies, waits for them, and re-layouts: 7.13 us -> 8.98 us
  transfers between devices with their start and end apart: 32 -> 30, of which waited for: 13 -> 16; matrix products, arithmetic and copies ran while one was open for 0% -> 0% of each run, Pallas kernels for 24% -> 22%
where the time goes in v12:
time: 222 us; the launch traced here: 221 us
  waiting for transfers between devices  82.2 us (37%)
  Pallas kernels  63.5 us (29%)
  starting transfers between devices  55.6 us (25%)
  local copies, waits for them, and re-layouts  9.15 us (4%)
  blocking collectives  9.03 us (4%)
    pallas_call x6, Pallas kernels, call(): pl.pallas_call(functools.partial(kernel, part, base['sorted']), out_shape...  49.7 us
    ppermute x5, waiting for transfers between devices, across(): lax.ppermute(array, 'ctx', [(d, (d + shift * part) % ctx) for d in range(...  29.5 us
    ppermute x12, waiting for transfers between devices, around(): lax.ppermute(array, 'ctx', [(d, d // part * part + (d + shift) % part) fo...  29.3 us
    ppermute x4, waiting for transfers between devices, twin(): return lax.ppermute(array, 'fsdp', [(d, d ^ bit) for d in range(fsdp)])  17.8 us
    ppermute x12, starting transfers between devices, around(): lax.ppermute(array, 'ctx', [(d, d // part * part + (d + shift) % part) fo...  16.2 us
    ppermute x5, starting transfers between devices, across(): lax.ppermute(array, 'ctx', [(d, (d + shift * part) % ctx) for d in range(...  14.5 us
    all_gather x1, blocking collectives, shards(): maps = lax.all_gather(near_maps, 'fsdp')  9.03 us
    unnamed x82, local copies, waits for them, and re-layouts  8.98 us
  transfers between devices with their start and end apart: 30, of which 16 were waited for; matrix products, arithmetic and copies ran while one was open for 0% of the time, Pallas kernels for 22%

profile of v12, /device:TPU:1, one launch (start us, length us, event | category | flops | bytes accessed | tf_op | source)
XLA Modules:
  0.0 221.1 jit_solution(2606709691343422340)
XLA Ops:
  13.7 9.0 %all-gather = bf16[8,8,32,128]{3,2,1,0:T(8,128)(2,1)S(1)} all-gather(bf16[2,8,32,128]{3,2,1,0:T(8,128)(2,1)S(1)} %pad_maximum_fusion.2), channel_id=2, replica_groups=mesh['ctx'=8,'fsdp'=4] {'fsdp'}, dimensions={0}, use_global_device_ids=true | all-gather | bytes 655360 | tf_op jit(solution)/shard_map/all_gather | solution.py:450
  22.8 3.4 %states.2.refs_0_ = bf16[8,144,128]{2,1,0:T(8,128)(2,1)S(1)} custom-call(s32[49]{0:T(128)S(1)} %stack.194.table, bf16[128,512]{1,0:T(8,128)(2,1)S(1)} %get-tuple-element.56.refs_0_.refs_4_, bf16[128,512]{1,0:T(8,128)(2,1)S(1)} %collective-permute-done.refs_1_.refs_5_, bf16[128,512]{1,0:T(8,128)(2,1)S(1)} %collective-permute-done.1.refs_2_.refs_6_, ...), custom_call_target="tpu_custom_call" | custom-call | flops 1000 | bytes 1000 | tf_op jit(solution)/shard_map/states/pallas_call | solution.py:486
  28.5 4.4 %all-to-all-start = ((bf16[4,128,2048]{2,1,0:T(8,128)(2,1)}), bf16[4,128,2048]{2,1,0:T(8,128)(2,1)}, u32[]{:S(2)}, u32[]{:S(2)}) async-start(bf16[4,128,2048]{2,1,0:T(8,128)(2,1)} %copy-done.15), calls=%async_computation | async-start | bytes 4194304 | tf_op jit(solution)/shard_map/all_to_all | solution.py:546
  33.1 3.4 %states.3 = bf16[8,144,128]{2,1,0:T(8,128)(2,1)S(1)} custom-call(s32[49]{0:T(128)S(1)} %stack.194.table, bf16[128,512]{1,0:T(8,128)(2,1)S(1)} %get-tuple-element.56.refs_0_.refs_4_, bf16[128,512]{1,0:T(8,128)(2,1)S(1)} %collective-permute-done.refs_1_.refs_5_, bf16[128,512]{1,0:T(8,128)(2,1)S(1)} %collective-permute-done.1.refs_2_.refs_6_, ...), custom_call_target="tpu_custom_call" | custom-call | flops 1000 | bytes 1000 | tf_op jit(solution)/shard_map/states/pallas_call | solution.py:486
  36.5 3.0 %collective-permute-start.4 = (bf16[8,144,128]{2,1,0:T(8,128)(2,1)S(1)}, bf16[8,144,128]{2,1,0:T(8,128)(2,1)S(1)}, u32[]{:S(2)}, u32[]{:S(2)}) collective-permute-start(bf16[8,144,128]{2,1,0:T(8,128)(2,1)S(1)} %states.3), channel_id=1, source_target_pairs={{0,16},{4,20},{8,24},{12,28},{16,0},{20,4},{24,8},{28,12},{1,17},{... | collective-permute-start | bytes 884744 | tf_op jit(solution)/shard_map/ppermute | solution.py:407
  39.5 22.6 %collective-permute-done.4.refs_1_ = bf16[8,144,128]{2,1,0:T(8,128)(2,1)S(1)} collective-permute-done((bf16[8,144,128]{2,1,0:T(8,128)(2,1)S(1)}, bf16[8,144,128]{2,1,0:T(8,128)(2,1)S(1)}, u32[]{:S(2)}, u32[]{:S(2)}) %collective-permute-start.4) | collective-permute-done | bytes 294944 | tf_op jit(solution)/shard_map/ppermute | solution.py:407
  66.1 7.7 %collective-permute-done.6.refs_3_ = bf16[8,144,128]{2,1,0:T(8,128)(2,1)S(1)} collective-permute-done((bf16[8,144,128]{2,1,0:T(8,128)(2,1)S(1)}, bf16[8,144,128]{2,1,0:T(8,128)(2,1)S(1)}, u32[]{:S(2)}, u32[]{:S(2)}) %collective-permute-start.6) | collective-permute-done | bytes 294944 | tf_op jit(solution)/shard_map/ppermute | solution.py:413
  75.3 3.1 %collective-permute-start.10 = (bf16[8,144,128]{2,1,0:T(8,128)(2,1)S(1)}, bf16[8,144,128]{2,1,0:T(8,128)(2,1)S(1)}, u32[]{:S(2)}, u32[]{:S(2)}) collective-permute-start(bf16[8,144,128]{2,1,0:T(8,128)(2,1)S(1)} %get-tuple-element.69), channel_id=1, source_target_pairs={{0,16},{4,20},{8,24},{12,28},{16,0},{20,4},{24,8},{28,12},{1,17},{... | collective-permute-start | bytes 884744 | tf_op jit(solution)/shard_map/ppermute | solution.py:407
  85.4 4.6 %collective-permute-done.10.refs_17_ = bf16[8,144,128]{2,1,0:T(8,128)(2,1)S(1)} collective-permute-done((bf16[8,144,128]{2,1,0:T(8,128)(2,1)S(1)}, bf16[8,144,128]{2,1,0:T(8,128)(2,1)S(1)}, u32[]{:S(2)}, u32[]{:S(2)}) %collective-permute-start.10) | collective-permute-done | bytes 294944 | tf_op jit(solution)/shard_map/ppermute | solution.py:407
  90.7 16.3 %blocks.3 = (bf16[128,1024]{1,0:T(8,128)(2,1)}, bf16[128,1024]{1,0:T(8,128)(2,1)}, bf16[128,1024]{1,0:T(8,128)(2,1)}, bf16[128,1024]{1,0:T(8,128)(2,1)}, f32[8,1...) custom-call(s32[49]{0:T(128)} %copy-done.27, ...), custom_call_target="tpu_custom_call" | custom-call | flops 1000 | bytes 1000 | tf_op jit(solution)/shard_map/blocks/pallas_call | solution.py:486
  108.6 16.0 %blocks.2 = (bf16[128,1024]{1,0:T(8,128)(2,1)}, bf16[128,1024]{1,0:T(8,128)(2,1)}, bf16[128,1024]{1,0:T(8,128)(2,1)}, bf16[128,1024]{1,0:T(8,128)(2,1)}, f32[8,1...) custom-call(s32[49]{0:T(128)} %copy-done.27, ...), custom_call_target="tpu_custom_call" | custom-call | flops 1000 | bytes 1000 | tf_op jit(solution)/shard_map/blocks/pallas_call | solution.py:486
  131.5 7.7 %collective-permute-done.13.refs_3_ = bf16[8,144,128]{2,1,0:T(8,128)(2,1)S(1)} collective-permute-done((bf16[8,144,128]{2,1,0:T(8,128)(2,1)S(1)}, bf16[8,144,128]{2,1,0:T(8,128)(2,1)S(1)}, u32[]{:S(2)}, u32[]{:S(2)}) %collective-permute-start.13) | collective-permute-done | bytes 294944 | tf_op jit(solution)/shard_map/ppermute | solution.py:413
  140.7 5.9 %collective-permute-start.20 = (bf16[8,144,128]{2,1,0:T(8,128)(2,1)S(1)}, bf16[8,144,128]{2,1,0:T(8,128)(2,1)S(1)}, u32[]{:S(2)}, u32[]{:S(2)}) collective-permute-start(bf16[8,144,128]{2,1,0:T(8,128)(2,1)S(1)} %get-tuple-element.91), channel_id=1, source_target_pairs={{0,16},{4,20},{8,24},{12,28},{16,0},{20,4},{24,8},{28,12},{1,17},{... | collective-permute-start | bytes 884744 | tf_op jit(solution)/shard_map/ppermute | solution.py:407
  147.0 3.0 %collective-permute-start.15 = (bf16[128,1024]{1,0:T(8,128)(2,1)S(1)}, bf16[128,1024]{1,0:T(8,128)(2,1)S(1)}, u32[]{:S(2)}, u32[]{:S(2)}) collective-permute-start(bf16[128,1024]{1,0:T(8,128)(2,1)S(1)} %copy-done.39), channel_id=1, source_target_pairs={{0,8},{4,12},{8,0},{12,4},{16,24},{20,28},{24,16},{28,20},{1,9},{5... | collective-permute-start | bytes 786440 | tf_op jit(solution)/shard_map/ppermute | solution.py:402
  150.1 4.8 %collective-permute-done.16 = bf16[128,1024]{1,0:T(8,128)(2,1)S(1)} collective-permute-done((bf16[128,1024]{1,0:T(8,128)(2,1)S(1)}, bf16[128,1024]{1,0:T(8,128)(2,1)S(1)}, u32[]{:S(2)}, u32[]{:S(2)}) %collective-permute-start.16) | collective-permute-done | bytes 262176 | tf_op jit(solution)/shard_map/ppermute | solution.py:402
  154.9 6.5 %collective-permute-done.15 = bf16[128,1024]{1,0:T(8,128)(2,1)S(1)} collective-permute-done((bf16[128,1024]{1,0:T(8,128)(2,1)S(1)}, bf16[128,1024]{1,0:T(8,128)(2,1)S(1)}, u32[]{:S(2)}, u32[]{:S(2)}) %collective-permute-start.15) | collective-permute-done | bytes 262176 | tf_op jit(solution)/shard_map/ppermute | solution.py:402
  164.7 5.3 %keys.2 = (bf16[4,128,512]{2,1,0:T(8,128)(2,1)}, bf16[4,128,128]{2,1,0:T(8,128)(2,1)S(1)}) custom-call(s32[49]{0:T(128)S(1)} %copy-done.28, bf16[128,512]{1,0:T(8,128)(2,1)S(1)} %copy-done.6, bf16[128,512]{1,0:T(8,128)(2,1)S(1)} %copy-done.8, bf16[128,512]{1,0:T(8,128)(2,1)S(1)} %copy-done.10, bf16[128,512]{1,0:T(8,128)(2,1)S(1)} %copy-done.12, ...), custom_call_target="tpu_custom_call" | custom-call | flops 1000 | bytes 1000 | tf_op jit(solution)/shard_map/keys/pallas_call | solution.py:486
  170.0 5.3 %keys.3 = (bf16[4,128,512]{2,1,0:T(8,128)(2,1)}, bf16[4,128,128]{2,1,0:T(8,128)(2,1)S(1)}) custom-call(s32[49]{0:T(128)S(1)} %copy-done.28, bf16[128,512]{1,0:T(8,128)(2,1)S(1)} %copy-done.6, bf16[128,512]{1,0:T(8,128)(2,1)S(1)} %copy-done.8, bf16[128,512]{1,0:T(8,128)(2,1)S(1)} %copy-done.10, ...), custom_call_target="tpu_custom_call", output_to_operand_aliasing={{0}: (13, {})} | custom-call | flops 1000 | bytes 1000 | tf_op jit(solution)/shard_map/keys/pallas_call | solution.py:486
  175.4 6.5 %all-to-all-start.1 = ((bf16[4,128,512]{2,1,0:T(8,128)(2,1)}), bf16[4,128,512]{2,1,0:T(8,128)(2,1)S(1)}, u32[]{:S(2)}, u32[]{:S(2)}) async-start(bf16[4,128,512]{2,1,0:T(8,128)(2,1)} %get-tuple-element.95), calls=%async_computation.1 | async-start | bytes 1048576 | tf_op jit(solution)/shard_map/all_to_all | solution.py:399
  185.8 8.1 %collective-permute-done.19 = bf16[128,1024]{1,0:T(8,128)(2,1)S(1)} collective-permute-done((bf16[128,1024]{1,0:T(8,128)(2,1)}, bf16[128,1024]{1,0:T(8,128)(2,1)S(1)}, u32[]{:S(2)}, u32[]{:S(2)}) %collective-permute-start.19) | collective-permute-done | bytes 262176 | tf_op jit(solution)/shard_map/ppermute | solution.py:402
  193.8 7.6 %collective-permute-done.17 = bf16[128,1024]{1,0:T(8,128)(2,1)S(1)} collective-permute-done((bf16[128,1024]{1,0:T(8,128)(2,1)S(1)}, bf16[128,1024]{1,0:T(8,128)(2,1)S(1)}, u32[]{:S(2)}, u32[]{:S(2)}) %collective-permute-start.17) | collective-permute-done | bytes 262176 | tf_op jit(solution)/shard_map/ppermute | solution.py:402
  201.5 4.1 %collective-permute-start.25 = (bf16[2,4,32,128]{3,2,1,0:T(8,128)(2,1)S(1)}, bf16[2,4,32,128]{3,2,1,0:T(8,128)(2,1)S(1)}, u32[]{:S(2)}, u32[]{:S(2)}) collective-permute-start(bf16[2,4,32,128]{3,2,1,0:T(8,128)(2,1)S(1)} %get-tuple-element.108), channel_id=1, source_target_pairs={{0,17},{1,18},{2,19},{3,16},{4,21},{5,22},{6,23},{7,20},{8,25},{9,... | collective-permute-start | bytes 196616 | tf_op jit(solution)/shard_map/ppermute | solution.py:421
  207.1 3.1 %collective-permute-start.21 = (bf16[2,4,32,128]{3,2,1,0:T(8,128)(2,1)S(1)}, bf16[2,4,32,128]{3,2,1,0:T(8,128)(2,1)S(1)}, u32[]{:S(2)}, u32[]{:S(2)}) collective-permute-start(bf16[2,4,32,128]{3,2,1,0:T(8,128)(2,1)S(1)} %get-tuple-element.112), channel_id=1, source_target_pairs={{0,1},{1,2},{2,3},{3,0},{4,5},{5,6},{6,7},{7,4},{8,9},{9,10},{10,1... | collective-permute-start | bytes 196616 | tf_op jit(solution)/shard_map/ppermute | solution.py:410
  210.7 3.9 %collective-permute-done.25.refs_4_ = bf16[2,4,32,128]{3,2,1,0:T(8,128)(2,1)S(1)} collective-permute-done((bf16[2,4,32,128]{3,2,1,0:T(8,128)(2,1)S(1)}, bf16[2,4,32,128]{3,2,1,0:T(8,128)(2,1)S(1)}, u32[]{:S(2)}, u32[]{:S(2)}) %collective-permute-start.25) | collective-permute-done | bytes 65568 | tf_op jit(solution)/shard_map/ppermute | solution.py:421
  (146 shorter events, 54.4 us)
Async XLA Ops:
  4.2 18.5 %collective-permute-start = (bf16[128,512]{1,0:T(8,128)(2,1)S(1)}, bf16[128,512]{1,0:T(8,128)(2,1)S(1)}, u32[]{:S(2)}, u32[]{:S(2)}) collective-permute-start(bf16[128,512]{1,0:T(8,128)(2,1)S(1)} %get-tuple-element.57), channel_id=1, source_target_pairs={{0,4},{4,8},{8,12},{12,0},{16,20},{20,24},{24,28},{28,16},{1,5},{5... | collective-permute-start | bytes 393224 | tf_op jit(solution)/shard_map/ppermute | solution.py:402
  6.3 16.4 %collective-permute-start.1 = (bf16[128,512]{1,0:T(8,128)(2,1)S(1)}, bf16[128,512]{1,0:T(8,128)(2,1)S(1)}, u32[]{:S(2)}, u32[]{:S(2)}) collective-permute-start(bf16[128,512]{1,0:T(8,128)(2,1)S(1)} %get-tuple-element.58), channel_id=1, source_target_pairs={{0,8},{4,12},{8,0},{12,4},{16,24},{20,28},{24,16},{28,20},{1,9},{5... | collective-permute-start | bytes 393224 | tf_op jit(solution)/shard_map/ppermute | solution.py:402
  7.6 15.1 %collective-permute-start.2 = (bf16[128,512]{1,0:T(8,128)(2,1)S(1)}, bf16[128,512]{1,0:T(8,128)(2,1)S(1)}, u32[]{:S(2)}, u32[]{:S(2)}) collective-permute-start(bf16[128,512]{1,0:T(8,128)(2,1)S(1)} %get-tuple-element.59), channel_id=1, source_target_pairs={{0,12},{4,0},{8,4},{12,8},{16,28},{20,16},{24,20},{28,24},{1,13},{... | collective-permute-start | bytes 393224 | tf_op jit(solution)/shard_map/ppermute | solution.py:402
  28.5 61.4 %all-to-all-start = ((bf16[4,128,2048]{2,1,0:T(8,128)(2,1)}), bf16[4,128,2048]{2,1,0:T(8,128)(2,1)}, u32[]{:S(2)}, u32[]{:S(2)}) async-start(bf16[4,128,2048]{2,1,0:T(8,128)(2,1)} %copy-done.15), calls=%async_computation | async-start | bytes 4194304 | tf_op jit(solution)/shard_map/all_to_all | solution.py:546
  36.5 25.6 %collective-permute-start.4 = (bf16[8,144,128]{2,1,0:T(8,128)(2,1)S(1)}, bf16[8,144,128]{2,1,0:T(8,128)(2,1)S(1)}, u32[]{:S(2)}, u32[]{:S(2)}) collective-permute-start(bf16[8,144,128]{2,1,0:T(8,128)(2,1)S(1)} %states.3), channel_id=1, source_target_pairs={{0,16},{4,20},{8,24},{12,28},{16,0},{20,4},{24,8},{28,12},{1,17},{... | collective-permute-start | bytes 884744 | tf_op jit(solution)/shard_map/ppermute | solution.py:407
  65.5 8.3 %collective-permute-start.6 = (bf16[8,144,128]{2,1,0:T(8,128)(2,1)S(1)}, bf16[8,144,128]{2,1,0:T(8,128)(2,1)S(1)}, u32[]{:S(2)}, u32[]{:S(2)}) collective-permute-start(bf16[8,144,128]{2,1,0:T(8,128)(2,1)S(1)} %totals.5), channel_id=1, source_target_pairs={{0,2},{1,3},{2,0},{3,1},{4,6},{5,7},{6,4},{7,5},{8,10},{9,11},{10,... | collective-permute-start | bytes 884744 | tf_op jit(solution)/shard_map/ppermute | solution.py:413
  75.3 14.6 %collective-permute-start.10 = (bf16[8,144,128]{2,1,0:T(8,128)(2,1)S(1)}, bf16[8,144,128]{2,1,0:T(8,128)(2,1)S(1)}, u32[]{:S(2)}, u32[]{:S(2)}) collective-permute-start(bf16[8,144,128]{2,1,0:T(8,128)(2,1)S(1)} %get-tuple-element.69), channel_id=1, source_target_pairs={{0,16},{4,20},{8,24},{12,28},{16,0},{20,4},{24,8},{28,12},{1,17},{... | collective-permute-start | bytes 884744 | tf_op jit(solution)/shard_map/ppermute | solution.py:407
  81.0 26.1 %collective-permute-start.7 = (bf16[128,2048]{1,0:T(8,128)(2,1)}, bf16[128,2048]{1,0:T(8,128)(2,1)S(1)}, u32[]{:S(2)}, u32[]{:S(2)}) collective-permute-start(bf16[128,2048]{1,0:T(8,128)(2,1)} %get-tuple-element.63), channel_id=1, source_target_pairs={{0,4},{4,8},{8,12},{12,0},{16,20},{20,24},{24,28},{28,16},{1,5},{5... | collective-permute-start | bytes 1572872 | tf_op jit(solution)/shard_map/ppermute | solution.py:402
  82.4 24.6 %collective-permute-start.8 = (bf16[128,2048]{1,0:T(8,128)(2,1)S(1)}, bf16[128,2048]{1,0:T(8,128)(2,1)S(1)}, u32[]{:S(2)}, u32[]{:S(2)}) collective-permute-start(bf16[128,2048]{1,0:T(8,128)(2,1)S(1)} %get-tuple-element.64), channel_id=1, source_target_pairs={{0,8},{4,12},{8,0},{12,4},{16,24},{20,28},{24,16},{28,20},{1,9},{5... | collective-permute-start | bytes 1572872 | tf_op jit(solution)/shard_map/ppermute | solution.py:402
  84.2 23.5 %collective-permute-start.9 = (bf16[128,2048]{1,0:T(8,128)(2,1)S(1)}, bf16[128,2048]{1,0:T(8,128)(2,1)S(1)}, u32[]{:S(2)}, u32[]{:S(2)}) collective-permute-start(bf16[128,2048]{1,0:T(8,128)(2,1)S(1)} %get-tuple-element.65), channel_id=1, source_target_pairs={{0,12},{4,0},{8,4},{12,8},{16,28},{20,16},{24,20},{28,24},{1,13},{... | collective-permute-start | bytes 1572872 | tf_op jit(solution)/shard_map/ppermute | solution.py:402
  107.0 17.7 %collective-permute-start.11 = (bf16[8,144,128]{2,1,0:T(8,128)(2,1)}, bf16[8,144,128]{2,1,0:T(8,128)(2,1)S(1)}, u32[]{:S(2)}, u32[]{:S(2)}) collective-permute-start(bf16[8,144,128]{2,1,0:T(8,128)(2,1)} %get-tuple-element.70), channel_id=1, source_target_pairs={{0,16},{4,20},{8,24},{12,28},{16,0},{20,4},{24,8},{28,12},{1,17},{... | collective-permute-start | bytes 884744 | tf_op jit(solution)/shard_map/ppermute | solution.py:407
  130.8 8.3 %collective-permute-start.13 = (bf16[8,144,128]{2,1,0:T(8,128)(2,1)S(1)}, bf16[8,144,128]{2,1,0:T(8,128)(2,1)S(1)}, u32[]{:S(2)}, u32[]{:S(2)}) collective-permute-start(bf16[8,144,128]{2,1,0:T(8,128)(2,1)S(1)} %totals.7), channel_id=1, source_target_pairs={{0,2},{1,3},{2,0},{3,1},{4,6},{5,7},{6,4},{7,5},{8,10},{9,11},{10,... | collective-permute-start | bytes 884744 | tf_op jit(solution)/shard_map/ppermute | solution.py:413
  140.7 29.3 %collective-permute-start.20 = (bf16[8,144,128]{2,1,0:T(8,128)(2,1)S(1)}, bf16[8,144,128]{2,1,0:T(8,128)(2,1)S(1)}, u32[]{:S(2)}, u32[]{:S(2)}) collective-permute-start(bf16[8,144,128]{2,1,0:T(8,128)(2,1)S(1)} %get-tuple-element.91), channel_id=1, source_target_pairs={{0,16},{4,20},{8,24},{12,28},{16,0},{20,4},{24,8},{28,12},{1,17},{... | collective-permute-start | bytes 884744 | tf_op jit(solution)/shard_map/ppermute | solution.py:407
  147.0 14.4 %collective-permute-start.15 = (bf16[128,1024]{1,0:T(8,128)(2,1)S(1)}, bf16[128,1024]{1,0:T(8,128)(2,1)S(1)}, u32[]{:S(2)}, u32[]{:S(2)}) collective-permute-start(bf16[128,1024]{1,0:T(8,128)(2,1)S(1)} %copy-done.39), channel_id=1, source_target_pairs={{0,8},{4,12},{8,0},{12,4},{16,24},{20,28},{24,16},{28,20},{1,9},{5... | collective-permute-start | bytes 786440 | tf_op jit(solution)/shard_map/ppermute | solution.py:402
  150.0 13.1 %collective-permute-start.14 = (bf16[128,1024]{1,0:T(8,128)(2,1)S(1)}, bf16[128,1024]{1,0:T(8,128)(2,1)S(1)}, u32[]{:S(2)}, u32[]{:S(2)}) collective-permute-start(bf16[128,1024]{1,0:T(8,128)(2,1)S(1)} %copy-done.38), channel_id=1, source_target_pairs={{0,12},{4,0},{8,4},{12,8},{16,28},{20,16},{24,20},{28,24},{1,13},{... | collective-permute-start | bytes 786440 | tf_op jit(solution)/shard_map/ppermute | solution.py:402
  175.4 44.3 %all-to-all-start.1 = ((bf16[4,128,512]{2,1,0:T(8,128)(2,1)}), bf16[4,128,512]{2,1,0:T(8,128)(2,1)S(1)}, u32[]{:S(2)}, u32[]{:S(2)}) async-start(bf16[4,128,512]{2,1,0:T(8,128)(2,1)} %get-tuple-element.95), calls=%async_computation.1 | async-start | bytes 1048576 | tf_op jit(solution)/shard_map/all_to_all | solution.py:399
  181.9 12.0 %collective-permute-start.19 = (bf16[128,1024]{1,0:T(8,128)(2,1)}, bf16[128,1024]{1,0:T(8,128)(2,1)S(1)}, u32[]{:S(2)}, u32[]{:S(2)}) collective-permute-start(bf16[128,1024]{1,0:T(8,128)(2,1)} %get-tuple-element.90), channel_id=1, source_target_pairs={{0,4},{4,8},{8,12},{12,0},{16,20},{20,24},{24,28},{28,16},{1,5},{5... | collective-permute-start | bytes 786440 | tf_op jit(solution)/shard_map/ppermute | solution.py:402
  184.1 9.7 %collective-permute-start.18 = (bf16[128,1024]{1,0:T(8,128)(2,1)}, bf16[128,1024]{1,0:T(8,128)(2,1)S(1)}, u32[]{:S(2)}, u32[]{:S(2)}) collective-permute-start(bf16[128,1024]{1,0:T(8,128)(2,1)} %get-tuple-element.88), channel_id=1, source_target_pairs={{0,8},{4,12},{8,0},{12,4},{16,24},{20,28},{24,16},{28,20},{1,9},{5... | collective-permute-start | bytes 786440 | tf_op jit(solution)/shard_map/ppermute | solution.py:402
  184.5 16.9 %collective-permute-start.17 = (bf16[128,1024]{1,0:T(8,128)(2,1)S(1)}, bf16[128,1024]{1,0:T(8,128)(2,1)S(1)}, u32[]{:S(2)}, u32[]{:S(2)}) collective-permute-start(bf16[128,1024]{1,0:T(8,128)(2,1)S(1)} %copy-done.37), channel_id=1, source_target_pairs={{0,12},{4,0},{8,4},{12,8},{16,28},{20,16},{24,20},{28,24},{1,13},{... | collective-permute-start | bytes 786440 | tf_op jit(solution)/shard_map/ppermute | solution.py:402
  201.4 8.7 %collective-permute-start.24 = (bf16[2,4,32,128]{3,2,1,0:T(8,128)(2,1)S(1)}, bf16[2,4,32,128]{3,2,1,0:T(8,128)(2,1)S(1)}, u32[]{:S(2)}, u32[]{:S(2)}) collective-permute-start(bf16[2,4,32,128]{3,2,1,0:T(8,128)(2,1)S(1)} %get-tuple-element.109), channel_id=1, source_target_pairs={{0,16},{1,17},{2,18},{3,19},{4,20},{5,21},{6,22},{7,23},{8,24},{9,... | collective-permute-start | bytes 196616 | tf_op jit(solution)/shard_map/ppermute | solution.py:421
  201.5 13.1 %collective-permute-start.25 = (bf16[2,4,32,128]{3,2,1,0:T(8,128)(2,1)S(1)}, bf16[2,4,32,128]{3,2,1,0:T(8,128)(2,1)S(1)}, u32[]{:S(2)}, u32[]{:S(2)}) collective-permute-start(bf16[2,4,32,128]{3,2,1,0:T(8,128)(2,1)S(1)} %get-tuple-element.108), channel_id=1, source_target_pairs={{0,17},{1,18},{2,19},{3,16},{4,21},{5,22},{6,23},{7,20},{8,25},{9,... | collective-permute-start | bytes 196616 | tf_op jit(solution)/shard_map/ppermute | solution.py:421
  205.7 10.9 %collective-permute-start.26 = (bf16[2,4,32,128]{3,2,1,0:T(8,128)(2,1)S(1)}, bf16[2,4,32,128]{3,2,1,0:T(8,128)(2,1)S(1)}, u32[]{:S(2)}, u32[]{:S(2)}) collective-permute-start(bf16[2,4,32,128]{3,2,1,0:T(8,128)(2,1)S(1)} %get-tuple-element.107), channel_id=1, source_target_pairs={{0,18},{1,19},{2,16},{3,17},{4,22},{5,23},{6,20},{7,21},{8,26},{9,... | collective-permute-start | bytes 196616 | tf_op jit(solution)/shard_map/ppermute | solution.py:421
  206.1 10.7 %collective-permute-start.27 = (bf16[2,4,32,128]{3,2,1,0:T(8,128)(2,1)S(1)}, bf16[2,4,32,128]{3,2,1,0:T(8,128)(2,1)S(1)}, u32[]{:S(2)}, u32[]{:S(2)}) collective-permute-start(bf16[2,4,32,128]{3,2,1,0:T(8,128)(2,1)S(1)} %get-tuple-element.106), channel_id=1, source_target_pairs={{0,19},{1,16},{2,17},{3,18},{4,23},{5,20},{6,21},{7,22},{8,27},{9,... | collective-permute-start | bytes 196616 | tf_op jit(solution)/shard_map/ppermute | solution.py:421
  207.1 9.7 %collective-permute-start.21 = (bf16[2,4,32,128]{3,2,1,0:T(8,128)(2,1)S(1)}, bf16[2,4,32,128]{3,2,1,0:T(8,128)(2,1)S(1)}, u32[]{:S(2)}, u32[]{:S(2)}) collective-permute-start(bf16[2,4,32,128]{3,2,1,0:T(8,128)(2,1)S(1)} %get-tuple-element.112), channel_id=1, source_target_pairs={{0,1},{1,2},{2,3},{3,0},{4,5},{5,6},{6,7},{7,4},{8,9},{9,10},{10,1... | collective-permute-start | bytes 196616 | tf_op jit(solution)/shard_map/ppermute | solution.py:410
  (47 other events, 864.7 us)

commit v13 on v12

--- a/solution.py
+++ b/solution.py
@@ -501,7 +501,7 @@
             name=name,
         )(table, *arrays)
 
-    def states_of(s):
+    def states_of(s, maps):
         return call(
             state_kernel,
             [ext_shape],
@@ -534,7 +534,9 @@
             others.append(twin(total, bit))
         return others
 
-    partial = {s: states_of(s) for s in order}
+    partial = {}
+    for s in order:
+        partial[s] = states_of(s, after(maps, *partial.values()))
     parts = [partial[0]] + [across(partial[s], s) for s in slots[1:]]
     bulk = stacked(
         after(table, partial[0]),
@@ -622,14 +624,13 @@
         )
         two = jnp.stack([blocks[s][4], key_gm[s]])
         if s:
-            two = after(two, *returned[0])
             moved += [apart(rows_for(two, seq + r), s, r) for r in range(fsdp)]
         else:
             two = after(two, *suffix[1:])
             moved += [along(rows_for(two, seq + r), r) for r in range(1, fsdp)]
             returned[s] = brought_back(s, key_gm[s])
 
-    pairs = within(pairs)
+    pairs = within(after(pairs, *returned[0]))
     back = [piece[None] for s in slots for piece in returned[s]]
     (grad_queries,) = unpack(table, base["back"], back, 1, 1, heads * hd)
     grad_keys, grad_values = unpack(table, base["owner"], [pairs], grp, 2, hd)

time: 222 us -> 205 us (0.923)
  waiting for transfers between devices: 82.2 us -> 57.6 us
  starting transfers between devices: 55.6 us -> 62 us
    ppermute x12, waiting for transfers between devices: 29.3 us -> 7.96 us  [around(): lax.ppermute(array, 'ctx', [(d, d // part * part + (d + shift) % part) fo...]
    ppermute x4, starting transfers between devices: 5.64 us -> 14 us  [apart(): return lax.ppermute(array, ('ctx', 'fsdp'), moves)]
    ppermute x4, waiting for transfers between devices: 17.8 us -> 11.6 us  [twin(): return lax.ppermute(array, 'fsdp', [(d, d ^ bit) for d in range(fsdp)])]
    ppermute x5, waiting for transfers between devices: 29.5 us -> 33.2 us  [across(): lax.ppermute(array, 'ctx', [(d, (d + shift * part) % ctx) for d in range(...]
    all_to_all x1, starting transfers between devices: 6.5 us -> 3.47 us  [within(): lax.all_to_all(array, 'ctx', 0, 0, axis_index_groups=blocks_of, tiled=True)]
    ppermute x12, starting transfers between devices: 16.2 us -> 18.7 us  [around(): lax.ppermute(array, 'ctx', [(d, d // part * part + (d + shift) % part) fo...]
    unnamed x82 -> x86, local copies, waits for them, and re-layouts: 8.98 us -> 10 us
  transfers between devices with their start and end apart: 30 -> 30, of which waited for: 16 -> 13; matrix products, arithmetic and copies ran while one was open for 0% -> 0% of each run, Pallas kernels for 22% -> 25%
where the time goes in v13:
time: 205 us; the launch traced here: 204 us
  Pallas kernels  63.4 us (31%)
  starting transfers between devices  62 us (30%)
  waiting for transfers between devices  57.6 us (28%)
  local copies, waits for them, and re-layouts  10.2 us (5%)
  blocking collectives  9.16 us (4%)
    pallas_call x6, Pallas kernels, call(): pl.pallas_call(functools.partial(kernel, part, base['sorted']), out_shape...  49.7 us
    ppermute x5, waiting for transfers between devices, across(): lax.ppermute(array, 'ctx', [(d, (d + shift * part) % ctx) for d in range(...  33.2 us
    ppermute x12, starting transfers between devices, around(): lax.ppermute(array, 'ctx', [(d, d // part * part + (d + shift) % part) fo...  18.7 us
    ppermute x5, starting transfers between devices, across(): lax.ppermute(array, 'ctx', [(d, (d + shift * part) % ctx) for d in range(...  15 us
    ppermute x4, starting transfers between devices, apart(): return lax.ppermute(array, ('ctx', 'fsdp'), moves)  14 us
    ppermute x4, waiting for transfers between devices, twin(): return lax.ppermute(array, 'fsdp', [(d, d ^ bit) for d in range(fsdp)])  11.6 us
    unnamed x86, local copies, waits for them, and re-layouts  10 us
    all_gather x1, blocking collectives, shards(): maps = lax.all_gather(near_maps, 'fsdp')  9.16 us
  transfers between devices with their start and end apart: 30, of which 13 were waited for; matrix products, arithmetic and copies ran while one was open for 0% of the time, Pallas kernels for 25%

profile of v13, /device:TPU:1, one launch (start us, length us, event | category | flops | bytes accessed | tf_op | source)
XLA Modules:
  0.0 204.1 jit_solution(2929224794577881061)
XLA Ops:
  4.2 2.1 %collective-permute-start = (bf16[128,512]{1,0:T(8,128)(2,1)S(1)}, bf16[128,512]{1,0:T(8,128)(2,1)S(1)}, u32[]{:S(2)}, u32[]{:S(2)}) collective-permute-start(bf16[128,512]{1,0:T(8,128)(2,1)S(1)} %get-tuple-element.58), channel_id=1, source_target_pairs={{0,4},{4,8},{8,12},{12,0},{16,20},{20,24},{24,28},{28,16},{1,5},{5... | collective-permute-start | bytes 393224 | tf_op jit(solution)/shard_map/ppermute | solution.py:402
  8.8 2.4 %collective-permute-start.3 = (bf16[8,32,128]{2,1,0:T(8,128)(2,1)S(1)}, bf16[8,32,128]{2,1,0:T(8,128)(2,1)S(1)}, u32[]{:S(2)}, u32[]{:S(2)}) collective-permute-start(bf16[8,32,128]{2,1,0:T(8,128)(2,1)S(1)} %pad_maximum_fusion.2), channel_id=1, source_target_pairs={{0,16},{4,20},{8,24},{12,28},{16,0},{20,4},{24,8},{28,12},{1,17},{... | collective-permute-start | bytes 196616 | tf_op jit(solution)/shard_map/ppermute | solution.py:407
  11.3 2.4 %collective-permute-done.3 = bf16[8,32,128]{2,1,0:T(8,128)(2,1)S(1)} collective-permute-done((bf16[8,32,128]{2,1,0:T(8,128)(2,1)S(1)}, bf16[8,32,128]{2,1,0:T(8,128)(2,1)S(1)}, u32[]{:S(2)}, u32[]{:S(2)}) %collective-permute-start.3) | collective-permute-done | bytes 65568 | tf_op jit(solution)/shard_map/ppermute | solution.py:407
  13.7 9.2 %all-gather = bf16[8,8,32,128]{3,2,1,0:T(8,128)(2,1)S(1)} all-gather(bf16[2,8,32,128]{3,2,1,0:T(8,128)(2,1)S(1)} %pad_maximum_fusion.1), channel_id=2, replica_groups=mesh['ctx'=8,'fsdp'=4] {'fsdp'}, dimensions={0}, use_global_device_ids=true | all-gather | bytes 655360 | tf_op jit(solution)/shard_map/all_gather | solution.py:450
  22.9 3.4 %states.2 = bf16[8,144,128]{2,1,0:T(8,128)(2,1)S(1)} custom-call(s32[49]{0:T(128)S(1)} %stack.194.table, bf16[128,512]{1,0:T(8,128)(2,1)S(1)} %get-tuple-element.57.refs_0_.refs_4_, bf16[128,512]{1,0:T(8,128)(2,1)S(1)} %collective-permute-done.refs_1_.refs_5_, bf16[128,512]{1,0:T(8,128)(2,1)S(1)} %collective-permute-done.1.refs_2_.refs_6_, ...), custom_call_target="tpu_custom_call" | custom-call | flops 1000 | bytes 1000 | tf_op jit(solution)/shard_map/states/pallas_call | solution.py:486
  27.1 3.4 %states.3.refs_0_ = bf16[8,144,128]{2,1,0:T(8,128)(2,1)S(1)} custom-call(s32[49]{0:T(128)S(1)} %stack.194.table, bf16[128,512]{1,0:T(8,128)(2,1)S(1)} %get-tuple-element.57.refs_0_.refs_4_, bf16[128,512]{1,0:T(8,128)(2,1)S(1)} %collective-permute-done.refs_1_.refs_5_, bf16[128,512]{1,0:T(8,128)(2,1)S(1)} %collective-permute-done.1.refs_2_.refs_6_, ...), custom_call_target="tpu_custom_call" | custom-call | flops 1000 | bytes 1000 | tf_op jit(solution)/shard_map/states/pallas_call | solution.py:486
  32.8 4.6 %all-to-all-start = ((bf16[4,128,2048]{2,1,0:T(8,128)(2,1)}), bf16[4,128,2048]{2,1,0:T(8,128)(2,1)}, u32[]{:S(2)}, u32[]{:S(2)}) async-start(bf16[4,128,2048]{2,1,0:T(8,128)(2,1)} %copy-done.15), calls=%async_computation | async-start | bytes 4194304 | tf_op jit(solution)/shard_map/all_to_all | solution.py:548
  37.4 3.0 %collective-permute-start.4 = (bf16[8,144,128]{2,1,0:T(8,128)(2,1)}, bf16[8,144,128]{2,1,0:T(8,128)(2,1)S(1)}, u32[]{:S(2)}, u32[]{:S(2)}) collective-permute-start(bf16[8,144,128]{2,1,0:T(8,128)(2,1)} %copy-done.23), channel_id=1, source_target_pairs={{0,16},{4,20},{8,24},{12,28},{16,0},{20,4},{24,8},{28,12},{1,17},{... | collective-permute-start | bytes 884744 | tf_op jit(solution)/shard_map/ppermute | solution.py:407
  40.5 26.2 %collective-permute-done.4.refs_1_ = bf16[8,144,128]{2,1,0:T(8,128)(2,1)S(1)} collective-permute-done((bf16[8,144,128]{2,1,0:T(8,128)(2,1)}, bf16[8,144,128]{2,1,0:T(8,128)(2,1)S(1)}, u32[]{:S(2)}, u32[]{:S(2)}) %collective-permute-start.4) | collective-permute-done | bytes 294944 | tf_op jit(solution)/shard_map/ppermute | solution.py:407
  70.7 7.7 %collective-permute-done.6.refs_3_ = bf16[8,144,128]{2,1,0:T(8,128)(2,1)S(1)} collective-permute-done((bf16[8,144,128]{2,1,0:T(8,128)(2,1)S(1)}, bf16[8,144,128]{2,1,0:T(8,128)(2,1)S(1)}, u32[]{:S(2)}, u32[]{:S(2)}) %collective-permute-start.6) | collective-permute-done | bytes 294944 | tf_op jit(solution)/shard_map/ppermute | solution.py:413
  80.9 3.0 %collective-permute-start.10 = (bf16[8,144,128]{2,1,0:T(8,128)(2,1)S(1)}, bf16[8,144,128]{2,1,0:T(8,128)(2,1)}, u32[]{:S(2)}, u32[]{:S(2)}) collective-permute-start(bf16[8,144,128]{2,1,0:T(8,128)(2,1)S(1)} %get-tuple-element.71), channel_id=1, source_target_pairs={{0,16},{4,20},{8,24},{12,28},{16,0},{20,4},{24,8},{28,12},{1,17},{... | collective-permute-start | bytes 884744 | tf_op jit(solution)/shard_map/ppermute | solution.py:407
  90.9 4.7 %collective-permute-done.10.refs_17_ = bf16[8,144,128]{2,1,0:T(8,128)(2,1)} collective-permute-done((bf16[8,144,128]{2,1,0:T(8,128)(2,1)S(1)}, bf16[8,144,128]{2,1,0:T(8,128)(2,1)}, u32[]{:S(2)}, u32[]{:S(2)}) %collective-permute-start.10) | collective-permute-done | bytes 294944 | tf_op jit(solution)/shard_map/ppermute | solution.py:407
  95.5 16.3 %blocks.3 = (bf16[128,1024]{1,0:T(8,128)(2,1)}, bf16[128,1024]{1,0:T(8,128)(2,1)}, bf16[128,1024]{1,0:T(8,128)(2,1)}, bf16[128,1024]{1,0:T(8,128)(2,1)}, f32[8,1...) custom-call(s32[49]{0:T(128)} %copy-done.28, ...), custom_call_target="tpu_custom_call" | custom-call | flops 1000 | bytes 1000 | tf_op jit(solution)/shard_map/blocks/pallas_call | solution.py:486
  114.0 16.0 %blocks.2 = (bf16[128,1024]{1,0:T(8,128)(2,1)}, bf16[128,1024]{1,0:T(8,128)(2,1)}, bf16[128,1024]{1,0:T(8,128)(2,1)}, bf16[128,1024]{1,0:T(8,128)(2,1)}, f32[8,1...) custom-call(s32[49]{0:T(128)} %copy-done.28, ...), custom_call_target="tpu_custom_call" | custom-call | flops 1000 | bytes 1000 | tf_op jit(solution)/shard_map/blocks/pallas_call | solution.py:486
  138.2 3.3 %collective-permute-start.15 = (bf16[128,1024]{1,0:T(8,128)(2,1)S(1)}, bf16[128,1024]{1,0:T(8,128)(2,1)S(1)}, u32[]{:S(2)}, u32[]{:S(2)}) collective-permute-start(bf16[128,1024]{1,0:T(8,128)(2,1)S(1)} %copy-done.41), channel_id=1, source_target_pairs={{0,8},{4,12},{8,0},{12,4},{16,24},{20,28},{24,16},{28,20},{1,9},{5... | collective-permute-start | bytes 786440 | tf_op jit(solution)/shard_map/ppermute | solution.py:402
  145.5 6.6 %collective-permute-start.20 = (bf16[8,144,128]{2,1,0:T(8,128)(2,1)S(1)}, bf16[8,144,128]{2,1,0:T(8,128)(2,1)S(1)}, u32[]{:S(2)}, u32[]{:S(2)}) collective-permute-start(bf16[8,144,128]{2,1,0:T(8,128)(2,1)S(1)} %get-tuple-element.93), channel_id=1, source_target_pairs={{0,16},{4,20},{8,24},{12,28},{16,0},{20,4},{24,8},{28,12},{1,17},{... | collective-permute-start | bytes 884744 | tf_op jit(solution)/shard_map/ppermute | solution.py:407
  155.3 5.3 %keys.2 = (bf16[4,128,512]{2,1,0:T(8,128)(2,1)}, bf16[4,128,128]{2,1,0:T(8,128)(2,1)S(1)}) custom-call(s32[49]{0:T(128)S(1)} %copy-done.29, bf16[128,512]{1,0:T(8,128)(2,1)S(1)} %copy-done.6, bf16[128,512]{1,0:T(8,128)(2,1)S(1)} %copy-done.8, bf16[128,512]{1,0:T(8,128)(2,1)S(1)} %copy-done.10, bf16[128,512]{1,0:T(8,128)(2,1)S(1)} %copy-done.12, ...), custom_call_target="tpu_custom_call" | custom-call | flops 1000 | bytes 1000 | tf_op jit(solution)/shard_map/keys/pallas_call | solution.py:486
  164.2 5.3 %keys.3 = (bf16[4,128,512]{2,1,0:T(8,128)(2,1)}, bf16[4,128,128]{2,1,0:T(8,128)(2,1)S(1)}) custom-call(s32[49]{0:T(128)S(1)} %copy-done.29, bf16[128,512]{1,0:T(8,128)(2,1)S(1)} %copy-done.6, bf16[128,512]{1,0:T(8,128)(2,1)S(1)} %copy-done.8, bf16[128,512]{1,0:T(8,128)(2,1)S(1)} %copy-done.10, ...), custom_call_target="tpu_custom_call", output_to_operand_aliasing={{0}: (13, {})} | custom-call | flops 1000 | bytes 1000 | tf_op jit(solution)/shard_map/keys/pallas_call | solution.py:486
  170.8 3.8 %collective-permute-done.17 = bf16[128,1024]{1,0:T(8,128)(2,1)S(1)} collective-permute-done((bf16[128,1024]{1,0:T(8,128)(2,1)S(1)}, bf16[128,1024]{1,0:T(8,128)(2,1)S(1)}, u32[]{:S(2)}, u32[]{:S(2)}) %collective-permute-start.17) | collective-permute-done | bytes 262176 | tf_op jit(solution)/shard_map/ppermute | solution.py:402
  174.6 3.5 %all-to-all-start.1 = ((bf16[4,128,512]{2,1,0:T(8,128)(2,1)}), bf16[4,128,512]{2,1,0:T(8,128)(2,1)S(1)}, u32[]{:S(2)}, u32[]{:S(2)}) async-start(bf16[4,128,512]{2,1,0:T(8,128)(2,1)} %get-tuple-element.98), calls=%async_computation.1 | async-start | bytes 1048576 | tf_op jit(solution)/shard_map/all_to_all | solution.py:399
  178.2 6.9 %collective-permute-start.24 = (bf16[2,4,32,128]{3,2,1,0:T(8,128)(2,1)S(1)}, bf16[2,4,32,128]{3,2,1,0:T(8,128)(2,1)S(1)}, u32[]{:S(2)}, u32[]{:S(2)}) collective-permute-start(bf16[2,4,32,128]{3,2,1,0:T(8,128)(2,1)S(1)} %get-tuple-element.109), channel_id=1, source_target_pairs={{0,16},{1,17},{2,18},{3,19},{4,20},{5,21},{6,22},{7,23},{8,24},{9,... | collective-permute-start | bytes 196616 | tf_op jit(solution)/shard_map/ppermute | solution.py:421
  185.1 4.2 %collective-permute-start.25 = (bf16[2,4,32,128]{3,2,1,0:T(8,128)(2,1)S(1)}, bf16[2,4,32,128]{3,2,1,0:T(8,128)(2,1)S(1)}, u32[]{:S(2)}, u32[]{:S(2)}) collective-permute-start(bf16[2,4,32,128]{3,2,1,0:T(8,128)(2,1)S(1)} %get-tuple-element.110), channel_id=1, source_target_pairs={{0,17},{1,18},{2,19},{3,16},{4,21},{5,22},{6,23},{7,20},{8,25},{9,... | collective-permute-start | bytes 196616 | tf_op jit(solution)/shard_map/ppermute | solution.py:421
  189.3 2.6 %collective-permute-start.26 = (bf16[2,4,32,128]{3,2,1,0:T(8,128)(2,1)S(1)}, bf16[2,4,32,128]{3,2,1,0:T(8,128)(2,1)S(1)}, u32[]{:S(2)}, u32[]{:S(2)}) collective-permute-start(bf16[2,4,32,128]{3,2,1,0:T(8,128)(2,1)S(1)} %get-tuple-element.111), channel_id=1, source_target_pairs={{0,18},{1,19},{2,16},{3,17},{4,22},{5,23},{6,20},{7,21},{8,26},{9,... | collective-permute-start | bytes 196616 | tf_op jit(solution)/shard_map/ppermute | solution.py:421
  196.4 3.5 %collective-permute-done.26.refs_5_ = bf16[2,4,32,128]{3,2,1,0:T(8,128)(2,1)S(1)} collective-permute-done((bf16[2,4,32,128]{3,2,1,0:T(8,128)(2,1)S(1)}, bf16[2,4,32,128]{3,2,1,0:T(8,128)(2,1)S(1)}, u32[]{:S(2)}, u32[]{:S(2)}) %collective-permute-start.26) | collective-permute-done | bytes 65568 | tf_op jit(solution)/shard_map/ppermute | solution.py:421
  (149 shorter events, 53.7 us)
Async XLA Ops:
  4.2 18.7 %collective-permute-start = (bf16[128,512]{1,0:T(8,128)(2,1)S(1)}, bf16[128,512]{1,0:T(8,128)(2,1)S(1)}, u32[]{:S(2)}, u32[]{:S(2)}) collective-permute-start(bf16[128,512]{1,0:T(8,128)(2,1)S(1)} %get-tuple-element.58), channel_id=1, source_target_pairs={{0,4},{4,8},{8,12},{12,0},{16,20},{20,24},{24,28},{28,16},{1,5},{5... | collective-permute-start | bytes 393224 | tf_op jit(solution)/shard_map/ppermute | solution.py:402
  6.3 16.6 %collective-permute-start.1 = (bf16[128,512]{1,0:T(8,128)(2,1)S(1)}, bf16[128,512]{1,0:T(8,128)(2,1)S(1)}, u32[]{:S(2)}, u32[]{:S(2)}) collective-permute-start(bf16[128,512]{1,0:T(8,128)(2,1)S(1)} %get-tuple-element.59), channel_id=1, source_target_pairs={{0,8},{4,12},{8,0},{12,4},{16,24},{20,28},{24,16},{28,20},{1,9},{5... | collective-permute-start | bytes 393224 | tf_op jit(solution)/shard_map/ppermute | solution.py:402
  7.6 15.3 %collective-permute-start.2 = (bf16[128,512]{1,0:T(8,128)(2,1)S(1)}, bf16[128,512]{1,0:T(8,128)(2,1)S(1)}, u32[]{:S(2)}, u32[]{:S(2)}) collective-permute-start(bf16[128,512]{1,0:T(8,128)(2,1)S(1)} %get-tuple-element.60), channel_id=1, source_target_pairs={{0,12},{4,0},{8,4},{12,8},{16,28},{20,16},{24,20},{28,24},{1,13},{... | collective-permute-start | bytes 393224 | tf_op jit(solution)/shard_map/ppermute | solution.py:402
  32.8 62.7 %all-to-all-start = ((bf16[4,128,2048]{2,1,0:T(8,128)(2,1)}), bf16[4,128,2048]{2,1,0:T(8,128)(2,1)}, u32[]{:S(2)}, u32[]{:S(2)}) async-start(bf16[4,128,2048]{2,1,0:T(8,128)(2,1)} %copy-done.15), calls=%async_computation | async-start | bytes 4194304 | tf_op jit(solution)/shard_map/all_to_all | solution.py:548
  37.4 29.2 %collective-permute-start.4 = (bf16[8,144,128]{2,1,0:T(8,128)(2,1)}, bf16[8,144,128]{2,1,0:T(8,128)(2,1)S(1)}, u32[]{:S(2)}, u32[]{:S(2)}) collective-permute-start(bf16[8,144,128]{2,1,0:T(8,128)(2,1)} %copy-done.23), channel_id=1, source_target_pairs={{0,16},{4,20},{8,24},{12,28},{16,0},{20,4},{24,8},{28,12},{1,17},{... | collective-permute-start | bytes 884744 | tf_op jit(solution)/shard_map/ppermute | solution.py:407
  80.9 14.6 %collective-permute-start.10 = (bf16[8,144,128]{2,1,0:T(8,128)(2,1)S(1)}, bf16[8,144,128]{2,1,0:T(8,128)(2,1)}, u32[]{:S(2)}, u32[]{:S(2)}) collective-permute-start(bf16[8,144,128]{2,1,0:T(8,128)(2,1)S(1)} %get-tuple-element.71), channel_id=1, source_target_pairs={{0,16},{4,20},{8,24},{12,28},{16,0},{20,4},{24,8},{28,12},{1,17},{... | collective-permute-start | bytes 884744 | tf_op jit(solution)/shard_map/ppermute | solution.py:407
  86.5 25.4 %collective-permute-start.7 = (bf16[128,2048]{1,0:T(8,128)(2,1)}, bf16[128,2048]{1,0:T(8,128)(2,1)S(1)}, u32[]{:S(2)}, u32[]{:S(2)}) collective-permute-start(bf16[128,2048]{1,0:T(8,128)(2,1)} %get-tuple-element.65), channel_id=1, source_target_pairs={{0,4},{4,8},{8,12},{12,0},{16,20},{20,24},{24,28},{28,16},{1,5},{5... | collective-permute-start | bytes 1572872 | tf_op jit(solution)/shard_map/ppermute | solution.py:402
  87.9 24.0 %collective-permute-start.8 = (bf16[128,2048]{1,0:T(8,128)(2,1)S(1)}, bf16[128,2048]{1,0:T(8,128)(2,1)S(1)}, u32[]{:S(2)}, u32[]{:S(2)}) collective-permute-start(bf16[128,2048]{1,0:T(8,128)(2,1)S(1)} %get-tuple-element.66), channel_id=1, source_target_pairs={{0,8},{4,12},{8,0},{12,4},{16,24},{20,28},{24,16},{28,20},{1,9},{5... | collective-permute-start | bytes 1572872 | tf_op jit(solution)/shard_map/ppermute | solution.py:402
  89.7 23.5 %collective-permute-start.9 = (bf16[128,2048]{1,0:T(8,128)(2,1)S(1)}, bf16[128,2048]{1,0:T(8,128)(2,1)S(1)}, u32[]{:S(2)}, u32[]{:S(2)}) collective-permute-start(bf16[128,2048]{1,0:T(8,128)(2,1)S(1)} %get-tuple-element.67), channel_id=1, source_target_pairs={{0,12},{4,0},{8,4},{12,8},{16,28},{20,16},{24,20},{28,24},{1,13},{... | collective-permute-start | bytes 1572872 | tf_op jit(solution)/shard_map/ppermute | solution.py:402
  111.8 18.3 %collective-permute-start.11 = (bf16[8,144,128]{2,1,0:T(8,128)(2,1)}, bf16[8,144,128]{2,1,0:T(8,128)(2,1)S(1)}, u32[]{:S(2)}, u32[]{:S(2)}) collective-permute-start(bf16[8,144,128]{2,1,0:T(8,128)(2,1)} %get-tuple-element.72), channel_id=1, source_target_pairs={{0,16},{4,20},{8,24},{12,28},{16,0},{20,4},{24,8},{28,12},{1,17},{... | collective-permute-start | bytes 884744 | tf_op jit(solution)/shard_map/ppermute | solution.py:407
  135.7 8.3 %collective-permute-start.13 = (bf16[8,144,128]{2,1,0:T(8,128)(2,1)S(1)}, bf16[8,144,128]{2,1,0:T(8,128)(2,1)S(1)}, u32[]{:S(2)}, u32[]{:S(2)}) collective-permute-start(bf16[8,144,128]{2,1,0:T(8,128)(2,1)S(1)} %totals.7), channel_id=1, source_target_pairs={{0,2},{1,3},{2,0},{3,1},{4,6},{5,7},{6,4},{7,5},{8,10},{9,11},{10,... | collective-permute-start | bytes 884744 | tf_op jit(solution)/shard_map/ppermute | solution.py:413
  136.3 15.8 %collective-permute-start.16 = (bf16[128,1024]{1,0:T(8,128)(2,1)S(1)}, bf16[128,1024]{1,0:T(8,128)(2,1)S(1)}, u32[]{:S(2)}, u32[]{:S(2)}) collective-permute-start(bf16[128,1024]{1,0:T(8,128)(2,1)S(1)} %copy-done.42), channel_id=1, source_target_pairs={{0,4},{4,8},{8,12},{12,0},{16,20},{20,24},{24,28},{28,16},{1,5},{5... | collective-permute-start | bytes 786440 | tf_op jit(solution)/shard_map/ppermute | solution.py:402
  138.2 13.9 %collective-permute-start.15 = (bf16[128,1024]{1,0:T(8,128)(2,1)S(1)}, bf16[128,1024]{1,0:T(8,128)(2,1)S(1)}, u32[]{:S(2)}, u32[]{:S(2)}) collective-permute-start(bf16[128,1024]{1,0:T(8,128)(2,1)S(1)} %copy-done.41), channel_id=1, source_target_pairs={{0,8},{4,12},{8,0},{12,4},{16,24},{20,28},{24,16},{28,20},{1,9},{5... | collective-permute-start | bytes 786440 | tf_op jit(solution)/shard_map/ppermute | solution.py:402
  141.5 12.1 %collective-permute-start.14 = (bf16[128,1024]{1,0:T(8,128)(2,1)S(1)}, bf16[128,1024]{1,0:T(8,128)(2,1)S(1)}, u32[]{:S(2)}, u32[]{:S(2)}) collective-permute-start(bf16[128,1024]{1,0:T(8,128)(2,1)S(1)} %copy-done.40), channel_id=1, source_target_pairs={{0,12},{4,0},{8,4},{12,8},{16,28},{20,16},{24,20},{28,24},{1,13},{... | collective-permute-start | bytes 786440 | tf_op jit(solution)/shard_map/ppermute | solution.py:402
  145.5 18.6 %collective-permute-start.20 = (bf16[8,144,128]{2,1,0:T(8,128)(2,1)S(1)}, bf16[8,144,128]{2,1,0:T(8,128)(2,1)S(1)}, u32[]{:S(2)}, u32[]{:S(2)}) collective-permute-start(bf16[8,144,128]{2,1,0:T(8,128)(2,1)S(1)} %get-tuple-element.93), channel_id=1, source_target_pairs={{0,16},{4,20},{8,24},{12,28},{16,0},{20,4},{24,8},{28,12},{1,17},{... | collective-permute-start | bytes 884744 | tf_op jit(solution)/shard_map/ppermute | solution.py:407
  160.6 10.2 %collective-permute-start.19 = (bf16[128,1024]{1,0:T(8,128)(2,1)S(1)}, bf16[128,1024]{1,0:T(8,128)(2,1)S(1)}, u32[]{:S(2)}, u32[]{:S(2)}) collective-permute-start(bf16[128,1024]{1,0:T(8,128)(2,1)S(1)} %copy-done.39), channel_id=1, source_target_pairs={{0,4},{4,8},{8,12},{12,0},{16,20},{20,24},{24,28},{28,16},{1,5},{5... | collective-permute-start | bytes 786440 | tf_op jit(solution)/shard_map/ppermute | solution.py:402
  161.0 9.8 %collective-permute-start.18 = (bf16[128,1024]{1,0:T(8,128)(2,1)S(1)}, bf16[128,1024]{1,0:T(8,128)(2,1)S(1)}, u32[]{:S(2)}, u32[]{:S(2)}) collective-permute-start(bf16[128,1024]{1,0:T(8,128)(2,1)S(1)} %copy-done.38), channel_id=1, source_target_pairs={{0,8},{4,12},{8,0},{12,4},{16,24},{20,28},{24,16},{28,20},{1,9},{5... | collective-permute-start | bytes 786440 | tf_op jit(solution)/shard_map/ppermute | solution.py:402
  162.4 12.1 %collective-permute-start.17 = (bf16[128,1024]{1,0:T(8,128)(2,1)S(1)}, bf16[128,1024]{1,0:T(8,128)(2,1)S(1)}, u32[]{:S(2)}, u32[]{:S(2)}) collective-permute-start(bf16[128,1024]{1,0:T(8,128)(2,1)S(1)} %copy-done.37), channel_id=1, source_target_pairs={{0,12},{4,0},{8,4},{12,8},{16,28},{20,16},{24,20},{28,24},{1,13},{... | collective-permute-start | bytes 786440 | tf_op jit(solution)/shard_map/ppermute | solution.py:402
  174.6 28.1 %all-to-all-start.1 = ((bf16[4,128,512]{2,1,0:T(8,128)(2,1)}), bf16[4,128,512]{2,1,0:T(8,128)(2,1)S(1)}, u32[]{:S(2)}, u32[]{:S(2)}) async-start(bf16[4,128,512]{2,1,0:T(8,128)(2,1)} %get-tuple-element.98), calls=%async_computation.1 | async-start | bytes 1048576 | tf_op jit(solution)/shard_map/all_to_all | solution.py:399
  178.2 15.3 %collective-permute-start.24 = (bf16[2,4,32,128]{3,2,1,0:T(8,128)(2,1)S(1)}, bf16[2,4,32,128]{3,2,1,0:T(8,128)(2,1)S(1)}, u32[]{:S(2)}, u32[]{:S(2)}) collective-permute-start(bf16[2,4,32,128]{3,2,1,0:T(8,128)(2,1)S(1)} %get-tuple-element.109), channel_id=1, source_target_pairs={{0,16},{1,17},{2,18},{3,19},{4,20},{5,21},{6,22},{7,23},{8,24},{9,... | collective-permute-start | bytes 196616 | tf_op jit(solution)/shard_map/ppermute | solution.py:421
  185.1 9.3 %collective-permute-start.25 = (bf16[2,4,32,128]{3,2,1,0:T(8,128)(2,1)S(1)}, bf16[2,4,32,128]{3,2,1,0:T(8,128)(2,1)S(1)}, u32[]{:S(2)}, u32[]{:S(2)}) collective-permute-start(bf16[2,4,32,128]{3,2,1,0:T(8,128)(2,1)S(1)} %get-tuple-element.110), channel_id=1, source_target_pairs={{0,17},{1,18},{2,19},{3,16},{4,21},{5,22},{6,23},{7,20},{8,25},{9,... | collective-permute-start | bytes 196616 | tf_op jit(solution)/shard_map/ppermute | solution.py:421
  189.3 10.5 %collective-permute-start.26 = (bf16[2,4,32,128]{3,2,1,0:T(8,128)(2,1)S(1)}, bf16[2,4,32,128]{3,2,1,0:T(8,128)(2,1)S(1)}, u32[]{:S(2)}, u32[]{:S(2)}) collective-permute-start(bf16[2,4,32,128]{3,2,1,0:T(8,128)(2,1)S(1)} %get-tuple-element.111), channel_id=1, source_target_pairs={{0,18},{1,19},{2,16},{3,17},{4,22},{5,23},{6,20},{7,21},{8,26},{9,... | collective-permute-start | bytes 196616 | tf_op jit(solution)/shard_map/ppermute | solution.py:421
  191.9 9.4 %collective-permute-start.27 = (bf16[2,4,32,128]{3,2,1,0:T(8,128)(2,1)S(1)}, bf16[2,4,32,128]{3,2,1,0:T(8,128)(2,1)S(1)}, u32[]{:S(2)}, u32[]{:S(2)}) collective-permute-start(bf16[2,4,32,128]{3,2,1,0:T(8,128)(2,1)S(1)} %get-tuple-element.108), channel_id=1, source_target_pairs={{0,19},{1,16},{2,17},{3,18},{4,23},{5,20},{6,21},{7,22},{8,27},{9,... | collective-permute-start | bytes 196616 | tf_op jit(solution)/shard_map/ppermute | solution.py:421
  192.2 9.0 %collective-permute-start.21 = (bf16[2,4,32,128]{3,2,1,0:T(8,128)(2,1)S(1)}, bf16[2,4,32,128]{3,2,1,0:T(8,128)(2,1)S(1)}, u32[]{:S(2)}, u32[]{:S(2)}) collective-permute-start(bf16[2,4,32,128]{3,2,1,0:T(8,128)(2,1)S(1)} %get-tuple-element.114), channel_id=1, source_target_pairs={{0,1},{1,2},{2,3},{3,0},{4,5},{5,6},{6,7},{7,4},{8,9},{9,10},{10,1... | collective-permute-start | bytes 196616 | tf_op jit(solution)/shard_map/ppermute | solution.py:410
  (49 other events, 668.9 us)

commit v14 on v10

--- a/solution.py
+++ b/solution.py
@@ -30,7 +30,7 @@
 
 
 def turned(array):
-    return array.astype(F32).T.astype(array.dtype)
+    return array.T
 
 
 def column(row, width):
@@ -158,12 +158,12 @@
         gather(table, base, k_refs, k_all)
         gather(table, base, v_refs, v_all)
 
-    for u in range(out.shape[0]):
-        weight = weight_rows(w_ref, u)
-        feats = features(weight[weight.shape[0] // 2 :], k_all[...]).astype(BF16)
-        out[u, :hd, :] = nn(feats, v_all[...]).astype(BF16)
-        ones = jnp.ones((EXT, feats.shape[1]), BF16)
-        out[u, hd:, :] = thirds(nt(ones, feats)[:1])
+    ones = jnp.ones((EXT, k_all.shape[0]), BF16)
+    weights = [weight_rows(w_ref, u) for u in range(PAIR)]
+    feats = [features(w[w.shape[0] // 2 :], k_all[...]).astype(BF16) for w in weights]
+    for u in range(PAIR):
+        out[u, :hd, :] = nn(feats[u], v_all[...]).astype(BF16)
+        out[u, hd:, :] = thirds(nt(ones, feats[u])[:1])
 
 
 def block_kernel(part, base, table, *refs):
@@ -192,53 +192,71 @@
         masked = jnp.where(earlier, array[begin:], 0.0)
         return masked if begin == 0 else jnp.concatenate([array[:begin], masked], axis=0)
 
-    for u in range(PAIR):
-        weight = weight_rows(w_ref, u)
-        half = weight.shape[0] // 2
-        lanes = slice(u * hd, (u + 1) * hd)
-        q_feat = features(weight[:half], q_all[:, lanes])
-        k_low = features(weight[half:], k_all[...]).astype(BF16)
-        q_low = q_feat.astype(BF16)
-        k_turned = turned(k_low)
-        state = st_ref[u, :hd, :]
-        state_turned = turned(state)
-        norm = column(whole_row(st_ref[u, hd:, :]), TILE)
-        g_turned = g_all[:, lanes].astype(F32).T
-        back = []
-        dkey = [jnp.zeros((2 * half, TILE), F32) for _ in range(BLK // TILE)]
-        dvalue = [jnp.zeros((hd, TILE), F32) for _ in range(BLK // TILE)]
-        suffix = jnp.zeros((2 * half, hd), F32)
-        suffix_norm = jnp.zeros((2 * half, 1), F32)
-        for j in range(BLK // TILE):
-            begin, end = j * TILE, (j + 1) * TILE
-            own = q_low[:, begin:end]
-            own_wide = own.astype(F32)
-            scores = causal(nn(k_turned[:end], own), begin)
-            scores_low = scores.astype(BF16)
-            numerator = nn(state_turned, own) + nn(vt_all[:, :end], scores_low)
-            denominator = jnp.sum(own_wide * norm, axis=0, keepdims=True) + jnp.sum(
-                scores, axis=0, keepdims=True
+    heads = range(PAIR)
+    lanes = [slice(u * hd, (u + 1) * hd) for u in heads]
+    weight = [weight_rows(w_ref, u) for u in heads]
+    half = weight[0].shape[0] // 2
+    q_feat = [features(weight[u][:half], q_all[:, lanes[u]]) for u in heads]
+    k_low = [features(weight[u][half:], k_all[...]).astype(BF16) for u in heads]
+    q_low = [q_feat[u].astype(BF16) for u in heads]
+    k_turned = [turned(k_low[u]) for u in heads]
+    state = [st_ref[u, :hd, :] for u in heads]
+    state_turned = [turned(state[u]) for u in heads]
+    norm = [column(whole_row(st_ref[u, hd:, :]), TILE) for u in heads]
+    g_turned = [g_all[:, lanes[u]].T for u in heads]
+    back = [[] for u in heads]
+    dkey = [[jnp.zeros((2 * half, TILE), F32) for _ in range(BLK // TILE)] for u in heads]
+    dvalue = [[jnp.zeros((hd, TILE), F32) for _ in range(BLK // TILE)] for u in heads]
+    suffix = [jnp.zeros((2 * half, hd), F32) for u in heads]
+    suffix_norm = [jnp.zeros((2 * half, 1), F32) for u in heads]
+    for j in range(BLK // TILE):
+        begin, end = j * TILE, (j + 1) * TILE
+        own = [q_low[u][:, begin:end] for u in heads]
+        scores = [causal(nn(k_turned[u][:end], own[u]), begin) for u in heads]
+        scores_low = [scores[u].astype(BF16) for u in heads]
+        inverse = [
+            1.0
+            / (
+                jnp.sum(own[u].astype(F32) * norm[u], axis=0, keepdims=True)
+                + jnp.sum(scores[u], axis=0, keepdims=True)
             )
-            inverse = 1.0 / denominator
-            scaled = g_turned[:, begin:end] * inverse
-            scaled_low = scaled.astype(BF16)
-            norm_grad = -jnp.sum(scaled * (numerator * inverse), axis=0, keepdims=True)
-            dscores = causal(nn(v_all[:end, :], scaled_low) + norm_grad, begin).astype(BF16)
-            dquery = nn(state, scaled_low) + norm * norm_grad + nn(k_low[:, :end], dscores)
-            back.append(feature_back(q_feat[:, begin:end], dquery))
+            for u in heads
+        ]
+        scaled = [g_turned[u][:, begin:end].astype(F32) * inverse[u] for u in heads]
+        scaled_low = [scaled[u].astype(BF16) for u in heads]
+        numerator = [
+            nn(state_turned[u], own[u]) + nn(vt_all[:, :end], scores_low[u]) for u in heads
+        ]
+        products = [nn(v_all[:end, :], scaled_low[u]) for u in heads]
+        norm_grad = [
+            -jnp.sum(scaled[u] * (numerator[u] * inverse[u]), axis=0, keepdims=True)
+            for u in heads
+        ]
+        dscores = [causal(products[u] + norm_grad[u], begin).astype(BF16) for u in heads]
+        dquery = [
+            nn(state[u], scaled_low[u])
+            + norm[u] * norm_grad[u]
+            + nn(k_low[u][:, :end], dscores[u])
+            for u in heads
+        ]
+        for u in heads:
+            back[u].append(feature_back(q_feat[u][:, begin:end], dquery[u]))
             for i in range(j + 1):
                 rows = slice(i * TILE, (i + 1) * TILE)
-                dkey[i] = dkey[i] + nt(own, dscores[rows])
-                dvalue[i] = dvalue[i] + nt(scaled_low, scores_low[rows])
-            suffix = suffix + nt(own, scaled_low)
-            suffix_norm = suffix_norm + jnp.sum(own_wide * norm_grad, axis=1, keepdims=True)
-        dlog = jnp.concatenate(back, axis=1)
-        gq_all[:, lanes] = nn(turned(dlog), weight[:half]).astype(BF16)
-        maps.append(nn(dlog, q_all[:, lanes]))
-        dk_ref[u] = jnp.concatenate(dkey, axis=1)
-        dv_ref[...] += jnp.concatenate(dvalue, axis=1)
-        sx_ref[u, :hd, :] = suffix.astype(BF16)
-        sx_ref[u, hd:, :] = thirds(jnp.broadcast_to(suffix_norm, (2 * half, 2 * half)).T[:1])
+                dkey[u][i] = dkey[u][i] + nt(own[u], dscores[u][rows])
+                dvalue[u][i] = dvalue[u][i] + nt(scaled_low[u], scores_low[u][rows])
+            suffix[u] = suffix[u] + nt(own[u], scaled_low[u])
+            suffix_norm[u] = suffix_norm[u] + jnp.sum(
+                own[u].astype(F32) * norm_grad[u], axis=1, keepdims=True
+            )
+    for u in heads:
+        dlog = jnp.concatenate(back[u], axis=1)
+        gq_all[:, lanes[u]] = nn(turned(dlog), weight[u][:half]).astype(BF16)
+        maps.append(nn(dlog, q_all[:, lanes[u]]))
+        dk_ref[u] = jnp.concatenate(dkey[u], axis=1)
+        dv_ref[...] += jnp.concatenate(dvalue[u], axis=1)
+        sx_ref[u, :hd, :] = suffix[u].astype(BF16)
+        sx_ref[u, hd:, :] = thirds(jnp.broadcast_to(suffix_norm[u], (2 * half, 2 * half)).T[:1])
     gm_ref[0] = jnp.concatenate(maps, axis=0).T.astype(gm_ref.dtype)
     for r, ref in enumerate(gq_refs):
         rows = ref.shape[0]
@@ -259,20 +277,22 @@
         vt_all[...] = turned(v_all[...])
         total[...] = dv_ref[...]
 
-    maps = []
-    for u in range(PAIR):
-        weight = weight_rows(w_ref, u)
-        half = weight.shape[0] // 2
-        weight = weight[half:]
-        feats = features(weight, k_all[...])
-        suffix = sx_ref[u, :hd, :]
-        norm = column(whole_row(sx_ref[u, hd:, :]), BLK)
-        dlog = feature_back(feats, dk_ref[u] + nn(suffix, vt_all[...]) + norm)
+    heads = range(PAIR)
+    weight = [weight_rows(w_ref, u) for u in heads]
+    half = weight[0].shape[0] // 2
+    feats = [features(weight[u][half:], k_all[...]) for u in heads]
+    suffix = [sx_ref[u, :hd, :] for u in heads]
+    upstream = [
+        dk_ref[u] + nn(suffix[u], vt_all[...]) + column(whole_row(sx_ref[u, hd:, :]), BLK)
+        for u in heads
+    ]
+    dlog = [feature_back(feats[u], upstream[u]) for u in heads]
+    maps = [nn(dlog[u], k_all[...]) for u in heads]
+    for u in heads:
         at = pl.ds(pl.multiple_of((step * PAIR + u) * half, half), half)
-        logs[at, :] = dlog
-        weights[at, :] = weight
-        maps.append(nn(dlog, k_all[...]))
-        total[...] += nn(turned(suffix), feats.astype(BF16))
+        logs[at, :] = dlog[u]
+        weights[at, :] = weight[u][half:]
+    total[...] += sum(nn(turned(suffix[u]), feats[u].astype(BF16)) for u in heads)
     gm_ref[0] = jnp.concatenate(maps, axis=0).T.astype(gm_ref.dtype)
 
     @pl.when(step == pl.num_programs(0) - 1)

time: 182 us -> 179 us (0.984)
  starting transfers between devices: 49.2 us -> 60.4 us
  Pallas kernels: 64.5 us -> 54 us
  waiting for transfers between devices: 49 us -> 44 us
    pallas_call x6, Pallas kernels: 51.3 us -> 40.8 us  [call(): pl.pallas_call(functools.partial(kernel, part, base['sorted']), out_shape...]
    ppermute x15, starting transfers between devices: 21.2 us -> 27.6 us  [around(): lax.ppermute(array, 'ctx', [(d, d // part * part + (d + shift) % part) fo...]
    ppermute x4, waiting for transfers between devices: 14.6 us -> 10.7 us  [twin(): return lax.ppermute(array, 'fsdp', [(d, d ^ bit) for d in range(fsdp)])]
    ppermute x5, waiting for transfers between devices: 17.5 us -> 14.2 us  [across(): lax.ppermute(array, 'ctx', [(d, (d + shift * part) % ctx) for d in range(...]
    ppermute x4, starting transfers between devices: 6.01 us -> 9.18 us  [twin(): return lax.ppermute(array, 'fsdp', [(d, d ^ bit) for d in range(fsdp)])]
    ppermute x15, waiting for transfers between devices: 12.2 us -> 15.1 us  [around(): lax.ppermute(array, 'ctx', [(d, d // part * part + (d + shift) % part) fo...]
    ppermute x4, starting transfers between devices: 9.71 us -> 7.27 us  [apart(): return lax.ppermute(array, ('ctx', 'fsdp'), moves)]
    ppermute x5, starting transfers between devices: 5.9 us -> 7.98 us  [across(): lax.ppermute(array, 'ctx', [(d, (d + shift * part) % ctx) for d in range(...]
  transfers between devices with their start and end apart: 32 -> 32, of which waited for: 12 -> 14; matrix products, arithmetic and copies ran while one was open for 0% -> 0% of each run, Pallas kernels for 31% -> 26%
where the time goes in v14:
time: 179 us; the launch traced here: 177 us
  starting transfers between devices  60.4 us (34%)
  Pallas kernels  54 us (30%)
  waiting for transfers between devices  44 us (25%)
  blocking collectives  9.99 us (6%)
  local copies, waits for them, and re-layouts  7.14 us (4%)
    pallas_call x6, Pallas kernels, call(): pl.pallas_call(functools.partial(kernel, part, base['sorted']), out_shape...  40.8 us
    ppermute x15, starting transfers between devices, around(): lax.ppermute(array, 'ctx', [(d, d // part * part + (d + shift) % part) fo...  27.6 us
    ppermute x15, waiting for transfers between devices, around(): lax.ppermute(array, 'ctx', [(d, d // part * part + (d + shift) % part) fo...  15.1 us
    ppermute x5, waiting for transfers between devices, across(): lax.ppermute(array, 'ctx', [(d, (d + shift * part) % ctx) for d in range(...  14.2 us
    ppermute x4, waiting for transfers between devices, twin(): return lax.ppermute(array, 'fsdp', [(d, d ^ bit) for d in range(fsdp)])  10.7 us
    all_gather x1, blocking collectives, shards(): maps = lax.all_gather(near_maps, 'fsdp')  9.99 us
    ppermute x4, starting transfers between devices, twin(): return lax.ppermute(array, 'fsdp', [(d, d ^ bit) for d in range(fsdp)])  9.18 us
    ppermute x5, starting transfers between devices, across(): lax.ppermute(array, 'ctx', [(d, (d + shift * part) % ctx) for d in range(...  7.98 us
  transfers between devices with their start and end apart: 32, of which 14 were waited for; matrix products, arithmetic and copies ran while one was open for 0% of the time, Pallas kernels for 26%

profile of v14, /device:TPU:1, one launch (start us, length us, event | category | flops | bytes accessed | tf_op | source)
XLA Modules:
  0.0 177.2 jit_solution(17332917146345784955)
XLA Ops:
  8.9 2.4 %collective-permute-start.3 = (bf16[8,32,128]{2,1,0:T(8,128)(2,1)S(1)}, bf16[8,32,128]{2,1,0:T(8,128)(2,1)S(1)}, u32[]{:S(2)}, u32[]{:S(2)}) collective-permute-start(bf16[8,32,128]{2,1,0:T(8,128)(2,1)S(1)} %pad_maximum_fusion.2), channel_id=1, source_target_pairs={{0,16},{4,20},{8,24},{12,28},{16,0},{20,4},{24,8},{28,12},{1,17},{... | collective-permute-start | bytes 196616 | tf_op jit(solution)/shard_map/ppermute | solution.py:402
  11.3 2.4 %collective-permute-done.3 = bf16[8,32,128]{2,1,0:T(8,128)(2,1)S(1)} collective-permute-done((bf16[8,32,128]{2,1,0:T(8,128)(2,1)S(1)}, bf16[8,32,128]{2,1,0:T(8,128)(2,1)S(1)}, u32[]{:S(2)}, u32[]{:S(2)}) %collective-permute-start.3) | collective-permute-done | bytes 65568 | tf_op jit(solution)/shard_map/ppermute | solution.py:402
  20.2 10.0 %all-gather = bf16[8,8,32,128]{3,2,1,0:T(8,128)(2,1)S(1)} all-gather(bf16[2,8,32,128]{3,2,1,0:T(8,128)(2,1)S(1)} %pad_maximum_fusion.1), channel_id=2, replica_groups=mesh['ctx'=8,'fsdp'=4] {'fsdp'}, dimensions={0}, use_global_device_ids=true | all-gather | bytes 655360 | tf_op jit(solution)/shard_map/all_gather | solution.py:445
  30.2 2.8 %states.3 = bf16[8,144,128]{2,1,0:T(8,128)(2,1)S(1)} custom-call(s32[49]{0:T(128)S(1)} %stack.194.table, bf16[128,512]{1,0:T(8,128)(2,1)S(1)} %get-tuple-element.61.refs_0_.refs_4_, bf16[128,512]{1,0:T(8,128)(2,1)S(1)} %collective-permute-done.refs_1_.refs_5_, bf16[128,512]{1,0:T(8,128)(2,1)S(1)} %collective-permute-done.1.refs_2_.refs_6_, ...), custom_call_target="tpu_custom_call" | custom-call | flops 1000 | bytes 1000 | tf_op jit(solution)/shard_map/states/pallas_call | solution.py:481
  33.2 2.8 %states.2.refs_0_ = bf16[8,144,128]{2,1,0:T(8,128)(2,1)S(1)} custom-call(s32[49]{0:T(128)S(1)} %stack.194.table, bf16[128,512]{1,0:T(8,128)(2,1)S(1)} %get-tuple-element.61.refs_0_.refs_4_, bf16[128,512]{1,0:T(8,128)(2,1)S(1)} %collective-permute-done.refs_1_.refs_5_, bf16[128,512]{1,0:T(8,128)(2,1)S(1)} %collective-permute-done.1.refs_2_.refs_6_, ...), custom_call_target="tpu_custom_call" | custom-call | flops 1000 | bytes 1000 | tf_op jit(solution)/shard_map/states/pallas_call | solution.py:481
  36.1 5.7 %collective-permute-done.6.refs_11_.refs_15_ = bf16[128,2048]{1,0:T(8,128)(2,1)S(1)} collective-permute-done((bf16[128,2048]{1,0:T(8,128)(2,1)S(1)}, bf16[128,2048]{1,0:T(8,128)(2,1)S(1)}, u32[]{:S(2)}, u32[]{:S(2)}) %collective-permute-start.6) | collective-permute-done | bytes 524320 | tf_op jit(solution)/shard_map/ppermute | solution.py:397
  41.7 3.6 %collective-permute-done.7.refs_1_ = bf16[8,144,128]{2,1,0:T(8,128)(2,1)S(1)} collective-permute-done((bf16[8,144,128]{2,1,0:T(8,128)(2,1)S(1)}, bf16[8,144,128]{2,1,0:T(8,128)(2,1)S(1)}, u32[]{:S(2)}, u32[]{:S(2)}) %collective-permute-start.7) | collective-permute-done | bytes 294944 | tf_op jit(solution)/shard_map/ppermute | solution.py:402
  46.0 2.8 %collective-permute-start.8 = (bf16[8,144,128]{2,1,0:T(8,128)(2,1)S(1)}, bf16[8,144,128]{2,1,0:T(8,128)(2,1)S(1)}, u32[]{:S(2)}, u32[]{:S(2)}) collective-permute-start(bf16[8,144,128]{2,1,0:T(8,128)(2,1)S(1)} %totals.4.refs_0_), channel_id=1, source_target_pairs={{0,1},{1,0},{2,3},{3,2},{4,5},{5,4},{6,7},{7,6},{8,9},{9,8},{10,11... | collective-permute-start | bytes 884744 | tf_op jit(solution)/shard_map/ppermute | solution.py:408
  51.9 7.0 %collective-permute-done.9.refs_3_ = bf16[8,144,128]{2,1,0:T(8,128)(2,1)S(1)} collective-permute-done((bf16[8,144,128]{2,1,0:T(8,128)(2,1)S(1)}, bf16[8,144,128]{2,1,0:T(8,128)(2,1)S(1)}, u32[]{:S(2)}, u32[]{:S(2)}) %collective-permute-start.9) | collective-permute-done | bytes 294944 | tf_op jit(solution)/shard_map/ppermute | solution.py:408
  59.8 3.2 %collective-permute-start.13 = (bf16[8,144,128]{2,1,0:T(8,128)(2,1)S(1)}, bf16[8,144,128]{2,1,0:T(8,128)(2,1)S(1)}, u32[]{:S(2)}, u32[]{:S(2)}) collective-permute-start(bf16[8,144,128]{2,1,0:T(8,128)(2,1)S(1)} %get-tuple-element.79), channel_id=1, source_target_pairs={{0,16},{4,20},{8,24},{12,28},{16,0},{20,4},{24,8},{28,12},{1,17},{... | collective-permute-start | bytes 884744 | tf_op jit(solution)/shard_map/ppermute | solution.py:402
  67.2 8.3 %collective-permute-done.13.refs_17_ = bf16[8,144,128]{2,1,0:T(8,128)(2,1)S(1)} collective-permute-done((bf16[8,144,128]{2,1,0:T(8,128)(2,1)S(1)}, bf16[8,144,128]{2,1,0:T(8,128)(2,1)S(1)}, u32[]{:S(2)}, u32[]{:S(2)}) %collective-permute-start.13) | collective-permute-done | bytes 294944 | tf_op jit(solution)/shard_map/ppermute | solution.py:402
  76.2 12.8 %blocks.3 = (bf16[128,1024]{1,0:T(8,128)(2,1)}, bf16[128,1024]{1,0:T(8,128)(2,1)}, bf16[128,1024]{1,0:T(8,128)(2,1)}, bf16[128,1024]{1,0:T(8,128)(2,1)}, f32[8,1...) custom-call(s32[49]{0:T(128)} %copy-done.26, ...), custom_call_target="tpu_custom_call" | custom-call | flops 1000 | bytes 1000 | tf_op jit(solution)/shard_map/blocks/pallas_call | solution.py:481
  91.5 12.9 %blocks.2 = (bf16[128,1024]{1,0:T(8,128)(2,1)}, bf16[128,1024]{1,0:T(8,128)(2,1)}, bf16[128,1024]{1,0:T(8,128)(2,1)}, bf16[128,1024]{1,0:T(8,128)(2,1)}, f32[8,1...) custom-call(s32[49]{0:T(128)} %copy-done.26, ...), custom_call_target="tpu_custom_call" | custom-call | flops 1000 | bytes 1000 | tf_op jit(solution)/shard_map/blocks/pallas_call | solution.py:481
  106.2 3.8 %collective-permute-start.15 = (bf16[8,144,128]{2,1,0:T(8,128)(2,1)S(1)}, bf16[8,144,128]{2,1,0:T(8,128)(2,1)S(1)}, u32[]{:S(2)}, u32[]{:S(2)}) collective-permute-start(bf16[8,144,128]{2,1,0:T(8,128)(2,1)S(1)} %totals.6.refs_0_), channel_id=1, source_target_pairs={{0,1},{1,0},{2,3},{3,2},{4,5},{5,4},{6,7},{7,6},{8,9},{9,8},{10,11... | collective-permute-start | bytes 884744 | tf_op jit(solution)/shard_map/ppermute | solution.py:408
  113.1 4.5 %collective-permute-start.19 = (bf16[128,1024]{1,0:T(8,128)(2,1)S(1)}, bf16[128,1024]{1,0:T(8,128)(2,1)S(1)}, u32[]{:S(2)}, u32[]{:S(2)}) collective-permute-start(bf16[128,1024]{1,0:T(8,128)(2,1)S(1)} %copy-done.44), channel_id=1, source_target_pairs={{0,4},{4,8},{8,12},{12,0},{16,20},{20,24},{24,28},{28,16},{1,5},{5... | collective-permute-start | bytes 786440 | tf_op jit(solution)/shard_map/ppermute | solution.py:397
  124.4 4.2 %collective-permute-done.17 = bf16[128,1024]{1,0:T(8,128)(2,1)S(1)} collective-permute-done((bf16[128,1024]{1,0:T(8,128)(2,1)S(1)}, bf16[128,1024]{1,0:T(8,128)(2,1)S(1)}, u32[]{:S(2)}, u32[]{:S(2)}) %collective-permute-start.17) | collective-permute-done | bytes 262176 | tf_op jit(solution)/shard_map/ppermute | solution.py:397
  130.3 4.7 %keys.2 = (bf16[4,128,512]{2,1,0:T(8,128)(2,1)}, bf16[4,128,128]{2,1,0:T(8,128)(2,1)S(1)}) custom-call(s32[49]{0:T(128)S(1)} %copy-done.27, bf16[128,512]{1,0:T(8,128)(2,1)S(1)} %copy-done.5, bf16[128,512]{1,0:T(8,128)(2,1)S(1)} %copy-done.7, bf16[128,512]{1,0:T(8,128)(2,1)S(1)} %copy-done.9, bf16[128,512]{1,0:T(8,128)(2,1)S(1)} %copy-done.11, ...), custom_call_target="tpu_custom_call" | custom-call | flops 1000 | bytes 1000 | tf_op jit(solution)/shard_map/keys/pallas_call | solution.py:481
  135.1 8.4 %collective-permute-start.22 = (bf16[128,1024]{1,0:T(8,128)(2,1)S(1)}, bf16[128,1024]{1,0:T(8,128)(2,1)S(1)}, u32[]{:S(2)}, u32[]{:S(2)}) collective-permute-start(bf16[128,1024]{1,0:T(8,128)(2,1)S(1)} %copy-done.41), channel_id=1, source_target_pairs={{0,4},{4,8},{8,12},{12,0},{16,20},{20,24},{24,28},{28,16},{1,5},{5... | collective-permute-start | bytes 786440 | tf_op jit(solution)/shard_map/ppermute | solution.py:397
  144.7 4.8 %keys.3 = (bf16[4,128,512]{2,1,0:T(8,128)(2,1)}, bf16[4,128,128]{2,1,0:T(8,128)(2,1)S(1)}) custom-call(s32[49]{0:T(128)S(1)} %copy-done.27, bf16[128,512]{1,0:T(8,128)(2,1)S(1)} %copy-done.5, bf16[128,512]{1,0:T(8,128)(2,1)S(1)} %copy-done.7, bf16[128,512]{1,0:T(8,128)(2,1)S(1)} %copy-done.9, ...), custom_call_target="tpu_custom_call", output_to_operand_aliasing={{0}: (13, {})} | custom-call | flops 1000 | bytes 1000 | tf_op jit(solution)/shard_map/keys/pallas_call | solution.py:481
  149.5 3.3 %collective-permute-done.20 = bf16[128,1024]{1,0:T(8,128)(2,1)S(1)} collective-permute-done((bf16[128,1024]{1,0:T(8,128)(2,1)S(1)}, bf16[128,1024]{1,0:T(8,128)(2,1)S(1)}, u32[]{:S(2)}, u32[]{:S(2)}) %collective-permute-start.20) | collective-permute-done | bytes 262176 | tf_op jit(solution)/shard_map/ppermute | solution.py:397
  152.8 4.9 %all-to-all-start = ((bf16[4,128,512]{2,1,0:T(8,128)(2,1)}), bf16[4,128,512]{2,1,0:T(8,128)(2,1)S(1)}, u32[]{:S(2)}, u32[]{:S(2)}) async-start(bf16[4,128,512]{2,1,0:T(8,128)(2,1)} %get-tuple-element.106), calls=%async_computation | async-start | bytes 1048576 | tf_op jit(solution)/shard_map/all_to_all | solution.py:394
  162.2 2.9 %collective-permute-start.29 = (bf16[2,4,32,128]{3,2,1,0:T(8,128)(2,1)S(1)}, bf16[2,4,32,128]{3,2,1,0:T(8,128)(2,1)S(1)}, u32[]{:S(2)}, u32[]{:S(2)}) collective-permute-start(bf16[2,4,32,128]{3,2,1,0:T(8,128)(2,1)S(1)} %get-tuple-element.119), channel_id=1, source_target_pairs={{0,18},{1,19},{2,16},{3,17},{4,22},{5,23},{6,20},{7,21},{8,26},{9,... | collective-permute-start | bytes 196616 | tf_op jit(solution)/shard_map/ppermute | solution.py:416
  165.1 2.9 %collective-permute-start.24 = (bf16[2,4,32,128]{3,2,1,0:T(8,128)(2,1)S(1)}, bf16[2,4,32,128]{3,2,1,0:T(8,128)(2,1)S(1)}, u32[]{:S(2)}, u32[]{:S(2)}) collective-permute-start(bf16[2,4,32,128]{3,2,1,0:T(8,128)(2,1)S(1)} %get-tuple-element.122), channel_id=1, source_target_pairs={{0,1},{1,2},{2,3},{3,0},{4,5},{5,6},{6,7},{7,4},{8,9},{9,10},{10,1... | collective-permute-start | bytes 196616 | tf_op jit(solution)/shard_map/ppermute | solution.py:405
  170.5 2.8 %collective-permute-done.29.refs_5_ = bf16[2,4,32,128]{3,2,1,0:T(8,128)(2,1)S(1)} collective-permute-done((bf16[2,4,32,128]{3,2,1,0:T(8,128)(2,1)S(1)}, bf16[2,4,32,128]{3,2,1,0:T(8,128)(2,1)S(1)}, u32[]{:S(2)}, u32[]{:S(2)}) %collective-permute-start.29) | collective-permute-done | bytes 65568 | tf_op jit(solution)/shard_map/ppermute | solution.py:416
  (157 shorter events, 51.9 us)
Async XLA Ops:
  4.2 9.5 %collective-permute-start = (bf16[128,512]{1,0:T(8,128)(2,1)S(1)}, bf16[128,512]{1,0:T(8,128)(2,1)S(1)}, u32[]{:S(2)}, u32[]{:S(2)}) collective-permute-start(bf16[128,512]{1,0:T(8,128)(2,1)S(1)} %get-tuple-element.62), channel_id=1, source_target_pairs={{0,4},{4,8},{8,12},{12,0},{16,20},{20,24},{24,28},{28,16},{1,5},{5... | collective-permute-start | bytes 393224 | tf_op jit(solution)/shard_map/ppermute | solution.py:397
  6.3 7.4 %collective-permute-start.1 = (bf16[128,512]{1,0:T(8,128)(2,1)S(1)}, bf16[128,512]{1,0:T(8,128)(2,1)S(1)}, u32[]{:S(2)}, u32[]{:S(2)}) collective-permute-start(bf16[128,512]{1,0:T(8,128)(2,1)S(1)} %get-tuple-element.63), channel_id=1, source_target_pairs={{0,8},{4,12},{8,0},{12,4},{16,24},{20,28},{24,16},{28,20},{1,9},{5... | collective-permute-start | bytes 393224 | tf_op jit(solution)/shard_map/ppermute | solution.py:397
  14.9 21.2 %collective-permute-start.4 = (bf16[128,2048]{1,0:T(8,128)(2,1)S(1)}, bf16[128,2048]{1,0:T(8,128)(2,1)S(1)}, u32[]{:S(2)}, u32[]{:S(2)}) collective-permute-start(bf16[128,2048]{1,0:T(8,128)(2,1)S(1)} %get-tuple-element.67), channel_id=1, source_target_pairs={{0,4},{4,8},{8,12},{12,0},{16,20},{20,24},{24,28},{28,16},{1,5},{5... | collective-permute-start | bytes 1572872 | tf_op jit(solution)/shard_map/ppermute | solution.py:397
  16.2 19.8 %collective-permute-start.5 = (bf16[128,2048]{1,0:T(8,128)(2,1)S(1)}, bf16[128,2048]{1,0:T(8,128)(2,1)S(1)}, u32[]{:S(2)}, u32[]{:S(2)}) collective-permute-start(bf16[128,2048]{1,0:T(8,128)(2,1)S(1)} %get-tuple-element.68), channel_id=1, source_target_pairs={{0,8},{4,12},{8,0},{12,4},{16,24},{20,28},{24,16},{28,20},{1,9},{5... | collective-permute-start | bytes 1572872 | tf_op jit(solution)/shard_map/ppermute | solution.py:397
  18.4 23.3 %collective-permute-start.6 = (bf16[128,2048]{1,0:T(8,128)(2,1)S(1)}, bf16[128,2048]{1,0:T(8,128)(2,1)S(1)}, u32[]{:S(2)}, u32[]{:S(2)}) collective-permute-start(bf16[128,2048]{1,0:T(8,128)(2,1)S(1)} %get-tuple-element.69), channel_id=1, source_target_pairs={{0,12},{4,0},{8,4},{12,8},{16,28},{20,16},{24,20},{28,24},{1,13},{... | collective-permute-start | bytes 1572872 | tf_op jit(solution)/shard_map/ppermute | solution.py:397
  33.1 12.3 %collective-permute-start.7 = (bf16[8,144,128]{2,1,0:T(8,128)(2,1)S(1)}, bf16[8,144,128]{2,1,0:T(8,128)(2,1)S(1)}, u32[]{:S(2)}, u32[]{:S(2)}) collective-permute-start(bf16[8,144,128]{2,1,0:T(8,128)(2,1)S(1)} %states.3), channel_id=1, source_target_pairs={{0,16},{4,20},{8,24},{12,28},{16,0},{20,4},{24,8},{28,12},{1,17},{... | collective-permute-start | bytes 884744 | tf_op jit(solution)/shard_map/ppermute | solution.py:402
  50.7 8.3 %collective-permute-start.9 = (bf16[8,144,128]{2,1,0:T(8,128)(2,1)S(1)}, bf16[8,144,128]{2,1,0:T(8,128)(2,1)S(1)}, u32[]{:S(2)}, u32[]{:S(2)}) collective-permute-start(bf16[8,144,128]{2,1,0:T(8,128)(2,1)S(1)} %totals.5), channel_id=1, source_target_pairs={{0,2},{1,3},{2,0},{3,1},{4,6},{5,7},{6,4},{7,5},{8,10},{9,11},{10,... | collective-permute-start | bytes 884744 | tf_op jit(solution)/shard_map/ppermute | solution.py:408
  59.8 15.7 %collective-permute-start.13 = (bf16[8,144,128]{2,1,0:T(8,128)(2,1)S(1)}, bf16[8,144,128]{2,1,0:T(8,128)(2,1)S(1)}, u32[]{:S(2)}, u32[]{:S(2)}) collective-permute-start(bf16[8,144,128]{2,1,0:T(8,128)(2,1)S(1)} %get-tuple-element.79), channel_id=1, source_target_pairs={{0,16},{4,20},{8,24},{12,28},{16,0},{20,4},{24,8},{28,12},{1,17},{... | collective-permute-start | bytes 884744 | tf_op jit(solution)/shard_map/ppermute | solution.py:402
  64.9 24.2 %collective-permute-start.10 = (bf16[128,2048]{1,0:T(8,128)(2,1)S(1)}, bf16[128,2048]{1,0:T(8,128)(2,1)S(1)}, u32[]{:S(2)}, u32[]{:S(2)}) collective-permute-start(bf16[128,2048]{1,0:T(8,128)(2,1)S(1)} %get-tuple-element.74), channel_id=1, source_target_pairs={{0,4},{4,8},{8,12},{12,0},{16,20},{20,24},{24,28},{28,16},{1,5},{5... | collective-permute-start | bytes 1572872 | tf_op jit(solution)/shard_map/ppermute | solution.py:397
  65.5 23.6 %collective-permute-start.11 = (bf16[128,2048]{1,0:T(8,128)(2,1)S(1)}, bf16[128,2048]{1,0:T(8,128)(2,1)S(1)}, u32[]{:S(2)}, u32[]{:S(2)}) collective-permute-start(bf16[128,2048]{1,0:T(8,128)(2,1)S(1)} %get-tuple-element.75), channel_id=1, source_target_pairs={{0,8},{4,12},{8,0},{12,4},{16,24},{20,28},{24,16},{28,20},{1,9},{5... | collective-permute-start | bytes 1572872 | tf_op jit(solution)/shard_map/ppermute | solution.py:397
  66.8 23.9 %collective-permute-start.12 = (bf16[128,2048]{1,0:T(8,128)(2,1)S(1)}, bf16[128,2048]{1,0:T(8,128)(2,1)S(1)}, u32[]{:S(2)}, u32[]{:S(2)}) collective-permute-start(bf16[128,2048]{1,0:T(8,128)(2,1)S(1)} %get-tuple-element.76), channel_id=1, source_target_pairs={{0,12},{4,0},{8,4},{12,8},{16,28},{20,16},{24,20},{28,24},{1,13},{... | collective-permute-start | bytes 1572872 | tf_op jit(solution)/shard_map/ppermute | solution.py:397
  89.0 15.4 %collective-permute-start.14 = (bf16[8,144,128]{2,1,0:T(8,128)(2,1)}, bf16[8,144,128]{2,1,0:T(8,128)(2,1)S(1)}, u32[]{:S(2)}, u32[]{:S(2)}) collective-permute-start(bf16[8,144,128]{2,1,0:T(8,128)(2,1)} %get-tuple-element.80), channel_id=1, source_target_pairs={{0,16},{4,20},{8,24},{12,28},{16,0},{20,4},{24,8},{28,12},{1,17},{... | collective-permute-start | bytes 884744 | tf_op jit(solution)/shard_map/ppermute | solution.py:402
  111.8 8.3 %collective-permute-start.16 = (bf16[8,144,128]{2,1,0:T(8,128)(2,1)S(1)}, bf16[8,144,128]{2,1,0:T(8,128)(2,1)S(1)}, u32[]{:S(2)}, u32[]{:S(2)}) collective-permute-start(bf16[8,144,128]{2,1,0:T(8,128)(2,1)S(1)} %totals.7), channel_id=1, source_target_pairs={{0,2},{1,3},{2,0},{3,1},{4,6},{5,7},{6,4},{7,5},{8,10},{9,11},{10,... | collective-permute-start | bytes 884744 | tf_op jit(solution)/shard_map/ppermute | solution.py:408
  113.1 10.9 %collective-permute-start.19 = (bf16[128,1024]{1,0:T(8,128)(2,1)S(1)}, bf16[128,1024]{1,0:T(8,128)(2,1)S(1)}, u32[]{:S(2)}, u32[]{:S(2)}) collective-permute-start(bf16[128,1024]{1,0:T(8,128)(2,1)S(1)} %copy-done.44), channel_id=1, source_target_pairs={{0,4},{4,8},{8,12},{12,0},{16,20},{20,24},{24,28},{28,16},{1,5},{5... | collective-permute-start | bytes 786440 | tf_op jit(solution)/shard_map/ppermute | solution.py:397
  117.6 11.1 %collective-permute-start.17 = (bf16[128,1024]{1,0:T(8,128)(2,1)S(1)}, bf16[128,1024]{1,0:T(8,128)(2,1)S(1)}, u32[]{:S(2)}, u32[]{:S(2)}) collective-permute-start(bf16[128,1024]{1,0:T(8,128)(2,1)S(1)} %copy-done.42), channel_id=1, source_target_pairs={{0,12},{4,0},{8,4},{12,8},{16,28},{20,16},{24,20},{28,24},{1,13},{... | collective-permute-start | bytes 786440 | tf_op jit(solution)/shard_map/ppermute | solution.py:397
  121.7 23.0 %collective-permute-start.23 = (bf16[8,144,128]{2,1,0:T(8,128)(2,1)S(1)}, bf16[8,144,128]{2,1,0:T(8,128)(2,1)S(1)}, u32[]{:S(2)}, u32[]{:S(2)}) collective-permute-start(bf16[8,144,128]{2,1,0:T(8,128)(2,1)S(1)} %get-tuple-element.101), channel_id=1, source_target_pairs={{0,16},{4,20},{8,24},{12,28},{16,0},{20,4},{24,8},{28,12},{1,17},{... | collective-permute-start | bytes 884744 | tf_op jit(solution)/shard_map/ppermute | solution.py:402
  135.1 14.5 %collective-permute-start.22 = (bf16[128,1024]{1,0:T(8,128)(2,1)S(1)}, bf16[128,1024]{1,0:T(8,128)(2,1)S(1)}, u32[]{:S(2)}, u32[]{:S(2)}) collective-permute-start(bf16[128,1024]{1,0:T(8,128)(2,1)S(1)} %copy-done.41), channel_id=1, source_target_pairs={{0,4},{4,8},{8,12},{12,0},{16,20},{20,24},{24,28},{28,16},{1,5},{5... | collective-permute-start | bytes 786440 | tf_op jit(solution)/shard_map/ppermute | solution.py:397
  143.5 9.4 %collective-permute-start.20 = (bf16[128,1024]{1,0:T(8,128)(2,1)S(1)}, bf16[128,1024]{1,0:T(8,128)(2,1)S(1)}, u32[]{:S(2)}, u32[]{:S(2)}) collective-permute-start(bf16[128,1024]{1,0:T(8,128)(2,1)S(1)} %copy-done.39), channel_id=1, source_target_pairs={{0,12},{4,0},{8,4},{12,8},{16,28},{20,16},{24,20},{28,24},{1,13},{... | collective-permute-start | bytes 786440 | tf_op jit(solution)/shard_map/ppermute | solution.py:397
  152.8 22.9 %all-to-all-start = ((bf16[4,128,512]{2,1,0:T(8,128)(2,1)}), bf16[4,128,512]{2,1,0:T(8,128)(2,1)S(1)}, u32[]{:S(2)}, u32[]{:S(2)}) async-start(bf16[4,128,512]{2,1,0:T(8,128)(2,1)} %get-tuple-element.106), calls=%async_computation | async-start | bytes 1048576 | tf_op jit(solution)/shard_map/all_to_all | solution.py:394
  157.8 10.2 %collective-permute-start.27 = (bf16[2,4,32,128]{3,2,1,0:T(8,128)(2,1)S(1)}, bf16[2,4,32,128]{3,2,1,0:T(8,128)(2,1)S(1)}, u32[]{:S(2)}, u32[]{:S(2)}) collective-permute-start(bf16[2,4,32,128]{3,2,1,0:T(8,128)(2,1)S(1)} %get-tuple-element.117), channel_id=1, source_target_pairs={{0,16},{1,17},{2,18},{3,19},{4,20},{5,21},{6,22},{7,23},{8,24},{9,... | collective-permute-start | bytes 196616 | tf_op jit(solution)/shard_map/ppermute | solution.py:416
  160.0 8.0 %collective-permute-start.28 = (bf16[2,4,32,128]{3,2,1,0:T(8,128)(2,1)S(1)}, bf16[2,4,32,128]{3,2,1,0:T(8,128)(2,1)S(1)}, u32[]{:S(2)}, u32[]{:S(2)}) collective-permute-start(bf16[2,4,32,128]{3,2,1,0:T(8,128)(2,1)S(1)} %get-tuple-element.118), channel_id=1, source_target_pairs={{0,17},{1,18},{2,19},{3,16},{4,21},{5,22},{6,23},{7,20},{8,25},{9,... | collective-permute-start | bytes 196616 | tf_op jit(solution)/shard_map/ppermute | solution.py:416
  162.2 11.1 %collective-permute-start.29 = (bf16[2,4,32,128]{3,2,1,0:T(8,128)(2,1)S(1)}, bf16[2,4,32,128]{3,2,1,0:T(8,128)(2,1)S(1)}, u32[]{:S(2)}, u32[]{:S(2)}) collective-permute-start(bf16[2,4,32,128]{3,2,1,0:T(8,128)(2,1)S(1)} %get-tuple-element.119), channel_id=1, source_target_pairs={{0,18},{1,19},{2,16},{3,17},{4,22},{5,23},{6,20},{7,21},{8,26},{9,... | collective-permute-start | bytes 196616 | tf_op jit(solution)/shard_map/ppermute | solution.py:416
  165.1 9.3 %collective-permute-start.30 = (bf16[2,4,32,128]{3,2,1,0:T(8,128)(2,1)S(1)}, bf16[2,4,32,128]{3,2,1,0:T(8,128)(2,1)S(1)}, u32[]{:S(2)}, u32[]{:S(2)}) collective-permute-start(bf16[2,4,32,128]{3,2,1,0:T(8,128)(2,1)S(1)} %get-tuple-element.116), channel_id=1, source_target_pairs={{0,19},{1,16},{2,17},{3,18},{4,23},{5,20},{6,21},{7,22},{8,27},{9,... | collective-permute-start | bytes 196616 | tf_op jit(solution)/shard_map/ppermute | solution.py:416
  165.1 9.2 %collective-permute-start.24 = (bf16[2,4,32,128]{3,2,1,0:T(8,128)(2,1)S(1)}, bf16[2,4,32,128]{3,2,1,0:T(8,128)(2,1)S(1)}, u32[]{:S(2)}, u32[]{:S(2)}) collective-permute-start(bf16[2,4,32,128]{3,2,1,0:T(8,128)(2,1)S(1)} %get-tuple-element.122), channel_id=1, source_target_pairs={{0,1},{1,2},{2,3},{3,0},{4,5},{5,6},{6,7},{7,4},{8,9},{9,10},{10,1... | collective-permute-start | bytes 196616 | tf_op jit(solution)/shard_map/ppermute | solution.py:405
  (53 other events, 767.4 us)

commit v15 on v14

--- a/solution.py
+++ b/solution.py
@@ -566,12 +566,12 @@
     total = totals_of(parts)
     others = around_all(total)
     suffix, (grad_prefix,) = spread(parts, others, "after", [], True)
-    def brought_back(s, begin):
-        pieces = [after(piece, begin) for piece in blocks[s][0]]
+    def brought_back(s, *begin):
+        pieces = [after(piece, *begin) for piece in blocks[s][0]]
         return [pieces[0]] + [around(pieces[r], -r) for r in shifts[1:]]
 
     returned = {s: brought_back(s, others[0]) for s in order if s}
-    suffix[0] = after(suffix[0], *[piece for s in returned for piece in returned[s]])
+    earlier = [piece for s in returned for piece in returned[s]]
 
     kv_type = BF16 if replicas == 1 else F32
     pairs = of(kv_type, part, tok, grp * 2 * hd)
@@ -603,7 +603,7 @@
         else:
             two = after(two, *suffix[1:])
             moved += [along(rows_for(two, seq + r), r) for r in range(1, fsdp)]
-            returned[s] = brought_back(s, key_gm[s])
+            returned[s] = brought_back(s, key_gm[s], *earlier)
 
     pairs = within(after(pairs, *returned[0]))
     back = [piece[None] for s in slots for piece in returned[s]]

time: 179 us -> 173 us (0.966)
  waiting for transfers between devices: 44 us -> 39.9 us
    ppermute x15, waiting for transfers between devices: 15.1 us -> 10.5 us  [around(): lax.ppermute(array, 'ctx', [(d, d // part * part + (d + shift) % part) fo...]
  transfers between devices with their start and end apart: 32 -> 32, of which waited for: 14 -> 12; matrix products, arithmetic and copies ran while one was open for 0% -> 0% of each run, Pallas kernels for 26% -> 27%
where the time goes in v15:
time: 173 us; the launch traced here: 172 us
  starting transfers between devices  59.5 us (34%)
  Pallas kernels  54 us (31%)
  waiting for transfers between devices  39.9 us (23%)
  blocking collectives  9.99 us (6%)
  local copies, waits for them, and re-layouts  7.14 us (4%)
    pallas_call x6, Pallas kernels, call(): pl.pallas_call(functools.partial(kernel, part, base['sorted']), out_shape...  40.8 us
    ppermute x15, starting transfers between devices, around(): lax.ppermute(array, 'ctx', [(d, d // part * part + (d + shift) % part) fo...  25.8 us
    ppermute x5, waiting for transfers between devices, across(): lax.ppermute(array, 'ctx', [(d, (d + shift * part) % ctx) for d in range(...  14.2 us
    ppermute x4, waiting for transfers between devices, twin(): return lax.ppermute(array, 'fsdp', [(d, d ^ bit) for d in range(fsdp)])  10.7 us
    ppermute x15, waiting for transfers between devices, around(): lax.ppermute(array, 'ctx', [(d, d // part * part + (d + shift) % part) fo...  10.5 us
    all_gather x1, blocking collectives, shards(): maps = lax.all_gather(near_maps, 'fsdp')  9.99 us
    ppermute x4, starting transfers between devices, twin(): return lax.ppermute(array, 'fsdp', [(d, d ^ bit) for d in range(fsdp)])  9.18 us
    ppermute x5, starting transfers between devices, across(): lax.ppermute(array, 'ctx', [(d, (d + shift * part) % ctx) for d in range(...  7.98 us
  transfers between devices with their start and end apart: 32, of which 12 were waited for; matrix products, arithmetic and copies ran while one was open for 0% of the time, Pallas kernels for 27%

profile of v15, /device:TPU:1, one launch (start us, length us, event | category | flops | bytes accessed | tf_op | source)
XLA Modules:
  0.0 172.2 jit_solution(14736919906246421830)
XLA Ops:
  8.9 2.4 %collective-permute-start.3 = (bf16[8,32,128]{2,1,0:T(8,128)(2,1)S(1)}, bf16[8,32,128]{2,1,0:T(8,128)(2,1)S(1)}, u32[]{:S(2)}, u32[]{:S(2)}) collective-permute-start(bf16[8,32,128]{2,1,0:T(8,128)(2,1)S(1)} %pad_maximum_fusion.2), channel_id=1, source_target_pairs={{0,16},{4,20},{8,24},{12,28},{16,0},{20,4},{24,8},{28,12},{1,17},{... | collective-permute-start | bytes 196616 | tf_op jit(solution)/shard_map/ppermute | solution.py:402
  11.3 2.4 %collective-permute-done.3 = bf16[8,32,128]{2,1,0:T(8,128)(2,1)S(1)} collective-permute-done((bf16[8,32,128]{2,1,0:T(8,128)(2,1)S(1)}, bf16[8,32,128]{2,1,0:T(8,128)(2,1)S(1)}, u32[]{:S(2)}, u32[]{:S(2)}) %collective-permute-start.3) | collective-permute-done | bytes 65568 | tf_op jit(solution)/shard_map/ppermute | solution.py:402
  20.2 10.0 %all-gather = bf16[8,8,32,128]{3,2,1,0:T(8,128)(2,1)S(1)} all-gather(bf16[2,8,32,128]{3,2,1,0:T(8,128)(2,1)S(1)} %pad_maximum_fusion.1), channel_id=2, replica_groups=mesh['ctx'=8,'fsdp'=4] {'fsdp'}, dimensions={0}, use_global_device_ids=true | all-gather | bytes 655360 | tf_op jit(solution)/shard_map/all_gather | solution.py:445
  30.2 2.8 %states.3 = bf16[8,144,128]{2,1,0:T(8,128)(2,1)S(1)} custom-call(s32[49]{0:T(128)S(1)} %stack.194.table, bf16[128,512]{1,0:T(8,128)(2,1)S(1)} %get-tuple-element.60.refs_0_.refs_4_, bf16[128,512]{1,0:T(8,128)(2,1)S(1)} %collective-permute-done.refs_1_.refs_5_, bf16[128,512]{1,0:T(8,128)(2,1)S(1)} %collective-permute-done.1.refs_2_.refs_6_, ...), custom_call_target="tpu_custom_call" | custom-call | flops 1000 | bytes 1000 | tf_op jit(solution)/shard_map/states/pallas_call | solution.py:481
  33.2 2.8 %states.2.refs_0_ = bf16[8,144,128]{2,1,0:T(8,128)(2,1)S(1)} custom-call(s32[49]{0:T(128)S(1)} %stack.194.table, bf16[128,512]{1,0:T(8,128)(2,1)S(1)} %get-tuple-element.60.refs_0_.refs_4_, bf16[128,512]{1,0:T(8,128)(2,1)S(1)} %collective-permute-done.refs_1_.refs_5_, bf16[128,512]{1,0:T(8,128)(2,1)S(1)} %collective-permute-done.1.refs_2_.refs_6_, ...), custom_call_target="tpu_custom_call" | custom-call | flops 1000 | bytes 1000 | tf_op jit(solution)/shard_map/states/pallas_call | solution.py:481
  36.1 5.7 %collective-permute-done.6.refs_11_.refs_15_ = bf16[128,2048]{1,0:T(8,128)(2,1)S(1)} collective-permute-done((bf16[128,2048]{1,0:T(8,128)(2,1)S(1)}, bf16[128,2048]{1,0:T(8,128)(2,1)S(1)}, u32[]{:S(2)}, u32[]{:S(2)}) %collective-permute-start.6) | collective-permute-done | bytes 524320 | tf_op jit(solution)/shard_map/ppermute | solution.py:397
  41.7 3.6 %collective-permute-done.7.refs_1_ = bf16[8,144,128]{2,1,0:T(8,128)(2,1)S(1)} collective-permute-done((bf16[8,144,128]{2,1,0:T(8,128)(2,1)S(1)}, bf16[8,144,128]{2,1,0:T(8,128)(2,1)S(1)}, u32[]{:S(2)}, u32[]{:S(2)}) %collective-permute-start.7) | collective-permute-done | bytes 294944 | tf_op jit(solution)/shard_map/ppermute | solution.py:402
  46.0 2.8 %collective-permute-start.8 = (bf16[8,144,128]{2,1,0:T(8,128)(2,1)S(1)}, bf16[8,144,128]{2,1,0:T(8,128)(2,1)S(1)}, u32[]{:S(2)}, u32[]{:S(2)}) collective-permute-start(bf16[8,144,128]{2,1,0:T(8,128)(2,1)S(1)} %totals.4.refs_0_), channel_id=1, source_target_pairs={{0,1},{1,0},{2,3},{3,2},{4,5},{5,4},{6,7},{7,6},{8,9},{9,8},{10,11... | collective-permute-start | bytes 884744 | tf_op jit(solution)/shard_map/ppermute | solution.py:408
  51.9 7.0 %collective-permute-done.9.refs_3_ = bf16[8,144,128]{2,1,0:T(8,128)(2,1)S(1)} collective-permute-done((bf16[8,144,128]{2,1,0:T(8,128)(2,1)S(1)}, bf16[8,144,128]{2,1,0:T(8,128)(2,1)S(1)}, u32[]{:S(2)}, u32[]{:S(2)}) %collective-permute-start.9) | collective-permute-done | bytes 294944 | tf_op jit(solution)/shard_map/ppermute | solution.py:408
  59.8 3.2 %collective-permute-start.13 = (bf16[8,144,128]{2,1,0:T(8,128)(2,1)S(1)}, bf16[8,144,128]{2,1,0:T(8,128)(2,1)S(1)}, u32[]{:S(2)}, u32[]{:S(2)}) collective-permute-start(bf16[8,144,128]{2,1,0:T(8,128)(2,1)S(1)} %get-tuple-element.78), channel_id=1, source_target_pairs={{0,16},{4,20},{8,24},{12,28},{16,0},{20,4},{24,8},{28,12},{1,17},{... | collective-permute-start | bytes 884744 | tf_op jit(solution)/shard_map/ppermute | solution.py:402
  67.2 8.3 %collective-permute-done.13.refs_17_ = bf16[8,144,128]{2,1,0:T(8,128)(2,1)S(1)} collective-permute-done((bf16[8,144,128]{2,1,0:T(8,128)(2,1)S(1)}, bf16[8,144,128]{2,1,0:T(8,128)(2,1)S(1)}, u32[]{:S(2)}, u32[]{:S(2)}) %collective-permute-start.13) | collective-permute-done | bytes 294944 | tf_op jit(solution)/shard_map/ppermute | solution.py:402
  76.2 12.8 %blocks.3 = (bf16[128,1024]{1,0:T(8,128)(2,1)}, bf16[128,1024]{1,0:T(8,128)(2,1)}, bf16[128,1024]{1,0:T(8,128)(2,1)}, bf16[128,1024]{1,0:T(8,128)(2,1)}, f32[8,1...) custom-call(s32[49]{0:T(128)} %copy-done.26, ...), custom_call_target="tpu_custom_call" | custom-call | flops 1000 | bytes 1000 | tf_op jit(solution)/shard_map/blocks/pallas_call | solution.py:481
  91.5 12.9 %blocks.2 = (bf16[128,1024]{1,0:T(8,128)(2,1)}, bf16[128,1024]{1,0:T(8,128)(2,1)}, bf16[128,1024]{1,0:T(8,128)(2,1)}, bf16[128,1024]{1,0:T(8,128)(2,1)}, f32[8,1...) custom-call(s32[49]{0:T(128)} %copy-done.26, ...), custom_call_target="tpu_custom_call" | custom-call | flops 1000 | bytes 1000 | tf_op jit(solution)/shard_map/blocks/pallas_call | solution.py:481
  106.2 3.8 %collective-permute-start.15 = (bf16[8,144,128]{2,1,0:T(8,128)(2,1)S(1)}, bf16[8,144,128]{2,1,0:T(8,128)(2,1)S(1)}, u32[]{:S(2)}, u32[]{:S(2)}) collective-permute-start(bf16[8,144,128]{2,1,0:T(8,128)(2,1)S(1)} %totals.6.refs_0_), channel_id=1, source_target_pairs={{0,1},{1,0},{2,3},{3,2},{4,5},{5,4},{6,7},{7,6},{8,9},{9,8},{10,11... | collective-permute-start | bytes 884744 | tf_op jit(solution)/shard_map/ppermute | solution.py:408
  113.1 4.5 %collective-permute-start.19 = (bf16[128,1024]{1,0:T(8,128)(2,1)S(1)}, bf16[128,1024]{1,0:T(8,128)(2,1)S(1)}, u32[]{:S(2)}, u32[]{:S(2)}) collective-permute-start(bf16[128,1024]{1,0:T(8,128)(2,1)S(1)} %copy-done.44), channel_id=1, source_target_pairs={{0,4},{4,8},{8,12},{12,0},{16,20},{20,24},{24,28},{28,16},{1,5},{5... | collective-permute-start | bytes 786440 | tf_op jit(solution)/shard_map/ppermute | solution.py:397
  121.7 2.3 %collective-permute-start.23 = (bf16[8,144,128]{2,1,0:T(8,128)(2,1)S(1)}, bf16[8,144,128]{2,1,0:T(8,128)(2,1)S(1)}, u32[]{:S(2)}, u32[]{:S(2)}) collective-permute-start(bf16[8,144,128]{2,1,0:T(8,128)(2,1)S(1)} %get-tuple-element.99), channel_id=1, source_target_pairs={{0,16},{4,20},{8,24},{12,28},{16,0},{20,4},{24,8},{28,12},{1,17},{... | collective-permute-start | bytes 884744 | tf_op jit(solution)/shard_map/ppermute | solution.py:402
  125.7 4.8 %keys.2 = (bf16[4,128,512]{2,1,0:T(8,128)(2,1)}, bf16[4,128,128]{2,1,0:T(8,128)(2,1)S(1)}) custom-call(s32[49]{0:T(128)S(1)} %copy-done.27, bf16[128,512]{1,0:T(8,128)(2,1)S(1)} %copy-done.5, bf16[128,512]{1,0:T(8,128)(2,1)S(1)} %copy-done.7, bf16[128,512]{1,0:T(8,128)(2,1)S(1)} %copy-done.9, bf16[128,512]{1,0:T(8,128)(2,1)S(1)} %copy-done.11, ...), custom_call_target="tpu_custom_call" | custom-call | flops 1000 | bytes 1000 | tf_op jit(solution)/shard_map/keys/pallas_call | solution.py:481
  130.4 6.6 %collective-permute-start.22 = (bf16[128,1024]{1,0:T(8,128)(2,1)S(1)}, bf16[128,1024]{1,0:T(8,128)(2,1)S(1)}, u32[]{:S(2)}, u32[]{:S(2)}) collective-permute-start(bf16[128,1024]{1,0:T(8,128)(2,1)S(1)} %copy-done.41), channel_id=1, source_target_pairs={{0,4},{4,8},{8,12},{12,0},{16,20},{20,24},{24,28},{28,16},{1,5},{5... | collective-permute-start | bytes 786440 | tf_op jit(solution)/shard_map/ppermute | solution.py:397
  138.3 4.8 %keys.3 = (bf16[4,128,512]{2,1,0:T(8,128)(2,1)}, bf16[4,128,128]{2,1,0:T(8,128)(2,1)S(1)}) custom-call(s32[49]{0:T(128)S(1)} %copy-done.27, bf16[128,512]{1,0:T(8,128)(2,1)S(1)} %copy-done.5, bf16[128,512]{1,0:T(8,128)(2,1)S(1)} %copy-done.7, bf16[128,512]{1,0:T(8,128)(2,1)S(1)} %copy-done.9, ...), custom_call_target="tpu_custom_call", output_to_operand_aliasing={{0}: (13, {})} | custom-call | flops 1000 | bytes 1000 | tf_op jit(solution)/shard_map/keys/pallas_call | solution.py:481
  143.1 3.3 %collective-permute-done.20 = bf16[128,1024]{1,0:T(8,128)(2,1)S(1)} collective-permute-done((bf16[128,1024]{1,0:T(8,128)(2,1)S(1)}, bf16[128,1024]{1,0:T(8,128)(2,1)S(1)}, u32[]{:S(2)}, u32[]{:S(2)}) %collective-permute-start.20) | collective-permute-done | bytes 262176 | tf_op jit(solution)/shard_map/ppermute | solution.py:397
  146.4 4.9 %all-to-all-start = ((bf16[4,128,512]{2,1,0:T(8,128)(2,1)}), bf16[4,128,512]{2,1,0:T(8,128)(2,1)S(1)}, u32[]{:S(2)}, u32[]{:S(2)}) async-start(bf16[4,128,512]{2,1,0:T(8,128)(2,1)} %get-tuple-element.104), calls=%async_computation | async-start | bytes 1048576 | tf_op jit(solution)/shard_map/all_to_all | solution.py:394
  153.6 4.1 %collective-permute-start.28 = (bf16[2,4,32,128]{3,2,1,0:T(8,128)(2,1)S(1)}, bf16[2,4,32,128]{3,2,1,0:T(8,128)(2,1)S(1)}, u32[]{:S(2)}, u32[]{:S(2)}) collective-permute-start(bf16[2,4,32,128]{3,2,1,0:T(8,128)(2,1)S(1)} %get-tuple-element.116), channel_id=1, source_target_pairs={{0,17},{1,18},{2,19},{3,16},{4,21},{5,22},{6,23},{7,20},{8,25},{9,... | collective-permute-start | bytes 196616 | tf_op jit(solution)/shard_map/ppermute | solution.py:416
  159.2 2.4 %collective-permute-start.24 = (bf16[2,4,32,128]{3,2,1,0:T(8,128)(2,1)S(1)}, bf16[2,4,32,128]{3,2,1,0:T(8,128)(2,1)S(1)}, u32[]{:S(2)}, u32[]{:S(2)}) collective-permute-start(bf16[2,4,32,128]{3,2,1,0:T(8,128)(2,1)S(1)} %get-tuple-element.120), channel_id=1, source_target_pairs={{0,1},{1,2},{2,3},{3,0},{4,5},{5,6},{6,7},{7,4},{8,9},{9,10},{10,1... | collective-permute-start | bytes 196616 | tf_op jit(solution)/shard_map/ppermute | solution.py:405
  165.0 3.2 %collective-permute-done.29.refs_5_ = bf16[2,4,32,128]{3,2,1,0:T(8,128)(2,1)S(1)} collective-permute-done((bf16[2,4,32,128]{3,2,1,0:T(8,128)(2,1)S(1)}, bf16[2,4,32,128]{3,2,1,0:T(8,128)(2,1)S(1)}, u32[]{:S(2)}, u32[]{:S(2)}) %collective-permute-start.29) | collective-permute-done | bytes 65568 | tf_op jit(solution)/shard_map/ppermute | solution.py:416
  (157 shorter events, 49.7 us)
Async XLA Ops:
  4.2 9.5 %collective-permute-start = (bf16[128,512]{1,0:T(8,128)(2,1)S(1)}, bf16[128,512]{1,0:T(8,128)(2,1)S(1)}, u32[]{:S(2)}, u32[]{:S(2)}) collective-permute-start(bf16[128,512]{1,0:T(8,128)(2,1)S(1)} %get-tuple-element.61), channel_id=1, source_target_pairs={{0,4},{4,8},{8,12},{12,0},{16,20},{20,24},{24,28},{28,16},{1,5},{5... | collective-permute-start | bytes 393224 | tf_op jit(solution)/shard_map/ppermute | solution.py:397
  14.9 21.2 %collective-permute-start.4 = (bf16[128,2048]{1,0:T(8,128)(2,1)S(1)}, bf16[128,2048]{1,0:T(8,128)(2,1)S(1)}, u32[]{:S(2)}, u32[]{:S(2)}) collective-permute-start(bf16[128,2048]{1,0:T(8,128)(2,1)S(1)} %get-tuple-element.66), channel_id=1, source_target_pairs={{0,4},{4,8},{8,12},{12,0},{16,20},{20,24},{24,28},{28,16},{1,5},{5... | collective-permute-start | bytes 1572872 | tf_op jit(solution)/shard_map/ppermute | solution.py:397
  16.2 19.8 %collective-permute-start.5 = (bf16[128,2048]{1,0:T(8,128)(2,1)S(1)}, bf16[128,2048]{1,0:T(8,128)(2,1)S(1)}, u32[]{:S(2)}, u32[]{:S(2)}) collective-permute-start(bf16[128,2048]{1,0:T(8,128)(2,1)S(1)} %get-tuple-element.67), channel_id=1, source_target_pairs={{0,8},{4,12},{8,0},{12,4},{16,24},{20,28},{24,16},{28,20},{1,9},{5... | collective-permute-start | bytes 1572872 | tf_op jit(solution)/shard_map/ppermute | solution.py:397
  18.4 23.3 %collective-permute-start.6 = (bf16[128,2048]{1,0:T(8,128)(2,1)S(1)}, bf16[128,2048]{1,0:T(8,128)(2,1)S(1)}, u32[]{:S(2)}, u32[]{:S(2)}) collective-permute-start(bf16[128,2048]{1,0:T(8,128)(2,1)S(1)} %get-tuple-element.68), channel_id=1, source_target_pairs={{0,12},{4,0},{8,4},{12,8},{16,28},{20,16},{24,20},{28,24},{1,13},{... | collective-permute-start | bytes 1572872 | tf_op jit(solution)/shard_map/ppermute | solution.py:397
  33.1 12.3 %collective-permute-start.7 = (bf16[8,144,128]{2,1,0:T(8,128)(2,1)S(1)}, bf16[8,144,128]{2,1,0:T(8,128)(2,1)S(1)}, u32[]{:S(2)}, u32[]{:S(2)}) collective-permute-start(bf16[8,144,128]{2,1,0:T(8,128)(2,1)S(1)} %states.3), channel_id=1, source_target_pairs={{0,16},{4,20},{8,24},{12,28},{16,0},{20,4},{24,8},{28,12},{1,17},{... | collective-permute-start | bytes 884744 | tf_op jit(solution)/shard_map/ppermute | solution.py:402
  50.7 8.3 %collective-permute-start.9 = (bf16[8,144,128]{2,1,0:T(8,128)(2,1)S(1)}, bf16[8,144,128]{2,1,0:T(8,128)(2,1)S(1)}, u32[]{:S(2)}, u32[]{:S(2)}) collective-permute-start(bf16[8,144,128]{2,1,0:T(8,128)(2,1)S(1)} %totals.5), channel_id=1, source_target_pairs={{0,2},{1,3},{2,0},{3,1},{4,6},{5,7},{6,4},{7,5},{8,10},{9,11},{10,... | collective-permute-start | bytes 884744 | tf_op jit(solution)/shard_map/ppermute | solution.py:408
  59.8 15.7 %collective-permute-start.13 = (bf16[8,144,128]{2,1,0:T(8,128)(2,1)S(1)}, bf16[8,144,128]{2,1,0:T(8,128)(2,1)S(1)}, u32[]{:S(2)}, u32[]{:S(2)}) collective-permute-start(bf16[8,144,128]{2,1,0:T(8,128)(2,1)S(1)} %get-tuple-element.78), channel_id=1, source_target_pairs={{0,16},{4,20},{8,24},{12,28},{16,0},{20,4},{24,8},{28,12},{1,17},{... | collective-permute-start | bytes 884744 | tf_op jit(solution)/shard_map/ppermute | solution.py:402
  64.9 24.2 %collective-permute-start.10 = (bf16[128,2048]{1,0:T(8,128)(2,1)S(1)}, bf16[128,2048]{1,0:T(8,128)(2,1)S(1)}, u32[]{:S(2)}, u32[]{:S(2)}) collective-permute-start(bf16[128,2048]{1,0:T(8,128)(2,1)S(1)} %get-tuple-element.73), channel_id=1, source_target_pairs={{0,4},{4,8},{8,12},{12,0},{16,20},{20,24},{24,28},{28,16},{1,5},{5... | collective-permute-start | bytes 1572872 | tf_op jit(solution)/shard_map/ppermute | solution.py:397
  65.5 23.6 %collective-permute-start.11 = (bf16[128,2048]{1,0:T(8,128)(2,1)S(1)}, bf16[128,2048]{1,0:T(8,128)(2,1)S(1)}, u32[]{:S(2)}, u32[]{:S(2)}) collective-permute-start(bf16[128,2048]{1,0:T(8,128)(2,1)S(1)} %get-tuple-element.74), channel_id=1, source_target_pairs={{0,8},{4,12},{8,0},{12,4},{16,24},{20,28},{24,16},{28,20},{1,9},{5... | collective-permute-start | bytes 1572872 | tf_op jit(solution)/shard_map/ppermute | solution.py:397
  66.8 23.9 %collective-permute-start.12 = (bf16[128,2048]{1,0:T(8,128)(2,1)S(1)}, bf16[128,2048]{1,0:T(8,128)(2,1)S(1)}, u32[]{:S(2)}, u32[]{:S(2)}) collective-permute-start(bf16[128,2048]{1,0:T(8,128)(2,1)S(1)} %get-tuple-element.75), channel_id=1, source_target_pairs={{0,12},{4,0},{8,4},{12,8},{16,28},{20,16},{24,20},{28,24},{1,13},{... | collective-permute-start | bytes 1572872 | tf_op jit(solution)/shard_map/ppermute | solution.py:397
  89.0 15.4 %collective-permute-start.14 = (bf16[8,144,128]{2,1,0:T(8,128)(2,1)}, bf16[8,144,128]{2,1,0:T(8,128)(2,1)S(1)}, u32[]{:S(2)}, u32[]{:S(2)}) collective-permute-start(bf16[8,144,128]{2,1,0:T(8,128)(2,1)} %get-tuple-element.79), channel_id=1, source_target_pairs={{0,16},{4,20},{8,24},{12,28},{16,0},{20,4},{24,8},{28,12},{1,17},{... | collective-permute-start | bytes 884744 | tf_op jit(solution)/shard_map/ppermute | solution.py:402
  111.8 8.3 %collective-permute-start.16 = (bf16[8,144,128]{2,1,0:T(8,128)(2,1)S(1)}, bf16[8,144,128]{2,1,0:T(8,128)(2,1)S(1)}, u32[]{:S(2)}, u32[]{:S(2)}) collective-permute-start(bf16[8,144,128]{2,1,0:T(8,128)(2,1)S(1)} %totals.7), channel_id=1, source_target_pairs={{0,2},{1,3},{2,0},{3,1},{4,6},{5,7},{6,4},{7,5},{8,10},{9,11},{10,... | collective-permute-start | bytes 884744 | tf_op jit(solution)/shard_map/ppermute | solution.py:408
  113.1 17.3 %collective-permute-start.19 = (bf16[128,1024]{1,0:T(8,128)(2,1)S(1)}, bf16[128,1024]{1,0:T(8,128)(2,1)S(1)}, u32[]{:S(2)}, u32[]{:S(2)}) collective-permute-start(bf16[128,1024]{1,0:T(8,128)(2,1)S(1)} %copy-done.44), channel_id=1, source_target_pairs={{0,4},{4,8},{8,12},{12,0},{16,20},{20,24},{24,28},{28,16},{1,5},{5... | collective-permute-start | bytes 786440 | tf_op jit(solution)/shard_map/ppermute | solution.py:397
  117.6 12.8 %collective-permute-start.18 = (bf16[128,1024]{1,0:T(8,128)(2,1)S(1)}, bf16[128,1024]{1,0:T(8,128)(2,1)S(1)}, u32[]{:S(2)}, u32[]{:S(2)}) collective-permute-start(bf16[128,1024]{1,0:T(8,128)(2,1)S(1)} %copy-done.43), channel_id=1, source_target_pairs={{0,8},{4,12},{8,0},{12,4},{16,24},{20,28},{24,16},{28,20},{1,9},{5... | collective-permute-start | bytes 786440 | tf_op jit(solution)/shard_map/ppermute | solution.py:397
  117.6 12.8 %collective-permute-start.17 = (bf16[128,1024]{1,0:T(8,128)(2,1)S(1)}, bf16[128,1024]{1,0:T(8,128)(2,1)S(1)}, u32[]{:S(2)}, u32[]{:S(2)}) collective-permute-start(bf16[128,1024]{1,0:T(8,128)(2,1)S(1)} %copy-done.42), channel_id=1, source_target_pairs={{0,12},{4,0},{8,4},{12,8},{16,28},{20,16},{24,20},{28,24},{1,13},{... | collective-permute-start | bytes 786440 | tf_op jit(solution)/shard_map/ppermute | solution.py:397
  121.7 16.6 %collective-permute-start.23 = (bf16[8,144,128]{2,1,0:T(8,128)(2,1)S(1)}, bf16[8,144,128]{2,1,0:T(8,128)(2,1)S(1)}, u32[]{:S(2)}, u32[]{:S(2)}) collective-permute-start(bf16[8,144,128]{2,1,0:T(8,128)(2,1)S(1)} %get-tuple-element.99), channel_id=1, source_target_pairs={{0,16},{4,20},{8,24},{12,28},{16,0},{20,4},{24,8},{28,12},{1,17},{... | collective-permute-start | bytes 884744 | tf_op jit(solution)/shard_map/ppermute | solution.py:402
  130.4 12.7 %collective-permute-start.22 = (bf16[128,1024]{1,0:T(8,128)(2,1)S(1)}, bf16[128,1024]{1,0:T(8,128)(2,1)S(1)}, u32[]{:S(2)}, u32[]{:S(2)}) collective-permute-start(bf16[128,1024]{1,0:T(8,128)(2,1)S(1)} %copy-done.41), channel_id=1, source_target_pairs={{0,4},{4,8},{8,12},{12,0},{16,20},{20,24},{24,28},{28,16},{1,5},{5... | collective-permute-start | bytes 786440 | tf_op jit(solution)/shard_map/ppermute | solution.py:397
  137.1 9.4 %collective-permute-start.20 = (bf16[128,1024]{1,0:T(8,128)(2,1)S(1)}, bf16[128,1024]{1,0:T(8,128)(2,1)S(1)}, u32[]{:S(2)}, u32[]{:S(2)}) collective-permute-start(bf16[128,1024]{1,0:T(8,128)(2,1)S(1)} %copy-done.39), channel_id=1, source_target_pairs={{0,12},{4,0},{8,4},{12,8},{16,28},{20,16},{24,20},{28,24},{1,13},{... | collective-permute-start | bytes 786440 | tf_op jit(solution)/shard_map/ppermute | solution.py:397
  146.4 24.4 %all-to-all-start = ((bf16[4,128,512]{2,1,0:T(8,128)(2,1)}), bf16[4,128,512]{2,1,0:T(8,128)(2,1)S(1)}, u32[]{:S(2)}, u32[]{:S(2)}) async-start(bf16[4,128,512]{2,1,0:T(8,128)(2,1)} %get-tuple-element.104), calls=%async_computation | async-start | bytes 1048576 | tf_op jit(solution)/shard_map/all_to_all | solution.py:394
  151.4 10.2 %collective-permute-start.27 = (bf16[2,4,32,128]{3,2,1,0:T(8,128)(2,1)S(1)}, bf16[2,4,32,128]{3,2,1,0:T(8,128)(2,1)S(1)}, u32[]{:S(2)}, u32[]{:S(2)}) collective-permute-start(bf16[2,4,32,128]{3,2,1,0:T(8,128)(2,1)S(1)} %get-tuple-element.115), channel_id=1, source_target_pairs={{0,16},{1,17},{2,18},{3,19},{4,20},{5,21},{6,22},{7,23},{8,24},{9,... | collective-permute-start | bytes 196616 | tf_op jit(solution)/shard_map/ppermute | solution.py:416
  153.6 9.2 %collective-permute-start.28 = (bf16[2,4,32,128]{3,2,1,0:T(8,128)(2,1)S(1)}, bf16[2,4,32,128]{3,2,1,0:T(8,128)(2,1)S(1)}, u32[]{:S(2)}, u32[]{:S(2)}) collective-permute-start(bf16[2,4,32,128]{3,2,1,0:T(8,128)(2,1)S(1)} %get-tuple-element.116), channel_id=1, source_target_pairs={{0,17},{1,18},{2,19},{3,16},{4,21},{5,22},{6,23},{7,20},{8,25},{9,... | collective-permute-start | bytes 196616 | tf_op jit(solution)/shard_map/ppermute | solution.py:416
  157.7 10.5 %collective-permute-start.29 = (bf16[2,4,32,128]{3,2,1,0:T(8,128)(2,1)S(1)}, bf16[2,4,32,128]{3,2,1,0:T(8,128)(2,1)S(1)}, u32[]{:S(2)}, u32[]{:S(2)}) collective-permute-start(bf16[2,4,32,128]{3,2,1,0:T(8,128)(2,1)S(1)} %get-tuple-element.117), channel_id=1, source_target_pairs={{0,18},{1,19},{2,16},{3,17},{4,22},{5,23},{6,20},{7,21},{8,26},{9,... | collective-permute-start | bytes 196616 | tf_op jit(solution)/shard_map/ppermute | solution.py:416
  158.7 10.7 %collective-permute-start.30 = (bf16[2,4,32,128]{3,2,1,0:T(8,128)(2,1)S(1)}, bf16[2,4,32,128]{3,2,1,0:T(8,128)(2,1)S(1)}, u32[]{:S(2)}, u32[]{:S(2)}) collective-permute-start(bf16[2,4,32,128]{3,2,1,0:T(8,128)(2,1)S(1)} %get-tuple-element.114), channel_id=1, source_target_pairs={{0,19},{1,16},{2,17},{3,18},{4,23},{5,20},{6,21},{7,22},{8,27},{9,... | collective-permute-start | bytes 196616 | tf_op jit(solution)/shard_map/ppermute | solution.py:416
  159.2 10.2 %collective-permute-start.24 = (bf16[2,4,32,128]{3,2,1,0:T(8,128)(2,1)S(1)}, bf16[2,4,32,128]{3,2,1,0:T(8,128)(2,1)S(1)}, u32[]{:S(2)}, u32[]{:S(2)}) collective-permute-start(bf16[2,4,32,128]{3,2,1,0:T(8,128)(2,1)S(1)} %get-tuple-element.120), channel_id=1, source_target_pairs={{0,1},{1,2},{2,3},{3,0},{4,5},{5,6},{6,7},{7,4},{8,9},{9,10},{10,1... | collective-permute-start | bytes 196616 | tf_op jit(solution)/shard_map/ppermute | solution.py:405
  (53 other events, 736.7 us)

commit v16 on v15

--- a/solution.py
+++ b/solution.py
@@ -209,46 +209,50 @@
     dvalue = [[jnp.zeros((hd, TILE), F32) for _ in range(BLK // TILE)] for u in heads]
     suffix = [jnp.zeros((2 * half, hd), F32) for u in heads]
     suffix_norm = [jnp.zeros((2 * half, 1), F32) for u in heads]
-    for j in range(BLK // TILE):
-        begin, end = j * TILE, (j + 1) * TILE
-        own = [q_low[u][:, begin:end] for u in heads]
-        scores = [causal(nn(k_turned[u][:end], own[u]), begin) for u in heads]
-        scores_low = [scores[u].astype(BF16) for u in heads]
-        inverse = [
-            1.0
-            / (
-                jnp.sum(own[u].astype(F32) * norm[u], axis=0, keepdims=True)
-                + jnp.sum(scores[u], axis=0, keepdims=True)
-            )
-            for u in heads
-        ]
-        scaled = [g_turned[u][:, begin:end].astype(F32) * inverse[u] for u in heads]
-        scaled_low = [scaled[u].astype(BF16) for u in heads]
-        numerator = [
-            nn(state_turned[u], own[u]) + nn(vt_all[:, :end], scores_low[u]) for u in heads
-        ]
-        products = [nn(v_all[:end, :], scaled_low[u]) for u in heads]
-        norm_grad = [
-            -jnp.sum(scaled[u] * (numerator[u] * inverse[u]), axis=0, keepdims=True)
-            for u in heads
-        ]
-        dscores = [causal(products[u] + norm_grad[u], begin).astype(BF16) for u in heads]
-        dquery = [
-            nn(state[u], scaled_low[u])
-            + norm[u] * norm_grad[u]
-            + nn(k_low[u][:, :end], dscores[u])
-            for u in heads
-        ]
-        for u in heads:
-            back[u].append(feature_back(q_feat[u][:, begin:end], dquery[u]))
-            for i in range(j + 1):
-                rows = slice(i * TILE, (i + 1) * TILE)
-                dkey[u][i] = dkey[u][i] + nt(own[u], dscores[u][rows])
-                dvalue[u][i] = dvalue[u][i] + nt(scaled_low[u], scores_low[u][rows])
-            suffix[u] = suffix[u] + nt(own[u], scaled_low[u])
-            suffix_norm[u] = suffix_norm[u] + jnp.sum(
-                own[u].astype(F32) * norm_grad[u], axis=1, keepdims=True
-            )
+    chains = [(u, j) for j in range(BLK // TILE) for u in heads]
+    tile = {(u, j): slice(j * TILE, (j + 1) * TILE) for u, j in chains}
+    own = {c: q_low[c[0]][:, tile[c]] for c in chains}
+    scores = {c: causal(nn(k_turned[c[0]][: tile[c].stop], own[c]), tile[c].start) for c in chains}
+    scores_low = {c: scores[c].astype(BF16) for c in chains}
+    inverse = {
+        c: 1.0
+        / (
+            jnp.sum(own[c].astype(F32) * norm[c[0]], axis=0, keepdims=True)
+            + jnp.sum(scores[c], axis=0, keepdims=True)
+        )
+        for c in chains
+    }
+    scaled = {c: g_turned[c[0]][:, tile[c]].astype(F32) * inverse[c] for c in chains}
+    scaled_low = {c: scaled[c].astype(BF16) for c in chains}
+    numerator = {
+        c: nn(state_turned[c[0]], own[c]) + nn(vt_all[:, : tile[c].stop], scores_low[c])
+        for c in chains
+    }
+    products = {c: nn(v_all[: tile[c].stop, :], scaled_low[c]) for c in chains}
+    norm_grad = {
+        c: -jnp.sum(scaled[c] * (numerator[c] * inverse[c]), axis=0, keepdims=True)
+        for c in chains
+    }
+    dscores = {
+        c: causal(products[c] + norm_grad[c], tile[c].start).astype(BF16) for c in chains
+    }
+    dquery = {
+        c: nn(state[c[0]], scaled_low[c])
+        + norm[c[0]] * norm_grad[c]
+        + nn(k_low[c[0]][:, : tile[c].stop], dscores[c])
+        for c in chains
+    }
+    for c in chains:
+        u, j = c
+        back[u].append(feature_back(q_feat[u][:, tile[c]], dquery[c]))
+        for i in range(j + 1):
+            rows = slice(i * TILE, (i + 1) * TILE)
+            dkey[u][i] = dkey[u][i] + nt(own[c], dscores[c][rows])
+            dvalue[u][i] = dvalue[u][i] + nt(scaled_low[c], scores_low[c][rows])
+        suffix[u] = suffix[u] + nt(own[c], scaled_low[c])
+        suffix_norm[u] = suffix_norm[u] + jnp.sum(
+            own[c].astype(F32) * norm_grad[c], axis=1, keepdims=True
+        )
     for u in heads:
         dlog = jnp.concatenate(back[u], axis=1)
         gq_all[:, lanes[u]] = nn(turned(dlog), weight[u][:half]).astype(BF16)

time: 173 us -> 173 us (level)
  Pallas kernels: 54 us -> 51.4 us
  starting transfers between devices: 59.5 us -> 61.9 us
    pallas_call x6, Pallas kernels: 40.8 us -> 38.3 us  [call(): pl.pallas_call(functools.partial(kernel, part, base['sorted']), out_shape...]
  transfers between devices with their start and end apart: 32 -> 32, of which waited for: 12 -> 12; matrix products, arithmetic and copies ran while one was open for 0% -> 0% of each run, Pallas kernels for 27% -> 26%
where the time goes in v16:
time: 173 us; the launch traced here: 172 us
  starting transfers between devices  61.9 us (36%)
  Pallas kernels  51.4 us (30%)
  waiting for transfers between devices  40.1 us (23%)
  blocking collectives  9.99 us (6%)
  local copies, waits for them, and re-layouts  7.14 us (4%)
    pallas_call x6, Pallas kernels, call(): pl.pallas_call(functools.partial(kernel, part, base['sorted']), out_shape...  38.3 us
    ppermute x15, starting transfers between devices, around(): lax.ppermute(array, 'ctx', [(d, d // part * part + (d + shift) % part) fo...  26.9 us
    ppermute x5, waiting for transfers between devices, across(): lax.ppermute(array, 'ctx', [(d, (d + shift * part) % ctx) for d in range(...  14.2 us
    ppermute x15, waiting for transfers between devices, around(): lax.ppermute(array, 'ctx', [(d, d // part * part + (d + shift) % part) fo...  11.8 us
    all_gather x1, blocking collectives, shards(): maps = lax.all_gather(near_maps, 'fsdp')  9.99 us
    ppermute x4, waiting for transfers between devices, twin(): return lax.ppermute(array, 'fsdp', [(d, d ^ bit) for d in range(fsdp)])  9.55 us
    ppermute x5, starting transfers between devices, across(): lax.ppermute(array, 'ctx', [(d, (d + shift * part) % ctx) for d in range(...  9.28 us
    ppermute x4, starting transfers between devices, twin(): return lax.ppermute(array, 'fsdp', [(d, d ^ bit) for d in range(fsdp)])  9.19 us
  transfers between devices with their start and end apart: 32, of which 12 were waited for; matrix products, arithmetic and copies ran while one was open for 0% of the time, Pallas kernels for 26%

profile of v16, /device:TPU:1, one launch (start us, length us, event | category | flops | bytes accessed | tf_op | source)
XLA Modules:
  0.0 172.2 jit_solution(5631341553415488388)
XLA Ops:
  8.9 2.4 %collective-permute-start.3 = (bf16[8,32,128]{2,1,0:T(8,128)(2,1)S(1)}, bf16[8,32,128]{2,1,0:T(8,128)(2,1)S(1)}, u32[]{:S(2)}, u32[]{:S(2)}) collective-permute-start(bf16[8,32,128]{2,1,0:T(8,128)(2,1)S(1)} %pad_maximum_fusion.2), channel_id=1, source_target_pairs={{0,16},{4,20},{8,24},{12,28},{16,0},{20,4},{24,8},{28,12},{1,17},{... | collective-permute-start | bytes 196616 | tf_op jit(solution)/shard_map/ppermute | solution.py:406
  11.3 2.4 %collective-permute-done.3 = bf16[8,32,128]{2,1,0:T(8,128)(2,1)S(1)} collective-permute-done((bf16[8,32,128]{2,1,0:T(8,128)(2,1)S(1)}, bf16[8,32,128]{2,1,0:T(8,128)(2,1)S(1)}, u32[]{:S(2)}, u32[]{:S(2)}) %collective-permute-start.3) | collective-permute-done | bytes 65568 | tf_op jit(solution)/shard_map/ppermute | solution.py:406
  20.2 10.0 %all-gather = bf16[8,8,32,128]{3,2,1,0:T(8,128)(2,1)S(1)} all-gather(bf16[2,8,32,128]{3,2,1,0:T(8,128)(2,1)S(1)} %pad_maximum_fusion.1), channel_id=2, replica_groups=mesh['ctx'=8,'fsdp'=4] {'fsdp'}, dimensions={0}, use_global_device_ids=true | all-gather | bytes 655360 | tf_op jit(solution)/shard_map/all_gather | solution.py:449
  30.2 2.8 %states.3 = bf16[8,144,128]{2,1,0:T(8,128)(2,1)S(1)} custom-call(s32[49]{0:T(128)S(1)} %stack.194.table, bf16[128,512]{1,0:T(8,128)(2,1)S(1)} %get-tuple-element.60.refs_0_.refs_4_, bf16[128,512]{1,0:T(8,128)(2,1)S(1)} %collective-permute-done.refs_1_.refs_5_, bf16[128,512]{1,0:T(8,128)(2,1)S(1)} %collective-permute-done.1.refs_2_.refs_6_, ...), custom_call_target="tpu_custom_call" | custom-call | flops 1000 | bytes 1000 | tf_op jit(solution)/shard_map/states/pallas_call | solution.py:485
  33.2 2.8 %states.2.refs_0_ = bf16[8,144,128]{2,1,0:T(8,128)(2,1)S(1)} custom-call(s32[49]{0:T(128)S(1)} %stack.194.table, bf16[128,512]{1,0:T(8,128)(2,1)S(1)} %get-tuple-element.60.refs_0_.refs_4_, bf16[128,512]{1,0:T(8,128)(2,1)S(1)} %collective-permute-done.refs_1_.refs_5_, bf16[128,512]{1,0:T(8,128)(2,1)S(1)} %collective-permute-done.1.refs_2_.refs_6_, ...), custom_call_target="tpu_custom_call" | custom-call | flops 1000 | bytes 1000 | tf_op jit(solution)/shard_map/states/pallas_call | solution.py:485
  36.1 5.7 %collective-permute-done.6.refs_11_.refs_15_ = bf16[128,2048]{1,0:T(8,128)(2,1)S(1)} collective-permute-done((bf16[128,2048]{1,0:T(8,128)(2,1)S(1)}, bf16[128,2048]{1,0:T(8,128)(2,1)S(1)}, u32[]{:S(2)}, u32[]{:S(2)}) %collective-permute-start.6) | collective-permute-done | bytes 524320 | tf_op jit(solution)/shard_map/ppermute | solution.py:401
  41.7 3.6 %collective-permute-done.7.refs_1_ = bf16[8,144,128]{2,1,0:T(8,128)(2,1)S(1)} collective-permute-done((bf16[8,144,128]{2,1,0:T(8,128)(2,1)S(1)}, bf16[8,144,128]{2,1,0:T(8,128)(2,1)S(1)}, u32[]{:S(2)}, u32[]{:S(2)}) %collective-permute-start.7) | collective-permute-done | bytes 294944 | tf_op jit(solution)/shard_map/ppermute | solution.py:406
  46.0 2.8 %collective-permute-start.8 = (bf16[8,144,128]{2,1,0:T(8,128)(2,1)S(1)}, bf16[8,144,128]{2,1,0:T(8,128)(2,1)S(1)}, u32[]{:S(2)}, u32[]{:S(2)}) collective-permute-start(bf16[8,144,128]{2,1,0:T(8,128)(2,1)S(1)} %totals.4.refs_0_), channel_id=1, source_target_pairs={{0,1},{1,0},{2,3},{3,2},{4,5},{5,4},{6,7},{7,6},{8,9},{9,8},{10,11... | collective-permute-start | bytes 884744 | tf_op jit(solution)/shard_map/ppermute | solution.py:412
  51.9 7.0 %collective-permute-done.9.refs_3_ = bf16[8,144,128]{2,1,0:T(8,128)(2,1)S(1)} collective-permute-done((bf16[8,144,128]{2,1,0:T(8,128)(2,1)S(1)}, bf16[8,144,128]{2,1,0:T(8,128)(2,1)S(1)}, u32[]{:S(2)}, u32[]{:S(2)}) %collective-permute-start.9) | collective-permute-done | bytes 294944 | tf_op jit(solution)/shard_map/ppermute | solution.py:412
  59.8 3.2 %collective-permute-start.13 = (bf16[8,144,128]{2,1,0:T(8,128)(2,1)S(1)}, bf16[8,144,128]{2,1,0:T(8,128)(2,1)S(1)}, u32[]{:S(2)}, u32[]{:S(2)}) collective-permute-start(bf16[8,144,128]{2,1,0:T(8,128)(2,1)S(1)} %get-tuple-element.78), channel_id=1, source_target_pairs={{0,16},{4,20},{8,24},{12,28},{16,0},{20,4},{24,8},{28,12},{1,17},{... | collective-permute-start | bytes 884744 | tf_op jit(solution)/shard_map/ppermute | solution.py:406
  67.2 8.3 %collective-permute-done.13.refs_17_ = bf16[8,144,128]{2,1,0:T(8,128)(2,1)S(1)} collective-permute-done((bf16[8,144,128]{2,1,0:T(8,128)(2,1)S(1)}, bf16[8,144,128]{2,1,0:T(8,128)(2,1)S(1)}, u32[]{:S(2)}, u32[]{:S(2)}) %collective-permute-start.13) | collective-permute-done | bytes 294944 | tf_op jit(solution)/shard_map/ppermute | solution.py:406
  76.2 11.5 %blocks.3 = (bf16[128,1024]{1,0:T(8,128)(2,1)}, bf16[128,1024]{1,0:T(8,128)(2,1)}, bf16[128,1024]{1,0:T(8,128)(2,1)}, bf16[128,1024]{1,0:T(8,128)(2,1)}, f32[8,1...) custom-call(s32[49]{0:T(128)} %copy-done.26, ...), custom_call_target="tpu_custom_call" | custom-call | flops 1000 | bytes 1000 | tf_op jit(solution)/shard_map/blocks/pallas_call | solution.py:485
  87.9 2.8 %collective-permute-done.12.refs_11_.refs_15_ = bf16[128,2048]{1,0:T(8,128)(2,1)S(1)} collective-permute-done((bf16[128,2048]{1,0:T(8,128)(2,1)S(1)}, bf16[128,2048]{1,0:T(8,128)(2,1)S(1)}, u32[]{:S(2)}, u32[]{:S(2)}) %collective-permute-start.12) | collective-permute-done | bytes 524320 | tf_op jit(solution)/shard_map/ppermute | solution.py:401
  91.5 11.6 %blocks.2 = (bf16[128,1024]{1,0:T(8,128)(2,1)}, bf16[128,1024]{1,0:T(8,128)(2,1)}, bf16[128,1024]{1,0:T(8,128)(2,1)}, bf16[128,1024]{1,0:T(8,128)(2,1)}, f32[8,1...) custom-call(s32[49]{0:T(128)} %copy-done.26, ...), custom_call_target="tpu_custom_call" | custom-call | flops 1000 | bytes 1000 | tf_op jit(solution)/shard_map/blocks/pallas_call | solution.py:485
  104.9 3.8 %collective-permute-start.15 = (bf16[8,144,128]{2,1,0:T(8,128)(2,1)S(1)}, bf16[8,144,128]{2,1,0:T(8,128)(2,1)S(1)}, u32[]{:S(2)}, u32[]{:S(2)}) collective-permute-start(bf16[8,144,128]{2,1,0:T(8,128)(2,1)S(1)} %totals.6.refs_0_), channel_id=1, source_target_pairs={{0,1},{1,0},{2,3},{3,2},{4,5},{5,4},{6,7},{7,6},{8,9},{9,8},{10,11... | collective-permute-start | bytes 884744 | tf_op jit(solution)/shard_map/ppermute | solution.py:412
  111.8 5.6 %collective-permute-start.19 = (bf16[128,1024]{1,0:T(8,128)(2,1)S(1)}, bf16[128,1024]{1,0:T(8,128)(2,1)S(1)}, u32[]{:S(2)}, u32[]{:S(2)}) collective-permute-start(bf16[128,1024]{1,0:T(8,128)(2,1)S(1)} %copy-done.44), channel_id=1, source_target_pairs={{0,4},{4,8},{8,12},{12,0},{16,20},{20,24},{24,28},{28,16},{1,5},{5... | collective-permute-start | bytes 786440 | tf_op jit(solution)/shard_map/ppermute | solution.py:401
  120.4 3.6 %collective-permute-start.23 = (bf16[8,144,128]{2,1,0:T(8,128)(2,1)S(1)}, bf16[8,144,128]{2,1,0:T(8,128)(2,1)S(1)}, u32[]{:S(2)}, u32[]{:S(2)}) collective-permute-start(bf16[8,144,128]{2,1,0:T(8,128)(2,1)S(1)} %get-tuple-element.99), channel_id=1, source_target_pairs={{0,16},{4,20},{8,24},{12,28},{16,0},{20,4},{24,8},{28,12},{1,17},{... | collective-permute-start | bytes 884744 | tf_op jit(solution)/shard_map/ppermute | solution.py:406
  125.7 4.7 %keys.2 = (bf16[4,128,512]{2,1,0:T(8,128)(2,1)}, bf16[4,128,128]{2,1,0:T(8,128)(2,1)S(1)}) custom-call(s32[49]{0:T(128)S(1)} %copy-done.27, bf16[128,512]{1,0:T(8,128)(2,1)S(1)} %copy-done.5, bf16[128,512]{1,0:T(8,128)(2,1)S(1)} %copy-done.7, bf16[128,512]{1,0:T(8,128)(2,1)S(1)} %copy-done.9, bf16[128,512]{1,0:T(8,128)(2,1)S(1)} %copy-done.11, ...), custom_call_target="tpu_custom_call" | custom-call | flops 1000 | bytes 1000 | tf_op jit(solution)/shard_map/keys/pallas_call | solution.py:485
  130.4 6.5 %collective-permute-start.22 = (bf16[128,1024]{1,0:T(8,128)(2,1)S(1)}, bf16[128,1024]{1,0:T(8,128)(2,1)S(1)}, u32[]{:S(2)}, u32[]{:S(2)}) collective-permute-start(bf16[128,1024]{1,0:T(8,128)(2,1)S(1)} %copy-done.41), channel_id=1, source_target_pairs={{0,4},{4,8},{8,12},{12,0},{16,20},{20,24},{24,28},{28,16},{1,5},{5... | collective-permute-start | bytes 786440 | tf_op jit(solution)/shard_map/ppermute | solution.py:401
  138.2 4.8 %keys.3 = (bf16[4,128,512]{2,1,0:T(8,128)(2,1)}, bf16[4,128,128]{2,1,0:T(8,128)(2,1)S(1)}) custom-call(s32[49]{0:T(128)S(1)} %copy-done.27, bf16[128,512]{1,0:T(8,128)(2,1)S(1)} %copy-done.5, bf16[128,512]{1,0:T(8,128)(2,1)S(1)} %copy-done.7, bf16[128,512]{1,0:T(8,128)(2,1)S(1)} %copy-done.9, ...), custom_call_target="tpu_custom_call", output_to_operand_aliasing={{0}: (13, {})} | custom-call | flops 1000 | bytes 1000 | tf_op jit(solution)/shard_map/keys/pallas_call | solution.py:485
  143.0 3.3 %collective-permute-done.20 = bf16[128,1024]{1,0:T(8,128)(2,1)S(1)} collective-permute-done((bf16[128,1024]{1,0:T(8,128)(2,1)S(1)}, bf16[128,1024]{1,0:T(8,128)(2,1)S(1)}, u32[]{:S(2)}, u32[]{:S(2)}) %collective-permute-start.20) | collective-permute-done | bytes 262176 | tf_op jit(solution)/shard_map/ppermute | solution.py:401
  146.3 4.9 %all-to-all-start = ((bf16[4,128,512]{2,1,0:T(8,128)(2,1)}), bf16[4,128,512]{2,1,0:T(8,128)(2,1)S(1)}, u32[]{:S(2)}, u32[]{:S(2)}) async-start(bf16[4,128,512]{2,1,0:T(8,128)(2,1)} %get-tuple-element.104), calls=%async_computation | async-start | bytes 1048576 | tf_op jit(solution)/shard_map/all_to_all | solution.py:398
  153.6 4.0 %collective-permute-start.28 = (bf16[2,4,32,128]{3,2,1,0:T(8,128)(2,1)S(1)}, bf16[2,4,32,128]{3,2,1,0:T(8,128)(2,1)S(1)}, u32[]{:S(2)}, u32[]{:S(2)}) collective-permute-start(bf16[2,4,32,128]{3,2,1,0:T(8,128)(2,1)S(1)} %get-tuple-element.116), channel_id=1, source_target_pairs={{0,17},{1,18},{2,19},{3,16},{4,21},{5,22},{6,23},{7,20},{8,25},{9,... | collective-permute-start | bytes 196616 | tf_op jit(solution)/shard_map/ppermute | solution.py:420
  164.9 3.2 %collective-permute-done.29.refs_5_ = bf16[2,4,32,128]{3,2,1,0:T(8,128)(2,1)S(1)} collective-permute-done((bf16[2,4,32,128]{3,2,1,0:T(8,128)(2,1)S(1)}, bf16[2,4,32,128]{3,2,1,0:T(8,128)(2,1)S(1)}, u32[]{:S(2)}, u32[]{:S(2)}) %collective-permute-start.29) | collective-permute-done | bytes 65568 | tf_op jit(solution)/shard_map/ppermute | solution.py:420
  (157 shorter events, 49.4 us)
Async XLA Ops:
  4.2 9.5 %collective-permute-start = (bf16[128,512]{1,0:T(8,128)(2,1)S(1)}, bf16[128,512]{1,0:T(8,128)(2,1)S(1)}, u32[]{:S(2)}, u32[]{:S(2)}) collective-permute-start(bf16[128,512]{1,0:T(8,128)(2,1)S(1)} %get-tuple-element.61), channel_id=1, source_target_pairs={{0,4},{4,8},{8,12},{12,0},{16,20},{20,24},{24,28},{28,16},{1,5},{5... | collective-permute-start | bytes 393224 | tf_op jit(solution)/shard_map/ppermute | solution.py:401
  14.9 21.2 %collective-permute-start.4 = (bf16[128,2048]{1,0:T(8,128)(2,1)S(1)}, bf16[128,2048]{1,0:T(8,128)(2,1)S(1)}, u32[]{:S(2)}, u32[]{:S(2)}) collective-permute-start(bf16[128,2048]{1,0:T(8,128)(2,1)S(1)} %get-tuple-element.66), channel_id=1, source_target_pairs={{0,4},{4,8},{8,12},{12,0},{16,20},{20,24},{24,28},{28,16},{1,5},{5... | collective-permute-start | bytes 1572872 | tf_op jit(solution)/shard_map/ppermute | solution.py:401
  16.2 19.8 %collective-permute-start.5 = (bf16[128,2048]{1,0:T(8,128)(2,1)S(1)}, bf16[128,2048]{1,0:T(8,128)(2,1)S(1)}, u32[]{:S(2)}, u32[]{:S(2)}) collective-permute-start(bf16[128,2048]{1,0:T(8,128)(2,1)S(1)} %get-tuple-element.67), channel_id=1, source_target_pairs={{0,8},{4,12},{8,0},{12,4},{16,24},{20,28},{24,16},{28,20},{1,9},{5... | collective-permute-start | bytes 1572872 | tf_op jit(solution)/shard_map/ppermute | solution.py:401
  18.4 23.3 %collective-permute-start.6 = (bf16[128,2048]{1,0:T(8,128)(2,1)S(1)}, bf16[128,2048]{1,0:T(8,128)(2,1)S(1)}, u32[]{:S(2)}, u32[]{:S(2)}) collective-permute-start(bf16[128,2048]{1,0:T(8,128)(2,1)S(1)} %get-tuple-element.68), channel_id=1, source_target_pairs={{0,12},{4,0},{8,4},{12,8},{16,28},{20,16},{24,20},{28,24},{1,13},{... | collective-permute-start | bytes 1572872 | tf_op jit(solution)/shard_map/ppermute | solution.py:401
  33.1 12.3 %collective-permute-start.7 = (bf16[8,144,128]{2,1,0:T(8,128)(2,1)S(1)}, bf16[8,144,128]{2,1,0:T(8,128)(2,1)S(1)}, u32[]{:S(2)}, u32[]{:S(2)}) collective-permute-start(bf16[8,144,128]{2,1,0:T(8,128)(2,1)S(1)} %states.3), channel_id=1, source_target_pairs={{0,16},{4,20},{8,24},{12,28},{16,0},{20,4},{24,8},{28,12},{1,17},{... | collective-permute-start | bytes 884744 | tf_op jit(solution)/shard_map/ppermute | solution.py:406
  50.7 8.3 %collective-permute-start.9 = (bf16[8,144,128]{2,1,0:T(8,128)(2,1)S(1)}, bf16[8,144,128]{2,1,0:T(8,128)(2,1)S(1)}, u32[]{:S(2)}, u32[]{:S(2)}) collective-permute-start(bf16[8,144,128]{2,1,0:T(8,128)(2,1)S(1)} %totals.5), channel_id=1, source_target_pairs={{0,2},{1,3},{2,0},{3,1},{4,6},{5,7},{6,4},{7,5},{8,10},{9,11},{10,... | collective-permute-start | bytes 884744 | tf_op jit(solution)/shard_map/ppermute | solution.py:412
  59.8 15.7 %collective-permute-start.13 = (bf16[8,144,128]{2,1,0:T(8,128)(2,1)S(1)}, bf16[8,144,128]{2,1,0:T(8,128)(2,1)S(1)}, u32[]{:S(2)}, u32[]{:S(2)}) collective-permute-start(bf16[8,144,128]{2,1,0:T(8,128)(2,1)S(1)} %get-tuple-element.78), channel_id=1, source_target_pairs={{0,16},{4,20},{8,24},{12,28},{16,0},{20,4},{24,8},{28,12},{1,17},{... | collective-permute-start | bytes 884744 | tf_op jit(solution)/shard_map/ppermute | solution.py:406
  64.9 22.9 %collective-permute-start.10 = (bf16[128,2048]{1,0:T(8,128)(2,1)S(1)}, bf16[128,2048]{1,0:T(8,128)(2,1)S(1)}, u32[]{:S(2)}, u32[]{:S(2)}) collective-permute-start(bf16[128,2048]{1,0:T(8,128)(2,1)S(1)} %get-tuple-element.73), channel_id=1, source_target_pairs={{0,4},{4,8},{8,12},{12,0},{16,20},{20,24},{24,28},{28,16},{1,5},{5... | collective-permute-start | bytes 1572872 | tf_op jit(solution)/shard_map/ppermute | solution.py:401
  65.5 22.3 %collective-permute-start.11 = (bf16[128,2048]{1,0:T(8,128)(2,1)S(1)}, bf16[128,2048]{1,0:T(8,128)(2,1)S(1)}, u32[]{:S(2)}, u32[]{:S(2)}) collective-permute-start(bf16[128,2048]{1,0:T(8,128)(2,1)S(1)} %get-tuple-element.74), channel_id=1, source_target_pairs={{0,8},{4,12},{8,0},{12,4},{16,24},{20,28},{24,16},{28,20},{1,9},{5... | collective-permute-start | bytes 1572872 | tf_op jit(solution)/shard_map/ppermute | solution.py:401
  66.8 23.9 %collective-permute-start.12 = (bf16[128,2048]{1,0:T(8,128)(2,1)S(1)}, bf16[128,2048]{1,0:T(8,128)(2,1)S(1)}, u32[]{:S(2)}, u32[]{:S(2)}) collective-permute-start(bf16[128,2048]{1,0:T(8,128)(2,1)S(1)} %get-tuple-element.75), channel_id=1, source_target_pairs={{0,12},{4,0},{8,4},{12,8},{16,28},{20,16},{24,20},{28,24},{1,13},{... | collective-permute-start | bytes 1572872 | tf_op jit(solution)/shard_map/ppermute | solution.py:401
  87.7 15.4 %collective-permute-start.14 = (bf16[8,144,128]{2,1,0:T(8,128)(2,1)}, bf16[8,144,128]{2,1,0:T(8,128)(2,1)S(1)}, u32[]{:S(2)}, u32[]{:S(2)}) collective-permute-start(bf16[8,144,128]{2,1,0:T(8,128)(2,1)} %get-tuple-element.79), channel_id=1, source_target_pairs={{0,16},{4,20},{8,24},{12,28},{16,0},{20,4},{24,8},{28,12},{1,17},{... | collective-permute-start | bytes 884744 | tf_op jit(solution)/shard_map/ppermute | solution.py:406
  110.5 8.3 %collective-permute-start.16 = (bf16[8,144,128]{2,1,0:T(8,128)(2,1)S(1)}, bf16[8,144,128]{2,1,0:T(8,128)(2,1)S(1)}, u32[]{:S(2)}, u32[]{:S(2)}) collective-permute-start(bf16[8,144,128]{2,1,0:T(8,128)(2,1)S(1)} %totals.7), channel_id=1, source_target_pairs={{0,2},{1,3},{2,0},{3,1},{4,6},{5,7},{6,4},{7,5},{8,10},{9,11},{10,... | collective-permute-start | bytes 884744 | tf_op jit(solution)/shard_map/ppermute | solution.py:412
  111.8 18.6 %collective-permute-start.19 = (bf16[128,1024]{1,0:T(8,128)(2,1)S(1)}, bf16[128,1024]{1,0:T(8,128)(2,1)S(1)}, u32[]{:S(2)}, u32[]{:S(2)}) collective-permute-start(bf16[128,1024]{1,0:T(8,128)(2,1)S(1)} %copy-done.44), channel_id=1, source_target_pairs={{0,4},{4,8},{8,12},{12,0},{16,20},{20,24},{24,28},{28,16},{1,5},{5... | collective-permute-start | bytes 786440 | tf_op jit(solution)/shard_map/ppermute | solution.py:401
  117.5 13.0 %collective-permute-start.18 = (bf16[128,1024]{1,0:T(8,128)(2,1)S(1)}, bf16[128,1024]{1,0:T(8,128)(2,1)S(1)}, u32[]{:S(2)}, u32[]{:S(2)}) collective-permute-start(bf16[128,1024]{1,0:T(8,128)(2,1)S(1)} %copy-done.43), channel_id=1, source_target_pairs={{0,8},{4,12},{8,0},{12,4},{16,24},{20,28},{24,16},{28,20},{1,9},{5... | collective-permute-start | bytes 786440 | tf_op jit(solution)/shard_map/ppermute | solution.py:401
  117.5 13.0 %collective-permute-start.17 = (bf16[128,1024]{1,0:T(8,128)(2,1)S(1)}, bf16[128,1024]{1,0:T(8,128)(2,1)S(1)}, u32[]{:S(2)}, u32[]{:S(2)}) collective-permute-start(bf16[128,1024]{1,0:T(8,128)(2,1)S(1)} %copy-done.42), channel_id=1, source_target_pairs={{0,12},{4,0},{8,4},{12,8},{16,28},{20,16},{24,20},{28,24},{1,13},{... | collective-permute-start | bytes 786440 | tf_op jit(solution)/shard_map/ppermute | solution.py:401
  120.4 17.8 %collective-permute-start.23 = (bf16[8,144,128]{2,1,0:T(8,128)(2,1)S(1)}, bf16[8,144,128]{2,1,0:T(8,128)(2,1)S(1)}, u32[]{:S(2)}, u32[]{:S(2)}) collective-permute-start(bf16[8,144,128]{2,1,0:T(8,128)(2,1)S(1)} %get-tuple-element.99), channel_id=1, source_target_pairs={{0,16},{4,20},{8,24},{12,28},{16,0},{20,4},{24,8},{28,12},{1,17},{... | collective-permute-start | bytes 884744 | tf_op jit(solution)/shard_map/ppermute | solution.py:406
  130.4 12.5 %collective-permute-start.22 = (bf16[128,1024]{1,0:T(8,128)(2,1)S(1)}, bf16[128,1024]{1,0:T(8,128)(2,1)S(1)}, u32[]{:S(2)}, u32[]{:S(2)}) collective-permute-start(bf16[128,1024]{1,0:T(8,128)(2,1)S(1)} %copy-done.41), channel_id=1, source_target_pairs={{0,4},{4,8},{8,12},{12,0},{16,20},{20,24},{24,28},{28,16},{1,5},{5... | collective-permute-start | bytes 786440 | tf_op jit(solution)/shard_map/ppermute | solution.py:401
  136.9 9.4 %collective-permute-start.20 = (bf16[128,1024]{1,0:T(8,128)(2,1)S(1)}, bf16[128,1024]{1,0:T(8,128)(2,1)S(1)}, u32[]{:S(2)}, u32[]{:S(2)}) collective-permute-start(bf16[128,1024]{1,0:T(8,128)(2,1)S(1)} %copy-done.39), channel_id=1, source_target_pairs={{0,12},{4,0},{8,4},{12,8},{16,28},{20,16},{24,20},{28,24},{1,13},{... | collective-permute-start | bytes 786440 | tf_op jit(solution)/shard_map/ppermute | solution.py:401
  146.3 24.4 %all-to-all-start = ((bf16[4,128,512]{2,1,0:T(8,128)(2,1)}), bf16[4,128,512]{2,1,0:T(8,128)(2,1)S(1)}, u32[]{:S(2)}, u32[]{:S(2)}) async-start(bf16[4,128,512]{2,1,0:T(8,128)(2,1)} %get-tuple-element.104), calls=%async_computation | async-start | bytes 1048576 | tf_op jit(solution)/shard_map/all_to_all | solution.py:398
  151.3 10.2 %collective-permute-start.27 = (bf16[2,4,32,128]{3,2,1,0:T(8,128)(2,1)S(1)}, bf16[2,4,32,128]{3,2,1,0:T(8,128)(2,1)S(1)}, u32[]{:S(2)}, u32[]{:S(2)}) collective-permute-start(bf16[2,4,32,128]{3,2,1,0:T(8,128)(2,1)S(1)} %get-tuple-element.115), channel_id=1, source_target_pairs={{0,16},{1,17},{2,18},{3,19},{4,20},{5,21},{6,22},{7,23},{8,24},{9,... | collective-permute-start | bytes 196616 | tf_op jit(solution)/shard_map/ppermute | solution.py:420
  153.6 9.1 %collective-permute-start.28 = (bf16[2,4,32,128]{3,2,1,0:T(8,128)(2,1)S(1)}, bf16[2,4,32,128]{3,2,1,0:T(8,128)(2,1)S(1)}, u32[]{:S(2)}, u32[]{:S(2)}) collective-permute-start(bf16[2,4,32,128]{3,2,1,0:T(8,128)(2,1)S(1)} %get-tuple-element.116), channel_id=1, source_target_pairs={{0,17},{1,18},{2,19},{3,16},{4,21},{5,22},{6,23},{7,20},{8,25},{9,... | collective-permute-start | bytes 196616 | tf_op jit(solution)/shard_map/ppermute | solution.py:420
  157.6 10.5 %collective-permute-start.29 = (bf16[2,4,32,128]{3,2,1,0:T(8,128)(2,1)S(1)}, bf16[2,4,32,128]{3,2,1,0:T(8,128)(2,1)S(1)}, u32[]{:S(2)}, u32[]{:S(2)}) collective-permute-start(bf16[2,4,32,128]{3,2,1,0:T(8,128)(2,1)S(1)} %get-tuple-element.117), channel_id=1, source_target_pairs={{0,18},{1,19},{2,16},{3,17},{4,22},{5,23},{6,20},{7,21},{8,26},{9,... | collective-permute-start | bytes 196616 | tf_op jit(solution)/shard_map/ppermute | solution.py:420
  158.7 10.7 %collective-permute-start.30 = (bf16[2,4,32,128]{3,2,1,0:T(8,128)(2,1)S(1)}, bf16[2,4,32,128]{3,2,1,0:T(8,128)(2,1)S(1)}, u32[]{:S(2)}, u32[]{:S(2)}) collective-permute-start(bf16[2,4,32,128]{3,2,1,0:T(8,128)(2,1)S(1)} %get-tuple-element.114), channel_id=1, source_target_pairs={{0,19},{1,16},{2,17},{3,18},{4,23},{5,20},{6,21},{7,22},{8,27},{9,... | collective-permute-start | bytes 196616 | tf_op jit(solution)/shard_map/ppermute | solution.py:420
  159.2 10.2 %collective-permute-start.24 = (bf16[2,4,32,128]{3,2,1,0:T(8,128)(2,1)S(1)}, bf16[2,4,32,128]{3,2,1,0:T(8,128)(2,1)S(1)}, u32[]{:S(2)}, u32[]{:S(2)}) collective-permute-start(bf16[2,4,32,128]{3,2,1,0:T(8,128)(2,1)S(1)} %get-tuple-element.120), channel_id=1, source_target_pairs={{0,1},{1,2},{2,3},{3,0},{4,5},{5,6},{6,7},{7,4},{8,9},{9,10},{10,1... | collective-permute-start | bytes 196616 | tf_op jit(solution)/shard_map/ppermute | solution.py:409
  (53 other events, 743.9 us)

commit v17 on v16

--- a/solution.py
+++ b/solution.py
@@ -448,8 +448,8 @@
     kv = [kv_sent[0]] + [around(kv_sent[r], r) for r in shifts[1:]]
     maps = lax.all_gather(near_maps, "fsdp")
 
-    def sent_rows(s, *earlier):
-        sent = pack(
+    def packed_rows(s, *earlier):
+        return pack(
             after(table, *earlier),
             base["sent"] + s * part,
             (query_rows, grad_out),
@@ -457,7 +457,9 @@
             1,
             heads * hd,
         )
-        return [sent[0]] + [around(sent[r], r) for r in shifts[1:]]
+
+    def sent_rows(sent, *begin):
+        return [sent[0]] + [around(after(sent[r], *begin), r) for r in shifts[1:]]
 
     def piece_specs(column, count):
         return [pl.BlockSpec((tok, count * hd), lambda h, t: (0, column(h)))] * part
@@ -535,12 +537,14 @@
 
     partial = {s: states_of(s) for s in order}
     parts = [partial[0]] + [across(partial[s], s) for s in slots[1:]]
-    rows = {order[0]: sent_rows(order[0], near_maps, *kv)}
+    rows = {order[0]: sent_rows(packed_rows(order[0], near_maps, *kv), near_maps)}
     parts[0] = after(parts[0], *rows[order[0]])
     others = around_all(totals_of(parts))
+    packed = {s: packed_rows(s, others[0]) for s in order[1:]}
+    others[-1] = after(others[-1], *[packed[s][0] for s in packed])
     state, _ = spread(parts, others, "before", [prefix_state, prefix_norm], False)
     for s in order[1:]:
-        rows[s] = sent_rows(s, state[0])
+        rows[s] = sent_rows(packed[s], state[0])
 
     def block_of(s):
         return call(

time: 173 us -> 172 us (level)
  starting transfers between devices: 61.9 us -> 52.7 us
  waiting for transfers between devices: 40.1 us -> 48.7 us
    ppermute x15, starting transfers between devices: 26.9 us -> 19.2 us  [around(): lax.ppermute(array, 'ctx', [(d, d // part * part + (d + shift) % part) fo...]
    ppermute x5, starting transfers between devices: 9.28 us -> 5.23 us  [across(): lax.ppermute(array, 'ctx', [(d, (d + shift * part) % ctx) for d in range(...]
    ppermute x15, waiting for transfers between devices: 11.8 us -> 15.8 us  [around(): lax.ppermute(array, 'ctx', [(d, d // part * part + (d + shift) % part) fo...]
    all_to_all x1, starting transfers between devices: 4.93 us -> 8.07 us  [within(): lax.all_to_all(array, 'ctx', 0, 0, axis_index_groups=blocks_of, tiled=True)]
    ppermute x4, waiting for transfers between devices: 9.55 us -> 12.5 us  [twin(): return lax.ppermute(array, 'fsdp', [(d, d ^ bit) for d in range(fsdp)])]
    ppermute x5, waiting for transfers between devices: 14.2 us -> 17.1 us  [across(): lax.ppermute(array, 'ctx', [(d, (d + shift * part) % ctx) for d in range(...]
  transfers between devices with their start and end apart: 32 -> 32, of which waited for: 12 -> 14; matrix products, arithmetic and copies ran while one was open for 0% -> 0% of each run, Pallas kernels for 26% -> 26%
where the time goes in v17:
time: 172 us
  starting transfers between devices  52.7 us (31%)
  Pallas kernels  51.2 us (30%)
  waiting for transfers between devices  48.7 us (28%)
  blocking collectives  9.99 us (6%)
  local copies, waits for them, and re-layouts  7.2 us (4%)
    pallas_call x6, Pallas kernels, call(): pl.pallas_call(functools.partial(kernel, part, base['sorted']), out_shape...  38.1 us
    ppermute x15, starting transfers between devices, around(): lax.ppermute(array, 'ctx', [(d, d // part * part + (d + shift) % part) fo...  19.2 us
    ppermute x5, waiting for transfers between devices, across(): lax.ppermute(array, 'ctx', [(d, (d + shift * part) % ctx) for d in range(...  17.1 us
    ppermute x15, waiting for transfers between devices, around(): lax.ppermute(array, 'ctx', [(d, d // part * part + (d + shift) % part) fo...  15.8 us
    ppermute x4, waiting for transfers between devices, twin(): return lax.ppermute(array, 'fsdp', [(d, d ^ bit) for d in range(fsdp)])  12.5 us
    all_gather x1, blocking collectives, shards(): maps = lax.all_gather(near_maps, 'fsdp')  9.99 us
    ppermute x4, starting transfers between devices, twin(): return lax.ppermute(array, 'fsdp', [(d, d ^ bit) for d in range(fsdp)])  9.69 us
    all_to_all x1, starting transfers between devices, within(): lax.all_to_all(array, 'ctx', 0, 0, axis_index_groups=blocks_of, tiled=True)  8.07 us
  transfers between devices with their start and end apart: 32, of which 14 were waited for; matrix products, arithmetic and copies ran while one was open for 0% of the time, Pallas kernels for 26%

profile of v17, /device:TPU:1, one launch (start us, length us, event | category | flops | bytes accessed | tf_op | source)
XLA Modules:
  0.0 171.5 jit_solution(10407069340880532206)
XLA Ops:
  8.9 2.4 %collective-permute-start.3 = (bf16[8,32,128]{2,1,0:T(8,128)(2,1)S(1)}, bf16[8,32,128]{2,1,0:T(8,128)(2,1)S(1)}, u32[]{:S(2)}, u32[]{:S(2)}) collective-permute-start(bf16[8,32,128]{2,1,0:T(8,128)(2,1)S(1)} %pad_maximum_fusion.2), channel_id=1, source_target_pairs={{0,16},{4,20},{8,24},{12,28},{16,0},{20,4},{24,8},{28,12},{1,17},{... | collective-permute-start | bytes 196616 | tf_op jit(solution)/shard_map/ppermute | solution.py:406
  11.3 2.4 %collective-permute-done.3 = bf16[8,32,128]{2,1,0:T(8,128)(2,1)S(1)} collective-permute-done((bf16[8,32,128]{2,1,0:T(8,128)(2,1)S(1)}, bf16[8,32,128]{2,1,0:T(8,128)(2,1)S(1)}, u32[]{:S(2)}, u32[]{:S(2)}) %collective-permute-start.3) | collective-permute-done | bytes 65568 | tf_op jit(solution)/shard_map/ppermute | solution.py:406
  14.9 3.0 %collective-permute-start.5 = (bf16[128,2048]{1,0:T(8,128)(2,1)S(1)}, bf16[128,2048]{1,0:T(8,128)(2,1)S(1)}, u32[]{:S(2)}, u32[]{:S(2)}) collective-permute-start(bf16[128,2048]{1,0:T(8,128)(2,1)S(1)} %get-tuple-element.76), channel_id=1, source_target_pairs={{0,8},{4,12},{8,0},{12,4},{16,24},{20,28},{24,16},{28,20},{1,9},{5... | collective-permute-start | bytes 1572872 | tf_op jit(solution)/shard_map/ppermute | solution.py:401
  19.3 10.0 %all-gather = bf16[8,8,32,128]{3,2,1,0:T(8,128)(2,1)S(1)} all-gather(bf16[2,8,32,128]{3,2,1,0:T(8,128)(2,1)S(1)} %pad_maximum_fusion.1), channel_id=2, replica_groups=mesh['ctx'=8,'fsdp'=4] {'fsdp'}, dimensions={0}, use_global_device_ids=true | all-gather | bytes 655360 | tf_op jit(solution)/shard_map/all_gather | solution.py:449
  29.3 2.8 %states.3 = bf16[8,144,128]{2,1,0:T(8,128)(2,1)S(1)} custom-call(s32[49]{0:T(128)S(1)} %stack.194.table, bf16[128,512]{1,0:T(8,128)(2,1)S(1)} %get-tuple-element.67.refs_0_.refs_4_, bf16[128,512]{1,0:T(8,128)(2,1)S(1)} %collective-permute-done.refs_1_.refs_5_, bf16[128,512]{1,0:T(8,128)(2,1)S(1)} %collective-permute-done.1.refs_2_.refs_6_, ...), custom_call_target="tpu_custom_call" | custom-call | flops 1000 | bytes 1000 | tf_op jit(solution)/shard_map/states/pallas_call | solution.py:487
  32.9 2.8 %states.2.refs_0_ = bf16[8,144,128]{2,1,0:T(8,128)(2,1)S(1)} custom-call(s32[49]{0:T(128)S(1)} %stack.194.table, bf16[128,512]{1,0:T(8,128)(2,1)S(1)} %get-tuple-element.67.refs_0_.refs_4_, bf16[128,512]{1,0:T(8,128)(2,1)S(1)} %collective-permute-done.refs_1_.refs_5_, bf16[128,512]{1,0:T(8,128)(2,1)S(1)} %collective-permute-done.1.refs_2_.refs_6_, ...), custom_call_target="tpu_custom_call" | custom-call | flops 1000 | bytes 1000 | tf_op jit(solution)/shard_map/states/pallas_call | solution.py:487
  35.7 2.5 %collective-permute-done.6.refs_11_.refs_15_ = bf16[128,2048]{1,0:T(8,128)(2,1)S(1)} collective-permute-done((bf16[128,2048]{1,0:T(8,128)(2,1)S(1)}, bf16[128,2048]{1,0:T(8,128)(2,1)S(1)}, u32[]{:S(2)}, u32[]{:S(2)}) %collective-permute-start.6) | collective-permute-done | bytes 524320 | tf_op jit(solution)/shard_map/ppermute | solution.py:401
  38.2 7.6 %collective-permute-done.4.refs_9_.refs_13_ = bf16[128,2048]{1,0:T(8,128)(2,1)S(1)} collective-permute-done((bf16[128,2048]{1,0:T(8,128)(2,1)S(1)}, bf16[128,2048]{1,0:T(8,128)(2,1)S(1)}, u32[]{:S(2)}, u32[]{:S(2)}) %collective-permute-start.4) | collective-permute-done | bytes 524320 | tf_op jit(solution)/shard_map/ppermute | solution.py:401
  46.5 2.8 %collective-permute-start.8 = (bf16[8,144,128]{2,1,0:T(8,128)(2,1)S(1)}, bf16[8,144,128]{2,1,0:T(8,128)(2,1)S(1)}, u32[]{:S(2)}, u32[]{:S(2)}) collective-permute-start(bf16[8,144,128]{2,1,0:T(8,128)(2,1)S(1)} %totals.4.refs_0_), channel_id=1, source_target_pairs={{0,1},{1,0},{2,3},{3,2},{4,5},{5,4},{6,7},{7,6},{8,9},{9,8},{10,11... | collective-permute-start | bytes 884744 | tf_op jit(solution)/shard_map/ppermute | solution.py:412
  53.6 5.9 %collective-permute-done.9.refs_3_ = bf16[8,144,128]{2,1,0:T(8,128)(2,1)S(1)} collective-permute-done((bf16[8,144,128]{2,1,0:T(8,128)(2,1)S(1)}, bf16[8,144,128]{2,1,0:T(8,128)(2,1)S(1)}, u32[]{:S(2)}, u32[]{:S(2)}) %collective-permute-start.9) | collective-permute-done | bytes 294944 | tf_op jit(solution)/shard_map/ppermute | solution.py:412
  65.6 10.8 %collective-permute-done.13.refs_17_ = bf16[8,144,128]{2,1,0:T(8,128)(2,1)S(1)} collective-permute-done((bf16[8,144,128]{2,1,0:T(8,128)(2,1)S(1)}, bf16[8,144,128]{2,1,0:T(8,128)(2,1)S(1)}, u32[]{:S(2)}, u32[]{:S(2)}) %collective-permute-start.13) | collective-permute-done | bytes 294944 | tf_op jit(solution)/shard_map/ppermute | solution.py:406
  77.2 11.5 %blocks.3 = (bf16[128,1024]{1,0:T(8,128)(2,1)}, bf16[128,1024]{1,0:T(8,128)(2,1)}, bf16[128,1024]{1,0:T(8,128)(2,1)}, bf16[128,1024]{1,0:T(8,128)(2,1)}, f32[8,1...) custom-call(s32[49]{0:T(128)} %copy-done.26, ...), custom_call_target="tpu_custom_call" | custom-call | flops 1000 | bytes 1000 | tf_op jit(solution)/shard_map/blocks/pallas_call | solution.py:487
  88.8 3.3 %collective-permute-done.11.refs_10_.refs_14_ = bf16[128,2048]{1,0:T(8,128)(2,1)S(1)} collective-permute-done((bf16[128,2048]{1,0:T(8,128)(2,1)S(1)}, bf16[128,2048]{1,0:T(8,128)(2,1)S(1)}, u32[]{:S(2)}, u32[]{:S(2)}) %collective-permute-start.11) | collective-permute-done | bytes 524320 | tf_op jit(solution)/shard_map/ppermute | solution.py:401
  93.7 11.5 %blocks.2 = (bf16[128,1024]{1,0:T(8,128)(2,1)}, bf16[128,1024]{1,0:T(8,128)(2,1)}, bf16[128,1024]{1,0:T(8,128)(2,1)}, bf16[128,1024]{1,0:T(8,128)(2,1)}, f32[8,1...) custom-call(s32[49]{0:T(128)} %copy-done.26, ...), custom_call_target="tpu_custom_call" | custom-call | flops 1000 | bytes 1000 | tf_op jit(solution)/shard_map/blocks/pallas_call | solution.py:487
  106.9 4.3 %collective-permute-start.15 = (bf16[8,144,128]{2,1,0:T(8,128)(2,1)S(1)}, bf16[8,144,128]{2,1,0:T(8,128)(2,1)S(1)}, u32[]{:S(2)}, u32[]{:S(2)}) collective-permute-start(bf16[8,144,128]{2,1,0:T(8,128)(2,1)S(1)} %totals.6.refs_0_), channel_id=1, source_target_pairs={{0,1},{1,0},{2,3},{3,2},{4,5},{5,4},{6,7},{7,6},{8,9},{9,8},{10,11... | collective-permute-start | bytes 884744 | tf_op jit(solution)/shard_map/ppermute | solution.py:412
  115.0 2.3 %collective-permute-start.17 = (bf16[128,1024]{1,0:T(8,128)(2,1)S(1)}, bf16[128,1024]{1,0:T(8,128)(2,1)S(1)}, u32[]{:S(2)}, u32[]{:S(2)}) collective-permute-start(bf16[128,1024]{1,0:T(8,128)(2,1)S(1)} %copy-done.42), channel_id=1, source_target_pairs={{0,12},{4,0},{8,4},{12,8},{16,28},{20,16},{24,20},{28,24},{1,13},{... | collective-permute-start | bytes 786440 | tf_op jit(solution)/shard_map/ppermute | solution.py:401
  117.3 4.1 %collective-permute-done.16.refs_3_ = bf16[8,144,128]{2,1,0:T(8,128)(2,1)S(1)} collective-permute-done((bf16[8,144,128]{2,1,0:T(8,128)(2,1)S(1)}, bf16[8,144,128]{2,1,0:T(8,128)(2,1)S(1)}, u32[]{:S(2)}, u32[]{:S(2)}) %collective-permute-start.16) | collective-permute-done | bytes 294944 | tf_op jit(solution)/shard_map/ppermute | solution.py:412
  124.6 4.8 %keys.2 = (bf16[4,128,512]{2,1,0:T(8,128)(2,1)}, bf16[4,128,128]{2,1,0:T(8,128)(2,1)S(1)}) custom-call(s32[49]{0:T(128)S(1)} %copy-done.27, bf16[128,512]{1,0:T(8,128)(2,1)S(1)} %copy-done.5, bf16[128,512]{1,0:T(8,128)(2,1)S(1)} %copy-done.7, bf16[128,512]{1,0:T(8,128)(2,1)S(1)} %copy-done.9, bf16[128,512]{1,0:T(8,128)(2,1)S(1)} %copy-done.11, ...), custom_call_target="tpu_custom_call" | custom-call | flops 1000 | bytes 1000 | tf_op jit(solution)/shard_map/keys/pallas_call | solution.py:487
  129.4 3.7 %collective-permute-start.22 = (bf16[128,1024]{1,0:T(8,128)(2,1)S(1)}, bf16[128,1024]{1,0:T(8,128)(2,1)S(1)}, u32[]{:S(2)}, u32[]{:S(2)}) collective-permute-start(bf16[128,1024]{1,0:T(8,128)(2,1)S(1)} %copy-done.41), channel_id=1, source_target_pairs={{0,4},{4,8},{8,12},{12,0},{16,20},{20,24},{24,28},{28,16},{1,5},{5... | collective-permute-start | bytes 786440 | tf_op jit(solution)/shard_map/ppermute | solution.py:401
  134.4 3.9 %collective-permute-done.23.refs_9_ = bf16[8,144,128]{2,1,0:T(8,128)(2,1)S(1)} collective-permute-done((bf16[8,144,128]{2,1,0:T(8,128)(2,1)S(1)}, bf16[8,144,128]{2,1,0:T(8,128)(2,1)S(1)}, u32[]{:S(2)}, u32[]{:S(2)}) %collective-permute-start.23) | collective-permute-done | bytes 294944 | tf_op jit(solution)/shard_map/ppermute | solution.py:406
  138.2 4.8 %keys.3 = (bf16[4,128,512]{2,1,0:T(8,128)(2,1)}, bf16[4,128,128]{2,1,0:T(8,128)(2,1)S(1)}) custom-call(s32[49]{0:T(128)S(1)} %copy-done.27, bf16[128,512]{1,0:T(8,128)(2,1)S(1)} %copy-done.5, bf16[128,512]{1,0:T(8,128)(2,1)S(1)} %copy-done.7, bf16[128,512]{1,0:T(8,128)(2,1)S(1)} %copy-done.9, ...), custom_call_target="tpu_custom_call", output_to_operand_aliasing={{0}: (13, {})} | custom-call | flops 1000 | bytes 1000 | tf_op jit(solution)/shard_map/keys/pallas_call | solution.py:487
  144.8 8.1 %all-to-all-start = ((bf16[4,128,512]{2,1,0:T(8,128)(2,1)}), bf16[4,128,512]{2,1,0:T(8,128)(2,1)S(1)}, u32[]{:S(2)}, u32[]{:S(2)}) async-start(bf16[4,128,512]{2,1,0:T(8,128)(2,1)} %get-tuple-element.118), calls=%async_computation | async-start | bytes 1048576 | tf_op jit(solution)/shard_map/all_to_all | solution.py:398
  153.3 3.9 %collective-permute-start.28 = (bf16[2,4,32,128]{3,2,1,0:T(8,128)(2,1)S(1)}, bf16[2,4,32,128]{3,2,1,0:T(8,128)(2,1)S(1)}, u32[]{:S(2)}, u32[]{:S(2)}) collective-permute-start(bf16[2,4,32,128]{3,2,1,0:T(8,128)(2,1)S(1)} %get-tuple-element.130), channel_id=1, source_target_pairs={{0,17},{1,18},{2,19},{3,16},{4,21},{5,22},{6,23},{7,20},{8,25},{9,... | collective-permute-start | bytes 196616 | tf_op jit(solution)/shard_map/ppermute | solution.py:420
  165.4 2.4 %collective-permute-done.29.refs_5_ = bf16[2,4,32,128]{3,2,1,0:T(8,128)(2,1)S(1)} collective-permute-done((bf16[2,4,32,128]{3,2,1,0:T(8,128)(2,1)S(1)}, bf16[2,4,32,128]{3,2,1,0:T(8,128)(2,1)S(1)}, u32[]{:S(2)}, u32[]{:S(2)}) %collective-permute-start.29) | collective-permute-done | bytes 65568 | tf_op jit(solution)/shard_map/ppermute | solution.py:420
  (157 shorter events, 48.7 us)
Async XLA Ops:
  4.2 9.5 %collective-permute-start = (bf16[128,512]{1,0:T(8,128)(2,1)S(1)}, bf16[128,512]{1,0:T(8,128)(2,1)S(1)}, u32[]{:S(2)}, u32[]{:S(2)}) collective-permute-start(bf16[128,512]{1,0:T(8,128)(2,1)S(1)} %get-tuple-element.68), channel_id=1, source_target_pairs={{0,4},{4,8},{8,12},{12,0},{16,20},{20,24},{24,28},{28,16},{1,5},{5... | collective-permute-start | bytes 393224 | tf_op jit(solution)/shard_map/ppermute | solution.py:401
  14.9 20.9 %collective-permute-start.5 = (bf16[128,2048]{1,0:T(8,128)(2,1)S(1)}, bf16[128,2048]{1,0:T(8,128)(2,1)S(1)}, u32[]{:S(2)}, u32[]{:S(2)}) collective-permute-start(bf16[128,2048]{1,0:T(8,128)(2,1)S(1)} %get-tuple-element.76), channel_id=1, source_target_pairs={{0,8},{4,12},{8,0},{12,4},{16,24},{20,28},{24,16},{28,20},{1,9},{5... | collective-permute-start | bytes 1572872 | tf_op jit(solution)/shard_map/ppermute | solution.py:401
  17.9 20.3 %collective-permute-start.6 = (bf16[128,2048]{1,0:T(8,128)(2,1)S(1)}, bf16[128,2048]{1,0:T(8,128)(2,1)S(1)}, u32[]{:S(2)}, u32[]{:S(2)}) collective-permute-start(bf16[128,2048]{1,0:T(8,128)(2,1)S(1)} %get-tuple-element.78), channel_id=1, source_target_pairs={{0,12},{4,0},{8,4},{12,8},{16,28},{20,16},{24,20},{28,24},{1,13},{... | collective-permute-start | bytes 1572872 | tf_op jit(solution)/shard_map/ppermute | solution.py:401
  18.2 27.6 %collective-permute-start.4 = (bf16[128,2048]{1,0:T(8,128)(2,1)S(1)}, bf16[128,2048]{1,0:T(8,128)(2,1)S(1)}, u32[]{:S(2)}, u32[]{:S(2)}) collective-permute-start(bf16[128,2048]{1,0:T(8,128)(2,1)S(1)} %get-tuple-element.74), channel_id=1, source_target_pairs={{0,4},{4,8},{8,12},{12,0},{16,20},{20,24},{24,28},{28,16},{1,5},{5... | collective-permute-start | bytes 1572872 | tf_op jit(solution)/shard_map/ppermute | solution.py:401
  32.2 13.7 %collective-permute-start.7 = (bf16[8,144,128]{2,1,0:T(8,128)(2,1)S(1)}, bf16[8,144,128]{2,1,0:T(8,128)(2,1)S(1)}, u32[]{:S(2)}, u32[]{:S(2)}) collective-permute-start(bf16[8,144,128]{2,1,0:T(8,128)(2,1)S(1)} %states.3), channel_id=1, source_target_pairs={{0,16},{4,20},{8,24},{12,28},{16,0},{20,4},{24,8},{28,12},{1,17},{... | collective-permute-start | bytes 884744 | tf_op jit(solution)/shard_map/ppermute | solution.py:406
  51.2 8.3 %collective-permute-start.9 = (bf16[8,144,128]{2,1,0:T(8,128)(2,1)S(1)}, bf16[8,144,128]{2,1,0:T(8,128)(2,1)S(1)}, u32[]{:S(2)}, u32[]{:S(2)}) collective-permute-start(bf16[8,144,128]{2,1,0:T(8,128)(2,1)S(1)} %totals.5), channel_id=1, source_target_pairs={{0,2},{1,3},{2,0},{3,1},{4,6},{5,7},{6,4},{7,5},{8,10},{9,11},{10,... | collective-permute-start | bytes 884744 | tf_op jit(solution)/shard_map/ppermute | solution.py:412
  61.1 15.3 %collective-permute-start.13 = (bf16[8,144,128]{2,1,0:T(8,128)(2,1)S(1)}, bf16[8,144,128]{2,1,0:T(8,128)(2,1)S(1)}, u32[]{:S(2)}, u32[]{:S(2)}) collective-permute-start(bf16[8,144,128]{2,1,0:T(8,128)(2,1)S(1)} %get-tuple-element.92), channel_id=1, source_target_pairs={{0,16},{4,20},{8,24},{12,28},{16,0},{20,4},{24,8},{28,12},{1,17},{... | collective-permute-start | bytes 884744 | tf_op jit(solution)/shard_map/ppermute | solution.py:406
  63.2 25.6 %collective-permute-start.12 = (bf16[128,2048]{1,0:T(8,128)(2,1)S(1)}, bf16[128,2048]{1,0:T(8,128)(2,1)S(1)}, u32[]{:S(2)}, u32[]{:S(2)}) collective-permute-start(bf16[128,2048]{1,0:T(8,128)(2,1)S(1)} %get-tuple-element.89), channel_id=1, source_target_pairs={{0,12},{4,0},{8,4},{12,8},{16,28},{20,16},{24,20},{28,24},{1,13},{... | collective-permute-start | bytes 1572872 | tf_op jit(solution)/shard_map/ppermute | solution.py:401
  64.1 28.0 %collective-permute-start.11 = (bf16[128,2048]{1,0:T(8,128)(2,1)S(1)}, bf16[128,2048]{1,0:T(8,128)(2,1)S(1)}, u32[]{:S(2)}, u32[]{:S(2)}) collective-permute-start(bf16[128,2048]{1,0:T(8,128)(2,1)S(1)} %get-tuple-element.87), channel_id=1, source_target_pairs={{0,8},{4,12},{8,0},{12,4},{16,24},{20,28},{24,16},{28,20},{1,9},{5... | collective-permute-start | bytes 1572872 | tf_op jit(solution)/shard_map/ppermute | solution.py:401
  64.9 27.9 %collective-permute-start.10 = (bf16[128,2048]{1,0:T(8,128)(2,1)S(1)}, bf16[128,2048]{1,0:T(8,128)(2,1)S(1)}, u32[]{:S(2)}, u32[]{:S(2)}) collective-permute-start(bf16[128,2048]{1,0:T(8,128)(2,1)S(1)} %get-tuple-element.85), channel_id=1, source_target_pairs={{0,4},{4,8},{8,12},{12,0},{16,20},{20,24},{24,28},{28,16},{1,5},{5... | collective-permute-start | bytes 1572872 | tf_op jit(solution)/shard_map/ppermute | solution.py:401
  88.7 16.5 %collective-permute-start.14 = (bf16[8,144,128]{2,1,0:T(8,128)(2,1)}, bf16[8,144,128]{2,1,0:T(8,128)(2,1)S(1)}, u32[]{:S(2)}, u32[]{:S(2)}) collective-permute-start(bf16[8,144,128]{2,1,0:T(8,128)(2,1)} %get-tuple-element.93), channel_id=1, source_target_pairs={{0,16},{4,20},{8,24},{12,28},{16,0},{20,4},{24,8},{28,12},{1,17},{... | collective-permute-start | bytes 884744 | tf_op jit(solution)/shard_map/ppermute | solution.py:406
  113.1 8.3 %collective-permute-start.16 = (bf16[8,144,128]{2,1,0:T(8,128)(2,1)S(1)}, bf16[8,144,128]{2,1,0:T(8,128)(2,1)S(1)}, u32[]{:S(2)}, u32[]{:S(2)}) collective-permute-start(bf16[8,144,128]{2,1,0:T(8,128)(2,1)S(1)} %totals.7), channel_id=1, source_target_pairs={{0,2},{1,3},{2,0},{3,1},{4,6},{5,7},{6,4},{7,5},{8,10},{9,11},{10,... | collective-permute-start | bytes 884744 | tf_op jit(solution)/shard_map/ppermute | solution.py:412
  114.4 15.0 %collective-permute-start.19 = (bf16[128,1024]{1,0:T(8,128)(2,1)S(1)}, bf16[128,1024]{1,0:T(8,128)(2,1)S(1)}, u32[]{:S(2)}, u32[]{:S(2)}) collective-permute-start(bf16[128,1024]{1,0:T(8,128)(2,1)S(1)} %copy-done.44), channel_id=1, source_target_pairs={{0,4},{4,8},{8,12},{12,0},{16,20},{20,24},{24,28},{28,16},{1,5},{5... | collective-permute-start | bytes 786440 | tf_op jit(solution)/shard_map/ppermute | solution.py:401
  114.4 15.0 %collective-permute-start.18 = (bf16[128,1024]{1,0:T(8,128)(2,1)S(1)}, bf16[128,1024]{1,0:T(8,128)(2,1)S(1)}, u32[]{:S(2)}, u32[]{:S(2)}) collective-permute-start(bf16[128,1024]{1,0:T(8,128)(2,1)S(1)} %copy-done.43), channel_id=1, source_target_pairs={{0,8},{4,12},{8,0},{12,4},{16,24},{20,28},{24,16},{28,20},{1,9},{5... | collective-permute-start | bytes 786440 | tf_op jit(solution)/shard_map/ppermute | solution.py:401
  115.0 14.4 %collective-permute-start.17 = (bf16[128,1024]{1,0:T(8,128)(2,1)S(1)}, bf16[128,1024]{1,0:T(8,128)(2,1)S(1)}, u32[]{:S(2)}, u32[]{:S(2)}) collective-permute-start(bf16[128,1024]{1,0:T(8,128)(2,1)S(1)} %copy-done.42), channel_id=1, source_target_pairs={{0,12},{4,0},{8,4},{12,8},{16,28},{20,16},{24,20},{28,24},{1,13},{... | collective-permute-start | bytes 786440 | tf_op jit(solution)/shard_map/ppermute | solution.py:401
  123.0 15.2 %collective-permute-start.23 = (bf16[8,144,128]{2,1,0:T(8,128)(2,1)S(1)}, bf16[8,144,128]{2,1,0:T(8,128)(2,1)S(1)}, u32[]{:S(2)}, u32[]{:S(2)}) collective-permute-start(bf16[8,144,128]{2,1,0:T(8,128)(2,1)S(1)} %get-tuple-element.113), channel_id=1, source_target_pairs={{0,16},{4,20},{8,24},{12,28},{16,0},{20,4},{24,8},{28,12},{1,17},{... | collective-permute-start | bytes 884744 | tf_op jit(solution)/shard_map/ppermute | solution.py:406
  129.4 13.6 %collective-permute-start.22 = (bf16[128,1024]{1,0:T(8,128)(2,1)S(1)}, bf16[128,1024]{1,0:T(8,128)(2,1)S(1)}, u32[]{:S(2)}, u32[]{:S(2)}) collective-permute-start(bf16[128,1024]{1,0:T(8,128)(2,1)S(1)} %copy-done.41), channel_id=1, source_target_pairs={{0,4},{4,8},{8,12},{12,0},{16,20},{20,24},{24,28},{28,16},{1,5},{5... | collective-permute-start | bytes 786440 | tf_op jit(solution)/shard_map/ppermute | solution.py:401
  133.1 11.7 %collective-permute-start.21 = (bf16[128,1024]{1,0:T(8,128)(2,1)S(1)}, bf16[128,1024]{1,0:T(8,128)(2,1)S(1)}, u32[]{:S(2)}, u32[]{:S(2)}) collective-permute-start(bf16[128,1024]{1,0:T(8,128)(2,1)S(1)} %copy-done.40), channel_id=1, source_target_pairs={{0,8},{4,12},{8,0},{12,4},{16,24},{20,28},{24,16},{28,20},{1,9},{5... | collective-permute-start | bytes 786440 | tf_op jit(solution)/shard_map/ppermute | solution.py:401
  133.1 11.6 %collective-permute-start.20 = (bf16[128,1024]{1,0:T(8,128)(2,1)S(1)}, bf16[128,1024]{1,0:T(8,128)(2,1)S(1)}, u32[]{:S(2)}, u32[]{:S(2)}) collective-permute-start(bf16[128,1024]{1,0:T(8,128)(2,1)S(1)} %copy-done.39), channel_id=1, source_target_pairs={{0,12},{4,0},{8,4},{12,8},{16,28},{20,16},{24,20},{28,24},{1,13},{... | collective-permute-start | bytes 786440 | tf_op jit(solution)/shard_map/ppermute | solution.py:401
  144.8 25.4 %all-to-all-start = ((bf16[4,128,512]{2,1,0:T(8,128)(2,1)}), bf16[4,128,512]{2,1,0:T(8,128)(2,1)S(1)}, u32[]{:S(2)}, u32[]{:S(2)}) async-start(bf16[4,128,512]{2,1,0:T(8,128)(2,1)} %get-tuple-element.118), calls=%async_computation | async-start | bytes 1048576 | tf_op jit(solution)/shard_map/all_to_all | solution.py:398
  153.3 9.0 %collective-permute-start.28 = (bf16[2,4,32,128]{3,2,1,0:T(8,128)(2,1)S(1)}, bf16[2,4,32,128]{3,2,1,0:T(8,128)(2,1)S(1)}, u32[]{:S(2)}, u32[]{:S(2)}) collective-permute-start(bf16[2,4,32,128]{3,2,1,0:T(8,128)(2,1)S(1)} %get-tuple-element.130), channel_id=1, source_target_pairs={{0,17},{1,18},{2,19},{3,16},{4,21},{5,22},{6,23},{7,20},{8,25},{9,... | collective-permute-start | bytes 196616 | tf_op jit(solution)/shard_map/ppermute | solution.py:420
  157.2 10.6 %collective-permute-start.29 = (bf16[2,4,32,128]{3,2,1,0:T(8,128)(2,1)S(1)}, bf16[2,4,32,128]{3,2,1,0:T(8,128)(2,1)S(1)}, u32[]{:S(2)}, u32[]{:S(2)}) collective-permute-start(bf16[2,4,32,128]{3,2,1,0:T(8,128)(2,1)S(1)} %get-tuple-element.131), channel_id=1, source_target_pairs={{0,18},{1,19},{2,16},{3,17},{4,22},{5,23},{6,20},{7,21},{8,26},{9,... | collective-permute-start | bytes 196616 | tf_op jit(solution)/shard_map/ppermute | solution.py:420
  158.0 10.8 %collective-permute-start.30 = (bf16[2,4,32,128]{3,2,1,0:T(8,128)(2,1)S(1)}, bf16[2,4,32,128]{3,2,1,0:T(8,128)(2,1)S(1)}, u32[]{:S(2)}, u32[]{:S(2)}) collective-permute-start(bf16[2,4,32,128]{3,2,1,0:T(8,128)(2,1)S(1)} %get-tuple-element.128), channel_id=1, source_target_pairs={{0,19},{1,16},{2,17},{3,18},{4,23},{5,20},{6,21},{7,22},{8,27},{9,... | collective-permute-start | bytes 196616 | tf_op jit(solution)/shard_map/ppermute | solution.py:420
  159.2 9.5 %collective-permute-start.24 = (bf16[2,4,32,128]{3,2,1,0:T(8,128)(2,1)S(1)}, bf16[2,4,32,128]{3,2,1,0:T(8,128)(2,1)S(1)}, u32[]{:S(2)}, u32[]{:S(2)}) collective-permute-start(bf16[2,4,32,128]{3,2,1,0:T(8,128)(2,1)S(1)} %get-tuple-element.134), channel_id=1, source_target_pairs={{0,1},{1,2},{2,3},{3,0},{4,5},{5,6},{6,7},{7,4},{8,9},{9,10},{10,1... | collective-permute-start | bytes 196616 | tf_op jit(solution)/shard_map/ppermute | solution.py:409
  (53 other events, 663.5 us)

commit v18 on v17

--- a/solution.py
+++ b/solution.py
@@ -586,6 +586,7 @@
     moved, key_gm = [], {}
     for s in slots:
         begun = [] if s == 0 else [pairs]
+        suffix[s] = after(suffix[s], *moved)
         pairs, key_gm[s] = call(
             functools.partial(key_kernel, bool(begun)),
             [of(kv_type, *pairs.shape), gm_shape],
@@ -609,7 +610,6 @@
         if s:
             moved += [apart(rows_for(two, seq + r), s, r) for r in range(fsdp)]
         else:
-            two = after(two, *suffix[1:])
             moved += [along(rows_for(two, seq + r), r) for r in range(1, fsdp)]
             returned[s] = brought_back(s, key_gm[s], *earlier)
 

time: 172 us -> 177 us (1.029)
  waiting for transfers between devices: 48.7 us -> 55.1 us
  starting transfers between devices: 52.7 us -> 47.3 us
  local copies, waits for them, and re-layouts: 7.2 us -> 11.7 us
    ppermute x3, waiting for transfers between devices: 0.01 us -> 7.55 us  [along(): lax.ppermute(array, 'fsdp', [(d, (d + shift) % fsdp) for d in range(fsdp)])]
    all_to_all x1, starting transfers between devices: 8.07 us -> 3.47 us  [within(): lax.all_to_all(array, 'ctx', 0, 0, axis_index_groups=blocks_of, tiled=True)]
    unnamed x90 -> x104, local copies, waits for them, and re-layouts: 7.05 us -> 11.5 us
    ppermute x4, waiting for transfers between devices: 3.35 us -> 7.62 us  [apart(): return lax.ppermute(array, ('ctx', 'fsdp'), moves)]
    ppermute x5, waiting for transfers between devices: 17.1 us -> 13.2 us  [across(): lax.ppermute(array, 'ctx', [(d, (d + shift * part) % ctx) for d in range(...]
  transfers between devices with their start and end apart: 32 -> 32, of which waited for: 14 -> 16; matrix products, arithmetic and copies ran while one was open for 0% -> 0% of each run, Pallas kernels for 26% -> 25%
where the time goes in v18:
time: 177 us
  waiting for transfers between devices  55.1 us (31%)
  Pallas kernels  51.1 us (29%)
  starting transfers between devices  47.3 us (27%)
  local copies, waits for them, and re-layouts  11.7 us (7%)
  blocking collectives  9.99 us (6%)
    pallas_call x6, Pallas kernels, call(): pl.pallas_call(functools.partial(kernel, part, base['sorted']), out_shape...  38 us
    ppermute x15, starting transfers between devices, around(): lax.ppermute(array, 'ctx', [(d, d // part * part + (d + shift) % part) fo...  17.8 us
    ppermute x15, waiting for transfers between devices, around(): lax.ppermute(array, 'ctx', [(d, d // part * part + (d + shift) % part) fo...  14.2 us
    ppermute x5, waiting for transfers between devices, across(): lax.ppermute(array, 'ctx', [(d, (d + shift * part) % ctx) for d in range(...  13.2 us
    ppermute x4, waiting for transfers between devices, twin(): return lax.ppermute(array, 'fsdp', [(d, d ^ bit) for d in range(fsdp)])  12.5 us
    unnamed x104, local copies, waits for them, and re-layouts  11.5 us
    all_gather x1, blocking collectives, shards(): maps = lax.all_gather(near_maps, 'fsdp')  9.99 us
    ppermute x4, starting transfers between devices, twin(): return lax.ppermute(array, 'fsdp', [(d, d ^ bit) for d in range(fsdp)])  9.76 us
  transfers between devices with their start and end apart: 32, of which 16 were waited for; matrix products, arithmetic and copies ran while one was open for 0% of the time, Pallas kernels for 25%

profile of v18, /device:TPU:1, one launch (start us, length us, event | category | flops | bytes accessed | tf_op | source)
XLA Modules:
  0.0 176.8 jit_solution(4776614489098777361)
XLA Ops:
  8.9 2.4 %collective-permute-start.3 = (bf16[8,32,128]{2,1,0:T(8,128)(2,1)S(1)}, bf16[8,32,128]{2,1,0:T(8,128)(2,1)S(1)}, u32[]{:S(2)}, u32[]{:S(2)}) collective-permute-start(bf16[8,32,128]{2,1,0:T(8,128)(2,1)S(1)} %pad_maximum_fusion.1), channel_id=1, source_target_pairs={{0,16},{4,20},{8,24},{12,28},{16,0},{20,4},{24,8},{28,12},{1,17},{... | collective-permute-start | bytes 196616 | tf_op jit(solution)/shard_map/ppermute | solution.py:406
  11.3 2.4 %collective-permute-done.3 = bf16[8,32,128]{2,1,0:T(8,128)(2,1)S(1)} collective-permute-done((bf16[8,32,128]{2,1,0:T(8,128)(2,1)S(1)}, bf16[8,32,128]{2,1,0:T(8,128)(2,1)S(1)}, u32[]{:S(2)}, u32[]{:S(2)}) %collective-permute-start.3) | collective-permute-done | bytes 65568 | tf_op jit(solution)/shard_map/ppermute | solution.py:406
  14.9 3.0 %collective-permute-start.5 = (bf16[128,2048]{1,0:T(8,128)(2,1)S(1)}, bf16[128,2048]{1,0:T(8,128)(2,1)S(1)}, u32[]{:S(2)}, u32[]{:S(2)}) collective-permute-start(bf16[128,2048]{1,0:T(8,128)(2,1)S(1)} %get-tuple-element.76), channel_id=1, source_target_pairs={{0,8},{4,12},{8,0},{12,4},{16,24},{20,28},{24,16},{28,20},{1,9},{5... | collective-permute-start | bytes 1572872 | tf_op jit(solution)/shard_map/ppermute | solution.py:401
  19.3 10.0 %all-gather = bf16[8,8,32,128]{3,2,1,0:T(8,128)(2,1)S(1)} all-gather(bf16[2,8,32,128]{3,2,1,0:T(8,128)(2,1)S(1)} %pad_maximum_fusion), channel_id=2, replica_groups=mesh['ctx'=8,'fsdp'=4] {'fsdp'}, dimensions={0}, use_global_device_ids=true | all-gather | bytes 655360 | tf_op jit(solution)/shard_map/all_gather | solution.py:449
  29.3 2.8 %states.3 = bf16[8,144,128]{2,1,0:T(8,128)(2,1)S(1)} custom-call(s32[49]{0:T(128)S(1)} %stack.194.table, bf16[128,512]{1,0:T(8,128)(2,1)S(1)} %get-tuple-element.67.refs_0_.refs_4_, bf16[128,512]{1,0:T(8,128)(2,1)S(1)} %collective-permute-done.refs_1_.refs_5_, bf16[128,512]{1,0:T(8,128)(2,1)S(1)} %collective-permute-done.1.refs_2_.refs_6_, ...), custom_call_target="tpu_custom_call" | custom-call | flops 1000 | bytes 1000 | tf_op jit(solution)/shard_map/states/pallas_call | solution.py:487
  32.9 2.8 %states.2.refs_0_ = bf16[8,144,128]{2,1,0:T(8,128)(2,1)S(1)} custom-call(s32[49]{0:T(128)S(1)} %stack.194.table, bf16[128,512]{1,0:T(8,128)(2,1)S(1)} %get-tuple-element.67.refs_0_.refs_4_, bf16[128,512]{1,0:T(8,128)(2,1)S(1)} %collective-permute-done.refs_1_.refs_5_, bf16[128,512]{1,0:T(8,128)(2,1)S(1)} %collective-permute-done.1.refs_2_.refs_6_, ...), custom_call_target="tpu_custom_call" | custom-call | flops 1000 | bytes 1000 | tf_op jit(solution)/shard_map/states/pallas_call | solution.py:487
  35.7 2.5 %collective-permute-done.6.refs_11_.refs_15_ = bf16[128,2048]{1,0:T(8,128)(2,1)S(1)} collective-permute-done((bf16[128,2048]{1,0:T(8,128)(2,1)S(1)}, bf16[128,2048]{1,0:T(8,128)(2,1)S(1)}, u32[]{:S(2)}, u32[]{:S(2)}) %collective-permute-start.6) | collective-permute-done | bytes 524320 | tf_op jit(solution)/shard_map/ppermute | solution.py:401
  38.2 7.6 %collective-permute-done.4.refs_9_.refs_13_ = bf16[128,2048]{1,0:T(8,128)(2,1)S(1)} collective-permute-done((bf16[128,2048]{1,0:T(8,128)(2,1)S(1)}, bf16[128,2048]{1,0:T(8,128)(2,1)S(1)}, u32[]{:S(2)}, u32[]{:S(2)}) %collective-permute-start.4) | collective-permute-done | bytes 524320 | tf_op jit(solution)/shard_map/ppermute | solution.py:401
  46.5 2.8 %collective-permute-start.8 = (bf16[8,144,128]{2,1,0:T(8,128)(2,1)S(1)}, bf16[8,144,128]{2,1,0:T(8,128)(2,1)S(1)}, u32[]{:S(2)}, u32[]{:S(2)}) collective-permute-start(bf16[8,144,128]{2,1,0:T(8,128)(2,1)S(1)} %totals.4.refs_0_), channel_id=1, source_target_pairs={{0,1},{1,0},{2,3},{3,2},{4,5},{5,4},{6,7},{7,6},{8,9},{9,8},{10,11... | collective-permute-start | bytes 884744 | tf_op jit(solution)/shard_map/ppermute | solution.py:412
  53.6 5.9 %collective-permute-done.9.refs_3_ = bf16[8,144,128]{2,1,0:T(8,128)(2,1)S(1)} collective-permute-done((bf16[8,144,128]{2,1,0:T(8,128)(2,1)S(1)}, bf16[8,144,128]{2,1,0:T(8,128)(2,1)S(1)}, u32[]{:S(2)}, u32[]{:S(2)}) %collective-permute-start.9) | collective-permute-done | bytes 294944 | tf_op jit(solution)/shard_map/ppermute | solution.py:412
  65.6 10.8 %collective-permute-done.13.refs_17_ = bf16[8,144,128]{2,1,0:T(8,128)(2,1)S(1)} collective-permute-done((bf16[8,144,128]{2,1,0:T(8,128)(2,1)S(1)}, bf16[8,144,128]{2,1,0:T(8,128)(2,1)S(1)}, u32[]{:S(2)}, u32[]{:S(2)}) %collective-permute-start.13) | collective-permute-done | bytes 294944 | tf_op jit(solution)/shard_map/ppermute | solution.py:406
  77.2 11.5 %blocks.3 = (bf16[128,1024]{1,0:T(8,128)(2,1)}, bf16[128,1024]{1,0:T(8,128)(2,1)}, bf16[128,1024]{1,0:T(8,128)(2,1)}, bf16[128,1024]{1,0:T(8,128)(2,1)}, f32[8,1...) custom-call(s32[49]{0:T(128)} %copy-done.29, ...), custom_call_target="tpu_custom_call" | custom-call | flops 1000 | bytes 1000 | tf_op jit(solution)/shard_map/blocks/pallas_call | solution.py:487
  88.7 3.4 %collective-permute-done.11.refs_10_.refs_14_ = bf16[128,2048]{1,0:T(8,128)(2,1)S(1)} collective-permute-done((bf16[128,2048]{1,0:T(8,128)(2,1)S(1)}, bf16[128,2048]{1,0:T(8,128)(2,1)S(1)}, u32[]{:S(2)}, u32[]{:S(2)}) %collective-permute-start.11) | collective-permute-done | bytes 524320 | tf_op jit(solution)/shard_map/ppermute | solution.py:401
  93.7 11.5 %blocks.2 = (bf16[128,1024]{1,0:T(8,128)(2,1)}, bf16[128,1024]{1,0:T(8,128)(2,1)}, bf16[128,1024]{1,0:T(8,128)(2,1)}, bf16[128,1024]{1,0:T(8,128)(2,1)}, f32[8,1...) custom-call(s32[49]{0:T(128)} %copy-done.29, ...), custom_call_target="tpu_custom_call" | custom-call | flops 1000 | bytes 1000 | tf_op jit(solution)/shard_map/blocks/pallas_call | solution.py:487
  107.0 4.4 %collective-permute-start.15 = (bf16[8,144,128]{2,1,0:T(8,128)(2,1)S(1)}, bf16[8,144,128]{2,1,0:T(8,128)(2,1)S(1)}, u32[]{:S(2)}, u32[]{:S(2)}) collective-permute-start(bf16[8,144,128]{2,1,0:T(8,128)(2,1)S(1)} %totals.6.refs_0_), channel_id=1, source_target_pairs={{0,1},{1,0},{2,3},{3,2},{4,5},{5,4},{6,7},{7,6},{8,9},{9,8},{10,11... | collective-permute-start | bytes 884744 | tf_op jit(solution)/shard_map/ppermute | solution.py:412
  114.9 2.4 %collective-permute-start.17 = (bf16[128,1024]{1,0:T(8,128)(2,1)S(1)}, bf16[128,1024]{1,0:T(8,128)(2,1)S(1)}, u32[]{:S(2)}, u32[]{:S(2)}) collective-permute-start(bf16[128,1024]{1,0:T(8,128)(2,1)S(1)} %copy-done.51), channel_id=1, source_target_pairs={{0,12},{4,0},{8,4},{12,8},{16,28},{20,16},{24,20},{28,24},{1,13},{... | collective-permute-start | bytes 786440 | tf_op jit(solution)/shard_map/ppermute | solution.py:401
  117.3 4.2 %collective-permute-done.16.refs_3_ = bf16[8,144,128]{2,1,0:T(8,128)(2,1)S(1)} collective-permute-done((bf16[8,144,128]{2,1,0:T(8,128)(2,1)S(1)}, bf16[8,144,128]{2,1,0:T(8,128)(2,1)S(1)}, u32[]{:S(2)}, u32[]{:S(2)}) %collective-permute-start.16) | collective-permute-done | bytes 294944 | tf_op jit(solution)/shard_map/ppermute | solution.py:412
  125.7 4.7 %keys.2 = (bf16[4,128,512]{2,1,0:T(8,128)(2,1)}, bf16[4,128,128]{2,1,0:T(8,128)(2,1)S(1)}) custom-call(s32[49]{0:T(128)S(1)} %copy-done.30, bf16[128,512]{1,0:T(8,128)(2,1)S(1)} %copy-done.5, bf16[128,512]{1,0:T(8,128)(2,1)S(1)} %copy-done.7, bf16[128,512]{1,0:T(8,128)(2,1)S(1)} %copy-done.9, bf16[128,512]{1,0:T(8,128)(2,1)S(1)} %copy-done.11, ...), custom_call_target="tpu_custom_call" | custom-call | flops 1000 | bytes 1000 | tf_op jit(solution)/shard_map/keys/pallas_call | solution.py:487
  134.0 3.4 %collective-permute-start.24 = (bf16[2,4,32,128]{3,2,1,0:T(8,128)(2,1)S(1)}, bf16[2,4,32,128]{3,2,1,0:T(8,128)(2,1)S(1)}, u32[]{:S(2)}, u32[]{:S(2)}) collective-permute-start(bf16[2,4,32,128]{3,2,1,0:T(8,128)(2,1)S(1)} %get-tuple-element.133), channel_id=1, source_target_pairs={{0,1},{1,2},{2,3},{3,0},{4,5},{5,6},{6,7},{7,4},{8,9},{9,10},{10,1... | collective-permute-start | bytes 196616 | tf_op jit(solution)/shard_map/ppermute | solution.py:409
  139.6 3.2 %collective-permute-done.25.refs_1_ = bf16[2,4,32,128]{3,2,1,0:T(8,128)(2,1)S(1)} collective-permute-done((bf16[2,4,32,128]{3,2,1,0:T(8,128)(2,1)S(1)}, bf16[2,4,32,128]{3,2,1,0:T(8,128)(2,1)S(1)}, u32[]{:S(2)}, u32[]{:S(2)}) %collective-permute-start.25) | collective-permute-done | bytes 65568 | tf_op jit(solution)/shard_map/ppermute | solution.py:409
  145.5 3.1 %collective-permute-done.26.refs_2_ = bf16[2,4,32,128]{3,2,1,0:T(8,128)(2,1)S(1)} collective-permute-done((bf16[2,4,32,128]{3,2,1,0:T(8,128)(2,1)S(1)}, bf16[2,4,32,128]{3,2,1,0:T(8,128)(2,1)S(1)}, u32[]{:S(2)}, u32[]{:S(2)}) %collective-permute-start.26) | collective-permute-done | bytes 65568 | tf_op jit(solution)/shard_map/ppermute | solution.py:409
  149.2 4.7 %keys.3 = (bf16[4,128,512]{2,1,0:T(8,128)(2,1)}, bf16[4,128,128]{2,1,0:T(8,128)(2,1)S(1)}) custom-call(s32[49]{0:T(128)S(1)} %copy-done.30, bf16[128,512]{1,0:T(8,128)(2,1)S(1)} %copy-done.5, bf16[128,512]{1,0:T(8,128)(2,1)S(1)} %copy-done.7, bf16[128,512]{1,0:T(8,128)(2,1)S(1)} %copy-done.9, ...), custom_call_target="tpu_custom_call", output_to_operand_aliasing={{0}: (13, {})} | custom-call | flops 1000 | bytes 1000 | tf_op jit(solution)/shard_map/keys/pallas_call | solution.py:487
  154.7 3.5 %all-to-all-start = ((bf16[4,128,512]{2,1,0:T(8,128)(2,1)}), bf16[4,128,512]{2,1,0:T(8,128)(2,1)S(1)}, u32[]{:S(2)}, u32[]{:S(2)}) async-start(bf16[4,128,512]{2,1,0:T(8,128)(2,1)} %get-tuple-element.120), calls=%async_computation | async-start | bytes 1048576 | tf_op jit(solution)/shard_map/all_to_all | solution.py:398
  168.5 5.6 %collective-permute-done.30.refs_6_ = bf16[2,4,32,128]{3,2,1,0:T(8,128)(2,1)S(1)} collective-permute-done((bf16[2,4,32,128]{3,2,1,0:T(8,128)(2,1)S(1)}, bf16[2,4,32,128]{3,2,1,0:T(8,128)(2,1)S(1)}, u32[]{:S(2)}, u32[]{:S(2)}) %collective-permute-start.30) | collective-permute-done | bytes 65568 | tf_op jit(solution)/shard_map/ppermute | solution.py:420
  (170 shorter events, 57.0 us)
Async XLA Ops:
  4.2 9.5 %collective-permute-start = (bf16[128,512]{1,0:T(8,128)(2,1)S(1)}, bf16[128,512]{1,0:T(8,128)(2,1)S(1)}, u32[]{:S(2)}, u32[]{:S(2)}) collective-permute-start(bf16[128,512]{1,0:T(8,128)(2,1)S(1)} %get-tuple-element.68), channel_id=1, source_target_pairs={{0,4},{4,8},{8,12},{12,0},{16,20},{20,24},{24,28},{28,16},{1,5},{5... | collective-permute-start | bytes 393224 | tf_op jit(solution)/shard_map/ppermute | solution.py:401
  6.3 7.4 %collective-permute-start.1 = (bf16[128,512]{1,0:T(8,128)(2,1)S(1)}, bf16[128,512]{1,0:T(8,128)(2,1)S(1)}, u32[]{:S(2)}, u32[]{:S(2)}) collective-permute-start(bf16[128,512]{1,0:T(8,128)(2,1)S(1)} %get-tuple-element.69), channel_id=1, source_target_pairs={{0,8},{4,12},{8,0},{12,4},{16,24},{20,28},{24,16},{28,20},{1,9},{5... | collective-permute-start | bytes 393224 | tf_op jit(solution)/shard_map/ppermute | solution.py:401
  14.9 20.9 %collective-permute-start.5 = (bf16[128,2048]{1,0:T(8,128)(2,1)S(1)}, bf16[128,2048]{1,0:T(8,128)(2,1)S(1)}, u32[]{:S(2)}, u32[]{:S(2)}) collective-permute-start(bf16[128,2048]{1,0:T(8,128)(2,1)S(1)} %get-tuple-element.76), channel_id=1, source_target_pairs={{0,8},{4,12},{8,0},{12,4},{16,24},{20,28},{24,16},{28,20},{1,9},{5... | collective-permute-start | bytes 1572872 | tf_op jit(solution)/shard_map/ppermute | solution.py:401
  17.9 20.3 %collective-permute-start.6 = (bf16[128,2048]{1,0:T(8,128)(2,1)S(1)}, bf16[128,2048]{1,0:T(8,128)(2,1)S(1)}, u32[]{:S(2)}, u32[]{:S(2)}) collective-permute-start(bf16[128,2048]{1,0:T(8,128)(2,1)S(1)} %get-tuple-element.78), channel_id=1, source_target_pairs={{0,12},{4,0},{8,4},{12,8},{16,28},{20,16},{24,20},{28,24},{1,13},{... | collective-permute-start | bytes 1572872 | tf_op jit(solution)/shard_map/ppermute | solution.py:401
  18.2 27.6 %collective-permute-start.4 = (bf16[128,2048]{1,0:T(8,128)(2,1)S(1)}, bf16[128,2048]{1,0:T(8,128)(2,1)S(1)}, u32[]{:S(2)}, u32[]{:S(2)}) collective-permute-start(bf16[128,2048]{1,0:T(8,128)(2,1)S(1)} %get-tuple-element.74), channel_id=1, source_target_pairs={{0,4},{4,8},{8,12},{12,0},{16,20},{20,24},{24,28},{28,16},{1,5},{5... | collective-permute-start | bytes 1572872 | tf_op jit(solution)/shard_map/ppermute | solution.py:401
  32.2 13.7 %collective-permute-start.7 = (bf16[8,144,128]{2,1,0:T(8,128)(2,1)S(1)}, bf16[8,144,128]{2,1,0:T(8,128)(2,1)S(1)}, u32[]{:S(2)}, u32[]{:S(2)}) collective-permute-start(bf16[8,144,128]{2,1,0:T(8,128)(2,1)S(1)} %states.3), channel_id=1, source_target_pairs={{0,16},{4,20},{8,24},{12,28},{16,0},{20,4},{24,8},{28,12},{1,17},{... | collective-permute-start | bytes 884744 | tf_op jit(solution)/shard_map/ppermute | solution.py:406
  51.2 8.3 %collective-permute-start.9 = (bf16[8,144,128]{2,1,0:T(8,128)(2,1)S(1)}, bf16[8,144,128]{2,1,0:T(8,128)(2,1)S(1)}, u32[]{:S(2)}, u32[]{:S(2)}) collective-permute-start(bf16[8,144,128]{2,1,0:T(8,128)(2,1)S(1)} %totals.5), channel_id=1, source_target_pairs={{0,2},{1,3},{2,0},{3,1},{4,6},{5,7},{6,4},{7,5},{8,10},{9,11},{10,... | collective-permute-start | bytes 884744 | tf_op jit(solution)/shard_map/ppermute | solution.py:412
  61.1 15.3 %collective-permute-start.13 = (bf16[8,144,128]{2,1,0:T(8,128)(2,1)S(1)}, bf16[8,144,128]{2,1,0:T(8,128)(2,1)S(1)}, u32[]{:S(2)}, u32[]{:S(2)}) collective-permute-start(bf16[8,144,128]{2,1,0:T(8,128)(2,1)S(1)} %get-tuple-element.92), channel_id=1, source_target_pairs={{0,16},{4,20},{8,24},{12,28},{16,0},{20,4},{24,8},{28,12},{1,17},{... | collective-permute-start | bytes 884744 | tf_op jit(solution)/shard_map/ppermute | solution.py:406
  63.2 25.5 %collective-permute-start.12 = (bf16[128,2048]{1,0:T(8,128)(2,1)S(1)}, bf16[128,2048]{1,0:T(8,128)(2,1)S(1)}, u32[]{:S(2)}, u32[]{:S(2)}) collective-permute-start(bf16[128,2048]{1,0:T(8,128)(2,1)S(1)} %get-tuple-element.89), channel_id=1, source_target_pairs={{0,12},{4,0},{8,4},{12,8},{16,28},{20,16},{24,20},{28,24},{1,13},{... | collective-permute-start | bytes 1572872 | tf_op jit(solution)/shard_map/ppermute | solution.py:401
  64.1 28.0 %collective-permute-start.11 = (bf16[128,2048]{1,0:T(8,128)(2,1)S(1)}, bf16[128,2048]{1,0:T(8,128)(2,1)S(1)}, u32[]{:S(2)}, u32[]{:S(2)}) collective-permute-start(bf16[128,2048]{1,0:T(8,128)(2,1)S(1)} %get-tuple-element.87), channel_id=1, source_target_pairs={{0,8},{4,12},{8,0},{12,4},{16,24},{20,28},{24,16},{28,20},{1,9},{5... | collective-permute-start | bytes 1572872 | tf_op jit(solution)/shard_map/ppermute | solution.py:401
  64.9 27.9 %collective-permute-start.10 = (bf16[128,2048]{1,0:T(8,128)(2,1)S(1)}, bf16[128,2048]{1,0:T(8,128)(2,1)S(1)}, u32[]{:S(2)}, u32[]{:S(2)}) collective-permute-start(bf16[128,2048]{1,0:T(8,128)(2,1)S(1)} %get-tuple-element.85), channel_id=1, source_target_pairs={{0,4},{4,8},{8,12},{12,0},{16,20},{20,24},{24,28},{28,16},{1,5},{5... | collective-permute-start | bytes 1572872 | tf_op jit(solution)/shard_map/ppermute | solution.py:401
  88.6 16.6 %collective-permute-start.14 = (bf16[8,144,128]{2,1,0:T(8,128)(2,1)}, bf16[8,144,128]{2,1,0:T(8,128)(2,1)S(1)}, u32[]{:S(2)}, u32[]{:S(2)}) collective-permute-start(bf16[8,144,128]{2,1,0:T(8,128)(2,1)} %get-tuple-element.93), channel_id=1, source_target_pairs={{0,16},{4,20},{8,24},{12,28},{16,0},{20,4},{24,8},{28,12},{1,17},{... | collective-permute-start | bytes 884744 | tf_op jit(solution)/shard_map/ppermute | solution.py:406
  113.2 8.3 %collective-permute-start.16 = (bf16[8,144,128]{2,1,0:T(8,128)(2,1)S(1)}, bf16[8,144,128]{2,1,0:T(8,128)(2,1)S(1)}, u32[]{:S(2)}, u32[]{:S(2)}) collective-permute-start(bf16[8,144,128]{2,1,0:T(8,128)(2,1)S(1)} %totals.7), channel_id=1, source_target_pairs={{0,2},{1,3},{2,0},{3,1},{4,6},{5,7},{6,4},{7,5},{8,10},{9,11},{10,... | collective-permute-start | bytes 884744 | tf_op jit(solution)/shard_map/ppermute | solution.py:412
  114.5 16.0 %collective-permute-start.19 = (bf16[128,1024]{1,0:T(8,128)(2,1)}, bf16[128,1024]{1,0:T(8,128)(2,1)S(1)}, u32[]{:S(2)}, u32[]{:S(2)}) collective-permute-start(bf16[128,1024]{1,0:T(8,128)(2,1)} %get-tuple-element.105), channel_id=1, source_target_pairs={{0,4},{4,8},{8,12},{12,0},{16,20},{20,24},{24,28},{28,16},{1,5},{5... | collective-permute-start | bytes 786440 | tf_op jit(solution)/shard_map/ppermute | solution.py:401
  114.5 16.0 %collective-permute-start.18 = (bf16[128,1024]{1,0:T(8,128)(2,1)}, bf16[128,1024]{1,0:T(8,128)(2,1)S(1)}, u32[]{:S(2)}, u32[]{:S(2)}) collective-permute-start(bf16[128,1024]{1,0:T(8,128)(2,1)} %get-tuple-element.103), channel_id=1, source_target_pairs={{0,8},{4,12},{8,0},{12,4},{16,24},{20,28},{24,16},{28,20},{1,9},{5... | collective-permute-start | bytes 786440 | tf_op jit(solution)/shard_map/ppermute | solution.py:401
  114.9 15.5 %collective-permute-start.17 = (bf16[128,1024]{1,0:T(8,128)(2,1)S(1)}, bf16[128,1024]{1,0:T(8,128)(2,1)S(1)}, u32[]{:S(2)}, u32[]{:S(2)}) collective-permute-start(bf16[128,1024]{1,0:T(8,128)(2,1)S(1)} %copy-done.51), channel_id=1, source_target_pairs={{0,12},{4,0},{8,4},{12,8},{16,28},{20,16},{24,20},{28,24},{1,13},{... | collective-permute-start | bytes 786440 | tf_op jit(solution)/shard_map/ppermute | solution.py:401
  124.0 25.1 %collective-permute-start.23 = (bf16[8,144,128]{2,1,0:T(8,128)(2,1)S(1)}, bf16[8,144,128]{2,1,0:T(8,128)(2,1)S(1)}, u32[]{:S(2)}, u32[]{:S(2)}) collective-permute-start(bf16[8,144,128]{2,1,0:T(8,128)(2,1)S(1)} %get-tuple-element.113), channel_id=1, source_target_pairs={{0,16},{4,20},{8,24},{12,28},{16,0},{20,4},{24,8},{28,12},{1,17},{... | collective-permute-start | bytes 884744 | tf_op jit(solution)/shard_map/ppermute | solution.py:406
  130.5 23.5 %collective-permute-start.22 = (bf16[128,1024]{1,0:T(8,128)(2,1)S(1)}, bf16[128,1024]{1,0:T(8,128)(2,1)S(1)}, u32[]{:S(2)}, u32[]{:S(2)}) collective-permute-start(bf16[128,1024]{1,0:T(8,128)(2,1)S(1)} %copy-done.50), channel_id=1, source_target_pairs={{0,4},{4,8},{8,12},{12,0},{16,20},{20,24},{24,28},{28,16},{1,5},{5... | collective-permute-start | bytes 786440 | tf_op jit(solution)/shard_map/ppermute | solution.py:401
  132.7 21.2 %collective-permute-start.21 = (bf16[128,1024]{1,0:T(8,128)(2,1)S(1)}, bf16[128,1024]{1,0:T(8,128)(2,1)S(1)}, u32[]{:S(2)}, u32[]{:S(2)}) collective-permute-start(bf16[128,1024]{1,0:T(8,128)(2,1)S(1)} %copy-done.49), channel_id=1, source_target_pairs={{0,8},{4,12},{8,0},{12,4},{16,24},{20,28},{24,16},{28,20},{1,9},{5... | collective-permute-start | bytes 786440 | tf_op jit(solution)/shard_map/ppermute | solution.py:401
  132.7 21.2 %collective-permute-start.20 = (bf16[128,1024]{1,0:T(8,128)(2,1)S(1)}, bf16[128,1024]{1,0:T(8,128)(2,1)S(1)}, u32[]{:S(2)}, u32[]{:S(2)}) collective-permute-start(bf16[128,1024]{1,0:T(8,128)(2,1)S(1)} %copy-done.48), channel_id=1, source_target_pairs={{0,12},{4,0},{8,4},{12,8},{16,28},{20,16},{24,20},{28,24},{1,13},{... | collective-permute-start | bytes 786440 | tf_op jit(solution)/shard_map/ppermute | solution.py:401
  154.7 20.8 %all-to-all-start = ((bf16[4,128,512]{2,1,0:T(8,128)(2,1)}), bf16[4,128,512]{2,1,0:T(8,128)(2,1)S(1)}, u32[]{:S(2)}, u32[]{:S(2)}) async-start(bf16[4,128,512]{2,1,0:T(8,128)(2,1)} %get-tuple-element.120), calls=%async_computation | async-start | bytes 1048576 | tf_op jit(solution)/shard_map/all_to_all | solution.py:398
  158.2 8.2 %collective-permute-start.27 = (bf16[2,4,32,128]{3,2,1,0:T(8,128)(2,1)S(1)}, bf16[2,4,32,128]{3,2,1,0:T(8,128)(2,1)S(1)}, u32[]{:S(2)}, u32[]{:S(2)}) collective-permute-start(bf16[2,4,32,128]{3,2,1,0:T(8,128)(2,1)S(1)} %get-tuple-element.129), channel_id=1, source_target_pairs={{0,16},{1,17},{2,18},{3,19},{4,20},{5,21},{6,22},{7,23},{8,24},{9,... | collective-permute-start | bytes 196616 | tf_op jit(solution)/shard_map/ppermute | solution.py:420
  160.6 7.9 %collective-permute-start.29 = (bf16[2,4,32,128]{3,2,1,0:T(8,128)(2,1)S(1)}, bf16[2,4,32,128]{3,2,1,0:T(8,128)(2,1)S(1)}, u32[]{:S(2)}, u32[]{:S(2)}) collective-permute-start(bf16[2,4,32,128]{3,2,1,0:T(8,128)(2,1)S(1)} %get-tuple-element.131), channel_id=1, source_target_pairs={{0,18},{1,19},{2,16},{3,17},{4,22},{5,23},{6,20},{7,21},{8,26},{9,... | collective-permute-start | bytes 196616 | tf_op jit(solution)/shard_map/ppermute | solution.py:420
  162.3 11.7 %collective-permute-start.30 = (bf16[2,4,32,128]{3,2,1,0:T(8,128)(2,1)S(1)}, bf16[2,4,32,128]{3,2,1,0:T(8,128)(2,1)S(1)}, u32[]{:S(2)}, u32[]{:S(2)}) collective-permute-start(bf16[2,4,32,128]{3,2,1,0:T(8,128)(2,1)S(1)} %get-tuple-element.128), channel_id=1, source_target_pairs={{0,19},{1,16},{2,17},{3,18},{4,23},{5,20},{6,21},{7,22},{8,27},{9,... | collective-permute-start | bytes 196616 | tf_op jit(solution)/shard_map/ppermute | solution.py:420
  (60 other events, 635.3 us)
